TPU v7x, 32 devices: a whole 2x2x4 slice. The times are simulated.
32 devices in a mesh: grp: 16 (over z, x, core), slab: 2 (over y).
Axes of the slice: x: 2, y: 2, z: 4, core: 2. Of those that a mesh axis runs over, the one named last changes fastest.
Arguments:
- fwd_fields: float32 [16, 6, 16, 128, 128], P('grp', None, 'slab'), may hold values from -6 to 6
- adj_fields: float32 [16, 6, 16, 128, 128], P('grp', None, 'slab'), may hold values from -6 to 6
- density: float32 [16, 128, 128], P('slab', 'grp'), may hold values from 0 to 1
- block_ids: int32 [16], replicated, may hold values from 0 to 15, each once
- material_idx: int32 [16], replicated, may hold values from 0 to 3
- material_eps: float32 [4], replicated, may hold values from 1 to 12
- source_pos: int32 [16, 3], P('grp'), may hold values from 0 to 127, as said below
- wave_idx: int32 [16], P('grp'), may hold values from 0 to 3
Outputs:
- final_fields: float32 [16, 6, 16, 128, 128], P('grp', None, 'slab')
- grad_density: float32 [16, 128, 128], P('slab', 'grp')
Inputs may be any that keep to these rules, and one draw needn't show every extreme that they name: `block_ids`: a permutation of the 16 blocks. `source_pos`: cells inside the window: z below 16, x below 128, y below 128; some group's z is 0, some group's x is 127 and some group's y is 127.
All inputs are finite; a program needn't handle non-finite values.
Results may differ from a plain program's by a relative error of at most 0.0003.
Values sent between devices are 32-bit elements; how exact they have to be, the bound alone decides.
No kernel may reach another device: no remote copies, remote signals or barrier semaphores. Data moves between devices by JAX's collectives and lax.ppermute only.
A program may use at most 64 MiB of HBM per device.

v0:
```python
import math

import jax
import jax.numpy as jnp
from jax import lax
from jax.sharding import PartitionSpec as P

STEPS = 4


COURANT = 0.5
AMPLITUDE = 4.0


def from_behind(block, axis, distance):
    devices = range(lax.axis_size(axis))
    route = [(i - distance, i) for i in devices if i - distance in devices]
    return lax.ppermute(block, axis, route)


def fwd_diff(field, axis):
    pads = [(0, 0)] * field.ndim
    pads[axis] = (0, 1)
    padded = jnp.pad(field, pads)
    return lax.slice_in_dim(padded, 1, field.shape[axis] + 1, axis=axis) - field


def bwd_diff(field, axis):
    pads = [(0, 0)] * field.ndim
    pads[axis] = (1, 0)
    padded = jnp.pad(field, pads)
    return field - lax.slice_in_dim(padded, 0, field.shape[axis], axis=axis)


def above_diff(field, upper):
    return jnp.concatenate([field[:, 1:], upper], axis=1) - field


def below_diff(field, lower):
    return field - jnp.concatenate([lower, field[:, :-1]], axis=1)


def filter_xy(values):
    padded = jnp.pad(values, ((0, 0), (1, 1), (1, 1)))
    rows = padded[:, :-2] + 2.0 * padded[:, 1:-1] + padded[:, 2:]
    return (rows[:, :, :-2] + 2.0 * rows[:, :, 1:-1] + rows[:, :, 2:]) / 16.0


def source_profile(zcoord, xcoord, ycoord, position, width_x, width_y):
    in_plane = (zcoord == position[0]).astype(jnp.float32)
    offset_x = (xcoord - position[1]).astype(jnp.float32) / (width_x / 4.0)
    offset_y = (ycoord - position[2]).astype(jnp.float32) / (width_y / 4.0)
    return in_plane * jnp.exp(-0.5 * (offset_x * offset_x + offset_y * offset_y))


def layer_grid(first, layers, width_x, width_y):
    shape = (layers, width_x, width_y)
    zcoord = lax.broadcasted_iota(jnp.int32, shape, 0) + first
    xcoord = lax.broadcasted_iota(jnp.int32, shape, 1)
    ycoord = lax.broadcasted_iota(jnp.int32, shape, 2)
    return (zcoord, xcoord, ycoord)


def per_device(
    fwd_fields, adj_fields, density, block_ids, material_idx, material_eps, source_pos, wave_idx
):
    depth = fwd_fields.shape[2]
    width_x = fwd_fields.shape[3]
    width_y = fwd_fields.shape[4]
    nblock = block_ids.shape[0]
    block_rows = width_x // nblock
    slab_first = lax.axis_index("slab") * depth
    owned = lax.all_gather(density, "grp", axis=1, tiled=True)
    blocks = owned.reshape(depth, nblock, block_rows, width_y)
    placed = jnp.zeros_like(blocks).at[:, block_ids].set(blocks).reshape(depth, width_x, width_y)
    smooth = filter_xy(placed)
    onehot = (
        material_idx[:, None] == jnp.arange(material_eps.shape[0], dtype=jnp.int32)[None, :]
    ).astype(jnp.float32)
    base = jnp.sum(onehot * material_eps[None, :], axis=1)
    base_rows = jnp.repeat(base, block_rows)
    eps = base_rows[None, :, None] + 3.0 * smooth
    coef = 0.5 / eps
    position = source_pos[0]
    omega = 2.0 * math.pi / (6.0 + 2.0 * wave_idx[0].astype(jnp.float32))
    comps = [jnp.stack([fwd_fields[0, c], adj_fields[0, c]]) for c in range(6)]
    ex, ey, ez, hx, hy, hz = comps
    intersections = []
    zcoord, xcoord, ycoord = layer_grid(slab_first, depth, width_x, width_y)
    profile = source_profile(zcoord, xcoord, ycoord, position, width_x, width_y)
    zeros_field = jnp.zeros_like(profile)
    for step in range(STEPS):
        upper = from_behind(jnp.stack([ex[:, :1], ey[:, :1]]), "slab", -1)
        hx = hx - COURANT * (fwd_diff(ez, 3) - above_diff(ey, upper[1]))
        hy = hy - COURANT * (above_diff(ex, upper[0]) - fwd_diff(ez, 2))
        hz = hz - COURANT * (fwd_diff(ey, 2) - fwd_diff(ex, 3))
        lower = from_behind(jnp.stack([hx[:, -1:], hy[:, -1:]]), "slab", 1)
        drive = jnp.stack([AMPLITUDE * jnp.sin(omega * (step + 1.0)) * profile, zeros_field])
        ex = ex + coef * (bwd_diff(hz, 3) - below_diff(hy, lower[1]))
        ey = ey + coef * (below_diff(hx, lower[0]) - bwd_diff(hz, 2))
        ez = ez + coef * (bwd_diff(hy, 2) - bwd_diff(hx, 3)) + drive
        intersections.append(ex[0] * ex[1] + ey[0] * ey[1] + ez[0] * ez[1])
    total = intersections[0]
    for intersection in intersections[1:]:
        total = total + intersection
    grad_sum = lax.psum_scatter(
        filter_xy(total)
        .reshape(depth, nblock, block_rows, width_y)[:, block_ids]
        .reshape(depth, width_x, width_y),
        "grp",
        scatter_dimension=1,
        tiled=True,
    )
    scale = 3.0 / (STEPS * math.sqrt(lax.axis_size("grp")))
    finals = jnp.stack([ex[0], ey[0], ez[0], hx[0], hy[0], hz[0]])[None]
    return (finals, grad_sum * scale)


def solution(mesh):
    placed = (
        P("grp", None, "slab", None, None),
        P("grp", None, "slab", None, None),
        P("slab", "grp", None),
        P(),
        P(),
        P(),
        P("grp", None),
        P("grp"),
    )
    return jax.shard_map(
        per_device,
        mesh=mesh,
        in_specs=placed,
        out_specs=(P("grp", None, "slab", None, None), P("slab", "grp", None)),
        check_vma=False,
    )
```

profile of v0, /device:TPU:0, one launch (start us, length us, event | category | flops | bytes accessed | tf_op | source)
XLA Modules:
  0.0 195.0 jit_solution(3255392824071180334)
XLA Ops:
  7.2 3.5 %slice_bitcast_fusion = (f32[1,8,128,128]{3,2,1,0:T(8,128)}, f32[1,8,128,128]{3,2,1,0:T(8,128)}, f32[1,8,128,128]{3,2,1,0:T(8,128)S(1)}, f32[1,8,128,128]{3,2,1,...) fusion(f32[1,6,8,128,128]{4,3,2,1,0:T(8,128)} %param.9), kind=kLoop, calls=%fused_computation.226 | loop fusion | bytes 6291456 | tf_op jit(solution)/shard_map/stack;squeeze | solution.py:86
  10.7 1.4 slice_bitcast_fusion.1
  18.9 24.6 %all_gather.3 = f32[8,128,128]{2,1,0:T(8,128)S(1)} all-gather(f32[8,8,128]{2,1,0:T(8,128)S(1)} %copy-done.21), channel_id=1, replica_groups=mesh['grp'=16,'slab'=2] {'grp'}, dimensions={1}, use_global_device_ids=true | all-gather | bytes 557056 | tf_op jit(solution)/shard_map/all_gather | solution.py:73
  44.8 1.9 fusion.67
  46.7 1.3 pad_maximum_fusion.2
  49.9 1.6 fusion.133
  53.9 2.2 %fusion.131 = f32[8,128,128]{2,1,0:T(8,128)S(1)} fusion(f32[8,128,130]{2,1,0:T(8,128)} %fusion.67, f32[128]{0:T(128)S(1)} %add.241), kind=kLoop, calls=%fused_computation.216 | loop fusion | flops 786432 | bytes 2097664 | tf_op jit(solution)/shard_map/div | solution.py:83
  59.0 4.7 %collective-permute-start.1 = (f32[2,2,1,128,128]{4,3,1,2,0:T(8,128)S(1)}, f32[2,2,1,128,128]{4,3,1,2,0:T(8,128)S(1)}, u32[]{:S(2)}, u32[]{:S(2)}) collective-permute-start(f32[2,2,1,128,128]{4,3,1,2,0:T(8,128)S(1)} %pad_maximum_fusion.4), channel_id=1, source_target_pairs={{0,1},{2,3},{4,5},{6,7},{8,9},{10,11},{12,13},{14,15},{16,17},{18,... | collective-permute-start | bytes 786440 | tf_op jit(solution)/shard_map/ppermute | solution.py:18
  64.2 5.5 %collective-permute-done.1 = f32[2,2,1,128,128]{4,3,1,2,0:T(8,128)S(1)} collective-permute-done((f32[2,2,1,128,128]{4,3,1,2,0:T(8,128)S(1)}, f32[2,2,1,128,128]{4,3,1,2,0:T(8,128)S(1)}, u32[]{:S(2)}, u32[]{:S(2)}) %collective-permute-start.1) | collective-permute-done | bytes 262176 | tf_op jit(solution)/shard_map/ppermute | solution.py:18
  69.8 1.7 fusion.18
  73.0 8.3 %collective-permute-done.2 = f32[2,2,1,128,128]{4,3,1,2,0:T(8,128)S(1)} collective-permute-done((f32[2,2,1,128,128]{4,3,1,2,0:T(8,128)S(1)}, f32[2,2,1,128,128]{4,3,1,2,0:T(8,128)S(1)}, u32[]{:S(2)}, u32[]{:S(2)}) %collective-permute-start.2) | collective-permute-done | bytes 262176 | tf_op jit(solution)/shard_map/ppermute | solution.py:18
  81.4 1.7 fusion.90
  83.1 1.6 collective-permute-start.3
  84.9 4.4 %collective-permute-done.3 = f32[2,2,1,128,128]{4,3,1,2,0:T(8,128)S(1)} collective-permute-done((f32[2,2,1,128,128]{4,3,1,2,0:T(8,128)S(1)}, f32[2,2,1,128,128]{4,3,1,2,0:T(8,128)S(1)}, u32[]{:S(2)}, u32[]{:S(2)}) %collective-permute-start.3) | collective-permute-done | bytes 262176 | tf_op jit(solution)/shard_map/ppermute | solution.py:18
  89.4 1.4 fusion.35
  90.9 1.3 collective-permute-start.4
  92.3 6.8 %collective-permute-done.4 = f32[2,2,1,128,128]{4,3,1,2,0:T(8,128)S(1)} collective-permute-done((f32[2,2,1,128,128]{4,3,1,2,0:T(8,128)S(1)}, f32[2,2,1,128,128]{4,3,1,2,0:T(8,128)S(1)}, u32[]{:S(2)}, u32[]{:S(2)}) %collective-permute-start.4) | collective-permute-done | bytes 262176 | tf_op jit(solution)/shard_map/ppermute | solution.py:18
  99.2 1.4 fusion.100
  100.6 1.8 collective-permute-start.5
  102.5 3.5 %collective-permute-done.5 = f32[2,2,1,128,128]{4,3,1,2,0:T(8,128)S(1)} collective-permute-done((f32[2,2,1,128,128]{4,3,1,2,0:T(8,128)S(1)}, f32[2,2,1,128,128]{4,3,1,2,0:T(8,128)S(1)}, u32[]{:S(2)}, u32[]{:S(2)}) %collective-permute-start.5) | collective-permute-done | bytes 262176 | tf_op jit(solution)/shard_map/ppermute | solution.py:18
  106.1 1.4 fusion.52
  109.0 6.8 %collective-permute-done.6 = f32[2,2,1,128,128]{4,3,1,2,0:T(8,128)S(1)} collective-permute-done((f32[2,2,1,128,128]{4,3,1,2,0:T(8,128)S(1)}, f32[2,2,1,128,128]{4,3,1,2,0:T(8,128)S(1)}, u32[]{:S(2)}, u32[]{:S(2)}) %collective-permute-start.6) | collective-permute-done | bytes 262176 | tf_op jit(solution)/shard_map/ppermute | solution.py:18
  115.9 1.3 fusion.110
  117.3 1.5 collective-permute-start.7
  118.9 3.7 %collective-permute-done.7 = f32[2,2,1,128,128]{4,3,1,2,0:T(8,128)S(1)} collective-permute-done((f32[2,2,1,128,128]{4,3,1,2,0:T(8,128)S(1)}, f32[2,2,1,128,128]{4,3,1,2,0:T(8,128)S(1)}, u32[]{:S(2)}, u32[]{:S(2)}) %collective-permute-start.7) | collective-permute-done | bytes 262176 | tf_op jit(solution)/shard_map/ppermute | solution.py:18
  122.6 1.3 fusion.65
  124.8 1.4 fusion.119
  128.3 2.4 %gather_fusion = f32[16,8,8,128]{3,2,1,0:T(8,128)} fusion(f32[8,16,8,128]{3,2,1,0:T(8,128)} %fusion.115, s32[1024]{0:T(1024)S(1)} %pad_clamp_fusion), kind=kCustom, calls=%fused_computation | custom fusion | bytes 1048640 | tf_op jit(solution)/shard_map/gather | solution.py:107
  130.7 1.9 copy_bitcast_fusion
  132.6 2.0 %slice_dynamic-update-slice_fusion.4 = f32[6,8,128,128]{3,2,1,0:T(8,128)} fusion(f32[6,8,128,128]{3,2,1,0:T(8,128)} %slice_dynamic-update-slice_fusion.5, f32[2,8,128,128]{3,2,1,0:T(8,128)} %copy-done), kind=kLoop, calls=%fused_computation.239 | loop fusion | bytes 1048576
  137.9 48.9 %reduce-scatter.2.cloned.1.call-done = f32[8,8,128]{2,1,0:T(8,128)} async-done(((f32[8,128,128]{2,1,0:T(8,128)}), f32[8,8,128]{2,1,0:T(8,128)}) %reduce-scatter.2.cloned.1.call-update) | async-done | bytes 32784 | tf_op jit(solution)/shard_map/reduce_scatter | solution.py:106
  186.8 1.4 broadcast_multiply_fusion
  (131 shorter events, 24.5 us)
Async XLA Ops:
  7.2 179.6 %reduce-scatter.2.cloned.1.call-start = ((), (), s32[]{:S(2)}) async-start(), calls=%async_computation.1 | async-start | bytes 557056 | tf_op jit(solution)/shard_map/reduce_scatter | solution.py:106
  7.2 3.5 %copy-start.12 = (f32[1,6,8,128,128]{4,3,2,1,0:T(8,128)S(1)}, f32[1,6,8,128,128]{4,3,2,1,0:T(8,128)}, u32[]{:S(2)}) copy-start(f32[1,6,8,128,128]{4,3,2,1,0:T(8,128)} %param.8) | copy-start | bytes 9437188
  12.9 43.2 %collective-permute-start = (f32[2,2,1,128,128]{4,3,1,2,0:T(8,128)}, f32[2,2,1,128,128]{4,3,1,2,0:T(8,128)S(1)}, u32[]{:S(2)}, u32[]{:S(2)}) collective-permute-start(f32[2,2,1,128,128]{4,3,1,2,0:T(8,128)} %pad_maximum_fusion.3), channel_id=1, source_target_pairs={{1,0},{3,2},{5,4},{7,6},{9,8},{11,10},{13,12},{15,14},{17,16},{19,... | collective-permute-start | bytes 786440 | tf_op jit(solution)/shard_map/ppermute | solution.py:18
  15.2 2.8 %copy-start.22 = (s32[1,3]{1,0:T(1,128)S(1)}, s32[1,3]{1,0:T(1,128)}, u32[]{:S(2)}) copy-start(s32[1,3]{1,0:T(1,128)} %param.14) | copy-start | bytes 40
  15.2 3.7 %copy-start.23 = (s32[16]{0:T(128)S(1)}, s32[16]{0:T(128)}, u32[]{:S(2)}) copy-start(s32[16]{0:T(128)} %param.11) | copy-start | bytes 196
  15.2 3.7 %copy-start.21 = (f32[8,8,128]{2,1,0:T(8,128)S(1)}, f32[8,8,128]{2,1,0:T(8,128)}, u32[]{:S(2)}) copy-start(f32[8,8,128]{2,1,0:T(8,128)} %param.10) | copy-start | bytes 98308
  46.7 4.8 %copy-start.24 = (f32[4]{0:T(128)S(1)}, f32[4]{0:T(128)}, u32[]{:S(2)}) copy-start(f32[4]{0:T(128)} %param.13) | copy-start | bytes 52
  46.7 4.8 %copy-start.25 = (s32[16]{0:T(128)S(1)}, s32[16]{0:T(128)}, u32[]{:S(2)}) copy-start(s32[16]{0:T(128)} %param.12) | copy-start | bytes 196
  49.9 2.7 %copy-start.9 = (f32[2,8,128,128]{3,2,1,0:T(8,128)S(1)}, f32[2,8,128,128]{3,2,1,0:T(8,128)}, u32[]{:S(2)}) copy-start(f32[2,8,128,128]{3,2,1,0:T(8,128)} %pad_maximum_fusion.1) | copy-start | bytes 3145732
  53.8 2.3 %copy-start.8 = (f32[2,8,128,128]{3,2,0,1:T(8,128)S(1)}, f32[2,8,128,128]{3,2,0,1:T(8,128)}, u32[]{:S(2)}) copy-start(f32[2,8,128,128]{3,2,0,1:T(8,128)} %copy.113) | copy-start | bytes 3145732
  53.9 2.3 %copy-start.10 = (f32[2,7,128,128]{3,2,0,1:T(8,128)S(1)}, f32[2,7,128,128]{3,2,0,1:T(8,128)}, u32[]{:S(2)}) copy-start(f32[2,7,128,128]{3,2,0,1:T(8,128)} %fusion.113) | copy-start | bytes 2752516
  56.2 1.6 copy-start.18
  56.2 1.8 copy-start.19
  58.8 4.9 %copy-start.7 = (f32[2,8,128,128]{3,2,0,1:T(8,128)S(1)}, f32[2,8,128,128]{3,2,0,1:T(8,128)}, u32[]{:S(2)}) copy-start(f32[2,8,128,128]{3,2,0,1:T(8,128)} %copy.108) | copy-start | bytes 3145732
  58.9 5.1 %copy-start.3 = (f32[1,8,128,128]{3,2,1,0:T(8,128)S(1)}, f32[1,8,128,128]{3,2,1,0:T(8,128)}, u32[]{:S(2)}) copy-start(f32[1,8,128,128]{3,2,1,0:T(8,128)} %get-tuple-element.11) | copy-start | bytes 1572868
  58.9 5.1 %copy-start.4 = (f32[1,8,128,128]{3,2,1,0:T(8,128)S(1)}, f32[1,8,128,128]{3,2,1,0:T(8,128)}, u32[]{:S(2)}) copy-start(f32[1,8,128,128]{3,2,1,0:T(8,128)} %get-tuple-element.5) | copy-start | bytes 1572868
  59.0 10.8 %collective-permute-start.1 = (f32[2,2,1,128,128]{4,3,1,2,0:T(8,128)S(1)}, f32[2,2,1,128,128]{4,3,1,2,0:T(8,128)S(1)}, u32[]{:S(2)}, u32[]{:S(2)}) collective-permute-start(f32[2,2,1,128,128]{4,3,1,2,0:T(8,128)S(1)} %pad_maximum_fusion.4), channel_id=1, source_target_pairs={{0,1},{2,3},{4,5},{6,7},{8,9},{10,11},{12,13},{14,15},{16,17},{18,... | collective-permute-start | bytes 786440 | tf_op jit(solution)/shard_map/ppermute | solution.py:18
  64.0 5.7 %copy-start.5 = (f32[1,8,128,128]{3,2,1,0:T(8,128)S(1)}, f32[1,8,128,128]{3,2,1,0:T(8,128)}, u32[]{:S(2)}) copy-start(f32[1,8,128,128]{3,2,1,0:T(8,128)} %get-tuple-element.13) | copy-start | bytes 1572868
  64.1 5.7 %copy-start.6 = (f32[1,8,128,128]{3,2,1,0:T(8,128)S(1)}, f32[1,8,128,128]{3,2,1,0:T(8,128)}, u32[]{:S(2)}) copy-start(f32[1,8,128,128]{3,2,1,0:T(8,128)} %get-tuple-element.7) | copy-start | bytes 1572868
  64.1 5.7 %copy-start.20 = (f32[1,8,128,128]{3,2,1,0:T(8,128)S(1)}, f32[1,8,128,128]{3,2,1,0:T(8,128)}, u32[]{:S(2)}) copy-start(f32[1,8,128,128]{3,2,1,0:T(8,128)} %get-tuple-element.56) | copy-start | bytes 1572868
  71.6 9.8 %collective-permute-start.2 = (f32[2,2,1,128,128]{4,3,1,2,0:T(8,128)S(1)}, f32[2,2,1,128,128]{4,3,1,2,0:T(8,128)S(1)}, u32[]{:S(2)}, u32[]{:S(2)}) collective-permute-start(f32[2,2,1,128,128]{4,3,1,2,0:T(8,128)S(1)} %pad_maximum_fusion.5), channel_id=1, source_target_pairs={{1,0},{3,2},{5,4},{7,6},{9,8},{11,10},{13,12},{15,14},{17,16},{19,... | collective-permute-start | bytes 786440 | tf_op jit(solution)/shard_map/ppermute | solution.py:18
  83.1 6.2 %copy-start.15 = (f32[1,8,128,128]{3,2,1,0:T(8,128)S(1)}, f32[1,8,128,128]{3,2,1,0:T(8,128)}, u32[]{:S(2)}) copy-start(f32[1,8,128,128]{3,2,1,0:T(8,128)} %get-tuple-element.55) | copy-start | bytes 1572868
  83.1 6.2 %collective-permute-start.3 = (f32[2,2,1,128,128]{4,3,1,2,0:T(8,128)S(1)}, f32[2,2,1,128,128]{4,3,1,2,0:T(8,128)S(1)}, u32[]{:S(2)}, u32[]{:S(2)}) collective-permute-start(f32[2,2,1,128,128]{4,3,1,2,0:T(8,128)S(1)} %pad_maximum_fusion.6), channel_id=1, source_target_pairs={{0,1},{2,3},{4,5},{6,7},{8,9},{10,11},{12,13},{14,15},{16,17},{18,... | collective-permute-start | bytes 786440 | tf_op jit(solution)/shard_map/ppermute | solution.py:18
  90.9 8.3 %collective-permute-start.4 = (f32[2,2,1,128,128]{4,3,1,2,0:T(8,128)S(1)}, f32[2,2,1,128,128]{4,3,1,2,0:T(8,128)S(1)}, u32[]{:S(2)}, u32[]{:S(2)}) collective-permute-start(f32[2,2,1,128,128]{4,3,1,2,0:T(8,128)S(1)} %pad_maximum_fusion.7), channel_id=1, source_target_pairs={{1,0},{3,2},{5,4},{7,6},{9,8},{11,10},{13,12},{15,14},{17,16},{19,... | collective-permute-start | bytes 786440 | tf_op jit(solution)/shard_map/ppermute | solution.py:18
  100.6 5.5 %copy-start.14 = (f32[1,8,128,128]{3,2,1,0:T(8,128)S(1)}, f32[1,8,128,128]{3,2,1,0:T(8,128)}, u32[]{:S(2)}) copy-start(f32[1,8,128,128]{3,2,1,0:T(8,128)} %get-tuple-element.54) | copy-start | bytes 1572868
  100.6 5.5 %collective-permute-start.5 = (f32[2,2,1,128,128]{4,3,1,2,0:T(8,128)S(1)}, f32[2,2,1,128,128]{4,3,1,2,0:T(8,128)S(1)}, u32[]{:S(2)}, u32[]{:S(2)}) collective-permute-start(f32[2,2,1,128,128]{4,3,1,2,0:T(8,128)S(1)} %pad_maximum_fusion.8), channel_id=1, source_target_pairs={{0,1},{2,3},{4,5},{6,7},{8,9},{10,11},{12,13},{14,15},{16,17},{18,... | collective-permute-start | bytes 786440 | tf_op jit(solution)/shard_map/ppermute | solution.py:18
  107.6 8.3 %collective-permute-start.6 = (f32[2,2,1,128,128]{4,3,1,2,0:T(8,128)S(1)}, f32[2,2,1,128,128]{4,3,1,2,0:T(8,128)S(1)}, u32[]{:S(2)}, u32[]{:S(2)}) collective-permute-start(f32[2,2,1,128,128]{4,3,1,2,0:T(8,128)S(1)} %pad_maximum_fusion.9), channel_id=1, source_target_pairs={{1,0},{3,2},{5,4},{7,6},{9,8},{11,10},{13,12},{15,14},{17,16},{19,... | collective-permute-start | bytes 786440 | tf_op jit(solution)/shard_map/ppermute | solution.py:18
  117.2 5.4 %copy-start.1 = (f32[2,8,128,128]{3,2,1,0:T(8,128)}, f32[2,8,128,128]{3,2,1,0:T(8,128)S(1)}, u32[]{:S(2)}) copy-start(f32[2,8,128,128]{3,2,1,0:T(8,128)S(1)} %get-tuple-element.27) | copy-start | bytes 3145732
  117.3 5.3 %collective-permute-start.7 = (f32[2,2,1,128,128]{4,3,1,2,0:T(8,128)S(1)}, f32[2,2,1,128,128]{4,3,1,2,0:T(8,128)S(1)}, u32[]{:S(2)}, u32[]{:S(2)}) collective-permute-start(f32[2,2,1,128,128]{4,3,1,2,0:T(8,128)S(1)} %pad_maximum_fusion.10), channel_id=1, source_target_pairs={{0,1},{2,3},{4,5},{6,7},{8,9},{10,11},{12,13},{14,15},{16,17},{18,... | collective-permute-start | bytes 786440 | tf_op jit(solution)/shard_map/ppermute | solution.py:18
  118.8 3.9 %copy-start.13 = (f32[1,8,128,128]{3,2,1,0:T(8,128)S(1)}, f32[1,8,128,128]{3,2,1,0:T(8,128)}, u32[]{:S(2)}) copy-start(f32[1,8,128,128]{3,2,1,0:T(8,128)} %get-tuple-element.53) | copy-start | bytes 1572868
  123.9 2.3 %copy-start = (f32[2,8,128,128]{3,2,1,0:T(8,128)}, f32[2,8,128,128]{3,2,1,0:T(8,128)S(1)}, u32[]{:S(2)}) copy-start(f32[2,8,128,128]{3,2,1,0:T(8,128)S(1)} %get-tuple-element.15) | copy-start | bytes 3145732
  132.6 4.5 %copy-start.2 = (f32[2,8,128,128]{3,2,1,0:T(8,128)S(1)}, f32[2,8,128,128]{3,2,1,0:T(8,128)}, u32[]{:S(2)}) copy-start(f32[2,8,128,128]{3,2,1,0:T(8,128)} %copy-done.1) | copy-start | bytes 3145732
  (3 other events, 3.9 us)
Sparse Core Ops, SparseCore 0:
  132.7 54.0 reduce-scatter.1
where the time goes:
time: 196 us; the launch traced here: 195 us
  waiting for transfers between devices  88 us (45%)
  other arithmetic  29.4 us (15%)
  blocking collectives  24.6 us (13%)
  local copies, waits for them, and re-layouts  22.4 us (11%)
  between operations  15.9 us (8%)
  starting transfers between devices  14.7 us (8%)
    reduce_scatter x1, waiting for transfers between devices, per_device(): lax.psum_scatter(filter_xy(total).reshape(depth, nblock, block_rows, widt...  48.9 us
    ppermute x8, waiting for transfers between devices, from_behind(): return lax.ppermute(block, axis, route)  39.1 us
    all_gather x1, blocking collectives, per_device(): owned = lax.all_gather(density, 'grp', axis=1, tiled=True)  24.6 us
    ppermute x8, starting transfers between devices, from_behind(): return lax.ppermute(block, axis, route)  14.7 us
    another operation x4, local copies, waits for them, and re-layouts, per_device(): comps = [jnp.stack([fwd_fields[0, c], adj_fields[0, c]]) for c in range(6)]  7.04 us
    unnamed x57, local copies, waits for them, and re-layouts  6.87 us
    add x4, other arithmetic, per_device(): ez = ez + coef * (bwd_diff(hy, 2) - bwd_diff(hx, 3)) + drive  5.87 us
    sub x4, other arithmetic, per_device(): hx = hx - COURANT * (fwd_diff(ez, 3) - above_diff(ey, upper[1]))  5.18 us
  transfers between devices with their start and end apart: 9, of which 8 were waited for; matrix products, arithmetic and copies ran while one was open for 12% of the time, Pallas kernels for 0%

commit v1 on v0

v1 whole, which is shorter than its diff:
```python
import functools
import math

import jax
import jax.numpy as jnp
from jax import lax
from jax.experimental import pallas as pl
from jax.experimental.pallas import tpu as pltpu
from jax.sharding import PartitionSpec as P

STEPS = 4
AMPLITUDE = 4.0
PAD = 8
F32 = jnp.float32

VMEM = pltpu.MemorySpace.VMEM
IN_VMEM = pl.BlockSpec(memory_space=pltpu.VMEM)
IN_SMEM = pl.BlockSpec(memory_space=pltpu.SMEM)
IN_HBM = pl.BlockSpec(memory_space=pltpu.MemorySpace.HBM)


def on_chip(*shape):
    return VMEM(shape, F32)


def held(array, spec):
    if spec is IN_SMEM:
        return array
    space = VMEM if spec is IN_VMEM else pltpu.MemorySpace.HBM
    return pltpu.with_memory_space_constraint(array, space)


def call(kernel, outs, out_specs, operands, specs, scratch=(), aliases=None, flops=0):
    operands = [held(a, s) for a, s in zip(operands, specs)]
    return pl.pallas_call(
        kernel,
        out_shape=outs,
        in_specs=specs,
        out_specs=out_specs,
        scratch_shapes=scratch,
        input_output_aliases=aliases or {},
        compiler_params=pltpu.CompilerParams(vmem_limit_bytes=8 << 20),
        cost_estimate=pl.CostEstimate(flops=flops, bytes_accessed=flops // 4, transcendentals=0),
    )(*operands)


def chunks(rows):
    size = 32 if rows % 32 == 0 else rows
    return [(first, size) for first in range(0, rows, size)]


def last_lane(shape):
    return lax.broadcasted_iota(jnp.int32, shape, 1) == shape[1] - 1


def first_lane(shape):
    return lax.broadcasted_iota(jnp.int32, shape, 1) == 0


def next_col(value):
    return jnp.where(last_lane(value.shape), 0.0, pltpu.roll(value, value.shape[1] - 1, 1))


def prev_col(value):
    return jnp.where(first_lane(value.shape), 0.0, pltpu.roll(value, 1, 1))


def update_h(state, evo, layer, upper, rows, double=False):
    for first, size in chunks(rows):
        here = pl.ds(PAD + first, size)
        after = pl.ds(PAD + first + 1, size)
        ex = state[evo, 0, layer, here, :]
        ey = state[evo, 1, layer, here, :]
        ez = state[evo, 2, layer, here, :]
        hx = state[evo, 3, layer, here, :]
        hy = state[evo, 4, layer, here, :]
        hz = state[evo, 5, layer, here, :]
        if double:
            hx, hy, hz = hx + hx, hy + hy, hz + hz
        if upper is None:
            rise_x, rise_y = -ex, -ey
        else:
            rise_x, rise_y = upper(0, first, size) - ex, upper(1, first, size) - ey
        ez_after = state[evo, 2, layer, after, :]
        ey_after = state[evo, 1, layer, after, :]
        state[evo, 3, layer, here, :] = hx - ((next_col(ez) - ez) - rise_y)
        state[evo, 4, layer, here, :] = hy - (rise_x - (ez_after - ez))
        state[evo, 5, layer, here, :] = hz - ((ey_after - ey) - (next_col(ex) - ex))


def inner_upper(state, evo, layer):
    return lambda comp, first, size: state[evo, comp, layer + 1, pl.ds(PAD + first, size), :]


def update_e(state, coef, total, layer, lower, rows, add):
    for first, size in chunks(rows):
        here = pl.ds(PAD + first, size)
        before = pl.ds(PAD + first - 1, size)
        cell = coef[layer, pl.ds(first, size), :]
        news = []
        for evo in range(2):
            hx = state[evo, 3, layer, here, :]
            hy = state[evo, 4, layer, here, :]
            hz = state[evo, 5, layer, here, :]
            hy_before = state[evo, 4, layer, before, :]
            hz_before = state[evo, 5, layer, before, :]
            hx_below = lower(evo, 0, first, size)
            hy_below = lower(evo, 1, first, size)
            ex = state[evo, 0, layer, here, :] + cell * ((hz - prev_col(hz)) - (hy - hy_below))
            ey = state[evo, 1, layer, here, :] + cell * ((hx - hx_below) - (hz - hz_before))
            ez = state[evo, 2, layer, here, :] + cell * ((hy - hy_before) - (hx - prev_col(hx)))
            news.append((ex, ey, ez))
        if add is not None:
            news[0] = (news[0][0], news[0][1], news[0][2] + add(first, size))
        for evo in range(2):
            for comp in range(3):
                state[evo, comp, layer, here, :] = news[evo][comp]
        part = (
            news[0][0] * news[1][0] + news[0][1] * news[1][1] + news[0][2] * news[1][2]
        )
        total[layer, here, :] = total[layer, here, :] + part


def inner_lower(state, layer):
    return lambda evo, comp, first, size: state[
        evo, 3 + comp, layer - 1, pl.ds(PAD + first, size), :
    ]


def driver(ints, drives, profile, layer, step):
    amount = jnp.where(ints[3] == layer, drives[step], 0.0)
    return lambda first, size: amount * profile[pl.ds(first, size), :]


def write_payload(state, pays, ints, rows):
    depth = state.shape[2]

    def up(pay):
        for evo in range(2):
            for comp in range(2):
                pay[evo, comp] = state[evo, 3 + comp, depth - 1, pl.ds(PAD, rows), :]

    def down(pay):
        for evo in range(2):
            for comp in range(2):
                pay[evo, comp] = state[evo, comp, 0, pl.ds(PAD, rows), :]

    if len(pays) == 2:
        up(pays[0])
        down(pays[1])
    else:
        pl.when(ints[0] == 1)(lambda: up(pays[0]))
        pl.when(ints[0] != 1)(lambda: down(pays[0]))


def load_kernel(swap, fwd, adj, ints, state, total, profile, *rest):
    pays, sems = rest[:-1], rest[-1]
    depth, width_x, width_y = fwd.shape[2:]
    copies = []
    for evo, source in enumerate((fwd, adj)):
        for comp in range(6):
            copies.append(
                pltpu.make_async_copy(
                    source.at[0, comp],
                    state.at[evo, comp, :, pl.ds(PAD, width_x), :],
                    sems.at[evo, comp],
                )
            )
    for copy in copies:
        copy.start()
    edge = jnp.zeros((PAD, width_y), F32)

    def clear(layer, carry):
        for evo in range(2):
            for comp in range(6):
                state[evo, comp, layer, pl.ds(0, PAD), :] = edge
                state[evo, comp, layer, pl.ds(PAD + width_x, PAD), :] = edge
        total[layer] = jnp.zeros((width_x + 2 * PAD, width_y), F32)
        return carry

    lax.fori_loop(0, depth, clear, 0)
    xcoord = lax.broadcasted_iota(jnp.int32, (width_x, width_y), 0)
    ycoord = lax.broadcasted_iota(jnp.int32, (width_x, width_y), 1)
    offset_x = (xcoord - ints[4]).astype(F32) / (width_x / 4.0)
    offset_y = (ycoord - ints[5]).astype(F32) / (width_y / 4.0)
    profile[...] = jnp.exp(-0.5 * (offset_x * offset_x + offset_y * offset_y))
    for copy in copies:
        copy.wait()
    for evo in range(2):
        update_h(state, evo, depth - 1, None, width_x, double=True)
    write_payload(state, pays, ints, width_x)


def first_kernel(state_in, state):
    depth = state.shape[2]
    rows = state.shape[3] - 2 * PAD

    def body(layer, carry):
        for evo in range(2):
            update_h(state, evo, layer, inner_upper(state, evo, layer), rows, double=True)
        return carry

    lax.fori_loop(0, depth - 1, body, 0)


def coef_kernel(layout, count, *refs):
    parts = refs[:count]
    block_ids, material_idx, material_eps, ints, coef, blocks, placed, wide = refs[count:]
    nblock = blocks.shape[0]
    depth, rows, width_y = coef.shape
    block_rows = rows // nblock
    for part, masks in zip(parts, layout):
        for slot, mask in enumerate(masks):
            blocks[block_ids[ints[2] ^ mask]] = part[slot]
    edge = jnp.zeros((PAD, width_y), F32)

    def layer_of(layer, carry):
        placed[pl.ds(0, PAD), :] = edge
        placed[pl.ds(PAD + rows, PAD), :] = edge
        for block in range(nblock):
            source = pl.ds(pl.multiple_of(layer * block_rows, block_rows), block_rows)
            placed[pl.ds(PAD + block * block_rows, block_rows), :] = blocks[block, source, :]
        smooth = filtered(placed, rows)
        wide[...] = smooth
        for block in range(nblock):
            base = material_eps[material_idx[block]]
            here = pl.ds(block * block_rows, block_rows)
            coef[layer, here, :] = 0.25 / (base + 3.0 * wide[here, :])
        return carry

    lax.fori_loop(0, depth, layer_of, 0)


def filtered(padded, rows):
    here = padded[pl.ds(PAD, rows), :]
    along = (
        padded[pl.ds(PAD - 1, rows), :] + 2.0 * here + padded[pl.ds(PAD + 1, rows), :]
    )
    return (prev_col(along) + 2.0 * along + next_col(along)) * 0.0625


def bulk_kernel(step, state_in, total_in, coef, ints, drives, profile, state, total):
    depth = state.shape[2]
    rows = state.shape[3] - 2 * PAD
    if step > 0:
        for evo in range(2):
            update_h(state, evo, 0, inner_upper(state, evo, 0), rows)

    def body(layer, carry):
        if step > 0:
            for evo in range(2):
                update_h(state, evo, layer, inner_upper(state, evo, layer), rows)
        update_e(
            state,
            coef,
            total,
            layer,
            inner_lower(state, layer),
            rows,
            driver(ints, drives, profile, layer, step),
        )
        return carry

    lax.fori_loop(1, depth - 1, body, 0)


def edge_kernel(step, swap, state_in, total_in, coef, ints, drives, profile, *rest):
    arrived = rest[: 1 if swap else 2]
    state, total = rest[len(arrived) : len(arrived) + 2]
    pays, below = rest[len(arrived) + 2 : -1], rest[-1]
    from_below, from_above = arrived[0], arrived[-1]
    depth = state.shape[2]
    rows = state.shape[3] - 2 * PAD
    has_up = ints[0].astype(F32)
    has_low = ints[1].astype(F32)
    every = pl.ds(PAD, rows)
    top = depth - 1
    for evo in range(2):
        state[evo, 3, top, every, :] += has_up * from_above[evo, 1]
        state[evo, 4, top, every, :] -= has_up * from_above[evo, 0]
        below[evo, 0] = has_low * (from_below[evo, 0] + state[evo, 1, 0, every, :])
        below[evo, 1] = has_low * (from_below[evo, 1] - state[evo, 0, 0, every, :])
    update_e(
        state, coef, total, top, inner_lower(state, top), rows,
        driver(ints, drives, profile, top, step),
    )
    update_e(
        state,
        coef,
        total,
        0,
        lambda evo, comp, first, size: below[evo, comp, pl.ds(first, size), :],
        rows,
        driver(ints, drives, profile, 0, step),
    )
    if pays:
        for evo in range(2):
            update_h(state, evo, top, None, rows)
        write_payload(state, pays, ints, rows)


def pack_kernel(*refs):
    out = refs[-1]
    for slot, ref in enumerate(refs[:-1]):
        out[slot] = ref[...]


def filter_kernel(layout, total, block_ids, ints, *rest):
    parts, blocks, wide = rest[:-2], rest[-2], rest[-1]
    nblock = blocks.shape[0]
    depth = total.shape[0]
    rows = total.shape[1] - 2 * PAD
    block_rows = rows // nblock

    def layer_of(layer, carry):
        wide[...] = filtered(total.at[layer], rows)
        for block in range(nblock):
            target = pl.ds(pl.multiple_of(layer * block_rows, block_rows), block_rows)
            blocks[block, target, :] = wide[pl.ds(block * block_rows, block_rows), :]
        return carry

    lax.fori_loop(0, depth, layer_of, 0)
    for part, masks in zip(parts, layout):
        for slot, mask in enumerate(masks):
            part[slot] = blocks[block_ids[ints[2] ^ mask]]


def add_kernel(*refs):
    half = len(refs) // 3
    for a, b, out in zip(refs[:half], refs[half : 2 * half], refs[2 * half :]):
        out[...] = a[...] + b[...]


def add_split_kernel(count, *refs):
    terms, outs = refs[:count], refs[count:]
    for slot, out in enumerate(outs):
        value = terms[0][slot]
        for term in terms[1:]:
            value = value + term[slot]
        out[...] = value


def last_kernel(scale, *refs):
    value = refs[0][...]
    for ref in refs[1:-1]:
        value = value + ref[...]
    refs[-1][...] = value * scale


def out_kernel(state, finals, halves, sems):
    depth = state.shape[2]
    rows = state.shape[3] - 2 * PAD
    every = pl.ds(PAD, rows)
    copies = [
        pltpu.make_async_copy(
            state.at[0, comp, :, every, :], finals.at[0, comp], sems.at[comp]
        )
        for comp in range(3)
    ]
    for copy in copies:
        copy.start()
    for comp in range(3):

        def body(layer, carry):
            halves[comp, layer] = 0.5 * state[0, 3 + comp, layer, every, :]
            return carry

        lax.fori_loop(0, depth, body, 0)
        copy = pltpu.make_async_copy(halves.at[comp], finals.at[0, 3 + comp], sems.at[3 + comp])
        copy.start()
        copies.append(copy)
    for copy in copies:
        copy.wait()


def swap_over(array, axis, mask):
    return lax.ppermute(array, axis, [(i, i ^ mask) for i in range(lax.axis_size(axis))])


def shift_over(array, axis, distance):
    size = lax.axis_size(axis)
    route = [(i, i + distance) for i in range(size) if 0 <= i + distance < size]
    return lax.ppermute(array, axis, route)


def trade(pays):
    if len(pays) == 1:
        return [swap_over(pays[0], "slab", 1)]
    return [shift_over(pays[0], "slab", 1), shift_over(pays[1], "slab", -1)]


def per_device(
    fwd_fields, adj_fields, density, block_ids, material_idx, material_eps, source_pos, wave_idx
):
    depth, width_x, width_y = fwd_fields.shape[2:]
    nblock = block_ids.shape[0]
    block_rows = width_x // nblock
    ngrp = lax.axis_size("grp")
    nslab = lax.axis_size("slab")
    swap = nslab == 2
    slab = lax.axis_index("slab")
    me = lax.axis_index("grp")
    ints = jnp.stack(
        [
            (slab < nslab - 1).astype(jnp.int32),
            (slab > 0).astype(jnp.int32),
            me.astype(jnp.int32),
            source_pos[0, 0] - slab * depth,
            source_pos[0, 1],
            source_pos[0, 2],
        ]
    )
    omega = 2.0 * math.pi / (6.0 + 2.0 * wave_idx[0].astype(F32))
    drives = AMPLITUDE * jnp.sin(omega * (jnp.arange(STEPS, dtype=F32) + 1.0))

    far = 4
    middle = ngrp // (2 * far)
    far_masks = [2 * middle * j for j in range(far)]
    middle_masks = [2 * j for j in range(middle)]
    layout = [
        [core + mid + top for top in far_masks] for core in (0, 1) for mid in middle_masks
    ]
    piece = (depth * block_rows, width_y)
    group = (far,) + piece

    own = density.reshape(piece)
    pieces = [own] + [swap_over(own, "grp", mask) for mask in far_masks[1:]]
    near = call(pack_kernel, on_chip(*group), IN_VMEM, pieces, [IN_VMEM] * far)
    parts = [near] + [swap_over(near, "grp", mask) for mask in middle_masks[1:]]
    parts = parts + [swap_over(part, "grp", 1) for part in parts]

    state_shape = on_chip(2, 6, depth, width_x + 2 * PAD, width_y)
    total_shape = on_chip(depth, width_x + 2 * PAD, width_y)
    plane = on_chip(width_x, width_y)
    pay_shape = on_chip(2, 2, width_x, width_y)
    npay = 1 if swap else 2
    state, total, profile, *pays = call(
        functools.partial(load_kernel, swap),
        [state_shape, total_shape, plane] + [pay_shape] * npay,
        [IN_VMEM] * (3 + npay),
        [fwd_fields, adj_fields, ints],
        [IN_HBM, IN_HBM, IN_SMEM],
        [pltpu.SemaphoreType.DMA((2, 6))],
    )
    arrived = trade(pays)
    state = call(first_kernel, state_shape, IN_VMEM, [state], [IN_VMEM], aliases={0: 0})

    coef = call(
        functools.partial(coef_kernel, layout, len(parts)),
        on_chip(depth, width_x, width_y),
        IN_VMEM,
        parts + [block_ids, material_idx, material_eps, ints],
        [IN_VMEM] * len(parts) + [IN_SMEM] * 4,
        [
            pltpu.VMEM((nblock,) + piece, F32),
            pltpu.VMEM((width_x + 2 * PAD, width_y), F32),
            pltpu.VMEM((width_x, width_y), F32),
        ],
    )

    for step in range(STEPS):
        more = step < STEPS - 1
        state, total = call(
            functools.partial(bulk_kernel, step),
            [state_shape, total_shape],
            [IN_VMEM] * 2,
            [state, total, coef, ints, drives, profile],
            [IN_VMEM, IN_VMEM, IN_VMEM, IN_SMEM, IN_SMEM, IN_VMEM],
            aliases={0: 0, 1: 1},
        )
        state, total, *pays = call(
            functools.partial(edge_kernel, step, swap),
            [state_shape, total_shape] + [pay_shape] * (npay if more else 0),
            [IN_VMEM] * (2 + (npay if more else 0)),
            [state, total, coef, ints, drives, profile] + arrived,
            [IN_VMEM, IN_VMEM, IN_VMEM, IN_SMEM, IN_SMEM, IN_VMEM] + [IN_VMEM] * npay,
            [pltpu.VMEM((2, 2, width_x, width_y), F32)],
            aliases={0: 0, 1: 1},
        )
        if more:
            arrived = trade(pays)

    parts = call(
        functools.partial(filter_kernel, layout),
        [on_chip(*group)] * len(layout),
        [IN_VMEM] * len(layout),
        [total, block_ids, ints],
        [IN_VMEM, IN_SMEM, IN_SMEM],
        [pltpu.VMEM((nblock,) + piece, F32), pltpu.VMEM((width_x, width_y), F32)],
    )
    kept, sent = parts[:middle], parts[middle:]
    got = [swap_over(part, "grp", 1) for part in sent]
    sums = call(
        add_kernel,
        [on_chip(*group)] * middle,
        [IN_VMEM] * middle,
        list(kept) + got,
        [IN_VMEM] * (2 * middle),
    )
    got = [swap_over(part, "grp", mask) for part, mask in zip(sums[1:], middle_masks[1:])]
    pieces = call(
        functools.partial(add_split_kernel, middle),
        [on_chip(*piece)] * far,
        [IN_VMEM] * far,
        [sums[0]] + got,
        [IN_VMEM] * middle,
    )
    got = [swap_over(part, "grp", mask) for part, mask in zip(pieces[1:], far_masks[1:])]
    scale = 3.0 / (STEPS * math.sqrt(ngrp))
    grad = call(
        functools.partial(last_kernel, scale),
        jax.ShapeDtypeStruct(piece, F32),
        IN_VMEM,
        [pieces[0]] + got,
        [IN_VMEM] * far,
    )
    finals = call(
        out_kernel,
        jax.ShapeDtypeStruct(fwd_fields.shape, F32),
        IN_HBM,
        [state],
        [IN_VMEM],
        [
            pltpu.VMEM((3, depth, width_x, width_y), F32),
            pltpu.SemaphoreType.DMA((6,)),
        ],
    )
    return finals, grad.reshape(density.shape)


def solution(mesh):
    placed = (
        P("grp", None, "slab", None, None),
        P("grp", None, "slab", None, None),
        P("slab", "grp", None),
        P(),
        P(),
        P(),
        P("grp", None),
        P("grp"),
    )
    return jax.shard_map(
        per_device,
        mesh=mesh,
        in_specs=placed,
        out_specs=(P("grp", None, "slab", None, None), P("slab", "grp", None)),
        check_vma=False,
    )
```

time: 196 us -> 68.8 us (0.35)
  waiting for transfers between devices: 88 us -> 23.7 us
  other arithmetic: 29.4 us -> 0.05 us
  blocking collectives: 24.6 us -> 0 us
  Pallas kernels: 0 us -> 22.5 us
  local copies, waits for them, and re-layouts: 22.4 us -> 3.47 us
  between operations: 15.9 us -> 2.17 us
  starting transfers between devices: 14.7 us -> 16.8 us
    reduce_scatter x1 -> x0, waiting for transfers between devices: 48.9 us -> none  [per_device(): lax.psum_scatter(filter_xy(total).reshape(depth, nblock, block_rows, widt...]
    all_gather x1 -> x0, blocking collectives: 24.6 us -> none  [per_device(): owned = lax.all_gather(density, 'grp', axis=1, tiled=True)]
    pallas_call x0 -> x17, Pallas kernels: none -> 22.5 us  [call(): pl.pallas_call(kernel, out_shape=outs, in_specs=specs, out_specs=out_spec...]
    ppermute x8 -> x16, waiting for transfers between devices: 39.1 us -> 23.7 us  [swap_over(): lax.ppermute(array, axis, [(i, i ^ mask) for i in range(lax.axis_size(axi...]
    add x7 -> x0, other arithmetic: 10 us -> none  [the longest x4 5.87 us: per_device(): ez = ez + coef * (bwd_diff(hy, 2) - bwd_diff(hx, 3)) + drive]
    another operation x19 -> x1, local copies, waits for them, and re-layouts: 8.02 us -> 1.27 us  [per_device(): jnp.stack([(slab < nslab - 1).astype(jnp.int32), (slab > 0).astype(jnp.in...]
    unnamed x57 -> x8, local copies, waits for them, and re-layouts: 6.87 us -> 0.78 us
    sub x5 -> x0, other arithmetic: 5.31 us -> none  [the longest x4 5.18 us: per_device(): hx = hx - COURANT * (fwd_diff(ez, 3) - above_diff(ey, upper[1]))]
  transfers between devices with their start and end apart: 9 -> 16, of which waited for: 8 -> 8; matrix products, arithmetic and copies ran while one was open for 12% -> 4% of each run, Pallas kernels for 0% -> 24%
where the time goes in v1:
time: 68.8 us; the launch traced here: 68.6 us
  waiting for transfers between devices  23.7 us (34%)
  Pallas kernels  22.5 us (33%)
  starting transfers between devices  16.8 us (24%)
  local copies, waits for them, and re-layouts  3.47 us (5%)
  between operations  2.17 us (3%)
    ppermute x16, waiting for transfers between devices, swap_over(): lax.ppermute(array, axis, [(i, i ^ mask) for i in range(lax.axis_size(axi...  23.7 us
    pallas_call x17, Pallas kernels, call(): pl.pallas_call(kernel, out_shape=outs, in_specs=specs, out_specs=out_spec...  22.5 us
    ppermute x16, starting transfers between devices, swap_over(): lax.ppermute(array, axis, [(i, i ^ mask) for i in range(lax.axis_size(axi...  16.8 us
    slice x1, local copies, waits for them, and re-layouts, per_device(): source_pos[0, 2]  1.42 us
  transfers between devices with their start and end apart: 16, of which 8 were waited for; matrix products, arithmetic and copies ran while one was open for 4% of the time, Pallas kernels for 24%

profile of v1, /device:TPU:0, one launch (start us, length us, event | category | flops | bytes accessed | tf_op | source)
XLA Modules:
  0.0 68.6 jit_solution(17715964868041381457)
XLA Ops:
  0.6 5.1 %collective-permute-start.2 = (f32[64,128]{1,0:T(8,128)}, f32[64,128]{1,0:T(8,128)S(1)}, u32[]{:S(2)}, u32[]{:S(2)}) collective-permute-start(f32[64,128]{1,0:T(8,128)} %bitcast.10), channel_id=1, source_target_pairs={{0,24},{2,26},{4,28},{6,30},{8,16},{10,18},{12,20},{14,22},{16,8},... | collective-permute-start | bytes 98312 | tf_op jit(solution)/shard_map/ppermute | solution.py:377
  5.7 0.6 collective-permute-start
  6.4 1.4 %fusion = (s32[1,1]{1,0:T(1,128)}, s32[1,1]{1,0:T(1,128)}, s32[1,1]{1,0:T(1,128)}) fusion(s32[1,3]{1,0:T(1,128)} %param.14), kind=kLoop, calls=%fused_computation.1 | loop fusion | bytes 24 | tf_op jit(solution)/shard_map/slice | solution.py:410
  8.4 2.3 %collective-permute-done.1.refs_2_ = f32[64,128]{1,0:T(8,128)S(1)} collective-permute-done((f32[64,128]{1,0:T(8,128)}, f32[64,128]{1,0:T(8,128)S(1)}, u32[]{:S(2)}, u32[]{:S(2)}) %collective-permute-start.1) | collective-permute-done | bytes 32800 | tf_op jit(solution)/shard_map/ppermute | solution.py:377
  10.8 0.8 %copy-done = f32[8,8,128]{2,1,0:T(8,128)S(1)} copy-done((f32[8,8,128]{2,1,0:T(8,128)S(1)}, f32[8,8,128]{2,1,0:T(8,128)}, u32[]{:S(2)}) %copy-start) | copy-done | bytes 32792
  11.5 1.6 %collective-permute-start.3 = (f32[4,64,128]{2,1,0:T(8,128)S(1)}, f32[4,64,128]{2,1,0:T(8,128)S(1)}, u32[]{:S(2)}, u32[]{:S(2)}) collective-permute-start(f32[4,64,128]{2,1,0:T(8,128)S(1)} %shard_map.97.refs_0_), channel_id=1, source_target_pairs={{0,4},{2,6},{4,0},{6,2},{8,12},{10,14},{12,8},{14,10},{16,20},{18,... | collective-permute-start | bytes 393224 | tf_op jit(solution)/shard_map/ppermute | solution.py:377
  13.1 1.3 %stack.27.ints.refs_7_ = s32[6]{0:T(128)S(1)} concatenate(s32[1]{0:T(128)} %bitcast, s32[1]{0:T(128)} %bitcast.1, s32[1]{0:T(128)} %bitcast.2, s32[1]{0:T(128)} %bitcast.4, s32[1]{0:T(128)} %bitcast.5, s32[1]{0:T(128)} %bitcast.6), dimensions={0} | concatenate | bytes 48 | tf_op jit(solution)/shard_map/stack | solution.py:403
  14.4 3.6 %shard_map.95 = (f32[2,6,8,144,128]{4,3,2,1,0:T(8,128)S(1)}, f32[8,144,128]{2,1,0:T(8,128)S(1)}, f32[128,128]{1,0:T(8,128)S(1)}, f32[2,2,128,128]{3,2,1,0:T(8,128)S(1)}) custom-call(f32[1,6,8,128,128]{4,3,2,1,0:T(8,128)} %fwd.1, f32[1,6,8,128,128]{4,3,2,1,0:T(8,128)} %adj.1, s32[6]{0:T(128)S(1)} %stack.27.ints.refs_7_), custom_call_target="tpu_custom_call" | custom-call | tf_op jit(solution)/shard_map/pallas_call | solution.py:35
  18.0 1.6 %collective-permute-start.6 = (f32[2,2,128,128]{3,2,1,0:T(8,128)S(1)}, f32[2,2,128,128]{3,2,1,0:T(8,128)S(1)}, u32[]{:S(2)}, u32[]{:S(2)}) collective-permute-start(f32[2,2,128,128]{3,2,1,0:T(8,128)S(1)} %get-tuple-element.40), channel_id=1, source_target_pairs={{0,1},{1,0},{2,3},{3,2},{4,5},{5,4},{6,7},{7,6},{8,9},{9,8},{10,11... | collective-permute-start | bytes 786440 | tf_op jit(solution)/shard_map/ppermute | solution.py:377
  20.7 1.0 %shard_map.96.state_in = f32[2,6,8,144,128]{4,3,2,1,0:T(8,128)S(1)} custom-call(f32[2,6,8,144,128]{4,3,2,1,0:T(8,128)S(1)} %get-tuple-element.35.state_in), custom_call_target="tpu_custom_call", output_to_operand_aliasing={{}: (0, {})} | custom-call | tf_op jit(solution)/shard_map/pallas_call | solution.py:35
  21.9 1.6 %shard_map.98.coef = f32[8,128,128]{2,1,0:T(8,128)S(1)} custom-call(f32[4,64,128]{2,1,0:T(8,128)S(1)} %shard_map.97.refs_0_, f32[4,64,128]{2,1,0:T(8,128)S(1)} %collective-permute-done.3.refs_1_, f32[4,64,128]{2,1,0:T(8,128)S(1)} %collective-permute-done.4.refs_2_, f32[4,64,128]{2,1,0:T(8,128)S(1)} %collective-permute-done.5.refs_3_, s32[16]{0:T(128)S(1)} %copy-done.1, ...), custom_call_target="tpu_custom_call" | custom-call | tf_op jit(solution)/shard_map/pallas_call | solution.py:35
  23.5 1.6 %shard_map.99 = (f32[2,6,8,144,128]{4,3,2,1,0:T(8,128)S(1)}, f32[8,144,128]{2,1,0:T(8,128)S(1)}) custom-call(f32[2,6,8,144,128]{4,3,2,1,0:T(8,128)S(1)} %shard_map.96.state_in, f32[8,144,128]{2,1,0:T(8,128)S(1)} %get-tuple-element.36.total_in, f32[8,128,128]{2,1,0:T(8,128)S(1)} %shard_map.98.coef, ...), custom_call_target="tpu_custom_call", output_to_operand_aliasing={{0}: (0, {}), {1}: (1, {})} | custom-call | tf_op jit(solution)/shard_map/pallas_call | solution.py:35
  25.2 1.0 %shard_map.100 = (f32[2,6,8,144,128]{4,3,2,1,0:T(8,128)S(1)}, f32[8,144,128]{2,1,0:T(8,128)S(1)}, f32[2,2,128,128]{3,2,1,0:T(8,128)S(1)}) custom-call(f32[2,6,8,144,128]{4,3,2,1,0:T(8,128)S(1)} %get-tuple-element.38.state_in, f32[8,144,128]{2,1,0:T(8,128)S(1)} %get-tuple-element.39.total_in, ...), custom_call_target="tpu_custom_call", output_to_operand_aliasing={{0}: (0, {}), {1}: (1, {})} | custom-call | tf_op jit(solution)/shard_map/pallas_call | solution.py:35
  26.2 0.8 %collective-permute-start.7 = (f32[2,2,128,128]{3,2,1,0:T(8,128)S(1)}, f32[2,2,128,128]{3,2,1,0:T(8,128)S(1)}, u32[]{:S(2)}, u32[]{:S(2)}) collective-permute-start(f32[2,2,128,128]{3,2,1,0:T(8,128)S(1)} %get-tuple-element.45), channel_id=1, source_target_pairs={{0,1},{1,0},{2,3},{3,2},{4,5},{5,4},{6,7},{7,6},{8,9},{9,8},{10,11... | collective-permute-start | bytes 786440 | tf_op jit(solution)/shard_map/ppermute | solution.py:377
  27.0 2.4 %shard_map.101 = (f32[2,6,8,144,128]{4,3,2,1,0:T(8,128)S(1)}, f32[8,144,128]{2,1,0:T(8,128)S(1)}) custom-call(f32[2,6,8,144,128]{4,3,2,1,0:T(8,128)S(1)} %get-tuple-element.41.state_in, f32[8,144,128]{2,1,0:T(8,128)S(1)} %get-tuple-element.42.total_in, f32[8,128,128]{2,1,0:T(8,128)S(1)} %shard_map.98.coef, ...), custom_call_target="tpu_custom_call", output_to_operand_aliasing={{0}: (0, {}), {1}: (1, {})} | custom-call | tf_op jit(solution)/shard_map/pallas_call | solution.py:35
  29.3 5.1 %collective-permute-done.7.rest_0_ = f32[2,2,128,128]{3,2,1,0:T(8,128)S(1)} collective-permute-done((f32[2,2,128,128]{3,2,1,0:T(8,128)S(1)}, f32[2,2,128,128]{3,2,1,0:T(8,128)S(1)}, u32[]{:S(2)}, u32[]{:S(2)}) %collective-permute-start.7) | collective-permute-done | bytes 262176 | tf_op jit(solution)/shard_map/ppermute | solution.py:377
  34.4 1.0 %shard_map.102 = (f32[2,6,8,144,128]{4,3,2,1,0:T(8,128)S(1)}, f32[8,144,128]{2,1,0:T(8,128)S(1)}, f32[2,2,128,128]{3,2,1,0:T(8,128)S(1)}) custom-call(f32[2,6,8,144,128]{4,3,2,1,0:T(8,128)S(1)} %get-tuple-element.43.state_in, f32[8,144,128]{2,1,0:T(8,128)S(1)} %get-tuple-element.44.total_in, ...), custom_call_target="tpu_custom_call", output_to_operand_aliasing={{0}: (0, {}), {1}: (1, {})} | custom-call | tf_op jit(solution)/shard_map/pallas_call | solution.py:35
  36.0 2.4 %shard_map.103 = (f32[2,6,8,144,128]{4,3,2,1,0:T(8,128)S(1)}, f32[8,144,128]{2,1,0:T(8,128)S(1)}) custom-call(f32[2,6,8,144,128]{4,3,2,1,0:T(8,128)S(1)} %get-tuple-element.46.state_in, f32[8,144,128]{2,1,0:T(8,128)S(1)} %get-tuple-element.47.total_in, f32[8,128,128]{2,1,0:T(8,128)S(1)} %shard_map.98.coef, ...), custom_call_target="tpu_custom_call", output_to_operand_aliasing={{0}: (0, {}), {1}: (1, {})} | custom-call | tf_op jit(solution)/shard_map/pallas_call | solution.py:35
  38.4 4.5 %collective-permute-done.8.rest_0_ = f32[2,2,128,128]{3,2,1,0:T(8,128)S(1)} collective-permute-done((f32[2,2,128,128]{3,2,1,0:T(8,128)S(1)}, f32[2,2,128,128]{3,2,1,0:T(8,128)S(1)}, u32[]{:S(2)}, u32[]{:S(2)}) %collective-permute-start.8) | collective-permute-done | bytes 262176 | tf_op jit(solution)/shard_map/ppermute | solution.py:377
  42.8 1.0 %shard_map.104 = (f32[2,6,8,144,128]{4,3,2,1,0:T(8,128)S(1)}, f32[8,144,128]{2,1,0:T(8,128)S(1)}, f32[2,2,128,128]{3,2,1,0:T(8,128)S(1)}) custom-call(f32[2,6,8,144,128]{4,3,2,1,0:T(8,128)S(1)} %get-tuple-element.48.state_in, f32[8,144,128]{2,1,0:T(8,128)S(1)} %get-tuple-element.49.total_in, ...), custom_call_target="tpu_custom_call", output_to_operand_aliasing={{0}: (0, {}), {1}: (1, {})} | custom-call | tf_op jit(solution)/shard_map/pallas_call | solution.py:35
  44.2 2.4 %shard_map.105 = (f32[2,6,8,144,128]{4,3,2,1,0:T(8,128)S(1)}, f32[8,144,128]{2,1,0:T(8,128)S(1)}) custom-call(f32[2,6,8,144,128]{4,3,2,1,0:T(8,128)S(1)} %get-tuple-element.51.state_in, f32[8,144,128]{2,1,0:T(8,128)S(1)} %get-tuple-element.52.total_in, f32[8,128,128]{2,1,0:T(8,128)S(1)} %shard_map.98.coef, ...), custom_call_target="tpu_custom_call", output_to_operand_aliasing={{0}: (0, {}), {1}: (1, {})} | custom-call | tf_op jit(solution)/shard_map/pallas_call | solution.py:35
  46.5 3.8 %collective-permute-done.9.rest_0_ = f32[2,2,128,128]{3,2,1,0:T(8,128)S(1)} collective-permute-done((f32[2,2,128,128]{3,2,1,0:T(8,128)S(1)}, f32[2,2,128,128]{3,2,1,0:T(8,128)S(1)}, u32[]{:S(2)}, u32[]{:S(2)}) %collective-permute-start.9) | collective-permute-done | bytes 262176 | tf_op jit(solution)/shard_map/ppermute | solution.py:377
  50.3 0.9 %shard_map.106 = (f32[2,6,8,144,128]{4,3,2,1,0:T(8,128)S(1)}, f32[8,144,128]{2,1,0:T(8,128)S(1)}) custom-call(f32[2,6,8,144,128]{4,3,2,1,0:T(8,128)S(1)} %get-tuple-element.53.state_in, f32[8,144,128]{2,1,0:T(8,128)S(1)} %get-tuple-element.54.total_in, f32[8,128,128]{2,1,0:T(8,128)S(1)} %shard_map.98.coef, ...), custom_call_target="tpu_custom_call", output_to_operand_aliasing={{0}: (0, {}), {1}: (1, {})} | custom-call | tf_op jit(solution)/shard_map/pallas_call | solution.py:35
  51.2 1.4 %shard_map.108 = (f32[4,64,128]{2,1,0:T(8,128)S(1)}, f32[4,64,128]{2,1,0:T(8,128)S(1)}, f32[4,64,128]{2,1,0:T(8,128)S(1)}, f32[4,64,128]{2,1,0:T(8,128)S(1)}) custom-call(f32[8,144,128]{2,1,0:T(8,128)S(1)} %get-tuple-element.57.total, s32[16]{0:T(128)S(1)} %copy-done.1, s32[6]{0:T(128)S(1)} %stack.27.ints.refs_7_), custom_call_target="tpu_custom_call" | custom-call | tf_op jit(solution)/shard_map/pallas_call | solution.py:35
  53.2 0.8 %collective-permute-done.10.refs_2_ = f32[4,64,128]{2,1,0:T(8,128)S(1)} collective-permute-done((f32[4,64,128]{2,1,0:T(8,128)S(1)}, f32[4,64,128]{2,1,0:T(8,128)S(1)}, u32[]{:S(2)}, u32[]{:S(2)}) %collective-permute-start.10) | collective-permute-done | bytes 131104 | tf_op jit(solution)/shard_map/ppermute | solution.py:377
  54.3 0.6 collective-permute-start.12
  54.9 5.2 %collective-permute-done.12.refs_1_ = f32[4,64,128]{2,1,0:T(8,128)S(1)} collective-permute-done((f32[4,64,128]{2,1,0:T(8,128)S(1)}, f32[4,64,128]{2,1,0:T(8,128)S(1)}, u32[]{:S(2)}, u32[]{:S(2)}) %collective-permute-start.12) | collective-permute-done | bytes 131104 | tf_op jit(solution)/shard_map/ppermute | solution.py:377
  60.2 2.1 %collective-permute-start.14 = (f32[64,128]{1,0:T(8,128)S(1)}, f32[64,128]{1,0:T(8,128)S(1)}, u32[]{:S(2)}, u32[]{:S(2)}) collective-permute-start(f32[64,128]{1,0:T(8,128)S(1)} %get-tuple-element.66), channel_id=1, source_target_pairs={{0,16},{2,18},{4,20},{6,22},{8,24},{10,26},{12,28},{14,30},{16,0},... | collective-permute-start | bytes 98312 | tf_op jit(solution)/shard_map/ppermute | solution.py:377
  62.2 2.3 %collective-permute-start.15 = (f32[64,128]{1,0:T(8,128)S(1)}, f32[64,128]{1,0:T(8,128)S(1)}, u32[]{:S(2)}, u32[]{:S(2)}) collective-permute-start(f32[64,128]{1,0:T(8,128)S(1)} %get-tuple-element.67), channel_id=1, source_target_pairs={{0,24},{2,26},{4,28},{6,30},{8,16},{10,18},{12,20},{14,22},{16,8},... | collective-permute-start | bytes 98312 | tf_op jit(solution)/shard_map/ppermute | solution.py:377
  64.5 1.7 %shard_map.107 = f32[1,6,8,128,128]{4,3,2,1,0:T(8,128)} custom-call(f32[2,6,8,144,128]{4,3,2,1,0:T(8,128)S(1)} %get-tuple-element.56.state), custom_call_target="tpu_custom_call" | custom-call | tf_op jit(solution)/shard_map/pallas_call | solution.py:35
  66.3 1.7 %collective-permute-done.15.refs_3_ = f32[64,128]{1,0:T(8,128)S(1)} collective-permute-done((f32[64,128]{1,0:T(8,128)S(1)}, f32[64,128]{1,0:T(8,128)S(1)}, u32[]{:S(2)}, u32[]{:S(2)}) %collective-permute-start.15) | collective-permute-done | bytes 32800 | tf_op jit(solution)/shard_map/ppermute | solution.py:377
  68.0 0.6 shard_map.111
  (28 shorter events, 2.4 us)
Async XLA Ops:
  0.6 7.8 %collective-permute-start.2 = (f32[64,128]{1,0:T(8,128)}, f32[64,128]{1,0:T(8,128)S(1)}, u32[]{:S(2)}, u32[]{:S(2)}) collective-permute-start(f32[64,128]{1,0:T(8,128)} %bitcast.10), channel_id=1, source_target_pairs={{0,24},{2,26},{4,28},{6,30},{8,16},{10,18},{12,20},{14,22},{16,8},... | collective-permute-start | bytes 98312 | tf_op jit(solution)/shard_map/ppermute | solution.py:377
  5.7 5.0 %collective-permute-start.1 = (f32[64,128]{1,0:T(8,128)}, f32[64,128]{1,0:T(8,128)S(1)}, u32[]{:S(2)}, u32[]{:S(2)}) collective-permute-start(f32[64,128]{1,0:T(8,128)} %bitcast.11), channel_id=1, source_target_pairs={{0,16},{2,18},{4,20},{6,22},{8,24},{10,26},{12,28},{14,30},{16,0},... | collective-permute-start | bytes 98312 | tf_op jit(solution)/shard_map/ppermute | solution.py:377
  5.7 5.0 %collective-permute-start = (f32[64,128]{1,0:T(8,128)}, f32[64,128]{1,0:T(8,128)S(1)}, u32[]{:S(2)}, u32[]{:S(2)}) collective-permute-start(f32[64,128]{1,0:T(8,128)} %bitcast.12), channel_id=1, source_target_pairs={{0,8},{2,10},{4,12},{6,14},{8,0},{10,2},{12,4},{14,6},{16,24},{18,... | collective-permute-start | bytes 98312 | tf_op jit(solution)/shard_map/ppermute | solution.py:377
  10.8 0.8 %copy-start = (f32[8,8,128]{2,1,0:T(8,128)S(1)}, f32[8,8,128]{2,1,0:T(8,128)}, u32[]{:S(2)}) copy-start(f32[8,8,128]{2,1,0:T(8,128)} %param.10) | copy-start | bytes 98308
  11.5 8.0 %collective-permute-start.3 = (f32[4,64,128]{2,1,0:T(8,128)S(1)}, f32[4,64,128]{2,1,0:T(8,128)S(1)}, u32[]{:S(2)}, u32[]{:S(2)}) collective-permute-start(f32[4,64,128]{2,1,0:T(8,128)S(1)} %shard_map.97.refs_0_), channel_id=1, source_target_pairs={{0,4},{2,6},{4,0},{6,2},{8,12},{10,14},{12,8},{14,10},{16,20},{18,... | collective-permute-start | bytes 393224 | tf_op jit(solution)/shard_map/ppermute | solution.py:377
  18.0 7.2 %collective-permute-start.6 = (f32[2,2,128,128]{3,2,1,0:T(8,128)S(1)}, f32[2,2,128,128]{3,2,1,0:T(8,128)S(1)}, u32[]{:S(2)}, u32[]{:S(2)}) collective-permute-start(f32[2,2,128,128]{3,2,1,0:T(8,128)S(1)} %get-tuple-element.40), channel_id=1, source_target_pairs={{0,1},{1,0},{2,3},{3,2},{4,5},{5,4},{6,7},{7,6},{8,9},{9,8},{10,11... | collective-permute-start | bytes 786440 | tf_op jit(solution)/shard_map/ppermute | solution.py:377
  19.5 2.3 %collective-permute-start.4 = (f32[4,64,128]{2,1,0:T(8,128)S(1)}, f32[4,64,128]{2,1,0:T(8,128)S(1)}, u32[]{:S(2)}, u32[]{:S(2)}) collective-permute-start(f32[4,64,128]{2,1,0:T(8,128)S(1)} %shard_map.97.refs_0_), channel_id=1, source_target_pairs={{0,2},{2,0},{4,6},{6,4},{8,10},{10,8},{12,14},{14,12},{16,18},{18,... | collective-permute-start | bytes 393224 | tf_op jit(solution)/shard_map/ppermute | solution.py:377
  19.6 2.3 %collective-permute-start.5 = (f32[4,64,128]{2,1,0:T(8,128)S(1)}, f32[4,64,128]{2,1,0:T(8,128)S(1)}, u32[]{:S(2)}, u32[]{:S(2)}) collective-permute-start(f32[4,64,128]{2,1,0:T(8,128)S(1)} %collective-permute-done.3.refs_1_), channel_id=1, source_target_pairs={{0,2},{2,0},{4,6},{6,4},{8,10},{10,8},{12,14},{14,12},{16,18},{18,... | collective-permute-start | bytes 393224 | tf_op jit(solution)/shard_map/ppermute | solution.py:377
  20.7 1.1 %copy-start.1 = (s32[16]{0:T(128)S(1)}, s32[16]{0:T(128)}, u32[]{:S(2)}) copy-start(s32[16]{0:T(128)} %block_ids.1) | copy-start | bytes 196
  20.7 1.1 %copy-start.2 = (s32[16]{0:T(128)S(1)}, s32[16]{0:T(128)}, u32[]{:S(2)}) copy-start(s32[16]{0:T(128)} %refs_5_.1) | copy-start | bytes 196
  20.7 1.1 %copy-start.3 = (f32[4]{0:T(128)S(1)}, f32[4]{0:T(128)}, u32[]{:S(2)}) copy-start(f32[4]{0:T(128)} %refs_6_.1) | copy-start | bytes 52
  26.2 8.3 %collective-permute-start.7 = (f32[2,2,128,128]{3,2,1,0:T(8,128)S(1)}, f32[2,2,128,128]{3,2,1,0:T(8,128)S(1)}, u32[]{:S(2)}, u32[]{:S(2)}) collective-permute-start(f32[2,2,128,128]{3,2,1,0:T(8,128)S(1)} %get-tuple-element.45), channel_id=1, source_target_pairs={{0,1},{1,0},{2,3},{3,2},{4,5},{5,4},{6,7},{7,6},{8,9},{9,8},{10,11... | collective-permute-start | bytes 786440 | tf_op jit(solution)/shard_map/ppermute | solution.py:377
  35.4 7.4 %collective-permute-start.8 = (f32[2,2,128,128]{3,2,1,0:T(8,128)S(1)}, f32[2,2,128,128]{3,2,1,0:T(8,128)S(1)}, u32[]{:S(2)}, u32[]{:S(2)}) collective-permute-start(f32[2,2,128,128]{3,2,1,0:T(8,128)S(1)} %get-tuple-element.50), channel_id=1, source_target_pairs={{0,1},{1,0},{2,3},{3,2},{4,5},{5,4},{6,7},{7,6},{8,9},{9,8},{10,11... | collective-permute-start | bytes 786440 | tf_op jit(solution)/shard_map/ppermute | solution.py:377
  43.8 6.5 %collective-permute-start.9 = (f32[2,2,128,128]{3,2,1,0:T(8,128)S(1)}, f32[2,2,128,128]{3,2,1,0:T(8,128)S(1)}, u32[]{:S(2)}, u32[]{:S(2)}) collective-permute-start(f32[2,2,128,128]{3,2,1,0:T(8,128)S(1)} %get-tuple-element.55), channel_id=1, source_target_pairs={{0,1},{1,0},{2,3},{3,2},{4,5},{5,4},{6,7},{7,6},{8,9},{9,8},{10,11... | collective-permute-start | bytes 786440 | tf_op jit(solution)/shard_map/ppermute | solution.py:377
  52.6 1.4 %collective-permute-start.10 = (f32[4,64,128]{2,1,0:T(8,128)S(1)}, f32[4,64,128]{2,1,0:T(8,128)S(1)}, u32[]{:S(2)}, u32[]{:S(2)}) collective-permute-start(f32[4,64,128]{2,1,0:T(8,128)S(1)} %get-tuple-element.60), channel_id=1, source_target_pairs={{0,2},{2,0},{4,6},{6,4},{8,10},{10,8},{12,14},{14,12},{16,18},{18,... | collective-permute-start | bytes 393224 | tf_op jit(solution)/shard_map/ppermute | solution.py:377
  52.7 1.5 %collective-permute-start.11 = (f32[4,64,128]{2,1,0:T(8,128)S(1)}, f32[4,64,128]{2,1,0:T(8,128)S(1)}, u32[]{:S(2)}, u32[]{:S(2)}) collective-permute-start(f32[4,64,128]{2,1,0:T(8,128)S(1)} %get-tuple-element.61), channel_id=1, source_target_pairs={{0,2},{2,0},{4,6},{6,4},{8,10},{10,8},{12,14},{14,12},{16,18},{18,... | collective-permute-start | bytes 393224 | tf_op jit(solution)/shard_map/ppermute | solution.py:377
  54.3 5.8 %collective-permute-start.12 = (f32[4,64,128]{2,1,0:T(8,128)S(1)}, f32[4,64,128]{2,1,0:T(8,128)S(1)}, u32[]{:S(2)}, u32[]{:S(2)}) collective-permute-start(f32[4,64,128]{2,1,0:T(8,128)S(1)} %get-tuple-element.63), channel_id=1, source_target_pairs={{0,4},{2,6},{4,0},{6,2},{8,12},{10,14},{12,8},{14,10},{16,20},{18,... | collective-permute-start | bytes 393224 | tf_op jit(solution)/shard_map/ppermute | solution.py:377
  60.1 6.2 %collective-permute-start.13 = (f32[64,128]{1,0:T(8,128)S(1)}, f32[64,128]{1,0:T(8,128)S(1)}, u32[]{:S(2)}, u32[]{:S(2)}) collective-permute-start(f32[64,128]{1,0:T(8,128)S(1)} %get-tuple-element.65), channel_id=1, source_target_pairs={{0,8},{2,10},{4,12},{6,14},{8,0},{10,2},{12,4},{14,6},{16,24},{18,... | collective-permute-start | bytes 98312 | tf_op jit(solution)/shard_map/ppermute | solution.py:377
  60.2 6.1 %collective-permute-start.14 = (f32[64,128]{1,0:T(8,128)S(1)}, f32[64,128]{1,0:T(8,128)S(1)}, u32[]{:S(2)}, u32[]{:S(2)}) collective-permute-start(f32[64,128]{1,0:T(8,128)S(1)} %get-tuple-element.66), channel_id=1, source_target_pairs={{0,16},{2,18},{4,20},{6,22},{8,24},{10,26},{12,28},{14,30},{16,0},... | collective-permute-start | bytes 98312 | tf_op jit(solution)/shard_map/ppermute | solution.py:377
  62.2 5.7 %collective-permute-start.15 = (f32[64,128]{1,0:T(8,128)S(1)}, f32[64,128]{1,0:T(8,128)S(1)}, u32[]{:S(2)}, u32[]{:S(2)}) collective-permute-start(f32[64,128]{1,0:T(8,128)S(1)} %get-tuple-element.67), channel_id=1, source_target_pairs={{0,24},{2,26},{4,28},{6,30},{8,16},{10,18},{12,20},{14,22},{16,8},... | collective-permute-start | bytes 98312 | tf_op jit(solution)/shard_map/ppermute | solution.py:377

commit v2 on v1

v2 whole, which is shorter than its diff:
```python
import functools
import math

import jax
import jax.numpy as jnp
from jax import lax
from jax.experimental import pallas as pl
from jax.experimental.pallas import tpu as pltpu
from jax.sharding import PartitionSpec as P

STEPS = 4
AMPLITUDE = 4.0
PAD = 8
F32 = jnp.float32

VMEM = pltpu.MemorySpace.VMEM
IN_VMEM = pl.BlockSpec(memory_space=pltpu.VMEM)
IN_SMEM = pl.BlockSpec(memory_space=pltpu.SMEM)
IN_HBM = pl.BlockSpec(memory_space=pltpu.MemorySpace.HBM)


def on_chip(*shape):
    return VMEM(shape, F32)


def held(array, spec):
    if spec is IN_SMEM:
        return array
    space = VMEM if spec is IN_VMEM else pltpu.MemorySpace.HBM
    return pltpu.with_memory_space_constraint(array, space)


def call(kernel, outs, out_specs, operands, specs, scratch=(), aliases=None, flops=0):
    operands = [held(a, s) for a, s in zip(operands, specs)]
    return pl.pallas_call(
        kernel,
        out_shape=outs,
        in_specs=specs,
        out_specs=out_specs,
        scratch_shapes=scratch,
        input_output_aliases=aliases or {},
        compiler_params=pltpu.CompilerParams(vmem_limit_bytes=8 << 20),
        cost_estimate=pl.CostEstimate(flops=flops, bytes_accessed=flops // 4, transcendentals=0),
    )(*operands)


TOP_ALONE, BOTTOM_ALONE, ABOVE, BELOW, UNDER, SPARE = range(6)
EXTRA = 6
CHUNK = 16


def chunks(rows):
    size = CHUNK if rows % CHUNK == 0 else rows
    return [(first, size) for first in range(0, rows, size)]


def next_col(value):
    column = lax.broadcasted_iota(jnp.int32, value.shape, 1)
    moved = pltpu.roll(value, value.shape[1] - 1, 1)
    return jnp.where(column == value.shape[1] - 1, 0.0, moved)


def prev_col(value):
    column = lax.broadcasted_iota(jnp.int32, value.shape, 1)
    return jnp.where(column == 0, 0.0, pltpu.roll(value, 1, 1))


class Window:
    def __init__(self, state, coef=None, total=None, source=None, drives=None, profile=None):
        self.state, self.coef, self.total = state, coef, total
        self.source, self.drives, self.profile = source, drives, profile
        self.rows = state.shape[3] - 2 * PAD
        self.depth = state.shape[2] - EXTRA
        self.top = self.depth - 1
        self.slab = lax.axis_index("slab")
        self.has_up = self.slab < lax.axis_size("slab") - 1
        self.has_low = self.slab > 0

    def extra(self, which):
        return self.depth + which

    def read(self, evo, comp, layer, first, size, shift=0):
        return self.state[evo, comp, layer, pl.ds(PAD + first + shift, size), :]

    def write(self, evo, comp, layer, first, size, value):
        self.state[evo, comp, layer, pl.ds(PAD + first, size), :] = value

    def put_h(self, layer, upper, evos=(0, 1), e=None, h=None, flat=False):
        e = layer if e is None else e
        h = layer if h is None else h
        for evo in evos:
            for first, size in chunks(self.rows):
                ex, ey, ez = (self.read(evo, c, e, first, size) for c in range(3))
                if upper is None:
                    rise_x, rise_y = -ex, -ey
                else:
                    rise_x = self.read(evo, 0, upper, first, size) - ex
                    rise_y = self.read(evo, 1, upper, first, size) - ey
                ez_after = self.read(evo, 2, e, first, size, 1)
                hx = self.read(evo, 3, h, first, size) - ((next_col(ez) - ez) - rise_y)
                hy = self.read(evo, 4, h, first, size) - (rise_x - (ez_after - ez))
                self.write(evo, 3, layer, first, size, hx)
                self.write(evo, 4, layer, first, size, hy)
                if not flat:
                    ey_after = self.read(evo, 1, e, first, size, 1)
                    hz = self.read(evo, 5, h, first, size)
                    hz = hz - ((ey_after - ey) - (next_col(ex) - ex))
                    self.write(evo, 5, layer, first, size, hz)

    def curl_h(self, evo, h, lower, first, size):
        hx, hy, hz = (self.read(evo, c, h, first, size) for c in (3, 4, 5))
        if lower is None:
            step_x, step_y = hx, hy
        else:
            step_x = hx - self.read(evo, 3, lower, first, size)
            step_y = hy - self.read(evo, 4, lower, first, size)
        hy_before = self.read(evo, 4, h, first, size, -1)
        hz_before = self.read(evo, 5, h, first, size, -1)
        return (
            (hz - prev_col(hz)) - step_y,
            step_x - (hz - hz_before),
            (hy - hy_before) - (hx - prev_col(hx)),
        )

    def drive(self, step, layer, into=None):
        into = layer if into is None else into

        @pl.when(self.source[0, 0] - self.slab * self.depth == layer)
        def _():
            amount = self.drives[step]
            for first, size in chunks(self.rows):
                here = pl.ds(PAD + first, size)
                self.state[0, 2, into, here, :] += amount * self.profile[pl.ds(first, size), :]

    def put_e(self, layer, lower, step):
        self.drive(step, layer)
        for first, size in chunks(self.rows):
            cell = self.coef[layer, pl.ds(first, size), :]
            part = None
            news = []
            for evo in range(2):
                curl = self.curl_h(evo, layer, lower, first, size)
                news.append(
                    [self.read(evo, c, layer, first, size) + cell * curl[c] for c in range(3)]
                )
            for evo in range(2):
                for c in range(3):
                    self.write(evo, c, layer, first, size, news[evo][c])
            part = news[0][0] * news[1][0] + news[0][1] * news[1][1] + news[0][2] * news[1][2]
            self.total[layer, pl.ds(PAD + first, size), :] += part

    def put_e_of(self, out, e, h, lower, cell_layer):
        for evo in range(2):
            for first, size in chunks(self.rows):
                cell = self.coef[cell_layer, pl.ds(first, size), :]
                curl = self.curl_h(evo, h, lower, first, size)
                for c in range(3):
                    self.write(
                        evo, c, out, first, size, self.read(evo, c, e, first, size) + cell * curl[c]
                    )

    def lift_h(self, layer, edge, extra=None):
        for evo in range(2):
            for first, size in chunks(self.rows):
                here = pl.ds(first, size)
                ex, ey = edge[evo, 0, here, :], edge[evo, 1, here, :]
                if extra is not None:
                    ex = ex + self.read(evo, 0, extra, first, size)
                    ey = ey + self.read(evo, 1, extra, first, size)
                self.write(evo, 3, layer, first, size, self.read(evo, 3, layer, first, size) + ey)
                self.write(evo, 4, layer, first, size, self.read(evo, 4, layer, first, size) - ex)

    def spread(self, layer, e):
        for evo in range(2):
            for first, size in chunks(self.rows):
                self.write(evo, 3, layer, first, size, self.read(evo, 1, e, first, size))
                self.write(evo, 4, layer, first, size, -self.read(evo, 0, e, first, size))

    def set_under(self, edge):
        under, below = self.extra(UNDER), self.extra(BELOW)
        for evo in range(2):
            for c in range(2):
                for first, size in chunks(self.rows):
                    value = edge[evo, c, pl.ds(first, size), :]
                    value = value + self.read(evo, 3 + c, below, first, size)
                    self.write(evo, 3 + c, under, first, size, value)

    def send_h(self, pay, layer):
        for evo in range(2):
            for c in range(2):
                pay[evo, c] = self.state[evo, 3 + c, layer, pl.ds(PAD, self.rows), :]

    def send_e(self, pay, layer):
        for evo in range(2):
            for c in range(2):
                pay[evo, c] = self.state[evo, c, layer, pl.ds(PAD, self.rows), :]


def first_kernel(fwd, adj, state, total, *pays):
    win = Window(state)
    rows, width_y = win.rows, state.shape[4]
    edge = jnp.zeros((PAD, width_y), F32)

    def clear(layer, carry):
        for evo in range(2):
            for comp in range(6):
                state[evo, comp, layer, pl.ds(0, PAD), :] = edge
                state[evo, comp, layer, pl.ds(PAD + rows, PAD), :] = edge
        return carry

    lax.fori_loop(0, state.shape[2], clear, 0)
    for which in (ABOVE, BELOW, UNDER):
        for evo in range(2):
            for comp in range(6):
                state[evo, comp, win.extra(which)] = jnp.zeros((rows + 2 * PAD, width_y), F32)

    def copy(layer, carry):
        total[layer] = jnp.zeros((rows + 2 * PAD, width_y), F32)
        for evo, given in enumerate((fwd, adj)):
            for comp in range(6):
                for first, size in chunks(rows):
                    value = given[0, comp, layer, pl.ds(first, size), :]
                    win.write(evo, comp, layer, first, size, value + value if comp > 2 else value)
        return carry

    lax.fori_loop(0, win.depth, copy, 0)
    win.put_h(win.top, None)
    if len(pays) == 2:
        win.send_h(pays[0], win.top)
        win.send_e(pays[1], 0)
    else:
        pl.when(win.has_up)(lambda: win.send_h(pays[0], win.top))
        pl.when(win.has_low)(lambda: win.send_e(pays[0], 0))


def inner_kernel(state_in, source, state, profile):
    win = Window(state)
    rows, width_y = win.rows, state.shape[4]
    xcoord = lax.broadcasted_iota(jnp.int32, (rows, width_y), 0)
    ycoord = lax.broadcasted_iota(jnp.int32, (rows, width_y), 1)
    offset_x = (xcoord - source[0, 1]).astype(F32) / (rows / 4.0)
    offset_y = (ycoord - source[0, 2]).astype(F32) / (width_y / 4.0)
    profile[...] = jnp.exp(-0.5 * (offset_x * offset_x + offset_y * offset_y))

    def body(layer, carry):
        win.put_h(layer, layer + 1)
        return carry

    lax.fori_loop(0, win.top, body, 0)


def curl_kernel(state_in, from_below, from_above, state, curls):
    win = Window(state)
    pl.when(win.has_up)(lambda: win.lift_h(win.top, from_above))

    @pl.when(win.has_low)
    def _():
        win.spread(win.extra(BELOW), 0)
        win.set_under(from_below)

    def one(layer, lower):
        for evo in range(2):
            for first, size in chunks(win.rows):
                for c, value in enumerate(win.curl_h(evo, layer, lower, first, size)):
                    curls[evo, c, layer, pl.ds(first, size), :] = value

    def body(layer, carry):
        one(layer, layer - 1)
        return carry

    one(0, win.extra(UNDER))
    lax.fori_loop(1, win.depth, body, 0)


def coef_kernel(layout, count, depth, *refs):
    parts = refs[:count]
    block_ids, material_idx, material_eps, coef, blocks, placed, base = refs[count:]
    nblock = blocks.shape[0]
    rows, width_y = coef.shape[1:]
    block_rows = rows // nblock
    me = lax.axis_index("grp")
    for part, masks in zip(parts, layout):
        for slot, mask in enumerate(masks):
            blocks[block_ids[me ^ mask]] = part[slot]
    for block in range(nblock):
        level = jnp.full((block_rows, width_y), material_eps[material_idx[block]], F32)
        base[pl.ds(block * block_rows, block_rows), :] = level
    placed[pl.ds(0, PAD), :] = jnp.zeros((PAD, width_y), F32)
    placed[pl.ds(PAD + rows, PAD), :] = jnp.zeros((PAD, width_y), F32)

    def layer_of(layer, carry):
        for block in range(nblock):
            source = pl.ds(pl.multiple_of(layer * block_rows, block_rows), block_rows)
            placed[pl.ds(PAD + block * block_rows, block_rows), :] = blocks[block, source, :]
        for first, size in chunks(rows):
            here = pl.ds(first, size)
            smooth = filtered(placed, first, size)
            coef[layer, here, :] = 0.25 / (base[here, :] + 3.0 * smooth)
        return carry

    lax.fori_loop(0, depth, layer_of, 0)


def filtered(padded, first, size):
    here = padded[pl.ds(PAD + first, size), :]
    before = padded[pl.ds(PAD + first - 1, size), :]
    after = padded[pl.ds(PAD + first + 1, size), :]
    along = before + 2.0 * here + after
    return (prev_col(along) + 2.0 * along + next_col(along)) * 0.0625


def ahead_a_kernel(state_in, total_in, coef, curls, source, drives, profile, state, total, *pays):
    win = Window(state, coef, total, source, drives, profile)

    def body(layer, carry):
        win.drive(0, layer)
        for first, size in chunks(win.rows):
            here = pl.ds(first, size)
            cell = coef[layer, here, :]
            news = []
            for evo in range(2):
                news.append(
                    [
                        win.read(evo, c, layer, first, size) + cell * curls[evo, c, layer, here, :]
                        for c in range(3)
                    ]
                )
                for c in range(3):
                    win.write(evo, c, layer, first, size, news[evo][c])
            part = news[0][0] * news[1][0] + news[0][1] * news[1][1] + news[0][2] * news[1][2]
            total[layer, pl.ds(PAD + first, size), :] += part
        return carry

    lax.fori_loop(0, win.depth, body, 0)
    win.put_h(win.top, None)

    def up(pay, cells):
        win.send_h(pay, win.top)
        cells[...] = coef[win.top]

    def down(pay, cells):
        win.send_e(pay, 0)
        cells[...] = coef[0]

    half = len(pays) // 2
    if half == 2:
        up(pays[0], pays[2])
        down(pays[1], pays[3])
    else:
        pl.when(win.has_up)(lambda: up(*pays))
        pl.when(win.has_low)(lambda: down(*pays))


def ahead_b_kernel(state_in, coef, source, drives, profile, state, *pays):
    win = Window(state, coef, None, source, drives, profile)
    top = win.top
    win.put_h(top - 1, top)
    win.put_h(0, 1)

    def up(pay):
        alone = win.extra(TOP_ALONE)
        win.put_e_of(alone, top, top, top - 1, top)
        win.drive(1, top, alone)
        win.put_h(alone, None, h=top)
        win.send_h(pay, alone)

    def down(pay):
        alone = win.extra(BOTTOM_ALONE)
        win.put_e_of(alone, 0, 0, None, 0)
        win.drive(1, 0, alone)
        win.send_e(pay, alone)

    pl.when(win.has_up)(lambda: up(pays[0]))
    pl.when(win.has_low)(lambda: down(pays[-1]))


def ahead_c_kernel(state_in, total_in, coef, source, drives, profile, state, total, *pays):
    win = Window(state, coef, total, source, drives, profile)
    top = win.top
    win.put_h(top - 2, top - 1)
    win.put_h(1, 2)
    win.put_e(top - 1, top - 2, 1)
    win.put_e(1, 0, 1)

    def up(pay):
        alone, spare = win.extra(TOP_ALONE), win.extra(SPARE)
        win.put_h(spare, alone, e=top - 1, h=top - 1, flat=True)
        win.put_e_of(alone, alone, alone, spare, top)
        win.drive(2, top, alone)
        win.put_h(alone, None, flat=True)
        win.send_h(pay, alone)

    def down(pay):
        alone = win.extra(BOTTOM_ALONE)
        win.put_h(alone, 1, h=0)
        win.put_e_of(alone, alone, alone, None, 0)
        win.drive(2, 0, alone)
        win.send_e(pay, alone)

    pl.when(win.has_up)(lambda: up(pays[0]))
    pl.when(win.has_low)(lambda: down(pays[-1]))


def bulk_kernel(state_in, total_in, coef, source, drives, profile, state, total):
    win = Window(state, coef, total, source, drives, profile)
    top = win.top

    def sweep(step):
        def body(layer, carry):
            win.put_h(layer, layer + 1)
            win.put_e(layer, layer - 1, step)
            return carry

        return body

    lax.fori_loop(2, top - 2, sweep(1), 0)
    win.put_e(top - 2, top - 3, 1)
    win.put_h(1, 2)
    lax.fori_loop(2, top - 1, sweep(2), 0)
    win.put_h(2, 3)
    lax.fori_loop(3, top - 2, sweep(3), 0)


def behind_a_kernel(
    state_in, total_in, coef_in, below, above, below_cells, above_cells, source, drives, profile,
    state, total, coef,
):
    win = Window(state, coef, total, source, drives, profile)
    top, depth = win.top, win.depth

    @pl.when(win.has_up)
    def _():
        win.lift_h(top, above)
        coef[depth] = above_cells[...]

    @pl.when(win.has_low)
    def _():
        ghost = win.extra(BELOW)
        win.spread(ghost, 0)
        win.set_under(below)
        coef[depth + 1] = below_cells[...]
        for evo in range(2):
            for c in range(3):
                win.write(evo, c, ghost, 0, win.rows, jnp.zeros((win.rows, state.shape[4]), F32))
            win.write(evo, 5, ghost, 0, win.rows, jnp.zeros((win.rows, state.shape[4]), F32))
        win.put_e_of(ghost, ghost, ghost, None, depth + 1)

    win.put_e(top, top - 1, 1)
    win.put_e(0, win.extra(UNDER), 1)

    @pl.when(win.has_up)
    def _():
        ghost = win.extra(ABOVE)
        for evo in range(2):
            for first, size in chunks(win.rows):
                cell = coef[depth, pl.ds(first, size), :]
                win.write(evo, 0, ghost, first, size, cell * win.read(evo, 4, top, first, size))
                win.write(evo, 1, ghost, first, size, -cell * win.read(evo, 3, top, first, size))

    win.put_h(top - 1, top)
    win.put_h(top, None)
    win.put_h(0, 1)
    win.put_e(top - 1, top - 2, 2)
    win.put_e(1, 0, 2)


def behind_b_kernel(
    state_in, total_in, coef, below, above, source, drives, profile, state, total
):
    win = Window(state, coef, total, source, drives, profile)
    top, depth = win.top, win.depth

    @pl.when(win.has_up)
    def _():
        ghost = win.extra(ABOVE)
        win.lift_h(top, above, ghost)
        win.put_h(ghost, None)
        win.put_e_of(ghost, ghost, ghost, top, depth)

    @pl.when(win.has_low)
    def _():
        ghost, spare = win.extra(BELOW), win.extra(SPARE)
        win.put_h(ghost, 0)
        win.set_under(below)
        win.spread(spare, ghost)
        win.put_e_of(ghost, ghost, ghost, spare, depth + 1)

    win.put_e(top, top - 1, 2)
    win.put_e(0, win.extra(UNDER), 2)
    win.put_h(top - 1, top)
    win.put_h(top, None)
    win.put_h(top - 2, top - 1)
    win.put_h(0, 1)
    win.put_h(1, 2)
    win.put_e(top - 1, top - 2, 3)
    win.put_e(top - 2, top - 3, 3)
    win.put_e(1, 0, 3)
    win.put_e(2, 1, 3)


def behind_c_kernel(
    state_in, total_in, coef, below, above, source, drives, profile, state, total
):
    win = Window(state, coef, total, source, drives, profile)
    top = win.top
    pl.when(win.has_up)(lambda: win.lift_h(top, above, win.extra(ABOVE)))

    @pl.when(win.has_low)
    def _():
        win.put_h(win.extra(BELOW), 0, flat=True)
        win.set_under(below)

    win.put_e(top, top - 1, 3)
    win.put_e(0, win.extra(UNDER), 3)


def pack_kernel(*refs):
    out = refs[-1]
    for slot, ref in enumerate(refs[:-1]):
        out[slot] = ref[...]


def filter_kernel(layout, total, block_ids, *rest):
    parts, blocks, wide = rest[:-2], rest[-2], rest[-1]
    nblock = blocks.shape[0]
    depth = total.shape[0]
    rows = total.shape[1] - 2 * PAD
    block_rows = rows // nblock
    me = lax.axis_index("grp")

    def layer_of(layer, carry):
        for first, size in chunks(rows):
            wide[pl.ds(first, size), :] = filtered(total.at[layer], first, size)
        for block in range(nblock):
            target = pl.ds(pl.multiple_of(layer * block_rows, block_rows), block_rows)
            blocks[block, target, :] = wide[pl.ds(block * block_rows, block_rows), :]
        return carry

    lax.fori_loop(0, depth, layer_of, 0)
    for part, masks in zip(parts, layout):
        for slot, mask in enumerate(masks):
            part[slot] = blocks[block_ids[me ^ mask]]


def add_kernel(*refs):
    half = len(refs) // 3
    for a, b, out in zip(refs[:half], refs[half : 2 * half], refs[2 * half :]):
        out[...] = a[...] + b[...]


def add_split_kernel(count, *refs):
    terms, outs = refs[:count], refs[count:]
    for slot, out in enumerate(outs):
        value = terms[0][slot]
        for term in terms[1:]:
            value = value + term[slot]
        out[...] = value


def last_kernel(scale, *refs):
    value = refs[0][...]
    for ref in refs[1:-1]:
        value = value + ref[...]
    refs[-1][...] = value * scale


def out_kernel(state, finals, halves, sems):
    depth = state.shape[2] - EXTRA
    rows = state.shape[3] - 2 * PAD
    every = pl.ds(PAD, rows)
    copies = [
        pltpu.make_async_copy(
            state.at[0, comp, pl.ds(0, depth), every, :], finals.at[0, comp], sems.at[comp]
        )
        for comp in range(3)
    ]
    for copy in copies:
        copy.start()
    for comp in range(3):

        def body(layer, carry):
            halves[comp, layer] = 0.5 * state[0, 3 + comp, layer, every, :]
            return carry

        lax.fori_loop(0, depth, body, 0)
        copy = pltpu.make_async_copy(halves.at[comp], finals.at[0, 3 + comp], sems.at[3 + comp])
        copy.start()
        copies.append(copy)
    for copy in copies:
        copy.wait()


def swap_over(array, axis, mask):
    return lax.ppermute(array, axis, [(i, i ^ mask) for i in range(lax.axis_size(axis))])


def shift_over(array, axis, distance):
    size = lax.axis_size(axis)
    route = [(i, i + distance) for i in range(size) if 0 <= i + distance < size]
    return lax.ppermute(array, axis, route)


def trade(pays):
    if len(pays) == 1:
        return [swap_over(pays[0], "slab", 1)] * 2
    return [shift_over(pays[0], "slab", 1), shift_over(pays[1], "slab", -1)]


def per_device(
    fwd_fields, adj_fields, density, block_ids, material_idx, material_eps, source_pos, wave_idx
):
    depth, width_x, width_y = fwd_fields.shape[2:]
    nblock = block_ids.shape[0]
    block_rows = width_x // nblock
    ngrp = lax.axis_size("grp")
    npay = 1 if lax.axis_size("slab") == 2 else 2
    omega = 2.0 * math.pi / (6.0 + 2.0 * wave_idx[0].astype(F32))
    drives = AMPLITUDE * jnp.sin(omega * (jnp.arange(STEPS, dtype=F32) + 1.0))

    far = 4
    middle = ngrp // (2 * far)
    far_masks = [2 * middle * j for j in range(far)]
    middle_masks = [2 * j for j in range(middle)]
    layout = [
        [core + mid + top for top in far_masks] for core in (0, 1) for mid in middle_masks
    ]
    piece = (depth * block_rows, width_y)
    group = (far,) + piece

    state_shape = on_chip(2, 6, depth + EXTRA, width_x + 2 * PAD, width_y)
    total_shape = on_chip(depth, width_x + 2 * PAD, width_y)
    coef_shape = on_chip(depth + 2, width_x, width_y)
    plane = on_chip(width_x, width_y)
    pay_shape = on_chip(2, 2, width_x, width_y)

    own = density.reshape(piece)
    pieces = [own] + [swap_over(own, "grp", mask) for mask in far_masks[1:]]
    near = call(pack_kernel, on_chip(*group), IN_VMEM, pieces, [IN_VMEM] * far)
    parts = [near] + [swap_over(near, "grp", mask) for mask in middle_masks[1:]]
    parts = parts + [swap_over(part, "grp", 1) for part in parts]

    state, total, *pays = call(
        first_kernel,
        [state_shape, total_shape] + [pay_shape] * npay,
        [IN_VMEM] * (2 + npay),
        [fwd_fields, adj_fields],
        [IN_VMEM, IN_VMEM],
    )
    from_below, from_above = trade(pays)
    state, profile = call(
        inner_kernel, [state_shape, plane], [IN_VMEM] * 2, [state, source_pos],
        [IN_VMEM, IN_SMEM], aliases={0: 0},
    )
    state, curls = call(
        curl_kernel,
        [state_shape, on_chip(2, 3, depth, width_x, width_y)],
        [IN_VMEM] * 2,
        [state, from_below, from_above],
        [IN_VMEM] * 3,
        aliases={0: 0},
    )
    coef = call(
        functools.partial(coef_kernel, layout, len(parts), depth),
        coef_shape,
        IN_VMEM,
        parts + [block_ids, material_idx, material_eps],
        [IN_VMEM] * len(parts) + [IN_SMEM] * 3,
        [
            pltpu.VMEM((nblock,) + piece, F32),
            pltpu.VMEM((width_x + 2 * PAD, width_y), F32),
            pltpu.VMEM((width_x, width_y), F32),
        ],
    )

    about = [source_pos, drives, profile]
    about_specs = [IN_SMEM, IN_SMEM, IN_VMEM]
    state, total, *pays = call(
        ahead_a_kernel,
        [state_shape, total_shape] + [pay_shape] * npay + [plane] * npay,
        [IN_VMEM] * (2 + 2 * npay),
        [state, total, coef, curls] + about,
        [IN_VMEM] * 4 + about_specs,
        aliases={0: 0, 1: 1},
    )
    edges_a = trade(pays[:npay])
    cells = trade(pays[npay:])
    state, *pays = call(
        ahead_b_kernel,
        [state_shape] + [pay_shape] * npay,
        [IN_VMEM] * (1 + npay),
        [state, coef] + about,
        [IN_VMEM] * 2 + about_specs,
        aliases={0: 0},
    )
    edges_b = trade(pays)
    state, total, *pays = call(
        ahead_c_kernel,
        [state_shape, total_shape] + [pay_shape] * npay,
        [IN_VMEM] * (2 + npay),
        [state, total, coef] + about,
        [IN_VMEM] * 3 + about_specs,
        aliases={0: 0, 1: 1},
    )
    edges_c = trade(pays)
    state, total = call(
        bulk_kernel,
        [state_shape, total_shape],
        [IN_VMEM] * 2,
        [state, total, coef] + about,
        [IN_VMEM] * 3 + about_specs,
        aliases={0: 0, 1: 1},
    )
    state, total, coef = call(
        behind_a_kernel,
        [state_shape, total_shape, coef_shape],
        [IN_VMEM] * 3,
        [state, total, coef] + edges_a + cells + about,
        [IN_VMEM] * 7 + about_specs,
        aliases={0: 0, 1: 1, 2: 2},
    )
    for kernel, edges in ((behind_b_kernel, edges_b), (behind_c_kernel, edges_c)):
        state, total = call(
            kernel,
            [state_shape, total_shape],
            [IN_VMEM] * 2,
            [state, total, coef] + edges + about,
            [IN_VMEM] * 5 + about_specs,
            aliases={0: 0, 1: 1},
        )

    parts = call(
        functools.partial(filter_kernel, layout),
        [on_chip(*group)] * len(layout),
        [IN_VMEM] * len(layout),
        [total, block_ids],
        [IN_VMEM, IN_SMEM],
        [pltpu.VMEM((nblock,) + piece, F32), pltpu.VMEM((width_x, width_y), F32)],
    )
    kept, sent = parts[:middle], parts[middle:]
    got = [swap_over(part, "grp", 1) for part in sent]
    sums = call(
        add_kernel,
        [on_chip(*group)] * middle,
        [IN_VMEM] * middle,
        list(kept) + got,
        [IN_VMEM] * (2 * middle),
    )
    got = [swap_over(part, "grp", mask) for part, mask in zip(sums[1:], middle_masks[1:])]
    pieces = call(
        functools.partial(add_split_kernel, middle),
        [on_chip(*piece)] * far,
        [IN_VMEM] * far,
        [sums[0]] + got,
        [IN_VMEM] * middle,
    )
    got = [swap_over(part, "grp", mask) for part, mask in zip(pieces[1:], far_masks[1:])]
    scale = 3.0 / (STEPS * math.sqrt(ngrp))
    grad = call(
        functools.partial(last_kernel, scale),
        jax.ShapeDtypeStruct(piece, F32),
        IN_VMEM,
        [pieces[0]] + got,
        [IN_VMEM] * far,
    )
    finals = call(
        out_kernel,
        jax.ShapeDtypeStruct(fwd_fields.shape, F32),
        IN_HBM,
        [state],
        [IN_VMEM],
        [
            pltpu.VMEM((3, depth, width_x, width_y), F32),
            pltpu.SemaphoreType.DMA((6,)),
        ],
    )
    return finals, grad.reshape(density.shape)


def solution(mesh):
    placed = (
        P("grp", None, "slab", None, None),
        P("grp", None, "slab", None, None),
        P("slab", "grp", None),
        P(),
        P(),
        P(),
        P("grp", None),
        P("grp"),
    )
    return jax.shard_map(
        per_device,
        mesh=mesh,
        in_specs=placed,
        out_specs=(P("grp", None, "slab", None, None), P("slab", "grp", None)),
        check_vma=False,
    )
```

time: 68.8 us -> 71.7 us (1.042)
  starting transfers between devices: 16.8 us -> 19.7 us
  local copies, waits for them, and re-layouts: 3.47 us -> 5.2 us
  Pallas kernels: 22.5 us -> 21.3 us
    unnamed x8 -> x16, local copies, waits for them, and re-layouts: 0.78 us -> 5.2 us
    ppermute x16 -> x17, starting transfers between devices: 16.8 us -> 19.7 us  [swap_over(): lax.ppermute(array, axis, [(i, i ^ mask) for i in range(lax.axis_size(axi...]
    slice x1 -> x0, local copies, waits for them, and re-layouts: 1.42 us -> none  [per_device(): source_pos[0, 2]]
    another operation x1 -> x0, local copies, waits for them, and re-layouts: 1.27 us -> none  [per_device(): jnp.stack([(slab < nslab - 1).astype(jnp.int32), (slab > 0).astype(jnp.in...]
    pallas_call x17, Pallas kernels: 22.5 us -> 21.3 us  [call(): pl.pallas_call(kernel, out_shape=outs, in_specs=specs, out_specs=out_spec...]
    ppermute x16 -> x17, waiting for transfers between devices: 23.7 us -> 23.5 us  [swap_over(): lax.ppermute(array, axis, [(i, i ^ mask) for i in range(lax.axis_size(axi...]
  transfers between devices with their start and end apart: 16 -> 17, of which waited for: 8 -> 7; matrix products, arithmetic and copies ran while one was open for 4% -> 0% of each run, Pallas kernels for 24% -> 21%
where the time goes in v2:
time: 71.7 us; the launch traced here: 71.4 us
  waiting for transfers between devices  23.5 us (33%)
  Pallas kernels  21.3 us (30%)
  starting transfers between devices  19.7 us (27%)
  local copies, waits for them, and re-layouts  5.2 us (7%)
  between operations  1.56 us (2%)
    ppermute x17, waiting for transfers between devices, swap_over(): lax.ppermute(array, axis, [(i, i ^ mask) for i in range(lax.axis_size(axi...  23.5 us
    pallas_call x17, Pallas kernels, call(): pl.pallas_call(kernel, out_shape=outs, in_specs=specs, out_specs=out_spec...  21.3 us
    ppermute x17, starting transfers between devices, swap_over(): lax.ppermute(array, axis, [(i, i ^ mask) for i in range(lax.axis_size(axi...  19.7 us
    unnamed x16, local copies, waits for them, and re-layouts  5.2 us
  transfers between devices with their start and end apart: 17, of which 7 were waited for; matrix products, arithmetic and copies ran while one was open for 0% of the time, Pallas kernels for 21%

profile of v2, /device:TPU:0, one launch (start us, length us, event | category | flops | bytes accessed | tf_op | source)
XLA Modules:
  0.0 71.4 jit_solution(1398669401405032703)
XLA Ops:
  0.6 5.1 %collective-permute-start.3 = (f32[64,128]{1,0:T(8,128)}, f32[64,128]{1,0:T(8,128)S(1)}, u32[]{:S(2)}, u32[]{:S(2)}) collective-permute-start(f32[64,128]{1,0:T(8,128)} %bitcast.3), channel_id=1, source_target_pairs={{0,24},{2,26},{4,28},{6,30},{8,16},{10,18},{12,20},{14,22},{16,8},... | collective-permute-start | bytes 98312 | tf_op jit(solution)/shard_map/ppermute | solution.py:594
  5.7 0.6 collective-permute-start.1
  6.4 1.9 %copy-done = f32[1,6,8,128,128]{4,3,2,1,0:T(8,128)S(1)} copy-done((f32[1,6,8,128,128]{4,3,2,1,0:T(8,128)S(1)}, f32[1,6,8,128,128]{4,3,2,1,0:T(8,128)}, u32[]{:S(2)}) %copy-start) | copy-done | bytes 3145752
  8.3 1.9 %copy-done.1 = f32[1,6,8,128,128]{4,3,2,1,0:T(8,128)S(1)} copy-done((f32[1,6,8,128,128]{4,3,2,1,0:T(8,128)S(1)}, f32[1,6,8,128,128]{4,3,2,1,0:T(8,128)}, u32[]{:S(2)}) %copy-start.1) | copy-done | bytes 3145752
  10.2 0.9 %shard_map.95 = (f32[2,6,14,144,128]{4,3,2,1,0:T(8,128)S(1)}, f32[8,144,128]{2,1,0:T(8,128)S(1)}, f32[2,2,128,128]{3,2,1,0:T(8,128)S(1)}) custom-call(f32[1,6,8,128,128]{4,3,2,1,0:T(8,128)S(1)} %copy-done, f32[1,6,8,128,128]{4,3,2,1,0:T(8,128)S(1)} %copy-done.1), custom_call_target="tpu_custom_call" | custom-call | tf_op jit(solution)/shard_map/pallas_call | solution.py:35
  11.1 1.7 %collective-permute-start = (f32[2,2,128,128]{3,2,1,0:T(8,128)S(1)}, f32[2,2,128,128]{3,2,1,0:T(8,128)S(1)}, u32[]{:S(2)}, u32[]{:S(2)}) collective-permute-start(f32[2,2,128,128]{3,2,1,0:T(8,128)S(1)} %get-tuple-element.39), channel_id=1, source_target_pairs={{0,1},{1,0},{2,3},{3,2},{4,5},{5,4},{6,7},{7,6},{8,9},{9,8},{10,11... | collective-permute-start | bytes 786440 | tf_op jit(solution)/shard_map/ppermute | solution.py:594
  12.8 0.7 %copy-done.4 = f32[8,8,128]{2,1,0:T(8,128)S(1)} copy-done((f32[8,8,128]{2,1,0:T(8,128)S(1)}, f32[8,8,128]{2,1,0:T(8,128)}, u32[]{:S(2)}) %copy-start.4) | copy-done | bytes 32792
  13.6 1.6 %collective-permute-start.4 = (f32[4,64,128]{2,1,0:T(8,128)S(1)}, f32[4,64,128]{2,1,0:T(8,128)S(1)}, u32[]{:S(2)}, u32[]{:S(2)}) collective-permute-start(f32[4,64,128]{2,1,0:T(8,128)S(1)} %shard_map.98.refs_0_), channel_id=1, source_target_pairs={{0,4},{2,6},{4,0},{6,2},{8,12},{10,14},{12,8},{14,10},{16,20},{18,... | collective-permute-start | bytes 393224 | tf_op jit(solution)/shard_map/ppermute | solution.py:594
  15.1 3.5 %collective-permute-done.4.refs_1_ = f32[4,64,128]{2,1,0:T(8,128)S(1)} collective-permute-done((f32[4,64,128]{2,1,0:T(8,128)S(1)}, f32[4,64,128]{2,1,0:T(8,128)S(1)}, u32[]{:S(2)}, u32[]{:S(2)}) %collective-permute-start.4) | collective-permute-done | bytes 131104 | tf_op jit(solution)/shard_map/ppermute | solution.py:594
  19.3 0.6 copy-done.2
  20.0 1.6 %shard_map.96 = (f32[2,6,14,144,128]{4,3,2,1,0:T(8,128)S(1)}, f32[128,128]{1,0:T(8,128)S(1)}) custom-call(f32[2,6,14,144,128]{4,3,2,1,0:T(8,128)S(1)} %get-tuple-element.37.state_in, s32[1,3]{1,0:T(1,128)S(1)} %copy-done.2), custom_call_target="tpu_custom_call", output_to_operand_aliasing={{0}: (0, {})} | custom-call | tf_op jit(solution)/shard_map/pallas_call | solution.py:35
  21.6 1.2 %shard_map.97 = (f32[2,6,14,144,128]{4,3,2,1,0:T(8,128)S(1)}, f32[2,3,8,128,128]{4,3,2,1,0:T(8,128)S(1)}) custom-call(f32[2,6,14,144,128]{4,3,2,1,0:T(8,128)S(1)} %get-tuple-element.38.state_in, f32[2,2,128,128]{3,2,1,0:T(8,128)S(1)} %collective-permute-done.from_below.from_above, ...), custom_call_target="tpu_custom_call", output_to_operand_aliasing={{0}: (0, {})} | custom-call | tf_op jit(solution)/shard_map/pallas_call | solution.py:35
  22.9 1.6 %shard_map.99.coef.coef_in = f32[10,128,128]{2,1,0:T(8,128)S(1)} custom-call(f32[4,64,128]{2,1,0:T(8,128)S(1)} %shard_map.98.refs_0_, f32[4,64,128]{2,1,0:T(8,128)S(1)} %collective-permute-done.4.refs_1_, f32[4,64,128]{2,1,0:T(8,128)S(1)} %collective-permute-done.5.refs_2_, f32[4,64,128]{2,1,0:T(8,128)S(1)} %collective-permute-done.6.refs_3_, ...), custom_call_target="tpu_custom_call" | custom-call | tf_op jit(solution)/shard_map/pallas_call | solution.py:35
  24.5 1.3 %shard_map.100 = (f32[2,6,14,144,128]{4,3,2,1,0:T(8,128)S(1)}, f32[8,144,128]{2,1,0:T(8,128)S(1)}, f32[2,2,128,128]{3,2,1,0:T(8,128)S(1)}, f32[128,128]{1,0:T(8,128)S(1)}) custom-call(f32[2,6,14,144,128]{4,3,2,1,0:T(8,128)S(1)} %get-tuple-element.40.state_in, ...), custom_call_target="tpu_custom_call", output_to_operand_aliasing={{0}: (0, {}), {1}: (1, {})} | custom-call | tf_op jit(solution)/shard_map/pallas_call | solution.py:35
  26.3 1.0 %shard_map.101 = (f32[2,6,14,144,128]{4,3,2,1,0:T(8,128)S(1)}, f32[2,2,128,128]{3,2,1,0:T(8,128)S(1)}) custom-call(f32[2,6,14,144,128]{4,3,2,1,0:T(8,128)S(1)} %get-tuple-element.44.state_in, f32[10,128,128]{2,1,0:T(8,128)S(1)} %shard_map.99.coef.coef_in, s32[1,3]{1,0:T(1,128)S(1)} %copy-done.3, ...), custom_call_target="tpu_custom_call", output_to_operand_aliasing={{0}: (0, {})} | custom-call | tf_op jit(solution)/shard_map/pallas_call | solution.py:35
  27.3 1.6 %collective-permute-start.9 = (f32[2,2,128,128]{3,2,1,0:T(8,128)S(1)}, f32[2,2,128,128]{3,2,1,0:T(8,128)S(1)}, u32[]{:S(2)}, u32[]{:S(2)}) collective-permute-start(f32[2,2,128,128]{3,2,1,0:T(8,128)S(1)} %get-tuple-element.56), channel_id=1, source_target_pairs={{0,1},{1,0},{2,3},{3,2},{4,5},{5,4},{6,7},{7,6},{8,9},{9,8},{10,11... | collective-permute-start | bytes 786440 | tf_op jit(solution)/shard_map/ppermute | solution.py:594
  28.9 1.4 %shard_map.102 = (f32[2,6,14,144,128]{4,3,2,1,0:T(8,128)S(1)}, f32[8,144,128]{2,1,0:T(8,128)S(1)}, f32[2,2,128,128]{3,2,1,0:T(8,128)S(1)}) custom-call(f32[2,6,14,144,128]{4,3,2,1,0:T(8,128)S(1)} %get-tuple-element.45.state_in, f32[8,144,128]{2,1,0:T(8,128)S(1)} %get-tuple-element.46.total_in, ...), custom_call_target="tpu_custom_call", output_to_operand_aliasing={{0}: (0, {}), {1}: (1, {})} | custom-call | tf_op jit(solution)/shard_map/pallas_call | solution.py:35
  30.8 1.6 %collective-permute-start.8 = (f32[128,128]{1,0:T(8,128)S(1)}, f32[128,128]{1,0:T(8,128)S(1)}, u32[]{:S(2)}, u32[]{:S(2)}) collective-permute-start(f32[128,128]{1,0:T(8,128)S(1)} %get-tuple-element.52), channel_id=1, source_target_pairs={{0,1},{1,0},{2,3},{3,2},{4,5},{5,4},{6,7},{7,6},{8,9},{9,8},{10,11... | collective-permute-start | bytes 196616 | tf_op jit(solution)/shard_map/ppermute | solution.py:594
  32.4 3.9 %shard_map.103 = (f32[2,6,14,144,128]{4,3,2,1,0:T(8,128)S(1)}, f32[8,144,128]{2,1,0:T(8,128)S(1)}) custom-call(f32[2,6,14,144,128]{4,3,2,1,0:T(8,128)S(1)} %get-tuple-element.47.state_in, f32[8,144,128]{2,1,0:T(8,128)S(1)} %get-tuple-element.48.total_in, f32[10,128,128]{2,1,0:T(8,128)S(1)} %shard_map.99.coef.coef_in, ...), custom_call_target="tpu_custom_call", output_to_operand_aliasing={{0}: (0, {}), {1}: (1, {})} | custom-call | tf_op jit(solution)/shard_map/pallas_call | solution.py:35
  36.3 11.0 %collective-permute-done.8.below_cells.above_cells = f32[128,128]{1,0:T(8,128)S(1)} collective-permute-done((f32[128,128]{1,0:T(8,128)S(1)}, f32[128,128]{1,0:T(8,128)S(1)}, u32[]{:S(2)}, u32[]{:S(2)}) %collective-permute-start.8) | collective-permute-done | bytes 65568 | tf_op jit(solution)/shard_map/ppermute | solution.py:594
  47.3 1.5 %shard_map.104 = (f32[2,6,14,144,128]{4,3,2,1,0:T(8,128)S(1)}, f32[8,144,128]{2,1,0:T(8,128)S(1)}, f32[10,128,128]{2,1,0:T(8,128)S(1)}) custom-call(f32[2,6,14,144,128]{4,3,2,1,0:T(8,128)S(1)} %get-tuple-element.49.state_in, f32[8,144,128]{2,1,0:T(8,128)S(1)} %get-tuple-element.50.total_in, ...), custom_call_target="tpu_custom_call", output_to_operand_aliasing={{0}: (0, {}), {1}: (1, {}), {2}: (2, {})} | custom-call | tf_op jit(solution)/shard_map/pallas_call | solution.py:35
  48.8 2.2 %shard_map.105 = (f32[2,6,14,144,128]{4,3,2,1,0:T(8,128)S(1)}, f32[8,144,128]{2,1,0:T(8,128)S(1)}) custom-call(f32[2,6,14,144,128]{4,3,2,1,0:T(8,128)S(1)} %get-tuple-element.53.state_in, f32[8,144,128]{2,1,0:T(8,128)S(1)} %get-tuple-element.54.total_in, f32[10,128,128]{2,1,0:T(8,128)S(1)} %get-tuple-element.55.coef, ...), custom_call_target="tpu_custom_call", output_to_operand_aliasing={{0}: (0, {}), {1}: (1, {})} | custom-call | tf_op jit(solution)/shard_map/pallas_call | solution.py:35
  51.0 0.9 %shard_map.106 = (f32[2,6,14,144,128]{4,3,2,1,0:T(8,128)S(1)}, f32[8,144,128]{2,1,0:T(8,128)S(1)}) custom-call(f32[2,6,14,144,128]{4,3,2,1,0:T(8,128)S(1)} %get-tuple-element.57.state_in, f32[8,144,128]{2,1,0:T(8,128)S(1)} %get-tuple-element.58.total_in, f32[10,128,128]{2,1,0:T(8,128)S(1)} %get-tuple-element.55.coef, ...), custom_call_target="tpu_custom_call", output_to_operand_aliasing={{0}: (0, {}), {1}: (1, {})} | custom-call | tf_op jit(solution)/shard_map/pallas_call | solution.py:35
  52.0 1.4 %shard_map.108 = (f32[4,64,128]{2,1,0:T(8,128)S(1)}, f32[4,64,128]{2,1,0:T(8,128)S(1)}, f32[4,64,128]{2,1,0:T(8,128)S(1)}, f32[4,64,128]{2,1,0:T(8,128)S(1)}) custom-call(f32[8,144,128]{2,1,0:T(8,128)S(1)} %get-tuple-element.61.total, s32[16]{0:T(128)S(1)} %copy-done.5), custom_call_target="tpu_custom_call" | custom-call | tf_op jit(solution)/shard_map/pallas_call | solution.py:35
  54.0 0.8 %collective-permute-done.11.refs_2_ = f32[4,64,128]{2,1,0:T(8,128)S(1)} collective-permute-done((f32[4,64,128]{2,1,0:T(8,128)S(1)}, f32[4,64,128]{2,1,0:T(8,128)S(1)}, u32[]{:S(2)}, u32[]{:S(2)}) %collective-permute-start.11) | collective-permute-done | bytes 131104 | tf_op jit(solution)/shard_map/ppermute | solution.py:594
  55.0 1.5 %collective-permute-start.13 = (f32[4,64,128]{2,1,0:T(8,128)S(1)}, f32[4,64,128]{2,1,0:T(8,128)S(1)}, u32[]{:S(2)}, u32[]{:S(2)}) collective-permute-start(f32[4,64,128]{2,1,0:T(8,128)S(1)} %get-tuple-element.67), channel_id=1, source_target_pairs={{0,4},{2,6},{4,0},{6,2},{8,12},{10,14},{12,8},{14,10},{16,20},{18,... | collective-permute-start | bytes 393224 | tf_op jit(solution)/shard_map/ppermute | solution.py:594
  56.6 4.2 %collective-permute-done.13.refs_1_ = f32[4,64,128]{2,1,0:T(8,128)S(1)} collective-permute-done((f32[4,64,128]{2,1,0:T(8,128)S(1)}, f32[4,64,128]{2,1,0:T(8,128)S(1)}, u32[]{:S(2)}, u32[]{:S(2)}) %collective-permute-start.13) | collective-permute-done | bytes 131104 | tf_op jit(solution)/shard_map/ppermute | solution.py:594
  60.8 1.3 %collective-permute-start.14 = (f32[64,128]{1,0:T(8,128)S(1)}, f32[64,128]{1,0:T(8,128)S(1)}, u32[]{:S(2)}, u32[]{:S(2)}) collective-permute-start(f32[64,128]{1,0:T(8,128)S(1)} %get-tuple-element.69), channel_id=1, source_target_pairs={{0,8},{2,10},{4,12},{6,14},{8,0},{10,2},{12,4},{14,6},{16,24},{18,... | collective-permute-start | bytes 98312 | tf_op jit(solution)/shard_map/ppermute | solution.py:594
  62.1 2.9 %collective-permute-start.15 = (f32[64,128]{1,0:T(8,128)S(1)}, f32[64,128]{1,0:T(8,128)S(1)}, u32[]{:S(2)}, u32[]{:S(2)}) collective-permute-start(f32[64,128]{1,0:T(8,128)S(1)} %get-tuple-element.70), channel_id=1, source_target_pairs={{0,16},{2,18},{4,20},{6,22},{8,24},{10,26},{12,28},{14,30},{16,0},... | collective-permute-start | bytes 98312 | tf_op jit(solution)/shard_map/ppermute | solution.py:594
  65.3 1.7 %shard_map.107 = f32[1,6,8,128,128]{4,3,2,1,0:T(8,128)} custom-call(f32[2,6,14,144,128]{4,3,2,1,0:T(8,128)S(1)} %get-tuple-element.60.state), custom_call_target="tpu_custom_call" | custom-call | tf_op jit(solution)/shard_map/pallas_call | solution.py:35
  67.5 3.3 %collective-permute-done.16.refs_3_ = f32[64,128]{1,0:T(8,128)S(1)} collective-permute-done((f32[64,128]{1,0:T(8,128)S(1)}, f32[64,128]{1,0:T(8,128)S(1)}, u32[]{:S(2)}, u32[]{:S(2)}) %collective-permute-start.16) | collective-permute-done | bytes 32800 | tf_op jit(solution)/shard_map/ppermute | solution.py:594
  70.8 0.6 shard_map.111
  (36 shorter events, 2.5 us)
Async XLA Ops:
  0.6 12.2 %collective-permute-start.3 = (f32[64,128]{1,0:T(8,128)}, f32[64,128]{1,0:T(8,128)S(1)}, u32[]{:S(2)}, u32[]{:S(2)}) collective-permute-start(f32[64,128]{1,0:T(8,128)} %bitcast.3), channel_id=1, source_target_pairs={{0,24},{2,26},{4,28},{6,30},{8,16},{10,18},{12,20},{14,22},{16,8},... | collective-permute-start | bytes 98312 | tf_op jit(solution)/shard_map/ppermute | solution.py:594
  5.7 7.1 %collective-permute-start.2 = (f32[64,128]{1,0:T(8,128)}, f32[64,128]{1,0:T(8,128)S(1)}, u32[]{:S(2)}, u32[]{:S(2)}) collective-permute-start(f32[64,128]{1,0:T(8,128)} %bitcast.4), channel_id=1, source_target_pairs={{0,16},{2,18},{4,20},{6,22},{8,24},{10,26},{12,28},{14,30},{16,0},... | collective-permute-start | bytes 98312 | tf_op jit(solution)/shard_map/ppermute | solution.py:594
  5.7 7.1 %collective-permute-start.1 = (f32[64,128]{1,0:T(8,128)}, f32[64,128]{1,0:T(8,128)S(1)}, u32[]{:S(2)}, u32[]{:S(2)}) collective-permute-start(f32[64,128]{1,0:T(8,128)} %bitcast.5), channel_id=1, source_target_pairs={{0,8},{2,10},{4,12},{6,14},{8,0},{10,2},{12,4},{14,6},{16,24},{18,... | collective-permute-start | bytes 98312 | tf_op jit(solution)/shard_map/ppermute | solution.py:594
  6.4 1.9 %copy-start = (f32[1,6,8,128,128]{4,3,2,1,0:T(8,128)S(1)}, f32[1,6,8,128,128]{4,3,2,1,0:T(8,128)}, u32[]{:S(2)}) copy-start(f32[1,6,8,128,128]{4,3,2,1,0:T(8,128)} %fwd.1) | copy-start | bytes 9437188
  8.3 1.9 %copy-start.1 = (f32[1,6,8,128,128]{4,3,2,1,0:T(8,128)S(1)}, f32[1,6,8,128,128]{4,3,2,1,0:T(8,128)}, u32[]{:S(2)}) copy-start(f32[1,6,8,128,128]{4,3,2,1,0:T(8,128)} %adj.1) | copy-start | bytes 9437188
  11.1 10.5 %collective-permute-start = (f32[2,2,128,128]{3,2,1,0:T(8,128)S(1)}, f32[2,2,128,128]{3,2,1,0:T(8,128)S(1)}, u32[]{:S(2)}, u32[]{:S(2)}) collective-permute-start(f32[2,2,128,128]{3,2,1,0:T(8,128)S(1)} %get-tuple-element.39), channel_id=1, source_target_pairs={{0,1},{1,0},{2,3},{3,2},{4,5},{5,4},{6,7},{7,6},{8,9},{9,8},{10,11... | collective-permute-start | bytes 786440 | tf_op jit(solution)/shard_map/ppermute | solution.py:594
  12.8 0.8 %copy-start.4 = (f32[8,8,128]{2,1,0:T(8,128)S(1)}, f32[8,8,128]{2,1,0:T(8,128)}, u32[]{:S(2)}) copy-start(f32[8,8,128]{2,1,0:T(8,128)} %param.10) | copy-start | bytes 98308
  13.6 5.0 %collective-permute-start.4 = (f32[4,64,128]{2,1,0:T(8,128)S(1)}, f32[4,64,128]{2,1,0:T(8,128)S(1)}, u32[]{:S(2)}, u32[]{:S(2)}) collective-permute-start(f32[4,64,128]{2,1,0:T(8,128)S(1)} %shard_map.98.refs_0_), channel_id=1, source_target_pairs={{0,4},{2,6},{4,0},{6,2},{8,12},{10,14},{12,8},{14,10},{16,20},{18,... | collective-permute-start | bytes 393224 | tf_op jit(solution)/shard_map/ppermute | solution.py:594
  15.1 7.7 %collective-permute-start.5 = (f32[4,64,128]{2,1,0:T(8,128)S(1)}, f32[4,64,128]{2,1,0:T(8,128)S(1)}, u32[]{:S(2)}, u32[]{:S(2)}) collective-permute-start(f32[4,64,128]{2,1,0:T(8,128)S(1)} %shard_map.98.refs_0_), channel_id=1, source_target_pairs={{0,2},{2,0},{4,6},{6,4},{8,10},{10,8},{12,14},{14,12},{16,18},{18,... | collective-permute-start | bytes 393224 | tf_op jit(solution)/shard_map/ppermute | solution.py:594
  18.6 4.2 %collective-permute-start.6 = (f32[4,64,128]{2,1,0:T(8,128)S(1)}, f32[4,64,128]{2,1,0:T(8,128)S(1)}, u32[]{:S(2)}, u32[]{:S(2)}) collective-permute-start(f32[4,64,128]{2,1,0:T(8,128)S(1)} %collective-permute-done.4.refs_1_), channel_id=1, source_target_pairs={{0,2},{2,0},{4,6},{6,4},{8,10},{10,8},{12,14},{14,12},{16,18},{18,... | collective-permute-start | bytes 393224 | tf_op jit(solution)/shard_map/ppermute | solution.py:594
  19.3 0.7 copy-start.2
  20.0 2.9 %copy-start.5 = (s32[16]{0:T(128)S(1)}, s32[16]{0:T(128)}, u32[]{:S(2)}) copy-start(s32[16]{0:T(128)} %block_ids.1) | copy-start | bytes 196
  20.0 2.9 %copy-start.6 = (s32[16]{0:T(128)S(1)}, s32[16]{0:T(128)}, u32[]{:S(2)}) copy-start(s32[16]{0:T(128)} %refs_5_.1) | copy-start | bytes 196
  20.0 2.9 %copy-start.7 = (f32[4]{0:T(128)S(1)}, f32[4]{0:T(128)}, u32[]{:S(2)}) copy-start(f32[4]{0:T(128)} %refs_6_.1) | copy-start | bytes 52
  20.0 4.5 %copy-start.3 = (s32[1,3]{1,0:T(1,128)S(1)}, s32[1,3]{1,0:T(1,128)}, u32[]{:S(2)}) copy-start(s32[1,3]{1,0:T(1,128)} %source.15) | copy-start | bytes 40
  25.8 21.4 %collective-permute-start.7 = (f32[2,2,128,128]{3,2,1,0:T(8,128)S(1)}, f32[2,2,128,128]{3,2,1,0:T(8,128)S(1)}, u32[]{:S(2)}, u32[]{:S(2)}) collective-permute-start(f32[2,2,128,128]{3,2,1,0:T(8,128)S(1)} %get-tuple-element.51), channel_id=1, source_target_pairs={{0,1},{1,0},{2,3},{3,2},{4,5},{5,4},{6,7},{7,6},{8,9},{9,8},{10,11... | collective-permute-start | bytes 786440 | tf_op jit(solution)/shard_map/ppermute | solution.py:594
  27.3 21.5 %collective-permute-start.9 = (f32[2,2,128,128]{3,2,1,0:T(8,128)S(1)}, f32[2,2,128,128]{3,2,1,0:T(8,128)S(1)}, u32[]{:S(2)}, u32[]{:S(2)}) collective-permute-start(f32[2,2,128,128]{3,2,1,0:T(8,128)S(1)} %get-tuple-element.56), channel_id=1, source_target_pairs={{0,1},{1,0},{2,3},{3,2},{4,5},{5,4},{6,7},{7,6},{8,9},{9,8},{10,11... | collective-permute-start | bytes 786440 | tf_op jit(solution)/shard_map/ppermute | solution.py:594
  30.3 20.7 %collective-permute-start.10 = (f32[2,2,128,128]{3,2,1,0:T(8,128)S(1)}, f32[2,2,128,128]{3,2,1,0:T(8,128)S(1)}, u32[]{:S(2)}, u32[]{:S(2)}) collective-permute-start(f32[2,2,128,128]{3,2,1,0:T(8,128)S(1)} %get-tuple-element.59), channel_id=1, source_target_pairs={{0,1},{1,0},{2,3},{3,2},{4,5},{5,4},{6,7},{7,6},{8,9},{9,8},{10,11... | collective-permute-start | bytes 786440 | tf_op jit(solution)/shard_map/ppermute | solution.py:594
  30.8 16.5 %collective-permute-start.8 = (f32[128,128]{1,0:T(8,128)S(1)}, f32[128,128]{1,0:T(8,128)S(1)}, u32[]{:S(2)}, u32[]{:S(2)}) collective-permute-start(f32[128,128]{1,0:T(8,128)S(1)} %get-tuple-element.52), channel_id=1, source_target_pairs={{0,1},{1,0},{2,3},{3,2},{4,5},{5,4},{6,7},{7,6},{8,9},{9,8},{10,11... | collective-permute-start | bytes 196616 | tf_op jit(solution)/shard_map/ppermute | solution.py:594
  53.4 1.4 %collective-permute-start.11 = (f32[4,64,128]{2,1,0:T(8,128)S(1)}, f32[4,64,128]{2,1,0:T(8,128)S(1)}, u32[]{:S(2)}, u32[]{:S(2)}) collective-permute-start(f32[4,64,128]{2,1,0:T(8,128)S(1)} %get-tuple-element.64), channel_id=1, source_target_pairs={{0,2},{2,0},{4,6},{6,4},{8,10},{10,8},{12,14},{14,12},{16,18},{18,... | collective-permute-start | bytes 393224 | tf_op jit(solution)/shard_map/ppermute | solution.py:594
  53.5 1.5 %collective-permute-start.12 = (f32[4,64,128]{2,1,0:T(8,128)S(1)}, f32[4,64,128]{2,1,0:T(8,128)S(1)}, u32[]{:S(2)}, u32[]{:S(2)}) collective-permute-start(f32[4,64,128]{2,1,0:T(8,128)S(1)} %get-tuple-element.65), channel_id=1, source_target_pairs={{0,2},{2,0},{4,6},{6,4},{8,10},{10,8},{12,14},{14,12},{16,18},{18,... | collective-permute-start | bytes 393224 | tf_op jit(solution)/shard_map/ppermute | solution.py:594
  55.0 5.8 %collective-permute-start.13 = (f32[4,64,128]{2,1,0:T(8,128)S(1)}, f32[4,64,128]{2,1,0:T(8,128)S(1)}, u32[]{:S(2)}, u32[]{:S(2)}) collective-permute-start(f32[4,64,128]{2,1,0:T(8,128)S(1)} %get-tuple-element.67), channel_id=1, source_target_pairs={{0,4},{2,6},{4,0},{6,2},{8,12},{10,14},{12,8},{14,10},{16,20},{18,... | collective-permute-start | bytes 393224 | tf_op jit(solution)/shard_map/ppermute | solution.py:594
  60.8 6.2 %collective-permute-start.14 = (f32[64,128]{1,0:T(8,128)S(1)}, f32[64,128]{1,0:T(8,128)S(1)}, u32[]{:S(2)}, u32[]{:S(2)}) collective-permute-start(f32[64,128]{1,0:T(8,128)S(1)} %get-tuple-element.69), channel_id=1, source_target_pairs={{0,8},{2,10},{4,12},{6,14},{8,0},{10,2},{12,4},{14,6},{16,24},{18,... | collective-permute-start | bytes 98312 | tf_op jit(solution)/shard_map/ppermute | solution.py:594
  62.1 5.3 %collective-permute-start.15 = (f32[64,128]{1,0:T(8,128)S(1)}, f32[64,128]{1,0:T(8,128)S(1)}, u32[]{:S(2)}, u32[]{:S(2)}) collective-permute-start(f32[64,128]{1,0:T(8,128)S(1)} %get-tuple-element.70), channel_id=1, source_target_pairs={{0,16},{2,18},{4,20},{6,22},{8,24},{10,26},{12,28},{14,30},{16,0},... | collective-permute-start | bytes 98312 | tf_op jit(solution)/shard_map/ppermute | solution.py:594
  65.1 5.7 %collective-permute-start.16 = (f32[64,128]{1,0:T(8,128)S(1)}, f32[64,128]{1,0:T(8,128)S(1)}, u32[]{:S(2)}, u32[]{:S(2)}) collective-permute-start(f32[64,128]{1,0:T(8,128)S(1)} %get-tuple-element.71), channel_id=1, source_target_pairs={{0,24},{2,26},{4,28},{6,30},{8,16},{10,18},{12,20},{14,22},{16,8},... | collective-permute-start | bytes 98312 | tf_op jit(solution)/shard_map/ppermute | solution.py:594

commit v3 on v0

v3 whole, which is shorter than its diff:
```python
import functools
import math

import jax
import jax.numpy as jnp
from jax import lax
from jax.experimental import pallas as pl
from jax.experimental.pallas import tpu as pltpu
from jax.sharding import PartitionSpec as P

STEPS = 4
AMPLITUDE = 4.0
PAD = 8
F32 = jnp.float32

VMEM = pltpu.MemorySpace.VMEM
IN_VMEM = pl.BlockSpec(memory_space=pltpu.VMEM)
IN_SMEM = pl.BlockSpec(memory_space=pltpu.SMEM)
IN_HBM = pl.BlockSpec(memory_space=pltpu.MemorySpace.HBM)


def on_chip(*shape):
    return VMEM(shape, F32)


def held(array, spec):
    if spec is IN_SMEM:
        return array
    space = VMEM if spec is IN_VMEM else pltpu.MemorySpace.HBM
    return pltpu.with_memory_space_constraint(array, space)


def call(kernel, outs, out_specs, operands, specs, scratch=(), aliases=None, flops=0):
    operands = [held(a, s) for a, s in zip(operands, specs)]
    return pl.pallas_call(
        kernel,
        out_shape=outs,
        in_specs=specs,
        out_specs=out_specs,
        scratch_shapes=scratch,
        input_output_aliases=aliases or {},
        compiler_params=pltpu.CompilerParams(vmem_limit_bytes=8 << 20),
        cost_estimate=pl.CostEstimate(flops=flops, bytes_accessed=flops // 4, transcendentals=0),
    )(*operands)


EXTRA = 1
CHUNK = 16


def chunks(rows):
    size = CHUNK if rows % CHUNK == 0 else rows
    return [(first, size) for first in range(0, rows, size)]


def next_col(value):
    column = lax.broadcasted_iota(jnp.int32, value.shape, 1)
    moved = pltpu.roll(value, value.shape[1] - 1, 1)
    return jnp.where(column == value.shape[1] - 1, 0.0, moved)


def prev_col(value):
    column = lax.broadcasted_iota(jnp.int32, value.shape, 1)
    return jnp.where(column == 0, 0.0, pltpu.roll(value, 1, 1))


class Window:
    def __init__(self, state, coef=None, total=None, source=None, drives=None, profile=None):
        self.state, self.coef, self.total = state, coef, total
        self.source, self.drives, self.profile = source, drives, profile
        self.rows = state.shape[3] - 2 * PAD
        self.depth = state.shape[2] - EXTRA
        self.top, self.under = self.depth - 1, self.depth
        self.slab = lax.axis_index("slab")
        self.has_up = self.slab < lax.axis_size("slab") - 1
        self.has_low = self.slab > 0

    def read(self, evo, comp, layer, first, size, shift=0):
        return self.state[evo, comp, layer, pl.ds(PAD + first + shift, size), :]

    def write(self, evo, comp, layer, first, size, value):
        self.state[evo, comp, layer, pl.ds(PAD + first, size), :] = value

    def put_h(self, evo, layer, upper):
        for first, size in chunks(self.rows):
            ex, ey, ez, hx, hy, hz = (self.read(evo, c, layer, first, size) for c in range(6))
            if upper is None:
                rise_x, rise_y = -ex, -ey
            else:
                rise_x = self.read(evo, 0, upper, first, size) - ex
                rise_y = self.read(evo, 1, upper, first, size) - ey
            ey_after = self.read(evo, 1, layer, first, size, 1)
            ez_after = self.read(evo, 2, layer, first, size, 1)
            self.write(evo, 3, layer, first, size, hx - ((next_col(ez) - ez) - rise_y))
            self.write(evo, 4, layer, first, size, hy - (rise_x - (ez_after - ez)))
            self.write(evo, 5, layer, first, size, hz - ((ey_after - ey) - (next_col(ex) - ex)))

    def curl_h(self, evo, h, lower, first, size):
        hx, hy, hz = (self.read(evo, c, h, first, size) for c in (3, 4, 5))
        if lower is None:
            step_x, step_y = hx, hy
        else:
            step_x = hx - self.read(evo, 3, lower, first, size)
            step_y = hy - self.read(evo, 4, lower, first, size)
        hy_before = self.read(evo, 4, h, first, size, -1)
        hz_before = self.read(evo, 5, h, first, size, -1)
        return (
            (hz - prev_col(hz)) - step_y,
            step_x - (hz - hz_before),
            (hy - hy_before) - (hx - prev_col(hx)),
        )

    def drive(self, step, layer):
        @pl.when(self.source[0, 0] - self.slab * self.depth == layer)
        def _():
            amount = self.drives[step]
            for first, size in chunks(self.rows):
                here = pl.ds(PAD + first, size)
                self.state[0, 2, layer, here, :] += amount * self.profile[pl.ds(first, size), :]

    def next_e(self, evo, layer, lower, first, size):
        cell = self.coef[layer, pl.ds(first, size), :]
        curl = self.curl_h(evo, layer, lower, first, size)
        return [self.read(evo, c, layer, first, size) + cell * curl[c] for c in range(3)]

    def put_e(self, evo, layer, lower, step):
        if evo == 0:
            self.drive(step, layer)
        for first, size in chunks(self.rows):
            for c, value in enumerate(self.next_e(evo, layer, lower, first, size)):
                self.write(evo, c, layer, first, size, value)

    def put_both_e(self, layer, lower, step):
        self.drive(step, layer)
        for first, size in chunks(self.rows):
            fwd, adj = (self.next_e(evo, layer, lower, first, size) for evo in range(2))
            for evo, news in enumerate((fwd, adj)):
                for c in range(3):
                    self.write(evo, c, layer, first, size, news[c])
            part = fwd[0] * adj[0] + fwd[1] * adj[1] + fwd[2] * adj[2]
            self.total[layer, pl.ds(PAD + first, size), :] += part

    def add_edge(self, edges, slot, layer):
        for first, size in chunks(self.rows):
            part = edges[slot, pl.ds(PAD + first, size), :]
            for c in range(3):
                part += self.read(0, c, layer, first, size) * self.read(1, c, layer, first, size)
            edges[slot, pl.ds(PAD + first, size), :] = part

    def take(self, evo, below, above):
        top, under = self.top, self.under

        @pl.when(self.has_up)
        def _():
            for first, size in chunks(self.rows):
                here = pl.ds(first, size)
                hx = self.read(evo, 3, top, first, size) + above[1, here, :]
                hy = self.read(evo, 4, top, first, size) - above[0, here, :]
                self.write(evo, 3, top, first, size, hx)
                self.write(evo, 4, top, first, size, hy)

        @pl.when(self.has_low)
        def _():
            for first, size in chunks(self.rows):
                here = pl.ds(first, size)
                hx = below[0, here, :] + self.read(evo, 1, 0, first, size)
                hy = below[1, here, :] - self.read(evo, 0, 0, first, size)
                self.write(evo, 3, under, first, size, hx)
                self.write(evo, 4, under, first, size, hy)

    def give(self, evo, pays):
        def up(pay):
            for c in range(2):
                pay[c] = self.state[evo, 3 + c, self.top, pl.ds(PAD, self.rows), :]

        def down(pay):
            for c in range(2):
                pay[c] = self.state[evo, c, 0, pl.ds(PAD, self.rows), :]

        if len(pays) == 2:
            up(pays[0])
            down(pays[1])
        else:
            pl.when(self.has_up)(lambda: up(pays[0]))
            pl.when(self.has_low)(lambda: down(pays[0]))


def opening_kernel(fwd, adj, density, own, *rest):
    pays, (planes, sems) = rest[:-2], rest[-2:]
    depth, rows, width_y = fwd.shape[2:]
    top = depth - 1
    slab = lax.axis_index("slab")
    has_up, has_low = slab < lax.axis_size("slab") - 1, slab > 0
    held_copy = pltpu.make_async_copy(density, own, sems.at[2, 0])
    held_copy.start()

    def up(pay):
        copies = []
        for evo, given in enumerate((fwd, adj)):
            for c in range(5):
                copies.append(
                    pltpu.make_async_copy(given.at[0, c, top], planes.at[evo, c], sems.at[evo, c])
                )
        for copy in copies:
            copy.start()
        for copy in copies:
            copy.wait()
        for evo in range(2):
            for first, size in chunks(rows):
                here = pl.ds(first, size)
                ex, ey, ez, hx, hy = (planes[evo, c, here, :] for c in range(5))
                if first + size < rows:
                    ez_after = planes[evo, 2, pl.ds(first + 1, size), :]
                else:
                    row = lax.broadcasted_iota(jnp.int32, ez.shape, 0)
                    ez_after = jnp.where(row == size - 1, 0.0, pltpu.roll(ez, size - 1, 0))
                pay[evo, 0, here, :] = (hx + hx) - ((next_col(ez) - ez) + ey)
                pay[evo, 1, here, :] = (hy + hy) + (ex + (ez_after - ez))

    def down(pay):
        copies = []
        for evo, given in enumerate((fwd, adj)):
            for c in range(2):
                copies.append(
                    pltpu.make_async_copy(given.at[0, c, 0], pay.at[evo, c], sems.at[evo, c])
                )
        for copy in copies:
            copy.start()
        for copy in copies:
            copy.wait()

    if len(pays) == 2:
        up(pays[0])
        down(pays[1])
    else:
        pl.when(has_up)(lambda: up(pays[0]))
        pl.when(has_low)(lambda: down(pays[0]))
    held_copy.wait()


def first_kernel(fwd, adj, source, state, total, edges, profile):
    win = Window(state)
    rows, width_y = win.rows, state.shape[4]
    margin = jnp.zeros((PAD, width_y), F32)
    empty = jnp.zeros((rows + 2 * PAD, width_y), F32)

    def clear(layer, carry):
        for evo in range(2):
            for comp in range(6):
                state[evo, comp, layer, pl.ds(0, PAD), :] = margin
                state[evo, comp, layer, pl.ds(PAD + rows, PAD), :] = margin
        return carry

    lax.fori_loop(0, state.shape[2], clear, 0)
    for evo in range(2):
        for comp in (3, 4):
            state[evo, comp, win.under] = empty
        edges[evo] = empty

    def copy(layer, carry):
        total[layer] = empty
        for evo, given in enumerate((fwd, adj)):
            for comp in range(6):
                for first, size in chunks(rows):
                    value = given[0, comp, layer, pl.ds(first, size), :]
                    win.write(evo, comp, layer, first, size, value + value if comp > 2 else value)
        return carry

    lax.fori_loop(0, win.depth, copy, 0)

    def body(layer, carry):
        for evo in range(2):
            win.put_h(evo, layer, layer + 1)
        return carry

    lax.fori_loop(0, win.top, body, 0)
    for evo in range(2):
        win.put_h(evo, win.top, None)
    xcoord = lax.broadcasted_iota(jnp.int32, (rows, width_y), 0)
    ycoord = lax.broadcasted_iota(jnp.int32, (rows, width_y), 1)
    offset_x = (xcoord - source[0, 1]).astype(F32) / (rows / 4.0)
    offset_y = (ycoord - source[0, 2]).astype(F32) / (width_y / 4.0)
    profile[...] = jnp.exp(-0.5 * (offset_x * offset_x + offset_y * offset_y))


def take_kernel(state_in, below, above, state):
    win = Window(state)
    for evo in range(2):
        win.take(evo, below.at[evo], above.at[evo])


def edge_kernel(
    step, evo, state_in, edges_in, coef, source, drives, profile, *rest
):
    rest = list(rest)
    arrived = [rest.pop(0) for _ in range(2 if step > 0 else 0)]
    state, edges, pays = rest[0], rest[1], rest[2:]
    win = Window(state, coef, None, source, drives, profile)
    if step > 0:
        win.take(evo, *arrived)
    win.put_e(evo, win.top, win.top - 1, step)
    win.put_e(evo, 0, win.under, step)
    if pays:
        if evo == 1:
            win.add_edge(edges, 0, 0)
            win.add_edge(edges, 1, win.top)
        win.put_h(evo, win.top, None)
        win.give(evo, pays)
    elif evo == 1:
        win.add_edge(edges, 0, 0)
        win.add_edge(edges, 1, win.top)


def inner_kernel(step, state_in, total_in, coef, source, drives, profile, state, total):
    win = Window(state, coef, total, source, drives, profile)

    def first(layer, carry):
        win.put_both_e(layer, layer - 1, 0)
        return carry

    if step == 1:
        lax.fori_loop(1, win.top, first, 0)
    for evo in range(2):
        win.put_h(evo, 0, 1)

    def body(layer, carry):
        for evo in range(2):
            win.put_h(evo, layer, layer + 1)
        win.put_both_e(layer, layer - 1, step)
        return carry

    lax.fori_loop(1, win.top, body, 0)


def coef_layer(layer, coef, blocks, placed, base):
    nblock = blocks.shape[0]
    rows = base.shape[0]
    block_rows = rows // nblock
    for block in range(nblock):
        source = pl.ds(pl.multiple_of(layer * block_rows, block_rows), block_rows)
        placed[pl.ds(PAD + block * block_rows, block_rows), :] = blocks[block, source, :]
    for first, size in chunks(rows):
        here = pl.ds(first, size)
        coef[layer, here, :] = 0.25 / (base[here, :] + 3.0 * filtered(placed, first, size))


def coef_edge_kernel(layout, count, *refs):
    parts = refs[:count]
    block_ids, material_idx, material_eps, coef, blocks, base, placed = refs[count:]
    nblock = blocks.shape[0]
    depth, rows, width_y = coef.shape
    block_rows = rows // nblock
    me = lax.axis_index("grp")
    for part, masks in zip(parts, layout):
        for slot, mask in enumerate(masks):
            blocks[block_ids[me ^ mask]] = part[slot]
    for block in range(nblock):
        level = jnp.full((block_rows, width_y), material_eps[material_idx[block]], F32)
        base[pl.ds(block * block_rows, block_rows), :] = level
    placed[pl.ds(0, PAD), :] = jnp.zeros((PAD, width_y), F32)
    placed[pl.ds(PAD + rows, PAD), :] = jnp.zeros((PAD, width_y), F32)
    coef_layer(0, coef, blocks, placed, base)
    coef_layer(depth - 1, coef, blocks, placed, base)


def coef_inner_kernel(coef_in, blocks, base, coef, placed):
    depth, rows, width_y = coef.shape
    placed[pl.ds(0, PAD), :] = jnp.zeros((PAD, width_y), F32)
    placed[pl.ds(PAD + rows, PAD), :] = jnp.zeros((PAD, width_y), F32)

    def body(layer, carry):
        coef_layer(layer, coef, blocks, placed, base)
        return carry

    lax.fori_loop(1, depth - 1, body, 0)


def filtered(padded, first, size):
    here = padded[pl.ds(PAD + first, size), :]
    before = padded[pl.ds(PAD + first - 1, size), :]
    after = padded[pl.ds(PAD + first + 1, size), :]
    along = before + 2.0 * here + after
    return (prev_col(along) + 2.0 * along + next_col(along)) * 0.0625


def pack_kernel(*refs):
    out = refs[-1]
    for slot, ref in enumerate(refs[:-1]):
        out[slot] = ref[...]


def filter_kernel(layout, skip, total, block_ids, *rest):
    parts, blocks, wide = rest[:-2], rest[-2], rest[-1]
    nblock = blocks.shape[0]
    rows = total.shape[1] - 2 * PAD
    block_rows = rows // nblock
    me = lax.axis_index("grp")

    def layer_of(layer, carry):
        for first, size in chunks(rows):
            wide[pl.ds(first, size), :] = filtered(total.at[layer + skip], first, size)
        for block in range(nblock):
            target = pl.ds(pl.multiple_of(layer * block_rows, block_rows), block_rows)
            blocks[block, target, :] = wide[pl.ds(block * block_rows, block_rows), :]
        return carry

    lax.fori_loop(0, total.shape[0] - 2 * skip, layer_of, 0)
    for part, masks in zip(parts, layout):
        for slot, mask in enumerate(masks):
            part[slot] = blocks[block_ids[me ^ mask]]


def add_kernel(*refs):
    half = len(refs) // 3
    for a, b, out in zip(refs[:half], refs[half : 2 * half], refs[2 * half :]):
        out[...] = a[...] + b[...]


def join_kernel(count, block_rows, *refs):
    inner, edge, outs = refs[:count], refs[count : 2 * count], refs[2 * count :]
    rows = outs[0].shape[0]
    for slot, out in enumerate(outs):
        middle, ends = inner[0][slot], edge[0][slot]
        for a, b in zip(inner[1:], edge[1:]):
            middle, ends = middle + a[slot], ends + b[slot]
        out[pl.ds(0, block_rows), :] = ends[:block_rows]
        out[pl.ds(block_rows, rows - 2 * block_rows), :] = middle
        out[pl.ds(rows - block_rows, block_rows), :] = ends[block_rows:]


def last_kernel(scale, *refs):
    value = refs[0][...]
    for ref in refs[1:-1]:
        value = value + ref[...]
    refs[-1][...] = value * scale


def out_kernel(state, finals, halves, sems):
    depth = state.shape[2] - EXTRA
    rows = state.shape[3] - 2 * PAD
    every = pl.ds(PAD, rows)
    copies = [
        pltpu.make_async_copy(
            state.at[0, comp, pl.ds(0, depth), every, :], finals.at[0, comp], sems.at[comp]
        )
        for comp in range(3)
    ]
    for copy in copies:
        copy.start()
    for comp in range(3):

        def body(layer, carry):
            halves[comp, layer] = 0.5 * state[0, 3 + comp, layer, every, :]
            return carry

        lax.fori_loop(0, depth, body, 0)
        copy = pltpu.make_async_copy(halves.at[comp], finals.at[0, 3 + comp], sems.at[3 + comp])
        copy.start()
        copies.append(copy)
    for copy in copies:
        copy.wait()


def swap_over(array, axis, mask):
    return lax.ppermute(array, axis, [(i, i ^ mask) for i in range(lax.axis_size(axis))])


def shift_over(array, axis, distance):
    size = lax.axis_size(axis)
    route = [(i, i + distance) for i in range(size) if 0 <= i + distance < size]
    return lax.ppermute(array, axis, route)


def trade(pays):
    if len(pays) == 1:
        return [swap_over(pays[0], "slab", 1)] * 2
    return [shift_over(pays[0], "slab", 1), shift_over(pays[1], "slab", -1)]


def per_device(
    fwd_fields, adj_fields, density, block_ids, material_idx, material_eps, source_pos, wave_idx
):
    depth, width_x, width_y = fwd_fields.shape[2:]
    nblock = block_ids.shape[0]
    block_rows = width_x // nblock
    ngrp = lax.axis_size("grp")
    npay = 1 if lax.axis_size("slab") == 2 else 2
    omega = 2.0 * math.pi / (6.0 + 2.0 * wave_idx[0].astype(F32))
    drives = AMPLITUDE * jnp.sin(omega * (jnp.arange(STEPS, dtype=F32) + 1.0))

    far = 4
    middle = ngrp // (2 * far)
    far_masks = [2 * middle * j for j in range(far)]
    middle_masks = [2 * j for j in range(middle)]
    layout = [
        [core + mid + top for top in far_masks] for core in (0, 1) for mid in middle_masks
    ]
    piece = (depth * block_rows, width_y)
    group = (far,) + piece

    state_shape = on_chip(2, 6, depth + EXTRA, width_x + 2 * PAD, width_y)
    total_shape = on_chip(depth, width_x + 2 * PAD, width_y)
    edges_shape = on_chip(2, width_x + 2 * PAD, width_y)
    coef_shape = on_chip(depth, width_x, width_y)
    blocks_shape = on_chip(nblock, *piece)
    plane = on_chip(width_x, width_y)
    padded = pltpu.VMEM((width_x + 2 * PAD, width_y), F32)

    design = density.reshape(piece)
    got = [swap_over(design, "grp", mask) for mask in far_masks[1:]]
    own, *pays = call(
        opening_kernel,
        [on_chip(*piece)] + [on_chip(2, 2, width_x, width_y)] * npay,
        [IN_VMEM] * (1 + npay),
        [fwd_fields, adj_fields, design],
        [IN_HBM] * 3,
        [pltpu.VMEM((2, 5, width_x, width_y), F32), pltpu.SemaphoreType.DMA((3, 5))],
    )
    below, above = trade(pays)

    near = call(pack_kernel, on_chip(*group), IN_VMEM, [own] + got, [IN_VMEM] * far)
    parts = [near] + [swap_over(near, "grp", mask) for mask in middle_masks[1:]]
    parts = parts + [swap_over(part, "grp", 1) for part in parts]

    state, total, edges, profile = call(
        first_kernel,
        [state_shape, total_shape, edges_shape, plane],
        [IN_VMEM] * 4,
        [fwd_fields, adj_fields, source_pos],
        [IN_VMEM, IN_VMEM, IN_SMEM],
    )
    state = call(
        take_kernel, state_shape, IN_VMEM, [state, below, above], [IN_VMEM] * 3, aliases={0: 0}
    )
    coef, blocks, base = call(
        functools.partial(coef_edge_kernel, layout, len(parts)),
        [coef_shape, blocks_shape, plane],
        [IN_VMEM] * 3,
        parts + [block_ids, material_idx, material_eps],
        [IN_VMEM] * len(parts) + [IN_SMEM] * 3,
        [padded],
    )

    about = [source_pos, drives, profile]
    about_specs = [IN_SMEM, IN_SMEM, IN_VMEM]
    arrived = [[], []]
    for step in range(STEPS):
        more = npay if step < STEPS - 1 else 0
        for evo in range(2):
            state, edges, *pays = call(
                functools.partial(edge_kernel, step, evo),
                [state_shape, edges_shape] + [on_chip(2, width_x, width_y)] * more,
                [IN_VMEM] * (2 + more),
                [state, edges, coef] + about + arrived[evo],
                [IN_VMEM] * 3 + about_specs + [IN_VMEM] * len(arrived[evo]),
                aliases={0: 0, 1: 1},
            )
            if more:
                arrived[evo] = trade(pays)
        if step == 0:
            coef = call(
                coef_inner_kernel, coef_shape, IN_VMEM, [coef, blocks, base], [IN_VMEM] * 3,
                [padded], aliases={0: 0},
            )
        if more:
            state, total = call(
                functools.partial(inner_kernel, step + 1),
                [state_shape, total_shape],
                [IN_VMEM] * 2,
                [state, total, coef] + about,
                [IN_VMEM] * 3 + about_specs,
                aliases={0: 0, 1: 1},
            )

    def by_owner(values, skip):
        layers = values.shape[0] - 2 * skip
        shape = (far, layers * block_rows, width_y)
        parts = call(
            functools.partial(filter_kernel, layout, skip),
            [on_chip(*shape)] * len(layout),
            [IN_VMEM] * len(layout),
            [values, block_ids],
            [IN_VMEM, IN_SMEM],
            [pltpu.VMEM((nblock,) + shape[1:], F32), pltpu.VMEM((width_x, width_y), F32)],
        )
        got = [swap_over(part, "grp", 1) for part in parts[middle:]]
        sums = call(
            add_kernel,
            [on_chip(*shape)] * middle,
            [IN_VMEM] * middle,
            list(parts[:middle]) + got,
            [IN_VMEM] * (2 * middle),
        )
        return [sums[0]] + [
            swap_over(part, "grp", mask) for part, mask in zip(sums[1:], middle_masks[1:])
        ]

    inner = by_owner(total, 1)
    ends = by_owner(edges, 0)
    pieces = call(
        functools.partial(join_kernel, middle, block_rows),
        [on_chip(*piece)] * far,
        [IN_VMEM] * far,
        inner + ends,
        [IN_VMEM] * (2 * middle),
    )
    got = [swap_over(part, "grp", mask) for part, mask in zip(pieces[1:], far_masks[1:])]
    scale = 3.0 / (STEPS * math.sqrt(ngrp))
    grad = call(
        functools.partial(last_kernel, scale),
        jax.ShapeDtypeStruct(piece, F32),
        IN_VMEM,
        [pieces[0]] + got,
        [IN_VMEM] * far,
    )
    finals = call(
        out_kernel,
        jax.ShapeDtypeStruct(fwd_fields.shape, F32),
        IN_HBM,
        [state],
        [IN_VMEM],
        [
            pltpu.VMEM((3, depth, width_x, width_y), F32),
            pltpu.SemaphoreType.DMA((6,)),
        ],
    )
    return finals, grad.reshape(density.shape)


def solution(mesh):
    placed = (
        P("grp", None, "slab", None, None),
        P("grp", None, "slab", None, None),
        P("slab", "grp", None),
        P(),
        P(),
        P(),
        P("grp", None),
        P("grp"),
    )
    return jax.shard_map(
        per_device,
        mesh=mesh,
        in_specs=placed,
        out_specs=(P("grp", None, "slab", None, None), P("slab", "grp", None)),
        check_vma=False,
    )
```

time: 196 us -> 64.5 us (0.33)
  waiting for transfers between devices: 88 us -> 12.6 us
  other arithmetic: 29.4 us -> 0.05 us
  Pallas kernels: 0 us -> 25 us
  blocking collectives: 24.6 us -> 0 us
  local copies, waits for them, and re-layouts: 22.4 us -> 1.25 us
  between operations: 15.9 us -> 1.64 us
  starting transfers between devices: 14.7 us -> 23.7 us
    reduce_scatter x1 -> x0, waiting for transfers between devices: 48.9 us -> none  [per_device(): lax.psum_scatter(filter_xy(total).reshape(depth, nblock, block_rows, widt...]
    ppermute x8 -> x22, waiting for transfers between devices: 39.1 us -> 12.6 us  [swap_over(): lax.ppermute(array, axis, [(i, i ^ mask) for i in range(lax.axis_size(axi...]
    pallas_call x0 -> x24, Pallas kernels: none -> 25 us  [call(): pl.pallas_call(kernel, out_shape=outs, in_specs=specs, out_specs=out_spec...]
    all_gather x1 -> x0, blocking collectives: 24.6 us -> none  [per_device(): owned = lax.all_gather(density, 'grp', axis=1, tiled=True)]
    add x7 -> x0, other arithmetic: 10 us -> none  [the longest x4 5.87 us: per_device(): ez = ez + coef * (bwd_diff(hy, 2) - bwd_diff(hx, 3)) + drive]
    ppermute x8 -> x22, starting transfers between devices: 14.7 us -> 23.7 us  [swap_over(): lax.ppermute(array, axis, [(i, i ^ mask) for i in range(lax.axis_size(axi...]
    another operation x19 -> x0, local copies, waits for them, and re-layouts: 8.02 us -> none  [the longest x4 7.04 us: per_device(): comps = [jnp.stack([fwd_fields[0, c], adj_fields[0, c]]) for c in range(6)]]
    unnamed x57 -> x12, local copies, waits for them, and re-layouts: 6.87 us -> 1.25 us
  transfers between devices with their start and end apart: 9 -> 22, of which waited for: 8 -> 9; matrix products, arithmetic and copies ran while one was open for 12% -> 0% of each run, Pallas kernels for 0% -> 36%
where the time goes in v3:
time: 64.5 us; the launch traced here: 64.2 us
  Pallas kernels  25 us (39%)
  starting transfers between devices  23.7 us (37%)
  waiting for transfers between devices  12.6 us (20%)
  between operations  1.64 us (3%)
  local copies, waits for them, and re-layouts  1.25 us (2%)
    pallas_call x24, Pallas kernels, call(): pl.pallas_call(kernel, out_shape=outs, in_specs=specs, out_specs=out_spec...  25 us
    ppermute x22, starting transfers between devices, swap_over(): lax.ppermute(array, axis, [(i, i ^ mask) for i in range(lax.axis_size(axi...  23.7 us
    ppermute x22, waiting for transfers between devices, swap_over(): lax.ppermute(array, axis, [(i, i ^ mask) for i in range(lax.axis_size(axi...  12.6 us
  transfers between devices with their start and end apart: 22, of which 9 were waited for; matrix products, arithmetic and copies ran while one was open for 0% of the time, Pallas kernels for 36%

profile of v3, /device:TPU:0, one launch (start us, length us, event | category | flops | bytes accessed | tf_op | source)
XLA Modules:
  0.0 64.2 jit_solution(15390836288565036708)
XLA Ops:
  0.6 5.1 %collective-permute-start.3 = (f32[64,128]{1,0:T(8,128)}, f32[64,128]{1,0:T(8,128)S(1)}, u32[]{:S(2)}, u32[]{:S(2)}) collective-permute-start(f32[64,128]{1,0:T(8,128)} %bitcast.3), channel_id=1, source_target_pairs={{0,24},{2,26},{4,28},{6,30},{8,16},{10,18},{12,20},{14,22},{16,8},... | collective-permute-start | bytes 98312 | tf_op jit(solution)/shard_map/ppermute | solution.py:465
  6.4 1.4 %shard_map.96 = (f32[64,128]{1,0:T(8,128)S(1)}, f32[2,2,128,128]{3,2,1,0:T(8,128)S(1)}) custom-call(f32[1,6,8,128,128]{4,3,2,1,0:T(8,128)} %fwd.3, f32[1,6,8,128,128]{4,3,2,1,0:T(8,128)} %adj.3, f32[64,128]{1,0:T(8,128)} %bitcast.6), custom_call_target="tpu_custom_call" | custom-call | tf_op jit(solution)/shard_map/pallas_call | solution.py:35
  7.8 1.4 %collective-permute-start = (f32[2,2,128,128]{3,2,1,0:T(8,128)S(1)}, f32[2,2,128,128]{3,2,1,0:T(8,128)S(1)}, u32[]{:S(2)}, u32[]{:S(2)}) collective-permute-start(f32[2,2,128,128]{3,2,1,0:T(8,128)S(1)} %get-tuple-element.56), channel_id=1, source_target_pairs={{0,1},{1,0},{2,3},{3,2},{4,5},{5,4},{6,7},{7,6},{8,9},{9,8},{10,11... | collective-permute-start | bytes 786440 | tf_op jit(solution)/shard_map/ppermute | solution.py:465
  9.2 1.6 %collective-permute-done.2.refs_2_ = f32[64,128]{1,0:T(8,128)S(1)} collective-permute-done((f32[64,128]{1,0:T(8,128)}, f32[64,128]{1,0:T(8,128)S(1)}, u32[]{:S(2)}, u32[]{:S(2)}) %collective-permute-start.2) | collective-permute-done | bytes 32800 | tf_op jit(solution)/shard_map/ppermute | solution.py:465
  10.8 1.6 %collective-permute-start.4 = (f32[4,64,128]{2,1,0:T(8,128)S(1)}, f32[4,64,128]{2,1,0:T(8,128)S(1)}, u32[]{:S(2)}, u32[]{:S(2)}) collective-permute-start(f32[4,64,128]{2,1,0:T(8,128)S(1)} %shard_map.98.refs_0_), channel_id=1, source_target_pairs={{0,4},{2,6},{4,0},{6,2},{8,12},{10,14},{12,8},{14,10},{16,20},{18,... | collective-permute-start | bytes 393224 | tf_op jit(solution)/shard_map/ppermute | solution.py:465
  12.4 3.5 %collective-permute-done.4.refs_1_ = f32[4,64,128]{2,1,0:T(8,128)S(1)} collective-permute-done((f32[4,64,128]{2,1,0:T(8,128)S(1)}, f32[4,64,128]{2,1,0:T(8,128)S(1)}, u32[]{:S(2)}, u32[]{:S(2)}) %collective-permute-start.4) | collective-permute-done | bytes 131104 | tf_op jit(solution)/shard_map/ppermute | solution.py:465
  17.2 2.2 %shard_map.95 = (f32[2,6,9,144,128]{4,3,2,1,0:T(8,128)S(1)}, f32[8,144,128]{2,1,0:T(8,128)S(1)}, f32[2,144,128]{2,1,0:T(8,128)S(1)}, f32[128,128]{1,0:T(8,128)S(1)}) custom-call(f32[1,6,8,128,128]{4,3,2,1,0:T(8,128)S(1)} %copy-done, f32[1,6,8,128,128]{4,3,2,1,0:T(8,128)S(1)} %copy-done.1, s32[1,3]{1,0:T(1,128)S(1)} %copy-done.2), custom_call_target="tpu_custom_call" | custom-call | tf_op jit(solution)/shard_map/pallas_call | solution.py:35
  20.2 0.8 %shard_map.99 = (f32[8,128,128]{2,1,0:T(8,128)S(1)}, f32[16,64,128]{2,1,0:T(8,128)S(1)}, f32[128,128]{1,0:T(8,128)S(1)}) custom-call(f32[4,64,128]{2,1,0:T(8,128)S(1)} %shard_map.98.refs_0_, f32[4,64,128]{2,1,0:T(8,128)S(1)} %collective-permute-done.4.refs_1_, f32[4,64,128]{2,1,0:T(8,128)S(1)} %collective-permute-done.5.refs_2_, ...), custom_call_target="tpu_custom_call" | custom-call | tf_op jit(solution)/shard_map/pallas_call | solution.py:35
  21.0 0.8 %shard_map.100 = (f32[2,6,9,144,128]{4,3,2,1,0:T(8,128)S(1)}, f32[2,144,128]{2,1,0:T(8,128)S(1)}, f32[2,128,128]{2,1,0:T(8,128)S(1)}) custom-call(f32[2,6,9,144,128]{4,3,2,1,0:T(8,128)S(1)} %shard_map.97.state_in, f32[2,144,128]{2,1,0:T(8,128)S(1)} %get-tuple-element.57.edges_in, ...), custom_call_target="tpu_custom_call", output_to_operand_aliasing={{0}: (0, {}), {1}: (1, {})} | custom-call | tf_op jit(solution)/shard_map/pallas_call | solution.py:35
  21.8 1.6 %collective-permute-start.7 = (f32[2,128,128]{2,1,0:T(8,128)S(1)}, f32[2,128,128]{2,1,0:T(8,128)S(1)}, u32[]{:S(2)}, u32[]{:S(2)}) collective-permute-start(f32[2,128,128]{2,1,0:T(8,128)S(1)} %get-tuple-element.69), channel_id=1, source_target_pairs={{0,1},{1,0},{2,3},{3,2},{4,5},{5,4},{6,7},{7,6},{8,9},{9,8},{10,11... | collective-permute-start | bytes 393224 | tf_op jit(solution)/shard_map/ppermute | solution.py:465
  23.4 0.8 %shard_map.101 = (f32[2,6,9,144,128]{4,3,2,1,0:T(8,128)S(1)}, f32[2,144,128]{2,1,0:T(8,128)S(1)}, f32[2,128,128]{2,1,0:T(8,128)S(1)}) custom-call(f32[2,6,9,144,128]{4,3,2,1,0:T(8,128)S(1)} %get-tuple-element.61.state_in, f32[2,144,128]{2,1,0:T(8,128)S(1)} %get-tuple-element.62.edges_in, ...), custom_call_target="tpu_custom_call", output_to_operand_aliasing={{0}: (0, {}), {1}: (1, {})} | custom-call | tf_op jit(solution)/shard_map/pallas_call | solution.py:35
  25.5 3.8 %shard_map.103 = (f32[2,6,9,144,128]{4,3,2,1,0:T(8,128)S(1)}, f32[8,144,128]{2,1,0:T(8,128)S(1)}) custom-call(f32[2,6,9,144,128]{4,3,2,1,0:T(8,128)S(1)} %get-tuple-element.63.state_in, f32[8,144,128]{2,1,0:T(8,128)S(1)} %get-tuple-element.64.total_in, f32[8,128,128]{2,1,0:T(8,128)S(1)} %shard_map.102.coef, ...), custom_call_target="tpu_custom_call", output_to_operand_aliasing={{0}: (0, {}), {1}: (1, {})} | custom-call | tf_op jit(solution)/shard_map/pallas_call | solution.py:35
  29.3 0.8 %shard_map.104 = (f32[2,6,9,144,128]{4,3,2,1,0:T(8,128)S(1)}, f32[2,144,128]{2,1,0:T(8,128)S(1)}, f32[2,128,128]{2,1,0:T(8,128)S(1)}) custom-call(f32[2,6,9,144,128]{4,3,2,1,0:T(8,128)S(1)} %get-tuple-element.67.state_in, f32[2,144,128]{2,1,0:T(8,128)S(1)} %get-tuple-element.68.edges_in, ...), custom_call_target="tpu_custom_call", output_to_operand_aliasing={{0}: (0, {}), {1}: (1, {})} | custom-call | tf_op jit(solution)/shard_map/pallas_call | solution.py:35
  30.2 1.6 %collective-permute-start.9 = (f32[2,128,128]{2,1,0:T(8,128)S(1)}, f32[2,128,128]{2,1,0:T(8,128)S(1)}, u32[]{:S(2)}, u32[]{:S(2)}) collective-permute-start(f32[2,128,128]{2,1,0:T(8,128)S(1)} %get-tuple-element.77), channel_id=1, source_target_pairs={{0,1},{1,0},{2,3},{3,2},{4,5},{5,4},{6,7},{7,6},{8,9},{9,8},{10,11... | collective-permute-start | bytes 393224 | tf_op jit(solution)/shard_map/ppermute | solution.py:465
  31.8 0.8 %shard_map.105 = (f32[2,6,9,144,128]{4,3,2,1,0:T(8,128)S(1)}, f32[2,144,128]{2,1,0:T(8,128)S(1)}, f32[2,128,128]{2,1,0:T(8,128)S(1)}) custom-call(f32[2,6,9,144,128]{4,3,2,1,0:T(8,128)S(1)} %get-tuple-element.70.state_in, f32[2,144,128]{2,1,0:T(8,128)S(1)} %get-tuple-element.71.edges_in, ...), custom_call_target="tpu_custom_call", output_to_operand_aliasing={{0}: (0, {}), {1}: (1, {})} | custom-call | tf_op jit(solution)/shard_map/pallas_call | solution.py:35
  33.2 2.6 %shard_map.106 = (f32[2,6,9,144,128]{4,3,2,1,0:T(8,128)S(1)}, f32[8,144,128]{2,1,0:T(8,128)S(1)}) custom-call(f32[2,6,9,144,128]{4,3,2,1,0:T(8,128)S(1)} %get-tuple-element.73.state_in, f32[8,144,128]{2,1,0:T(8,128)S(1)} %get-tuple-element.74.total_in, f32[8,128,128]{2,1,0:T(8,128)S(1)} %shard_map.102.coef, ...), custom_call_target="tpu_custom_call", output_to_operand_aliasing={{0}: (0, {}), {1}: (1, {})} | custom-call | tf_op jit(solution)/shard_map/pallas_call | solution.py:35
  36.3 0.8 %shard_map.107 = (f32[2,6,9,144,128]{4,3,2,1,0:T(8,128)S(1)}, f32[2,144,128]{2,1,0:T(8,128)S(1)}, f32[2,128,128]{2,1,0:T(8,128)S(1)}) custom-call(f32[2,6,9,144,128]{4,3,2,1,0:T(8,128)S(1)} %get-tuple-element.75.state_in, f32[2,144,128]{2,1,0:T(8,128)S(1)} %get-tuple-element.76.edges_in, ...), custom_call_target="tpu_custom_call", output_to_operand_aliasing={{0}: (0, {}), {1}: (1, {})} | custom-call | tf_op jit(solution)/shard_map/pallas_call | solution.py:35
  37.1 1.9 %collective-permute-start.11 = (f32[2,128,128]{2,1,0:T(8,128)S(1)}, f32[2,128,128]{2,1,0:T(8,128)S(1)}, u32[]{:S(2)}, u32[]{:S(2)}) collective-permute-start(f32[2,128,128]{2,1,0:T(8,128)S(1)} %get-tuple-element.85), channel_id=1, source_target_pairs={{0,1},{1,0},{2,3},{3,2},{4,5},{5,4},{6,7},{7,6},{8,9},{9,8},{10,11... | collective-permute-start | bytes 393224 | tf_op jit(solution)/shard_map/ppermute | solution.py:465
  39.0 0.8 %shard_map.108 = (f32[2,6,9,144,128]{4,3,2,1,0:T(8,128)S(1)}, f32[2,144,128]{2,1,0:T(8,128)S(1)}, f32[2,128,128]{2,1,0:T(8,128)S(1)}) custom-call(f32[2,6,9,144,128]{4,3,2,1,0:T(8,128)S(1)} %get-tuple-element.78.state_in, f32[2,144,128]{2,1,0:T(8,128)S(1)} %get-tuple-element.79.edges_in, ...), custom_call_target="tpu_custom_call", output_to_operand_aliasing={{0}: (0, {}), {1}: (1, {})} | custom-call | tf_op jit(solution)/shard_map/pallas_call | solution.py:35
  39.9 0.9 %collective-permute-start.12 = (f32[2,128,128]{2,1,0:T(8,128)S(1)}, f32[2,128,128]{2,1,0:T(8,128)S(1)}, u32[]{:S(2)}, u32[]{:S(2)}) collective-permute-start(f32[2,128,128]{2,1,0:T(8,128)S(1)} %get-tuple-element.88), channel_id=1, source_target_pairs={{0,1},{1,0},{2,3},{3,2},{4,5},{5,4},{6,7},{7,6},{8,9},{9,8},{10,11... | collective-permute-start | bytes 393224 | tf_op jit(solution)/shard_map/ppermute | solution.py:465
  40.8 2.6 %shard_map.109 = (f32[2,6,9,144,128]{4,3,2,1,0:T(8,128)S(1)}, f32[8,144,128]{2,1,0:T(8,128)S(1)}) custom-call(f32[2,6,9,144,128]{4,3,2,1,0:T(8,128)S(1)} %get-tuple-element.81.state_in, f32[8,144,128]{2,1,0:T(8,128)S(1)} %get-tuple-element.82.total_in, f32[8,128,128]{2,1,0:T(8,128)S(1)} %shard_map.102.coef, ...), custom_call_target="tpu_custom_call", output_to_operand_aliasing={{0}: (0, {}), {1}: (1, {})} | custom-call | tf_op jit(solution)/shard_map/pallas_call | solution.py:35
  43.4 1.2 %shard_map.113 = (f32[4,48,128]{2,1,0:T(8,128)S(1)}, f32[4,48,128]{2,1,0:T(8,128)S(1)}, f32[4,48,128]{2,1,0:T(8,128)S(1)}, f32[4,48,128]{2,1,0:T(8,128)S(1)}) custom-call(f32[8,144,128]{2,1,0:T(8,128)S(1)} %get-tuple-element.90.total, s32[16]{0:T(128)S(1)} %copy-done.3), custom_call_target="tpu_custom_call" | custom-call | tf_op jit(solution)/shard_map/pallas_call | solution.py:35
  45.2 0.8 %collective-permute-done.13.refs_2_ = f32[4,48,128]{2,1,0:T(8,128)S(1)} collective-permute-done((f32[4,48,128]{2,1,0:T(8,128)S(1)}, f32[4,48,128]{2,1,0:T(8,128)S(1)}, u32[]{:S(2)}, u32[]{:S(2)}) %collective-permute-start.13) | collective-permute-done | bytes 98336 | tf_op jit(solution)/shard_map/ppermute | solution.py:465
  46.2 1.6 %collective-permute-start.15 = (f32[4,48,128]{2,1,0:T(8,128)S(1)}, f32[4,48,128]{2,1,0:T(8,128)S(1)}, u32[]{:S(2)}, u32[]{:S(2)}) collective-permute-start(f32[4,48,128]{2,1,0:T(8,128)S(1)} %get-tuple-element.96), channel_id=1, source_target_pairs={{0,4},{2,6},{4,0},{6,2},{8,12},{10,14},{12,8},{14,10},{16,20},{18,... | collective-permute-start | bytes 294920 | tf_op jit(solution)/shard_map/ppermute | solution.py:465
  47.8 0.8 %shard_map.110 = (f32[2,6,9,144,128]{4,3,2,1,0:T(8,128)S(1)}, f32[2,144,128]{2,1,0:T(8,128)S(1)}) custom-call(f32[2,6,9,144,128]{4,3,2,1,0:T(8,128)S(1)} %get-tuple-element.83.state_in, f32[2,144,128]{2,1,0:T(8,128)S(1)} %get-tuple-element.84.edges_in, f32[8,128,128]{2,1,0:T(8,128)S(1)} %shard_map.102.coef, ...), custom_call_target="tpu_custom_call", output_to_operand_aliasing={{0}: (0, {}), {1}: (1, {})} | custom-call | tf_op jit(solution)/shard_map/pallas_call | solution.py:35
  48.6 0.8 %shard_map.111 = (f32[2,6,9,144,128]{4,3,2,1,0:T(8,128)S(1)}, f32[2,144,128]{2,1,0:T(8,128)S(1)}) custom-call(f32[2,6,9,144,128]{4,3,2,1,0:T(8,128)S(1)} %get-tuple-element.86.state_in, f32[2,144,128]{2,1,0:T(8,128)S(1)} %get-tuple-element.87.edges_in, f32[8,128,128]{2,1,0:T(8,128)S(1)} %shard_map.102.coef, ...), custom_call_target="tpu_custom_call", output_to_operand_aliasing={{0}: (0, {}), {1}: (1, {})} | custom-call | tf_op jit(solution)/shard_map/pallas_call | solution.py:35
  49.4 0.8 %shard_map.115 = (f32[4,16,128]{2,1,0:T(8,128)S(1)}, f32[4,16,128]{2,1,0:T(8,128)S(1)}, f32[4,16,128]{2,1,0:T(8,128)S(1)}, f32[4,16,128]{2,1,0:T(8,128)S(1)}) custom-call(f32[2,144,128]{2,1,0:T(8,128)S(1)} %get-tuple-element.97.total, s32[16]{0:T(128)S(1)} %copy-done.3), custom_call_target="tpu_custom_call" | custom-call | tf_op jit(solution)/shard_map/pallas_call | solution.py:35
  52.2 3.4 %collective-permute-done.18.refs_3_ = f32[4,16,128]{2,1,0:T(8,128)S(1)} collective-permute-done((f32[4,16,128]{2,1,0:T(8,128)S(1)}, f32[4,16,128]{2,1,0:T(8,128)S(1)}, u32[]{:S(2)}, u32[]{:S(2)}) %collective-permute-start.18) | collective-permute-done | bytes 32800 | tf_op jit(solution)/shard_map/ppermute | solution.py:465
  55.7 2.2 %collective-permute-start.20 = (f32[64,128]{1,0:T(8,128)S(1)}, f32[64,128]{1,0:T(8,128)S(1)}, u32[]{:S(2)}, u32[]{:S(2)}) collective-permute-start(f32[64,128]{1,0:T(8,128)S(1)} %get-tuple-element.106), channel_id=1, source_target_pairs={{0,16},{2,18},{4,20},{6,22},{8,24},{10,26},{12,28},{14,30},{16,0},... | collective-permute-start | bytes 98312 | tf_op jit(solution)/shard_map/ppermute | solution.py:465
  57.9 2.1 %collective-permute-start.21 = (f32[64,128]{1,0:T(8,128)S(1)}, f32[64,128]{1,0:T(8,128)S(1)}, u32[]{:S(2)}, u32[]{:S(2)}) collective-permute-start(f32[64,128]{1,0:T(8,128)S(1)} %get-tuple-element.107), channel_id=1, source_target_pairs={{0,24},{2,26},{4,28},{6,30},{8,16},{10,18},{12,20},{14,22},{16,8},... | collective-permute-start | bytes 98312 | tf_op jit(solution)/shard_map/ppermute | solution.py:465
  60.1 1.7 %shard_map.112 = f32[1,6,8,128,128]{4,3,2,1,0:T(8,128)} custom-call(f32[2,6,9,144,128]{4,3,2,1,0:T(8,128)S(1)} %get-tuple-element.89.state), custom_call_target="tpu_custom_call" | custom-call | tf_op jit(solution)/shard_map/pallas_call | solution.py:35
  61.8 1.8 %collective-permute-done.21.refs_3_ = f32[64,128]{1,0:T(8,128)S(1)} collective-permute-done((f32[64,128]{1,0:T(8,128)S(1)}, f32[64,128]{1,0:T(8,128)S(1)}, u32[]{:S(2)}, u32[]{:S(2)}) %collective-permute-start.21) | collective-permute-done | bytes 32800 | tf_op jit(solution)/shard_map/ppermute | solution.py:465
  (49 shorter events, 7.9 us)
Async XLA Ops:
  0.6 15.9 %copy-start.1 = (f32[1,6,8,128,128]{4,3,2,1,0:T(8,128)S(1)}, f32[1,6,8,128,128]{4,3,2,1,0:T(8,128)}, u32[]{:S(2)}) copy-start(f32[1,6,8,128,128]{4,3,2,1,0:T(8,128)} %adj.3) | copy-start | bytes 9437188
  0.6 15.9 %copy-start = (f32[1,6,8,128,128]{4,3,2,1,0:T(8,128)S(1)}, f32[1,6,8,128,128]{4,3,2,1,0:T(8,128)}, u32[]{:S(2)}) copy-start(f32[1,6,8,128,128]{4,3,2,1,0:T(8,128)} %fwd.3) | copy-start | bytes 9437188
  0.6 8.6 %collective-permute-start.3 = (f32[64,128]{1,0:T(8,128)}, f32[64,128]{1,0:T(8,128)S(1)}, u32[]{:S(2)}, u32[]{:S(2)}) collective-permute-start(f32[64,128]{1,0:T(8,128)} %bitcast.3), channel_id=1, source_target_pairs={{0,24},{2,26},{4,28},{6,30},{8,16},{10,18},{12,20},{14,22},{16,8},... | collective-permute-start | bytes 98312 | tf_op jit(solution)/shard_map/ppermute | solution.py:465
  5.8 5.0 %collective-permute-start.2 = (f32[64,128]{1,0:T(8,128)}, f32[64,128]{1,0:T(8,128)S(1)}, u32[]{:S(2)}, u32[]{:S(2)}) collective-permute-start(f32[64,128]{1,0:T(8,128)} %bitcast.4), channel_id=1, source_target_pairs={{0,16},{2,18},{4,20},{6,22},{8,24},{10,26},{12,28},{14,30},{16,0},... | collective-permute-start | bytes 98312 | tf_op jit(solution)/shard_map/ppermute | solution.py:465
  5.8 5.0 %collective-permute-start.1 = (f32[64,128]{1,0:T(8,128)}, f32[64,128]{1,0:T(8,128)S(1)}, u32[]{:S(2)}, u32[]{:S(2)}) collective-permute-start(f32[64,128]{1,0:T(8,128)} %bitcast.5), channel_id=1, source_target_pairs={{0,8},{2,10},{4,12},{6,14},{8,0},{10,2},{12,4},{14,6},{16,24},{18,... | collective-permute-start | bytes 98312 | tf_op jit(solution)/shard_map/ppermute | solution.py:465
  7.8 11.7 %collective-permute-start = (f32[2,2,128,128]{3,2,1,0:T(8,128)S(1)}, f32[2,2,128,128]{3,2,1,0:T(8,128)S(1)}, u32[]{:S(2)}, u32[]{:S(2)}) collective-permute-start(f32[2,2,128,128]{3,2,1,0:T(8,128)S(1)} %get-tuple-element.56), channel_id=1, source_target_pairs={{0,1},{1,0},{2,3},{3,2},{4,5},{5,4},{6,7},{7,6},{8,9},{9,8},{10,11... | collective-permute-start | bytes 786440 | tf_op jit(solution)/shard_map/ppermute | solution.py:465
  10.8 5.0 %collective-permute-start.4 = (f32[4,64,128]{2,1,0:T(8,128)S(1)}, f32[4,64,128]{2,1,0:T(8,128)S(1)}, u32[]{:S(2)}, u32[]{:S(2)}) collective-permute-start(f32[4,64,128]{2,1,0:T(8,128)S(1)} %shard_map.98.refs_0_), channel_id=1, source_target_pairs={{0,4},{2,6},{4,0},{6,2},{8,12},{10,14},{12,8},{14,10},{16,20},{18,... | collective-permute-start | bytes 393224 | tf_op jit(solution)/shard_map/ppermute | solution.py:465
  12.4 7.2 %collective-permute-start.5 = (f32[4,64,128]{2,1,0:T(8,128)S(1)}, f32[4,64,128]{2,1,0:T(8,128)S(1)}, u32[]{:S(2)}, u32[]{:S(2)}) collective-permute-start(f32[4,64,128]{2,1,0:T(8,128)S(1)} %shard_map.98.refs_0_), channel_id=1, source_target_pairs={{0,2},{2,0},{4,6},{6,4},{8,10},{10,8},{12,14},{14,12},{16,18},{18,... | collective-permute-start | bytes 393224 | tf_op jit(solution)/shard_map/ppermute | solution.py:465
  15.8 3.8 %collective-permute-start.6 = (f32[4,64,128]{2,1,0:T(8,128)S(1)}, f32[4,64,128]{2,1,0:T(8,128)S(1)}, u32[]{:S(2)}, u32[]{:S(2)}) collective-permute-start(f32[4,64,128]{2,1,0:T(8,128)S(1)} %collective-permute-done.4.refs_1_), channel_id=1, source_target_pairs={{0,2},{2,0},{4,6},{6,4},{8,10},{10,8},{12,14},{14,12},{16,18},{18,... | collective-permute-start | bytes 393224 | tf_op jit(solution)/shard_map/ppermute | solution.py:465
  16.5 0.7 %copy-start.2 = (s32[1,3]{1,0:T(1,128)S(1)}, s32[1,3]{1,0:T(1,128)}, u32[]{:S(2)}) copy-start(s32[1,3]{1,0:T(1,128)} %source.23) | copy-start | bytes 40
  19.5 0.7 %copy-start.3 = (s32[16]{0:T(128)S(1)}, s32[16]{0:T(128)}, u32[]{:S(2)}) copy-start(s32[16]{0:T(128)} %block_ids.3) | copy-start | bytes 196
  19.5 0.7 %copy-start.4 = (s32[16]{0:T(128)S(1)}, s32[16]{0:T(128)}, u32[]{:S(2)}) copy-start(s32[16]{0:T(128)} %refs_5_.1) | copy-start | bytes 196
  19.5 0.7 %copy-start.5 = (f32[4]{0:T(128)S(1)}, f32[4]{0:T(128)}, u32[]{:S(2)}) copy-start(f32[4]{0:T(128)} %refs_6_.1) | copy-start | bytes 52
  21.8 7.5 %collective-permute-start.7 = (f32[2,128,128]{2,1,0:T(8,128)S(1)}, f32[2,128,128]{2,1,0:T(8,128)S(1)}, u32[]{:S(2)}, u32[]{:S(2)}) collective-permute-start(f32[2,128,128]{2,1,0:T(8,128)S(1)} %get-tuple-element.69), channel_id=1, source_target_pairs={{0,1},{1,0},{2,3},{3,2},{4,5},{5,4},{6,7},{7,6},{8,9},{9,8},{10,11... | collective-permute-start | bytes 393224 | tf_op jit(solution)/shard_map/ppermute | solution.py:465
  24.2 7.6 %collective-permute-start.8 = (f32[2,128,128]{2,1,0:T(8,128)S(1)}, f32[2,128,128]{2,1,0:T(8,128)S(1)}, u32[]{:S(2)}, u32[]{:S(2)}) collective-permute-start(f32[2,128,128]{2,1,0:T(8,128)S(1)} %get-tuple-element.72), channel_id=1, source_target_pairs={{0,1},{1,0},{2,3},{3,2},{4,5},{5,4},{6,7},{7,6},{8,9},{9,8},{10,11... | collective-permute-start | bytes 393224 | tf_op jit(solution)/shard_map/ppermute | solution.py:465
  30.2 6.1 %collective-permute-start.9 = (f32[2,128,128]{2,1,0:T(8,128)S(1)}, f32[2,128,128]{2,1,0:T(8,128)S(1)}, u32[]{:S(2)}, u32[]{:S(2)}) collective-permute-start(f32[2,128,128]{2,1,0:T(8,128)S(1)} %get-tuple-element.77), channel_id=1, source_target_pairs={{0,1},{1,0},{2,3},{3,2},{4,5},{5,4},{6,7},{7,6},{8,9},{9,8},{10,11... | collective-permute-start | bytes 393224 | tf_op jit(solution)/shard_map/ppermute | solution.py:465
  32.6 6.5 %collective-permute-start.10 = (f32[2,128,128]{2,1,0:T(8,128)S(1)}, f32[2,128,128]{2,1,0:T(8,128)S(1)}, u32[]{:S(2)}, u32[]{:S(2)}) collective-permute-start(f32[2,128,128]{2,1,0:T(8,128)S(1)} %get-tuple-element.80), channel_id=1, source_target_pairs={{0,1},{1,0},{2,3},{3,2},{4,5},{5,4},{6,7},{7,6},{8,9},{9,8},{10,11... | collective-permute-start | bytes 393224 | tf_op jit(solution)/shard_map/ppermute | solution.py:465
  37.1 10.7 %collective-permute-start.11 = (f32[2,128,128]{2,1,0:T(8,128)S(1)}, f32[2,128,128]{2,1,0:T(8,128)S(1)}, u32[]{:S(2)}, u32[]{:S(2)}) collective-permute-start(f32[2,128,128]{2,1,0:T(8,128)S(1)} %get-tuple-element.85), channel_id=1, source_target_pairs={{0,1},{1,0},{2,3},{3,2},{4,5},{5,4},{6,7},{7,6},{8,9},{9,8},{10,11... | collective-permute-start | bytes 393224 | tf_op jit(solution)/shard_map/ppermute | solution.py:465
  39.9 8.7 %collective-permute-start.12 = (f32[2,128,128]{2,1,0:T(8,128)S(1)}, f32[2,128,128]{2,1,0:T(8,128)S(1)}, u32[]{:S(2)}, u32[]{:S(2)}) collective-permute-start(f32[2,128,128]{2,1,0:T(8,128)S(1)} %get-tuple-element.88), channel_id=1, source_target_pairs={{0,1},{1,0},{2,3},{3,2},{4,5},{5,4},{6,7},{7,6},{8,9},{9,8},{10,11... | collective-permute-start | bytes 393224 | tf_op jit(solution)/shard_map/ppermute | solution.py:465
  44.7 1.4 %collective-permute-start.13 = (f32[4,48,128]{2,1,0:T(8,128)S(1)}, f32[4,48,128]{2,1,0:T(8,128)S(1)}, u32[]{:S(2)}, u32[]{:S(2)}) collective-permute-start(f32[4,48,128]{2,1,0:T(8,128)S(1)} %get-tuple-element.93), channel_id=1, source_target_pairs={{0,2},{2,0},{4,6},{6,4},{8,10},{10,8},{12,14},{14,12},{16,18},{18,... | collective-permute-start | bytes 294920 | tf_op jit(solution)/shard_map/ppermute | solution.py:465
  44.7 1.4 %collective-permute-start.14 = (f32[4,48,128]{2,1,0:T(8,128)S(1)}, f32[4,48,128]{2,1,0:T(8,128)S(1)}, u32[]{:S(2)}, u32[]{:S(2)}) collective-permute-start(f32[4,48,128]{2,1,0:T(8,128)S(1)} %get-tuple-element.94), channel_id=1, source_target_pairs={{0,2},{2,0},{4,6},{6,4},{8,10},{10,8},{12,14},{14,12},{16,18},{18,... | collective-permute-start | bytes 294920 | tf_op jit(solution)/shard_map/ppermute | solution.py:465
  46.2 6.0 %collective-permute-start.15 = (f32[4,48,128]{2,1,0:T(8,128)S(1)}, f32[4,48,128]{2,1,0:T(8,128)S(1)}, u32[]{:S(2)}, u32[]{:S(2)}) collective-permute-start(f32[4,48,128]{2,1,0:T(8,128)S(1)} %get-tuple-element.96), channel_id=1, source_target_pairs={{0,4},{2,6},{4,0},{6,2},{8,12},{10,14},{12,8},{14,10},{16,20},{18,... | collective-permute-start | bytes 294920 | tf_op jit(solution)/shard_map/ppermute | solution.py:465
  50.2 1.3 %collective-permute-start.16 = (f32[4,16,128]{2,1,0:T(8,128)S(1)}, f32[4,16,128]{2,1,0:T(8,128)S(1)}, u32[]{:S(2)}, u32[]{:S(2)}) collective-permute-start(f32[4,16,128]{2,1,0:T(8,128)S(1)} %get-tuple-element.100), channel_id=1, source_target_pairs={{0,2},{2,0},{4,6},{6,4},{8,10},{10,8},{12,14},{14,12},{16,18},{18,... | collective-permute-start | bytes 98312 | tf_op jit(solution)/shard_map/ppermute | solution.py:465
  50.3 1.3 %collective-permute-start.17 = (f32[4,16,128]{2,1,0:T(8,128)S(1)}, f32[4,16,128]{2,1,0:T(8,128)S(1)}, u32[]{:S(2)}, u32[]{:S(2)}) collective-permute-start(f32[4,16,128]{2,1,0:T(8,128)S(1)} %get-tuple-element.101), channel_id=1, source_target_pairs={{0,2},{2,0},{4,6},{6,4},{8,10},{10,8},{12,14},{14,12},{16,18},{18,... | collective-permute-start | bytes 98312 | tf_op jit(solution)/shard_map/ppermute | solution.py:465
  51.6 4.0 %collective-permute-start.18 = (f32[4,16,128]{2,1,0:T(8,128)S(1)}, f32[4,16,128]{2,1,0:T(8,128)S(1)}, u32[]{:S(2)}, u32[]{:S(2)}) collective-permute-start(f32[4,16,128]{2,1,0:T(8,128)S(1)} %get-tuple-element.103), channel_id=1, source_target_pairs={{0,4},{2,6},{4,0},{6,2},{8,12},{10,14},{12,8},{14,10},{16,20},{18,... | collective-permute-start | bytes 98312 | tf_op jit(solution)/shard_map/ppermute | solution.py:465
  55.6 6.2 %collective-permute-start.19 = (f32[64,128]{1,0:T(8,128)S(1)}, f32[64,128]{1,0:T(8,128)S(1)}, u32[]{:S(2)}, u32[]{:S(2)}) collective-permute-start(f32[64,128]{1,0:T(8,128)S(1)} %get-tuple-element.105), channel_id=1, source_target_pairs={{0,8},{2,10},{4,12},{6,14},{8,0},{10,2},{12,4},{14,6},{16,24},{18,... | collective-permute-start | bytes 98312 | tf_op jit(solution)/shard_map/ppermute | solution.py:465
  55.7 6.1 %collective-permute-start.20 = (f32[64,128]{1,0:T(8,128)S(1)}, f32[64,128]{1,0:T(8,128)S(1)}, u32[]{:S(2)}, u32[]{:S(2)}) collective-permute-start(f32[64,128]{1,0:T(8,128)S(1)} %get-tuple-element.106), channel_id=1, source_target_pairs={{0,16},{2,18},{4,20},{6,22},{8,24},{10,26},{12,28},{14,30},{16,0},... | collective-permute-start | bytes 98312 | tf_op jit(solution)/shard_map/ppermute | solution.py:465
  57.9 5.7 %collective-permute-start.21 = (f32[64,128]{1,0:T(8,128)S(1)}, f32[64,128]{1,0:T(8,128)S(1)}, u32[]{:S(2)}, u32[]{:S(2)}) collective-permute-start(f32[64,128]{1,0:T(8,128)S(1)} %get-tuple-element.107), channel_id=1, source_target_pairs={{0,24},{2,26},{4,28},{6,30},{8,16},{10,18},{12,20},{14,22},{16,8},... | collective-permute-start | bytes 98312 | tf_op jit(solution)/shard_map/ppermute | solution.py:465

commit v4 on v3

v4 whole, which is shorter than its diff:
```python
import functools
import math

import jax
import jax.numpy as jnp
from jax import lax
from jax.experimental import pallas as pl
from jax.experimental.pallas import tpu as pltpu
from jax.sharding import PartitionSpec as P

STEPS = 4
AMPLITUDE = 4.0
PAD = 8
F32 = jnp.float32

VMEM = pltpu.MemorySpace.VMEM
IN_VMEM = pl.BlockSpec(memory_space=pltpu.VMEM)
IN_SMEM = pl.BlockSpec(memory_space=pltpu.SMEM)
IN_HBM = pl.BlockSpec(memory_space=pltpu.MemorySpace.HBM)


def on_chip(*shape):
    return VMEM(shape, F32)


def held(array, spec):
    if spec is IN_SMEM:
        return array
    space = VMEM if spec is IN_VMEM else pltpu.MemorySpace.HBM
    return pltpu.with_memory_space_constraint(array, space)


def call(kernel, outs, out_specs, operands, specs, scratch=(), aliases=None, flops=0):
    operands = [held(a, s) for a, s in zip(operands, specs)]
    return pl.pallas_call(
        kernel,
        out_shape=outs,
        in_specs=specs,
        out_specs=out_specs,
        scratch_shapes=scratch,
        input_output_aliases=aliases or {},
        compiler_params=pltpu.CompilerParams(vmem_limit_bytes=8 << 20),
        cost_estimate=pl.CostEstimate(flops=flops, bytes_accessed=flops // 4, transcendentals=0),
    )(*operands)


CHUNK = 16


def chunks(rows):
    size = CHUNK if rows % CHUNK == 0 else rows
    return [(first, size) for first in range(0, rows, size)]


def next_col(value):
    column = lax.broadcasted_iota(jnp.int32, value.shape, 1)
    moved = pltpu.roll(value, value.shape[1] - 1, 1)
    return jnp.where(column == value.shape[1] - 1, 0.0, moved)


def prev_col(value):
    column = lax.broadcasted_iota(jnp.int32, value.shape, 1)
    return jnp.where(column == 0, 0.0, pltpu.roll(value, 1, 1))


class Window:
    def __init__(self, e, h, coef=None, total=None, source=None, drives=None, profile=None):
        self.e, self.h, self.coef, self.total = e, h, coef, total
        self.source, self.drives, self.profile = source, drives, profile
        self.rows = e.shape[3] - 2 * PAD
        self.depth = e.shape[2] - 1
        self.top, self.under = self.depth - 1, self.depth
        self.slab = lax.axis_index("slab")
        self.has_up = self.slab < lax.axis_size("slab") - 1
        self.has_low = self.slab > 0

    def read_e(self, evo, layer, first, size, shift=0):
        rows = pl.ds(PAD + first + shift, size)
        return [self.e[evo, c, layer, rows, :] for c in range(3)]

    def read_h(self, evo, layer, first, size, shift=0):
        rows = pl.ds(PAD + first + shift, size)
        return [self.h[evo, c, layer, rows, :] for c in range(3)]

    def write(self, ref, evo, layer, first, size, values):
        for c, value in enumerate(values):
            ref[evo, c, layer, pl.ds(PAD + first, size), :] = value

    def put_h(self, evo, layer, double=False):
        for first, size in chunks(self.rows):
            rows = pl.ds(PAD + first, size)
            after = pl.ds(PAD + first + 1, size)
            ex, ey, ez = self.read_e(evo, layer, first, size)
            hx, hy, hz = self.read_h(evo, layer, first, size)
            if double:
                hx, hy, hz = hx + hx, hy + hy, hz + hz
            rise_x = self.e[evo, 0, layer + 1, rows, :] - ex
            rise_y = self.e[evo, 1, layer + 1, rows, :] - ey
            ey_after = self.e[evo, 1, layer, after, :]
            ez_after = self.e[evo, 2, layer, after, :]
            hx = hx - ((next_col(ez) - ez) - rise_y)
            hy = hy - (rise_x - (ez_after - ez))
            hz = hz - ((ey_after - ey) - (next_col(ex) - ex))
            self.write(self.h, evo, layer, first, size, (hx, hy, hz))

    def put_top_h(self, evo):
        layer = self.top
        for first, size in chunks(self.rows):
            after = pl.ds(PAD + first + 1, size)
            ex, ey, ez = self.read_e(evo, layer, first, size)
            hx, hy, hz = self.read_h(evo, layer, first, size)
            ey_after = self.e[evo, 1, layer, after, :]
            ez_after = self.e[evo, 2, layer, after, :]
            hx = hx - ((next_col(ez) - ez) + ey)
            hy = hy + (ex + (ez_after - ez))
            hz = hz - ((ey_after - ey) - (next_col(ex) - ex))
            self.write(self.h, evo, layer, first, size, (hx, hy, hz))

    def curl_h(self, evo, layer, lower, first, size):
        rows = pl.ds(PAD + first, size)
        before = pl.ds(PAD + first - 1, size)
        hx, hy, hz = self.read_h(evo, layer, first, size)
        step_x = hx - self.h[evo, 0, lower, rows, :]
        step_y = hy - self.h[evo, 1, lower, rows, :]
        hy_before = self.h[evo, 1, layer, before, :]
        hz_before = self.h[evo, 2, layer, before, :]
        return (
            (hz - prev_col(hz)) - step_y,
            step_x - (hz - hz_before),
            (hy - hy_before) - (hx - prev_col(hx)),
        )

    def drive(self, step, layer):
        @pl.when(self.source[0, 0] - self.slab * self.depth == layer)
        def _():
            amount = self.drives[step]
            for first, size in chunks(self.rows):
                here = pl.ds(PAD + first, size)
                self.e[0, 2, layer, here, :] += amount * self.profile[pl.ds(first, size), :]

    def next_e(self, evo, layer, lower, first, size, curls):
        cell = self.coef[layer, pl.ds(first, size), :]
        if curls is None:
            curl = self.curl_h(evo, layer, lower, first, size)
        else:
            curl = [curls[evo, c, layer, pl.ds(first, size), :] for c in range(3)]
        old = self.read_e(evo, layer, first, size)
        return [a + cell * b for a, b in zip(old, curl)]

    def put_e(self, evo, layer, lower, step, curls=None):
        if evo == 0:
            self.drive(step, layer)
        for first, size in chunks(self.rows):
            news = self.next_e(evo, layer, lower, first, size, curls)
            self.write(self.e, evo, layer, first, size, news)

    def put_both_e(self, layer, lower, curls=None):
        for first, size in chunks(self.rows):
            fwd, adj = (self.next_e(evo, layer, lower, first, size, curls) for evo in range(2))
            self.write(self.e, 0, layer, first, size, fwd)
            self.write(self.e, 1, layer, first, size, adj)
            part = fwd[0] * adj[0] + fwd[1] * adj[1] + fwd[2] * adj[2]
            self.total[layer, pl.ds(PAD + first, size), :] += part

    def add_edge(self, edges, slot, layer):
        for first, size in chunks(self.rows):
            part = edges[slot, pl.ds(PAD + first, size), :]
            for fwd, adj in zip(
                self.read_e(0, layer, first, size), self.read_e(1, layer, first, size)
            ):
                part += fwd * adj
            edges[slot, pl.ds(PAD + first, size), :] = part

    def take_above(self, evo, above):
        for first, size in chunks(self.rows):
            here, rows = pl.ds(first, size), pl.ds(PAD + first, size)
            self.h[evo, 0, self.top, rows, :] += above[1, here, :]
            self.h[evo, 1, self.top, rows, :] -= above[0, here, :]

    def take_below(self, evo, below):
        for first, size in chunks(self.rows):
            here, rows = pl.ds(first, size), pl.ds(PAD + first, size)
            self.h[evo, 0, self.under, rows, :] = below[0, here, :] + self.e[evo, 1, 0, rows, :]
            self.h[evo, 1, self.under, rows, :] = below[1, here, :] - self.e[evo, 0, 0, rows, :]


def opening_kernel(fwd, adj, density, own, *rest):
    pays, (planes, sems) = rest[:-2], rest[-2:]
    depth, rows, width_y = fwd.shape[2:]
    top = depth - 1
    slab = lax.axis_index("slab")
    has_up, has_low = slab < lax.axis_size("slab") - 1, slab > 0
    held_copy = pltpu.make_async_copy(density, own, sems.at[2, 0])
    held_copy.start()

    def up(pay):
        copies = []
        for evo, given in enumerate((fwd, adj)):
            for c in range(5):
                copies.append(
                    pltpu.make_async_copy(given.at[0, c, top], planes.at[evo, c], sems.at[evo, c])
                )
        for copy in copies:
            copy.start()
        for copy in copies:
            copy.wait()
        for evo in range(2):
            for first, size in chunks(rows):
                here = pl.ds(first, size)
                ex, ey, ez, hx, hy = (planes[evo, c, here, :] for c in range(5))
                if first + size < rows:
                    ez_after = planes[evo, 2, pl.ds(first + 1, size), :]
                else:
                    row = lax.broadcasted_iota(jnp.int32, ez.shape, 0)
                    ez_after = jnp.where(row == size - 1, 0.0, pltpu.roll(ez, size - 1, 0))
                pay[evo, 0, here, :] = (hx + hx) - ((next_col(ez) - ez) + ey)
                pay[evo, 1, here, :] = (hy + hy) + (ex + (ez_after - ez))

    def down(pay):
        copies = []
        for evo, given in enumerate((fwd, adj)):
            for c in range(2):
                copies.append(
                    pltpu.make_async_copy(given.at[0, c, 0], pay.at[evo, c], sems.at[evo, c])
                )
        for copy in copies:
            copy.start()
        for copy in copies:
            copy.wait()

    if len(pays) == 2:
        up(pays[0])
        down(pays[1])
    else:
        pl.when(has_up)(lambda: up(pays[0]))
        pl.when(has_low)(lambda: down(pays[0]))
    held_copy.wait()


def first_kernel(fwd, adj, near, source, e, h, total, edges, profile, curls, sems):
    win = Window(e, h)
    rows, width_y = win.rows, e.shape[4]
    copies = ([], [])
    for evo, given in enumerate((fwd, adj)):
        for comp in range(6):
            ref = e if comp < 3 else h
            copies[evo].append(
                pltpu.make_async_copy(
                    given.at[0, comp],
                    ref.at[evo, comp % 3, pl.ds(0, win.depth), pl.ds(PAD, rows), :],
                    sems.at[evo, comp],
                )
            )
    for copy in copies[0] + copies[1]:
        copy.start()
    margin = jnp.zeros((PAD, width_y), F32)
    empty = jnp.zeros((rows + 2 * PAD, width_y), F32)

    def clear(layer, carry):
        for ref in (e, h):
            for evo in range(2):
                for comp in range(3):
                    ref[evo, comp, layer, pl.ds(0, PAD), :] = margin
                    ref[evo, comp, layer, pl.ds(PAD + rows, PAD), :] = margin
        total[layer] = empty
        return carry

    lax.fori_loop(0, win.depth, clear, 0)
    for evo in range(2):
        for comp in range(3):
            e[evo, comp, win.depth] = empty
            h[evo, comp, win.depth] = empty
        edges[evo] = empty
    xcoord = lax.broadcasted_iota(jnp.int32, (rows, width_y), 0)
    ycoord = lax.broadcasted_iota(jnp.int32, (rows, width_y), 1)
    offset_x = (xcoord - source[0, 1]).astype(F32) / (rows / 4.0)
    offset_y = (ycoord - source[0, 2]).astype(F32) / (width_y / 4.0)
    profile[...] = jnp.exp(-0.5 * (offset_x * offset_x + offset_y * offset_y))
    for evo in range(2):
        for copy in copies[evo]:
            copy.wait()
        win.put_h(evo, 0, True)
        win.put_h(evo, 1, True)

        def body(layer, carry, evo=evo):
            win.put_h(evo, layer + 1, True)
            put_curl(win, curls, evo, layer, layer - 1)
            return carry

        lax.fori_loop(1, win.top, body, 0)


def put_curl(win, curls, evo, layer, lower):
    for first, size in chunks(win.rows):
        for c, value in enumerate(win.curl_h(evo, layer, lower, first, size)):
            curls[evo, c, layer, pl.ds(first, size), :] = value


def take_kernel(h_in, curls_in, e, below, above, h, curls):
    win = Window(e, h)
    for evo in range(2):
        pl.when(win.has_up)(lambda: win.take_above(evo, above.at[evo]))
        pl.when(win.has_low)(lambda: win.take_below(evo, below.at[evo]))
    for evo in range(2):
        put_curl(win, curls, evo, win.top, win.top - 1)
        put_curl(win, curls, evo, 0, win.under)


def edge_kernel(step, evo, e_in, h_in, edges_in, coef, source, drives, profile, *rest):
    rest = list(rest)
    curls = rest.pop(0) if step == 0 else None
    below, above = [rest.pop(0) for _ in range(2)] if step > 0 else (None, None)
    e, h, edges = rest[:3]
    pays = rest[3:]
    win = Window(e, h, coef, None, source, drives, profile)
    top = win.top

    @pl.when(win.has_up)
    def _():
        if step > 0:
            win.take_above(evo, above)
        win.put_e(evo, top, top - 1, step, curls)
        if pays:
            win.put_top_h(evo)
            for c in range(2):
                pays[0][c] = h[evo, c, top, pl.ds(PAD, win.rows), :]
        if evo == 1:
            win.add_edge(edges, 1, top)

    @pl.when(win.has_low)
    def _():
        if step > 0:
            win.take_below(evo, below)
        win.put_e(evo, 0, win.under, step, curls)
        if pays:
            for c in range(2):
                pays[-1][c] = e[evo, c, 0, pl.ds(PAD, win.rows), :]
        if evo == 1:
            win.add_edge(edges, 0, 0)


def inner_kernel(step, e_in, h_in, total_in, coef, source, drives, profile, *rest):
    rest = list(rest)
    curls = rest.pop(0) if step == 1 else None
    e, h, total = rest
    win = Window(e, h, coef, total, source, drives, profile)
    lowest = jnp.where(win.has_low, 1, 0)
    highest = jnp.where(win.has_up, win.top - 1, win.top)

    def first(layer, carry):
        win.drive(0, layer)
        win.put_both_e(layer, None, curls)
        return carry

    if step == 1:
        lax.fori_loop(lowest, highest + 1, first, 0)
    for evo in range(2):
        win.put_h(evo, 0)

    @pl.when(win.has_low)
    def _():
        for evo in range(2):
            win.put_h(evo, 1)

    def body(layer, carry):
        win.drive(step, layer)
        for evo in range(2):
            win.put_h(evo, layer + 1)
        win.put_both_e(layer, jnp.where(layer == 0, win.under, layer - 1))
        return carry

    lax.fori_loop(lowest, highest, body, 0)
    win.drive(step, highest)
    win.put_both_e(highest, highest - 1)


def coef_layer(layer, coef, blocks, placed, base):
    nblock = blocks.shape[0]
    rows = base.shape[0]
    block_rows = rows // nblock
    for block in range(nblock):
        source = pl.ds(pl.multiple_of(layer * block_rows, block_rows), block_rows)
        placed[pl.ds(PAD + block * block_rows, block_rows), :] = blocks[block, source, :]
    for first, size in chunks(rows):
        here = pl.ds(first, size)
        coef[layer, here, :] = 0.25 / (base[here, :] + 3.0 * filtered(placed, first, size))


def coef_edge_kernel(layout, count, *refs):
    parts = refs[:count]
    block_ids, material_idx, material_eps, coef, blocks, base, placed = refs[count:]
    nblock = blocks.shape[0]
    depth, rows, width_y = coef.shape
    block_rows = rows // nblock
    me = lax.axis_index("grp")
    for part, masks in zip(parts, layout):
        for slot, mask in enumerate(masks):
            blocks[block_ids[me ^ mask]] = part[slot]
    for block in range(nblock):
        level = jnp.full((block_rows, width_y), material_eps[material_idx[block]], F32)
        base[pl.ds(block * block_rows, block_rows), :] = level
    placed[pl.ds(0, PAD), :] = jnp.zeros((PAD, width_y), F32)
    placed[pl.ds(PAD + rows, PAD), :] = jnp.zeros((PAD, width_y), F32)
    coef_layer(0, coef, blocks, placed, base)
    coef_layer(depth - 1, coef, blocks, placed, base)


def coef_inner_kernel(coef_in, blocks, base, coef, placed):
    depth, rows, width_y = coef.shape
    placed[pl.ds(0, PAD), :] = jnp.zeros((PAD, width_y), F32)
    placed[pl.ds(PAD + rows, PAD), :] = jnp.zeros((PAD, width_y), F32)

    def body(layer, carry):
        coef_layer(layer, coef, blocks, placed, base)
        return carry

    lax.fori_loop(1, depth - 1, body, 0)


def filtered(padded, first, size):
    here = padded[pl.ds(PAD + first, size), :]
    before = padded[pl.ds(PAD + first - 1, size), :]
    after = padded[pl.ds(PAD + first + 1, size), :]
    along = before + 2.0 * here + after
    return (prev_col(along) + 2.0 * along + next_col(along)) * 0.0625


def pack_kernel(*refs):
    out = refs[-1]
    for slot, ref in enumerate(refs[:-1]):
        out[slot] = ref[...]


def filter_layer(values, layer, blocks, wide):
    nblock = blocks.shape[0]
    rows = wide.shape[0]
    block_rows = rows // nblock
    for first, size in chunks(rows):
        wide[pl.ds(first, size), :] = filtered(values, first, size)
    for block in range(nblock):
        target = pl.ds(pl.multiple_of(layer * block_rows, block_rows), block_rows)
        blocks[block, target, :] = wide[pl.ds(block * block_rows, block_rows), :]


def filter_inner_kernel(total, blocks, wide):
    def body(layer, carry):
        filter_layer(total.at[layer], layer, blocks, wide)
        return carry

    lax.fori_loop(1, total.shape[0] - 1, body, 0)


def filter_edge_kernel(layout, blocks_in, total, edges, block_ids, blocks, *rest):
    parts, wide, ends = rest[:-2], rest[-2], rest[-1]
    me = lax.axis_index("grp")
    for slot, layer in enumerate((0, total.shape[0] - 1)):
        ends[slot] = total[layer] + edges[slot]
        filter_layer(ends.at[slot], layer, blocks, wide.at[slot])
    for part, masks in zip(parts, layout):
        for slot, mask in enumerate(masks):
            part[slot] = blocks[block_ids[me ^ mask]]


def add_kernel(*refs):
    half = len(refs) // 3
    for a, b, out in zip(refs[:half], refs[half : 2 * half], refs[2 * half :]):
        out[...] = a[...] + b[...]


def add_split_kernel(count, *refs):
    terms, outs = refs[:count], refs[count:]
    for slot, out in enumerate(outs):
        value = terms[0][slot]
        for term in terms[1:]:
            value = value + term[slot]
        out[...] = value


def last_kernel(scale, *refs):
    value = refs[0][...]
    for ref in refs[1:-1]:
        value = value + ref[...]
    refs[-1][...] = value * scale


def out_kernel(e, h, finals, halves, sems):
    depth = e.shape[2] - 1
    rows = e.shape[3] - 2 * PAD
    every = pl.ds(PAD, rows)
    copies = [
        pltpu.make_async_copy(
            e.at[0, c, pl.ds(0, depth), every, :], finals.at[0, c], sems.at[c]
        )
        for c in range(3)
    ]
    for copy in copies:
        copy.start()
    for c in range(3):

        def body(layer, carry, c=c):
            halves[c, layer] = 0.5 * h[0, c, layer, every, :]
            return carry

        lax.fori_loop(0, depth, body, 0)
        copy = pltpu.make_async_copy(halves.at[c], finals.at[0, 3 + c], sems.at[3 + c])
        copy.start()
        copies.append(copy)
    for copy in copies:
        copy.wait()


def swap_over(array, axis, mask):
    return lax.ppermute(array, axis, [(i, i ^ mask) for i in range(lax.axis_size(axis))])


def shift_over(array, axis, distance):
    size = lax.axis_size(axis)
    route = [(i, i + distance) for i in range(size) if 0 <= i + distance < size]
    return lax.ppermute(array, axis, route)


def trade(pays):
    if len(pays) == 1:
        return [swap_over(pays[0], "slab", 1)] * 2
    return [shift_over(pays[0], "slab", 1), shift_over(pays[1], "slab", -1)]


def per_device(
    fwd_fields, adj_fields, density, block_ids, material_idx, material_eps, source_pos, wave_idx
):
    depth, width_x, width_y = fwd_fields.shape[2:]
    nblock = block_ids.shape[0]
    block_rows = width_x // nblock
    ngrp = lax.axis_size("grp")
    npay = 1 if lax.axis_size("slab") == 2 else 2
    omega = 2.0 * math.pi / (6.0 + 2.0 * wave_idx[0].astype(F32))
    drives = AMPLITUDE * jnp.sin(omega * (jnp.arange(STEPS, dtype=F32) + 1.0))

    far = 4
    middle = ngrp // (2 * far)
    far_masks = [2 * middle * j for j in range(far)]
    middle_masks = [2 * j for j in range(middle)]
    layout = [
        [core + mid + top for top in far_masks] for core in (0, 1) for mid in middle_masks
    ]
    piece = (depth * block_rows, width_y)
    group = (far,) + piece

    field_shape = on_chip(2, 3, depth + 1, width_x + 2 * PAD, width_y)
    curls_shape = on_chip(2, 3, depth, width_x, width_y)
    total_shape = on_chip(depth, width_x + 2 * PAD, width_y)
    edges_shape = on_chip(2, width_x + 2 * PAD, width_y)
    coef_shape = on_chip(depth, width_x, width_y)
    blocks_shape = on_chip(nblock, *piece)
    plane = on_chip(width_x, width_y)
    padded = pltpu.VMEM((width_x + 2 * PAD, width_y), F32)

    design = density.reshape(piece)
    got = [swap_over(design, "grp", mask) for mask in far_masks[1:]]
    own, *pays = call(
        opening_kernel,
        [on_chip(*piece)] + [on_chip(2, 2, width_x, width_y)] * npay,
        [IN_VMEM] * (1 + npay),
        [fwd_fields, adj_fields, design],
        [IN_HBM] * 3,
        [pltpu.VMEM((2, 5, width_x, width_y), F32), pltpu.SemaphoreType.DMA((3, 5))],
    )
    below, above = trade(pays)

    near = call(pack_kernel, on_chip(*group), IN_VMEM, [own] + got, [IN_VMEM] * far)
    parts = [near] + [swap_over(near, "grp", mask) for mask in middle_masks[1:]]
    parts = parts + [swap_over(part, "grp", 1) for part in parts]

    e, h, total, edges, profile, curls = call(
        first_kernel,
        [field_shape, field_shape, total_shape, edges_shape, plane, curls_shape],
        [IN_VMEM] * 6,
        [fwd_fields, adj_fields, near, source_pos],
        [IN_HBM, IN_HBM, IN_VMEM, IN_SMEM],
        [pltpu.SemaphoreType.DMA((2, 6))],
    )
    h, curls = call(
        take_kernel,
        [field_shape, curls_shape],
        [IN_VMEM] * 2,
        [h, curls, e, below, above],
        [IN_VMEM] * 5,
        aliases={0: 0, 1: 1},
    )
    coef, blocks, base = call(
        functools.partial(coef_edge_kernel, layout, len(parts)),
        [coef_shape, blocks_shape, plane],
        [IN_VMEM] * 3,
        parts + [block_ids, material_idx, material_eps],
        [IN_VMEM] * len(parts) + [IN_SMEM] * 3,
        [padded],
    )

    about = [source_pos, drives, profile]
    about_specs = [IN_SMEM, IN_SMEM, IN_VMEM]
    arrived = [[curls], [curls]]
    for step in range(STEPS):
        more = npay if step < STEPS - 1 else 0
        for evo in range(2):
            e, h, edges, *pays = call(
                functools.partial(edge_kernel, step, evo),
                [field_shape, field_shape, edges_shape] + [on_chip(2, width_x, width_y)] * more,
                [IN_VMEM] * (3 + more),
                [e, h, edges, coef] + about + arrived[evo],
                [IN_VMEM] * 4 + about_specs + [IN_VMEM] * len(arrived[evo]),
                aliases={0: 0, 1: 1, 2: 2},
            )
            if more:
                arrived[evo] = trade(pays)
        if step == 0:
            coef = call(
                coef_inner_kernel, coef_shape, IN_VMEM, [coef, blocks, base], [IN_VMEM] * 3,
                [padded], aliases={0: 0},
            )
        if more:
            late = [curls] if step == 0 else []
            e, h, total = call(
                functools.partial(inner_kernel, step + 1),
                [field_shape, field_shape, total_shape],
                [IN_VMEM] * 3,
                [e, h, total, coef] + about + late,
                [IN_VMEM] * 4 + about_specs + [IN_VMEM] * len(late),
                aliases={0: 0, 1: 1, 2: 2},
            )
        if step == STEPS - 2:
            blocks = call(
                filter_inner_kernel, blocks_shape, IN_VMEM, [total], [IN_VMEM],
                [pltpu.VMEM((width_x, width_y), F32)],
            )

    blocks, *parts = call(
        functools.partial(filter_edge_kernel, layout),
        [blocks_shape] + [on_chip(*group)] * len(layout),
        [IN_VMEM] * (1 + len(layout)),
        [blocks, total, edges, block_ids],
        [IN_VMEM] * 3 + [IN_SMEM],
        [
            pltpu.VMEM((2, width_x, width_y), F32),
            pltpu.VMEM((2, width_x + 2 * PAD, width_y), F32),
        ],
        aliases={0: 0},
    )
    got = [swap_over(part, "grp", 1) for part in parts[middle:]]
    sums = call(
        add_kernel,
        [on_chip(*group)] * middle,
        [IN_VMEM] * middle,
        list(parts[:middle]) + got,
        [IN_VMEM] * (2 * middle),
    )
    got = [swap_over(part, "grp", mask) for part, mask in zip(sums[1:], middle_masks[1:])]
    pieces = call(
        functools.partial(add_split_kernel, middle),
        [on_chip(*piece)] * far,
        [IN_VMEM] * far,
        [sums[0]] + got,
        [IN_VMEM] * middle,
    )
    got = [swap_over(part, "grp", mask) for part, mask in zip(pieces[1:], far_masks[1:])]
    scale = 3.0 / (STEPS * math.sqrt(ngrp))
    grad = call(
        functools.partial(last_kernel, scale),
        jax.ShapeDtypeStruct(piece, F32),
        IN_VMEM,
        [pieces[0]] + got,
        [IN_VMEM] * far,
    )
    finals = call(
        out_kernel,
        jax.ShapeDtypeStruct(fwd_fields.shape, F32),
        IN_HBM,
        [e, h],
        [IN_VMEM] * 2,
        [
            pltpu.VMEM((3, depth, width_x, width_y), F32),
            pltpu.SemaphoreType.DMA((6,)),
        ],
    )
    return finals, grad.reshape(density.shape)


def solution(mesh):
    placed = (
        P("grp", None, "slab", None, None),
        P("grp", None, "slab", None, None),
        P("slab", "grp", None),
        P(),
        P(),
        P(),
        P("grp", None),
        P("grp"),
    )
    return jax.shard_map(
        per_device,
        mesh=mesh,
        in_specs=placed,
        out_specs=(P("grp", None, "slab", None, None), P("slab", "grp", None)),
        check_vma=False,
    )
```

time: 64.5 us -> 63.5 us (0.984)
  local copies, waits for them, and re-layouts: 1.25 us -> 0.38 us
    unnamed x12 -> x8, local copies, waits for them, and re-layouts: 1.25 us -> 0.38 us
    ppermute x22 -> x19, starting transfers between devices: 23.7 us -> 23.1 us  [swap_over(): lax.ppermute(array, axis, [(i, i ^ mask) for i in range(lax.axis_size(axi...]
    ppermute x22 -> x19, waiting for transfers between devices: 12.6 us -> 13 us  [swap_over(): lax.ppermute(array, axis, [(i, i ^ mask) for i in range(lax.axis_size(axi...]
    pallas_call x24 -> x23, Pallas kernels: 25 us -> 25.2 us  [call(): pl.pallas_call(kernel, out_shape=outs, in_specs=specs, out_specs=out_spec...]
  transfers between devices with their start and end apart: 22 -> 19, of which waited for: 9 -> 7; matrix products, arithmetic and copies ran while one was open for 0% -> 0% of each run, Pallas kernels for 36% -> 34%
where the time goes in v4:
time: 63.5 us; the launch traced here: 63.3 us
  Pallas kernels  25.2 us (40%)
  starting transfers between devices  23.1 us (36%)
  waiting for transfers between devices  13 us (20%)
  between operations  1.61 us (3%)
    pallas_call x23, Pallas kernels, call(): pl.pallas_call(kernel, out_shape=outs, in_specs=specs, out_specs=out_spec...  25.2 us
    ppermute x19, starting transfers between devices, swap_over(): lax.ppermute(array, axis, [(i, i ^ mask) for i in range(lax.axis_size(axi...  23.1 us
    ppermute x19, waiting for transfers between devices, swap_over(): lax.ppermute(array, axis, [(i, i ^ mask) for i in range(lax.axis_size(axi...  13 us
  transfers between devices with their start and end apart: 19, of which 7 were waited for; matrix products, arithmetic and copies ran while one was open for 0% of the time, Pallas kernels for 34%

profile of v4, /device:TPU:0, one launch (start us, length us, event | category | flops | bytes accessed | tf_op | source)
XLA Modules:
  0.0 63.3 jit_solution(11528785542526790472)
XLA Ops:
  0.6 5.1 %collective-permute-start.2 = (f32[64,128]{1,0:T(8,128)}, f32[64,128]{1,0:T(8,128)S(1)}, u32[]{:S(2)}, u32[]{:S(2)}) collective-permute-start(f32[64,128]{1,0:T(8,128)} %bitcast.3), channel_id=1, source_target_pairs={{0,24},{2,26},{4,28},{6,30},{8,16},{10,18},{12,20},{14,22},{16,8},... | collective-permute-start | bytes 98312 | tf_op jit(solution)/shard_map/ppermute | solution.py:513
  6.4 1.4 %shard_map.95 = (f32[64,128]{1,0:T(8,128)S(1)}, f32[2,2,128,128]{3,2,1,0:T(8,128)S(1)}) custom-call(f32[1,6,8,128,128]{4,3,2,1,0:T(8,128)} %fwd.3, f32[1,6,8,128,128]{4,3,2,1,0:T(8,128)} %adj.3, f32[64,128]{1,0:T(8,128)} %bitcast.6), custom_call_target="tpu_custom_call" | custom-call | tf_op jit(solution)/shard_map/pallas_call | solution.py:35
  7.8 1.4 %collective-permute-start.3 = (f32[2,2,128,128]{3,2,1,0:T(8,128)S(1)}, f32[2,2,128,128]{3,2,1,0:T(8,128)S(1)}, u32[]{:S(2)}, u32[]{:S(2)}) collective-permute-start(f32[2,2,128,128]{3,2,1,0:T(8,128)S(1)} %get-tuple-element.68), channel_id=1, source_target_pairs={{0,1},{1,0},{2,3},{3,2},{4,5},{5,4},{6,7},{7,6},{8,9},{9,8},{10,11... | collective-permute-start | bytes 786440 | tf_op jit(solution)/shard_map/ppermute | solution.py:513
  9.2 1.6 %collective-permute-done.1.refs_2_ = f32[64,128]{1,0:T(8,128)S(1)} collective-permute-done((f32[64,128]{1,0:T(8,128)}, f32[64,128]{1,0:T(8,128)S(1)}, u32[]{:S(2)}, u32[]{:S(2)}) %collective-permute-start.1) | collective-permute-done | bytes 32800 | tf_op jit(solution)/shard_map/ppermute | solution.py:513
  10.8 1.6 %collective-permute-start.4 = (f32[4,64,128]{2,1,0:T(8,128)S(1)}, f32[4,64,128]{2,1,0:T(8,128)S(1)}, u32[]{:S(2)}, u32[]{:S(2)}) collective-permute-start(f32[4,64,128]{2,1,0:T(8,128)S(1)} %shard_map.96.near.refs_0_), channel_id=1, source_target_pairs={{0,4},{2,6},{4,0},{6,2},{8,12},{10,14},{12,8},{14,10},{16,20},{18,... | collective-permute-start | bytes 393224 | tf_op jit(solution)/shard_map/ppermute | solution.py:513
  12.4 3.5 %collective-permute-done.4.refs_1_ = f32[4,64,128]{2,1,0:T(8,128)S(1)} collective-permute-done((f32[4,64,128]{2,1,0:T(8,128)S(1)}, f32[4,64,128]{2,1,0:T(8,128)S(1)}, u32[]{:S(2)}, u32[]{:S(2)}) %collective-permute-start.4) | collective-permute-done | bytes 131104 | tf_op jit(solution)/shard_map/ppermute | solution.py:513
  16.6 4.5 %shard_map.97 = (f32[2,3,9,144,128]{4,3,2,1,0:T(8,128)S(1)}, f32[2,3,9,144,128]{4,3,2,1,0:T(8,128)S(1)}, f32[8,144,128]{2,1,0:T(8,128)S(1)}, f32[2,144,128]{2,1,...) custom-call(f32[1,6,8,128,128]{4,3,2,1,0:T(8,128)} %fwd.3, f32[1,6,8,128,128]{4,3,2,1,0:T(8,128)} %adj.3, ...), custom_call_target="tpu_custom_call" | custom-call | tf_op jit(solution)/shard_map/pallas_call | solution.py:35
  21.8 0.8 %shard_map.99 = (f32[8,128,128]{2,1,0:T(8,128)S(1)}, f32[16,64,128]{2,1,0:T(8,128)S(1)}, f32[128,128]{1,0:T(8,128)S(1)}) custom-call(f32[4,64,128]{2,1,0:T(8,128)S(1)} %shard_map.96.near.refs_0_, f32[4,64,128]{2,1,0:T(8,128)S(1)} %collective-permute-done.4.refs_1_, f32[4,64,128]{2,1,0:T(8,128)S(1)} %collective-permute-done.5.refs_2_, ...), custom_call_target="tpu_custom_call" | custom-call | tf_op jit(solution)/shard_map/pallas_call | solution.py:35
  22.6 0.7 %shard_map.100 = (f32[2,3,9,144,128]{4,3,2,1,0:T(8,128)S(1)}, f32[2,3,9,144,128]{4,3,2,1,0:T(8,128)S(1)}, f32[2,144,128]{2,1,0:T(8,128)S(1)}, f32[2,128,128]{2,1,0:T(8,128)S(1)}) custom-call(f32[2,3,9,144,128]{4,3,2,1,0:T(8,128)S(1)} %get-tuple-element.65.e.e_in, ...), custom_call_target="tpu_custom_call", output_to_operand_aliasing={{0}: (0, {}), {1}: (1, {}), {2}: (2, {})} | custom-call | tf_op jit(solution)/shard_map/pallas_call | solution.py:35
  23.3 1.5 %collective-permute-start.7 = (f32[2,128,128]{2,1,0:T(8,128)S(1)}, f32[2,128,128]{2,1,0:T(8,128)S(1)}, u32[]{:S(2)}, u32[]{:S(2)}) collective-permute-start(f32[2,128,128]{2,1,0:T(8,128)S(1)} %get-tuple-element.85), channel_id=1, source_target_pairs={{0,1},{1,0},{2,3},{3,2},{4,5},{5,4},{6,7},{7,6},{8,9},{9,8},{10,11... | collective-permute-start | bytes 393224 | tf_op jit(solution)/shard_map/ppermute | solution.py:513
  24.8 0.7 %shard_map.101 = (f32[2,3,9,144,128]{4,3,2,1,0:T(8,128)S(1)}, f32[2,3,9,144,128]{4,3,2,1,0:T(8,128)S(1)}, f32[2,144,128]{2,1,0:T(8,128)S(1)}, f32[2,128,128]{2,1,0:T(8,128)S(1)}) custom-call(f32[2,3,9,144,128]{4,3,2,1,0:T(8,128)S(1)} %get-tuple-element.74.e_in, ...), custom_call_target="tpu_custom_call", output_to_operand_aliasing={{0}: (0, {}), {1}: (1, {}), {2}: (2, {})} | custom-call | tf_op jit(solution)/shard_map/pallas_call | solution.py:35
  26.0 0.8 %shard_map.102.coef = f32[8,128,128]{2,1,0:T(8,128)S(1)} custom-call(f32[8,128,128]{2,1,0:T(8,128)S(1)} %get-tuple-element.71.coef.coef_in, f32[16,64,128]{2,1,0:T(8,128)S(1)} %get-tuple-element.80.blocks, f32[128,128]{1,0:T(8,128)S(1)} %get-tuple-element.81.base), custom_call_target="tpu_custom_call", output_to_operand_aliasing={{}: (0, {})} | custom-call | tf_op jit(solution)/shard_map/pallas_call | solution.py:35
  26.8 3.0 %shard_map.103 = (f32[2,3,9,144,128]{4,3,2,1,0:T(8,128)S(1)}, f32[2,3,9,144,128]{4,3,2,1,0:T(8,128)S(1)}, f32[8,144,128]{2,1,0:T(8,128)S(1)}) custom-call(f32[2,3,9,144,128]{4,3,2,1,0:T(8,128)S(1)} %get-tuple-element.77.e_in, f32[2,3,9,144,128]{4,3,2,1,0:T(8,128)S(1)} %get-tuple-element.78.h_in, ...), custom_call_target="tpu_custom_call", output_to_operand_aliasing={{0}: (0, {}), {1}: (1, {}), {2}: (2, {})} | custom-call | tf_op jit(solution)/shard_map/pallas_call | solution.py:35
  29.8 0.8 %shard_map.104 = (f32[2,3,9,144,128]{4,3,2,1,0:T(8,128)S(1)}, f32[2,3,9,144,128]{4,3,2,1,0:T(8,128)S(1)}, f32[2,144,128]{2,1,0:T(8,128)S(1)}, f32[2,128,128]{2,1,0:T(8,128)S(1)}) custom-call(f32[2,3,9,144,128]{4,3,2,1,0:T(8,128)S(1)} %get-tuple-element.82.e_in, ...), custom_call_target="tpu_custom_call", output_to_operand_aliasing={{0}: (0, {}), {1}: (1, {}), {2}: (2, {})} | custom-call | tf_op jit(solution)/shard_map/pallas_call | solution.py:35
  30.6 1.6 %collective-permute-start.9 = (f32[2,128,128]{2,1,0:T(8,128)S(1)}, f32[2,128,128]{2,1,0:T(8,128)S(1)}, u32[]{:S(2)}, u32[]{:S(2)}) collective-permute-start(f32[2,128,128]{2,1,0:T(8,128)S(1)} %get-tuple-element.96), channel_id=1, source_target_pairs={{0,1},{1,0},{2,3},{3,2},{4,5},{5,4},{6,7},{7,6},{8,9},{9,8},{10,11... | collective-permute-start | bytes 393224 | tf_op jit(solution)/shard_map/ppermute | solution.py:513
  32.2 0.8 %shard_map.105 = (f32[2,3,9,144,128]{4,3,2,1,0:T(8,128)S(1)}, f32[2,3,9,144,128]{4,3,2,1,0:T(8,128)S(1)}, f32[2,144,128]{2,1,0:T(8,128)S(1)}, f32[2,128,128]{2,1,0:T(8,128)S(1)}) custom-call(f32[2,3,9,144,128]{4,3,2,1,0:T(8,128)S(1)} %get-tuple-element.86.e_in, ...), custom_call_target="tpu_custom_call", output_to_operand_aliasing={{0}: (0, {}), {1}: (1, {}), {2}: (2, {})} | custom-call | tf_op jit(solution)/shard_map/pallas_call | solution.py:35
  33.0 1.2 %collective-permute-start.10 = (f32[2,128,128]{2,1,0:T(8,128)S(1)}, f32[2,128,128]{2,1,0:T(8,128)S(1)}, u32[]{:S(2)}, u32[]{:S(2)}) collective-permute-start(f32[2,128,128]{2,1,0:T(8,128)S(1)} %get-tuple-element.100), channel_id=1, source_target_pairs={{0,1},{1,0},{2,3},{3,2},{4,5},{5,4},{6,7},{7,6},{8,9},{9,8},{10,11... | collective-permute-start | bytes 393224 | tf_op jit(solution)/shard_map/ppermute | solution.py:513
  34.2 2.5 %shard_map.106 = (f32[2,3,9,144,128]{4,3,2,1,0:T(8,128)S(1)}, f32[2,3,9,144,128]{4,3,2,1,0:T(8,128)S(1)}, f32[8,144,128]{2,1,0:T(8,128)S(1)}) custom-call(f32[2,3,9,144,128]{4,3,2,1,0:T(8,128)S(1)} %get-tuple-element.90.e_in, f32[2,3,9,144,128]{4,3,2,1,0:T(8,128)S(1)} %get-tuple-element.91.h_in, ...), custom_call_target="tpu_custom_call", output_to_operand_aliasing={{0}: (0, {}), {1}: (1, {}), {2}: (2, {})} | custom-call | tf_op jit(solution)/shard_map/pallas_call | solution.py:35
  36.7 0.8 %shard_map.107 = (f32[2,3,9,144,128]{4,3,2,1,0:T(8,128)S(1)}, f32[2,3,9,144,128]{4,3,2,1,0:T(8,128)S(1)}, f32[2,144,128]{2,1,0:T(8,128)S(1)}, f32[2,128,128]{2,1,0:T(8,128)S(1)}) custom-call(f32[2,3,9,144,128]{4,3,2,1,0:T(8,128)S(1)} %get-tuple-element.93.e_in, ...), custom_call_target="tpu_custom_call", output_to_operand_aliasing={{0}: (0, {}), {1}: (1, {}), {2}: (2, {})} | custom-call | tf_op jit(solution)/shard_map/pallas_call | solution.py:35
  37.5 1.8 %collective-permute-start.11 = (f32[2,128,128]{2,1,0:T(8,128)S(1)}, f32[2,128,128]{2,1,0:T(8,128)S(1)}, u32[]{:S(2)}, u32[]{:S(2)}) collective-permute-start(f32[2,128,128]{2,1,0:T(8,128)S(1)} %get-tuple-element.107), channel_id=1, source_target_pairs={{0,1},{1,0},{2,3},{3,2},{4,5},{5,4},{6,7},{7,6},{8,9},{9,8},{10,11... | collective-permute-start | bytes 393224 | tf_op jit(solution)/shard_map/ppermute | solution.py:513
  39.3 0.8 %shard_map.108 = (f32[2,3,9,144,128]{4,3,2,1,0:T(8,128)S(1)}, f32[2,3,9,144,128]{4,3,2,1,0:T(8,128)S(1)}, f32[2,144,128]{2,1,0:T(8,128)S(1)}, f32[2,128,128]{2,1,0:T(8,128)S(1)}) custom-call(f32[2,3,9,144,128]{4,3,2,1,0:T(8,128)S(1)} %get-tuple-element.97.e_in, ...), custom_call_target="tpu_custom_call", output_to_operand_aliasing={{0}: (0, {}), {1}: (1, {}), {2}: (2, {})} | custom-call | tf_op jit(solution)/shard_map/pallas_call | solution.py:35
  40.1 1.0 %collective-permute-start.12 = (f32[2,128,128]{2,1,0:T(8,128)S(1)}, f32[2,128,128]{2,1,0:T(8,128)S(1)}, u32[]{:S(2)}, u32[]{:S(2)}) collective-permute-start(f32[2,128,128]{2,1,0:T(8,128)S(1)} %get-tuple-element.111), channel_id=1, source_target_pairs={{0,1},{1,0},{2,3},{3,2},{4,5},{5,4},{6,7},{7,6},{8,9},{9,8},{10,11... | collective-permute-start | bytes 393224 | tf_op jit(solution)/shard_map/ppermute | solution.py:513
  41.1 2.5 %shard_map.109 = (f32[2,3,9,144,128]{4,3,2,1,0:T(8,128)S(1)}, f32[2,3,9,144,128]{4,3,2,1,0:T(8,128)S(1)}, f32[8,144,128]{2,1,0:T(8,128)S(1)}) custom-call(f32[2,3,9,144,128]{4,3,2,1,0:T(8,128)S(1)} %get-tuple-element.101.e_in, f32[2,3,9,144,128]{4,3,2,1,0:T(8,128)S(1)} %get-tuple-element.102.h_in, ...), custom_call_target="tpu_custom_call", output_to_operand_aliasing={{0}: (0, {}), {1}: (1, {}), {2}: (2, {})} | custom-call | tf_op jit(solution)/shard_map/pallas_call | solution.py:35
  44.3 0.7 %shard_map.110 = (f32[2,3,9,144,128]{4,3,2,1,0:T(8,128)S(1)}, f32[2,3,9,144,128]{4,3,2,1,0:T(8,128)S(1)}, f32[2,144,128]{2,1,0:T(8,128)S(1)}) custom-call(f32[2,3,9,144,128]{4,3,2,1,0:T(8,128)S(1)} %get-tuple-element.104.e_in, f32[2,3,9,144,128]{4,3,2,1,0:T(8,128)S(1)} %get-tuple-element.105.h_in, ...), custom_call_target="tpu_custom_call", output_to_operand_aliasing={{0}: (0, {}), {1}: (1, {}), {2}: (2, {})} | custom-call | tf_op jit(solution)/shard_map/pallas_call | solution.py:35
  46.0 0.7 %shard_map.114 = (f32[16,64,128]{2,1,0:T(8,128)S(1)}, f32[4,64,128]{2,1,0:T(8,128)S(1)}, f32[4,64,128]{2,1,0:T(8,128)S(1)}, f32[4,64,128]{2,1,0:T(8,128)S(1)}, f32[4,64,128]{2,1,0:T(8,128)S(1)}) custom-call(f32[16,64,128]{2,1,0:T(8,128)S(1)} %shard_map.113.blocks_in, f32[8,144,128]{2,1,0:T(8,128)S(1)} %get-tuple-element.114.total, ...), custom_call_target="tpu_custom_call", output_to_operand_aliasing={{0}: (0, {})} | custom-call | tf_op jit(solution)/shard_map/pallas_call | solution.py:35
  47.3 0.8 %collective-permute-done.13.refs_2_ = f32[4,64,128]{2,1,0:T(8,128)S(1)} collective-permute-done((f32[4,64,128]{2,1,0:T(8,128)S(1)}, f32[4,64,128]{2,1,0:T(8,128)S(1)}, u32[]{:S(2)}, u32[]{:S(2)}) %collective-permute-start.13) | collective-permute-done | bytes 131104 | tf_op jit(solution)/shard_map/ppermute | solution.py:513
  48.4 1.6 %collective-permute-start.15 = (f32[4,64,128]{2,1,0:T(8,128)S(1)}, f32[4,64,128]{2,1,0:T(8,128)S(1)}, u32[]{:S(2)}, u32[]{:S(2)}) collective-permute-start(f32[4,64,128]{2,1,0:T(8,128)S(1)} %get-tuple-element.121), channel_id=1, source_target_pairs={{0,4},{2,6},{4,0},{6,2},{8,12},{10,14},{12,8},{14,10},{16,20},{18,... | collective-permute-start | bytes 393224 | tf_op jit(solution)/shard_map/ppermute | solution.py:513
  49.9 4.2 %collective-permute-done.15.refs_1_ = f32[4,64,128]{2,1,0:T(8,128)S(1)} collective-permute-done((f32[4,64,128]{2,1,0:T(8,128)S(1)}, f32[4,64,128]{2,1,0:T(8,128)S(1)}, u32[]{:S(2)}, u32[]{:S(2)}) %collective-permute-start.15) | collective-permute-done | bytes 131104 | tf_op jit(solution)/shard_map/ppermute | solution.py:513
  54.3 2.7 %collective-permute-start.17 = (f32[64,128]{1,0:T(8,128)S(1)}, f32[64,128]{1,0:T(8,128)S(1)}, u32[]{:S(2)}, u32[]{:S(2)}) collective-permute-start(f32[64,128]{1,0:T(8,128)S(1)} %get-tuple-element.124), channel_id=1, source_target_pairs={{0,16},{2,18},{4,20},{6,22},{8,24},{10,26},{12,28},{14,30},{16,0},... | collective-permute-start | bytes 98312 | tf_op jit(solution)/shard_map/ppermute | solution.py:513
  57.0 1.7 %collective-permute-start.18 = (f32[64,128]{1,0:T(8,128)S(1)}, f32[64,128]{1,0:T(8,128)S(1)}, u32[]{:S(2)}, u32[]{:S(2)}) collective-permute-start(f32[64,128]{1,0:T(8,128)S(1)} %get-tuple-element.125), channel_id=1, source_target_pairs={{0,24},{2,26},{4,28},{6,30},{8,16},{10,18},{12,20},{14,22},{16,8},... | collective-permute-start | bytes 98312 | tf_op jit(solution)/shard_map/ppermute | solution.py:513
  58.6 1.7 %shard_map.112 = f32[1,6,8,128,128]{4,3,2,1,0:T(8,128)} custom-call(f32[2,3,9,144,128]{4,3,2,1,0:T(8,128)S(1)} %get-tuple-element.112.e, f32[2,3,9,144,128]{4,3,2,1,0:T(8,128)S(1)} %get-tuple-element.113.h), custom_call_target="tpu_custom_call" | custom-call | tf_op jit(solution)/shard_map/pallas_call | solution.py:35
  60.4 2.3 %collective-permute-done.18.refs_3_ = f32[64,128]{1,0:T(8,128)S(1)} collective-permute-done((f32[64,128]{1,0:T(8,128)S(1)}, f32[64,128]{1,0:T(8,128)S(1)}, u32[]{:S(2)}, u32[]{:S(2)}) %collective-permute-start.18) | collective-permute-done | bytes 32800 | tf_op jit(solution)/shard_map/ppermute | solution.py:513
  (38 shorter events, 5.1 us)
Async XLA Ops:
  0.6 15.9 %copy-start = (s32[1,3]{1,0:T(1,128)S(1)}, s32[1,3]{1,0:T(1,128)}, u32[]{:S(2)}) copy-start(s32[1,3]{1,0:T(1,128)} %source.23) | copy-start | bytes 40
  0.6 8.6 %collective-permute-start.2 = (f32[64,128]{1,0:T(8,128)}, f32[64,128]{1,0:T(8,128)S(1)}, u32[]{:S(2)}, u32[]{:S(2)}) collective-permute-start(f32[64,128]{1,0:T(8,128)} %bitcast.3), channel_id=1, source_target_pairs={{0,24},{2,26},{4,28},{6,30},{8,16},{10,18},{12,20},{14,22},{16,8},... | collective-permute-start | bytes 98312 | tf_op jit(solution)/shard_map/ppermute | solution.py:513
  5.8 5.0 %collective-permute-start.1 = (f32[64,128]{1,0:T(8,128)}, f32[64,128]{1,0:T(8,128)S(1)}, u32[]{:S(2)}, u32[]{:S(2)}) collective-permute-start(f32[64,128]{1,0:T(8,128)} %bitcast.4), channel_id=1, source_target_pairs={{0,16},{2,18},{4,20},{6,22},{8,24},{10,26},{12,28},{14,30},{16,0},... | collective-permute-start | bytes 98312 | tf_op jit(solution)/shard_map/ppermute | solution.py:513
  5.8 5.0 %collective-permute-start = (f32[64,128]{1,0:T(8,128)}, f32[64,128]{1,0:T(8,128)S(1)}, u32[]{:S(2)}, u32[]{:S(2)}) collective-permute-start(f32[64,128]{1,0:T(8,128)} %bitcast.5), channel_id=1, source_target_pairs={{0,8},{2,10},{4,12},{6,14},{8,0},{10,2},{12,4},{14,6},{16,24},{18,... | collective-permute-start | bytes 98312 | tf_op jit(solution)/shard_map/ppermute | solution.py:513
  7.8 13.3 %collective-permute-start.3 = (f32[2,2,128,128]{3,2,1,0:T(8,128)S(1)}, f32[2,2,128,128]{3,2,1,0:T(8,128)S(1)}, u32[]{:S(2)}, u32[]{:S(2)}) collective-permute-start(f32[2,2,128,128]{3,2,1,0:T(8,128)S(1)} %get-tuple-element.68), channel_id=1, source_target_pairs={{0,1},{1,0},{2,3},{3,2},{4,5},{5,4},{6,7},{7,6},{8,9},{9,8},{10,11... | collective-permute-start | bytes 786440 | tf_op jit(solution)/shard_map/ppermute | solution.py:513
  10.8 5.0 %collective-permute-start.4 = (f32[4,64,128]{2,1,0:T(8,128)S(1)}, f32[4,64,128]{2,1,0:T(8,128)S(1)}, u32[]{:S(2)}, u32[]{:S(2)}) collective-permute-start(f32[4,64,128]{2,1,0:T(8,128)S(1)} %shard_map.96.near.refs_0_), channel_id=1, source_target_pairs={{0,4},{2,6},{4,0},{6,2},{8,12},{10,14},{12,8},{14,10},{16,20},{18,... | collective-permute-start | bytes 393224 | tf_op jit(solution)/shard_map/ppermute | solution.py:513
  12.4 9.1 %collective-permute-start.5 = (f32[4,64,128]{2,1,0:T(8,128)S(1)}, f32[4,64,128]{2,1,0:T(8,128)S(1)}, u32[]{:S(2)}, u32[]{:S(2)}) collective-permute-start(f32[4,64,128]{2,1,0:T(8,128)S(1)} %shard_map.96.near.refs_0_), channel_id=1, source_target_pairs={{0,2},{2,0},{4,6},{6,4},{8,10},{10,8},{12,14},{14,12},{16,18},{18,... | collective-permute-start | bytes 393224 | tf_op jit(solution)/shard_map/ppermute | solution.py:513
  15.8 5.6 %collective-permute-start.6 = (f32[4,64,128]{2,1,0:T(8,128)S(1)}, f32[4,64,128]{2,1,0:T(8,128)S(1)}, u32[]{:S(2)}, u32[]{:S(2)}) collective-permute-start(f32[4,64,128]{2,1,0:T(8,128)S(1)} %collective-permute-done.4.refs_1_), channel_id=1, source_target_pairs={{0,2},{2,0},{4,6},{6,4},{8,10},{10,8},{12,14},{14,12},{16,18},{18,... | collective-permute-start | bytes 393224 | tf_op jit(solution)/shard_map/ppermute | solution.py:513
  21.1 0.7 %copy-start.1 = (s32[16]{0:T(128)S(1)}, s32[16]{0:T(128)}, u32[]{:S(2)}) copy-start(s32[16]{0:T(128)} %block_ids.1) | copy-start | bytes 196
  21.1 0.7 %copy-start.2 = (s32[16]{0:T(128)S(1)}, s32[16]{0:T(128)}, u32[]{:S(2)}) copy-start(s32[16]{0:T(128)} %refs_5_.1) | copy-start | bytes 196
  21.1 0.7 %copy-start.3 = (f32[4]{0:T(128)S(1)}, f32[4]{0:T(128)}, u32[]{:S(2)}) copy-start(f32[4]{0:T(128)} %refs_6_.1) | copy-start | bytes 52
  23.3 6.5 %collective-permute-start.7 = (f32[2,128,128]{2,1,0:T(8,128)S(1)}, f32[2,128,128]{2,1,0:T(8,128)S(1)}, u32[]{:S(2)}, u32[]{:S(2)}) collective-permute-start(f32[2,128,128]{2,1,0:T(8,128)S(1)} %get-tuple-element.85), channel_id=1, source_target_pairs={{0,1},{1,0},{2,3},{3,2},{4,5},{5,4},{6,7},{7,6},{8,9},{9,8},{10,11... | collective-permute-start | bytes 393224 | tf_op jit(solution)/shard_map/ppermute | solution.py:513
  25.4 6.8 %collective-permute-start.8 = (f32[2,128,128]{2,1,0:T(8,128)S(1)}, f32[2,128,128]{2,1,0:T(8,128)S(1)}, u32[]{:S(2)}, u32[]{:S(2)}) collective-permute-start(f32[2,128,128]{2,1,0:T(8,128)S(1)} %get-tuple-element.89), channel_id=1, source_target_pairs={{0,1},{1,0},{2,3},{3,2},{4,5},{5,4},{6,7},{7,6},{8,9},{9,8},{10,11... | collective-permute-start | bytes 393224 | tf_op jit(solution)/shard_map/ppermute | solution.py:513
  30.6 6.1 %collective-permute-start.9 = (f32[2,128,128]{2,1,0:T(8,128)S(1)}, f32[2,128,128]{2,1,0:T(8,128)S(1)}, u32[]{:S(2)}, u32[]{:S(2)}) collective-permute-start(f32[2,128,128]{2,1,0:T(8,128)S(1)} %get-tuple-element.96), channel_id=1, source_target_pairs={{0,1},{1,0},{2,3},{3,2},{4,5},{5,4},{6,7},{7,6},{8,9},{9,8},{10,11... | collective-permute-start | bytes 393224 | tf_op jit(solution)/shard_map/ppermute | solution.py:513
  33.0 6.3 %collective-permute-start.10 = (f32[2,128,128]{2,1,0:T(8,128)S(1)}, f32[2,128,128]{2,1,0:T(8,128)S(1)}, u32[]{:S(2)}, u32[]{:S(2)}) collective-permute-start(f32[2,128,128]{2,1,0:T(8,128)S(1)} %get-tuple-element.100), channel_id=1, source_target_pairs={{0,1},{1,0},{2,3},{3,2},{4,5},{5,4},{6,7},{7,6},{8,9},{9,8},{10,11... | collective-permute-start | bytes 393224 | tf_op jit(solution)/shard_map/ppermute | solution.py:513
  37.5 6.8 %collective-permute-start.11 = (f32[2,128,128]{2,1,0:T(8,128)S(1)}, f32[2,128,128]{2,1,0:T(8,128)S(1)}, u32[]{:S(2)}, u32[]{:S(2)}) collective-permute-start(f32[2,128,128]{2,1,0:T(8,128)S(1)} %get-tuple-element.107), channel_id=1, source_target_pairs={{0,1},{1,0},{2,3},{3,2},{4,5},{5,4},{6,7},{7,6},{8,9},{9,8},{10,11... | collective-permute-start | bytes 393224 | tf_op jit(solution)/shard_map/ppermute | solution.py:513
  40.1 5.2 %collective-permute-start.12 = (f32[2,128,128]{2,1,0:T(8,128)S(1)}, f32[2,128,128]{2,1,0:T(8,128)S(1)}, u32[]{:S(2)}, u32[]{:S(2)}) collective-permute-start(f32[2,128,128]{2,1,0:T(8,128)S(1)} %get-tuple-element.111), channel_id=1, source_target_pairs={{0,1},{1,0},{2,3},{3,2},{4,5},{5,4},{6,7},{7,6},{8,9},{9,8},{10,11... | collective-permute-start | bytes 393224 | tf_op jit(solution)/shard_map/ppermute | solution.py:513
  46.7 1.4 %collective-permute-start.13 = (f32[4,64,128]{2,1,0:T(8,128)S(1)}, f32[4,64,128]{2,1,0:T(8,128)S(1)}, u32[]{:S(2)}, u32[]{:S(2)}) collective-permute-start(f32[4,64,128]{2,1,0:T(8,128)S(1)} %get-tuple-element.118), channel_id=1, source_target_pairs={{0,2},{2,0},{4,6},{6,4},{8,10},{10,8},{12,14},{14,12},{16,18},{18,... | collective-permute-start | bytes 393224 | tf_op jit(solution)/shard_map/ppermute | solution.py:513
  46.8 1.5 %collective-permute-start.14 = (f32[4,64,128]{2,1,0:T(8,128)S(1)}, f32[4,64,128]{2,1,0:T(8,128)S(1)}, u32[]{:S(2)}, u32[]{:S(2)}) collective-permute-start(f32[4,64,128]{2,1,0:T(8,128)S(1)} %get-tuple-element.119), channel_id=1, source_target_pairs={{0,2},{2,0},{4,6},{6,4},{8,10},{10,8},{12,14},{14,12},{16,18},{18,... | collective-permute-start | bytes 393224 | tf_op jit(solution)/shard_map/ppermute | solution.py:513
  48.4 5.8 %collective-permute-start.15 = (f32[4,64,128]{2,1,0:T(8,128)S(1)}, f32[4,64,128]{2,1,0:T(8,128)S(1)}, u32[]{:S(2)}, u32[]{:S(2)}) collective-permute-start(f32[4,64,128]{2,1,0:T(8,128)S(1)} %get-tuple-element.121), channel_id=1, source_target_pairs={{0,4},{2,6},{4,0},{6,2},{8,12},{10,14},{12,8},{14,10},{16,20},{18,... | collective-permute-start | bytes 393224 | tf_op jit(solution)/shard_map/ppermute | solution.py:513
  54.2 6.2 %collective-permute-start.16 = (f32[64,128]{1,0:T(8,128)S(1)}, f32[64,128]{1,0:T(8,128)S(1)}, u32[]{:S(2)}, u32[]{:S(2)}) collective-permute-start(f32[64,128]{1,0:T(8,128)S(1)} %get-tuple-element.123), channel_id=1, source_target_pairs={{0,8},{2,10},{4,12},{6,14},{8,0},{10,2},{12,4},{14,6},{16,24},{18,... | collective-permute-start | bytes 98312 | tf_op jit(solution)/shard_map/ppermute | solution.py:513
  54.3 6.1 %collective-permute-start.17 = (f32[64,128]{1,0:T(8,128)S(1)}, f32[64,128]{1,0:T(8,128)S(1)}, u32[]{:S(2)}, u32[]{:S(2)}) collective-permute-start(f32[64,128]{1,0:T(8,128)S(1)} %get-tuple-element.124), channel_id=1, source_target_pairs={{0,16},{2,18},{4,20},{6,22},{8,24},{10,26},{12,28},{14,30},{16,0},... | collective-permute-start | bytes 98312 | tf_op jit(solution)/shard_map/ppermute | solution.py:513
  57.0 5.7 %collective-permute-start.18 = (f32[64,128]{1,0:T(8,128)S(1)}, f32[64,128]{1,0:T(8,128)S(1)}, u32[]{:S(2)}, u32[]{:S(2)}) collective-permute-start(f32[64,128]{1,0:T(8,128)S(1)} %get-tuple-element.125), channel_id=1, source_target_pairs={{0,24},{2,26},{4,28},{6,30},{8,16},{10,18},{12,20},{14,22},{16,8},... | collective-permute-start | bytes 98312 | tf_op jit(solution)/shard_map/ppermute | solution.py:513

commit v5 on v4

v5 whole, which is shorter than its diff:
```python
import functools
import math

import jax
import jax.numpy as jnp
from jax import lax
from jax.experimental import pallas as pl
from jax.experimental.pallas import tpu as pltpu
from jax.sharding import PartitionSpec as P

STEPS = 4
AMPLITUDE = 4.0
PAD = 8
F32 = jnp.float32
HBM_PER_MICRO = 3.0e6

VMEM = pltpu.MemorySpace.VMEM
IN_VMEM = pl.BlockSpec(memory_space=pltpu.VMEM)
IN_SMEM = pl.BlockSpec(memory_space=pltpu.SMEM)
IN_HBM = pl.BlockSpec(memory_space=pltpu.MemorySpace.HBM)


def on_chip(*shape):
    return VMEM(shape, F32)


def held(array, spec):
    if spec is IN_SMEM:
        return array
    space = VMEM if spec is IN_VMEM else pltpu.MemorySpace.HBM
    return pltpu.with_memory_space_constraint(array, space)


def call(kernel, outs, out_specs, operands, specs, scratch=(), aliases=None, micros=0.3):
    operands = [held(a, s) for a, s in zip(operands, specs)]
    return pl.pallas_call(
        kernel,
        out_shape=outs,
        in_specs=specs,
        out_specs=out_specs,
        scratch_shapes=scratch,
        input_output_aliases=aliases or {},
        compiler_params=pltpu.CompilerParams(vmem_limit_bytes=8 << 20),
        cost_estimate=pl.CostEstimate(
            flops=0, bytes_accessed=int(micros * HBM_PER_MICRO), transcendentals=0
        ),
    )(*operands)


CHUNK = 16


def chunks(rows):
    size = CHUNK if rows % CHUNK == 0 else rows
    return [(first, size) for first in range(0, rows, size)]


def next_col(value):
    column = lax.broadcasted_iota(jnp.int32, value.shape, 1)
    moved = pltpu.roll(value, value.shape[1] - 1, 1)
    return jnp.where(column == value.shape[1] - 1, 0.0, moved)


def prev_col(value):
    column = lax.broadcasted_iota(jnp.int32, value.shape, 1)
    return jnp.where(column == 0, 0.0, pltpu.roll(value, 1, 1))


def neighbours():
    slab = lax.axis_index("slab")
    return slab < lax.axis_size("slab") - 1, slab > 0


class Window:
    def __init__(self, e, h, coef=None, force=None):
        self.e, self.h, self.coef, self.force = e, h, coef, force
        self.rows = e.shape[2] - 2 * PAD
        self.depth = e.shape[1] - 1
        self.top, self.under = self.depth - 1, self.depth

    def read(self, ref, layer, first, size):
        return [ref[c, layer, pl.ds(PAD + first, size), :] for c in range(3)]

    def write(self, ref, layer, first, size, values):
        for c, value in enumerate(values):
            ref[c, layer, pl.ds(PAD + first, size), :] = value

    def put_h(self, layer, double=False, alone=False):
        for first, size in chunks(self.rows):
            rows = pl.ds(PAD + first, size)
            after = pl.ds(PAD + first + 1, size)
            ex, ey, ez = self.read(self.e, layer, first, size)
            hx, hy, hz = self.read(self.h, layer, first, size)
            if double:
                hx, hy, hz = hx + hx, hy + hy, hz + hz
            if alone:
                rise_x, rise_y = -ex, -ey
            else:
                rise_x = self.e[0, layer + 1, rows, :] - ex
                rise_y = self.e[1, layer + 1, rows, :] - ey
            ey_after = self.e[1, layer, after, :]
            ez_after = self.e[2, layer, after, :]
            hx = hx - ((next_col(ez) - ez) - rise_y)
            hy = hy - (rise_x - (ez_after - ez))
            hz = hz - ((ey_after - ey) - (next_col(ex) - ex))
            self.write(self.h, layer, first, size, (hx, hy, hz))

    def curl_h(self, layer, lower, first, size):
        rows = pl.ds(PAD + first, size)
        before = pl.ds(PAD + first - 1, size)
        hx, hy, hz = self.read(self.h, layer, first, size)
        step_x = hx - self.h[0, lower, rows, :]
        step_y = hy - self.h[1, lower, rows, :]
        hy_before = self.h[1, layer, before, :]
        hz_before = self.h[2, layer, before, :]
        return (
            (hz - prev_col(hz)) - step_y,
            step_x - (hz - hz_before),
            (hy - hy_before) - (hx - prev_col(hx)),
        )

    def put_curl(self, curls, layer, lower):
        for first, size in chunks(self.rows):
            for c, value in enumerate(self.curl_h(layer, lower, first, size)):
                curls[c, layer, pl.ds(first, size), :] = value

    def next_e(self, layer, lower, first, size, curls=None):
        here = pl.ds(first, size)
        cell = self.coef[layer, here, :]
        if curls is None:
            curl = self.curl_h(layer, lower, first, size)
        else:
            curl = [curls[c, layer, here, :] for c in range(3)]
        ex, ey, ez = [a + cell * b for a, b in zip(self.read(self.e, layer, first, size), curl)]
        if self.force is not None:
            ez = ez + self.force(layer, here)
        return ex, ey, ez

    def put_e(self, layer, lower, curls=None, other=None, total=None, slot=None):
        for first, size in chunks(self.rows):
            news = self.next_e(layer, lower, first, size, curls)
            self.write(self.e, layer, first, size, news)
            if total is not None:
                rows = pl.ds(PAD + first, size)
                part = [a * other[c, layer, rows, :] for c, a in enumerate(news)]
                total[layer if slot is None else slot, rows, :] += part[0] + part[1] + part[2]

    def take_above(self, above):
        for first, size in chunks(self.rows):
            here, rows = pl.ds(first, size), pl.ds(PAD + first, size)
            self.h[0, self.top, rows, :] += above[1, here, :]
            self.h[1, self.top, rows, :] -= above[0, here, :]

    def take_below(self, below):
        for first, size in chunks(self.rows):
            here, rows = pl.ds(first, size), pl.ds(PAD + first, size)
            self.h[0, self.under, rows, :] = below[0, here, :] + self.e[1, 0, rows, :]
            self.h[1, self.under, rows, :] = below[1, here, :] - self.e[0, 0, rows, :]


def forcing(step, drives, forced):
    if drives is None:
        return None
    return lambda layer, here: drives[pl.ds(step, 1), :] * forced[layer, here, :]


def opening_kernel(fwd, adj, density, own, *rest):
    pays, (planes, sems) = rest[:-2], rest[-2:]
    depth, rows, width_y = fwd.shape[2:]
    top = depth - 1
    has_up, has_low = neighbours()
    held_copy = pltpu.make_async_copy(density, own, sems.at[2, 0])
    held_copy.start()

    def up(pay):
        copies = []
        for evo, given in enumerate((fwd, adj)):
            for c in range(5):
                copies.append(
                    pltpu.make_async_copy(given.at[0, c, top], planes.at[evo, c], sems.at[evo, c])
                )
        for copy in copies:
            copy.start()
        for copy in copies:
            copy.wait()
        for evo in range(2):
            for first, size in chunks(rows):
                here = pl.ds(first, size)
                ex, ey, ez, hx, hy = (planes[evo, c, here, :] for c in range(5))
                if first + size < rows:
                    ez_after = planes[evo, 2, pl.ds(first + 1, size), :]
                else:
                    row = lax.broadcasted_iota(jnp.int32, ez.shape, 0)
                    ez_after = jnp.where(row == size - 1, 0.0, pltpu.roll(ez, size - 1, 0))
                pay[evo, 0, here, :] = (hx + hx) - ((next_col(ez) - ez) + ey)
                pay[evo, 1, here, :] = (hy + hy) + (ex + (ez_after - ez))

    def down(pay):
        copies = []
        for evo, given in enumerate((fwd, adj)):
            for c in range(2):
                copies.append(
                    pltpu.make_async_copy(given.at[0, c, 0], pay.at[evo, c], sems.at[evo, c])
                )
        for copy in copies:
            copy.start()
        for copy in copies:
            copy.wait()

    if len(pays) == 2:
        up(pays[0])
        down(pays[1])
    else:
        pl.when(has_up)(lambda: up(pays[0]))
        pl.when(has_low)(lambda: down(pays[0]))
    held_copy.wait()


def prepare_kernel(source, total, edges, forced):
    depth, rows, width_y = forced.shape
    empty = jnp.zeros(total.shape[1:], F32)
    edges[0] = empty
    edges[1] = empty
    xcoord = lax.broadcasted_iota(jnp.int32, (rows, width_y), 0)
    ycoord = lax.broadcasted_iota(jnp.int32, (rows, width_y), 1)
    offset_x = (xcoord - source[0, 1]).astype(F32) / (rows / 4.0)
    offset_y = (ycoord - source[0, 2]).astype(F32) / (width_y / 4.0)
    profile = jnp.exp(-0.5 * (offset_x * offset_x + offset_y * offset_y))
    level = source[0, 0] - lax.axis_index("slab") * depth
    for layer in range(depth):
        total[layer] = empty
        forced[layer] = jnp.where(level == layer, 1.0, 0.0) * profile


def first_kernel(given, near, e, h, curls, sems):
    win = Window(e, h)
    rows, width_y = win.rows, e.shape[3]
    copies = [
        pltpu.make_async_copy(
            given.at[0, comp],
            (e if comp < 3 else h).at[comp % 3, pl.ds(0, win.depth), pl.ds(PAD, rows), :],
            sems.at[comp],
        )
        for comp in range(6)
    ]
    for copy in copies:
        copy.start()
    margin = jnp.zeros((PAD, width_y), F32)
    empty = jnp.zeros((rows + 2 * PAD, width_y), F32)

    def clear(layer, carry):
        for ref in (e, h):
            for comp in range(3):
                ref[comp, layer, pl.ds(0, PAD), :] = margin
                ref[comp, layer, pl.ds(PAD + rows, PAD), :] = margin
        return carry

    lax.fori_loop(0, win.depth, clear, 0)
    for comp in range(3):
        e[comp, win.depth] = empty
        h[comp, win.depth] = empty
    for copy in copies:
        copy.wait()
    win.put_h(0, True)
    win.put_h(1, True)

    def body(layer, carry):
        win.put_h(layer + 1, True)
        win.put_curl(curls, layer, layer - 1)
        return carry

    lax.fori_loop(1, win.top, body, 0)


def take_kernel(evo, h_in, curls_in, e, below, above, h, curls):
    win = Window(e, h)
    has_up, has_low = neighbours()
    pl.when(has_up)(lambda: win.take_above(above.at[evo]))
    pl.when(has_low)(lambda: win.take_below(below.at[evo]))
    win.put_curl(curls, win.top, win.top - 1)
    win.put_curl(curls, 0, win.under)


def edge_kernel(step, evo, *refs):
    refs = list(refs)
    e_in, h_in = refs.pop(0), refs.pop(0)
    if evo == 1:
        other_in, edges_in = refs.pop(0), refs.pop(0)
    coef = refs.pop(0)
    drives, forced = (refs.pop(0), refs.pop(0)) if evo == 0 else (None, None)
    curls = refs.pop(0) if step == 0 else None
    below, above = (refs.pop(0), refs.pop(0)) if step > 0 else (None, None)
    e, h = refs.pop(0), refs.pop(0)
    other, edges = (refs.pop(0), refs.pop(0)) if evo == 1 else (None, None)
    pays = refs
    win = Window(e, h, coef, forcing(step, drives, forced))
    top = win.top
    has_up, has_low = neighbours()

    @pl.when(has_up)
    def _():
        if step > 0:
            win.take_above(above)
        win.put_e(top, top - 1, curls, other, edges, 1)
        if pays:
            win.put_h(top, alone=True)
            for c in range(2):
                pays[0][c] = h[c, top, pl.ds(PAD, win.rows), :]

    @pl.when(has_low)
    def _():
        if step > 0:
            win.take_below(below)
        win.put_e(0, win.under, curls, other, edges, 0)
        if pays:
            for c in range(2):
                pays[-1][c] = e[c, 0, pl.ds(PAD, win.rows), :]


def inner_range(top):
    has_up, has_low = neighbours()
    return jnp.where(has_low, 1, 0), jnp.where(has_up, top - 1, top)


def begin_kernel(
    e_fwd_in, e_adj_in, total_in, coef, drives, forced, curls_fwd, curls_adj,
    e_fwd, e_adj, total,
):
    fwd = Window(e_fwd, None, coef, forcing(0, drives, forced))
    adj = Window(e_adj, None, coef)
    lowest, highest = inner_range(fwd.top)

    def body(layer, carry):
        fwd.put_e(layer, None, curls_fwd)
        adj.put_e(layer, None, curls_adj, e_fwd, total)
        return carry

    lax.fori_loop(lowest, highest + 1, body, 0)


def inner_kernel(step, evo, *refs):
    refs = list(refs)
    e_in, h_in = refs.pop(0), refs.pop(0)
    if evo == 1:
        other_in, total_in = refs.pop(0), refs.pop(0)
    coef = refs.pop(0)
    drives, forced = (refs.pop(0), refs.pop(0)) if evo == 0 else (None, None)
    e, h = refs.pop(0), refs.pop(0)
    other, total = (refs.pop(0), refs.pop(0)) if evo == 1 else (None, None)
    win = Window(e, h, coef, forcing(step, drives, forced))
    lowest, highest = inner_range(win.top)
    win.put_h(0)
    pl.when(lowest == 1)(lambda: win.put_h(1))

    def body(layer, carry):
        win.put_h(layer + 1)
        win.put_e(layer, jnp.where(layer == 0, win.under, layer - 1), None, other, total)
        return carry

    lax.fori_loop(lowest, highest, body, 0)
    win.put_e(highest, highest - 1, None, other, total)


def coef_layer(layer, coef, blocks, placed, base):
    nblock = blocks.shape[0]
    rows = base.shape[0]
    block_rows = rows // nblock
    for block in range(nblock):
        source = pl.ds(pl.multiple_of(layer * block_rows, block_rows), block_rows)
        placed[pl.ds(PAD + block * block_rows, block_rows), :] = blocks[block, source, :]
    for first, size in chunks(rows):
        here = pl.ds(first, size)
        coef[layer, here, :] = 0.25 / (base[here, :] + 3.0 * filtered(placed, first, size))


def coef_edge_kernel(layout, count, *refs):
    parts = refs[:count]
    block_ids, material_idx, material_eps, coef, blocks, base, placed = refs[count:]
    nblock = blocks.shape[0]
    depth, rows, width_y = coef.shape
    block_rows = rows // nblock
    me = lax.axis_index("grp")
    for part, masks in zip(parts, layout):
        for slot, mask in enumerate(masks):
            blocks[block_ids[me ^ mask]] = part[slot]
    for block in range(nblock):
        level = jnp.full((block_rows, width_y), material_eps[material_idx[block]], F32)
        base[pl.ds(block * block_rows, block_rows), :] = level
    placed[pl.ds(0, PAD), :] = jnp.zeros((PAD, width_y), F32)
    placed[pl.ds(PAD + rows, PAD), :] = jnp.zeros((PAD, width_y), F32)
    coef_layer(0, coef, blocks, placed, base)
    coef_layer(depth - 1, coef, blocks, placed, base)


def coef_inner_kernel(coef_in, blocks, base, coef, placed):
    depth, rows, width_y = coef.shape
    placed[pl.ds(0, PAD), :] = jnp.zeros((PAD, width_y), F32)
    placed[pl.ds(PAD + rows, PAD), :] = jnp.zeros((PAD, width_y), F32)

    def body(layer, carry):
        coef_layer(layer, coef, blocks, placed, base)
        return carry

    lax.fori_loop(1, depth - 1, body, 0)


def filtered(padded, first, size):
    here = padded[pl.ds(PAD + first, size), :]
    before = padded[pl.ds(PAD + first - 1, size), :]
    after = padded[pl.ds(PAD + first + 1, size), :]
    along = before + 2.0 * here + after
    return (prev_col(along) + 2.0 * along + next_col(along)) * 0.0625


def pack_kernel(*refs):
    out = refs[-1]
    for slot, ref in enumerate(refs[:-1]):
        out[slot] = ref[...]


def filter_layer(values, layer, blocks, wide):
    nblock = blocks.shape[0]
    rows = wide.shape[0]
    block_rows = rows // nblock
    for first, size in chunks(rows):
        wide[pl.ds(first, size), :] = filtered(values, first, size)
    for block in range(nblock):
        target = pl.ds(pl.multiple_of(layer * block_rows, block_rows), block_rows)
        blocks[block, target, :] = wide[pl.ds(block * block_rows, block_rows), :]


def filter_inner_kernel(total, blocks, wide):
    def body(layer, carry):
        filter_layer(total.at[layer], layer, blocks, wide)
        return carry

    lax.fori_loop(1, total.shape[0] - 1, body, 0)


def filter_edge_kernel(layout, blocks_in, total, edges, block_ids, blocks, *rest):
    parts, wide, ends = rest[:-2], rest[-2], rest[-1]
    me = lax.axis_index("grp")
    for slot, layer in enumerate((0, total.shape[0] - 1)):
        ends[slot] = total[layer] + edges[slot]
        filter_layer(ends.at[slot], layer, blocks, wide.at[slot])
    for part, masks in zip(parts, layout):
        for slot, mask in enumerate(masks):
            part[slot] = blocks[block_ids[me ^ mask]]


def add_kernel(*refs):
    half = len(refs) // 3
    for a, b, out in zip(refs[:half], refs[half : 2 * half], refs[2 * half :]):
        out[...] = a[...] + b[...]


def add_split_kernel(count, *refs):
    terms, outs = refs[:count], refs[count:]
    for slot, out in enumerate(outs):
        value = terms[0][slot]
        for term in terms[1:]:
            value = value + term[slot]
        out[...] = value


def last_kernel(scale, *refs):
    value = refs[0][...]
    for ref in refs[1:-1]:
        value = value + ref[...]
    refs[-1][...] = value * scale


def out_kernel(e, h, finals, halves, sems):
    depth = e.shape[1] - 1
    rows = e.shape[2] - 2 * PAD
    every = pl.ds(PAD, rows)
    copies = [
        pltpu.make_async_copy(e.at[c, pl.ds(0, depth), every, :], finals.at[0, c], sems.at[c])
        for c in range(3)
    ]
    for copy in copies:
        copy.start()
    for c in range(3):

        def body(layer, carry, c=c):
            halves[c, layer] = 0.5 * h[c, layer, every, :]
            return carry

        lax.fori_loop(0, depth, body, 0)
        copy = pltpu.make_async_copy(halves.at[c], finals.at[0, 3 + c], sems.at[3 + c])
        copy.start()
        copies.append(copy)
    for copy in copies:
        copy.wait()


def swap_over(array, axis, mask):
    return lax.ppermute(array, axis, [(i, i ^ mask) for i in range(lax.axis_size(axis))])


def shift_over(array, axis, distance):
    size = lax.axis_size(axis)
    route = [(i, i + distance) for i in range(size) if 0 <= i + distance < size]
    return lax.ppermute(array, axis, route)


def trade(pays):
    if len(pays) == 1:
        return [swap_over(pays[0], "slab", 1)] * 2
    return [shift_over(pays[0], "slab", 1), shift_over(pays[1], "slab", -1)]


def per_device(
    fwd_fields, adj_fields, density, block_ids, material_idx, material_eps, source_pos, wave_idx
):
    depth, width_x, width_y = fwd_fields.shape[2:]
    nblock = block_ids.shape[0]
    block_rows = width_x // nblock
    ngrp = lax.axis_size("grp")
    npay = 1 if lax.axis_size("slab") == 2 else 2
    omega = 2.0 * math.pi / (6.0 + 2.0 * wave_idx[0].astype(F32))
    steps = lax.broadcasted_iota(jnp.int32, (STEPS, width_y), 0).astype(F32)
    drives = AMPLITUDE * jnp.sin(omega * (steps + 1.0))

    far = 4
    middle = ngrp // (2 * far)
    far_masks = [2 * middle * j for j in range(far)]
    middle_masks = [2 * j for j in range(middle)]
    layout = [
        [core + mid + top for top in far_masks] for core in (0, 1) for mid in middle_masks
    ]
    piece = (depth * block_rows, width_y)
    group = (far,) + piece

    field_shape = on_chip(3, depth + 1, width_x + 2 * PAD, width_y)
    curls_shape = on_chip(3, depth, width_x, width_y)
    halo_shape = on_chip(2, width_x, width_y)
    total_shape = on_chip(depth, width_x + 2 * PAD, width_y)
    edges_shape = on_chip(2, width_x + 2 * PAD, width_y)
    coef_shape = on_chip(depth, width_x, width_y)
    blocks_shape = on_chip(nblock, *piece)
    plane = on_chip(width_x, width_y)
    padded = pltpu.VMEM((width_x + 2 * PAD, width_y), F32)

    design = density.reshape(piece)
    got = [swap_over(design, "grp", mask) for mask in far_masks[1:]]
    own, *pays = call(
        opening_kernel,
        [on_chip(*piece)] + [on_chip(2, 2, width_x, width_y)] * npay,
        [IN_VMEM] * (1 + npay),
        [fwd_fields, adj_fields, design],
        [IN_HBM] * 3,
        [pltpu.VMEM((2, 5, width_x, width_y), F32), pltpu.SemaphoreType.DMA((3, 5))],
    )
    below, above = trade(pays)

    near = call(pack_kernel, on_chip(*group), IN_VMEM, [own] + got, [IN_VMEM] * far)
    parts = [near] + [swap_over(near, "grp", mask) for mask in middle_masks[1:]]
    parts = parts + [swap_over(part, "grp", 1) for part in parts]

    total, edges, forced = call(
        prepare_kernel,
        [total_shape, edges_shape, on_chip(depth, width_x, width_y)],
        [IN_VMEM] * 3,
        [source_pos],
        [IN_SMEM],
    )
    fields = []
    for evo, given in enumerate((fwd_fields, adj_fields)):
        e, h, curls = call(
            first_kernel,
            [field_shape, field_shape, curls_shape],
            [IN_VMEM] * 3,
            [given, near],
            [IN_HBM, IN_VMEM],
            [pltpu.SemaphoreType.DMA((6,))],
            micros=2.3,
        )
        fields.append((e, h, curls))
    taken = []
    for evo, (e, h, curls) in enumerate(fields):
        h, curls = call(
            functools.partial(take_kernel, evo),
            [field_shape, curls_shape],
            [IN_VMEM] * 2,
            [h, curls, e, below, above],
            [IN_VMEM] * 5,
            aliases={0: 0, 1: 1},
        )
        taken.append((e, h, curls))
    (e_fwd, h_fwd, curls_fwd), (e_adj, h_adj, curls_adj) = taken
    coef, blocks, base = call(
        functools.partial(coef_edge_kernel, layout, len(parts)),
        [coef_shape, blocks_shape, plane],
        [IN_VMEM] * 3,
        parts + [block_ids, material_idx, material_eps],
        [IN_VMEM] * len(parts) + [IN_SMEM] * 3,
        [padded],
    )

    arrived_fwd, arrived_adj = [curls_fwd], [curls_adj]
    for step in range(STEPS):
        more = npay if step < STEPS - 1 else 0
        e_fwd, h_fwd, *pays = call(
            functools.partial(edge_kernel, step, 0),
            [field_shape] * 2 + [halo_shape] * more,
            [IN_VMEM] * (2 + more),
            [e_fwd, h_fwd, coef, drives, forced] + arrived_fwd,
            [IN_VMEM] * (5 + len(arrived_fwd)),
            aliases={0: 0, 1: 1},
        )
        if more:
            arrived_fwd = trade(pays)
        if step == 0:
            coef = call(
                coef_inner_kernel, coef_shape, IN_VMEM, [coef, blocks, base], [IN_VMEM] * 3,
                [padded], aliases={0: 0}, micros=0.7,
            )
            e_fwd, e_adj, total = call(
                begin_kernel,
                [field_shape, field_shape, total_shape],
                [IN_VMEM] * 3,
                [e_fwd, e_adj, total, coef, drives, forced, curls_fwd, curls_adj],
                [IN_VMEM] * 8,
                aliases={0: 0, 1: 1, 2: 2},
                micros=0.7,
            )
        else:
            e_adj, h_adj, e_fwd, total = call(
                functools.partial(inner_kernel, step, 1),
                [field_shape] * 3 + [total_shape],
                [IN_VMEM] * 4,
                [e_adj, h_adj, e_fwd, total, coef],
                [IN_VMEM] * 5,
                aliases={0: 0, 1: 1, 2: 2, 3: 3},
                micros=1.2,
            )
        if not more:
            blocks = call(
                filter_inner_kernel, blocks_shape, IN_VMEM, [total], [IN_VMEM],
                [pltpu.VMEM((width_x, width_y), F32)], micros=0.6,
            )
        e_adj, h_adj, e_fwd, edges, *pays = call(
            functools.partial(edge_kernel, step, 1),
            [field_shape] * 3 + [edges_shape] + [halo_shape] * more,
            [IN_VMEM] * (4 + more),
            [e_adj, h_adj, e_fwd, edges, coef] + arrived_adj,
            [IN_VMEM] * (5 + len(arrived_adj)),
            aliases={0: 0, 1: 1, 2: 2, 3: 3},
        )
        if more:
            arrived_adj = trade(pays)
            e_fwd, h_fwd = call(
                functools.partial(inner_kernel, step + 1, 0),
                [field_shape] * 2,
                [IN_VMEM] * 2,
                [e_fwd, h_fwd, coef, drives, forced],
                [IN_VMEM] * 5,
                aliases={0: 0, 1: 1},
                micros=1.1,
            )

    blocks, *parts = call(
        functools.partial(filter_edge_kernel, layout),
        [blocks_shape] + [on_chip(*group)] * len(layout),
        [IN_VMEM] * (1 + len(layout)),
        [blocks, total, edges, block_ids],
        [IN_VMEM] * 3 + [IN_SMEM],
        [
            pltpu.VMEM((2, width_x, width_y), F32),
            pltpu.VMEM((2, width_x + 2 * PAD, width_y), F32),
        ],
        aliases={0: 0},
    )
    got = [swap_over(part, "grp", 1) for part in parts[middle:]]
    sums = call(
        add_kernel,
        [on_chip(*group)] * middle,
        [IN_VMEM] * middle,
        list(parts[:middle]) + got,
        [IN_VMEM] * (2 * middle),
    )
    got = [swap_over(part, "grp", mask) for part, mask in zip(sums[1:], middle_masks[1:])]
    pieces = call(
        functools.partial(add_split_kernel, middle),
        [on_chip(*piece)] * far,
        [IN_VMEM] * far,
        [sums[0]] + got,
        [IN_VMEM] * middle,
    )
    got = [swap_over(part, "grp", mask) for part, mask in zip(pieces[1:], far_masks[1:])]
    scale = 3.0 / (STEPS * math.sqrt(ngrp))
    grad = call(
        functools.partial(last_kernel, scale),
        jax.ShapeDtypeStruct(piece, F32),
        IN_VMEM,
        [pieces[0]] + got,
        [IN_VMEM] * far,
    )
    finals = call(
        out_kernel,
        jax.ShapeDtypeStruct(fwd_fields.shape, F32),
        IN_HBM,
        [e_fwd, h_fwd],
        [IN_VMEM] * 2,
        [
            pltpu.VMEM((3, depth, width_x, width_y), F32),
            pltpu.SemaphoreType.DMA((6,)),
        ],
        micros=1.7,
    )
    return finals, grad.reshape(density.shape)


def solution(mesh):
    placed = (
        P("grp", None, "slab", None, None),
        P("grp", None, "slab", None, None),
        P("slab", "grp", None),
        P(),
        P(),
        P(),
        P("grp", None),
        P("grp"),
    )
    return jax.shard_map(
        per_device,
        mesh=mesh,
        in_specs=placed,
        out_specs=(P("grp", None, "slab", None, None), P("slab", "grp", None)),
        check_vma=False,
    )
```

time: 63.5 us -> 63.3 us (level)
  Pallas kernels: 25.2 us -> 23.7 us
  waiting for transfers between devices: 13 us -> 14.2 us
    pallas_call x23 -> x30, Pallas kernels: 25.2 us -> 23.7 us  [call(): pl.pallas_call(kernel, out_shape=outs, in_specs=specs, out_specs=out_spec...]
    ppermute x19, waiting for transfers between devices: 13 us -> 14.2 us  [swap_over(): lax.ppermute(array, axis, [(i, i ^ mask) for i in range(lax.axis_size(axi...]
  transfers between devices with their start and end apart: 19 -> 19, of which waited for: 7 -> 9; matrix products, arithmetic and copies ran while one was open for 0% -> 0% of each run, Pallas kernels for 34% -> 34%
where the time goes in v5:
time: 63.3 us; the launch traced here: 63.1 us
  Pallas kernels  23.7 us (37%)
  starting transfers between devices  22.9 us (36%)
  waiting for transfers between devices  14.2 us (22%)
  between operations  1.67 us (3%)
    pallas_call x30, Pallas kernels, call(): pl.pallas_call(kernel, out_shape=outs, in_specs=specs, out_specs=out_spec...  23.7 us
    ppermute x19, starting transfers between devices, swap_over(): lax.ppermute(array, axis, [(i, i ^ mask) for i in range(lax.axis_size(axi...  22.9 us
    ppermute x19, waiting for transfers between devices, swap_over(): lax.ppermute(array, axis, [(i, i ^ mask) for i in range(lax.axis_size(axi...  14.2 us
  transfers between devices with their start and end apart: 19, of which 9 were waited for; matrix products, arithmetic and copies ran while one was open for 0% of the time, Pallas kernels for 34%

profile of v5, /device:TPU:0, one launch (start us, length us, event | category | flops | bytes accessed | tf_op | source)
XLA Modules:
  0.0 63.1 jit_solution(17750552969030790867)
XLA Ops:
  0.6 5.1 %collective-permute-start.2 = (f32[64,128]{1,0:T(8,128)}, f32[64,128]{1,0:T(8,128)S(1)}, u32[]{:S(2)}, u32[]{:S(2)}) collective-permute-start(f32[64,128]{1,0:T(8,128)} %bitcast.3), channel_id=1, source_target_pairs={{0,24},{2,26},{4,28},{6,30},{8,16},{10,18},{12,20},{14,22},{16,8},... | collective-permute-start | bytes 98312 | tf_op jit(solution)/shard_map/ppermute | solution.py:498
  5.8 0.6 %collective-permute-start = (f32[64,128]{1,0:T(8,128)}, f32[64,128]{1,0:T(8,128)S(1)}, u32[]{:S(2)}, u32[]{:S(2)}) collective-permute-start(f32[64,128]{1,0:T(8,128)} %bitcast.5), channel_id=1, source_target_pairs={{0,8},{2,10},{4,12},{6,14},{8,0},{10,2},{12,4},{14,6},{16,24},{18,... | collective-permute-start | bytes 98312 | tf_op jit(solution)/shard_map/ppermute | solution.py:498
  6.4 1.4 %shard_map.95 = (f32[64,128]{1,0:T(8,128)S(1)}, f32[2,2,128,128]{3,2,1,0:T(8,128)S(1)}) custom-call(f32[1,6,8,128,128]{4,3,2,1,0:T(8,128)} %given.2, f32[1,6,8,128,128]{4,3,2,1,0:T(8,128)} %given.3, f32[64,128]{1,0:T(8,128)} %bitcast.6), custom_call_target="tpu_custom_call" | custom-call | bytes 900000 | tf_op jit(solution)/shard_map/pallas_call | solution.py:36
  7.8 1.4 %collective-permute-start.3 = (f32[2,2,128,128]{3,2,1,0:T(8,128)S(1)}, f32[2,2,128,128]{3,2,1,0:T(8,128)S(1)}, u32[]{:S(2)}, u32[]{:S(2)}) collective-permute-start(f32[2,2,128,128]{3,2,1,0:T(8,128)S(1)} %get-tuple-element.83), channel_id=1, source_target_pairs={{0,1},{1,0},{2,3},{3,2},{4,5},{5,4},{6,7},{7,6},{8,9},{9,8},{10,11... | collective-permute-start | bytes 786440 | tf_op jit(solution)/shard_map/ppermute | solution.py:498
  9.2 1.6 %collective-permute-done.1.refs_2_ = f32[64,128]{1,0:T(8,128)S(1)} collective-permute-done((f32[64,128]{1,0:T(8,128)}, f32[64,128]{1,0:T(8,128)S(1)}, u32[]{:S(2)}, u32[]{:S(2)}) %collective-permute-start.1) | collective-permute-done | bytes 32800 | tf_op jit(solution)/shard_map/ppermute | solution.py:498
  10.8 1.6 %collective-permute-start.4 = (f32[4,64,128]{2,1,0:T(8,128)S(1)}, f32[4,64,128]{2,1,0:T(8,128)S(1)}, u32[]{:S(2)}, u32[]{:S(2)}) collective-permute-start(f32[4,64,128]{2,1,0:T(8,128)S(1)} %shard_map.96.near.refs_0_), channel_id=1, source_target_pairs={{0,4},{2,6},{4,0},{6,2},{8,12},{10,14},{12,8},{14,10},{16,20},{18,... | collective-permute-start | bytes 393224 | tf_op jit(solution)/shard_map/ppermute | solution.py:498
  12.4 3.5 %collective-permute-done.4.refs_1_ = f32[4,64,128]{2,1,0:T(8,128)S(1)} collective-permute-done((f32[4,64,128]{2,1,0:T(8,128)S(1)}, f32[4,64,128]{2,1,0:T(8,128)S(1)}, u32[]{:S(2)}, u32[]{:S(2)}) %collective-permute-start.4) | collective-permute-done | bytes 131104 | tf_op jit(solution)/shard_map/ppermute | solution.py:498
  17.2 3.0 %shard_map.102 = (f32[3,9,144,128]{3,2,1,0:T(8,128)S(1)}, f32[3,9,144,128]{3,2,1,0:T(8,128)S(1)}, f32[3,8,128,128]{3,2,1,0:T(8,128)S(1)}) custom-call(f32[1,6,8,128,128]{4,3,2,1,0:T(8,128)} %given.3, f32[4,64,128]{2,1,0:T(8,128)S(1)} %shard_map.96.near.refs_0_), custom_call_target="tpu_custom_call" | custom-call | bytes 6899999 | tf_op jit(solution)/shard_map/pallas_call | solution.py:36
  20.2 3.0 %shard_map.97 = (f32[3,9,144,128]{3,2,1,0:T(8,128)S(1)}, f32[3,9,144,128]{3,2,1,0:T(8,128)S(1)}, f32[3,8,128,128]{3,2,1,0:T(8,128)S(1)}) custom-call(f32[1,6,8,128,128]{4,3,2,1,0:T(8,128)} %given.2, f32[4,64,128]{2,1,0:T(8,128)S(1)} %shard_map.96.near.refs_0_), custom_call_target="tpu_custom_call" | custom-call | bytes 6899999 | tf_op jit(solution)/shard_map/pallas_call | solution.py:36
  24.1 0.8 %shard_map.99 = (f32[8,128,128]{2,1,0:T(8,128)S(1)}, f32[16,64,128]{2,1,0:T(8,128)S(1)}, f32[128,128]{1,0:T(8,128)S(1)}) custom-call(f32[4,64,128]{2,1,0:T(8,128)S(1)} %shard_map.96.near.refs_0_, f32[4,64,128]{2,1,0:T(8,128)S(1)} %collective-permute-done.4.refs_1_, f32[4,64,128]{2,1,0:T(8,128)S(1)} %collective-permute-done.5.refs_2_, ...), custom_call_target="tpu_custom_call" | custom-call | bytes 900000 | tf_op jit(solution)/shard_map/pallas_call | solution.py:36
  25.1 1.5 %collective-permute-start.7 = (f32[2,128,128]{2,1,0:T(8,128)S(1)}, f32[2,128,128]{2,1,0:T(8,128)S(1)}, u32[]{:S(2)}, u32[]{:S(2)}) collective-permute-start(f32[2,128,128]{2,1,0:T(8,128)S(1)} %get-tuple-element.106), channel_id=1, source_target_pairs={{0,1},{1,0},{2,3},{3,2},{4,5},{5,4},{6,7},{7,6},{8,9},{9,8},{10,11... | collective-permute-start | bytes 393224 | tf_op jit(solution)/shard_map/ppermute | solution.py:498
  26.6 0.8 %shard_map.103.coef.refs_4_.refs_2_ = f32[8,128,128]{2,1,0:T(8,128)S(1)} custom-call(f32[8,128,128]{2,1,0:T(8,128)S(1)} %get-tuple-element.85.refs_2_.coef_in, f32[16,64,128]{2,1,0:T(8,128)S(1)} %get-tuple-element.91.blocks, f32[128,128]{1,0:T(8,128)S(1)} %get-tuple-element.92.base), custom_call_target="tpu_custom_call", output_to_operand_aliasing={{}: (0, {})} | custom-call | bytes 2100000 | tf_op jit(solution)/shard_map/pallas_call | solution.py:36
  28.6 1.3 %shard_map.107 = (f32[3,9,144,128]{3,2,1,0:T(8,128)S(1)}, f32[3,9,144,128]{3,2,1,0:T(8,128)S(1)}) custom-call(f32[3,9,144,128]{3,2,1,0:T(8,128)S(1)} %get-tuple-element.102.refs_0_, f32[3,9,144,128]{3,2,1,0:T(8,128)S(1)} %get-tuple-element.103.refs_1_, ...), custom_call_target="tpu_custom_call", output_to_operand_aliasing={{0}: (0, {}), {1}: (1, {})} | custom-call | bytes 3300000 | tf_op jit(solution)/shard_map/pallas_call | solution.py:36
  29.9 1.2 %collective-permute-done.7.refs_5_.refs_6_ = f32[2,128,128]{2,1,0:T(8,128)S(1)} collective-permute-done((f32[2,128,128]{2,1,0:T(8,128)S(1)}, f32[2,128,128]{2,1,0:T(8,128)S(1)}, u32[]{:S(2)}, u32[]{:S(2)}) %collective-permute-start.7) | collective-permute-done | bytes 131104 | tf_op jit(solution)/shard_map/ppermute | solution.py:498
  31.4 1.7 %collective-permute-start.9 = (f32[2,128,128]{2,1,0:T(8,128)S(1)}, f32[2,128,128]{2,1,0:T(8,128)S(1)}, u32[]{:S(2)}, u32[]{:S(2)}) collective-permute-start(f32[2,128,128]{2,1,0:T(8,128)S(1)} %get-tuple-element.120), channel_id=1, source_target_pairs={{0,1},{1,0},{2,3},{3,2},{4,5},{5,4},{6,7},{7,6},{8,9},{9,8},{10,11... | collective-permute-start | bytes 393224 | tf_op jit(solution)/shard_map/ppermute | solution.py:498
  33.0 1.4 %shard_map.109 = (f32[3,9,144,128]{3,2,1,0:T(8,128)S(1)}, f32[3,9,144,128]{3,2,1,0:T(8,128)S(1)}, f32[3,9,144,128]{3,2,1,0:T(8,128)S(1)}, f32[8,144,128]{2,1,0:T(8,128)S(1)}) custom-call(f32[3,9,144,128]{3,2,1,0:T(8,128)S(1)} %get-tuple-element.100.refs_0_, ...), custom_call_target="tpu_custom_call", output_to_operand_aliasing={{0}: (0, {}), {1}: (1, {}), {2}: (2, {}), {3}: (3, {})} | custom-call | bytes 3600000 | tf_op jit(solution)/shard_map/pallas_call | solution.py:36
  34.7 1.0 %collective-permute-start.10 = (f32[2,128,128]{2,1,0:T(8,128)S(1)}, f32[2,128,128]{2,1,0:T(8,128)S(1)}, u32[]{:S(2)}, u32[]{:S(2)}) collective-permute-start(f32[2,128,128]{2,1,0:T(8,128)S(1)} %get-tuple-element.127), channel_id=1, source_target_pairs={{0,1},{1,0},{2,3},{3,2},{4,5},{5,4},{6,7},{7,6},{8,9},{9,8},{10,11... | collective-permute-start | bytes 393224 | tf_op jit(solution)/shard_map/ppermute | solution.py:498
  35.7 1.3 %shard_map.111 = (f32[3,9,144,128]{3,2,1,0:T(8,128)S(1)}, f32[3,9,144,128]{3,2,1,0:T(8,128)S(1)}) custom-call(f32[3,9,144,128]{3,2,1,0:T(8,128)S(1)} %get-tuple-element.116.refs_0_, f32[3,9,144,128]{3,2,1,0:T(8,128)S(1)} %get-tuple-element.117.refs_1_, ...), custom_call_target="tpu_custom_call", output_to_operand_aliasing={{0}: (0, {}), {1}: (1, {})} | custom-call | bytes 3300000 | tf_op jit(solution)/shard_map/pallas_call | solution.py:36
  37.3 1.3 %collective-permute-start.11 = (f32[2,128,128]{2,1,0:T(8,128)S(1)}, f32[2,128,128]{2,1,0:T(8,128)S(1)}, u32[]{:S(2)}, u32[]{:S(2)}) collective-permute-start(f32[2,128,128]{2,1,0:T(8,128)S(1)} %get-tuple-element.134), channel_id=1, source_target_pairs={{0,1},{1,0},{2,3},{3,2},{4,5},{5,4},{6,7},{7,6},{8,9},{9,8},{10,11... | collective-permute-start | bytes 393224 | tf_op jit(solution)/shard_map/ppermute | solution.py:498
  38.5 1.4 %shard_map.113 = (f32[3,9,144,128]{3,2,1,0:T(8,128)S(1)}, f32[3,9,144,128]{3,2,1,0:T(8,128)S(1)}, f32[3,9,144,128]{3,2,1,0:T(8,128)S(1)}, f32[8,144,128]{2,1,0:T(8,128)S(1)}) custom-call(f32[3,9,144,128]{3,2,1,0:T(8,128)S(1)} %get-tuple-element.114.refs_0_, ...), custom_call_target="tpu_custom_call", output_to_operand_aliasing={{0}: (0, {}), {1}: (1, {}), {2}: (2, {}), {3}: (3, {})} | custom-call | bytes 3600000 | tf_op jit(solution)/shard_map/pallas_call | solution.py:36
  40.6 1.6 %collective-permute-start.12 = (f32[2,128,128]{2,1,0:T(8,128)S(1)}, f32[2,128,128]{2,1,0:T(8,128)S(1)}, u32[]{:S(2)}, u32[]{:S(2)}) collective-permute-start(f32[2,128,128]{2,1,0:T(8,128)S(1)} %get-tuple-element.141), channel_id=1, source_target_pairs={{0,1},{1,0},{2,3},{3,2},{4,5},{5,4},{6,7},{7,6},{8,9},{9,8},{10,11... | collective-permute-start | bytes 393224 | tf_op jit(solution)/shard_map/ppermute | solution.py:498
  42.2 1.3 %shard_map.115 = (f32[3,9,144,128]{3,2,1,0:T(8,128)S(1)}, f32[3,9,144,128]{3,2,1,0:T(8,128)S(1)}) custom-call(f32[3,9,144,128]{3,2,1,0:T(8,128)S(1)} %get-tuple-element.130.refs_0_, f32[3,9,144,128]{3,2,1,0:T(8,128)S(1)} %get-tuple-element.131.refs_1_, ...), custom_call_target="tpu_custom_call", output_to_operand_aliasing={{0}: (0, {}), {1}: (1, {})} | custom-call | bytes 3300000 | tf_op jit(solution)/shard_map/pallas_call | solution.py:36
  43.9 1.4 %shard_map.117 = (f32[3,9,144,128]{3,2,1,0:T(8,128)S(1)}, f32[3,9,144,128]{3,2,1,0:T(8,128)S(1)}, f32[3,9,144,128]{3,2,1,0:T(8,128)S(1)}, f32[8,144,128]{2,1,0:T(8,128)S(1)}) custom-call(f32[3,9,144,128]{3,2,1,0:T(8,128)S(1)} %get-tuple-element.128.refs_0_, ...), custom_call_target="tpu_custom_call", output_to_operand_aliasing={{0}: (0, {}), {1}: (1, {}), {2}: (2, {}), {3}: (3, {})} | custom-call | bytes 3600000 | tf_op jit(solution)/shard_map/pallas_call | solution.py:36
  45.3 0.6 %shard_map.120.blocks_in = f32[16,64,128]{2,1,0:T(8,128)S(1)} custom-call(f32[8,144,128]{2,1,0:T(8,128)S(1)} %get-tuple-element.144.total), custom_call_target="tpu_custom_call" | custom-call | bytes 1800000 | tf_op jit(solution)/shard_map/pallas_call | solution.py:36
  46.1 0.7 %shard_map.121 = (f32[16,64,128]{2,1,0:T(8,128)S(1)}, f32[4,64,128]{2,1,0:T(8,128)S(1)}, f32[4,64,128]{2,1,0:T(8,128)S(1)}, f32[4,64,128]{2,1,0:T(8,128)S(1)}, f32[4,64,128]{2,1,0:T(8,128)S(1)}) custom-call(f32[16,64,128]{2,1,0:T(8,128)S(1)} %shard_map.120.blocks_in, f32[8,144,128]{2,1,0:T(8,128)S(1)} %get-tuple-element.144.total, ...), custom_call_target="tpu_custom_call", output_to_operand_aliasing={{0}: (0, {})} | custom-call | bytes 900000 | tf_op jit(solution)/shard_map/pallas_call | solution.py:36
  47.4 0.8 %collective-permute-done.13.refs_2_ = f32[4,64,128]{2,1,0:T(8,128)S(1)} collective-permute-done((f32[4,64,128]{2,1,0:T(8,128)S(1)}, f32[4,64,128]{2,1,0:T(8,128)S(1)}, u32[]{:S(2)}, u32[]{:S(2)}) %collective-permute-start.13) | collective-permute-done | bytes 131104 | tf_op jit(solution)/shard_map/ppermute | solution.py:498
  48.5 1.6 %collective-permute-start.15 = (f32[4,64,128]{2,1,0:T(8,128)S(1)}, f32[4,64,128]{2,1,0:T(8,128)S(1)}, u32[]{:S(2)}, u32[]{:S(2)}) collective-permute-start(f32[4,64,128]{2,1,0:T(8,128)S(1)} %get-tuple-element.151), channel_id=1, source_target_pairs={{0,4},{2,6},{4,0},{6,2},{8,12},{10,14},{12,8},{14,10},{16,20},{18,... | collective-permute-start | bytes 393224 | tf_op jit(solution)/shard_map/ppermute | solution.py:498
  50.0 4.2 %collective-permute-done.15.refs_1_ = f32[4,64,128]{2,1,0:T(8,128)S(1)} collective-permute-done((f32[4,64,128]{2,1,0:T(8,128)S(1)}, f32[4,64,128]{2,1,0:T(8,128)S(1)}, u32[]{:S(2)}, u32[]{:S(2)}) %collective-permute-start.15) | collective-permute-done | bytes 131104 | tf_op jit(solution)/shard_map/ppermute | solution.py:498
  54.4 2.3 %collective-permute-start.17 = (f32[64,128]{1,0:T(8,128)S(1)}, f32[64,128]{1,0:T(8,128)S(1)}, u32[]{:S(2)}, u32[]{:S(2)}) collective-permute-start(f32[64,128]{1,0:T(8,128)S(1)} %get-tuple-element.154), channel_id=1, source_target_pairs={{0,16},{2,18},{4,20},{6,22},{8,24},{10,26},{12,28},{14,30},{16,0},... | collective-permute-start | bytes 98312 | tf_op jit(solution)/shard_map/ppermute | solution.py:498
  56.7 2.0 %collective-permute-start.18 = (f32[64,128]{1,0:T(8,128)S(1)}, f32[64,128]{1,0:T(8,128)S(1)}, u32[]{:S(2)}, u32[]{:S(2)}) collective-permute-start(f32[64,128]{1,0:T(8,128)S(1)} %get-tuple-element.155), channel_id=1, source_target_pairs={{0,24},{2,26},{4,28},{6,30},{8,16},{10,18},{12,20},{14,22},{16,8},... | collective-permute-start | bytes 98312 | tf_op jit(solution)/shard_map/ppermute | solution.py:498
  58.8 1.7 %shard_map.119 = f32[1,6,8,128,128]{4,3,2,1,0:T(8,128)} custom-call(f32[3,9,144,128]{3,2,1,0:T(8,128)S(1)} %get-tuple-element.142.e, f32[3,9,144,128]{3,2,1,0:T(8,128)S(1)} %get-tuple-element.143.h), custom_call_target="tpu_custom_call" | custom-call | bytes 5100000 | tf_op jit(solution)/shard_map/pallas_call | solution.py:36
  60.5 2.0 %collective-permute-done.18.refs_3_ = f32[64,128]{1,0:T(8,128)S(1)} collective-permute-done((f32[64,128]{1,0:T(8,128)S(1)}, f32[64,128]{1,0:T(8,128)S(1)}, u32[]{:S(2)}, u32[]{:S(2)}) %collective-permute-start.18) | collective-permute-done | bytes 32800 | tf_op jit(solution)/shard_map/ppermute | solution.py:498
  (46 shorter events, 6.4 us)
Async XLA Ops:
  0.6 15.9 %copy-start.3 = (s32[1,3]{1,0:T(1,128)S(1)}, s32[1,3]{1,0:T(1,128)}, u32[]{:S(2)}) copy-start(s32[1,3]{1,0:T(1,128)} %source.1) | copy-start | bytes 40
  0.6 8.6 %collective-permute-start.2 = (f32[64,128]{1,0:T(8,128)}, f32[64,128]{1,0:T(8,128)S(1)}, u32[]{:S(2)}, u32[]{:S(2)}) collective-permute-start(f32[64,128]{1,0:T(8,128)} %bitcast.3), channel_id=1, source_target_pairs={{0,24},{2,26},{4,28},{6,30},{8,16},{10,18},{12,20},{14,22},{16,8},... | collective-permute-start | bytes 98312 | tf_op jit(solution)/shard_map/ppermute | solution.py:498
  5.8 5.0 %collective-permute-start.1 = (f32[64,128]{1,0:T(8,128)}, f32[64,128]{1,0:T(8,128)S(1)}, u32[]{:S(2)}, u32[]{:S(2)}) collective-permute-start(f32[64,128]{1,0:T(8,128)} %bitcast.4), channel_id=1, source_target_pairs={{0,16},{2,18},{4,20},{6,22},{8,24},{10,26},{12,28},{14,30},{16,0},... | collective-permute-start | bytes 98312 | tf_op jit(solution)/shard_map/ppermute | solution.py:498
  5.8 5.0 %collective-permute-start = (f32[64,128]{1,0:T(8,128)}, f32[64,128]{1,0:T(8,128)S(1)}, u32[]{:S(2)}, u32[]{:S(2)}) collective-permute-start(f32[64,128]{1,0:T(8,128)} %bitcast.5), channel_id=1, source_target_pairs={{0,8},{2,10},{4,12},{6,14},{8,0},{10,2},{12,4},{14,6},{16,24},{18,... | collective-permute-start | bytes 98312 | tf_op jit(solution)/shard_map/ppermute | solution.py:498
  7.8 15.4 %collective-permute-start.3 = (f32[2,2,128,128]{3,2,1,0:T(8,128)S(1)}, f32[2,2,128,128]{3,2,1,0:T(8,128)S(1)}, u32[]{:S(2)}, u32[]{:S(2)}) collective-permute-start(f32[2,2,128,128]{3,2,1,0:T(8,128)S(1)} %get-tuple-element.83), channel_id=1, source_target_pairs={{0,1},{1,0},{2,3},{3,2},{4,5},{5,4},{6,7},{7,6},{8,9},{9,8},{10,11... | collective-permute-start | bytes 786440 | tf_op jit(solution)/shard_map/ppermute | solution.py:498
  10.8 5.0 %collective-permute-start.4 = (f32[4,64,128]{2,1,0:T(8,128)S(1)}, f32[4,64,128]{2,1,0:T(8,128)S(1)}, u32[]{:S(2)}, u32[]{:S(2)}) collective-permute-start(f32[4,64,128]{2,1,0:T(8,128)S(1)} %shard_map.96.near.refs_0_), channel_id=1, source_target_pairs={{0,4},{2,6},{4,0},{6,2},{8,12},{10,14},{12,8},{14,10},{16,20},{18,... | collective-permute-start | bytes 393224 | tf_op jit(solution)/shard_map/ppermute | solution.py:498
  12.4 11.3 %collective-permute-start.5 = (f32[4,64,128]{2,1,0:T(8,128)S(1)}, f32[4,64,128]{2,1,0:T(8,128)S(1)}, u32[]{:S(2)}, u32[]{:S(2)}) collective-permute-start(f32[4,64,128]{2,1,0:T(8,128)S(1)} %shard_map.96.near.refs_0_), channel_id=1, source_target_pairs={{0,2},{2,0},{4,6},{6,4},{8,10},{10,8},{12,14},{14,12},{16,18},{18,... | collective-permute-start | bytes 393224 | tf_op jit(solution)/shard_map/ppermute | solution.py:498
  15.8 7.8 %collective-permute-start.6 = (f32[4,64,128]{2,1,0:T(8,128)S(1)}, f32[4,64,128]{2,1,0:T(8,128)S(1)}, u32[]{:S(2)}, u32[]{:S(2)}) collective-permute-start(f32[4,64,128]{2,1,0:T(8,128)S(1)} %collective-permute-done.4.refs_1_), channel_id=1, source_target_pairs={{0,2},{2,0},{4,6},{6,4},{8,10},{10,8},{12,14},{14,12},{16,18},{18,... | collective-permute-start | bytes 393224 | tf_op jit(solution)/shard_map/ppermute | solution.py:498
  23.4 0.7 %copy-start = (s32[16]{0:T(128)S(1)}, s32[16]{0:T(128)}, u32[]{:S(2)}) copy-start(s32[16]{0:T(128)} %block_ids.1) | copy-start | bytes 196
  23.4 0.7 %copy-start.1 = (s32[16]{0:T(128)S(1)}, s32[16]{0:T(128)}, u32[]{:S(2)}) copy-start(s32[16]{0:T(128)} %refs_5_.1) | copy-start | bytes 196
  23.4 0.7 %copy-start.2 = (f32[4]{0:T(128)S(1)}, f32[4]{0:T(128)}, u32[]{:S(2)}) copy-start(f32[4]{0:T(128)} %refs_6_.1) | copy-start | bytes 52
  25.1 6.1 %collective-permute-start.7 = (f32[2,128,128]{2,1,0:T(8,128)S(1)}, f32[2,128,128]{2,1,0:T(8,128)S(1)}, u32[]{:S(2)}, u32[]{:S(2)}) collective-permute-start(f32[2,128,128]{2,1,0:T(8,128)S(1)} %get-tuple-element.106), channel_id=1, source_target_pairs={{0,1},{1,0},{2,3},{3,2},{4,5},{5,4},{6,7},{7,6},{8,9},{9,8},{10,11... | collective-permute-start | bytes 393224 | tf_op jit(solution)/shard_map/ppermute | solution.py:498
  28.0 6.5 %collective-permute-start.8 = (f32[2,128,128]{2,1,0:T(8,128)S(1)}, f32[2,128,128]{2,1,0:T(8,128)S(1)}, u32[]{:S(2)}, u32[]{:S(2)}) collective-permute-start(f32[2,128,128]{2,1,0:T(8,128)S(1)} %get-tuple-element.113), channel_id=1, source_target_pairs={{0,1},{1,0},{2,3},{3,2},{4,5},{5,4},{6,7},{7,6},{8,9},{9,8},{10,11... | collective-permute-start | bytes 393224 | tf_op jit(solution)/shard_map/ppermute | solution.py:498
  31.4 5.7 %collective-permute-start.9 = (f32[2,128,128]{2,1,0:T(8,128)S(1)}, f32[2,128,128]{2,1,0:T(8,128)S(1)}, u32[]{:S(2)}, u32[]{:S(2)}) collective-permute-start(f32[2,128,128]{2,1,0:T(8,128)S(1)} %get-tuple-element.120), channel_id=1, source_target_pairs={{0,1},{1,0},{2,3},{3,2},{4,5},{5,4},{6,7},{7,6},{8,9},{9,8},{10,11... | collective-permute-start | bytes 393224 | tf_op jit(solution)/shard_map/ppermute | solution.py:498
  34.7 5.7 %collective-permute-start.10 = (f32[2,128,128]{2,1,0:T(8,128)S(1)}, f32[2,128,128]{2,1,0:T(8,128)S(1)}, u32[]{:S(2)}, u32[]{:S(2)}) collective-permute-start(f32[2,128,128]{2,1,0:T(8,128)S(1)} %get-tuple-element.127), channel_id=1, source_target_pairs={{0,1},{1,0},{2,3},{3,2},{4,5},{5,4},{6,7},{7,6},{8,9},{9,8},{10,11... | collective-permute-start | bytes 393224 | tf_op jit(solution)/shard_map/ppermute | solution.py:498
  37.3 6.5 %collective-permute-start.11 = (f32[2,128,128]{2,1,0:T(8,128)S(1)}, f32[2,128,128]{2,1,0:T(8,128)S(1)}, u32[]{:S(2)}, u32[]{:S(2)}) collective-permute-start(f32[2,128,128]{2,1,0:T(8,128)S(1)} %get-tuple-element.134), channel_id=1, source_target_pairs={{0,1},{1,0},{2,3},{3,2},{4,5},{5,4},{6,7},{7,6},{8,9},{9,8},{10,11... | collective-permute-start | bytes 393224 | tf_op jit(solution)/shard_map/ppermute | solution.py:498
  40.6 5.3 %collective-permute-start.12 = (f32[2,128,128]{2,1,0:T(8,128)S(1)}, f32[2,128,128]{2,1,0:T(8,128)S(1)}, u32[]{:S(2)}, u32[]{:S(2)}) collective-permute-start(f32[2,128,128]{2,1,0:T(8,128)S(1)} %get-tuple-element.141), channel_id=1, source_target_pairs={{0,1},{1,0},{2,3},{3,2},{4,5},{5,4},{6,7},{7,6},{8,9},{9,8},{10,11... | collective-permute-start | bytes 393224 | tf_op jit(solution)/shard_map/ppermute | solution.py:498
  46.9 1.4 %collective-permute-start.13 = (f32[4,64,128]{2,1,0:T(8,128)S(1)}, f32[4,64,128]{2,1,0:T(8,128)S(1)}, u32[]{:S(2)}, u32[]{:S(2)}) collective-permute-start(f32[4,64,128]{2,1,0:T(8,128)S(1)} %get-tuple-element.148), channel_id=1, source_target_pairs={{0,2},{2,0},{4,6},{6,4},{8,10},{10,8},{12,14},{14,12},{16,18},{18,... | collective-permute-start | bytes 393224 | tf_op jit(solution)/shard_map/ppermute | solution.py:498
  46.9 1.5 %collective-permute-start.14 = (f32[4,64,128]{2,1,0:T(8,128)S(1)}, f32[4,64,128]{2,1,0:T(8,128)S(1)}, u32[]{:S(2)}, u32[]{:S(2)}) collective-permute-start(f32[4,64,128]{2,1,0:T(8,128)S(1)} %get-tuple-element.149), channel_id=1, source_target_pairs={{0,2},{2,0},{4,6},{6,4},{8,10},{10,8},{12,14},{14,12},{16,18},{18,... | collective-permute-start | bytes 393224 | tf_op jit(solution)/shard_map/ppermute | solution.py:498
  48.5 5.8 %collective-permute-start.15 = (f32[4,64,128]{2,1,0:T(8,128)S(1)}, f32[4,64,128]{2,1,0:T(8,128)S(1)}, u32[]{:S(2)}, u32[]{:S(2)}) collective-permute-start(f32[4,64,128]{2,1,0:T(8,128)S(1)} %get-tuple-element.151), channel_id=1, source_target_pairs={{0,4},{2,6},{4,0},{6,2},{8,12},{10,14},{12,8},{14,10},{16,20},{18,... | collective-permute-start | bytes 393224 | tf_op jit(solution)/shard_map/ppermute | solution.py:498
  54.3 6.2 %collective-permute-start.16 = (f32[64,128]{1,0:T(8,128)S(1)}, f32[64,128]{1,0:T(8,128)S(1)}, u32[]{:S(2)}, u32[]{:S(2)}) collective-permute-start(f32[64,128]{1,0:T(8,128)S(1)} %get-tuple-element.153), channel_id=1, source_target_pairs={{0,8},{2,10},{4,12},{6,14},{8,0},{10,2},{12,4},{14,6},{16,24},{18,... | collective-permute-start | bytes 98312 | tf_op jit(solution)/shard_map/ppermute | solution.py:498
  54.4 6.1 %collective-permute-start.17 = (f32[64,128]{1,0:T(8,128)S(1)}, f32[64,128]{1,0:T(8,128)S(1)}, u32[]{:S(2)}, u32[]{:S(2)}) collective-permute-start(f32[64,128]{1,0:T(8,128)S(1)} %get-tuple-element.154), channel_id=1, source_target_pairs={{0,16},{2,18},{4,20},{6,22},{8,24},{10,26},{12,28},{14,30},{16,0},... | collective-permute-start | bytes 98312 | tf_op jit(solution)/shard_map/ppermute | solution.py:498
  56.7 5.7 %collective-permute-start.18 = (f32[64,128]{1,0:T(8,128)S(1)}, f32[64,128]{1,0:T(8,128)S(1)}, u32[]{:S(2)}, u32[]{:S(2)}) collective-permute-start(f32[64,128]{1,0:T(8,128)S(1)} %get-tuple-element.155), channel_id=1, source_target_pairs={{0,24},{2,26},{4,28},{6,30},{8,16},{10,18},{12,20},{14,22},{16,8},... | collective-permute-start | bytes 98312 | tf_op jit(solution)/shard_map/ppermute | solution.py:498

commit v6 on v5

--- a/solution.py
+++ b/solution.py
@@ -85,14 +85,15 @@
         for c, value in enumerate(values):
             ref[c, layer, pl.ds(PAD + first, size), :] = value
 
-    def put_h(self, layer, double=False, alone=False):
+    def put_h(self, layer, given=None, alone=False):
         for first, size in chunks(self.rows):
             rows = pl.ds(PAD + first, size)
             after = pl.ds(PAD + first + 1, size)
             ex, ey, ez = self.read(self.e, layer, first, size)
-            hx, hy, hz = self.read(self.h, layer, first, size)
-            if double:
-                hx, hy, hz = hx + hx, hy + hy, hz + hz
+            if given is None:
+                hx, hy, hz = self.read(self.h, layer, first, size)
+            else:
+                hx, hy, hz = (value + value for value in given(layer, first, size))
             if alone:
                 rise_x, rise_y = -ex, -ey
             else:
@@ -216,8 +217,12 @@
     held_copy.wait()
 
 
-def prepare_kernel(source, total, edges, forced):
+def prepare_kernel(
+    layout, source, block_ids, material_idx, material_eps, total, edges, forced, base, place
+):
     depth, rows, width_y = forced.shape
+    nblock = block_ids.shape[0]
+    block_rows = rows // nblock
     empty = jnp.zeros(total.shape[1:], F32)
     edges[0] = empty
     edges[1] = empty
@@ -230,42 +235,45 @@
     for layer in range(depth):
         total[layer] = empty
         forced[layer] = jnp.where(level == layer, 1.0, 0.0) * profile
-
-
-def first_kernel(given, near, e, h, curls, sems):
+    for block in range(nblock):
+        value = jnp.full((block_rows, width_y), material_eps[material_idx[block]], F32)
+        base[pl.ds(block * block_rows, block_rows), :] = value
+    me = lax.axis_index("grp")
+    block = lax.broadcasted_iota(jnp.int32, (nblock, width_y), 0)
+    for slot, mask in enumerate(mask for masks in layout for mask in masks):
+        place[slot] = jnp.where(block == block_ids[me ^ mask], 1.0, 0.0)
+
+
+def first_kernel(given, near, e, h, curls):
     win = Window(e, h)
     rows, width_y = win.rows, e.shape[3]
-    copies = [
-        pltpu.make_async_copy(
-            given.at[0, comp],
-            (e if comp < 3 else h).at[comp % 3, pl.ds(0, win.depth), pl.ds(PAD, rows), :],
-            sems.at[comp],
-        )
-        for comp in range(6)
-    ]
-    for copy in copies:
-        copy.start()
     margin = jnp.zeros((PAD, width_y), F32)
     empty = jnp.zeros((rows + 2 * PAD, width_y), F32)
-
-    def clear(layer, carry):
-        for ref in (e, h):
-            for comp in range(3):
-                ref[comp, layer, pl.ds(0, PAD), :] = margin
-                ref[comp, layer, pl.ds(PAD + rows, PAD), :] = margin
-        return carry
-
-    lax.fori_loop(0, win.depth, clear, 0)
     for comp in range(3):
         e[comp, win.depth] = empty
         h[comp, win.depth] = empty
-    for copy in copies:
-        copy.wait()
-    win.put_h(0, True)
-    win.put_h(1, True)
+
+    def copy(layer):
+        for comp in range(3):
+            for ref in (e, h):
+                ref[comp, layer, pl.ds(0, PAD), :] = margin
+                ref[comp, layer, pl.ds(PAD + rows, PAD), :] = margin
+            for first, size in chunks(rows):
+                here = pl.ds(first, size)
+                e[comp, layer, pl.ds(PAD + first, size), :] = given[0, comp, layer, here, :]
+
+    def from_given(layer, first, size):
+        return [given[0, 3 + c, layer, pl.ds(first, size), :] for c in range(3)]
+
+    copy(0)
+    copy(1)
+    win.put_h(0, from_given)
+    copy(2)
+    win.put_h(1, from_given)
 
     def body(layer, carry):
-        win.put_h(layer + 1, True)
+        pl.when(layer + 2 < win.depth)(lambda: copy(layer + 2))
+        win.put_h(layer + 1, from_given)
         win.put_curl(curls, layer, layer - 1)
         return carry
 
@@ -361,44 +369,55 @@
     win.put_e(highest, highest - 1, None, other, total)
 
 
-def coef_layer(layer, coef, blocks, placed, base):
-    nblock = blocks.shape[0]
-    rows = base.shape[0]
-    block_rows = rows // nblock
-    for block in range(nblock):
-        source = pl.ds(pl.multiple_of(layer * block_rows, block_rows), block_rows)
-        placed[pl.ds(PAD + block * block_rows, block_rows), :] = blocks[block, source, :]
-    for first, size in chunks(rows):
+def coef_layer(layer, coef, placed, base):
+    for first, size in chunks(base.shape[0]):
         here = pl.ds(first, size)
         coef[layer, here, :] = 0.25 / (base[here, :] + 3.0 * filtered(placed, first, size))
 
 
-def coef_edge_kernel(layout, count, *refs):
-    parts = refs[:count]
-    block_ids, material_idx, material_eps, coef, blocks, base, placed = refs[count:]
+def clear_margins(placed):
+    rows = placed.shape[0] - 2 * PAD
+    margin = jnp.zeros((PAD, placed.shape[1]), F32)
+    placed[pl.ds(0, PAD), :] = margin
+    placed[pl.ds(PAD + rows, PAD), :] = margin
+
+
+def coef_edge_kernel(count, *refs):
+    parts, (place, base, coef, placed) = refs[:count], refs[count:]
+    depth, rows, width_y = coef.shape
+    nblock = place.shape[0]
+    block_rows = rows // nblock
+    for which, layer in enumerate((0, depth - 1)):
+        there = placed.at[which]
+        clear_margins(there)
+        source = pl.ds(layer * block_rows, block_rows)
+        pieces = [part[slot, source, :] for part in parts for slot in range(part.shape[0])]
+        for block in range(nblock):
+            value = None
+            for slot, piece in enumerate(pieces):
+                term = place[slot, pl.ds(block, 1), :] * piece
+                value = term if value is None else value + term
+            there[pl.ds(PAD + block * block_rows, block_rows), :] = value
+    for which, layer in enumerate((0, depth - 1)):
+        coef_layer(layer, coef, placed.at[which], base)
+
+
+def coef_inner_kernel(layout, coef_in, *refs):
+    parts, (block_ids, base, coef, blocks, placed) = refs[: len(layout)], refs[len(layout) :]
+    depth, rows, width_y = coef.shape
     nblock = blocks.shape[0]
-    depth, rows, width_y = coef.shape
     block_rows = rows // nblock
     me = lax.axis_index("grp")
+    clear_margins(placed)
     for part, masks in zip(parts, layout):
         for slot, mask in enumerate(masks):
             blocks[block_ids[me ^ mask]] = part[slot]
-    for block in range(nblock):
-        level = jnp.full((block_rows, width_y), material_eps[material_idx[block]], F32)
-        base[pl.ds(block * block_rows, block_rows), :] = level
-    placed[pl.ds(0, PAD), :] = jnp.zeros((PAD, width_y), F32)
-    placed[pl.ds(PAD + rows, PAD), :] = jnp.zeros((PAD, width_y), F32)
-    coef_layer(0, coef, blocks, placed, base)
-    coef_layer(depth - 1, coef, blocks, placed, base)
-
-
-def coef_inner_kernel(coef_in, blocks, base, coef, placed):
-    depth, rows, width_y = coef.shape
-    placed[pl.ds(0, PAD), :] = jnp.zeros((PAD, width_y), F32)
-    placed[pl.ds(PAD + rows, PAD), :] = jnp.zeros((PAD, width_y), F32)
 
     def body(layer, carry):
-        coef_layer(layer, coef, blocks, placed, base)
+        for block in range(nblock):
+            source = pl.ds(pl.multiple_of(layer * block_rows, block_rows), block_rows)
+            placed[pl.ds(PAD + block * block_rows, block_rows), :] = blocks[block, source, :]
+        coef_layer(layer, coef, placed, base)
         return carry
 
     lax.fori_loop(1, depth - 1, body, 0)
@@ -412,40 +431,68 @@
     return (prev_col(along) + 2.0 * along + next_col(along)) * 0.0625
 
 
+def tie_kernel(*refs):
+    pass
+
+
+def tie(array, others):
+    return call(
+        tie_kernel, on_chip(*array.shape), IN_VMEM, [array] + others,
+        [IN_VMEM] * (1 + len(others)), aliases={0: 0},
+    )
+
+
 def pack_kernel(*refs):
     out = refs[-1]
     for slot, ref in enumerate(refs[:-1]):
         out[slot] = ref[...]
 
 
-def filter_layer(values, layer, blocks, wide):
+def filter_inner_kernel(layout, total, block_ids, *rest):
+    parts, (blocks, wide) = rest[:-2], rest[-2:]
+    depth = total.shape[0]
     nblock = blocks.shape[0]
     rows = wide.shape[0]
     block_rows = rows // nblock
-    for first, size in chunks(rows):
-        wide[pl.ds(first, size), :] = filtered(values, first, size)
-    for block in range(nblock):
-        target = pl.ds(pl.multiple_of(layer * block_rows, block_rows), block_rows)
-        blocks[block, target, :] = wide[pl.ds(block * block_rows, block_rows), :]
-
-
-def filter_inner_kernel(total, blocks, wide):
+    me = lax.axis_index("grp")
+
     def body(layer, carry):
-        filter_layer(total.at[layer], layer, blocks, wide)
+        for first, size in chunks(rows):
+            wide[pl.ds(first, size), :] = filtered(total.at[layer], first, size)
+        for block in range(nblock):
+            target = pl.ds(pl.multiple_of(layer * block_rows, block_rows), block_rows)
+            blocks[block, target, :] = wide[pl.ds(block * block_rows, block_rows), :]
         return carry
 
-    lax.fori_loop(1, total.shape[0] - 1, body, 0)
-
-
-def filter_edge_kernel(layout, blocks_in, total, edges, block_ids, blocks, *rest):
-    parts, wide, ends = rest[:-2], rest[-2], rest[-1]
-    me = lax.axis_index("grp")
-    for slot, layer in enumerate((0, total.shape[0] - 1)):
-        ends[slot] = total[layer] + edges[slot]
-        filter_layer(ends.at[slot], layer, blocks, wide.at[slot])
+    lax.fori_loop(1, depth - 1, body, 0)
+    inner = pl.ds(block_rows, (depth - 2) * block_rows)
     for part, masks in zip(parts, layout):
         for slot, mask in enumerate(masks):
-            part[slot] = blocks[block_ids[me ^ mask]]
+            part[slot, inner, :] = blocks[block_ids[me ^ mask], inner, :]
+
+
+def filter_edge_kernel(count, *refs):
+    total, edges, place = refs[count : count + 3]
+    parts, (sums, wide) = refs[count + 3 : -2], refs[-2:]
+    depth = total.shape[0]
+    nblock = place.shape[0]
+    rows = wide.shape[1]
+    block_rows = rows // nblock
+    for which, layer in enumerate((0, depth - 1)):
+        sums[which] = total[layer] + edges[which]
+        for first, size in chunks(rows):
+            wide[which, pl.ds(first, size), :] = filtered(sums.at[which], first, size)
+    for which, layer in enumerate((0, depth - 1)):
+        blocks = [
+            wide[which, pl.ds(block * block_rows, block_rows), :] for block in range(nblock)
+        ]
+        target = pl.ds(layer * block_rows, block_rows)
+        for slot in range(nblock):
+            value = None
+            for block, piece in enumerate(blocks):
+                term = place[slot, pl.ds(block, 1), :] * piece
+                value = term if value is None else value + term
+            parts[slot // parts[0].shape[0]][slot % parts[0].shape[0], target, :] = value
 
 
 def add_kernel(*refs):
@@ -538,7 +585,6 @@
     total_shape = on_chip(depth, width_x + 2 * PAD, width_y)
     edges_shape = on_chip(2, width_x + 2 * PAD, width_y)
     coef_shape = on_chip(depth, width_x, width_y)
-    blocks_shape = on_chip(nblock, *piece)
     plane = on_chip(width_x, width_y)
     padded = pltpu.VMEM((width_x + 2 * PAD, width_y), F32)
 
@@ -555,15 +601,16 @@
     below, above = trade(pays)
 
     near = call(pack_kernel, on_chip(*group), IN_VMEM, [own] + got, [IN_VMEM] * far)
-    parts = [near] + [swap_over(near, "grp", mask) for mask in middle_masks[1:]]
-    parts = parts + [swap_over(part, "grp", 1) for part in parts]
-
-    total, edges, forced = call(
-        prepare_kernel,
-        [total_shape, edges_shape, on_chip(depth, width_x, width_y)],
-        [IN_VMEM] * 3,
-        [source_pos],
-        [IN_SMEM],
+    others = [swap_over(near, "grp", mask) for mask in middle_masks[1:]]
+    near_across = swap_over(near, "grp", 1)
+
+    place_shape = on_chip(nblock, nblock, width_y)
+    total, edges, forced, base, place = call(
+        functools.partial(prepare_kernel, layout),
+        [total_shape, edges_shape, on_chip(depth, width_x, width_y), plane, place_shape],
+        [IN_VMEM] * 5,
+        [source_pos, block_ids, material_idx, material_eps],
+        [IN_SMEM] * 4,
     )
     fields = []
     for evo, given in enumerate((fwd_fields, adj_fields)):
@@ -572,11 +619,13 @@
             [field_shape, field_shape, curls_shape],
             [IN_VMEM] * 3,
             [given, near],
-            [IN_HBM, IN_VMEM],
-            [pltpu.SemaphoreType.DMA((6,))],
-            micros=2.3,
+            [IN_VMEM, IN_VMEM],
+            micros=1.5,
         )
         fields.append((e, h, curls))
+    others = [tie(part, [forced] + [e for e, _, _ in fields]) for part in others]
+    parts = [near] + others + [near_across] + [swap_over(part, "grp", 1) for part in others]
+
     taken = []
     for evo, (e, h, curls) in enumerate(fields):
         h, curls = call(
@@ -589,13 +638,13 @@
         )
         taken.append((e, h, curls))
     (e_fwd, h_fwd, curls_fwd), (e_adj, h_adj, curls_adj) = taken
-    coef, blocks, base = call(
-        functools.partial(coef_edge_kernel, layout, len(parts)),
-        [coef_shape, blocks_shape, plane],
-        [IN_VMEM] * 3,
-        parts + [block_ids, material_idx, material_eps],
-        [IN_VMEM] * len(parts) + [IN_SMEM] * 3,
-        [padded],
+    coef = call(
+        functools.partial(coef_edge_kernel, len(parts)),
+        coef_shape,
+        IN_VMEM,
+        parts + [place, base],
+        [IN_VMEM] * (len(parts) + 2),
+        [pltpu.VMEM((2, width_x + 2 * PAD, width_y), F32)],
     )
 
     arrived_fwd, arrived_adj = [curls_fwd], [curls_adj]
@@ -613,8 +662,14 @@
             arrived_fwd = trade(pays)
         if step == 0:
             coef = call(
-                coef_inner_kernel, coef_shape, IN_VMEM, [coef, blocks, base], [IN_VMEM] * 3,
-                [padded], aliases={0: 0}, micros=0.7,
+                functools.partial(coef_inner_kernel, layout),
+                coef_shape,
+                IN_VMEM,
+                [coef] + parts + [block_ids, base],
+                [IN_VMEM] * (1 + len(parts)) + [IN_SMEM, IN_VMEM],
+                [pltpu.VMEM((nblock,) + piece, F32), padded],
+                aliases={0: 0},
+                micros=0.9,
             )
             e_fwd, e_adj, total = call(
                 begin_kernel,
@@ -636,9 +691,14 @@
                 micros=1.2,
             )
         if not more:
-            blocks = call(
-                filter_inner_kernel, blocks_shape, IN_VMEM, [total], [IN_VMEM],
-                [pltpu.VMEM((width_x, width_y), F32)], micros=0.6,
+            parts = call(
+                functools.partial(filter_inner_kernel, layout),
+                [on_chip(*group)] * len(layout),
+                [IN_VMEM] * len(layout),
+                [total, block_ids],
+                [IN_VMEM, IN_SMEM],
+                [pltpu.VMEM((nblock,) + piece, F32), pltpu.VMEM((width_x, width_y), F32)],
+                micros=1.1,
             )
         e_adj, h_adj, e_fwd, edges, *pays = call(
             functools.partial(edge_kernel, step, 1),
@@ -660,17 +720,17 @@
                 micros=1.1,
             )
 
-    blocks, *parts = call(
-        functools.partial(filter_edge_kernel, layout),
-        [blocks_shape] + [on_chip(*group)] * len(layout),
-        [IN_VMEM] * (1 + len(layout)),
-        [blocks, total, edges, block_ids],
-        [IN_VMEM] * 3 + [IN_SMEM],
+    parts = call(
+        functools.partial(filter_edge_kernel, len(layout)),
+        [on_chip(*group)] * len(layout),
+        [IN_VMEM] * len(layout),
+        list(parts) + [total, edges, place],
+        [IN_VMEM] * (len(layout) + 3),
         [
+            pltpu.VMEM((2, width_x + 2 * PAD, width_y), F32),
             pltpu.VMEM((2, width_x, width_y), F32),
-            pltpu.VMEM((2, width_x + 2 * PAD, width_y), F32),
         ],
-        aliases={0: 0},
+        aliases={slot: slot for slot in range(len(layout))},
     )
     got = [swap_over(part, "grp", 1) for part in parts[middle:]]
     sums = call(

time: 63.3 us -> 56.4 us (0.89)
  Pallas kernels: 23.7 us -> 19.7 us
  starting transfers between devices: 22.9 us -> 21.5 us
  waiting for transfers between devices: 14.2 us -> 13.2 us
    pallas_call x30 -> x31, Pallas kernels: 23.7 us -> 19.7 us  [call(): pl.pallas_call(kernel, out_shape=outs, in_specs=specs, out_specs=out_spec...]
    ppermute x19, starting transfers between devices: 22.9 us -> 21.5 us  [swap_over(): lax.ppermute(array, axis, [(i, i ^ mask) for i in range(lax.axis_size(axi...]
    ppermute x19, waiting for transfers between devices: 14.2 us -> 13.2 us  [swap_over(): lax.ppermute(array, axis, [(i, i ^ mask) for i in range(lax.axis_size(axi...]
  transfers between devices with their start and end apart: 19 -> 19, of which waited for: 9 -> 11; matrix products, arithmetic and copies ran while one was open for 0% -> 0% of each run, Pallas kernels for 34% -> 32%
where the time goes in v6:
time: 56.4 us; the launch traced here: 56.2 us
  starting transfers between devices  21.5 us (38%)
  Pallas kernels  19.7 us (35%)
  waiting for transfers between devices  13.2 us (23%)
  between operations  1.67 us (3%)
    ppermute x19, starting transfers between devices, swap_over(): lax.ppermute(array, axis, [(i, i ^ mask) for i in range(lax.axis_size(axi...  21.5 us
    pallas_call x31, Pallas kernels, call(): pl.pallas_call(kernel, out_shape=outs, in_specs=specs, out_specs=out_spec...  19.7 us
    ppermute x19, waiting for transfers between devices, swap_over(): lax.ppermute(array, axis, [(i, i ^ mask) for i in range(lax.axis_size(axi...  13.2 us
  transfers between devices with their start and end apart: 19, of which 11 were waited for; matrix products, arithmetic and copies ran while one was open for 0% of the time, Pallas kernels for 32%

profile of v6, /device:TPU:0, one launch (start us, length us, event | category | flops | bytes accessed | tf_op | source)
XLA Modules:
  0.0 56.2 jit_solution(10340170701277531564)
XLA Ops:
  0.7 5.1 %collective-permute-start.2 = (f32[64,128]{1,0:T(8,128)}, f32[64,128]{1,0:T(8,128)S(1)}, u32[]{:S(2)}, u32[]{:S(2)}) collective-permute-start(f32[64,128]{1,0:T(8,128)} %bitcast.3), channel_id=1, source_target_pairs={{0,24},{2,26},{4,28},{6,30},{8,16},{10,18},{12,20},{14,22},{16,8},... | collective-permute-start | bytes 98312 | tf_op jit(solution)/shard_map/ppermute | solution.py:545
  5.8 0.6 %collective-permute-start = (f32[64,128]{1,0:T(8,128)}, f32[64,128]{1,0:T(8,128)S(1)}, u32[]{:S(2)}, u32[]{:S(2)}) collective-permute-start(f32[64,128]{1,0:T(8,128)} %bitcast.5), channel_id=1, source_target_pairs={{0,8},{2,10},{4,12},{6,14},{8,0},{10,2},{12,4},{14,6},{16,24},{18,... | collective-permute-start | bytes 98312 | tf_op jit(solution)/shard_map/ppermute | solution.py:545
  6.4 1.4 %shard_map.95 = (f32[64,128]{1,0:T(8,128)S(1)}, f32[2,2,128,128]{3,2,1,0:T(8,128)S(1)}) custom-call(f32[1,6,8,128,128]{4,3,2,1,0:T(8,128)} %given.2, f32[1,6,8,128,128]{4,3,2,1,0:T(8,128)} %given.3, f32[64,128]{1,0:T(8,128)} %bitcast.6), custom_call_target="tpu_custom_call" | custom-call | bytes 900000 | tf_op jit(solution)/shard_map/pallas_call | solution.py:36
  7.8 1.4 %collective-permute-start.3 = (f32[2,2,128,128]{3,2,1,0:T(8,128)S(1)}, f32[2,2,128,128]{3,2,1,0:T(8,128)S(1)}, u32[]{:S(2)}, u32[]{:S(2)}) collective-permute-start(f32[2,2,128,128]{3,2,1,0:T(8,128)S(1)} %get-tuple-element.86), channel_id=1, source_target_pairs={{0,1},{1,0},{2,3},{3,2},{4,5},{5,4},{6,7},{7,6},{8,9},{9,8},{10,11... | collective-permute-start | bytes 786440 | tf_op jit(solution)/shard_map/ppermute | solution.py:545
  9.3 1.5 %collective-permute-done.1.refs_2_ = f32[64,128]{1,0:T(8,128)S(1)} collective-permute-done((f32[64,128]{1,0:T(8,128)}, f32[64,128]{1,0:T(8,128)S(1)}, u32[]{:S(2)}, u32[]{:S(2)}) %collective-permute-start.1) | collective-permute-done | bytes 32800 | tf_op jit(solution)/shard_map/ppermute | solution.py:545
  10.8 1.6 %collective-permute-start.4 = (f32[4,64,128]{2,1,0:T(8,128)S(1)}, f32[4,64,128]{2,1,0:T(8,128)S(1)}, u32[]{:S(2)}, u32[]{:S(2)}) collective-permute-start(f32[4,64,128]{2,1,0:T(8,128)S(1)} %shard_map.96.near.refs_0_), channel_id=1, source_target_pairs={{0,4},{2,6},{4,0},{6,2},{8,12},{10,14},{12,8},{14,10},{16,20},{18,... | collective-permute-start | bytes 393224 | tf_op jit(solution)/shard_map/ppermute | solution.py:545
  12.4 0.7 %shard_map.99 = (f32[8,144,128]{2,1,0:T(8,128)S(1)}, f32[2,144,128]{2,1,0:T(8,128)S(1)}, f32[8,128,128]{2,1,0:T(8,128)S(1)}, f32[128,128]{1,0:T(8,128)S(1)}, f32[16,16,128]{2,1,0:T(8,128)S(1)}) custom-call(s32[1,3]{1,0:T(1,128)S(1)} %copy-done.3, s32[16]{0:T(128)S(1)} %copy-done.2, s32[16]{0:T(128)S(1)} %copy-done.4, f32[4]{0:T(128)S(1)} %copy-done.5), custom_call_target="tpu_custom_call" | custom-call | bytes 900000 | tf_op jit(solution)/shard_map/pallas_call | solution.py:36
  13.2 1.2 %shard_map.100 = (f32[3,9,144,128]{3,2,1,0:T(8,128)S(1)}, f32[3,9,144,128]{3,2,1,0:T(8,128)S(1)}, f32[3,8,128,128]{3,2,1,0:T(8,128)S(1)}) custom-call(f32[1,6,8,128,128]{4,3,2,1,0:T(8,128)S(1)} %copy-done, f32[4,64,128]{2,1,0:T(8,128)S(1)} %shard_map.96.near.refs_0_), custom_call_target="tpu_custom_call" | custom-call | bytes 4500000 | tf_op jit(solution)/shard_map/pallas_call | solution.py:36
  14.4 1.2 %shard_map.97 = (f32[3,9,144,128]{3,2,1,0:T(8,128)S(1)}, f32[3,9,144,128]{3,2,1,0:T(8,128)S(1)}, f32[3,8,128,128]{3,2,1,0:T(8,128)S(1)}) custom-call(f32[1,6,8,128,128]{4,3,2,1,0:T(8,128)S(1)} %copy-done.1, f32[4,64,128]{2,1,0:T(8,128)S(1)} %shard_map.96.near.refs_0_), custom_call_target="tpu_custom_call" | custom-call | bytes 4500000 | tf_op jit(solution)/shard_map/pallas_call | solution.py:36
  17.8 1.5 %collective-permute-start.7 = (f32[2,128,128]{2,1,0:T(8,128)S(1)}, f32[2,128,128]{2,1,0:T(8,128)S(1)}, u32[]{:S(2)}, u32[]{:S(2)}) collective-permute-start(f32[2,128,128]{2,1,0:T(8,128)S(1)} %get-tuple-element.108), channel_id=1, source_target_pairs={{0,1},{1,0},{2,3},{3,2},{4,5},{5,4},{6,7},{7,6},{8,9},{9,8},{10,11... | collective-permute-start | bytes 393224 | tf_op jit(solution)/shard_map/ppermute | solution.py:545
  19.3 1.4 %shard_map.104.coef.refs_4_.refs_2_ = f32[8,128,128]{2,1,0:T(8,128)S(1)} custom-call(f32[8,128,128]{2,1,0:T(8,128)S(1)} %shard_map.102.refs_2_.coef_in, f32[4,64,128]{2,1,0:T(8,128)S(1)} %shard_map.96.near.refs_0_, f32[4,64,128]{2,1,0:T(8,128)S(1)} %shard_map.101.refs_1_, ...), custom_call_target="tpu_custom_call", output_to_operand_aliasing={{}: (0, {})} | custom-call | bytes 2700000 | tf_op jit(solution)/shard_map/pallas_call | solution.py:36
  21.9 1.2 %shard_map.108 = (f32[3,9,144,128]{3,2,1,0:T(8,128)S(1)}, f32[3,9,144,128]{3,2,1,0:T(8,128)S(1)}) custom-call(f32[3,9,144,128]{3,2,1,0:T(8,128)S(1)} %get-tuple-element.104.refs_0_, f32[3,9,144,128]{3,2,1,0:T(8,128)S(1)} %get-tuple-element.105.refs_1_, ...), custom_call_target="tpu_custom_call", output_to_operand_aliasing={{0}: (0, {}), {1}: (1, {})} | custom-call | bytes 3300000 | tf_op jit(solution)/shard_map/pallas_call | solution.py:36
  23.7 1.8 %collective-permute-start.9 = (f32[2,128,128]{2,1,0:T(8,128)S(1)}, f32[2,128,128]{2,1,0:T(8,128)S(1)}, u32[]{:S(2)}, u32[]{:S(2)}) collective-permute-start(f32[2,128,128]{2,1,0:T(8,128)S(1)} %get-tuple-element.122), channel_id=1, source_target_pairs={{0,1},{1,0},{2,3},{3,2},{4,5},{5,4},{6,7},{7,6},{8,9},{9,8},{10,11... | collective-permute-start | bytes 393224 | tf_op jit(solution)/shard_map/ppermute | solution.py:545
  25.5 1.3 %shard_map.110 = (f32[3,9,144,128]{3,2,1,0:T(8,128)S(1)}, f32[3,9,144,128]{3,2,1,0:T(8,128)S(1)}, f32[3,9,144,128]{3,2,1,0:T(8,128)S(1)}, f32[8,144,128]{2,1,0:T(8,128)S(1)}) custom-call(f32[3,9,144,128]{3,2,1,0:T(8,128)S(1)} %get-tuple-element.102.refs_0_, ...), custom_call_target="tpu_custom_call", output_to_operand_aliasing={{0}: (0, {}), {1}: (1, {}), {2}: (2, {}), {3}: (3, {})} | custom-call | bytes 3600000 | tf_op jit(solution)/shard_map/pallas_call | solution.py:36
  26.9 0.9 %collective-permute-done.8.refs_5_.refs_6_ = f32[2,128,128]{2,1,0:T(8,128)S(1)} collective-permute-done((f32[2,128,128]{2,1,0:T(8,128)S(1)}, f32[2,128,128]{2,1,0:T(8,128)S(1)}, u32[]{:S(2)}, u32[]{:S(2)}) %collective-permute-start.8) | collective-permute-done | bytes 131104 | tf_op jit(solution)/shard_map/ppermute | solution.py:545
  28.5 1.2 %shard_map.112 = (f32[3,9,144,128]{3,2,1,0:T(8,128)S(1)}, f32[3,9,144,128]{3,2,1,0:T(8,128)S(1)}) custom-call(f32[3,9,144,128]{3,2,1,0:T(8,128)S(1)} %get-tuple-element.118.refs_0_, f32[3,9,144,128]{3,2,1,0:T(8,128)S(1)} %get-tuple-element.119.refs_1_, ...), custom_call_target="tpu_custom_call", output_to_operand_aliasing={{0}: (0, {}), {1}: (1, {})} | custom-call | bytes 3300000 | tf_op jit(solution)/shard_map/pallas_call | solution.py:36
  29.7 0.6 %collective-permute-done.9.refs_5_.refs_6_ = f32[2,128,128]{2,1,0:T(8,128)S(1)} collective-permute-done((f32[2,128,128]{2,1,0:T(8,128)S(1)}, f32[2,128,128]{2,1,0:T(8,128)S(1)}, u32[]{:S(2)}, u32[]{:S(2)}) %collective-permute-start.9) | collective-permute-done | bytes 131104 | tf_op jit(solution)/shard_map/ppermute | solution.py:545
  30.5 1.0 %collective-permute-start.11 = (f32[2,128,128]{2,1,0:T(8,128)S(1)}, f32[2,128,128]{2,1,0:T(8,128)S(1)}, u32[]{:S(2)}, u32[]{:S(2)}) collective-permute-start(f32[2,128,128]{2,1,0:T(8,128)S(1)} %get-tuple-element.136), channel_id=1, source_target_pairs={{0,1},{1,0},{2,3},{3,2},{4,5},{5,4},{6,7},{7,6},{8,9},{9,8},{10,11... | collective-permute-start | bytes 393224 | tf_op jit(solution)/shard_map/ppermute | solution.py:545
  31.6 1.3 %shard_map.114 = (f32[3,9,144,128]{3,2,1,0:T(8,128)S(1)}, f32[3,9,144,128]{3,2,1,0:T(8,128)S(1)}, f32[3,9,144,128]{3,2,1,0:T(8,128)S(1)}, f32[8,144,128]{2,1,0:T(8,128)S(1)}) custom-call(f32[3,9,144,128]{3,2,1,0:T(8,128)S(1)} %get-tuple-element.116.refs_0_, ...), custom_call_target="tpu_custom_call", output_to_operand_aliasing={{0}: (0, {}), {1}: (1, {}), {2}: (2, {}), {3}: (3, {})} | custom-call | bytes 3600000 | tf_op jit(solution)/shard_map/pallas_call | solution.py:36
  32.9 1.5 %collective-permute-done.10.refs_5_.refs_6_ = f32[2,128,128]{2,1,0:T(8,128)S(1)} collective-permute-done((f32[2,128,128]{2,1,0:T(8,128)S(1)}, f32[2,128,128]{2,1,0:T(8,128)S(1)}, u32[]{:S(2)}, u32[]{:S(2)}) %collective-permute-start.10) | collective-permute-done | bytes 131104 | tf_op jit(solution)/shard_map/ppermute | solution.py:545
  35.0 1.2 %shard_map.116 = (f32[3,9,144,128]{3,2,1,0:T(8,128)S(1)}, f32[3,9,144,128]{3,2,1,0:T(8,128)S(1)}) custom-call(f32[3,9,144,128]{3,2,1,0:T(8,128)S(1)} %get-tuple-element.132.refs_0_, f32[3,9,144,128]{3,2,1,0:T(8,128)S(1)} %get-tuple-element.133.refs_1_, ...), custom_call_target="tpu_custom_call", output_to_operand_aliasing={{0}: (0, {}), {1}: (1, {})} | custom-call | bytes 3300000 | tf_op jit(solution)/shard_map/pallas_call | solution.py:36
  36.2 1.0 %collective-permute-done.11.refs_5_.refs_6_ = f32[2,128,128]{2,1,0:T(8,128)S(1)} collective-permute-done((f32[2,128,128]{2,1,0:T(8,128)S(1)}, f32[2,128,128]{2,1,0:T(8,128)S(1)}, u32[]{:S(2)}, u32[]{:S(2)}) %collective-permute-start.11) | collective-permute-done | bytes 131104 | tf_op jit(solution)/shard_map/ppermute | solution.py:545
  37.3 1.3 %shard_map.118 = (f32[3,9,144,128]{3,2,1,0:T(8,128)S(1)}, f32[3,9,144,128]{3,2,1,0:T(8,128)S(1)}, f32[3,9,144,128]{3,2,1,0:T(8,128)S(1)}, f32[8,144,128]{2,1,0:T(8,128)S(1)}) custom-call(f32[3,9,144,128]{3,2,1,0:T(8,128)S(1)} %get-tuple-element.130.refs_0_, ...), custom_call_target="tpu_custom_call", output_to_operand_aliasing={{0}: (0, {}), {1}: (1, {}), {2}: (2, {}), {3}: (3, {})} | custom-call | bytes 3600000 | tf_op jit(solution)/shard_map/pallas_call | solution.py:36
  38.6 1.2 %shard_map.121 = (f32[4,64,128]{2,1,0:T(8,128)S(1)}, f32[4,64,128]{2,1,0:T(8,128)S(1)}, f32[4,64,128]{2,1,0:T(8,128)S(1)}, f32[4,64,128]{2,1,0:T(8,128)S(1)}) custom-call(f32[8,144,128]{2,1,0:T(8,128)S(1)} %get-tuple-element.146.total.refs_4_, s32[16]{0:T(128)S(1)} %copy-done.2), custom_call_target="tpu_custom_call" | custom-call | bytes 3300000 | tf_op jit(solution)/shard_map/pallas_call | solution.py:36
  40.8 0.8 %collective-permute-done.13.refs_2_ = f32[4,64,128]{2,1,0:T(8,128)S(1)} collective-permute-done((f32[4,64,128]{2,1,0:T(8,128)S(1)}, f32[4,64,128]{2,1,0:T(8,128)S(1)}, u32[]{:S(2)}, u32[]{:S(2)}) %collective-permute-start.13) | collective-permute-done | bytes 131104 | tf_op jit(solution)/shard_map/ppermute | solution.py:545
  41.9 1.6 %collective-permute-start.15 = (f32[4,64,128]{2,1,0:T(8,128)S(1)}, f32[4,64,128]{2,1,0:T(8,128)S(1)}, u32[]{:S(2)}, u32[]{:S(2)}) collective-permute-start(f32[4,64,128]{2,1,0:T(8,128)S(1)} %get-tuple-element.157), channel_id=1, source_target_pairs={{0,4},{2,6},{4,0},{6,2},{8,12},{10,14},{12,8},{14,10},{16,20},{18,... | collective-permute-start | bytes 393224 | tf_op jit(solution)/shard_map/ppermute | solution.py:545
  43.4 4.2 %collective-permute-done.15.refs_1_ = f32[4,64,128]{2,1,0:T(8,128)S(1)} collective-permute-done((f32[4,64,128]{2,1,0:T(8,128)S(1)}, f32[4,64,128]{2,1,0:T(8,128)S(1)}, u32[]{:S(2)}, u32[]{:S(2)}) %collective-permute-start.15) | collective-permute-done | bytes 131104 | tf_op jit(solution)/shard_map/ppermute | solution.py:545
  47.8 2.1 %collective-permute-start.17 = (f32[64,128]{1,0:T(8,128)S(1)}, f32[64,128]{1,0:T(8,128)S(1)}, u32[]{:S(2)}, u32[]{:S(2)}) collective-permute-start(f32[64,128]{1,0:T(8,128)S(1)} %get-tuple-element.160), channel_id=1, source_target_pairs={{0,16},{2,18},{4,20},{6,22},{8,24},{10,26},{12,28},{14,30},{16,0},... | collective-permute-start | bytes 98312 | tf_op jit(solution)/shard_map/ppermute | solution.py:545
  49.9 2.3 %collective-permute-start.18 = (f32[64,128]{1,0:T(8,128)S(1)}, f32[64,128]{1,0:T(8,128)S(1)}, u32[]{:S(2)}, u32[]{:S(2)}) collective-permute-start(f32[64,128]{1,0:T(8,128)S(1)} %get-tuple-element.161), channel_id=1, source_target_pairs={{0,24},{2,26},{4,28},{6,30},{8,16},{10,18},{12,20},{14,22},{16,8},... | collective-permute-start | bytes 98312 | tf_op jit(solution)/shard_map/ppermute | solution.py:545
  52.2 1.7 %shard_map.120 = f32[1,6,8,128,128]{4,3,2,1,0:T(8,128)} custom-call(f32[3,9,144,128]{3,2,1,0:T(8,128)S(1)} %get-tuple-element.144.e, f32[3,9,144,128]{3,2,1,0:T(8,128)S(1)} %get-tuple-element.145.h), custom_call_target="tpu_custom_call" | custom-call | bytes 5100000 | tf_op jit(solution)/shard_map/pallas_call | solution.py:36
  53.9 1.7 %collective-permute-done.18.refs_3_ = f32[64,128]{1,0:T(8,128)S(1)} collective-permute-done((f32[64,128]{1,0:T(8,128)S(1)}, f32[64,128]{1,0:T(8,128)S(1)}, u32[]{:S(2)}, u32[]{:S(2)}) %collective-permute-start.18) | collective-permute-done | bytes 32800 | tf_op jit(solution)/shard_map/ppermute | solution.py:545
  55.6 0.6 %shard_map.125 = f32[64,128]{1,0:T(8,128)} custom-call(f32[64,128]{1,0:T(8,128)S(1)} %get-tuple-element.158.refs_0_, f32[64,128]{1,0:T(8,128)S(1)} %collective-permute-done.16.refs_1_, f32[64,128]{1,0:T(8,128)S(1)} %collective-permute-done.17.refs_2_, f32[64,128]{1,0:T(8,128)S(1)} %collective-permute-done.18.refs_3_), custom_call_target="tpu_custom_call" | custom-call | bytes 900000 | tf_op jit(solution)/shard_map/pallas_call | solution.py:36
  (51 shorter events, 6.6 us)
Async XLA Ops:
  0.6 11.8 %copy-start.2 = (s32[16]{0:T(128)S(1)}, s32[16]{0:T(128)}, u32[]{:S(2)}) copy-start(s32[16]{0:T(128)} %block_ids.3) | copy-start | bytes 196
  0.6 11.8 %copy-start.3 = (s32[1,3]{1,0:T(1,128)S(1)}, s32[1,3]{1,0:T(1,128)}, u32[]{:S(2)}) copy-start(s32[1,3]{1,0:T(1,128)} %source.1) | copy-start | bytes 40
  0.7 11.8 %copy-start.4 = (s32[16]{0:T(128)S(1)}, s32[16]{0:T(128)}, u32[]{:S(2)}) copy-start(s32[16]{0:T(128)} %material_idx.1) | copy-start | bytes 196
  0.7 11.7 %copy-start.5 = (f32[4]{0:T(128)S(1)}, f32[4]{0:T(128)}, u32[]{:S(2)}) copy-start(f32[4]{0:T(128)} %material_eps.1) | copy-start | bytes 52
  0.7 12.5 %copy-start = (f32[1,6,8,128,128]{4,3,2,1,0:T(8,128)S(1)}, f32[1,6,8,128,128]{4,3,2,1,0:T(8,128)}, u32[]{:S(2)}) copy-start(f32[1,6,8,128,128]{4,3,2,1,0:T(8,128)} %given.3) | copy-start | bytes 9437188
  0.7 8.6 %collective-permute-start.2 = (f32[64,128]{1,0:T(8,128)}, f32[64,128]{1,0:T(8,128)S(1)}, u32[]{:S(2)}, u32[]{:S(2)}) collective-permute-start(f32[64,128]{1,0:T(8,128)} %bitcast.3), channel_id=1, source_target_pairs={{0,24},{2,26},{4,28},{6,30},{8,16},{10,18},{12,20},{14,22},{16,8},... | collective-permute-start | bytes 98312 | tf_op jit(solution)/shard_map/ppermute | solution.py:545
  5.8 5.0 %collective-permute-start.1 = (f32[64,128]{1,0:T(8,128)}, f32[64,128]{1,0:T(8,128)S(1)}, u32[]{:S(2)}, u32[]{:S(2)}) collective-permute-start(f32[64,128]{1,0:T(8,128)} %bitcast.4), channel_id=1, source_target_pairs={{0,16},{2,18},{4,20},{6,22},{8,24},{10,26},{12,28},{14,30},{16,0},... | collective-permute-start | bytes 98312 | tf_op jit(solution)/shard_map/ppermute | solution.py:545
  5.8 5.0 %collective-permute-start = (f32[64,128]{1,0:T(8,128)}, f32[64,128]{1,0:T(8,128)S(1)}, u32[]{:S(2)}, u32[]{:S(2)}) collective-permute-start(f32[64,128]{1,0:T(8,128)} %bitcast.5), channel_id=1, source_target_pairs={{0,8},{2,10},{4,12},{6,14},{8,0},{10,2},{12,4},{14,6},{16,24},{18,... | collective-permute-start | bytes 98312 | tf_op jit(solution)/shard_map/ppermute | solution.py:545
  7.8 6.5 %copy-start.1 = (f32[1,6,8,128,128]{4,3,2,1,0:T(8,128)S(1)}, f32[1,6,8,128,128]{4,3,2,1,0:T(8,128)}, u32[]{:S(2)}) copy-start(f32[1,6,8,128,128]{4,3,2,1,0:T(8,128)} %given.2) | copy-start | bytes 9437188
  7.8 9.0 %collective-permute-start.3 = (f32[2,2,128,128]{3,2,1,0:T(8,128)S(1)}, f32[2,2,128,128]{3,2,1,0:T(8,128)S(1)}, u32[]{:S(2)}, u32[]{:S(2)}) collective-permute-start(f32[2,2,128,128]{3,2,1,0:T(8,128)S(1)} %get-tuple-element.86), channel_id=1, source_target_pairs={{0,1},{1,0},{2,3},{3,2},{4,5},{5,4},{6,7},{7,6},{8,9},{9,8},{10,11... | collective-permute-start | bytes 786440 | tf_op jit(solution)/shard_map/ppermute | solution.py:545
  10.8 5.0 %collective-permute-start.4 = (f32[4,64,128]{2,1,0:T(8,128)S(1)}, f32[4,64,128]{2,1,0:T(8,128)S(1)}, u32[]{:S(2)}, u32[]{:S(2)}) collective-permute-start(f32[4,64,128]{2,1,0:T(8,128)S(1)} %shard_map.96.near.refs_0_), channel_id=1, source_target_pairs={{0,4},{2,6},{4,0},{6,2},{8,12},{10,14},{12,8},{14,10},{16,20},{18,... | collective-permute-start | bytes 393224 | tf_op jit(solution)/shard_map/ppermute | solution.py:545
  13.1 4.1 %collective-permute-start.5 = (f32[4,64,128]{2,1,0:T(8,128)S(1)}, f32[4,64,128]{2,1,0:T(8,128)S(1)}, u32[]{:S(2)}, u32[]{:S(2)}) collective-permute-start(f32[4,64,128]{2,1,0:T(8,128)S(1)} %shard_map.96.near.refs_0_), channel_id=1, source_target_pairs={{0,2},{2,0},{4,6},{6,4},{8,10},{10,8},{12,14},{14,12},{16,18},{18,... | collective-permute-start | bytes 393224 | tf_op jit(solution)/shard_map/ppermute | solution.py:545
  15.9 1.3 %collective-permute-start.6 = (f32[4,64,128]{2,1,0:T(8,128)S(1)}, f32[4,64,128]{2,1,0:T(8,128)S(1)}, u32[]{:S(2)}, u32[]{:S(2)}) collective-permute-start(f32[4,64,128]{2,1,0:T(8,128)S(1)} %shard_map.101.refs_1_), channel_id=1, source_target_pairs={{0,2},{2,0},{4,6},{6,4},{8,10},{10,8},{12,14},{14,12},{16,18},{18,... | collective-permute-start | bytes 393224 | tf_op jit(solution)/shard_map/ppermute | solution.py:545
  17.8 5.7 %collective-permute-start.7 = (f32[2,128,128]{2,1,0:T(8,128)S(1)}, f32[2,128,128]{2,1,0:T(8,128)S(1)}, u32[]{:S(2)}, u32[]{:S(2)}) collective-permute-start(f32[2,128,128]{2,1,0:T(8,128)S(1)} %get-tuple-element.108), channel_id=1, source_target_pairs={{0,1},{1,0},{2,3},{3,2},{4,5},{5,4},{6,7},{7,6},{8,9},{9,8},{10,11... | collective-permute-start | bytes 393224 | tf_op jit(solution)/shard_map/ppermute | solution.py:545
  21.3 6.4 %collective-permute-start.8 = (f32[2,128,128]{2,1,0:T(8,128)S(1)}, f32[2,128,128]{2,1,0:T(8,128)S(1)}, u32[]{:S(2)}, u32[]{:S(2)}) collective-permute-start(f32[2,128,128]{2,1,0:T(8,128)S(1)} %get-tuple-element.115), channel_id=1, source_target_pairs={{0,1},{1,0},{2,3},{3,2},{4,5},{5,4},{6,7},{7,6},{8,9},{9,8},{10,11... | collective-permute-start | bytes 393224 | tf_op jit(solution)/shard_map/ppermute | solution.py:545
  23.7 6.5 %collective-permute-start.9 = (f32[2,128,128]{2,1,0:T(8,128)S(1)}, f32[2,128,128]{2,1,0:T(8,128)S(1)}, u32[]{:S(2)}, u32[]{:S(2)}) collective-permute-start(f32[2,128,128]{2,1,0:T(8,128)S(1)} %get-tuple-element.122), channel_id=1, source_target_pairs={{0,1},{1,0},{2,3},{3,2},{4,5},{5,4},{6,7},{7,6},{8,9},{9,8},{10,11... | collective-permute-start | bytes 393224 | tf_op jit(solution)/shard_map/ppermute | solution.py:545
  28.0 6.4 %collective-permute-start.10 = (f32[2,128,128]{2,1,0:T(8,128)S(1)}, f32[2,128,128]{2,1,0:T(8,128)S(1)}, u32[]{:S(2)}, u32[]{:S(2)}) collective-permute-start(f32[2,128,128]{2,1,0:T(8,128)S(1)} %get-tuple-element.129), channel_id=1, source_target_pairs={{0,1},{1,0},{2,3},{3,2},{4,5},{5,4},{6,7},{7,6},{8,9},{9,8},{10,11... | collective-permute-start | bytes 393224 | tf_op jit(solution)/shard_map/ppermute | solution.py:545
  30.5 6.6 %collective-permute-start.11 = (f32[2,128,128]{2,1,0:T(8,128)S(1)}, f32[2,128,128]{2,1,0:T(8,128)S(1)}, u32[]{:S(2)}, u32[]{:S(2)}) collective-permute-start(f32[2,128,128]{2,1,0:T(8,128)S(1)} %get-tuple-element.136), channel_id=1, source_target_pairs={{0,1},{1,0},{2,3},{3,2},{4,5},{5,4},{6,7},{7,6},{8,9},{9,8},{10,11... | collective-permute-start | bytes 393224 | tf_op jit(solution)/shard_map/ppermute | solution.py:545
  34.6 5.2 %collective-permute-start.12 = (f32[2,128,128]{2,1,0:T(8,128)S(1)}, f32[2,128,128]{2,1,0:T(8,128)S(1)}, u32[]{:S(2)}, u32[]{:S(2)}) collective-permute-start(f32[2,128,128]{2,1,0:T(8,128)S(1)} %get-tuple-element.143), channel_id=1, source_target_pairs={{0,1},{1,0},{2,3},{3,2},{4,5},{5,4},{6,7},{7,6},{8,9},{9,8},{10,11... | collective-permute-start | bytes 393224 | tf_op jit(solution)/shard_map/ppermute | solution.py:545
  40.2 1.4 %collective-permute-start.13 = (f32[4,64,128]{2,1,0:T(8,128)S(1)}, f32[4,64,128]{2,1,0:T(8,128)S(1)}, u32[]{:S(2)}, u32[]{:S(2)}) collective-permute-start(f32[4,64,128]{2,1,0:T(8,128)S(1)} %get-tuple-element.154), channel_id=1, source_target_pairs={{0,2},{2,0},{4,6},{6,4},{8,10},{10,8},{12,14},{14,12},{16,18},{18,... | collective-permute-start | bytes 393224 | tf_op jit(solution)/shard_map/ppermute | solution.py:545
  40.3 1.5 %collective-permute-start.14 = (f32[4,64,128]{2,1,0:T(8,128)S(1)}, f32[4,64,128]{2,1,0:T(8,128)S(1)}, u32[]{:S(2)}, u32[]{:S(2)}) collective-permute-start(f32[4,64,128]{2,1,0:T(8,128)S(1)} %get-tuple-element.155), channel_id=1, source_target_pairs={{0,2},{2,0},{4,6},{6,4},{8,10},{10,8},{12,14},{14,12},{16,18},{18,... | collective-permute-start | bytes 393224 | tf_op jit(solution)/shard_map/ppermute | solution.py:545
  41.9 5.8 %collective-permute-start.15 = (f32[4,64,128]{2,1,0:T(8,128)S(1)}, f32[4,64,128]{2,1,0:T(8,128)S(1)}, u32[]{:S(2)}, u32[]{:S(2)}) collective-permute-start(f32[4,64,128]{2,1,0:T(8,128)S(1)} %get-tuple-element.157), channel_id=1, source_target_pairs={{0,4},{2,6},{4,0},{6,2},{8,12},{10,14},{12,8},{14,10},{16,20},{18,... | collective-permute-start | bytes 393224 | tf_op jit(solution)/shard_map/ppermute | solution.py:545
  47.7 6.2 %collective-permute-start.16 = (f32[64,128]{1,0:T(8,128)S(1)}, f32[64,128]{1,0:T(8,128)S(1)}, u32[]{:S(2)}, u32[]{:S(2)}) collective-permute-start(f32[64,128]{1,0:T(8,128)S(1)} %get-tuple-element.159), channel_id=1, source_target_pairs={{0,8},{2,10},{4,12},{6,14},{8,0},{10,2},{12,4},{14,6},{16,24},{18,... | collective-permute-start | bytes 98312 | tf_op jit(solution)/shard_map/ppermute | solution.py:545
  47.8 6.1 %collective-permute-start.17 = (f32[64,128]{1,0:T(8,128)S(1)}, f32[64,128]{1,0:T(8,128)S(1)}, u32[]{:S(2)}, u32[]{:S(2)}) collective-permute-start(f32[64,128]{1,0:T(8,128)S(1)} %get-tuple-element.160), channel_id=1, source_target_pairs={{0,16},{2,18},{4,20},{6,22},{8,24},{10,26},{12,28},{14,30},{16,0},... | collective-permute-start | bytes 98312 | tf_op jit(solution)/shard_map/ppermute | solution.py:545
  49.9 5.7 %collective-permute-start.18 = (f32[64,128]{1,0:T(8,128)S(1)}, f32[64,128]{1,0:T(8,128)S(1)}, u32[]{:S(2)}, u32[]{:S(2)}) collective-permute-start(f32[64,128]{1,0:T(8,128)S(1)} %get-tuple-element.161), channel_id=1, source_target_pairs={{0,24},{2,26},{4,28},{6,30},{8,16},{10,18},{12,20},{14,22},{16,8},... | collective-permute-start | bytes 98312 | tf_op jit(solution)/shard_map/ppermute | solution.py:545

commit v7 on v6

--- a/solution.py
+++ b/solution.py
@@ -218,7 +218,8 @@
 
 
 def prepare_kernel(
-    layout, source, block_ids, material_idx, material_eps, total, edges, forced, base, place
+    layout, source, wave_idx, block_ids, material_idx, material_eps,
+    total, edges, forced, drives, base, place,
 ):
     depth, rows, width_y = forced.shape
     nblock = block_ids.shape[0]
@@ -231,6 +232,9 @@
     offset_x = (xcoord - source[0, 1]).astype(F32) / (rows / 4.0)
     offset_y = (ycoord - source[0, 2]).astype(F32) / (width_y / 4.0)
     profile = jnp.exp(-0.5 * (offset_x * offset_x + offset_y * offset_y))
+    step = lax.broadcasted_iota(jnp.int32, drives.shape, 0).astype(F32) + 1.0
+    wave = jnp.full(drives.shape, wave_idx[0], jnp.int32).astype(F32)
+    drives[...] = AMPLITUDE * jnp.sin(2.0 * math.pi / (6.0 + 2.0 * wave) * step)
     level = source[0, 0] - lax.axis_index("slab") * depth
     for layer in range(depth):
         total[layer] = empty
@@ -365,7 +369,10 @@
         win.put_e(layer, jnp.where(layer == 0, win.under, layer - 1), None, other, total)
         return carry
 
-    lax.fori_loop(lowest, highest, body, 0)
+    if lax.axis_size("slab") == 2:
+        lax.fori_loop(0, win.depth - 2, lambda i, carry: body(lowest + i, carry), 0, unroll=2)
+    else:
+        lax.fori_loop(lowest, highest, body, 0)
     win.put_e(highest, highest - 1, None, other, total)
 
 
@@ -382,45 +389,50 @@
     placed[pl.ds(PAD + rows, PAD), :] = margin
 
 
-def coef_edge_kernel(count, *refs):
-    parts, (place, base, coef, placed) = refs[:count], refs[count:]
-    depth, rows, width_y = coef.shape
-    nblock = place.shape[0]
-    block_rows = rows // nblock
-    for which, layer in enumerate((0, depth - 1)):
-        there = placed.at[which]
-        clear_margins(there)
-        source = pl.ds(layer * block_rows, block_rows)
-        pieces = [part[slot, source, :] for part in parts for slot in range(part.shape[0])]
-        for block in range(nblock):
-            value = None
-            for slot, piece in enumerate(pieces):
-                term = place[slot, pl.ds(block, 1), :] * piece
-                value = term if value is None else value + term
-            there[pl.ds(PAD + block * block_rows, block_rows), :] = value
-    for which, layer in enumerate((0, depth - 1)):
-        coef_layer(layer, coef, placed.at[which], base)
-
-
-def coef_inner_kernel(layout, coef_in, *refs):
-    parts, (block_ids, base, coef, blocks, placed) = refs[: len(layout)], refs[len(layout) :]
-    depth, rows, width_y = coef.shape
-    nblock = blocks.shape[0]
-    block_rows = rows // nblock
+def scatter_kernel(layout, *refs):
+    parts, (block_ids, blocks) = refs[: len(layout)], refs[len(layout) :]
     me = lax.axis_index("grp")
-    clear_margins(placed)
+    nothing = jnp.zeros(blocks.shape[1:], F32)
+    for block in range(blocks.shape[0]):
+        blocks[block] = nothing
     for part, masks in zip(parts, layout):
         for slot, mask in enumerate(masks):
             blocks[block_ids[me ^ mask]] = part[slot]
 
+
+def place_layer(layer, first_slot, parts, place, blocks, placed):
+    nblock = blocks.shape[0]
+    block_rows = (placed.shape[0] - 2 * PAD) // nblock
+    clear_margins(placed)
+    start = layer * block_rows
+    source = pl.ds(start if isinstance(layer, int) else pl.multiple_of(start, block_rows), block_rows)
+    pieces = [part[slot, source, :] for part in parts for slot in range(part.shape[0])]
+    for block in range(nblock):
+        value = blocks[block, source, :]
+        for slot, piece in enumerate(pieces):
+            value = value + place[first_slot + slot, pl.ds(block, 1), :] * piece
+        placed[pl.ds(PAD + block * block_rows, block_rows), :] = value
+
+
+def coef_edge_kernel(first_slot, count, *refs):
+    parts, (place, base, blocks, coef, placed) = refs[:count], refs[count:]
+    edge_layers = (0, coef.shape[0] - 1)
+    for which, layer in enumerate(edge_layers):
+        place_layer(layer, first_slot, parts, place, blocks, placed.at[which])
+    for which, layer in enumerate(edge_layers):
+        coef_layer(layer, coef, placed.at[which], base)
+
+
+def coef_inner_kernel(first_slot, count, coef_in, *refs):
+    parts, (place, base, blocks, coef, placed) = refs[:count], refs[count:]
+
     def body(layer, carry):
-        for block in range(nblock):
-            source = pl.ds(pl.multiple_of(layer * block_rows, block_rows), block_rows)
-            placed[pl.ds(PAD + block * block_rows, block_rows), :] = blocks[block, source, :]
-        coef_layer(layer, coef, placed, base)
+        there = placed.at[lax.rem(layer, 2)]
+        place_layer(layer, first_slot, parts, place, blocks, there)
+        coef_layer(layer, coef, there, base)
         return carry
 
-    lax.fori_loop(1, depth - 1, body, 0)
+    lax.fori_loop(1, coef.shape[0] - 1, body, 0, unroll=2)
 
 
 def filtered(padded, first, size):
@@ -448,23 +460,27 @@
         out[slot] = ref[...]
 
 
-def filter_inner_kernel(layout, total, block_ids, *rest):
-    parts, (blocks, wide) = rest[:-2], rest[-2:]
+def filter_inner_kernel(layout, total, block_ids_far, *rest):
+    parts, (blocks, wide, block_ids, sem) = rest[:-4], rest[-4:]
+    fetch = pltpu.make_async_copy(block_ids_far, block_ids, sem)
+    fetch.start()
     depth = total.shape[0]
     nblock = blocks.shape[0]
-    rows = wide.shape[0]
+    rows = wide.shape[1]
     block_rows = rows // nblock
     me = lax.axis_index("grp")
 
     def body(layer, carry):
+        there = wide.at[lax.rem(layer, 2)]
         for first, size in chunks(rows):
-            wide[pl.ds(first, size), :] = filtered(total.at[layer], first, size)
+            there[pl.ds(first, size), :] = filtered(total.at[layer], first, size)
         for block in range(nblock):
             target = pl.ds(pl.multiple_of(layer * block_rows, block_rows), block_rows)
-            blocks[block, target, :] = wide[pl.ds(block * block_rows, block_rows), :]
+            blocks[block, target, :] = there[pl.ds(block * block_rows, block_rows), :]
         return carry
 
-    lax.fori_loop(1, depth - 1, body, 0)
+    lax.fori_loop(1, depth - 1, body, 0, unroll=2)
+    fetch.wait()
     inner = pl.ds(block_rows, (depth - 2) * block_rows)
     for part, masks in zip(parts, layout):
         for slot, mask in enumerate(masks):
@@ -565,9 +581,6 @@
     block_rows = width_x // nblock
     ngrp = lax.axis_size("grp")
     npay = 1 if lax.axis_size("slab") == 2 else 2
-    omega = 2.0 * math.pi / (6.0 + 2.0 * wave_idx[0].astype(F32))
-    steps = lax.broadcasted_iota(jnp.int32, (STEPS, width_y), 0).astype(F32)
-    drives = AMPLITUDE * jnp.sin(omega * (steps + 1.0))
 
     far = 4
     middle = ngrp // (2 * far)
@@ -586,7 +599,6 @@
     edges_shape = on_chip(2, width_x + 2 * PAD, width_y)
     coef_shape = on_chip(depth, width_x, width_y)
     plane = on_chip(width_x, width_y)
-    padded = pltpu.VMEM((width_x + 2 * PAD, width_y), F32)
 
     design = density.reshape(piece)
     got = [swap_over(design, "grp", mask) for mask in far_masks[1:]]
@@ -605,12 +617,19 @@
     near_across = swap_over(near, "grp", 1)
 
     place_shape = on_chip(nblock, nblock, width_y)
-    total, edges, forced, base, place = call(
+    total, edges, forced, drives, base, place = call(
         functools.partial(prepare_kernel, layout),
-        [total_shape, edges_shape, on_chip(depth, width_x, width_y), plane, place_shape],
-        [IN_VMEM] * 5,
-        [source_pos, block_ids, material_idx, material_eps],
-        [IN_SMEM] * 4,
+        [
+            total_shape,
+            edges_shape,
+            on_chip(depth, width_x, width_y),
+            on_chip(STEPS, width_y),
+            plane,
+            place_shape,
+        ],
+        [IN_VMEM] * 6,
+        [source_pos, wave_idx, block_ids, material_idx, material_eps],
+        [IN_SMEM] * 5,
     )
     fields = []
     for evo, given in enumerate((fwd_fields, adj_fields)):
@@ -624,7 +643,17 @@
         )
         fields.append((e, h, curls))
     others = [tie(part, [forced] + [e for e, _, _ in fields]) for part in others]
-    parts = [near] + others + [near_across] + [swap_over(part, "grp", 1) for part in others]
+    early = [near] + others + [near_across]
+    last = [swap_over(part, "grp", 1) for part in others]
+    blocks = call(
+        functools.partial(scatter_kernel, layout[: len(early)]),
+        on_chip(nblock, *piece),
+        IN_VMEM,
+        early + [block_ids],
+        [IN_VMEM] * len(early) + [IN_SMEM],
+        micros=0.7,
+    )
+    first_slot = far * len(early)
 
     taken = []
     for evo, (e, h, curls) in enumerate(fields):
@@ -638,13 +667,14 @@
         )
         taken.append((e, h, curls))
     (e_fwd, h_fwd, curls_fwd), (e_adj, h_adj, curls_adj) = taken
+    placed = pltpu.VMEM((2, width_x + 2 * PAD, width_y), F32)
     coef = call(
-        functools.partial(coef_edge_kernel, len(parts)),
+        functools.partial(coef_edge_kernel, first_slot, len(last)),
         coef_shape,
         IN_VMEM,
-        parts + [place, base],
-        [IN_VMEM] * (len(parts) + 2),
-        [pltpu.VMEM((2, width_x + 2 * PAD, width_y), F32)],
+        last + [place, base, blocks],
+        [IN_VMEM] * (len(last) + 3),
+        [placed],
     )
 
     arrived_fwd, arrived_adj = [curls_fwd], [curls_adj]
@@ -662,12 +692,12 @@
             arrived_fwd = trade(pays)
         if step == 0:
             coef = call(
-                functools.partial(coef_inner_kernel, layout),
+                functools.partial(coef_inner_kernel, first_slot, len(last)),
                 coef_shape,
                 IN_VMEM,
-                [coef] + parts + [block_ids, base],
-                [IN_VMEM] * (1 + len(parts)) + [IN_SMEM, IN_VMEM],
-                [pltpu.VMEM((nblock,) + piece, F32), padded],
+                [coef] + last + [place, base, blocks],
+                [IN_VMEM] * (len(last) + 4),
+                [placed],
                 aliases={0: 0},
                 micros=0.9,
             )
@@ -696,9 +726,14 @@
                 [on_chip(*group)] * len(layout),
                 [IN_VMEM] * len(layout),
                 [total, block_ids],
-                [IN_VMEM, IN_SMEM],
-                [pltpu.VMEM((nblock,) + piece, F32), pltpu.VMEM((width_x, width_y), F32)],
-                micros=1.1,
+                [IN_VMEM, IN_HBM],
+                [
+                    pltpu.VMEM((nblock,) + piece, F32),
+                    pltpu.VMEM((2, width_x, width_y), F32),
+                    pltpu.SMEM(block_ids.shape, jnp.int32),
+                    pltpu.SemaphoreType.DMA,
+                ],
+                micros=0.8,
             )
         e_adj, h_adj, e_fwd, edges, *pays = call(
             functools.partial(edge_kernel, step, 1),

time: 56.4 us -> 56.2 us (level)
  starting transfers between devices: 21.5 us -> 24 us
  Pallas kernels: 19.7 us -> 17.7 us
  waiting for transfers between devices: 13.2 us -> 12.6 us
    ppermute x19, starting transfers between devices: 21.5 us -> 24 us  [swap_over(): lax.ppermute(array, axis, [(i, i ^ mask) for i in range(lax.axis_size(axi...]
    pallas_call x31 -> x32, Pallas kernels: 19.7 us -> 17.7 us  [call(): pl.pallas_call(kernel, out_shape=outs, in_specs=specs, out_specs=out_spec...]
    ppermute x19, waiting for transfers between devices: 13.2 us -> 12.6 us  [swap_over(): lax.ppermute(array, axis, [(i, i ^ mask) for i in range(lax.axis_size(axi...]
  transfers between devices with their start and end apart: 19 -> 19, of which waited for: 11 -> 10; matrix products, arithmetic and copies ran while one was open for 0% -> 0% of each run, Pallas kernels for 32% -> 29%
where the time goes in v7:
time: 56.2 us; the launch traced here: 56 us
  starting transfers between devices  24 us (43%)
  Pallas kernels  17.7 us (31%)
  waiting for transfers between devices  12.6 us (22%)
  between operations  1.67 us (3%)
    ppermute x19, starting transfers between devices, swap_over(): lax.ppermute(array, axis, [(i, i ^ mask) for i in range(lax.axis_size(axi...  24 us
    pallas_call x32, Pallas kernels, call(): pl.pallas_call(kernel, out_shape=outs, in_specs=specs, out_specs=out_spec...  17.7 us
    ppermute x19, waiting for transfers between devices, swap_over(): lax.ppermute(array, axis, [(i, i ^ mask) for i in range(lax.axis_size(axi...  12.6 us
  transfers between devices with their start and end apart: 19, of which 10 were waited for; matrix products, arithmetic and copies ran while one was open for 0% of the time, Pallas kernels for 29%

profile of v7, /device:TPU:0, one launch (start us, length us, event | category | flops | bytes accessed | tf_op | source)
XLA Modules:
  0.0 56.0 jit_solution(1338818513594690729)
XLA Ops:
  0.7 5.1 %collective-permute-start.2 = (f32[64,128]{1,0:T(8,128)}, f32[64,128]{1,0:T(8,128)S(1)}, u32[]{:S(2)}, u32[]{:S(2)}) collective-permute-start(f32[64,128]{1,0:T(8,128)} %bitcast.2), channel_id=1, source_target_pairs={{0,24},{2,26},{4,28},{6,30},{8,16},{10,18},{12,20},{14,22},{16,8},... | collective-permute-start | bytes 98312 | tf_op jit(solution)/shard_map/ppermute | solution.py:561
  5.8 0.6 %collective-permute-start = (f32[64,128]{1,0:T(8,128)}, f32[64,128]{1,0:T(8,128)S(1)}, u32[]{:S(2)}, u32[]{:S(2)}) collective-permute-start(f32[64,128]{1,0:T(8,128)} %bitcast.4), channel_id=1, source_target_pairs={{0,8},{2,10},{4,12},{6,14},{8,0},{10,2},{12,4},{14,6},{16,24},{18,... | collective-permute-start | bytes 98312 | tf_op jit(solution)/shard_map/ppermute | solution.py:561
  6.4 1.4 %shard_map.95 = (f32[64,128]{1,0:T(8,128)S(1)}, f32[2,2,128,128]{3,2,1,0:T(8,128)S(1)}) custom-call(f32[1,6,8,128,128]{4,3,2,1,0:T(8,128)} %given.2, f32[1,6,8,128,128]{4,3,2,1,0:T(8,128)} %given.3, f32[64,128]{1,0:T(8,128)} %bitcast.5), custom_call_target="tpu_custom_call" | custom-call | bytes 900000 | tf_op jit(solution)/shard_map/pallas_call | solution.py:36
  7.8 1.4 %collective-permute-start.3 = (f32[2,2,128,128]{3,2,1,0:T(8,128)S(1)}, f32[2,2,128,128]{3,2,1,0:T(8,128)S(1)}, u32[]{:S(2)}, u32[]{:S(2)}) collective-permute-start(f32[2,2,128,128]{3,2,1,0:T(8,128)S(1)} %get-tuple-element.87), channel_id=1, source_target_pairs={{0,1},{1,0},{2,3},{3,2},{4,5},{5,4},{6,7},{7,6},{8,9},{9,8},{10,11... | collective-permute-start | bytes 786440 | tf_op jit(solution)/shard_map/ppermute | solution.py:561
  9.3 1.5 %collective-permute-done.1.refs_2_ = f32[64,128]{1,0:T(8,128)S(1)} collective-permute-done((f32[64,128]{1,0:T(8,128)}, f32[64,128]{1,0:T(8,128)S(1)}, u32[]{:S(2)}, u32[]{:S(2)}) %collective-permute-start.1) | collective-permute-done | bytes 32800 | tf_op jit(solution)/shard_map/ppermute | solution.py:561
  10.8 1.6 %collective-permute-start.4 = (f32[4,64,128]{2,1,0:T(8,128)S(1)}, f32[4,64,128]{2,1,0:T(8,128)S(1)}, u32[]{:S(2)}, u32[]{:S(2)}) collective-permute-start(f32[4,64,128]{2,1,0:T(8,128)S(1)} %shard_map.96.near.refs_0_), channel_id=1, source_target_pairs={{0,4},{2,6},{4,0},{6,2},{8,12},{10,14},{12,8},{14,10},{16,20},{18,... | collective-permute-start | bytes 393224 | tf_op jit(solution)/shard_map/ppermute | solution.py:561
  13.2 0.7 %shard_map.99 = (f32[8,144,128]{2,1,0:T(8,128)S(1)}, f32[2,144,128]{2,1,0:T(8,128)S(1)}, f32[8,128,128]{2,1,0:T(8,128)S(1)}, f32[4,128]{1,0:T(4,128)S(1)}, f32[1...) custom-call(s32[1,3]{1,0:T(1,128)S(1)} %copy-done.3, s32[1]{0:T(128)S(6)} %copy.120.wave_idx, s32[16]{0:T(128)S(1)} %copy-done.2, ...), custom_call_target="tpu_custom_call" | custom-call | bytes 900000 | tf_op jit(solution)/shard_map/pallas_call | solution.py:36
  13.9 1.2 %shard_map.100 = (f32[3,9,144,128]{3,2,1,0:T(8,128)S(1)}, f32[3,9,144,128]{3,2,1,0:T(8,128)S(1)}, f32[3,8,128,128]{3,2,1,0:T(8,128)S(1)}) custom-call(f32[1,6,8,128,128]{4,3,2,1,0:T(8,128)S(1)} %copy-done, f32[4,64,128]{2,1,0:T(8,128)S(1)} %shard_map.96.near.refs_0_), custom_call_target="tpu_custom_call" | custom-call | bytes 4500000 | tf_op jit(solution)/shard_map/pallas_call | solution.py:36
  15.0 1.2 %shard_map.97 = (f32[3,9,144,128]{3,2,1,0:T(8,128)S(1)}, f32[3,9,144,128]{3,2,1,0:T(8,128)S(1)}, f32[3,8,128,128]{3,2,1,0:T(8,128)S(1)}) custom-call(f32[1,6,8,128,128]{4,3,2,1,0:T(8,128)S(1)} %copy-done.1, f32[4,64,128]{2,1,0:T(8,128)S(1)} %shard_map.96.near.refs_0_), custom_call_target="tpu_custom_call" | custom-call | bytes 4500000 | tf_op jit(solution)/shard_map/pallas_call | solution.py:36
  18.1 1.5 %collective-permute-start.7 = (f32[2,128,128]{2,1,0:T(8,128)S(1)}, f32[2,128,128]{2,1,0:T(8,128)S(1)}, u32[]{:S(2)}, u32[]{:S(2)}) collective-permute-start(f32[2,128,128]{2,1,0:T(8,128)S(1)} %get-tuple-element.110), channel_id=1, source_target_pairs={{0,1},{1,0},{2,3},{3,2},{4,5},{5,4},{6,7},{7,6},{8,9},{9,8},{10,11... | collective-permute-start | bytes 393224 | tf_op jit(solution)/shard_map/ppermute | solution.py:561
  19.6 0.6 %shard_map.105.coef.refs_4_.refs_2_ = f32[8,128,128]{2,1,0:T(8,128)S(1)} custom-call(f32[8,128,128]{2,1,0:T(8,128)S(1)} %shard_map.103.refs_2_.coef_in, f32[4,64,128]{2,1,0:T(8,128)S(1)} %collective-permute-done.5.refs_0_, f32[16,16,128]{2,1,0:T(8,128)S(1)} %get-tuple-element.91.refs_1_.refs_6_, ...), custom_call_target="tpu_custom_call", output_to_operand_aliasing={{}: (0, {})} | custom-call | bytes 2700000 | tf_op jit(solution)/shard_map/pallas_call | solution.py:36
  21.5 0.9 %shard_map.109 = (f32[3,9,144,128]{3,2,1,0:T(8,128)S(1)}, f32[3,9,144,128]{3,2,1,0:T(8,128)S(1)}) custom-call(f32[3,9,144,128]{3,2,1,0:T(8,128)S(1)} %get-tuple-element.106.refs_0_, f32[3,9,144,128]{3,2,1,0:T(8,128)S(1)} %get-tuple-element.107.refs_1_, ...), custom_call_target="tpu_custom_call", output_to_operand_aliasing={{0}: (0, {}), {1}: (1, {})} | custom-call | bytes 3300000 | tf_op jit(solution)/shard_map/pallas_call | solution.py:36
  22.4 1.7 %collective-permute-done.7.refs_5_.refs_6_ = f32[2,128,128]{2,1,0:T(8,128)S(1)} collective-permute-done((f32[2,128,128]{2,1,0:T(8,128)S(1)}, f32[2,128,128]{2,1,0:T(8,128)S(1)}, u32[]{:S(2)}, u32[]{:S(2)}) %collective-permute-start.7) | collective-permute-done | bytes 131104 | tf_op jit(solution)/shard_map/ppermute | solution.py:561
  24.4 1.7 %collective-permute-start.9 = (f32[2,128,128]{2,1,0:T(8,128)S(1)}, f32[2,128,128]{2,1,0:T(8,128)S(1)}, u32[]{:S(2)}, u32[]{:S(2)}) collective-permute-start(f32[2,128,128]{2,1,0:T(8,128)S(1)} %get-tuple-element.124), channel_id=1, source_target_pairs={{0,1},{1,0},{2,3},{3,2},{4,5},{5,4},{6,7},{7,6},{8,9},{9,8},{10,11... | collective-permute-start | bytes 393224 | tf_op jit(solution)/shard_map/ppermute | solution.py:561
  26.1 1.2 %shard_map.111 = (f32[3,9,144,128]{3,2,1,0:T(8,128)S(1)}, f32[3,9,144,128]{3,2,1,0:T(8,128)S(1)}, f32[3,9,144,128]{3,2,1,0:T(8,128)S(1)}, f32[8,144,128]{2,1,0:T(8,128)S(1)}) custom-call(f32[3,9,144,128]{3,2,1,0:T(8,128)S(1)} %get-tuple-element.104.refs_0_, ...), custom_call_target="tpu_custom_call", output_to_operand_aliasing={{0}: (0, {}), {1}: (1, {}), {2}: (2, {}), {3}: (3, {})} | custom-call | bytes 3600000 | tf_op jit(solution)/shard_map/pallas_call | solution.py:36
  27.5 1.2 %collective-permute-start.10 = (f32[2,128,128]{2,1,0:T(8,128)S(1)}, f32[2,128,128]{2,1,0:T(8,128)S(1)}, u32[]{:S(2)}, u32[]{:S(2)}) collective-permute-start(f32[2,128,128]{2,1,0:T(8,128)S(1)} %get-tuple-element.131), channel_id=1, source_target_pairs={{0,1},{1,0},{2,3},{3,2},{4,5},{5,4},{6,7},{7,6},{8,9},{9,8},{10,11... | collective-permute-start | bytes 393224 | tf_op jit(solution)/shard_map/ppermute | solution.py:561
  28.8 0.9 %shard_map.113 = (f32[3,9,144,128]{3,2,1,0:T(8,128)S(1)}, f32[3,9,144,128]{3,2,1,0:T(8,128)S(1)}) custom-call(f32[3,9,144,128]{3,2,1,0:T(8,128)S(1)} %get-tuple-element.120.refs_0_, f32[3,9,144,128]{3,2,1,0:T(8,128)S(1)} %get-tuple-element.121.refs_1_, ...), custom_call_target="tpu_custom_call", output_to_operand_aliasing={{0}: (0, {}), {1}: (1, {})} | custom-call | bytes 3300000 | tf_op jit(solution)/shard_map/pallas_call | solution.py:36
  30.1 1.7 %collective-permute-start.11 = (f32[2,128,128]{2,1,0:T(8,128)S(1)}, f32[2,128,128]{2,1,0:T(8,128)S(1)}, u32[]{:S(2)}, u32[]{:S(2)}) collective-permute-start(f32[2,128,128]{2,1,0:T(8,128)S(1)} %get-tuple-element.138), channel_id=1, source_target_pairs={{0,1},{1,0},{2,3},{3,2},{4,5},{5,4},{6,7},{7,6},{8,9},{9,8},{10,11... | collective-permute-start | bytes 393224 | tf_op jit(solution)/shard_map/ppermute | solution.py:561
  31.8 1.2 %shard_map.115 = (f32[3,9,144,128]{3,2,1,0:T(8,128)S(1)}, f32[3,9,144,128]{3,2,1,0:T(8,128)S(1)}, f32[3,9,144,128]{3,2,1,0:T(8,128)S(1)}, f32[8,144,128]{2,1,0:T(8,128)S(1)}) custom-call(f32[3,9,144,128]{3,2,1,0:T(8,128)S(1)} %get-tuple-element.118.refs_0_, ...), custom_call_target="tpu_custom_call", output_to_operand_aliasing={{0}: (0, {}), {1}: (1, {}), {2}: (2, {}), {3}: (3, {})} | custom-call | bytes 3600000 | tf_op jit(solution)/shard_map/pallas_call | solution.py:36
  33.0 0.6 %collective-permute-done.10.refs_5_.refs_6_ = f32[2,128,128]{2,1,0:T(8,128)S(1)} collective-permute-done((f32[2,128,128]{2,1,0:T(8,128)S(1)}, f32[2,128,128]{2,1,0:T(8,128)S(1)}, u32[]{:S(2)}, u32[]{:S(2)}) %collective-permute-start.10) | collective-permute-done | bytes 131104 | tf_op jit(solution)/shard_map/ppermute | solution.py:561
  33.9 1.5 %collective-permute-start.12 = (f32[2,128,128]{2,1,0:T(8,128)S(1)}, f32[2,128,128]{2,1,0:T(8,128)S(1)}, u32[]{:S(2)}, u32[]{:S(2)}) collective-permute-start(f32[2,128,128]{2,1,0:T(8,128)S(1)} %get-tuple-element.145), channel_id=1, source_target_pairs={{0,1},{1,0},{2,3},{3,2},{4,5},{5,4},{6,7},{7,6},{8,9},{9,8},{10,11... | collective-permute-start | bytes 393224 | tf_op jit(solution)/shard_map/ppermute | solution.py:561
  35.4 0.9 %shard_map.117 = (f32[3,9,144,128]{3,2,1,0:T(8,128)S(1)}, f32[3,9,144,128]{3,2,1,0:T(8,128)S(1)}) custom-call(f32[3,9,144,128]{3,2,1,0:T(8,128)S(1)} %get-tuple-element.134.refs_0_, f32[3,9,144,128]{3,2,1,0:T(8,128)S(1)} %get-tuple-element.135.refs_1_, ...), custom_call_target="tpu_custom_call", output_to_operand_aliasing={{0}: (0, {}), {1}: (1, {})} | custom-call | bytes 3300000 | tf_op jit(solution)/shard_map/pallas_call | solution.py:36
  36.7 1.2 %shard_map.119 = (f32[3,9,144,128]{3,2,1,0:T(8,128)S(1)}, f32[3,9,144,128]{3,2,1,0:T(8,128)S(1)}, f32[3,9,144,128]{3,2,1,0:T(8,128)S(1)}, f32[8,144,128]{2,1,0:T(8,128)S(1)}) custom-call(f32[3,9,144,128]{3,2,1,0:T(8,128)S(1)} %get-tuple-element.132.refs_0_, ...), custom_call_target="tpu_custom_call", output_to_operand_aliasing={{0}: (0, {}), {1}: (1, {}), {2}: (2, {}), {3}: (3, {})} | custom-call | bytes 3600000 | tf_op jit(solution)/shard_map/pallas_call | solution.py:36
  37.9 0.7 %shard_map.122 = (f32[4,64,128]{2,1,0:T(8,128)S(1)}, f32[4,64,128]{2,1,0:T(8,128)S(1)}, f32[4,64,128]{2,1,0:T(8,128)S(1)}, f32[4,64,128]{2,1,0:T(8,128)S(1)}) custom-call(f32[8,144,128]{2,1,0:T(8,128)S(1)} %get-tuple-element.148.total.refs_4_, s32[16]{0:T(128)} %block_ids_far.1), custom_call_target="tpu_custom_call" | custom-call | bytes 2400000 | tf_op jit(solution)/shard_map/pallas_call | solution.py:36
  39.9 0.8 %collective-permute-done.13.refs_2_ = f32[4,64,128]{2,1,0:T(8,128)S(1)} collective-permute-done((f32[4,64,128]{2,1,0:T(8,128)S(1)}, f32[4,64,128]{2,1,0:T(8,128)S(1)}, u32[]{:S(2)}, u32[]{:S(2)}) %collective-permute-start.13) | collective-permute-done | bytes 131104 | tf_op jit(solution)/shard_map/ppermute | solution.py:561
  41.0 1.3 %collective-permute-start.15 = (f32[4,64,128]{2,1,0:T(8,128)S(1)}, f32[4,64,128]{2,1,0:T(8,128)S(1)}, u32[]{:S(2)}, u32[]{:S(2)}) collective-permute-start(f32[4,64,128]{2,1,0:T(8,128)S(1)} %get-tuple-element.159), channel_id=1, source_target_pairs={{0,4},{2,6},{4,0},{6,2},{8,12},{10,14},{12,8},{14,10},{16,20},{18,... | collective-permute-start | bytes 393224 | tf_op jit(solution)/shard_map/ppermute | solution.py:561
  42.2 4.5 %collective-permute-done.15.refs_1_ = f32[4,64,128]{2,1,0:T(8,128)S(1)} collective-permute-done((f32[4,64,128]{2,1,0:T(8,128)S(1)}, f32[4,64,128]{2,1,0:T(8,128)S(1)}, u32[]{:S(2)}, u32[]{:S(2)}) %collective-permute-start.15) | collective-permute-done | bytes 131104 | tf_op jit(solution)/shard_map/ppermute | solution.py:561
  46.9 2.8 %collective-permute-start.17 = (f32[64,128]{1,0:T(8,128)S(1)}, f32[64,128]{1,0:T(8,128)S(1)}, u32[]{:S(2)}, u32[]{:S(2)}) collective-permute-start(f32[64,128]{1,0:T(8,128)S(1)} %get-tuple-element.162), channel_id=1, source_target_pairs={{0,16},{2,18},{4,20},{6,22},{8,24},{10,26},{12,28},{14,30},{16,0},... | collective-permute-start | bytes 98312 | tf_op jit(solution)/shard_map/ppermute | solution.py:561
  49.6 1.6 %collective-permute-start.18 = (f32[64,128]{1,0:T(8,128)S(1)}, f32[64,128]{1,0:T(8,128)S(1)}, u32[]{:S(2)}, u32[]{:S(2)}) collective-permute-start(f32[64,128]{1,0:T(8,128)S(1)} %get-tuple-element.163), channel_id=1, source_target_pairs={{0,24},{2,26},{4,28},{6,30},{8,16},{10,18},{12,20},{14,22},{16,8},... | collective-permute-start | bytes 98312 | tf_op jit(solution)/shard_map/ppermute | solution.py:561
  51.2 1.7 %shard_map.121 = f32[1,6,8,128,128]{4,3,2,1,0:T(8,128)} custom-call(f32[3,9,144,128]{3,2,1,0:T(8,128)S(1)} %get-tuple-element.146.e, f32[3,9,144,128]{3,2,1,0:T(8,128)S(1)} %get-tuple-element.147.h), custom_call_target="tpu_custom_call" | custom-call | bytes 5100000 | tf_op jit(solution)/shard_map/pallas_call | solution.py:36
  53.0 2.4 %collective-permute-done.18.refs_3_ = f32[64,128]{1,0:T(8,128)S(1)} collective-permute-done((f32[64,128]{1,0:T(8,128)S(1)}, f32[64,128]{1,0:T(8,128)S(1)}, u32[]{:S(2)}, u32[]{:S(2)}) %collective-permute-start.18) | collective-permute-done | bytes 32800 | tf_op jit(solution)/shard_map/ppermute | solution.py:561
  55.3 0.6 %shard_map.126 = f32[64,128]{1,0:T(8,128)} custom-call(f32[64,128]{1,0:T(8,128)S(1)} %get-tuple-element.160.refs_0_, f32[64,128]{1,0:T(8,128)S(1)} %collective-permute-done.16.refs_1_, f32[64,128]{1,0:T(8,128)S(1)} %collective-permute-done.17.refs_2_, f32[64,128]{1,0:T(8,128)S(1)} %collective-permute-done.18.refs_3_), custom_call_target="tpu_custom_call" | custom-call | bytes 900000 | tf_op jit(solution)/shard_map/pallas_call | solution.py:36
  (50 shorter events, 6.2 us)
Async XLA Ops:
  0.6 12.5 %copy-start.2 = (s32[16]{0:T(128)S(1)}, s32[16]{0:T(128)}, u32[]{:S(2)}) copy-start(s32[16]{0:T(128)} %block_ids_far.1) | copy-start | bytes 196
  0.6 12.5 %copy-start.3 = (s32[1,3]{1,0:T(1,128)S(1)}, s32[1,3]{1,0:T(1,128)}, u32[]{:S(2)}) copy-start(s32[1,3]{1,0:T(1,128)} %source.1) | copy-start | bytes 40
  0.7 12.5 %copy-start.4 = (s32[16]{0:T(128)S(1)}, s32[16]{0:T(128)}, u32[]{:S(2)}) copy-start(s32[16]{0:T(128)} %material_idx.1) | copy-start | bytes 196
  0.7 12.5 %copy-start.5 = (f32[4]{0:T(128)S(1)}, f32[4]{0:T(128)}, u32[]{:S(2)}) copy-start(f32[4]{0:T(128)} %material_eps.1) | copy-start | bytes 52
  0.7 13.2 %copy-start = (f32[1,6,8,128,128]{4,3,2,1,0:T(8,128)S(1)}, f32[1,6,8,128,128]{4,3,2,1,0:T(8,128)}, u32[]{:S(2)}) copy-start(f32[1,6,8,128,128]{4,3,2,1,0:T(8,128)} %given.3) | copy-start | bytes 9437188
  0.7 8.6 %collective-permute-start.2 = (f32[64,128]{1,0:T(8,128)}, f32[64,128]{1,0:T(8,128)S(1)}, u32[]{:S(2)}, u32[]{:S(2)}) collective-permute-start(f32[64,128]{1,0:T(8,128)} %bitcast.2), channel_id=1, source_target_pairs={{0,24},{2,26},{4,28},{6,30},{8,16},{10,18},{12,20},{14,22},{16,8},... | collective-permute-start | bytes 98312 | tf_op jit(solution)/shard_map/ppermute | solution.py:561
  5.8 5.0 %collective-permute-start.1 = (f32[64,128]{1,0:T(8,128)}, f32[64,128]{1,0:T(8,128)S(1)}, u32[]{:S(2)}, u32[]{:S(2)}) collective-permute-start(f32[64,128]{1,0:T(8,128)} %bitcast.3), channel_id=1, source_target_pairs={{0,16},{2,18},{4,20},{6,22},{8,24},{10,26},{12,28},{14,30},{16,0},... | collective-permute-start | bytes 98312 | tf_op jit(solution)/shard_map/ppermute | solution.py:561
  5.8 5.0 %collective-permute-start = (f32[64,128]{1,0:T(8,128)}, f32[64,128]{1,0:T(8,128)S(1)}, u32[]{:S(2)}, u32[]{:S(2)}) collective-permute-start(f32[64,128]{1,0:T(8,128)} %bitcast.4), channel_id=1, source_target_pairs={{0,8},{2,10},{4,12},{6,14},{8,0},{10,2},{12,4},{14,6},{16,24},{18,... | collective-permute-start | bytes 98312 | tf_op jit(solution)/shard_map/ppermute | solution.py:561
  7.8 7.2 %copy-start.1 = (f32[1,6,8,128,128]{4,3,2,1,0:T(8,128)S(1)}, f32[1,6,8,128,128]{4,3,2,1,0:T(8,128)}, u32[]{:S(2)}) copy-start(f32[1,6,8,128,128]{4,3,2,1,0:T(8,128)} %given.2) | copy-start | bytes 9437188
  7.8 9.5 %collective-permute-start.3 = (f32[2,2,128,128]{3,2,1,0:T(8,128)S(1)}, f32[2,2,128,128]{3,2,1,0:T(8,128)S(1)}, u32[]{:S(2)}, u32[]{:S(2)}) collective-permute-start(f32[2,2,128,128]{3,2,1,0:T(8,128)S(1)} %get-tuple-element.87), channel_id=1, source_target_pairs={{0,1},{1,0},{2,3},{3,2},{4,5},{5,4},{6,7},{7,6},{8,9},{9,8},{10,11... | collective-permute-start | bytes 786440 | tf_op jit(solution)/shard_map/ppermute | solution.py:561
  10.8 5.4 %collective-permute-start.4 = (f32[4,64,128]{2,1,0:T(8,128)S(1)}, f32[4,64,128]{2,1,0:T(8,128)S(1)}, u32[]{:S(2)}, u32[]{:S(2)}) collective-permute-start(f32[4,64,128]{2,1,0:T(8,128)S(1)} %shard_map.96.near.refs_0_), channel_id=1, source_target_pairs={{0,4},{2,6},{4,0},{6,2},{8,12},{10,14},{12,8},{14,10},{16,20},{18,... | collective-permute-start | bytes 393224 | tf_op jit(solution)/shard_map/ppermute | solution.py:561
  13.0 3.7 %collective-permute-start.6 = (f32[4,64,128]{2,1,0:T(8,128)S(1)}, f32[4,64,128]{2,1,0:T(8,128)S(1)}, u32[]{:S(2)}, u32[]{:S(2)}) collective-permute-start(f32[4,64,128]{2,1,0:T(8,128)S(1)} %shard_map.96.near.refs_0_), channel_id=1, source_target_pairs={{0,2},{2,0},{4,6},{6,4},{8,10},{10,8},{12,14},{14,12},{16,18},{18,... | collective-permute-start | bytes 393224 | tf_op jit(solution)/shard_map/ppermute | solution.py:561
  16.2 1.5 %collective-permute-start.5 = (f32[4,64,128]{2,1,0:T(8,128)S(1)}, f32[4,64,128]{2,1,0:T(8,128)S(1)}, u32[]{:S(2)}, u32[]{:S(2)}) collective-permute-start(f32[4,64,128]{2,1,0:T(8,128)S(1)} %shard_map.101.refs_1_), channel_id=1, source_target_pairs={{0,2},{2,0},{4,6},{6,4},{8,10},{10,8},{12,14},{14,12},{16,18},{18,... | collective-permute-start | bytes 393224 | tf_op jit(solution)/shard_map/ppermute | solution.py:561
  18.1 6.1 %collective-permute-start.7 = (f32[2,128,128]{2,1,0:T(8,128)S(1)}, f32[2,128,128]{2,1,0:T(8,128)S(1)}, u32[]{:S(2)}, u32[]{:S(2)}) collective-permute-start(f32[2,128,128]{2,1,0:T(8,128)S(1)} %get-tuple-element.110), channel_id=1, source_target_pairs={{0,1},{1,0},{2,3},{3,2},{4,5},{5,4},{6,7},{7,6},{8,9},{9,8},{10,11... | collective-permute-start | bytes 393224 | tf_op jit(solution)/shard_map/ppermute | solution.py:561
  20.9 6.4 %collective-permute-start.8 = (f32[2,128,128]{2,1,0:T(8,128)S(1)}, f32[2,128,128]{2,1,0:T(8,128)S(1)}, u32[]{:S(2)}, u32[]{:S(2)}) collective-permute-start(f32[2,128,128]{2,1,0:T(8,128)S(1)} %get-tuple-element.117), channel_id=1, source_target_pairs={{0,1},{1,0},{2,3},{3,2},{4,5},{5,4},{6,7},{7,6},{8,9},{9,8},{10,11... | collective-permute-start | bytes 393224 | tf_op jit(solution)/shard_map/ppermute | solution.py:561
  24.4 5.5 %collective-permute-start.9 = (f32[2,128,128]{2,1,0:T(8,128)S(1)}, f32[2,128,128]{2,1,0:T(8,128)S(1)}, u32[]{:S(2)}, u32[]{:S(2)}) collective-permute-start(f32[2,128,128]{2,1,0:T(8,128)S(1)} %get-tuple-element.124), channel_id=1, source_target_pairs={{0,1},{1,0},{2,3},{3,2},{4,5},{5,4},{6,7},{7,6},{8,9},{9,8},{10,11... | collective-permute-start | bytes 393224 | tf_op jit(solution)/shard_map/ppermute | solution.py:561
  27.5 6.1 %collective-permute-start.10 = (f32[2,128,128]{2,1,0:T(8,128)S(1)}, f32[2,128,128]{2,1,0:T(8,128)S(1)}, u32[]{:S(2)}, u32[]{:S(2)}) collective-permute-start(f32[2,128,128]{2,1,0:T(8,128)S(1)} %get-tuple-element.131), channel_id=1, source_target_pairs={{0,1},{1,0},{2,3},{3,2},{4,5},{5,4},{6,7},{7,6},{8,9},{9,8},{10,11... | collective-permute-start | bytes 393224 | tf_op jit(solution)/shard_map/ppermute | solution.py:561
  30.1 6.5 %collective-permute-start.11 = (f32[2,128,128]{2,1,0:T(8,128)S(1)}, f32[2,128,128]{2,1,0:T(8,128)S(1)}, u32[]{:S(2)}, u32[]{:S(2)}) collective-permute-start(f32[2,128,128]{2,1,0:T(8,128)S(1)} %get-tuple-element.138), channel_id=1, source_target_pairs={{0,1},{1,0},{2,3},{3,2},{4,5},{5,4},{6,7},{7,6},{8,9},{9,8},{10,11... | collective-permute-start | bytes 393224 | tf_op jit(solution)/shard_map/ppermute | solution.py:561
  33.9 5.0 %collective-permute-start.12 = (f32[2,128,128]{2,1,0:T(8,128)S(1)}, f32[2,128,128]{2,1,0:T(8,128)S(1)}, u32[]{:S(2)}, u32[]{:S(2)}) collective-permute-start(f32[2,128,128]{2,1,0:T(8,128)S(1)} %get-tuple-element.145), channel_id=1, source_target_pairs={{0,1},{1,0},{2,3},{3,2},{4,5},{5,4},{6,7},{7,6},{8,9},{9,8},{10,11... | collective-permute-start | bytes 393224 | tf_op jit(solution)/shard_map/ppermute | solution.py:561
  39.3 1.4 %collective-permute-start.13 = (f32[4,64,128]{2,1,0:T(8,128)S(1)}, f32[4,64,128]{2,1,0:T(8,128)S(1)}, u32[]{:S(2)}, u32[]{:S(2)}) collective-permute-start(f32[4,64,128]{2,1,0:T(8,128)S(1)} %get-tuple-element.156), channel_id=1, source_target_pairs={{0,2},{2,0},{4,6},{6,4},{8,10},{10,8},{12,14},{14,12},{16,18},{18,... | collective-permute-start | bytes 393224 | tf_op jit(solution)/shard_map/ppermute | solution.py:561
  39.4 1.5 %collective-permute-start.14 = (f32[4,64,128]{2,1,0:T(8,128)S(1)}, f32[4,64,128]{2,1,0:T(8,128)S(1)}, u32[]{:S(2)}, u32[]{:S(2)}) collective-permute-start(f32[4,64,128]{2,1,0:T(8,128)S(1)} %get-tuple-element.157), channel_id=1, source_target_pairs={{0,2},{2,0},{4,6},{6,4},{8,10},{10,8},{12,14},{14,12},{16,18},{18,... | collective-permute-start | bytes 393224 | tf_op jit(solution)/shard_map/ppermute | solution.py:561
  41.0 5.8 %collective-permute-start.15 = (f32[4,64,128]{2,1,0:T(8,128)S(1)}, f32[4,64,128]{2,1,0:T(8,128)S(1)}, u32[]{:S(2)}, u32[]{:S(2)}) collective-permute-start(f32[4,64,128]{2,1,0:T(8,128)S(1)} %get-tuple-element.159), channel_id=1, source_target_pairs={{0,4},{2,6},{4,0},{6,2},{8,12},{10,14},{12,8},{14,10},{16,20},{18,... | collective-permute-start | bytes 393224 | tf_op jit(solution)/shard_map/ppermute | solution.py:561
  46.8 6.2 %collective-permute-start.16 = (f32[64,128]{1,0:T(8,128)S(1)}, f32[64,128]{1,0:T(8,128)S(1)}, u32[]{:S(2)}, u32[]{:S(2)}) collective-permute-start(f32[64,128]{1,0:T(8,128)S(1)} %get-tuple-element.161), channel_id=1, source_target_pairs={{0,8},{2,10},{4,12},{6,14},{8,0},{10,2},{12,4},{14,6},{16,24},{18,... | collective-permute-start | bytes 98312 | tf_op jit(solution)/shard_map/ppermute | solution.py:561
  46.9 6.1 %collective-permute-start.17 = (f32[64,128]{1,0:T(8,128)S(1)}, f32[64,128]{1,0:T(8,128)S(1)}, u32[]{:S(2)}, u32[]{:S(2)}) collective-permute-start(f32[64,128]{1,0:T(8,128)S(1)} %get-tuple-element.162), channel_id=1, source_target_pairs={{0,16},{2,18},{4,20},{6,22},{8,24},{10,26},{12,28},{14,30},{16,0},... | collective-permute-start | bytes 98312 | tf_op jit(solution)/shard_map/ppermute | solution.py:561
  49.6 5.7 %collective-permute-start.18 = (f32[64,128]{1,0:T(8,128)S(1)}, f32[64,128]{1,0:T(8,128)S(1)}, u32[]{:S(2)}, u32[]{:S(2)}) collective-permute-start(f32[64,128]{1,0:T(8,128)S(1)} %get-tuple-element.163), channel_id=1, source_target_pairs={{0,24},{2,26},{4,28},{6,30},{8,16},{10,18},{12,20},{14,22},{16,8},... | collective-permute-start | bytes 98312 | tf_op jit(solution)/shard_map/ppermute | solution.py:561

commit v8 on v7

--- a/solution.py
+++ b/solution.py
@@ -217,9 +217,14 @@
     held_copy.wait()
 
 
+def owners(count):
+    core = lax.rem(lax.axis_index("grp"), 2)
+    return [2 * chip + side for side in (core, 1 - core) for chip in range(count // 2)]
+
+
 def prepare_kernel(
-    layout, source, wave_idx, block_ids, material_idx, material_eps,
-    total, edges, forced, drives, base, place,
+    masks, source, wave_idx, block_ids, material_idx, material_eps,
+    total, edges, forced, drives, base, place, owned,
 ):
     depth, rows, width_y = forced.shape
     nblock = block_ids.shape[0]
@@ -244,8 +249,10 @@
         base[pl.ds(block * block_rows, block_rows), :] = value
     me = lax.axis_index("grp")
     block = lax.broadcasted_iota(jnp.int32, (nblock, width_y), 0)
-    for slot, mask in enumerate(mask for masks in layout for mask in masks):
+    for slot, mask in enumerate(masks):
         place[slot] = jnp.where(block == block_ids[me ^ mask], 1.0, 0.0)
+    for slot, owner in enumerate(owners(nblock)):
+        owned[slot] = jnp.where(block == block_ids[owner], 1.0, 0.0)
 
 
 def first_kernel(given, near, e, h, curls):
@@ -293,40 +300,44 @@
     win.put_curl(curls, 0, win.under)
 
 
-def edge_kernel(step, evo, *refs):
+def edge_kernel(step, *refs):
     refs = list(refs)
-    e_in, h_in = refs.pop(0), refs.pop(0)
-    if evo == 1:
-        other_in, edges_in = refs.pop(0), refs.pop(0)
-    coef = refs.pop(0)
-    drives, forced = (refs.pop(0), refs.pop(0)) if evo == 0 else (None, None)
-    curls = refs.pop(0) if step == 0 else None
+    del refs[:5]
+    coef, drives, forced = (refs.pop(0) for _ in range(3))
+    first_curls = (refs.pop(0), refs.pop(0)) if step == 0 else (None, None)
     below, above = (refs.pop(0), refs.pop(0)) if step > 0 else (None, None)
-    e, h = refs.pop(0), refs.pop(0)
-    other, edges = (refs.pop(0), refs.pop(0)) if evo == 1 else (None, None)
-    pays = refs
-    win = Window(e, h, coef, forcing(step, drives, forced))
-    top = win.top
+    e_fwd, h_fwd, e_adj, h_adj, edges = refs[:5]
+    pays = refs[5:]
+    fwd = Window(e_fwd, h_fwd, coef, forcing(step, drives, forced))
+    adj = Window(e_adj, h_adj, coef)
+    top = fwd.top
+    every = pl.ds(PAD, fwd.rows)
     has_up, has_low = neighbours()
 
     @pl.when(has_up)
     def _():
         if step > 0:
-            win.take_above(above)
-        win.put_e(top, top - 1, curls, other, edges, 1)
+            for evo, win in enumerate((fwd, adj)):
+                win.take_above(above.at[evo])
+        fwd.put_e(top, top - 1, first_curls[0])
+        adj.put_e(top, top - 1, first_curls[1], e_fwd, edges, 1)
         if pays:
-            win.put_h(top, alone=True)
-            for c in range(2):
-                pays[0][c] = h[c, top, pl.ds(PAD, win.rows), :]
+            for evo, win in enumerate((fwd, adj)):
+                win.put_h(top, alone=True)
+                for c in range(2):
+                    pays[0][evo, c] = win.h[c, top, every, :]
 
     @pl.when(has_low)
     def _():
         if step > 0:
-            win.take_below(below)
-        win.put_e(0, win.under, curls, other, edges, 0)
+            for evo, win in enumerate((fwd, adj)):
+                win.take_below(below.at[evo])
+        fwd.put_e(0, fwd.under, first_curls[0])
+        adj.put_e(0, fwd.under, first_curls[1], e_fwd, edges, 0)
         if pays:
-            for c in range(2):
-                pays[-1][c] = e[c, 0, pl.ds(PAD, win.rows), :]
+            for evo, win in enumerate((fwd, adj)):
+                for c in range(2):
+                    pays[-1][evo, c] = win.e[c, 0, every, :]
 
 
 def inner_range(top):
@@ -350,30 +361,32 @@
     lax.fori_loop(lowest, highest + 1, body, 0)
 
 
-def inner_kernel(step, evo, *refs):
-    refs = list(refs)
-    e_in, h_in = refs.pop(0), refs.pop(0)
-    if evo == 1:
-        other_in, total_in = refs.pop(0), refs.pop(0)
-    coef = refs.pop(0)
-    drives, forced = (refs.pop(0), refs.pop(0)) if evo == 0 else (None, None)
-    e, h = refs.pop(0), refs.pop(0)
-    other, total = (refs.pop(0), refs.pop(0)) if evo == 1 else (None, None)
-    win = Window(e, h, coef, forcing(step, drives, forced))
-    lowest, highest = inner_range(win.top)
-    win.put_h(0)
-    pl.when(lowest == 1)(lambda: win.put_h(1))
+def inner_kernel(step, *refs):
+    coef, drives, forced, e_fwd, h_fwd, e_adj, h_adj, total = refs[5:]
+    fwd = Window(e_fwd, h_fwd, coef, forcing(step, drives, forced))
+    adj = Window(e_adj, h_adj, coef)
+    lowest, highest = inner_range(fwd.top)
+
+    def put_h(layer):
+        fwd.put_h(layer)
+        adj.put_h(layer)
+
+    def put_e(layer, lower):
+        fwd.put_e(layer, lower)
+        adj.put_e(layer, lower, None, e_fwd, total)
 
     def body(layer, carry):
-        win.put_h(layer + 1)
-        win.put_e(layer, jnp.where(layer == 0, win.under, layer - 1), None, other, total)
+        put_h(layer + 1)
+        put_e(layer, jnp.where(layer == 0, fwd.under, layer - 1))
         return carry
 
+    put_h(0)
+    pl.when(lowest == 1)(lambda: put_h(1))
     if lax.axis_size("slab") == 2:
-        lax.fori_loop(0, win.depth - 2, lambda i, carry: body(lowest + i, carry), 0, unroll=2)
+        lax.fori_loop(0, fwd.depth - 2, lambda i, carry: body(lowest + i, carry), 0, unroll=2)
     else:
         lax.fori_loop(lowest, highest, body, 0)
-    win.put_e(highest, highest - 1, None, other, total)
+    put_e(highest, highest - 1)
 
 
 def coef_layer(layer, coef, placed, base):
@@ -400,7 +413,7 @@
             blocks[block_ids[me ^ mask]] = part[slot]
 
 
-def place_layer(layer, first_slot, parts, place, blocks, placed):
+def place_layer(layer, parts, place, blocks, placed):
     nblock = blocks.shape[0]
     block_rows = (placed.shape[0] - 2 * PAD) // nblock
     clear_margins(placed)
@@ -410,25 +423,25 @@
     for block in range(nblock):
         value = blocks[block, source, :]
         for slot, piece in enumerate(pieces):
-            value = value + place[first_slot + slot, pl.ds(block, 1), :] * piece
+            value = value + place[slot, pl.ds(block, 1), :] * piece
         placed[pl.ds(PAD + block * block_rows, block_rows), :] = value
 
 
-def coef_edge_kernel(first_slot, count, *refs):
+def coef_edge_kernel(count, *refs):
     parts, (place, base, blocks, coef, placed) = refs[:count], refs[count:]
     edge_layers = (0, coef.shape[0] - 1)
     for which, layer in enumerate(edge_layers):
-        place_layer(layer, first_slot, parts, place, blocks, placed.at[which])
+        place_layer(layer, parts, place, blocks, placed.at[which])
     for which, layer in enumerate(edge_layers):
         coef_layer(layer, coef, placed.at[which], base)
 
 
-def coef_inner_kernel(first_slot, count, coef_in, *refs):
+def coef_inner_kernel(count, coef_in, *refs):
     parts, (place, base, blocks, coef, placed) = refs[:count], refs[count:]
 
     def body(layer, carry):
         there = placed.at[lax.rem(layer, 2)]
-        place_layer(layer, first_slot, parts, place, blocks, there)
+        place_layer(layer, parts, place, blocks, there)
         coef_layer(layer, coef, there, base)
         return carry
 
@@ -460,15 +473,13 @@
         out[slot] = ref[...]
 
 
-def filter_inner_kernel(layout, total, block_ids_far, *rest):
-    parts, (blocks, wide, block_ids, sem) = rest[:-4], rest[-4:]
+def filter_inner_kernel(total, block_ids_far, kept, sent, blocks, wide, block_ids, sem):
     fetch = pltpu.make_async_copy(block_ids_far, block_ids, sem)
     fetch.start()
     depth = total.shape[0]
     nblock = blocks.shape[0]
     rows = wide.shape[1]
     block_rows = rows // nblock
-    me = lax.axis_index("grp")
 
     def body(layer, carry):
         there = wide.at[lax.rem(layer, 2)]
@@ -482,16 +493,16 @@
     lax.fori_loop(1, depth - 1, body, 0, unroll=2)
     fetch.wait()
     inner = pl.ds(block_rows, (depth - 2) * block_rows)
-    for part, masks in zip(parts, layout):
-        for slot, mask in enumerate(masks):
-            part[slot, inner, :] = blocks[block_ids[me ^ mask], inner, :]
-
-
-def filter_edge_kernel(count, *refs):
-    total, edges, place = refs[count : count + 3]
-    parts, (sums, wide) = refs[count + 3 : -2], refs[-2:]
+    chips = nblock // 2
+    for slot, owner in enumerate(owners(nblock)):
+        part = kept if slot < chips else sent
+        part[slot % chips, inner, :] = blocks[block_ids[owner], inner, :]
+
+
+def filter_edge_kernel(kept_in, sent_in, total, edges, owned, kept, sent, sums, wide):
     depth = total.shape[0]
-    nblock = place.shape[0]
+    nblock = owned.shape[0]
+    chips = nblock // 2
     rows = wide.shape[1]
     block_rows = rows // nblock
     for which, layer in enumerate((0, depth - 1)):
@@ -506,53 +517,44 @@
         for slot in range(nblock):
             value = None
             for block, piece in enumerate(blocks):
-                term = place[slot, pl.ds(block, 1), :] * piece
+                term = owned[slot, pl.ds(block, 1), :] * piece
                 value = term if value is None else value + term
-            parts[slot // parts[0].shape[0]][slot % parts[0].shape[0], target, :] = value
-
-
-def add_kernel(*refs):
-    half = len(refs) // 3
-    for a, b, out in zip(refs[:half], refs[half : 2 * half], refs[2 * half :]):
-        out[...] = a[...] + b[...]
-
-
-def add_split_kernel(count, *refs):
-    terms, outs = refs[:count], refs[count:]
-    for slot, out in enumerate(outs):
-        value = terms[0][slot]
-        for term in terms[1:]:
-            value = value + term[slot]
-        out[...] = value
-
-
-def last_kernel(scale, *refs):
-    value = refs[0][...]
-    for ref in refs[1:-1]:
-        value = value + ref[...]
-    refs[-1][...] = value * scale
-
-
-def out_kernel(e, h, finals, halves, sems):
-    depth = e.shape[1] - 1
+            part = kept if slot < chips else sent
+            part[slot % chips, target, :] = value
+
+
+def add_kernel(kept, got, out):
+    out[...] = kept[...] + got[...]
+
+
+def last_kernel(scale, got, out):
+    value = got[0]
+    for slot in range(1, got.shape[0]):
+        value = value + got[slot]
+    out[...] = value * scale
+
+
+def out_kernel(lowest, stride, count, e, h, *refs):
+    finals, halves, sems = refs[-5], refs[-2], refs[-1]
     rows = e.shape[2] - 2 * PAD
     every = pl.ds(PAD, rows)
-    copies = [
-        pltpu.make_async_copy(e.at[c, pl.ds(0, depth), every, :], finals.at[0, c], sems.at[c])
-        for c in range(3)
-    ]
-    for copy in copies:
-        copy.start()
-    for c in range(3):
-
-        def body(layer, carry, c=c):
-            halves[c, layer] = 0.5 * h[c, layer, every, :]
-            return carry
-
-        lax.fori_loop(0, depth, body, 0)
-        copy = pltpu.make_async_copy(halves.at[c], finals.at[0, 3 + c], sems.at[3 + c])
-        copy.start()
-        copies.append(copy)
+    runs = [(lowest, count)] if stride == 1 else [(lowest + stride * i, 1) for i in range(count)]
+    copies = []
+    for run, (first, size) in enumerate(runs):
+        layers = pl.ds(first, size)
+        for c in range(3):
+            source = e.at[c, layers, every, :]
+            copies.append(pltpu.make_async_copy(source, finals.at[0, c, layers], sems.at[run, c]))
+            copies[-1].start()
+    for run, (first, size) in enumerate(runs):
+        for c in range(3):
+            for layer in range(first, first + size):
+                halves[c, layer] = 0.5 * h[c, layer, every, :]
+            layers = pl.ds(first, size)
+            source = halves.at[c, layers]
+            target = finals.at[0, 3 + c, layers]
+            copies.append(pltpu.make_async_copy(source, target, sems.at[run, 3 + c]))
+            copies[-1].start()
     for copy in copies:
         copy.wait()
 
@@ -591,20 +593,37 @@
     ]
     piece = (depth * block_rows, width_y)
     group = (far,) + piece
+    chips = nblock // 2
 
     field_shape = on_chip(3, depth + 1, width_x + 2 * PAD, width_y)
     curls_shape = on_chip(3, depth, width_x, width_y)
-    halo_shape = on_chip(2, width_x, width_y)
+    pay_shape = on_chip(2, 2, width_x, width_y)
     total_shape = on_chip(depth, width_x + 2 * PAD, width_y)
     edges_shape = on_chip(2, width_x + 2 * PAD, width_y)
     coef_shape = on_chip(depth, width_x, width_y)
     plane = on_chip(width_x, width_y)
 
+    def write_out(lowest, stride, count, fields, finals, micros):
+        finals, fields[0], fields[1] = call(
+            functools.partial(out_kernel, lowest, stride, count),
+            [jax.ShapeDtypeStruct(fwd_fields.shape, F32), field_shape, field_shape],
+            [IN_HBM, IN_VMEM, IN_VMEM],
+            fields[:2] + finals,
+            [IN_VMEM] * 2 + [IN_HBM] * len(finals),
+            [
+                pltpu.VMEM((3, depth, width_x, width_y), F32),
+                pltpu.SemaphoreType.DMA((2, 6)),
+            ],
+            aliases={0: 1, 1: 2, 2: 0} if finals else {0: 1, 1: 2},
+            micros=micros,
+        )
+        return finals
+
     design = density.reshape(piece)
     got = [swap_over(design, "grp", mask) for mask in far_masks[1:]]
     own, *pays = call(
         opening_kernel,
-        [on_chip(*piece)] + [on_chip(2, 2, width_x, width_y)] * npay,
+        [on_chip(*piece)] + [pay_shape] * npay,
         [IN_VMEM] * (1 + npay),
         [fwd_fields, adj_fields, design],
         [IN_HBM] * 3,
@@ -616,18 +635,18 @@
     others = [swap_over(near, "grp", mask) for mask in middle_masks[1:]]
     near_across = swap_over(near, "grp", 1)
 
-    place_shape = on_chip(nblock, nblock, width_y)
-    total, edges, forced, drives, base, place = call(
-        functools.partial(prepare_kernel, layout),
+    total, edges, forced, drives, base, place, owned = call(
+        functools.partial(prepare_kernel, [m for masks in layout[middle + 1 :] for m in masks]),
         [
             total_shape,
             edges_shape,
             on_chip(depth, width_x, width_y),
             on_chip(STEPS, width_y),
             plane,
-            place_shape,
+            on_chip(far * (middle - 1), nblock, width_y),
+            on_chip(nblock, nblock, width_y),
         ],
-        [IN_VMEM] * 6,
+        [IN_VMEM] * 7,
         [source_pos, wave_idx, block_ids, material_idx, material_eps],
         [IN_SMEM] * 5,
     )
@@ -653,7 +672,6 @@
         [IN_VMEM] * len(early) + [IN_SMEM],
         micros=0.7,
     )
-    first_slot = far * len(early)
 
     taken = []
     for evo, (e, h, curls) in enumerate(fields):
@@ -669,7 +687,7 @@
     (e_fwd, h_fwd, curls_fwd), (e_adj, h_adj, curls_adj) = taken
     placed = pltpu.VMEM((2, width_x + 2 * PAD, width_y), F32)
     coef = call(
-        functools.partial(coef_edge_kernel, first_slot, len(last)),
+        functools.partial(coef_edge_kernel, len(last)),
         coef_shape,
         IN_VMEM,
         last + [place, base, blocks],
@@ -677,54 +695,57 @@
         [placed],
     )
 
-    arrived_fwd, arrived_adj = [curls_fwd], [curls_adj]
+    fields = [e_fwd, h_fwd, e_adj, h_adj]
+    about = [drives, forced]
+    late = [curls_fwd, curls_adj]
     for step in range(STEPS):
         more = npay if step < STEPS - 1 else 0
-        e_fwd, h_fwd, *pays = call(
-            functools.partial(edge_kernel, step, 0),
-            [field_shape] * 2 + [halo_shape] * more,
-            [IN_VMEM] * (2 + more),
-            [e_fwd, h_fwd, coef, drives, forced] + arrived_fwd,
-            [IN_VMEM] * (5 + len(arrived_fwd)),
-            aliases={0: 0, 1: 1},
+        outcome = call(
+            functools.partial(edge_kernel, step),
+            [field_shape] * 4 + [edges_shape] + [pay_shape] * more,
+            [IN_VMEM] * (5 + more),
+            fields + [edges, coef] + about + late,
+            [IN_VMEM] * 10,
+            aliases={slot: slot for slot in range(5)},
         )
-        if more:
-            arrived_fwd = trade(pays)
+        fields, edges, pays = list(outcome[:4]), outcome[4], outcome[5:]
+        if not more:
+            break
+        late = trade(pays)
         if step == 0:
             coef = call(
-                functools.partial(coef_inner_kernel, first_slot, len(last)),
+                functools.partial(coef_inner_kernel, len(last)),
                 coef_shape,
                 IN_VMEM,
                 [coef] + last + [place, base, blocks],
                 [IN_VMEM] * (len(last) + 4),
                 [placed],
                 aliases={0: 0},
-                micros=0.9,
+                micros=0.6,
             )
-            e_fwd, e_adj, total = call(
+            fields[0], fields[2], total = call(
                 begin_kernel,
                 [field_shape, field_shape, total_shape],
                 [IN_VMEM] * 3,
-                [e_fwd, e_adj, total, coef, drives, forced, curls_fwd, curls_adj],
+                [fields[0], fields[2], total, coef] + about + [curls_fwd, curls_adj],
                 [IN_VMEM] * 8,
                 aliases={0: 0, 1: 1, 2: 2},
-                micros=0.7,
+                micros=0.5,
             )
-        else:
-            e_adj, h_adj, e_fwd, total = call(
-                functools.partial(inner_kernel, step, 1),
-                [field_shape] * 3 + [total_shape],
-                [IN_VMEM] * 4,
-                [e_adj, h_adj, e_fwd, total, coef],
-                [IN_VMEM] * 5,
-                aliases={0: 0, 1: 1, 2: 2, 3: 3},
-                micros=1.2,
-            )
-        if not more:
-            parts = call(
-                functools.partial(filter_inner_kernel, layout),
-                [on_chip(*group)] * len(layout),
-                [IN_VMEM] * len(layout),
+        *fields, total = call(
+            functools.partial(inner_kernel, step + 1),
+            [field_shape] * 4 + [total_shape],
+            [IN_VMEM] * 5,
+            fields + [total, coef] + about,
+            [IN_VMEM] * 8,
+            aliases={slot: slot for slot in range(5)},
+            micros=2.3,
+        )
+        if step == STEPS - 2:
+            kept, sent = call(
+                filter_inner_kernel,
+                [on_chip(chips, *piece)] * 2,
+                [IN_VMEM] * 2,
                 [total, block_ids],
                 [IN_VMEM, IN_HBM],
                 [
@@ -735,74 +756,33 @@
                 ],
                 micros=0.8,
             )
-        e_adj, h_adj, e_fwd, edges, *pays = call(
-            functools.partial(edge_kernel, step, 1),
-            [field_shape] * 3 + [edges_shape] + [halo_shape] * more,
-            [IN_VMEM] * (4 + more),
-            [e_adj, h_adj, e_fwd, edges, coef] + arrived_adj,
-            [IN_VMEM] * (5 + len(arrived_adj)),
-            aliases={0: 0, 1: 1, 2: 2, 3: 3},
-        )
-        if more:
-            arrived_adj = trade(pays)
-            e_fwd, h_fwd = call(
-                functools.partial(inner_kernel, step + 1, 0),
-                [field_shape] * 2,
-                [IN_VMEM] * 2,
-                [e_fwd, h_fwd, coef, drives, forced],
-                [IN_VMEM] * 5,
-                aliases={0: 0, 1: 1},
-                micros=1.1,
-            )
-
-    parts = call(
-        functools.partial(filter_edge_kernel, len(layout)),
-        [on_chip(*group)] * len(layout),
-        [IN_VMEM] * len(layout),
-        list(parts) + [total, edges, place],
-        [IN_VMEM] * (len(layout) + 3),
+            finals = write_out(1, 1, depth - 2, fields, [], 1.3)
+    finals = write_out(0, depth - 1, 2, fields, [finals], 0.7)
+
+    kept, sent = call(
+        filter_edge_kernel,
+        [on_chip(chips, *piece)] * 2,
+        [IN_VMEM] * 2,
+        [kept, sent, total, edges, owned],
+        [IN_VMEM] * 5,
         [
             pltpu.VMEM((2, width_x + 2 * PAD, width_y), F32),
             pltpu.VMEM((2, width_x, width_y), F32),
         ],
-        aliases={slot: slot for slot in range(len(layout))},
-    )
-    got = [swap_over(part, "grp", 1) for part in parts[middle:]]
-    sums = call(
-        add_kernel,
-        [on_chip(*group)] * middle,
-        [IN_VMEM] * middle,
-        list(parts[:middle]) + got,
-        [IN_VMEM] * (2 * middle),
-    )
-    got = [swap_over(part, "grp", mask) for part, mask in zip(sums[1:], middle_masks[1:])]
-    pieces = call(
-        functools.partial(add_split_kernel, middle),
-        [on_chip(*piece)] * far,
-        [IN_VMEM] * far,
-        [sums[0]] + got,
-        [IN_VMEM] * middle,
-    )
-    got = [swap_over(part, "grp", mask) for part, mask in zip(pieces[1:], far_masks[1:])]
+        aliases={0: 0, 1: 1},
+    )
+    got = swap_over(sent, "grp", 1)
+    sums = call(add_kernel, on_chip(chips, *piece), IN_VMEM, [kept, got], [IN_VMEM] * 2)
+    got = lax.all_to_all(
+        sums, "grp", 0, 0, axis_index_groups=[list(range(core, ngrp, 2)) for core in (0, 1)]
+    )
     scale = 3.0 / (STEPS * math.sqrt(ngrp))
     grad = call(
         functools.partial(last_kernel, scale),
         jax.ShapeDtypeStruct(piece, F32),
         IN_VMEM,
-        [pieces[0]] + got,
-        [IN_VMEM] * far,
-    )
-    finals = call(
-        out_kernel,
-        jax.ShapeDtypeStruct(fwd_fields.shape, F32),
-        IN_HBM,
-        [e_fwd, h_fwd],
-        [IN_VMEM] * 2,
-        [
-            pltpu.VMEM((3, depth, width_x, width_y), F32),
-            pltpu.SemaphoreType.DMA((6,)),
-        ],
-        micros=1.7,
+        [got],
+        [IN_VMEM],
     )
     return finals, grad.reshape(density.shape)
 

time: 56.2 us -> 60.2 us (1.071)
  starting transfers between devices: 24 us -> 16.9 us
  waiting for transfers between devices: 12.6 us -> 19.2 us
  local copies, waits for them, and re-layouts: 0.03 us -> 2.88 us
  Pallas kernels: 17.7 us -> 19.3 us
    ppermute x19 -> x11, starting transfers between devices: 24 us -> 13.4 us  [swap_over(): lax.ppermute(array, axis, [(i, i ^ mask) for i in range(lax.axis_size(axi...]
    all_to_all x0 -> x1, waiting for transfers between devices: none -> 6.9 us  [per_device(): lax.all_to_all(sums, 'grp', 0, 0, axis_index_groups=[list(range(core, ngr...]
    all_to_all x0 -> x1, starting transfers between devices: none -> 3.41 us  [per_device(): lax.all_to_all(sums, 'grp', 0, 0, axis_index_groups=[list(range(core, ngr...]
    unnamed x12 -> x16, local copies, waits for them, and re-layouts: 0.03 us -> 2.88 us
    pallas_call x32 -> x25, Pallas kernels: 17.7 us -> 19.3 us  [call(): pl.pallas_call(kernel, out_shape=outs, in_specs=specs, out_specs=out_spec...]
    ppermute x19 -> x11, waiting for transfers between devices: 12.6 us -> 12.3 us  [swap_over(): lax.ppermute(array, axis, [(i, i ^ mask) for i in range(lax.axis_size(axi...]
  transfers between devices with their start and end apart: 19 -> 12, of which waited for: 10 -> 6; matrix products, arithmetic and copies ran while one was open for 0% -> 0% of each run, Pallas kernels for 29% -> 27%
where the time goes in v8:
time: 60.2 us; the launch traced here: 59.9 us
  Pallas kernels  19.3 us (32%)
  waiting for transfers between devices  19.2 us (32%)
  starting transfers between devices  16.9 us (28%)
  local copies, waits for them, and re-layouts  2.88 us (5%)
  between operations  1.61 us (3%)
    pallas_call x25, Pallas kernels, call(): pl.pallas_call(kernel, out_shape=outs, in_specs=specs, out_specs=out_spec...  19.3 us
    ppermute x11, starting transfers between devices, swap_over(): lax.ppermute(array, axis, [(i, i ^ mask) for i in range(lax.axis_size(axi...  13.4 us
    ppermute x11, waiting for transfers between devices, swap_over(): lax.ppermute(array, axis, [(i, i ^ mask) for i in range(lax.axis_size(axi...  12.3 us
    all_to_all x1, waiting for transfers between devices, per_device(): lax.all_to_all(sums, 'grp', 0, 0, axis_index_groups=[list(range(core, ngr...  6.9 us
    all_to_all x1, starting transfers between devices, per_device(): lax.all_to_all(sums, 'grp', 0, 0, axis_index_groups=[list(range(core, ngr...  3.41 us
    unnamed x16, local copies, waits for them, and re-layouts  2.88 us
  transfers between devices with their start and end apart: 12, of which 6 were waited for; matrix products, arithmetic and copies ran while one was open for 0% of the time, Pallas kernels for 27%

profile of v8, /device:TPU:0, one launch (start us, length us, event | category | flops | bytes accessed | tf_op | source)
XLA Modules:
  0.0 59.9 jit_solution(3223480200715915585)
XLA Ops:
  0.7 5.1 %collective-permute-start.2 = (f32[64,128]{1,0:T(8,128)}, f32[64,128]{1,0:T(8,128)S(1)}, u32[]{:S(2)}, u32[]{:S(2)}) collective-permute-start(f32[64,128]{1,0:T(8,128)} %bitcast.2), channel_id=1, source_target_pairs={{0,24},{2,26},{4,28},{6,30},{8,16},{10,18},{12,20},{14,22},{16,8},... | collective-permute-start | bytes 98312 | tf_op jit(solution)/shard_map/ppermute | solution.py:563
  5.8 0.6 %collective-permute-start = (f32[64,128]{1,0:T(8,128)}, f32[64,128]{1,0:T(8,128)S(1)}, u32[]{:S(2)}, u32[]{:S(2)}) collective-permute-start(f32[64,128]{1,0:T(8,128)} %bitcast.4), channel_id=1, source_target_pairs={{0,8},{2,10},{4,12},{6,14},{8,0},{10,2},{12,4},{14,6},{16,24},{18,... | collective-permute-start | bytes 98312 | tf_op jit(solution)/shard_map/ppermute | solution.py:563
  6.4 1.4 %shard_map.95 = (f32[64,128]{1,0:T(8,128)S(1)}, f32[2,2,128,128]{3,2,1,0:T(8,128)S(1)}) custom-call(f32[1,6,8,128,128]{4,3,2,1,0:T(8,128)} %given.2, f32[1,6,8,128,128]{4,3,2,1,0:T(8,128)} %given.3, f32[64,128]{1,0:T(8,128)} %bitcast.5), custom_call_target="tpu_custom_call" | custom-call | bytes 900000 | tf_op jit(solution)/shard_map/pallas_call | solution.py:36
  7.8 1.4 %collective-permute-start.3 = (f32[2,2,128,128]{3,2,1,0:T(8,128)S(1)}, f32[2,2,128,128]{3,2,1,0:T(8,128)S(1)}, u32[]{:S(2)}, u32[]{:S(2)}) collective-permute-start(f32[2,2,128,128]{3,2,1,0:T(8,128)S(1)} %get-tuple-element.72), channel_id=1, source_target_pairs={{0,1},{1,0},{2,3},{3,2},{4,5},{5,4},{6,7},{7,6},{8,9},{9,8},{10,11... | collective-permute-start | bytes 786440 | tf_op jit(solution)/shard_map/ppermute | solution.py:563
  9.3 1.5 %collective-permute-done.1.refs_2_ = f32[64,128]{1,0:T(8,128)S(1)} collective-permute-done((f32[64,128]{1,0:T(8,128)}, f32[64,128]{1,0:T(8,128)S(1)}, u32[]{:S(2)}, u32[]{:S(2)}) %collective-permute-start.1) | collective-permute-done | bytes 32800 | tf_op jit(solution)/shard_map/ppermute | solution.py:563
  10.8 1.6 %collective-permute-start.4 = (f32[4,64,128]{2,1,0:T(8,128)S(1)}, f32[4,64,128]{2,1,0:T(8,128)S(1)}, u32[]{:S(2)}, u32[]{:S(2)}) collective-permute-start(f32[4,64,128]{2,1,0:T(8,128)S(1)} %shard_map.96.near.refs_0_), channel_id=1, source_target_pairs={{0,4},{2,6},{4,0},{6,2},{8,12},{10,14},{12,8},{14,10},{16,20},{18,... | collective-permute-start | bytes 393224 | tf_op jit(solution)/shard_map/ppermute | solution.py:563
  13.2 0.7 %shard_map.101 = (f32[8,144,128]{2,1,0:T(8,128)S(1)}, f32[2,144,128]{2,1,0:T(8,128)S(1)}, f32[8,128,128]{2,1,0:T(8,128)S(1)}, f32[4,128]{1,0:T(4,128)S(1)}, f32[...) custom-call(s32[1,3]{1,0:T(1,128)S(1)} %copy-done.5, s32[1]{0:T(128)S(6)} %copy.112.wave_idx, ...), custom_call_target="tpu_custom_call" | custom-call | bytes 900000 | tf_op jit(solution)/shard_map/pallas_call | solution.py:36
  13.9 1.2 %shard_map.99 = (f32[3,9,144,128]{3,2,1,0:T(8,128)S(1)}, f32[3,9,144,128]{3,2,1,0:T(8,128)S(1)}, f32[3,8,128,128]{3,2,1,0:T(8,128)S(1)}) custom-call(f32[1,6,8,128,128]{4,3,2,1,0:T(8,128)S(1)} %copy-done.2, f32[4,64,128]{2,1,0:T(8,128)S(1)} %shard_map.96.near.refs_0_), custom_call_target="tpu_custom_call" | custom-call | bytes 4500000 | tf_op jit(solution)/shard_map/pallas_call | solution.py:36
  15.1 1.2 %shard_map.97 = (f32[3,9,144,128]{3,2,1,0:T(8,128)S(1)}, f32[3,9,144,128]{3,2,1,0:T(8,128)S(1)}, f32[3,8,128,128]{3,2,1,0:T(8,128)S(1)}) custom-call(f32[1,6,8,128,128]{4,3,2,1,0:T(8,128)S(1)} %copy-done.3, f32[4,64,128]{2,1,0:T(8,128)S(1)} %shard_map.96.near.refs_0_), custom_call_target="tpu_custom_call" | custom-call | bytes 4500000 | tf_op jit(solution)/shard_map/pallas_call | solution.py:36
  16.3 0.5 collective-permute-start.5
  16.8 0.6 %shard_map.103.refs_3_ = f32[16,64,128]{2,1,0:T(8,128)S(1)} custom-call(f32[4,64,128]{2,1,0:T(8,128)S(1)} %shard_map.96.near.refs_0_, f32[4,64,128]{2,1,0:T(8,128)S(1)} %shard_map.102.refs_1_, f32[4,64,128]{2,1,0:T(8,128)S(1)} %collective-permute-done.6.refs_2_, s32[16]{0:T(128)S(1)} %copy-done.4), custom_call_target="tpu_custom_call" | custom-call | bytes 2100000 | tf_op jit(solution)/shard_map/pallas_call | solution.py:36
  18.2 1.5 %collective-permute-start.7 = (f32[2,2,128,128]{3,2,1,0:T(8,128)S(1)}, f32[2,2,128,128]{3,2,1,0:T(8,128)S(1)}, u32[]{:S(2)}, u32[]{:S(2)}) collective-permute-start(f32[2,2,128,128]{3,2,1,0:T(8,128)S(1)} %get-tuple-element.98), channel_id=1, source_target_pairs={{0,1},{1,0},{2,3},{3,2},{4,5},{5,4},{6,7},{7,6},{8,9},{9,8},{10,11... | collective-permute-start | bytes 786440 | tf_op jit(solution)/shard_map/ppermute | solution.py:563
  19.7 0.6 %shard_map.106.coef.refs_5_ = f32[8,128,128]{2,1,0:T(8,128)S(1)} custom-call(f32[8,128,128]{2,1,0:T(8,128)S(1)} %shard_map.104.refs_5_.coef_in, f32[4,64,128]{2,1,0:T(8,128)S(1)} %collective-permute-done.5.refs_0_, f32[4,16,128]{2,1,0:T(8,128)S(1)} %get-tuple-element.80.refs_1_, ...), custom_call_target="tpu_custom_call", output_to_operand_aliasing={{}: (0, {})} | custom-call | bytes 1800000 | tf_op jit(solution)/shard_map/pallas_call | solution.py:36
  20.3 0.5 shard_map.107
  20.9 2.2 %shard_map.108 = (f32[3,9,144,128]{3,2,1,0:T(8,128)S(1)}, f32[3,9,144,128]{3,2,1,0:T(8,128)S(1)}, f32[3,9,144,128]{3,2,1,0:T(8,128)S(1)}, f32[3,9,144,128]{3,2,1,0:T(8,128)S(1)}, f32[8,144,128]{2,1,0:T(8,128)S(1)}) custom-call(f32[3,9,144,128]{3,2,1,0:T(8,128)S(1)} %get-tuple-element.8, ...), custom_call_target="tpu_custom_call", output_to_operand_aliasing={{0}: (0, {}), {1}: (1, {}), {2}: (2, {}), {3}: (3, {}), {4}... | custom-call | bytes 6899999 | tf_op jit(solution)/shard_map/pallas_call | solution.py:36
  23.1 3.7 %collective-permute-done.7.refs_8_.refs_9_ = f32[2,2,128,128]{3,2,1,0:T(8,128)S(1)} collective-permute-done((f32[2,2,128,128]{3,2,1,0:T(8,128)S(1)}, f32[2,2,128,128]{3,2,1,0:T(8,128)S(1)}, u32[]{:S(2)}, u32[]{:S(2)}) %collective-permute-start.7) | collective-permute-done | bytes 262176 | tf_op jit(solution)/shard_map/ppermute | solution.py:563
  27.2 1.3 %collective-permute-start.8 = (f32[2,2,128,128]{3,2,1,0:T(8,128)S(1)}, f32[2,2,128,128]{3,2,1,0:T(8,128)S(1)}, u32[]{:S(2)}, u32[]{:S(2)}) collective-permute-start(f32[2,2,128,128]{3,2,1,0:T(8,128)S(1)} %get-tuple-element.109), channel_id=1, source_target_pairs={{0,1},{1,0},{2,3},{3,2},{4,5},{5,4},{6,7},{7,6},{8,9},{9,8},{10,11... | collective-permute-start | bytes 786440 | tf_op jit(solution)/shard_map/ppermute | solution.py:563
  28.5 2.2 %shard_map.110 = (f32[3,9,144,128]{3,2,1,0:T(8,128)S(1)}, f32[3,9,144,128]{3,2,1,0:T(8,128)S(1)}, f32[3,9,144,128]{3,2,1,0:T(8,128)S(1)}, f32[3,9,144,128]{3,2,1,0:T(8,128)S(1)}, f32[8,144,128]{2,1,0:T(8,128)S(1)}) custom-call(f32[3,9,144,128]{3,2,1,0:T(8,128)S(1)} %get-tuple-element.9, ...), custom_call_target="tpu_custom_call", output_to_operand_aliasing={{0}: (0, {}), {1}: (1, {}), {2}: (2, {}), {3}: (3, {}), {4}... | custom-call | bytes 6899999 | tf_op jit(solution)/shard_map/pallas_call | solution.py:36
  30.7 4.3 %collective-permute-done.8.refs_8_.refs_9_ = f32[2,2,128,128]{3,2,1,0:T(8,128)S(1)} collective-permute-done((f32[2,2,128,128]{3,2,1,0:T(8,128)S(1)}, f32[2,2,128,128]{3,2,1,0:T(8,128)S(1)}, u32[]{:S(2)}, u32[]{:S(2)}) %collective-permute-start.8) | collective-permute-done | bytes 262176 | tf_op jit(solution)/shard_map/ppermute | solution.py:563
  35.3 1.2 %collective-permute-start.9 = (f32[2,2,128,128]{3,2,1,0:T(8,128)S(1)}, f32[2,2,128,128]{3,2,1,0:T(8,128)S(1)}, u32[]{:S(2)}, u32[]{:S(2)}) collective-permute-start(f32[2,2,128,128]{3,2,1,0:T(8,128)S(1)} %get-tuple-element.122), channel_id=1, source_target_pairs={{0,1},{1,0},{2,3},{3,2},{4,5},{5,4},{6,7},{7,6},{8,9},{9,8},{10,11... | collective-permute-start | bytes 786440 | tf_op jit(solution)/shard_map/ppermute | solution.py:563
  36.5 2.2 %shard_map.112 = (f32[3,9,144,128]{3,2,1,0:T(8,128)S(1)}, f32[3,9,144,128]{3,2,1,0:T(8,128)S(1)}, f32[3,9,144,128]{3,2,1,0:T(8,128)S(1)}, f32[3,9,144,128]{3,2,1,0:T(8,128)S(1)}, f32[8,144,128]{2,1,0:T(8,128)S(1)}) custom-call(f32[3,9,144,128]{3,2,1,0:T(8,128)S(1)} %get-tuple-element.1, ...), custom_call_target="tpu_custom_call", output_to_operand_aliasing={{0}: (0, {}), {1}: (1, {}), {2}: (2, {}), {3}: (3, {}), {4}... | custom-call | bytes 6899999 | tf_op jit(solution)/shard_map/pallas_call | solution.py:36
  38.8 0.7 %shard_map.116 = (f32[8,64,128]{2,1,0:T(8,128)S(1)}, f32[8,64,128]{2,1,0:T(8,128)S(1)}) custom-call(f32[8,144,128]{2,1,0:T(8,128)S(1)} %get-tuple-element.127.total, s32[16]{0:T(128)} %block_ids_far.1), custom_call_target="tpu_custom_call" | custom-call | bytes 2400000 | tf_op jit(solution)/shard_map/pallas_call | solution.py:36
  39.5 1.5 %shard_map.113 = (f32[1,6,8,128,128]{4,3,2,1,0:T(8,128)}, f32[3,9,144,128]{3,2,1,0:T(8,128)S(1)}, f32[3,9,144,128]{3,2,1,0:T(8,128)S(1)}) custom-call(f32[3,9,144,128]{3,2,1,0:T(8,128)S(1)} %get-tuple-element.115.e, f32[3,9,144,128]{3,2,1,0:T(8,128)S(1)} %get-tuple-element.116.h), custom_call_target="tpu_custom_call", output_to_operand_aliasing={{1}: (0, {}), {2}: (1, {})} | custom-call | bytes 3900000 | tf_op jit(solution)/shard_map/pallas_call | solution.py:36
  41.0 1.2 %collective-permute-done.9.refs_8_.refs_9_ = f32[2,2,128,128]{3,2,1,0:T(8,128)S(1)} collective-permute-done((f32[2,2,128,128]{3,2,1,0:T(8,128)S(1)}, f32[2,2,128,128]{3,2,1,0:T(8,128)S(1)}, u32[]{:S(2)}, u32[]{:S(2)}) %collective-permute-start.9) | collective-permute-done | bytes 262176 | tf_op jit(solution)/shard_map/ppermute | solution.py:563
  42.5 1.3 %copy-done = f32[3,9,144,128]{3,2,1,0:T(8,128)} copy-done((f32[3,9,144,128]{3,2,1,0:T(8,128)}, f32[3,9,144,128]{3,2,1,0:T(8,128)S(1)}, u32[]{:S(2)}) %copy-start) | copy-done | bytes 1990680
  44.1 1.5 %collective-permute-done.10.got = f32[8,64,128]{2,1,0:T(8,128)S(1)} collective-permute-done((f32[8,64,128]{2,1,0:T(8,128)S(1)}, f32[8,64,128]{2,1,0:T(8,128)S(1)}, u32[]{:S(2)}, u32[]{:S(2)}) %collective-permute-start.10) | collective-permute-done | bytes 262176 | tf_op jit(solution)/shard_map/ppermute | solution.py:563
  45.7 0.7 %shard_map.118 = f32[8,64,128]{2,1,0:T(8,128)} custom-call(f32[8,64,128]{2,1,0:T(8,128)S(1)} %get-tuple-element.132.kept, f32[8,64,128]{2,1,0:T(8,128)S(1)} %collective-permute-done.10.got), custom_call_target="tpu_custom_call" | custom-call | bytes 900000 | tf_op jit(solution)/shard_map/pallas_call | solution.py:36
  46.4 3.4 %all-to-all-start = ((f32[8,64,128]{2,1,0:T(8,128)}), f32[8,64,128]{2,1,0:T(8,128)S(1)}, u32[]{:S(2)}, u32[]{:S(2)}) async-start(f32[8,64,128]{2,1,0:T(8,128)} %shard_map.118), calls=%async_computation | async-start | bytes 524288 | tf_op jit(solution)/shard_map/all_to_all | solution.py:776
  49.8 1.5 %copy-done.1 = f32[3,9,144,128]{3,2,1,0:T(8,128)S(1)} copy-done((f32[3,9,144,128]{3,2,1,0:T(8,128)S(1)}, f32[3,9,144,128]{3,2,1,0:T(8,128)}, u32[]{:S(2)}) %copy-start.1) | copy-done | bytes 1990680
  51.4 1.0 %shard_map.115 = (f32[1,6,8,128,128]{4,3,2,1,0:T(8,128)}, f32[3,9,144,128]{3,2,1,0:T(8,128)S(1)}, f32[3,9,144,128]{3,2,1,0:T(8,128)S(1)}) custom-call(f32[3,9,144,128]{3,2,1,0:T(8,128)S(1)} %get-tuple-element.123.e, f32[3,9,144,128]{3,2,1,0:T(8,128)S(1)} %copy-done.1, ...), custom_call_target="tpu_custom_call", output_to_operand_aliasing={{1}: (0, {}), {2}: (1, {}), {0}: (2, {})} | custom-call | bytes 2100000 | tf_op jit(solution)/shard_map/pallas_call | solution.py:36
  52.3 6.9 %all-to-all-done.got = f32[8,64,128]{2,1,0:T(8,128)S(1)} async-done(((f32[8,64,128]{2,1,0:T(8,128)}), f32[8,64,128]{2,1,0:T(8,128)S(1)}, u32[]{:S(2)}, u32[]{:S(2)}) %all-to-all-start) | async-done | bytes 262176 | tf_op jit(solution)/shard_map/all_to_all | solution.py:776
  59.3 0.6 %shard_map.119 = f32[64,128]{1,0:T(8,128)} custom-call(f32[8,64,128]{2,1,0:T(8,128)S(1)} %all-to-all-done.got), custom_call_target="tpu_custom_call" | custom-call | bytes 900000 | tf_op jit(solution)/shard_map/pallas_call | solution.py:36
  (33 shorter events, 2.1 us)
Async XLA Ops:
  0.6 12.5 %copy-start.4 = (s32[16]{0:T(128)S(1)}, s32[16]{0:T(128)}, u32[]{:S(2)}) copy-start(s32[16]{0:T(128)} %block_ids_far.1) | copy-start | bytes 196
  0.6 12.5 %copy-start.5 = (s32[1,3]{1,0:T(1,128)S(1)}, s32[1,3]{1,0:T(1,128)}, u32[]{:S(2)}) copy-start(s32[1,3]{1,0:T(1,128)} %source.1) | copy-start | bytes 40
  0.7 12.5 %copy-start.6 = (s32[16]{0:T(128)S(1)}, s32[16]{0:T(128)}, u32[]{:S(2)}) copy-start(s32[16]{0:T(128)} %material_idx.1) | copy-start | bytes 196
  0.7 12.5 %copy-start.7 = (f32[4]{0:T(128)S(1)}, f32[4]{0:T(128)}, u32[]{:S(2)}) copy-start(f32[4]{0:T(128)} %material_eps.1) | copy-start | bytes 52
  0.7 13.2 %copy-start.2 = (f32[1,6,8,128,128]{4,3,2,1,0:T(8,128)S(1)}, f32[1,6,8,128,128]{4,3,2,1,0:T(8,128)}, u32[]{:S(2)}) copy-start(f32[1,6,8,128,128]{4,3,2,1,0:T(8,128)} %given.3) | copy-start | bytes 9437188
  0.7 8.6 %collective-permute-start.2 = (f32[64,128]{1,0:T(8,128)}, f32[64,128]{1,0:T(8,128)S(1)}, u32[]{:S(2)}, u32[]{:S(2)}) collective-permute-start(f32[64,128]{1,0:T(8,128)} %bitcast.2), channel_id=1, source_target_pairs={{0,24},{2,26},{4,28},{6,30},{8,16},{10,18},{12,20},{14,22},{16,8},... | collective-permute-start | bytes 98312 | tf_op jit(solution)/shard_map/ppermute | solution.py:563
  5.8 5.0 %collective-permute-start.1 = (f32[64,128]{1,0:T(8,128)}, f32[64,128]{1,0:T(8,128)S(1)}, u32[]{:S(2)}, u32[]{:S(2)}) collective-permute-start(f32[64,128]{1,0:T(8,128)} %bitcast.3), channel_id=1, source_target_pairs={{0,16},{2,18},{4,20},{6,22},{8,24},{10,26},{12,28},{14,30},{16,0},... | collective-permute-start | bytes 98312 | tf_op jit(solution)/shard_map/ppermute | solution.py:563
  5.8 5.0 %collective-permute-start = (f32[64,128]{1,0:T(8,128)}, f32[64,128]{1,0:T(8,128)S(1)}, u32[]{:S(2)}, u32[]{:S(2)}) collective-permute-start(f32[64,128]{1,0:T(8,128)} %bitcast.4), channel_id=1, source_target_pairs={{0,8},{2,10},{4,12},{6,14},{8,0},{10,2},{12,4},{14,6},{16,24},{18,... | collective-permute-start | bytes 98312 | tf_op jit(solution)/shard_map/ppermute | solution.py:563
  7.8 7.2 %copy-start.3 = (f32[1,6,8,128,128]{4,3,2,1,0:T(8,128)S(1)}, f32[1,6,8,128,128]{4,3,2,1,0:T(8,128)}, u32[]{:S(2)}) copy-start(f32[1,6,8,128,128]{4,3,2,1,0:T(8,128)} %given.2) | copy-start | bytes 9437188
  7.8 9.6 %collective-permute-start.3 = (f32[2,2,128,128]{3,2,1,0:T(8,128)S(1)}, f32[2,2,128,128]{3,2,1,0:T(8,128)S(1)}, u32[]{:S(2)}, u32[]{:S(2)}) collective-permute-start(f32[2,2,128,128]{3,2,1,0:T(8,128)S(1)} %get-tuple-element.72), channel_id=1, source_target_pairs={{0,1},{1,0},{2,3},{3,2},{4,5},{5,4},{6,7},{7,6},{8,9},{9,8},{10,11... | collective-permute-start | bytes 786440 | tf_op jit(solution)/shard_map/ppermute | solution.py:563
  10.8 5.4 %collective-permute-start.4 = (f32[4,64,128]{2,1,0:T(8,128)S(1)}, f32[4,64,128]{2,1,0:T(8,128)S(1)}, u32[]{:S(2)}, u32[]{:S(2)}) collective-permute-start(f32[4,64,128]{2,1,0:T(8,128)S(1)} %shard_map.96.near.refs_0_), channel_id=1, source_target_pairs={{0,4},{2,6},{4,0},{6,2},{8,12},{10,14},{12,8},{14,10},{16,20},{18,... | collective-permute-start | bytes 393224 | tf_op jit(solution)/shard_map/ppermute | solution.py:563
  13.0 3.8 %collective-permute-start.6 = (f32[4,64,128]{2,1,0:T(8,128)S(1)}, f32[4,64,128]{2,1,0:T(8,128)S(1)}, u32[]{:S(2)}, u32[]{:S(2)}) collective-permute-start(f32[4,64,128]{2,1,0:T(8,128)S(1)} %shard_map.96.near.refs_0_), channel_id=1, source_target_pairs={{0,2},{2,0},{4,6},{6,4},{8,10},{10,8},{12,14},{14,12},{16,18},{18,... | collective-permute-start | bytes 393224 | tf_op jit(solution)/shard_map/ppermute | solution.py:563
  16.3 1.5 %collective-permute-start.5 = (f32[4,64,128]{2,1,0:T(8,128)S(1)}, f32[4,64,128]{2,1,0:T(8,128)S(1)}, u32[]{:S(2)}, u32[]{:S(2)}) collective-permute-start(f32[4,64,128]{2,1,0:T(8,128)S(1)} %shard_map.102.refs_1_), channel_id=1, source_target_pairs={{0,2},{2,0},{4,6},{6,4},{8,10},{10,8},{12,14},{14,12},{16,18},{18,... | collective-permute-start | bytes 393224 | tf_op jit(solution)/shard_map/ppermute | solution.py:563
  18.2 8.6 %collective-permute-start.7 = (f32[2,2,128,128]{3,2,1,0:T(8,128)S(1)}, f32[2,2,128,128]{3,2,1,0:T(8,128)S(1)}, u32[]{:S(2)}, u32[]{:S(2)}) collective-permute-start(f32[2,2,128,128]{3,2,1,0:T(8,128)S(1)} %get-tuple-element.98), channel_id=1, source_target_pairs={{0,1},{1,0},{2,3},{3,2},{4,5},{5,4},{6,7},{7,6},{8,9},{9,8},{10,11... | collective-permute-start | bytes 786440 | tf_op jit(solution)/shard_map/ppermute | solution.py:563
  27.2 7.8 %collective-permute-start.8 = (f32[2,2,128,128]{3,2,1,0:T(8,128)S(1)}, f32[2,2,128,128]{3,2,1,0:T(8,128)S(1)}, u32[]{:S(2)}, u32[]{:S(2)}) collective-permute-start(f32[2,2,128,128]{3,2,1,0:T(8,128)S(1)} %get-tuple-element.109), channel_id=1, source_target_pairs={{0,1},{1,0},{2,3},{3,2},{4,5},{5,4},{6,7},{7,6},{8,9},{9,8},{10,11... | collective-permute-start | bytes 786440 | tf_op jit(solution)/shard_map/ppermute | solution.py:563
  35.3 6.9 %collective-permute-start.9 = (f32[2,2,128,128]{3,2,1,0:T(8,128)S(1)}, f32[2,2,128,128]{3,2,1,0:T(8,128)S(1)}, u32[]{:S(2)}, u32[]{:S(2)}) collective-permute-start(f32[2,2,128,128]{3,2,1,0:T(8,128)S(1)} %get-tuple-element.122), channel_id=1, source_target_pairs={{0,1},{1,0},{2,3},{3,2},{4,5},{5,4},{6,7},{7,6},{8,9},{9,8},{10,11... | collective-permute-start | bytes 786440 | tf_op jit(solution)/shard_map/ppermute | solution.py:563
  42.5 1.3 %copy-start = (f32[3,9,144,128]{3,2,1,0:T(8,128)}, f32[3,9,144,128]{3,2,1,0:T(8,128)S(1)}, u32[]{:S(2)}) copy-start(f32[3,9,144,128]{3,2,1,0:T(8,128)S(1)} %get-tuple-element.124.h) | copy-start | bytes 5971972
  44.1 1.6 %collective-permute-start.10 = (f32[8,64,128]{2,1,0:T(8,128)S(1)}, f32[8,64,128]{2,1,0:T(8,128)S(1)}, u32[]{:S(2)}, u32[]{:S(2)}) collective-permute-start(f32[8,64,128]{2,1,0:T(8,128)S(1)} %get-tuple-element.133), channel_id=1, source_target_pairs={{0,2},{2,0},{4,6},{6,4},{8,10},{10,8},{12,14},{14,12},{16,18},{18,... | collective-permute-start | bytes 786440 | tf_op jit(solution)/shard_map/ppermute | solution.py:563
  46.4 12.9 %all-to-all-start = ((f32[8,64,128]{2,1,0:T(8,128)}), f32[8,64,128]{2,1,0:T(8,128)S(1)}, u32[]{:S(2)}, u32[]{:S(2)}) async-start(f32[8,64,128]{2,1,0:T(8,128)} %shard_map.118), calls=%async_computation | async-start | bytes 524288 | tf_op jit(solution)/shard_map/all_to_all | solution.py:776
  49.8 1.6 %copy-start.1 = (f32[3,9,144,128]{3,2,1,0:T(8,128)S(1)}, f32[3,9,144,128]{3,2,1,0:T(8,128)}, u32[]{:S(2)}) copy-start(f32[3,9,144,128]{3,2,1,0:T(8,128)} %copy-done) | copy-start | bytes 5971972

commit v9 on v7

--- a/solution.py
+++ b/solution.py
@@ -218,15 +218,33 @@
 
 
 def prepare_kernel(
-    layout, source, wave_idx, block_ids, material_idx, material_eps,
+    layout, wave_idx, source_far, ids_far, idx_far, eps_far,
     total, edges, forced, drives, base, place,
+    source, block_ids, material_idx, material_eps, sems,
 ):
     depth, rows, width_y = forced.shape
+    fetches = [
+        pltpu.make_async_copy(far, near, sems.at[slot])
+        for slot, (far, near) in enumerate(
+            (
+                (source_far, source),
+                (ids_far, block_ids),
+                (idx_far, material_idx),
+                (eps_far, material_eps),
+            )
+        )
+    ]
+    for fetch in fetches:
+        fetch.start()
     nblock = block_ids.shape[0]
     block_rows = rows // nblock
     empty = jnp.zeros(total.shape[1:], F32)
     edges[0] = empty
     edges[1] = empty
+    for layer in range(depth):
+        total[layer] = empty
+    for fetch in fetches:
+        fetch.wait()
     xcoord = lax.broadcasted_iota(jnp.int32, (rows, width_y), 0)
     ycoord = lax.broadcasted_iota(jnp.int32, (rows, width_y), 1)
     offset_x = (xcoord - source[0, 1]).astype(F32) / (rows / 4.0)
@@ -237,7 +255,6 @@
     drives[...] = AMPLITUDE * jnp.sin(2.0 * math.pi / (6.0 + 2.0 * wave) * step)
     level = source[0, 0] - lax.axis_index("slab") * depth
     for layer in range(depth):
-        total[layer] = empty
         forced[layer] = jnp.where(level == layer, 1.0, 0.0) * profile
     for block in range(nblock):
         value = jnp.full((block_rows, width_y), material_eps[material_idx[block]], F32)
@@ -284,13 +301,29 @@
     lax.fori_loop(1, win.top, body, 0)
 
 
-def take_kernel(evo, h_in, curls_in, e, below, above, h, curls):
-    win = Window(e, h)
+def settle_kernel(layout, *refs):
+    refs = list(refs)
+    del refs[:4]
+    e_fwd, e_adj, below, above = (refs.pop(0) for _ in range(4))
+    parts = [refs.pop(0) for _ in layout]
+    ids_far, h_fwd, curls_fwd, h_adj, curls_adj, blocks, block_ids, sem = refs
+    fetch = pltpu.make_async_copy(ids_far, block_ids, sem)
+    fetch.start()
+    nothing = jnp.zeros(blocks.shape[1:], F32)
+    for block in range(blocks.shape[0]):
+        blocks[block] = nothing
     has_up, has_low = neighbours()
-    pl.when(has_up)(lambda: win.take_above(above.at[evo]))
-    pl.when(has_low)(lambda: win.take_below(below.at[evo]))
-    win.put_curl(curls, win.top, win.top - 1)
-    win.put_curl(curls, 0, win.under)
+    for evo, (e, h, curls) in enumerate(((e_fwd, h_fwd, curls_fwd), (e_adj, h_adj, curls_adj))):
+        win = Window(e, h)
+        pl.when(has_up)(lambda: win.take_above(above.at[evo]))
+        pl.when(has_low)(lambda: win.take_below(below.at[evo]))
+        win.put_curl(curls, win.top, win.top - 1)
+        win.put_curl(curls, 0, win.under)
+    fetch.wait()
+    me = lax.axis_index("grp")
+    for part, masks in zip(parts, layout):
+        for slot, mask in enumerate(masks):
+            blocks[block_ids[me ^ mask]] = part[slot]
 
 
 def edge_kernel(step, evo, *refs):
@@ -389,17 +422,6 @@
     placed[pl.ds(PAD + rows, PAD), :] = margin
 
 
-def scatter_kernel(layout, *refs):
-    parts, (block_ids, blocks) = refs[: len(layout)], refs[len(layout) :]
-    me = lax.axis_index("grp")
-    nothing = jnp.zeros(blocks.shape[1:], F32)
-    for block in range(blocks.shape[0]):
-        blocks[block] = nothing
-    for part, masks in zip(parts, layout):
-        for slot, mask in enumerate(masks):
-            blocks[block_ids[me ^ mask]] = part[slot]
-
-
 def place_layer(layer, first_slot, parts, place, blocks, placed):
     nblock = blocks.shape[0]
     block_rows = (placed.shape[0] - 2 * PAD) // nblock
@@ -475,21 +497,20 @@
         for first, size in chunks(rows):
             there[pl.ds(first, size), :] = filtered(total.at[layer], first, size)
         for block in range(nblock):
-            target = pl.ds(pl.multiple_of(layer * block_rows, block_rows), block_rows)
+            target = pl.ds(pl.multiple_of((layer - 1) * block_rows, block_rows), block_rows)
             blocks[block, target, :] = there[pl.ds(block * block_rows, block_rows), :]
         return carry
 
     lax.fori_loop(1, depth - 1, body, 0, unroll=2)
     fetch.wait()
-    inner = pl.ds(block_rows, (depth - 2) * block_rows)
+    inner = pl.ds(0, (depth - 2) * block_rows)
     for part, masks in zip(parts, layout):
         for slot, mask in enumerate(masks):
-            part[slot, inner, :] = blocks[block_ids[me ^ mask], inner, :]
-
-
-def filter_edge_kernel(count, *refs):
-    total, edges, place = refs[count : count + 3]
-    parts, (sums, wide) = refs[count + 3 : -2], refs[-2:]
+            part[slot] = blocks[block_ids[me ^ mask], inner, :]
+
+
+def filter_edge_kernel(layout, total, edges, place, *rest):
+    parts, (sums, wide) = rest[:-2], rest[-2:]
     depth = total.shape[0]
     nblock = place.shape[0]
     rows = wide.shape[1]
@@ -498,11 +519,11 @@
         sums[which] = total[layer] + edges[which]
         for first, size in chunks(rows):
             wide[which, pl.ds(first, size), :] = filtered(sums.at[which], first, size)
-    for which, layer in enumerate((0, depth - 1)):
+    for which in range(2):
         blocks = [
             wide[which, pl.ds(block * block_rows, block_rows), :] for block in range(nblock)
         ]
-        target = pl.ds(layer * block_rows, block_rows)
+        target = pl.ds(which * block_rows, block_rows)
         for slot in range(nblock):
             value = None
             for block, piece in enumerate(blocks):
@@ -517,13 +538,16 @@
         out[...] = a[...] + b[...]
 
 
-def add_split_kernel(count, *refs):
-    terms, outs = refs[:count], refs[count:]
+def join_kernel(count, block_rows, *refs):
+    inner, edge, outs = refs[:count], refs[count : 2 * count], refs[2 * count :]
+    rows = outs[0].shape[0]
     for slot, out in enumerate(outs):
-        value = terms[0][slot]
-        for term in terms[1:]:
-            value = value + term[slot]
-        out[...] = value
+        middle, ends = inner[0][slot], edge[0][slot]
+        for a, b in zip(inner[1:], edge[1:]):
+            middle, ends = middle + a[slot], ends + b[slot]
+        out[pl.ds(0, block_rows), :] = ends[:block_rows]
+        out[pl.ds(block_rows, rows - 2 * block_rows), :] = middle
+        out[pl.ds(rows - block_rows, block_rows), :] = ends[block_rows:]
 
 
 def last_kernel(scale, *refs):
@@ -599,6 +623,29 @@
     edges_shape = on_chip(2, width_x + 2 * PAD, width_y)
     coef_shape = on_chip(depth, width_x, width_y)
     plane = on_chip(width_x, width_y)
+
+    def by_owner(kernel, layers, operands, specs, scratch, micros):
+        shape = on_chip(far, layers * block_rows, width_y)
+        parts = call(
+            kernel,
+            [shape] * len(layout),
+            [IN_VMEM] * len(layout),
+            operands,
+            specs,
+            scratch,
+            micros=micros,
+        )
+        got = [swap_over(part, "grp", 1) for part in parts[middle:]]
+        sums = call(
+            add_kernel,
+            [shape] * middle,
+            [IN_VMEM] * middle,
+            list(parts[:middle]) + got,
+            [IN_VMEM] * (2 * middle),
+        )
+        return [sums[0]] + [
+            swap_over(part, "grp", mask) for part, mask in zip(sums[1:], middle_masks[1:])
+        ]
 
     design = density.reshape(piece)
     got = [swap_over(design, "grp", mask) for mask in far_masks[1:]]
@@ -628,8 +675,15 @@
             place_shape,
         ],
         [IN_VMEM] * 6,
-        [source_pos, wave_idx, block_ids, material_idx, material_eps],
-        [IN_SMEM] * 5,
+        [wave_idx, source_pos, block_ids, material_idx, material_eps],
+        [IN_SMEM] + [IN_HBM] * 4,
+        [
+            pltpu.SMEM(source_pos.shape, jnp.int32),
+            pltpu.SMEM(block_ids.shape, jnp.int32),
+            pltpu.SMEM(material_idx.shape, jnp.int32),
+            pltpu.SMEM(material_eps.shape, F32),
+            pltpu.SemaphoreType.DMA((4,)),
+        ],
     )
     fields = []
     for evo, given in enumerate((fwd_fields, adj_fields)):
@@ -645,28 +699,19 @@
     others = [tie(part, [forced] + [e for e, _, _ in fields]) for part in others]
     early = [near] + others + [near_across]
     last = [swap_over(part, "grp", 1) for part in others]
-    blocks = call(
-        functools.partial(scatter_kernel, layout[: len(early)]),
-        on_chip(nblock, *piece),
-        IN_VMEM,
-        early + [block_ids],
-        [IN_VMEM] * len(early) + [IN_SMEM],
-        micros=0.7,
-    )
     first_slot = far * len(early)
 
-    taken = []
-    for evo, (e, h, curls) in enumerate(fields):
-        h, curls = call(
-            functools.partial(take_kernel, evo),
-            [field_shape, curls_shape],
-            [IN_VMEM] * 2,
-            [h, curls, e, below, above],
-            [IN_VMEM] * 5,
-            aliases={0: 0, 1: 1},
-        )
-        taken.append((e, h, curls))
-    (e_fwd, h_fwd, curls_fwd), (e_adj, h_adj, curls_adj) = taken
+    (e_fwd, h_fwd, curls_fwd), (e_adj, h_adj, curls_adj) = fields
+    h_fwd, curls_fwd, h_adj, curls_adj, blocks = call(
+        functools.partial(settle_kernel, layout[: len(early)]),
+        [field_shape, curls_shape] * 2 + [on_chip(nblock, *piece)],
+        [IN_VMEM] * 5,
+        [h_fwd, curls_fwd, h_adj, curls_adj, e_fwd, e_adj, below, above] + early + [block_ids],
+        [IN_VMEM] * (8 + len(early)) + [IN_HBM],
+        [pltpu.SMEM(block_ids.shape, jnp.int32), pltpu.SemaphoreType.DMA],
+        aliases={0: 0, 1: 1, 2: 2, 3: 3},
+        micros=0.6,
+    )
     placed = pltpu.VMEM((2, width_x + 2 * PAD, width_y), F32)
     coef = call(
         functools.partial(coef_edge_kernel, first_slot, len(last)),
@@ -680,37 +725,21 @@
     arrived_fwd, arrived_adj = [curls_fwd], [curls_adj]
     for step in range(STEPS):
         more = npay if step < STEPS - 1 else 0
-        e_fwd, h_fwd, *pays = call(
-            functools.partial(edge_kernel, step, 0),
-            [field_shape] * 2 + [halo_shape] * more,
-            [IN_VMEM] * (2 + more),
-            [e_fwd, h_fwd, coef, drives, forced] + arrived_fwd,
-            [IN_VMEM] * (5 + len(arrived_fwd)),
-            aliases={0: 0, 1: 1},
-        )
+
+        def edge_fwd(e_fwd, h_fwd):
+            return call(
+                functools.partial(edge_kernel, step, 0),
+                [field_shape] * 2 + [halo_shape] * more,
+                [IN_VMEM] * (2 + more),
+                [e_fwd, h_fwd, coef, drives, forced] + arrived_fwd,
+                [IN_VMEM] * (5 + len(arrived_fwd)),
+                aliases={0: 0, 1: 1},
+            )
+
         if more:
-            arrived_fwd = trade(pays)
-        if step == 0:
-            coef = call(
-                functools.partial(coef_inner_kernel, first_slot, len(last)),
-                coef_shape,
-                IN_VMEM,
-                [coef] + last + [place, base, blocks],
-                [IN_VMEM] * (len(last) + 4),
-                [placed],
-                aliases={0: 0},
-                micros=0.9,
-            )
-            e_fwd, e_adj, total = call(
-                begin_kernel,
-                [field_shape, field_shape, total_shape],
-                [IN_VMEM] * 3,
-                [e_fwd, e_adj, total, coef, drives, forced, curls_fwd, curls_adj],
-                [IN_VMEM] * 8,
-                aliases={0: 0, 1: 1, 2: 2},
-                micros=0.7,
-            )
-        else:
+            e_fwd, h_fwd, *pays = edge_fwd(e_fwd, h_fwd)
+            arrived_fwd_next = trade(pays)
+        if step > 0:
             e_adj, h_adj, e_fwd, total = call(
                 functools.partial(inner_kernel, step, 1),
                 [field_shape] * 3 + [total_shape],
@@ -721,10 +750,9 @@
                 micros=1.2,
             )
         if not more:
-            parts = call(
+            inner = by_owner(
                 functools.partial(filter_inner_kernel, layout),
-                [on_chip(*group)] * len(layout),
-                [IN_VMEM] * len(layout),
+                depth - 2,
                 [total, block_ids],
                 [IN_VMEM, IN_HBM],
                 [
@@ -733,8 +761,9 @@
                     pltpu.SMEM(block_ids.shape, jnp.int32),
                     pltpu.SemaphoreType.DMA,
                 ],
-                micros=0.8,
+                0.8,
             )
+            e_fwd, h_fwd = edge_fwd(e_fwd, h_fwd)
         e_adj, h_adj, e_fwd, edges, *pays = call(
             functools.partial(edge_kernel, step, 1),
             [field_shape] * 3 + [edges_shape] + [halo_shape] * more,
@@ -743,45 +772,56 @@
             [IN_VMEM] * (5 + len(arrived_adj)),
             aliases={0: 0, 1: 1, 2: 2, 3: 3},
         )
-        if more:
-            arrived_adj = trade(pays)
-            e_fwd, h_fwd = call(
-                functools.partial(inner_kernel, step + 1, 0),
-                [field_shape] * 2,
-                [IN_VMEM] * 2,
-                [e_fwd, h_fwd, coef, drives, forced],
-                [IN_VMEM] * 5,
-                aliases={0: 0, 1: 1},
-                micros=1.1,
+        if not more:
+            break
+        arrived_fwd, arrived_adj = arrived_fwd_next, trade(pays)
+        if step == 0:
+            coef = call(
+                functools.partial(coef_inner_kernel, first_slot, len(last)),
+                coef_shape,
+                IN_VMEM,
+                [coef] + last + [place, base, blocks],
+                [IN_VMEM] * (len(last) + 4),
+                [placed],
+                aliases={0: 0},
+                micros=0.6,
             )
-
-    parts = call(
-        functools.partial(filter_edge_kernel, len(layout)),
-        [on_chip(*group)] * len(layout),
-        [IN_VMEM] * len(layout),
-        list(parts) + [total, edges, place],
-        [IN_VMEM] * (len(layout) + 3),
+            e_fwd, e_adj, total = call(
+                begin_kernel,
+                [field_shape, field_shape, total_shape],
+                [IN_VMEM] * 3,
+                [e_fwd, e_adj, total, coef, drives, forced, curls_fwd, curls_adj],
+                [IN_VMEM] * 8,
+                aliases={0: 0, 1: 1, 2: 2},
+                micros=0.5,
+            )
+        e_fwd, h_fwd = call(
+            functools.partial(inner_kernel, step + 1, 0),
+            [field_shape] * 2,
+            [IN_VMEM] * 2,
+            [e_fwd, h_fwd, coef, drives, forced],
+            [IN_VMEM] * 5,
+            aliases={0: 0, 1: 1},
+            micros=1.1,
+        )
+
+    ends = by_owner(
+        functools.partial(filter_edge_kernel, layout),
+        2,
+        [total, edges, place],
+        [IN_VMEM] * 3,
         [
             pltpu.VMEM((2, width_x + 2 * PAD, width_y), F32),
             pltpu.VMEM((2, width_x, width_y), F32),
         ],
-        aliases={slot: slot for slot in range(len(layout))},
-    )
-    got = [swap_over(part, "grp", 1) for part in parts[middle:]]
-    sums = call(
-        add_kernel,
-        [on_chip(*group)] * middle,
-        [IN_VMEM] * middle,
-        list(parts[:middle]) + got,
-        [IN_VMEM] * (2 * middle),
-    )
-    got = [swap_over(part, "grp", mask) for part, mask in zip(sums[1:], middle_masks[1:])]
+        0.3,
+    )
     pieces = call(
-        functools.partial(add_split_kernel, middle),
+        functools.partial(join_kernel, middle, block_rows),
         [on_chip(*piece)] * far,
         [IN_VMEM] * far,
-        [sums[0]] + got,
-        [IN_VMEM] * middle,
+        inner + ends,
+        [IN_VMEM] * (2 * middle),
     )
     got = [swap_over(part, "grp", mask) for part, mask in zip(pieces[1:], far_masks[1:])]
     scale = 3.0 / (STEPS * math.sqrt(ngrp))

time: 56.2 us -> 55.6 us (0.989)
    ppermute x19 -> x22, waiting for transfers between devices: 12.6 us -> 12.2 us  [swap_over(): lax.ppermute(array, axis, [(i, i ^ mask) for i in range(lax.axis_size(axi...]
    pallas_call x32 -> x31, Pallas kernels: 17.7 us -> 17.6 us  [call(): pl.pallas_call(kernel, out_shape=outs, in_specs=specs, out_specs=out_spec...]
    ppermute x19 -> x22, starting transfers between devices: 24 us -> 24 us  [swap_over(): lax.ppermute(array, axis, [(i, i ^ mask) for i in range(lax.axis_size(axi...]
  transfers between devices with their start and end apart: 19 -> 22, of which waited for: 10 -> 12; matrix products, arithmetic and copies ran while one was open for 0% -> 0% of each run, Pallas kernels for 29% -> 30%
where the time goes in v9:
time: 55.6 us; the launch traced here: 55.4 us
  starting transfers between devices  24 us (43%)
  Pallas kernels  17.6 us (32%)
  waiting for transfers between devices  12.2 us (22%)
  between operations  1.59 us (3%)
    ppermute x22, starting transfers between devices, swap_over(): lax.ppermute(array, axis, [(i, i ^ mask) for i in range(lax.axis_size(axi...  24 us
    pallas_call x31, Pallas kernels, call(): pl.pallas_call(kernel, out_shape=outs, in_specs=specs, out_specs=out_spec...  17.6 us
    ppermute x22, waiting for transfers between devices, swap_over(): lax.ppermute(array, axis, [(i, i ^ mask) for i in range(lax.axis_size(axi...  12.2 us
  transfers between devices with their start and end apart: 22, of which 12 were waited for; matrix products, arithmetic and copies ran while one was open for 0% of the time, Pallas kernels for 30%

profile of v9, /device:TPU:0, one launch (start us, length us, event | category | flops | bytes accessed | tf_op | source)
XLA Modules:
  0.0 55.4 jit_solution(16503893388006105362)
XLA Ops:
  0.6 5.1 %collective-permute-start.2 = (f32[64,128]{1,0:T(8,128)}, f32[64,128]{1,0:T(8,128)S(1)}, u32[]{:S(2)}, u32[]{:S(2)}) collective-permute-start(f32[64,128]{1,0:T(8,128)} %bitcast.2), channel_id=1, source_target_pairs={{0,24},{2,26},{4,28},{6,30},{8,16},{10,18},{12,20},{14,22},{16,8},... | collective-permute-start | bytes 98312 | tf_op jit(solution)/shard_map/ppermute | solution.py:585
  6.4 1.4 %shard_map.95 = (f32[64,128]{1,0:T(8,128)S(1)}, f32[2,2,128,128]{3,2,1,0:T(8,128)S(1)}) custom-call(f32[1,6,8,128,128]{4,3,2,1,0:T(8,128)} %given.3, f32[1,6,8,128,128]{4,3,2,1,0:T(8,128)} %given.2, f32[64,128]{1,0:T(8,128)} %bitcast.5), custom_call_target="tpu_custom_call" | custom-call | bytes 900000 | tf_op jit(solution)/shard_map/pallas_call | solution.py:36
  7.8 1.4 %collective-permute-start.3 = (f32[2,2,128,128]{3,2,1,0:T(8,128)S(1)}, f32[2,2,128,128]{3,2,1,0:T(8,128)S(1)}, u32[]{:S(2)}, u32[]{:S(2)}) collective-permute-start(f32[2,2,128,128]{3,2,1,0:T(8,128)S(1)} %get-tuple-element.93), channel_id=1, source_target_pairs={{0,1},{1,0},{2,3},{3,2},{4,5},{5,4},{6,7},{7,6},{8,9},{9,8},{10,11... | collective-permute-start | bytes 786440 | tf_op jit(solution)/shard_map/ppermute | solution.py:585
  9.2 1.5 %collective-permute-done.1.refs_2_ = f32[64,128]{1,0:T(8,128)S(1)} collective-permute-done((f32[64,128]{1,0:T(8,128)}, f32[64,128]{1,0:T(8,128)S(1)}, u32[]{:S(2)}, u32[]{:S(2)}) %collective-permute-start.1) | collective-permute-done | bytes 32800 | tf_op jit(solution)/shard_map/ppermute | solution.py:585
  10.8 1.6 %collective-permute-start.4 = (f32[4,64,128]{2,1,0:T(8,128)S(1)}, f32[4,64,128]{2,1,0:T(8,128)S(1)}, u32[]{:S(2)}, u32[]{:S(2)}) collective-permute-start(f32[4,64,128]{2,1,0:T(8,128)S(1)} %shard_map.96.near.refs_8_), channel_id=1, source_target_pairs={{0,4},{2,6},{4,0},{6,2},{8,12},{10,14},{12,8},{14,10},{16,20},{18,... | collective-permute-start | bytes 393224 | tf_op jit(solution)/shard_map/ppermute | solution.py:585
  13.0 0.8 %shard_map.99 = (f32[8,144,128]{2,1,0:T(8,128)S(1)}, f32[2,144,128]{2,1,0:T(8,128)S(1)}, f32[8,128,128]{2,1,0:T(8,128)S(1)}, f32[4,128]{1,0:T(4,128)S(1)}, f32[1...) custom-call(s32[1]{0:T(128)S(6)} %copy.112.wave_idx, s32[1,3]{1,0:T(1,128)} %source_far.1, s32[16]{0:T(128)} %block_ids_far.1, ...), custom_call_target="tpu_custom_call" | custom-call | bytes 900000 | tf_op jit(solution)/shard_map/pallas_call | solution.py:36
  13.9 1.2 %shard_map.98 = (f32[3,9,144,128]{3,2,1,0:T(8,128)S(1)}, f32[3,9,144,128]{3,2,1,0:T(8,128)S(1)}, f32[3,8,128,128]{3,2,1,0:T(8,128)S(1)}) custom-call(f32[1,6,8,128,128]{4,3,2,1,0:T(8,128)S(1)} %copy-done, f32[4,64,128]{2,1,0:T(8,128)S(1)} %shard_map.96.near.refs_8_), custom_call_target="tpu_custom_call" | custom-call | bytes 4500000 | tf_op jit(solution)/shard_map/pallas_call | solution.py:36
  15.1 1.2 %shard_map.97 = (f32[3,9,144,128]{3,2,1,0:T(8,128)S(1)}, f32[3,9,144,128]{3,2,1,0:T(8,128)S(1)}, f32[3,8,128,128]{3,2,1,0:T(8,128)S(1)}) custom-call(f32[1,6,8,128,128]{4,3,2,1,0:T(8,128)S(1)} %copy-done.1, f32[4,64,128]{2,1,0:T(8,128)S(1)} %shard_map.96.near.refs_8_), custom_call_target="tpu_custom_call" | custom-call | bytes 4500000 | tf_op jit(solution)/shard_map/pallas_call | solution.py:36
  16.8 0.7 %shard_map.101 = (f32[3,9,144,128]{3,2,1,0:T(8,128)S(1)}, f32[3,8,128,128]{3,2,1,0:T(8,128)S(1)}, f32[3,9,144,128]{3,2,1,0:T(8,128)S(1)}, f32[3,8,128,128]{3,2,1,0:T(8,128)S(1)}, f32[16,64,128]{2,1,0:T(8,128)S(1)}) custom-call(f32[3,9,144,128]{3,2,1,0:T(8,128)S(1)} %get-tuple-element.88.refs_, ...), custom_call_target="tpu_custom_call", output_to_operand_aliasing={{0}: (0, {}), {1}: (1, {}), {2}: (2, {}), {3}: (3, {})} | custom-call | bytes 1800000 | tf_op jit(solution)/shard_map/pallas_call | solution.py:36
  18.1 1.5 %collective-permute-start.7 = (f32[2,128,128]{2,1,0:T(8,128)S(1)}, f32[2,128,128]{2,1,0:T(8,128)S(1)}, u32[]{:S(2)}, u32[]{:S(2)}) collective-permute-start(f32[2,128,128]{2,1,0:T(8,128)S(1)} %get-tuple-element.114), channel_id=1, source_target_pairs={{0,1},{1,0},{2,3},{3,2},{4,5},{5,4},{6,7},{7,6},{8,9},{9,8},{10,11... | collective-permute-start | bytes 393224 | tf_op jit(solution)/shard_map/ppermute | solution.py:585
  21.5 0.9 %shard_map.107 = (f32[3,9,144,128]{3,2,1,0:T(8,128)S(1)}, f32[3,9,144,128]{3,2,1,0:T(8,128)S(1)}) custom-call(f32[3,9,144,128]{3,2,1,0:T(8,128)S(1)} %get-tuple-element.110.refs_0_, f32[3,9,144,128]{3,2,1,0:T(8,128)S(1)} %get-tuple-element.111.refs_1_, ...), custom_call_target="tpu_custom_call", output_to_operand_aliasing={{0}: (0, {}), {1}: (1, {})} | custom-call | bytes 3300000 | tf_op jit(solution)/shard_map/pallas_call | solution.py:36
  22.5 2.1 %collective-permute-done.7.refs_5_.refs_6_ = f32[2,128,128]{2,1,0:T(8,128)S(1)} collective-permute-done((f32[2,128,128]{2,1,0:T(8,128)S(1)}, f32[2,128,128]{2,1,0:T(8,128)S(1)}, u32[]{:S(2)}, u32[]{:S(2)}) %collective-permute-start.7) | collective-permute-done | bytes 131104 | tf_op jit(solution)/shard_map/ppermute | solution.py:585
  24.8 1.4 %collective-permute-start.9 = (f32[2,128,128]{2,1,0:T(8,128)S(1)}, f32[2,128,128]{2,1,0:T(8,128)S(1)}, u32[]{:S(2)}, u32[]{:S(2)}) collective-permute-start(f32[2,128,128]{2,1,0:T(8,128)S(1)} %get-tuple-element.128), channel_id=1, source_target_pairs={{0,1},{1,0},{2,3},{3,2},{4,5},{5,4},{6,7},{7,6},{8,9},{9,8},{10,11... | collective-permute-start | bytes 393224 | tf_op jit(solution)/shard_map/ppermute | solution.py:585
  26.2 1.2 %shard_map.109 = (f32[3,9,144,128]{3,2,1,0:T(8,128)S(1)}, f32[3,9,144,128]{3,2,1,0:T(8,128)S(1)}, f32[3,9,144,128]{3,2,1,0:T(8,128)S(1)}, f32[8,144,128]{2,1,0:T(8,128)S(1)}) custom-call(f32[3,9,144,128]{3,2,1,0:T(8,128)S(1)} %get-tuple-element.108.refs_0_, ...), custom_call_target="tpu_custom_call", output_to_operand_aliasing={{0}: (0, {}), {1}: (1, {}), {2}: (2, {}), {3}: (3, {})} | custom-call | bytes 3600000 | tf_op jit(solution)/shard_map/pallas_call | solution.py:36
  27.6 1.3 %collective-permute-start.10 = (f32[2,128,128]{2,1,0:T(8,128)S(1)}, f32[2,128,128]{2,1,0:T(8,128)S(1)}, u32[]{:S(2)}, u32[]{:S(2)}) collective-permute-start(f32[2,128,128]{2,1,0:T(8,128)S(1)} %get-tuple-element.135), channel_id=1, source_target_pairs={{0,1},{1,0},{2,3},{3,2},{4,5},{5,4},{6,7},{7,6},{8,9},{9,8},{10,11... | collective-permute-start | bytes 393224 | tf_op jit(solution)/shard_map/ppermute | solution.py:585
  28.8 0.9 %shard_map.111 = (f32[3,9,144,128]{3,2,1,0:T(8,128)S(1)}, f32[3,9,144,128]{3,2,1,0:T(8,128)S(1)}) custom-call(f32[3,9,144,128]{3,2,1,0:T(8,128)S(1)} %get-tuple-element.124.refs_0_, f32[3,9,144,128]{3,2,1,0:T(8,128)S(1)} %get-tuple-element.125.refs_1_, ...), custom_call_target="tpu_custom_call", output_to_operand_aliasing={{0}: (0, {}), {1}: (1, {})} | custom-call | bytes 3300000 | tf_op jit(solution)/shard_map/pallas_call | solution.py:36
  30.6 1.2 %shard_map.113 = (f32[3,9,144,128]{3,2,1,0:T(8,128)S(1)}, f32[3,9,144,128]{3,2,1,0:T(8,128)S(1)}, f32[3,9,144,128]{3,2,1,0:T(8,128)S(1)}, f32[8,144,128]{2,1,0:T(8,128)S(1)}) custom-call(f32[3,9,144,128]{3,2,1,0:T(8,128)S(1)} %get-tuple-element.122.refs_0_, ...), custom_call_target="tpu_custom_call", output_to_operand_aliasing={{0}: (0, {}), {1}: (1, {}), {2}: (2, {}), {3}: (3, {})} | custom-call | bytes 3600000 | tf_op jit(solution)/shard_map/pallas_call | solution.py:36
  31.7 0.9 %collective-permute-done.10.refs_5_.refs_6_ = f32[2,128,128]{2,1,0:T(8,128)S(1)} collective-permute-done((f32[2,128,128]{2,1,0:T(8,128)S(1)}, f32[2,128,128]{2,1,0:T(8,128)S(1)}, u32[]{:S(2)}, u32[]{:S(2)}) %collective-permute-start.10) | collective-permute-done | bytes 131104 | tf_op jit(solution)/shard_map/ppermute | solution.py:585
  32.9 1.3 %collective-permute-start.12 = (f32[2,128,128]{2,1,0:T(8,128)S(1)}, f32[2,128,128]{2,1,0:T(8,128)S(1)}, u32[]{:S(2)}, u32[]{:S(2)}) collective-permute-start(f32[2,128,128]{2,1,0:T(8,128)S(1)} %get-tuple-element.149), channel_id=1, source_target_pairs={{0,1},{1,0},{2,3},{3,2},{4,5},{5,4},{6,7},{7,6},{8,9},{9,8},{10,11... | collective-permute-start | bytes 393224 | tf_op jit(solution)/shard_map/ppermute | solution.py:585
  34.1 0.8 %collective-permute-start.11 = (f32[2,128,128]{2,1,0:T(8,128)S(1)}, f32[2,128,128]{2,1,0:T(8,128)S(1)}, u32[]{:S(2)}, u32[]{:S(2)}) collective-permute-start(f32[2,128,128]{2,1,0:T(8,128)S(1)} %get-tuple-element.146), channel_id=1, source_target_pairs={{0,1},{1,0},{2,3},{3,2},{4,5},{5,4},{6,7},{7,6},{8,9},{9,8},{10,11... | collective-permute-start | bytes 393224 | tf_op jit(solution)/shard_map/ppermute | solution.py:585
  34.9 0.9 %shard_map.115 = (f32[3,9,144,128]{3,2,1,0:T(8,128)S(1)}, f32[3,9,144,128]{3,2,1,0:T(8,128)S(1)}) custom-call(f32[3,9,144,128]{3,2,1,0:T(8,128)S(1)} %get-tuple-element.138.refs_0_, f32[3,9,144,128]{3,2,1,0:T(8,128)S(1)} %get-tuple-element.139.refs_1_, ...), custom_call_target="tpu_custom_call", output_to_operand_aliasing={{0}: (0, {}), {1}: (1, {})} | custom-call | bytes 3300000 | tf_op jit(solution)/shard_map/pallas_call | solution.py:36
  35.9 1.2 %shard_map.116 = (f32[3,9,144,128]{3,2,1,0:T(8,128)S(1)}, f32[3,9,144,128]{3,2,1,0:T(8,128)S(1)}, f32[3,9,144,128]{3,2,1,0:T(8,128)S(1)}, f32[8,144,128]{2,1,0:T(8,128)S(1)}) custom-call(f32[3,9,144,128]{3,2,1,0:T(8,128)S(1)} %get-tuple-element.136.refs_0_, ...), custom_call_target="tpu_custom_call", output_to_operand_aliasing={{0}: (0, {}), {1}: (1, {}), {2}: (2, {}), {3}: (3, {})} | custom-call | bytes 3600000 | tf_op jit(solution)/shard_map/pallas_call | solution.py:36
  37.1 0.7 %shard_map.120 = (f32[4,48,128]{2,1,0:T(8,128)S(1)}, f32[4,48,128]{2,1,0:T(8,128)S(1)}, f32[4,48,128]{2,1,0:T(8,128)S(1)}, f32[4,48,128]{2,1,0:T(8,128)S(1)}) custom-call(f32[8,144,128]{2,1,0:T(8,128)S(1)} %get-tuple-element.152.total, s32[16]{0:T(128)} %block_ids_far.1), custom_call_target="tpu_custom_call" | custom-call | bytes 2400000 | tf_op jit(solution)/shard_map/pallas_call | solution.py:36
  38.3 0.8 %collective-permute-done.13.refs_2_ = f32[4,48,128]{2,1,0:T(8,128)S(1)} collective-permute-done((f32[4,48,128]{2,1,0:T(8,128)S(1)}, f32[4,48,128]{2,1,0:T(8,128)S(1)}, u32[]{:S(2)}, u32[]{:S(2)}) %collective-permute-start.13) | collective-permute-done | bytes 98336 | tf_op jit(solution)/shard_map/ppermute | solution.py:585
  39.3 0.9 %collective-permute-start.15 = (f32[4,48,128]{2,1,0:T(8,128)S(1)}, f32[4,48,128]{2,1,0:T(8,128)S(1)}, u32[]{:S(2)}, u32[]{:S(2)}) collective-permute-start(f32[4,48,128]{2,1,0:T(8,128)S(1)} %get-tuple-element.158), channel_id=1, source_target_pairs={{0,4},{2,6},{4,0},{6,2},{8,12},{10,14},{12,8},{14,10},{16,20},{18,... | collective-permute-start | bytes 294920 | tf_op jit(solution)/shard_map/ppermute | solution.py:585
  42.3 1.2 %collective-permute-start.18 = (f32[4,16,128]{2,1,0:T(8,128)S(1)}, f32[4,16,128]{2,1,0:T(8,128)S(1)}, u32[]{:S(2)}, u32[]{:S(2)}) collective-permute-start(f32[4,16,128]{2,1,0:T(8,128)S(1)} %get-tuple-element.165), channel_id=1, source_target_pairs={{0,4},{2,6},{4,0},{6,2},{8,12},{10,14},{12,8},{14,10},{16,20},{18,... | collective-permute-start | bytes 98312 | tf_op jit(solution)/shard_map/ppermute | solution.py:585
  43.5 0.9 %collective-permute-done.15.refs_1_ = f32[4,48,128]{2,1,0:T(8,128)S(1)} collective-permute-done((f32[4,48,128]{2,1,0:T(8,128)S(1)}, f32[4,48,128]{2,1,0:T(8,128)S(1)}, u32[]{:S(2)}, u32[]{:S(2)}) %collective-permute-start.15) | collective-permute-done | bytes 98336 | tf_op jit(solution)/shard_map/ppermute | solution.py:585
  44.4 1.8 %collective-permute-done.18.refs_3_ = f32[4,16,128]{2,1,0:T(8,128)S(1)} collective-permute-done((f32[4,16,128]{2,1,0:T(8,128)S(1)}, f32[4,16,128]{2,1,0:T(8,128)S(1)}, u32[]{:S(2)}, u32[]{:S(2)}) %collective-permute-start.18) | collective-permute-done | bytes 32800 | tf_op jit(solution)/shard_map/ppermute | solution.py:585
  46.4 2.6 %collective-permute-start.20 = (f32[64,128]{1,0:T(8,128)S(1)}, f32[64,128]{1,0:T(8,128)S(1)}, u32[]{:S(2)}, u32[]{:S(2)}) collective-permute-start(f32[64,128]{1,0:T(8,128)S(1)} %get-tuple-element.168), channel_id=1, source_target_pairs={{0,16},{2,18},{4,20},{6,22},{8,24},{10,26},{12,28},{14,30},{16,0},... | collective-permute-start | bytes 98312 | tf_op jit(solution)/shard_map/ppermute | solution.py:585
  49.1 1.7 %collective-permute-start.21 = (f32[64,128]{1,0:T(8,128)S(1)}, f32[64,128]{1,0:T(8,128)S(1)}, u32[]{:S(2)}, u32[]{:S(2)}) collective-permute-start(f32[64,128]{1,0:T(8,128)S(1)} %get-tuple-element.169), channel_id=1, source_target_pairs={{0,24},{2,26},{4,28},{6,30},{8,16},{10,18},{12,20},{14,22},{16,8},... | collective-permute-start | bytes 98312 | tf_op jit(solution)/shard_map/ppermute | solution.py:585
  50.7 1.7 %shard_map.119 = f32[1,6,8,128,128]{4,3,2,1,0:T(8,128)} custom-call(f32[3,9,144,128]{3,2,1,0:T(8,128)S(1)} %get-tuple-element.150.e, f32[3,9,144,128]{3,2,1,0:T(8,128)S(1)} %get-tuple-element.151.h), custom_call_target="tpu_custom_call" | custom-call | bytes 5100000 | tf_op jit(solution)/shard_map/pallas_call | solution.py:36
  52.5 2.3 %collective-permute-done.21.refs_3_ = f32[64,128]{1,0:T(8,128)S(1)} collective-permute-done((f32[64,128]{1,0:T(8,128)S(1)}, f32[64,128]{1,0:T(8,128)S(1)}, u32[]{:S(2)}, u32[]{:S(2)}) %collective-permute-start.21) | collective-permute-done | bytes 32800 | tf_op jit(solution)/shard_map/ppermute | solution.py:585
  (47 shorter events, 8.7 us)
Async XLA Ops:
  0.6 13.3 %copy-start = (f32[1,6,8,128,128]{4,3,2,1,0:T(8,128)S(1)}, f32[1,6,8,128,128]{4,3,2,1,0:T(8,128)}, u32[]{:S(2)}) copy-start(f32[1,6,8,128,128]{4,3,2,1,0:T(8,128)} %given.3) | copy-start | bytes 9437188
  0.6 8.6 %collective-permute-start.2 = (f32[64,128]{1,0:T(8,128)}, f32[64,128]{1,0:T(8,128)S(1)}, u32[]{:S(2)}, u32[]{:S(2)}) collective-permute-start(f32[64,128]{1,0:T(8,128)} %bitcast.2), channel_id=1, source_target_pairs={{0,24},{2,26},{4,28},{6,30},{8,16},{10,18},{12,20},{14,22},{16,8},... | collective-permute-start | bytes 98312 | tf_op jit(solution)/shard_map/ppermute | solution.py:585
  5.8 5.0 %collective-permute-start.1 = (f32[64,128]{1,0:T(8,128)}, f32[64,128]{1,0:T(8,128)S(1)}, u32[]{:S(2)}, u32[]{:S(2)}) collective-permute-start(f32[64,128]{1,0:T(8,128)} %bitcast.3), channel_id=1, source_target_pairs={{0,16},{2,18},{4,20},{6,22},{8,24},{10,26},{12,28},{14,30},{16,0},... | collective-permute-start | bytes 98312 | tf_op jit(solution)/shard_map/ppermute | solution.py:585
  5.8 5.0 %collective-permute-start = (f32[64,128]{1,0:T(8,128)}, f32[64,128]{1,0:T(8,128)S(1)}, u32[]{:S(2)}, u32[]{:S(2)}) collective-permute-start(f32[64,128]{1,0:T(8,128)} %bitcast.4), channel_id=1, source_target_pairs={{0,8},{2,10},{4,12},{6,14},{8,0},{10,2},{12,4},{14,6},{16,24},{18,... | collective-permute-start | bytes 98312 | tf_op jit(solution)/shard_map/ppermute | solution.py:585
  7.8 7.3 %copy-start.1 = (f32[1,6,8,128,128]{4,3,2,1,0:T(8,128)S(1)}, f32[1,6,8,128,128]{4,3,2,1,0:T(8,128)}, u32[]{:S(2)}) copy-start(f32[1,6,8,128,128]{4,3,2,1,0:T(8,128)} %given.2) | copy-start | bytes 9437188
  7.8 9.0 %collective-permute-start.3 = (f32[2,2,128,128]{3,2,1,0:T(8,128)S(1)}, f32[2,2,128,128]{3,2,1,0:T(8,128)S(1)}, u32[]{:S(2)}, u32[]{:S(2)}) collective-permute-start(f32[2,2,128,128]{3,2,1,0:T(8,128)S(1)} %get-tuple-element.93), channel_id=1, source_target_pairs={{0,1},{1,0},{2,3},{3,2},{4,5},{5,4},{6,7},{7,6},{8,9},{9,8},{10,11... | collective-permute-start | bytes 786440 | tf_op jit(solution)/shard_map/ppermute | solution.py:585
  10.8 5.5 %collective-permute-start.4 = (f32[4,64,128]{2,1,0:T(8,128)S(1)}, f32[4,64,128]{2,1,0:T(8,128)S(1)}, u32[]{:S(2)}, u32[]{:S(2)}) collective-permute-start(f32[4,64,128]{2,1,0:T(8,128)S(1)} %shard_map.96.near.refs_8_), channel_id=1, source_target_pairs={{0,4},{2,6},{4,0},{6,2},{8,12},{10,14},{12,8},{14,10},{16,20},{18,... | collective-permute-start | bytes 393224 | tf_op jit(solution)/shard_map/ppermute | solution.py:585
  13.8 3.0 %collective-permute-start.5 = (f32[4,64,128]{2,1,0:T(8,128)S(1)}, f32[4,64,128]{2,1,0:T(8,128)S(1)}, u32[]{:S(2)}, u32[]{:S(2)}) collective-permute-start(f32[4,64,128]{2,1,0:T(8,128)S(1)} %shard_map.96.near.refs_8_), channel_id=1, source_target_pairs={{0,2},{2,0},{4,6},{6,4},{8,10},{10,8},{12,14},{14,12},{16,18},{18,... | collective-permute-start | bytes 393224 | tf_op jit(solution)/shard_map/ppermute | solution.py:585
  16.3 1.5 %collective-permute-start.6 = (f32[4,64,128]{2,1,0:T(8,128)S(1)}, f32[4,64,128]{2,1,0:T(8,128)S(1)}, u32[]{:S(2)}, u32[]{:S(2)}) collective-permute-start(f32[4,64,128]{2,1,0:T(8,128)S(1)} %shard_map.100.refs_9_), channel_id=1, source_target_pairs={{0,2},{2,0},{4,6},{6,4},{8,10},{10,8},{12,14},{14,12},{16,18},{18,... | collective-permute-start | bytes 393224 | tf_op jit(solution)/shard_map/ppermute | solution.py:585
  18.1 6.4 %collective-permute-start.7 = (f32[2,128,128]{2,1,0:T(8,128)S(1)}, f32[2,128,128]{2,1,0:T(8,128)S(1)}, u32[]{:S(2)}, u32[]{:S(2)}) collective-permute-start(f32[2,128,128]{2,1,0:T(8,128)S(1)} %get-tuple-element.114), channel_id=1, source_target_pairs={{0,1},{1,0},{2,3},{3,2},{4,5},{5,4},{6,7},{7,6},{8,9},{9,8},{10,11... | collective-permute-start | bytes 393224 | tf_op jit(solution)/shard_map/ppermute | solution.py:585
  19.8 7.5 %collective-permute-start.8 = (f32[2,128,128]{2,1,0:T(8,128)S(1)}, f32[2,128,128]{2,1,0:T(8,128)S(1)}, u32[]{:S(2)}, u32[]{:S(2)}) collective-permute-start(f32[2,128,128]{2,1,0:T(8,128)S(1)} %get-tuple-element.121), channel_id=1, source_target_pairs={{0,1},{1,0},{2,3},{3,2},{4,5},{5,4},{6,7},{7,6},{8,9},{9,8},{10,11... | collective-permute-start | bytes 393224 | tf_op jit(solution)/shard_map/ppermute | solution.py:585
  24.8 5.6 %collective-permute-start.9 = (f32[2,128,128]{2,1,0:T(8,128)S(1)}, f32[2,128,128]{2,1,0:T(8,128)S(1)}, u32[]{:S(2)}, u32[]{:S(2)}) collective-permute-start(f32[2,128,128]{2,1,0:T(8,128)S(1)} %get-tuple-element.128), channel_id=1, source_target_pairs={{0,1},{1,0},{2,3},{3,2},{4,5},{5,4},{6,7},{7,6},{8,9},{9,8},{10,11... | collective-permute-start | bytes 393224 | tf_op jit(solution)/shard_map/ppermute | solution.py:585
  27.6 5.0 %collective-permute-start.10 = (f32[2,128,128]{2,1,0:T(8,128)S(1)}, f32[2,128,128]{2,1,0:T(8,128)S(1)}, u32[]{:S(2)}, u32[]{:S(2)}) collective-permute-start(f32[2,128,128]{2,1,0:T(8,128)S(1)} %get-tuple-element.135), channel_id=1, source_target_pairs={{0,1},{1,0},{2,3},{3,2},{4,5},{5,4},{6,7},{7,6},{8,9},{9,8},{10,11... | collective-permute-start | bytes 393224 | tf_op jit(solution)/shard_map/ppermute | solution.py:585
  32.9 7.5 %collective-permute-start.12 = (f32[2,128,128]{2,1,0:T(8,128)S(1)}, f32[2,128,128]{2,1,0:T(8,128)S(1)}, u32[]{:S(2)}, u32[]{:S(2)}) collective-permute-start(f32[2,128,128]{2,1,0:T(8,128)S(1)} %get-tuple-element.149), channel_id=1, source_target_pairs={{0,1},{1,0},{2,3},{3,2},{4,5},{5,4},{6,7},{7,6},{8,9},{9,8},{10,11... | collective-permute-start | bytes 393224 | tf_op jit(solution)/shard_map/ppermute | solution.py:585
  34.1 6.1 %collective-permute-start.11 = (f32[2,128,128]{2,1,0:T(8,128)S(1)}, f32[2,128,128]{2,1,0:T(8,128)S(1)}, u32[]{:S(2)}, u32[]{:S(2)}) collective-permute-start(f32[2,128,128]{2,1,0:T(8,128)S(1)} %get-tuple-element.146), channel_id=1, source_target_pairs={{0,1},{1,0},{2,3},{3,2},{4,5},{5,4},{6,7},{7,6},{8,9},{9,8},{10,11... | collective-permute-start | bytes 393224 | tf_op jit(solution)/shard_map/ppermute | solution.py:585
  37.8 1.4 %collective-permute-start.13 = (f32[4,48,128]{2,1,0:T(8,128)S(1)}, f32[4,48,128]{2,1,0:T(8,128)S(1)}, u32[]{:S(2)}, u32[]{:S(2)}) collective-permute-start(f32[4,48,128]{2,1,0:T(8,128)S(1)} %get-tuple-element.155), channel_id=1, source_target_pairs={{0,2},{2,0},{4,6},{6,4},{8,10},{10,8},{12,14},{14,12},{16,18},{18,... | collective-permute-start | bytes 294920 | tf_op jit(solution)/shard_map/ppermute | solution.py:585
  37.9 1.4 %collective-permute-start.14 = (f32[4,48,128]{2,1,0:T(8,128)S(1)}, f32[4,48,128]{2,1,0:T(8,128)S(1)}, u32[]{:S(2)}, u32[]{:S(2)}) collective-permute-start(f32[4,48,128]{2,1,0:T(8,128)S(1)} %get-tuple-element.156), channel_id=1, source_target_pairs={{0,2},{2,0},{4,6},{6,4},{8,10},{10,8},{12,14},{14,12},{16,18},{18,... | collective-permute-start | bytes 294920 | tf_op jit(solution)/shard_map/ppermute | solution.py:585
  39.3 5.1 %collective-permute-start.15 = (f32[4,48,128]{2,1,0:T(8,128)S(1)}, f32[4,48,128]{2,1,0:T(8,128)S(1)}, u32[]{:S(2)}, u32[]{:S(2)}) collective-permute-start(f32[4,48,128]{2,1,0:T(8,128)S(1)} %get-tuple-element.158), channel_id=1, source_target_pairs={{0,4},{2,6},{4,0},{6,2},{8,12},{10,14},{12,8},{14,10},{16,20},{18,... | collective-permute-start | bytes 294920 | tf_op jit(solution)/shard_map/ppermute | solution.py:585
  40.8 1.3 %collective-permute-start.16 = (f32[4,16,128]{2,1,0:T(8,128)S(1)}, f32[4,16,128]{2,1,0:T(8,128)S(1)}, u32[]{:S(2)}, u32[]{:S(2)}) collective-permute-start(f32[4,16,128]{2,1,0:T(8,128)S(1)} %get-tuple-element.162), channel_id=1, source_target_pairs={{0,2},{2,0},{4,6},{6,4},{8,10},{10,8},{12,14},{14,12},{16,18},{18,... | collective-permute-start | bytes 98312 | tf_op jit(solution)/shard_map/ppermute | solution.py:585
  40.9 1.3 %collective-permute-start.17 = (f32[4,16,128]{2,1,0:T(8,128)S(1)}, f32[4,16,128]{2,1,0:T(8,128)S(1)}, u32[]{:S(2)}, u32[]{:S(2)}) collective-permute-start(f32[4,16,128]{2,1,0:T(8,128)S(1)} %get-tuple-element.163), channel_id=1, source_target_pairs={{0,2},{2,0},{4,6},{6,4},{8,10},{10,8},{12,14},{14,12},{16,18},{18,... | collective-permute-start | bytes 98312 | tf_op jit(solution)/shard_map/ppermute | solution.py:585
  42.3 4.0 %collective-permute-start.18 = (f32[4,16,128]{2,1,0:T(8,128)S(1)}, f32[4,16,128]{2,1,0:T(8,128)S(1)}, u32[]{:S(2)}, u32[]{:S(2)}) collective-permute-start(f32[4,16,128]{2,1,0:T(8,128)S(1)} %get-tuple-element.165), channel_id=1, source_target_pairs={{0,4},{2,6},{4,0},{6,2},{8,12},{10,14},{12,8},{14,10},{16,20},{18,... | collective-permute-start | bytes 98312 | tf_op jit(solution)/shard_map/ppermute | solution.py:585
  46.3 6.2 %collective-permute-start.19 = (f32[64,128]{1,0:T(8,128)S(1)}, f32[64,128]{1,0:T(8,128)S(1)}, u32[]{:S(2)}, u32[]{:S(2)}) collective-permute-start(f32[64,128]{1,0:T(8,128)S(1)} %get-tuple-element.167), channel_id=1, source_target_pairs={{0,8},{2,10},{4,12},{6,14},{8,0},{10,2},{12,4},{14,6},{16,24},{18,... | collective-permute-start | bytes 98312 | tf_op jit(solution)/shard_map/ppermute | solution.py:585
  46.4 6.0 %collective-permute-start.20 = (f32[64,128]{1,0:T(8,128)S(1)}, f32[64,128]{1,0:T(8,128)S(1)}, u32[]{:S(2)}, u32[]{:S(2)}) collective-permute-start(f32[64,128]{1,0:T(8,128)S(1)} %get-tuple-element.168), channel_id=1, source_target_pairs={{0,16},{2,18},{4,20},{6,22},{8,24},{10,26},{12,28},{14,30},{16,0},... | collective-permute-start | bytes 98312 | tf_op jit(solution)/shard_map/ppermute | solution.py:585
  49.1 5.7 %collective-permute-start.21 = (f32[64,128]{1,0:T(8,128)S(1)}, f32[64,128]{1,0:T(8,128)S(1)}, u32[]{:S(2)}, u32[]{:S(2)}) collective-permute-start(f32[64,128]{1,0:T(8,128)S(1)} %get-tuple-element.169), channel_id=1, source_target_pairs={{0,24},{2,26},{4,28},{6,30},{8,16},{10,18},{12,20},{14,22},{16,8},... | collective-permute-start | bytes 98312 | tf_op jit(solution)/shard_map/ppermute | solution.py:585

commit v10 on v9

--- a/solution.py
+++ b/solution.py
@@ -12,7 +12,7 @@
 AMPLITUDE = 4.0
 PAD = 8
 F32 = jnp.float32
-HBM_PER_MICRO = 3.0e6
+HBM_PER_MICRO = 1.0e5
 
 VMEM = pltpu.MemorySpace.VMEM
 IN_VMEM = pl.BlockSpec(memory_space=pltpu.VMEM)
@@ -165,13 +165,16 @@
     return lambda layer, here: drives[pl.ds(step, 1), :] * forced[layer, here, :]
 
 
-def opening_kernel(fwd, adj, density, own, *rest):
+def opening_kernel(fwd, adj, density, wave_idx, own, drives, *rest):
     pays, (planes, sems) = rest[:-2], rest[-2:]
     depth, rows, width_y = fwd.shape[2:]
     top = depth - 1
     has_up, has_low = neighbours()
     held_copy = pltpu.make_async_copy(density, own, sems.at[2, 0])
     held_copy.start()
+    step = lax.broadcasted_iota(jnp.int32, drives.shape, 0).astype(F32) + 1.0
+    wave = jnp.full(drives.shape, wave_idx[0], jnp.int32).astype(F32)
+    drives[...] = AMPLITUDE * jnp.sin(2.0 * math.pi / (6.0 + 2.0 * wave) * step)
 
     def up(pay):
         copies = []
@@ -217,15 +220,14 @@
     held_copy.wait()
 
 
-def prepare_kernel(
-    layout, wave_idx, source_far, ids_far, idx_far, eps_far,
-    total, edges, forced, drives, base, place,
+def first_fwd_kernel(
+    layout, given, near, source_far, ids_far, idx_far, eps_far,
+    e, h, curls, total, edges, forced, base, place,
     source, block_ids, material_idx, material_eps, sems,
 ):
-    depth, rows, width_y = forced.shape
     fetches = [
-        pltpu.make_async_copy(far, near, sems.at[slot])
-        for slot, (far, near) in enumerate(
+        pltpu.make_async_copy(far, here, sems.at[slot])
+        for slot, (far, here) in enumerate(
             (
                 (source_far, source),
                 (ids_far, block_ids),
@@ -236,6 +238,8 @@
     ]
     for fetch in fetches:
         fetch.start()
+    first_kernel(given, near, e, h, curls)
+    depth, rows, width_y = forced.shape
     nblock = block_ids.shape[0]
     block_rows = rows // nblock
     empty = jnp.zeros(total.shape[1:], F32)
@@ -250,9 +254,6 @@
     offset_x = (xcoord - source[0, 1]).astype(F32) / (rows / 4.0)
     offset_y = (ycoord - source[0, 2]).astype(F32) / (width_y / 4.0)
     profile = jnp.exp(-0.5 * (offset_x * offset_x + offset_y * offset_y))
-    step = lax.broadcasted_iota(jnp.int32, drives.shape, 0).astype(F32) + 1.0
-    wave = jnp.full(drives.shape, wave_idx[0], jnp.int32).astype(F32)
-    drives[...] = AMPLITUDE * jnp.sin(2.0 * math.pi / (6.0 + 2.0 * wave) * step)
     level = source[0, 0] - lax.axis_index("slab") * depth
     for layer in range(depth):
         forced[layer] = jnp.where(level == layer, 1.0, 0.0) * profile
@@ -482,7 +483,7 @@
         out[slot] = ref[...]
 
 
-def filter_inner_kernel(layout, total, block_ids_far, *rest):
+def filter_inner_kernel(layout, total, after, block_ids_far, *rest):
     parts, (blocks, wide, block_ids, sem) = rest[:-4], rest[-4:]
     fetch = pltpu.make_async_copy(block_ids_far, block_ids, sem)
     fetch.start()
@@ -649,12 +650,12 @@
 
     design = density.reshape(piece)
     got = [swap_over(design, "grp", mask) for mask in far_masks[1:]]
-    own, *pays = call(
+    own, drives, *pays = call(
         opening_kernel,
-        [on_chip(*piece)] + [on_chip(2, 2, width_x, width_y)] * npay,
-        [IN_VMEM] * (1 + npay),
-        [fwd_fields, adj_fields, design],
-        [IN_HBM] * 3,
+        [on_chip(*piece), on_chip(STEPS, width_y)] + [on_chip(2, 2, width_x, width_y)] * npay,
+        [IN_VMEM] * (2 + npay),
+        [fwd_fields, adj_fields, design, wave_idx],
+        [IN_HBM] * 3 + [IN_SMEM],
         [pltpu.VMEM((2, 5, width_x, width_y), F32), pltpu.SemaphoreType.DMA((3, 5))],
     )
     below, above = trade(pays)
@@ -663,20 +664,21 @@
     others = [swap_over(near, "grp", mask) for mask in middle_masks[1:]]
     near_across = swap_over(near, "grp", 1)
 
-    place_shape = on_chip(nblock, nblock, width_y)
-    total, edges, forced, drives, base, place = call(
-        functools.partial(prepare_kernel, layout),
+    e_fwd, h_fwd, curls_fwd, total, edges, forced, base, place = call(
+        functools.partial(first_fwd_kernel, layout),
         [
+            field_shape,
+            field_shape,
+            curls_shape,
             total_shape,
             edges_shape,
             on_chip(depth, width_x, width_y),
-            on_chip(STEPS, width_y),
             plane,
-            place_shape,
+            on_chip(nblock, nblock, width_y),
         ],
-        [IN_VMEM] * 6,
-        [wave_idx, source_pos, block_ids, material_idx, material_eps],
-        [IN_SMEM] + [IN_HBM] * 4,
+        [IN_VMEM] * 8,
+        [fwd_fields, near, source_pos, block_ids, material_idx, material_eps],
+        [IN_VMEM] * 2 + [IN_HBM] * 4,
         [
             pltpu.SMEM(source_pos.shape, jnp.int32),
             pltpu.SMEM(block_ids.shape, jnp.int32),
@@ -684,24 +686,21 @@
             pltpu.SMEM(material_eps.shape, F32),
             pltpu.SemaphoreType.DMA((4,)),
         ],
-    )
-    fields = []
-    for evo, given in enumerate((fwd_fields, adj_fields)):
-        e, h, curls = call(
-            first_kernel,
-            [field_shape, field_shape, curls_shape],
-            [IN_VMEM] * 3,
-            [given, near],
-            [IN_VMEM, IN_VMEM],
-            micros=1.5,
-        )
-        fields.append((e, h, curls))
-    others = [tie(part, [forced] + [e for e, _, _ in fields]) for part in others]
+        micros=1.5,
+    )
+    e_adj, h_adj, curls_adj = call(
+        first_kernel,
+        [field_shape, field_shape, curls_shape],
+        [IN_VMEM] * 3,
+        [adj_fields, near],
+        [IN_VMEM, IN_VMEM],
+        micros=1.2,
+    )
+    others = [tie(part, [e_fwd, e_adj]) for part in others]
     early = [near] + others + [near_across]
     last = [swap_over(part, "grp", 1) for part in others]
     first_slot = far * len(early)
 
-    (e_fwd, h_fwd, curls_fwd), (e_adj, h_adj, curls_adj) = fields
     h_fwd, curls_fwd, h_adj, curls_adj, blocks = call(
         functools.partial(settle_kernel, layout[: len(early)]),
         [field_shape, curls_shape] * 2 + [on_chip(nblock, *piece)],
@@ -750,11 +749,12 @@
                 micros=1.2,
             )
         if not more:
+            e_fwd, h_fwd = edge_fwd(e_fwd, h_fwd)
             inner = by_owner(
                 functools.partial(filter_inner_kernel, layout),
                 depth - 2,
-                [total, block_ids],
-                [IN_VMEM, IN_HBM],
+                [total, e_fwd, block_ids],
+                [IN_VMEM, IN_VMEM, IN_HBM],
                 [
                     pltpu.VMEM((nblock,) + piece, F32),
                     pltpu.VMEM((2, width_x, width_y), F32),
@@ -763,7 +763,6 @@
                 ],
                 0.8,
             )
-            e_fwd, h_fwd = edge_fwd(e_fwd, h_fwd)
         e_adj, h_adj, e_fwd, edges, *pays = call(
             functools.partial(edge_kernel, step, 1),
             [field_shape] * 3 + [edges_shape] + [halo_shape] * more,

time: 55.6 us -> 56.6 us (1.018)
  waiting for transfers between devices: 12.2 us -> 14 us
    ppermute x22, waiting for transfers between devices: 12.2 us -> 14 us  [swap_over(): lax.ppermute(array, axis, [(i, i ^ mask) for i in range(lax.axis_size(axi...]
    pallas_call x31 -> x30, Pallas kernels: 17.6 us -> 17.1 us  [call(): pl.pallas_call(kernel, out_shape=outs, in_specs=specs, out_specs=out_spec...]
  transfers between devices with their start and end apart: 22 -> 22, of which waited for: 12 -> 13; matrix products, arithmetic and copies ran while one was open for 0% -> 0% of each run, Pallas kernels for 30% -> 29%
where the time goes in v10:
time: 56.6 us; the launch traced here: 56.4 us
  starting transfers between devices  23.8 us (42%)
  Pallas kernels  17.1 us (30%)
  waiting for transfers between devices  14 us (25%)
  between operations  1.56 us (3%)
    ppermute x22, starting transfers between devices, swap_over(): lax.ppermute(array, axis, [(i, i ^ mask) for i in range(lax.axis_size(axi...  23.8 us
    pallas_call x30, Pallas kernels, call(): pl.pallas_call(kernel, out_shape=outs, in_specs=specs, out_specs=out_spec...  17.1 us
    ppermute x22, waiting for transfers between devices, swap_over(): lax.ppermute(array, axis, [(i, i ^ mask) for i in range(lax.axis_size(axi...  14 us
  transfers between devices with their start and end apart: 22, of which 13 were waited for; matrix products, arithmetic and copies ran while one was open for 0% of the time, Pallas kernels for 29%

profile of v10, /device:TPU:0, one launch (start us, length us, event | category | flops | bytes accessed | tf_op | source)
XLA Modules:
  0.0 56.4 jit_solution(7419531228379173719)
XLA Ops:
  0.6 5.1 %collective-permute-start.2 = (f32[64,128]{1,0:T(8,128)}, f32[64,128]{1,0:T(8,128)S(1)}, u32[]{:S(2)}, u32[]{:S(2)}) collective-permute-start(f32[64,128]{1,0:T(8,128)} %bitcast.2), channel_id=1, source_target_pairs={{0,24},{2,26},{4,28},{6,30},{8,16},{10,18},{12,20},{14,22},{16,8},... | collective-permute-start | bytes 98312 | tf_op jit(solution)/shard_map/ppermute | solution.py:586
  5.7 0.6 %collective-permute-start = (f32[64,128]{1,0:T(8,128)}, f32[64,128]{1,0:T(8,128)S(1)}, u32[]{:S(2)}, u32[]{:S(2)}) collective-permute-start(f32[64,128]{1,0:T(8,128)} %bitcast.4), channel_id=1, source_target_pairs={{0,8},{2,10},{4,12},{6,14},{8,0},{10,2},{12,4},{14,6},{16,24},{18,... | collective-permute-start | bytes 98312 | tf_op jit(solution)/shard_map/ppermute | solution.py:586
  7.0 1.5 %shard_map.95 = (f32[64,128]{1,0:T(8,128)S(1)}, f32[4,128]{1,0:T(4,128)S(1)}, f32[2,2,128,128]{3,2,1,0:T(8,128)S(1)}) custom-call(f32[1,6,8,128,128]{4,3,2,1,0:T(8,128)} %given.3, f32[1,6,8,128,128]{4,3,2,1,0:T(8,128)} %given.2, f32[64,128]{1,0:T(8,128)} %bitcast.5, s32[1]{0:T(128)S(6)} %copy.112.wave_idx), custom_call_target="tpu_custom_call" | custom-call | bytes 30000 | tf_op jit(solution)/shard_map/pallas_call | solution.py:36
  8.6 1.4 %collective-permute-start.3 = (f32[2,2,128,128]{3,2,1,0:T(8,128)S(1)}, f32[2,2,128,128]{3,2,1,0:T(8,128)S(1)}, u32[]{:S(2)}, u32[]{:S(2)}) collective-permute-start(f32[2,2,128,128]{3,2,1,0:T(8,128)S(1)} %get-tuple-element.93), channel_id=1, source_target_pairs={{0,1},{1,0},{2,3},{3,2},{4,5},{5,4},{6,7},{7,6},{8,9},{9,8},{10,11... | collective-permute-start | bytes 786440 | tf_op jit(solution)/shard_map/ppermute | solution.py:586
  10.0 0.7 %collective-permute-done.1.refs_2_ = f32[64,128]{1,0:T(8,128)S(1)} collective-permute-done((f32[64,128]{1,0:T(8,128)}, f32[64,128]{1,0:T(8,128)S(1)}, u32[]{:S(2)}, u32[]{:S(2)}) %collective-permute-start.1) | collective-permute-done | bytes 32800 | tf_op jit(solution)/shard_map/ppermute | solution.py:586
  10.8 1.6 %collective-permute-start.4 = (f32[4,64,128]{2,1,0:T(8,128)S(1)}, f32[4,64,128]{2,1,0:T(8,128)S(1)}, u32[]{:S(2)}, u32[]{:S(2)}) collective-permute-start(f32[4,64,128]{2,1,0:T(8,128)S(1)} %shard_map.96.near.refs_8_), channel_id=1, source_target_pairs={{0,4},{2,6},{4,0},{6,2},{8,12},{10,14},{12,8},{14,10},{16,20},{18,... | collective-permute-start | bytes 393224 | tf_op jit(solution)/shard_map/ppermute | solution.py:586
  12.3 1.2 %shard_map.97 = (f32[3,9,144,128]{3,2,1,0:T(8,128)S(1)}, f32[3,9,144,128]{3,2,1,0:T(8,128)S(1)}, f32[3,8,128,128]{3,2,1,0:T(8,128)S(1)}) custom-call(f32[1,6,8,128,128]{4,3,2,1,0:T(8,128)S(1)} %copy-done, f32[4,64,128]{2,1,0:T(8,128)S(1)} %shard_map.96.near.refs_8_), custom_call_target="tpu_custom_call" | custom-call | bytes 120000 | tf_op jit(solution)/shard_map/pallas_call | solution.py:36
  13.5 1.3 %shard_map.98 = (f32[3,9,144,128]{3,2,1,0:T(8,128)S(1)}, f32[3,9,144,128]{3,2,1,0:T(8,128)S(1)}, f32[3,8,128,128]{3,2,1,0:T(8,128)S(1)}, f32[8,144,128]{2,1,0:T(...) custom-call(f32[1,6,8,128,128]{4,3,2,1,0:T(8,128)S(1)} %copy-done.1,, ...), custom_call_target="tpu_custom_call" | custom-call | bytes 150000 | tf_op jit(solution)/shard_map/pallas_call | solution.py:36
  14.9 0.9 %collective-permute-done.4.refs_0_ = f32[4,64,128]{2,1,0:T(8,128)S(1)} collective-permute-done((f32[4,64,128]{2,1,0:T(8,128)S(1)}, f32[4,64,128]{2,1,0:T(8,128)S(1)}, u32[]{:S(2)}, u32[]{:S(2)}) %collective-permute-start.4) | collective-permute-done | bytes 131104 | tf_op jit(solution)/shard_map/ppermute | solution.py:586
  16.1 0.7 %shard_map.100 = (f32[3,9,144,128]{3,2,1,0:T(8,128)S(1)}, f32[3,8,128,128]{3,2,1,0:T(8,128)S(1)}, f32[3,9,144,128]{3,2,1,0:T(8,128)S(1)}, f32[3,8,128,128]{3,2,1,0:T(8,128)S(1)}, f32[16,64,128]{2,1,0:T(8,128)S(1)}) custom-call(f32[3,9,144,128]{3,2,1,0:T(8,128)S(1)} %get-tuple-element.88.refs_, ...), custom_call_target="tpu_custom_call", output_to_operand_aliasing={{0}: (0, {}), {1}: (1, {}), {2}: (2, {}), {3}: (3, {})} | custom-call | bytes 60000 | tf_op jit(solution)/shard_map/pallas_call | solution.py:36
  17.5 1.5 %collective-permute-start.7 = (f32[2,128,128]{2,1,0:T(8,128)S(1)}, f32[2,128,128]{2,1,0:T(8,128)S(1)}, u32[]{:S(2)}, u32[]{:S(2)}) collective-permute-start(f32[2,128,128]{2,1,0:T(8,128)S(1)} %get-tuple-element.114), channel_id=1, source_target_pairs={{0,1},{1,0},{2,3},{3,2},{4,5},{5,4},{6,7},{7,6},{8,9},{9,8},{10,11... | collective-permute-start | bytes 393224 | tf_op jit(solution)/shard_map/ppermute | solution.py:586
  20.8 0.9 %shard_map.106 = (f32[3,9,144,128]{3,2,1,0:T(8,128)S(1)}, f32[3,9,144,128]{3,2,1,0:T(8,128)S(1)}) custom-call(f32[3,9,144,128]{3,2,1,0:T(8,128)S(1)} %get-tuple-element.110.refs_0_, f32[3,9,144,128]{3,2,1,0:T(8,128)S(1)} %get-tuple-element.111.refs_1_, ...), custom_call_target="tpu_custom_call", output_to_operand_aliasing={{0}: (0, {}), {1}: (1, {})} | custom-call | bytes 110000 | tf_op jit(solution)/shard_map/pallas_call | solution.py:36
  21.8 2.1 %collective-permute-done.7.refs_5_.refs_6_ = f32[2,128,128]{2,1,0:T(8,128)S(1)} collective-permute-done((f32[2,128,128]{2,1,0:T(8,128)S(1)}, f32[2,128,128]{2,1,0:T(8,128)S(1)}, u32[]{:S(2)}, u32[]{:S(2)}) %collective-permute-start.7) | collective-permute-done | bytes 131104 | tf_op jit(solution)/shard_map/ppermute | solution.py:586
  24.1 1.4 %collective-permute-start.9 = (f32[2,128,128]{2,1,0:T(8,128)S(1)}, f32[2,128,128]{2,1,0:T(8,128)S(1)}, u32[]{:S(2)}, u32[]{:S(2)}) collective-permute-start(f32[2,128,128]{2,1,0:T(8,128)S(1)} %get-tuple-element.128), channel_id=1, source_target_pairs={{0,1},{1,0},{2,3},{3,2},{4,5},{5,4},{6,7},{7,6},{8,9},{9,8},{10,11... | collective-permute-start | bytes 393224 | tf_op jit(solution)/shard_map/ppermute | solution.py:586
  25.5 1.2 %shard_map.108 = (f32[3,9,144,128]{3,2,1,0:T(8,128)S(1)}, f32[3,9,144,128]{3,2,1,0:T(8,128)S(1)}, f32[3,9,144,128]{3,2,1,0:T(8,128)S(1)}, f32[8,144,128]{2,1,0:T(8,128)S(1)}) custom-call(f32[3,9,144,128]{3,2,1,0:T(8,128)S(1)} %get-tuple-element.108.refs_0_, ...), custom_call_target="tpu_custom_call", output_to_operand_aliasing={{0}: (0, {}), {1}: (1, {}), {2}: (2, {}), {3}: (3, {})} | custom-call | bytes 120000 | tf_op jit(solution)/shard_map/pallas_call | solution.py:36
  27.0 1.2 %collective-permute-start.10 = (f32[2,128,128]{2,1,0:T(8,128)S(1)}, f32[2,128,128]{2,1,0:T(8,128)S(1)}, u32[]{:S(2)}, u32[]{:S(2)}) collective-permute-start(f32[2,128,128]{2,1,0:T(8,128)S(1)} %get-tuple-element.135), channel_id=1, source_target_pairs={{0,1},{1,0},{2,3},{3,2},{4,5},{5,4},{6,7},{7,6},{8,9},{9,8},{10,11... | collective-permute-start | bytes 393224 | tf_op jit(solution)/shard_map/ppermute | solution.py:586
  28.2 0.9 %shard_map.110 = (f32[3,9,144,128]{3,2,1,0:T(8,128)S(1)}, f32[3,9,144,128]{3,2,1,0:T(8,128)S(1)}) custom-call(f32[3,9,144,128]{3,2,1,0:T(8,128)S(1)} %get-tuple-element.124.refs_0_, f32[3,9,144,128]{3,2,1,0:T(8,128)S(1)} %get-tuple-element.125.refs_1_, ...), custom_call_target="tpu_custom_call", output_to_operand_aliasing={{0}: (0, {}), {1}: (1, {})} | custom-call | bytes 110000 | tf_op jit(solution)/shard_map/pallas_call | solution.py:36
  29.1 1.1 %collective-permute-done.9.refs_5_.refs_6_ = f32[2,128,128]{2,1,0:T(8,128)S(1)} collective-permute-done((f32[2,128,128]{2,1,0:T(8,128)S(1)}, f32[2,128,128]{2,1,0:T(8,128)S(1)}, u32[]{:S(2)}, u32[]{:S(2)}) %collective-permute-start.9) | collective-permute-done | bytes 131104 | tf_op jit(solution)/shard_map/ppermute | solution.py:586
  30.5 1.3 %collective-permute-start.11 = (f32[2,128,128]{2,1,0:T(8,128)S(1)}, f32[2,128,128]{2,1,0:T(8,128)S(1)}, u32[]{:S(2)}, u32[]{:S(2)}) collective-permute-start(f32[2,128,128]{2,1,0:T(8,128)S(1)} %get-tuple-element.146), channel_id=1, source_target_pairs={{0,1},{1,0},{2,3},{3,2},{4,5},{5,4},{6,7},{7,6},{8,9},{9,8},{10,11... | collective-permute-start | bytes 393224 | tf_op jit(solution)/shard_map/ppermute | solution.py:586
  31.8 1.2 %shard_map.112 = (f32[3,9,144,128]{3,2,1,0:T(8,128)S(1)}, f32[3,9,144,128]{3,2,1,0:T(8,128)S(1)}, f32[3,9,144,128]{3,2,1,0:T(8,128)S(1)}, f32[8,144,128]{2,1,0:T(8,128)S(1)}) custom-call(f32[3,9,144,128]{3,2,1,0:T(8,128)S(1)} %get-tuple-element.122.refs_0_, ...), custom_call_target="tpu_custom_call", output_to_operand_aliasing={{0}: (0, {}), {1}: (1, {}), {2}: (2, {}), {3}: (3, {})} | custom-call | bytes 120000 | tf_op jit(solution)/shard_map/pallas_call | solution.py:36
  33.6 1.2 %collective-permute-start.12 = (f32[2,128,128]{2,1,0:T(8,128)S(1)}, f32[2,128,128]{2,1,0:T(8,128)S(1)}, u32[]{:S(2)}, u32[]{:S(2)}) collective-permute-start(f32[2,128,128]{2,1,0:T(8,128)S(1)} %get-tuple-element.149), channel_id=1, source_target_pairs={{0,1},{1,0},{2,3},{3,2},{4,5},{5,4},{6,7},{7,6},{8,9},{9,8},{10,11... | collective-permute-start | bytes 393224 | tf_op jit(solution)/shard_map/ppermute | solution.py:586
  34.8 0.9 %shard_map.114 = (f32[3,9,144,128]{3,2,1,0:T(8,128)S(1)}, f32[3,9,144,128]{3,2,1,0:T(8,128)S(1)}) custom-call(f32[3,9,144,128]{3,2,1,0:T(8,128)S(1)} %get-tuple-element.138.refs_0_, f32[3,9,144,128]{3,2,1,0:T(8,128)S(1)} %get-tuple-element.139.refs_1_, ...), custom_call_target="tpu_custom_call", output_to_operand_aliasing={{0}: (0, {}), {1}: (1, {})} | custom-call | bytes 110000 | tf_op jit(solution)/shard_map/pallas_call | solution.py:36
  35.8 1.2 %shard_map.115 = (f32[3,9,144,128]{3,2,1,0:T(8,128)S(1)}, f32[3,9,144,128]{3,2,1,0:T(8,128)S(1)}, f32[3,9,144,128]{3,2,1,0:T(8,128)S(1)}, f32[8,144,128]{2,1,0:T(8,128)S(1)}) custom-call(f32[3,9,144,128]{3,2,1,0:T(8,128)S(1)} %get-tuple-element.136.refs_0_, ...), custom_call_target="tpu_custom_call", output_to_operand_aliasing={{0}: (0, {}), {1}: (1, {}), {2}: (2, {}), {3}: (3, {})} | custom-call | bytes 120000 | tf_op jit(solution)/shard_map/pallas_call | solution.py:36
  37.1 0.7 %shard_map.119 = (f32[4,48,128]{2,1,0:T(8,128)S(1)}, f32[4,48,128]{2,1,0:T(8,128)S(1)}, f32[4,48,128]{2,1,0:T(8,128)S(1)}, f32[4,48,128]{2,1,0:T(8,128)S(1)}) custom-call(f32[8,144,128]{2,1,0:T(8,128)S(1)} %get-tuple-element.152.total, f32[3,9,144,128]{3,2,1,0:T(8,128)S(1)} %get-tuple-element.147.refs_2_.after, s32[16]{0:T(128)} %block_ids_far.1), custom_call_target="tpu_custom_call" | custom-call | bytes 80000 | tf_op jit(solution)/shard_map/pallas_call | solution.py:36
  38.4 0.8 %collective-permute-done.13.refs_2_ = f32[4,48,128]{2,1,0:T(8,128)S(1)} collective-permute-done((f32[4,48,128]{2,1,0:T(8,128)S(1)}, f32[4,48,128]{2,1,0:T(8,128)S(1)}, u32[]{:S(2)}, u32[]{:S(2)}) %collective-permute-start.13) | collective-permute-done | bytes 98336 | tf_op jit(solution)/shard_map/ppermute | solution.py:586
  39.3 1.6 %collective-permute-start.15 = (f32[4,48,128]{2,1,0:T(8,128)S(1)}, f32[4,48,128]{2,1,0:T(8,128)S(1)}, u32[]{:S(2)}, u32[]{:S(2)}) collective-permute-start(f32[4,48,128]{2,1,0:T(8,128)S(1)} %get-tuple-element.158), channel_id=1, source_target_pairs={{0,4},{2,6},{4,0},{6,2},{8,12},{10,14},{12,8},{14,10},{16,20},{18,... | collective-permute-start | bytes 294920 | tf_op jit(solution)/shard_map/ppermute | solution.py:586
  41.9 0.7 %collective-permute-done.16.refs_2_ = f32[4,16,128]{2,1,0:T(8,128)S(1)} collective-permute-done((f32[4,16,128]{2,1,0:T(8,128)S(1)}, f32[4,16,128]{2,1,0:T(8,128)S(1)}, u32[]{:S(2)}, u32[]{:S(2)}) %collective-permute-start.16) | collective-permute-done | bytes 32800 | tf_op jit(solution)/shard_map/ppermute | solution.py:586
  43.4 3.4 %collective-permute-done.18.refs_3_ = f32[4,16,128]{2,1,0:T(8,128)S(1)} collective-permute-done((f32[4,16,128]{2,1,0:T(8,128)S(1)}, f32[4,16,128]{2,1,0:T(8,128)S(1)}, u32[]{:S(2)}, u32[]{:S(2)}) %collective-permute-start.18) | collective-permute-done | bytes 32800 | tf_op jit(solution)/shard_map/ppermute | solution.py:586
  46.9 3.2 %collective-permute-start.20 = (f32[64,128]{1,0:T(8,128)S(1)}, f32[64,128]{1,0:T(8,128)S(1)}, u32[]{:S(2)}, u32[]{:S(2)}) collective-permute-start(f32[64,128]{1,0:T(8,128)S(1)} %get-tuple-element.168), channel_id=1, source_target_pairs={{0,16},{2,18},{4,20},{6,22},{8,24},{10,26},{12,28},{14,30},{16,0},... | collective-permute-start | bytes 98312 | tf_op jit(solution)/shard_map/ppermute | solution.py:586
  50.1 1.1 %collective-permute-start.21 = (f32[64,128]{1,0:T(8,128)S(1)}, f32[64,128]{1,0:T(8,128)S(1)}, u32[]{:S(2)}, u32[]{:S(2)}) collective-permute-start(f32[64,128]{1,0:T(8,128)S(1)} %get-tuple-element.169), channel_id=1, source_target_pairs={{0,24},{2,26},{4,28},{6,30},{8,16},{10,18},{12,20},{14,22},{16,8},... | collective-permute-start | bytes 98312 | tf_op jit(solution)/shard_map/ppermute | solution.py:586
  51.2 1.7 %shard_map.118 = f32[1,6,8,128,128]{4,3,2,1,0:T(8,128)} custom-call(f32[3,9,144,128]{3,2,1,0:T(8,128)S(1)} %get-tuple-element.150.e, f32[3,9,144,128]{3,2,1,0:T(8,128)S(1)} %get-tuple-element.151.h), custom_call_target="tpu_custom_call" | custom-call | bytes 170000 | tf_op jit(solution)/shard_map/pallas_call | solution.py:36
  53.0 2.8 %collective-permute-done.21.refs_3_ = f32[64,128]{1,0:T(8,128)S(1)} collective-permute-done((f32[64,128]{1,0:T(8,128)S(1)}, f32[64,128]{1,0:T(8,128)S(1)}, u32[]{:S(2)}, u32[]{:S(2)}) %collective-permute-start.21) | collective-permute-done | bytes 32800 | tf_op jit(solution)/shard_map/ppermute | solution.py:586
  (46 shorter events, 7.5 us)
Async XLA Ops:
  0.6 9.4 %collective-permute-start.2 = (f32[64,128]{1,0:T(8,128)}, f32[64,128]{1,0:T(8,128)S(1)}, u32[]{:S(2)}, u32[]{:S(2)}) collective-permute-start(f32[64,128]{1,0:T(8,128)} %bitcast.2), channel_id=1, source_target_pairs={{0,24},{2,26},{4,28},{6,30},{8,16},{10,18},{12,20},{14,22},{16,8},... | collective-permute-start | bytes 98312 | tf_op jit(solution)/shard_map/ppermute | solution.py:586
  5.7 5.0 %collective-permute-start.1 = (f32[64,128]{1,0:T(8,128)}, f32[64,128]{1,0:T(8,128)S(1)}, u32[]{:S(2)}, u32[]{:S(2)}) collective-permute-start(f32[64,128]{1,0:T(8,128)} %bitcast.3), channel_id=1, source_target_pairs={{0,16},{2,18},{4,20},{6,22},{8,24},{10,26},{12,28},{14,30},{16,0},... | collective-permute-start | bytes 98312 | tf_op jit(solution)/shard_map/ppermute | solution.py:586
  5.7 5.0 %collective-permute-start = (f32[64,128]{1,0:T(8,128)}, f32[64,128]{1,0:T(8,128)S(1)}, u32[]{:S(2)}, u32[]{:S(2)}) collective-permute-start(f32[64,128]{1,0:T(8,128)} %bitcast.4), channel_id=1, source_target_pairs={{0,8},{2,10},{4,12},{6,14},{8,0},{10,2},{12,4},{14,6},{16,24},{18,... | collective-permute-start | bytes 98312 | tf_op jit(solution)/shard_map/ppermute | solution.py:586
  7.0 5.3 %copy-start = (f32[1,6,8,128,128]{4,3,2,1,0:T(8,128)S(1)}, f32[1,6,8,128,128]{4,3,2,1,0:T(8,128)}, u32[]{:S(2)}) copy-start(f32[1,6,8,128,128]{4,3,2,1,0:T(8,128)} %given.2) | copy-start | bytes 9437188
  8.6 5.0 %copy-start.1 = (f32[1,6,8,128,128]{4,3,2,1,0:T(8,128)S(1)}, f32[1,6,8,128,128]{4,3,2,1,0:T(8,128)}, u32[]{:S(2)}) copy-start(f32[1,6,8,128,128]{4,3,2,1,0:T(8,128)} %given.3) | copy-start | bytes 9437188
  8.6 7.6 %collective-permute-start.3 = (f32[2,2,128,128]{3,2,1,0:T(8,128)S(1)}, f32[2,2,128,128]{3,2,1,0:T(8,128)S(1)}, u32[]{:S(2)}, u32[]{:S(2)}) collective-permute-start(f32[2,2,128,128]{3,2,1,0:T(8,128)S(1)} %get-tuple-element.93), channel_id=1, source_target_pairs={{0,1},{1,0},{2,3},{3,2},{4,5},{5,4},{6,7},{7,6},{8,9},{9,8},{10,11... | collective-permute-start | bytes 786440 | tf_op jit(solution)/shard_map/ppermute | solution.py:586
  10.8 5.0 %collective-permute-start.4 = (f32[4,64,128]{2,1,0:T(8,128)S(1)}, f32[4,64,128]{2,1,0:T(8,128)S(1)}, u32[]{:S(2)}, u32[]{:S(2)}) collective-permute-start(f32[4,64,128]{2,1,0:T(8,128)S(1)} %shard_map.96.near.refs_8_), channel_id=1, source_target_pairs={{0,4},{2,6},{4,0},{6,2},{8,12},{10,14},{12,8},{14,10},{16,20},{18,... | collective-permute-start | bytes 393224 | tf_op jit(solution)/shard_map/ppermute | solution.py:586
  12.3 3.5 %collective-permute-start.5 = (f32[4,64,128]{2,1,0:T(8,128)S(1)}, f32[4,64,128]{2,1,0:T(8,128)S(1)}, u32[]{:S(2)}, u32[]{:S(2)}) collective-permute-start(f32[4,64,128]{2,1,0:T(8,128)S(1)} %shard_map.96.near.refs_8_), channel_id=1, source_target_pairs={{0,2},{2,0},{4,6},{6,4},{8,10},{10,8},{12,14},{14,12},{16,18},{18,... | collective-permute-start | bytes 393224 | tf_op jit(solution)/shard_map/ppermute | solution.py:586
  15.8 1.3 %collective-permute-start.6 = (f32[4,64,128]{2,1,0:T(8,128)S(1)}, f32[4,64,128]{2,1,0:T(8,128)S(1)}, u32[]{:S(2)}, u32[]{:S(2)}) collective-permute-start(f32[4,64,128]{2,1,0:T(8,128)S(1)} %shard_map.99.refs_9_), channel_id=1, source_target_pairs={{0,2},{2,0},{4,6},{6,4},{8,10},{10,8},{12,14},{14,12},{16,18},{18,... | collective-permute-start | bytes 393224 | tf_op jit(solution)/shard_map/ppermute | solution.py:586
  17.5 6.4 %collective-permute-start.7 = (f32[2,128,128]{2,1,0:T(8,128)S(1)}, f32[2,128,128]{2,1,0:T(8,128)S(1)}, u32[]{:S(2)}, u32[]{:S(2)}) collective-permute-start(f32[2,128,128]{2,1,0:T(8,128)S(1)} %get-tuple-element.114), channel_id=1, source_target_pairs={{0,1},{1,0},{2,3},{3,2},{4,5},{5,4},{6,7},{7,6},{8,9},{9,8},{10,11... | collective-permute-start | bytes 393224 | tf_op jit(solution)/shard_map/ppermute | solution.py:586
  19.1 7.6 %collective-permute-start.8 = (f32[2,128,128]{2,1,0:T(8,128)S(1)}, f32[2,128,128]{2,1,0:T(8,128)S(1)}, u32[]{:S(2)}, u32[]{:S(2)}) collective-permute-start(f32[2,128,128]{2,1,0:T(8,128)S(1)} %get-tuple-element.121), channel_id=1, source_target_pairs={{0,1},{1,0},{2,3},{3,2},{4,5},{5,4},{6,7},{7,6},{8,9},{9,8},{10,11... | collective-permute-start | bytes 393224 | tf_op jit(solution)/shard_map/ppermute | solution.py:586
  24.1 6.1 %collective-permute-start.9 = (f32[2,128,128]{2,1,0:T(8,128)S(1)}, f32[2,128,128]{2,1,0:T(8,128)S(1)}, u32[]{:S(2)}, u32[]{:S(2)}) collective-permute-start(f32[2,128,128]{2,1,0:T(8,128)S(1)} %get-tuple-element.128), channel_id=1, source_target_pairs={{0,1},{1,0},{2,3},{3,2},{4,5},{5,4},{6,7},{7,6},{8,9},{9,8},{10,11... | collective-permute-start | bytes 393224 | tf_op jit(solution)/shard_map/ppermute | solution.py:586
  27.0 6.4 %collective-permute-start.10 = (f32[2,128,128]{2,1,0:T(8,128)S(1)}, f32[2,128,128]{2,1,0:T(8,128)S(1)}, u32[]{:S(2)}, u32[]{:S(2)}) collective-permute-start(f32[2,128,128]{2,1,0:T(8,128)S(1)} %get-tuple-element.135), channel_id=1, source_target_pairs={{0,1},{1,0},{2,3},{3,2},{4,5},{5,4},{6,7},{7,6},{8,9},{9,8},{10,11... | collective-permute-start | bytes 393224 | tf_op jit(solution)/shard_map/ppermute | solution.py:586
  30.5 6.5 %collective-permute-start.11 = (f32[2,128,128]{2,1,0:T(8,128)S(1)}, f32[2,128,128]{2,1,0:T(8,128)S(1)}, u32[]{:S(2)}, u32[]{:S(2)}) collective-permute-start(f32[2,128,128]{2,1,0:T(8,128)S(1)} %get-tuple-element.146), channel_id=1, source_target_pairs={{0,1},{1,0},{2,3},{3,2},{4,5},{5,4},{6,7},{7,6},{8,9},{9,8},{10,11... | collective-permute-start | bytes 393224 | tf_op jit(solution)/shard_map/ppermute | solution.py:586
  33.6 7.3 %collective-permute-start.12 = (f32[2,128,128]{2,1,0:T(8,128)S(1)}, f32[2,128,128]{2,1,0:T(8,128)S(1)}, u32[]{:S(2)}, u32[]{:S(2)}) collective-permute-start(f32[2,128,128]{2,1,0:T(8,128)S(1)} %get-tuple-element.149), channel_id=1, source_target_pairs={{0,1},{1,0},{2,3},{3,2},{4,5},{5,4},{6,7},{7,6},{8,9},{9,8},{10,11... | collective-permute-start | bytes 393224 | tf_op jit(solution)/shard_map/ppermute | solution.py:586
  37.8 1.4 %collective-permute-start.13 = (f32[4,48,128]{2,1,0:T(8,128)S(1)}, f32[4,48,128]{2,1,0:T(8,128)S(1)}, u32[]{:S(2)}, u32[]{:S(2)}) collective-permute-start(f32[4,48,128]{2,1,0:T(8,128)S(1)} %get-tuple-element.155), channel_id=1, source_target_pairs={{0,2},{2,0},{4,6},{6,4},{8,10},{10,8},{12,14},{14,12},{16,18},{18,... | collective-permute-start | bytes 294920 | tf_op jit(solution)/shard_map/ppermute | solution.py:586
  37.9 1.4 %collective-permute-start.14 = (f32[4,48,128]{2,1,0:T(8,128)S(1)}, f32[4,48,128]{2,1,0:T(8,128)S(1)}, u32[]{:S(2)}, u32[]{:S(2)}) collective-permute-start(f32[4,48,128]{2,1,0:T(8,128)S(1)} %get-tuple-element.156), channel_id=1, source_target_pairs={{0,2},{2,0},{4,6},{6,4},{8,10},{10,8},{12,14},{14,12},{16,18},{18,... | collective-permute-start | bytes 294920 | tf_op jit(solution)/shard_map/ppermute | solution.py:586
  39.3 7.4 %collective-permute-start.15 = (f32[4,48,128]{2,1,0:T(8,128)S(1)}, f32[4,48,128]{2,1,0:T(8,128)S(1)}, u32[]{:S(2)}, u32[]{:S(2)}) collective-permute-start(f32[4,48,128]{2,1,0:T(8,128)S(1)} %get-tuple-element.158), channel_id=1, source_target_pairs={{0,4},{2,6},{4,0},{6,2},{8,12},{10,14},{12,8},{14,10},{16,20},{18,... | collective-permute-start | bytes 294920 | tf_op jit(solution)/shard_map/ppermute | solution.py:586
  41.3 1.3 %collective-permute-start.16 = (f32[4,16,128]{2,1,0:T(8,128)S(1)}, f32[4,16,128]{2,1,0:T(8,128)S(1)}, u32[]{:S(2)}, u32[]{:S(2)}) collective-permute-start(f32[4,16,128]{2,1,0:T(8,128)S(1)} %get-tuple-element.162), channel_id=1, source_target_pairs={{0,2},{2,0},{4,6},{6,4},{8,10},{10,8},{12,14},{14,12},{16,18},{18,... | collective-permute-start | bytes 98312 | tf_op jit(solution)/shard_map/ppermute | solution.py:586
  41.5 1.3 %collective-permute-start.17 = (f32[4,16,128]{2,1,0:T(8,128)S(1)}, f32[4,16,128]{2,1,0:T(8,128)S(1)}, u32[]{:S(2)}, u32[]{:S(2)}) collective-permute-start(f32[4,16,128]{2,1,0:T(8,128)S(1)} %get-tuple-element.163), channel_id=1, source_target_pairs={{0,2},{2,0},{4,6},{6,4},{8,10},{10,8},{12,14},{14,12},{16,18},{18,... | collective-permute-start | bytes 98312 | tf_op jit(solution)/shard_map/ppermute | solution.py:586
  42.8 4.0 %collective-permute-start.18 = (f32[4,16,128]{2,1,0:T(8,128)S(1)}, f32[4,16,128]{2,1,0:T(8,128)S(1)}, u32[]{:S(2)}, u32[]{:S(2)}) collective-permute-start(f32[4,16,128]{2,1,0:T(8,128)S(1)} %get-tuple-element.165), channel_id=1, source_target_pairs={{0,4},{2,6},{4,0},{6,2},{8,12},{10,14},{12,8},{14,10},{16,20},{18,... | collective-permute-start | bytes 98312 | tf_op jit(solution)/shard_map/ppermute | solution.py:586
  46.8 6.2 %collective-permute-start.19 = (f32[64,128]{1,0:T(8,128)S(1)}, f32[64,128]{1,0:T(8,128)S(1)}, u32[]{:S(2)}, u32[]{:S(2)}) collective-permute-start(f32[64,128]{1,0:T(8,128)S(1)} %get-tuple-element.167), channel_id=1, source_target_pairs={{0,8},{2,10},{4,12},{6,14},{8,0},{10,2},{12,4},{14,6},{16,24},{18,... | collective-permute-start | bytes 98312 | tf_op jit(solution)/shard_map/ppermute | solution.py:586
  46.9 6.1 %collective-permute-start.20 = (f32[64,128]{1,0:T(8,128)S(1)}, f32[64,128]{1,0:T(8,128)S(1)}, u32[]{:S(2)}, u32[]{:S(2)}) collective-permute-start(f32[64,128]{1,0:T(8,128)S(1)} %get-tuple-element.168), channel_id=1, source_target_pairs={{0,16},{2,18},{4,20},{6,22},{8,24},{10,26},{12,28},{14,30},{16,0},... | collective-permute-start | bytes 98312 | tf_op jit(solution)/shard_map/ppermute | solution.py:586
  50.1 5.7 %collective-permute-start.21 = (f32[64,128]{1,0:T(8,128)S(1)}, f32[64,128]{1,0:T(8,128)S(1)}, u32[]{:S(2)}, u32[]{:S(2)}) collective-permute-start(f32[64,128]{1,0:T(8,128)S(1)} %get-tuple-element.169), channel_id=1, source_target_pairs={{0,24},{2,26},{4,28},{6,30},{8,16},{10,18},{12,20},{14,22},{16,8},... | collective-permute-start | bytes 98312 | tf_op jit(solution)/shard_map/ppermute | solution.py:586

commit v11 on v10

--- a/solution.py
+++ b/solution.py
@@ -165,16 +165,13 @@
     return lambda layer, here: drives[pl.ds(step, 1), :] * forced[layer, here, :]
 
 
-def opening_kernel(fwd, adj, density, wave_idx, own, drives, *rest):
+def opening_kernel(fwd, adj, density, own, *rest):
     pays, (planes, sems) = rest[:-2], rest[-2:]
     depth, rows, width_y = fwd.shape[2:]
     top = depth - 1
     has_up, has_low = neighbours()
     held_copy = pltpu.make_async_copy(density, own, sems.at[2, 0])
     held_copy.start()
-    step = lax.broadcasted_iota(jnp.int32, drives.shape, 0).astype(F32) + 1.0
-    wave = jnp.full(drives.shape, wave_idx[0], jnp.int32).astype(F32)
-    drives[...] = AMPLITUDE * jnp.sin(2.0 * math.pi / (6.0 + 2.0 * wave) * step)
 
     def up(pay):
         copies = []
@@ -221,8 +218,8 @@
 
 
 def first_fwd_kernel(
-    layout, given, near, source_far, ids_far, idx_far, eps_far,
-    e, h, curls, total, edges, forced, base, place,
+    layout, given, near, wave_idx, source_far, ids_far, idx_far, eps_far,
+    e, h, curls, total, edges, forced, drives, base, place,
     source, block_ids, material_idx, material_eps, sems,
 ):
     fetches = [
@@ -254,6 +251,9 @@
     offset_x = (xcoord - source[0, 1]).astype(F32) / (rows / 4.0)
     offset_y = (ycoord - source[0, 2]).astype(F32) / (width_y / 4.0)
     profile = jnp.exp(-0.5 * (offset_x * offset_x + offset_y * offset_y))
+    step = lax.broadcasted_iota(jnp.int32, drives.shape, 0).astype(F32) + 1.0
+    wave = jnp.full(drives.shape, wave_idx[0], jnp.int32).astype(F32)
+    drives[...] = AMPLITUDE * jnp.sin(2.0 * math.pi / (6.0 + 2.0 * wave) * step)
     level = source[0, 0] - lax.axis_index("slab") * depth
     for layer in range(depth):
         forced[layer] = jnp.where(level == layer, 1.0, 0.0) * profile
@@ -533,9 +533,8 @@
             parts[slot // parts[0].shape[0]][slot % parts[0].shape[0], target, :] = value
 
 
-def add_kernel(*refs):
-    half = len(refs) // 3
-    for a, b, out in zip(refs[:half], refs[half : 2 * half], refs[2 * half :]):
+def add_kernel(count, *refs):
+    for a, b, out in zip(refs[:count], refs[count : 2 * count], refs[-count:]):
         out[...] = a[...] + b[...]
 
 
@@ -636,13 +635,15 @@
             scratch,
             micros=micros,
         )
-        got = [swap_over(part, "grp", 1) for part in parts[middle:]]
+        return list(parts[:middle]), [swap_over(part, "grp", 1) for part in parts[middle:]]
+
+    def add_middle(kept, got, after):
         sums = call(
-            add_kernel,
-            [shape] * middle,
+            functools.partial(add_kernel, middle),
+            [on_chip(*part.shape) for part in kept],
             [IN_VMEM] * middle,
-            list(parts[:middle]) + got,
-            [IN_VMEM] * (2 * middle),
+            kept + got + after,
+            [IN_VMEM] * (2 * middle + len(after)),
         )
         return [sums[0]] + [
             swap_over(part, "grp", mask) for part, mask in zip(sums[1:], middle_masks[1:])
@@ -650,12 +651,12 @@
 
     design = density.reshape(piece)
     got = [swap_over(design, "grp", mask) for mask in far_masks[1:]]
-    own, drives, *pays = call(
+    own, *pays = call(
         opening_kernel,
-        [on_chip(*piece), on_chip(STEPS, width_y)] + [on_chip(2, 2, width_x, width_y)] * npay,
-        [IN_VMEM] * (2 + npay),
-        [fwd_fields, adj_fields, design, wave_idx],
-        [IN_HBM] * 3 + [IN_SMEM],
+        [on_chip(*piece)] + [on_chip(2, 2, width_x, width_y)] * npay,
+        [IN_VMEM] * (1 + npay),
+        [fwd_fields, adj_fields, design],
+        [IN_HBM] * 3,
         [pltpu.VMEM((2, 5, width_x, width_y), F32), pltpu.SemaphoreType.DMA((3, 5))],
     )
     below, above = trade(pays)
@@ -664,7 +665,7 @@
     others = [swap_over(near, "grp", mask) for mask in middle_masks[1:]]
     near_across = swap_over(near, "grp", 1)
 
-    e_fwd, h_fwd, curls_fwd, total, edges, forced, base, place = call(
+    e_fwd, h_fwd, curls_fwd, total, edges, forced, drives, base, place = call(
         functools.partial(first_fwd_kernel, layout),
         [
             field_shape,
@@ -673,12 +674,13 @@
             total_shape,
             edges_shape,
             on_chip(depth, width_x, width_y),
+            on_chip(STEPS, width_y),
             plane,
             on_chip(nblock, nblock, width_y),
         ],
-        [IN_VMEM] * 8,
-        [fwd_fields, near, source_pos, block_ids, material_idx, material_eps],
-        [IN_VMEM] * 2 + [IN_HBM] * 4,
+        [IN_VMEM] * 9,
+        [fwd_fields, near, wave_idx, source_pos, block_ids, material_idx, material_eps],
+        [IN_VMEM] * 2 + [IN_SMEM] + [IN_HBM] * 4,
         [
             pltpu.SMEM(source_pos.shape, jnp.int32),
             pltpu.SMEM(block_ids.shape, jnp.int32),
@@ -763,17 +765,6 @@
                 ],
                 0.8,
             )
-        e_adj, h_adj, e_fwd, edges, *pays = call(
-            functools.partial(edge_kernel, step, 1),
-            [field_shape] * 3 + [edges_shape] + [halo_shape] * more,
-            [IN_VMEM] * (4 + more),
-            [e_adj, h_adj, e_fwd, edges, coef] + arrived_adj,
-            [IN_VMEM] * (5 + len(arrived_adj)),
-            aliases={0: 0, 1: 1, 2: 2, 3: 3},
-        )
-        if not more:
-            break
-        arrived_fwd, arrived_adj = arrived_fwd_next, trade(pays)
         if step == 0:
             coef = call(
                 functools.partial(coef_inner_kernel, first_slot, len(last)),
@@ -794,6 +785,17 @@
                 aliases={0: 0, 1: 1, 2: 2},
                 micros=0.5,
             )
+        e_adj, h_adj, e_fwd, edges, *pays = call(
+            functools.partial(edge_kernel, step, 1),
+            [field_shape] * 3 + [edges_shape] + [halo_shape] * more,
+            [IN_VMEM] * (4 + more),
+            [e_adj, h_adj, e_fwd, edges, coef] + arrived_adj,
+            [IN_VMEM] * (5 + len(arrived_adj)),
+            aliases={0: 0, 1: 1, 2: 2, 3: 3},
+        )
+        if not more:
+            break
+        arrived_fwd, arrived_adj = arrived_fwd_next, trade(pays)
         e_fwd, h_fwd = call(
             functools.partial(inner_kernel, step + 1, 0),
             [field_shape] * 2,
@@ -815,6 +817,8 @@
         ],
         0.3,
     )
+    inner = add_middle(*inner, ends[0][:1])
+    ends = add_middle(*ends, [])
     pieces = call(
         functools.partial(join_kernel, middle, block_rows),
         [on_chip(*piece)] * far,

time: 56.6 us -> 55.4 us (0.979)
  waiting for transfers between devices: 14 us -> 11.4 us
  starting transfers between devices: 23.8 us -> 25.2 us
    ppermute x22, waiting for transfers between devices: 14 us -> 11.4 us  [swap_over(): lax.ppermute(array, axis, [(i, i ^ mask) for i in range(lax.axis_size(axi...]
    ppermute x22, starting transfers between devices: 23.8 us -> 25.2 us  [swap_over(): lax.ppermute(array, axis, [(i, i ^ mask) for i in range(lax.axis_size(axi...]
  transfers between devices with their start and end apart: 22 -> 22, of which waited for: 13 -> 12; matrix products, arithmetic and copies ran while one was open for 0% -> 0% of each run, Pallas kernels for 29% -> 29%
where the time goes in v11:
time: 55.4 us; the launch traced here: 55.2 us
  starting transfers between devices  25.2 us (45%)
  Pallas kernels  17 us (31%)
  waiting for transfers between devices  11.4 us (21%)
  between operations  1.58 us (3%)
    ppermute x22, starting transfers between devices, swap_over(): lax.ppermute(array, axis, [(i, i ^ mask) for i in range(lax.axis_size(axi...  25.2 us
    pallas_call x30, Pallas kernels, call(): pl.pallas_call(kernel, out_shape=outs, in_specs=specs, out_specs=out_spec...  17 us
    ppermute x22, waiting for transfers between devices, swap_over(): lax.ppermute(array, axis, [(i, i ^ mask) for i in range(lax.axis_size(axi...  11.4 us
  transfers between devices with their start and end apart: 22, of which 12 were waited for; matrix products, arithmetic and copies ran while one was open for 0% of the time, Pallas kernels for 29%

profile of v11, /device:TPU:0, one launch (start us, length us, event | category | flops | bytes accessed | tf_op | source)
XLA Modules:
  0.0 55.2 jit_solution(13929515782339489664)
XLA Ops:
  0.6 5.1 %collective-permute-start.2 = (f32[64,128]{1,0:T(8,128)}, f32[64,128]{1,0:T(8,128)S(1)}, u32[]{:S(2)}, u32[]{:S(2)}) collective-permute-start(f32[64,128]{1,0:T(8,128)} %bitcast.2), channel_id=1, source_target_pairs={{0,24},{2,26},{4,28},{6,30},{8,16},{10,18},{12,20},{14,22},{16,8},... | collective-permute-start | bytes 98312 | tf_op jit(solution)/shard_map/ppermute | solution.py:585
  5.8 0.6 %collective-permute-start = (f32[64,128]{1,0:T(8,128)}, f32[64,128]{1,0:T(8,128)S(1)}, u32[]{:S(2)}, u32[]{:S(2)}) collective-permute-start(f32[64,128]{1,0:T(8,128)} %bitcast.4), channel_id=1, source_target_pairs={{0,8},{2,10},{4,12},{6,14},{8,0},{10,2},{12,4},{14,6},{16,24},{18,... | collective-permute-start | bytes 98312 | tf_op jit(solution)/shard_map/ppermute | solution.py:585
  6.4 1.4 %shard_map.95 = (f32[64,128]{1,0:T(8,128)S(1)}, f32[2,2,128,128]{3,2,1,0:T(8,128)S(1)}) custom-call(f32[1,6,8,128,128]{4,3,2,1,0:T(8,128)} %given.2, f32[1,6,8,128,128]{4,3,2,1,0:T(8,128)} %given.3, f32[64,128]{1,0:T(8,128)} %bitcast.5), custom_call_target="tpu_custom_call" | custom-call | bytes 30000 | tf_op jit(solution)/shard_map/pallas_call | solution.py:36
  7.8 1.4 %collective-permute-start.3 = (f32[2,2,128,128]{3,2,1,0:T(8,128)S(1)}, f32[2,2,128,128]{3,2,1,0:T(8,128)S(1)}, u32[]{:S(2)}, u32[]{:S(2)}) collective-permute-start(f32[2,2,128,128]{3,2,1,0:T(8,128)S(1)} %get-tuple-element.93), channel_id=1, source_target_pairs={{0,1},{1,0},{2,3},{3,2},{4,5},{5,4},{6,7},{7,6},{8,9},{9,8},{10,11... | collective-permute-start | bytes 786440 | tf_op jit(solution)/shard_map/ppermute | solution.py:585
  9.2 1.5 %collective-permute-done.1.refs_2_ = f32[64,128]{1,0:T(8,128)S(1)} collective-permute-done((f32[64,128]{1,0:T(8,128)}, f32[64,128]{1,0:T(8,128)S(1)}, u32[]{:S(2)}, u32[]{:S(2)}) %collective-permute-start.1) | collective-permute-done | bytes 32800 | tf_op jit(solution)/shard_map/ppermute | solution.py:585
  10.8 1.6 %collective-permute-start.4 = (f32[4,64,128]{2,1,0:T(8,128)S(1)}, f32[4,64,128]{2,1,0:T(8,128)S(1)}, u32[]{:S(2)}, u32[]{:S(2)}) collective-permute-start(f32[4,64,128]{2,1,0:T(8,128)S(1)} %shard_map.96.near.refs_8_), channel_id=1, source_target_pairs={{0,4},{2,6},{4,0},{6,2},{8,12},{10,14},{12,8},{14,10},{16,20},{18,... | collective-permute-start | bytes 393224 | tf_op jit(solution)/shard_map/ppermute | solution.py:585
  13.1 1.2 %shard_map.98 = (f32[3,9,144,128]{3,2,1,0:T(8,128)S(1)}, f32[3,9,144,128]{3,2,1,0:T(8,128)S(1)}, f32[3,8,128,128]{3,2,1,0:T(8,128)S(1)}) custom-call(f32[1,6,8,128,128]{4,3,2,1,0:T(8,128)S(1)} %copy-done, f32[4,64,128]{2,1,0:T(8,128)S(1)} %shard_map.96.near.refs_8_), custom_call_target="tpu_custom_call" | custom-call | bytes 120000 | tf_op jit(solution)/shard_map/pallas_call | solution.py:36
  14.3 1.4 %shard_map.97 = (f32[3,9,144,128]{3,2,1,0:T(8,128)S(1)}, f32[3,9,144,128]{3,2,1,0:T(8,128)S(1)}, f32[3,8,128,128]{3,2,1,0:T(8,128)S(1)}, f32[8,144,128]{2,1,0:T(...) custom-call(f32[1,6,8,128,128]{4,3,2,1,0:T(8,128)S(1)} %copy-done.1,, ...), custom_call_target="tpu_custom_call" | custom-call | bytes 150000 | tf_op jit(solution)/shard_map/pallas_call | solution.py:36
  16.2 0.7 %shard_map.100 = (f32[3,9,144,128]{3,2,1,0:T(8,128)S(1)}, f32[3,8,128,128]{3,2,1,0:T(8,128)S(1)}, f32[3,9,144,128]{3,2,1,0:T(8,128)S(1)}, f32[3,8,128,128]{3,2,1,0:T(8,128)S(1)}, f32[16,64,128]{2,1,0:T(8,128)S(1)}) custom-call(f32[3,9,144,128]{3,2,1,0:T(8,128)S(1)} %get-tuple-element.88.refs_, ...), custom_call_target="tpu_custom_call", output_to_operand_aliasing={{0}: (0, {}), {1}: (1, {}), {2}: (2, {}), {3}: (3, {})} | custom-call | bytes 60000 | tf_op jit(solution)/shard_map/pallas_call | solution.py:36
  17.5 1.5 %collective-permute-start.7 = (f32[2,128,128]{2,1,0:T(8,128)S(1)}, f32[2,128,128]{2,1,0:T(8,128)S(1)}, u32[]{:S(2)}, u32[]{:S(2)}) collective-permute-start(f32[2,128,128]{2,1,0:T(8,128)S(1)} %get-tuple-element.114), channel_id=1, source_target_pairs={{0,1},{1,0},{2,3},{3,2},{4,5},{5,4},{6,7},{7,6},{8,9},{9,8},{10,11... | collective-permute-start | bytes 393224 | tf_op jit(solution)/shard_map/ppermute | solution.py:585
  19.0 0.6 %shard_map.103.coef.refs_4_.refs_2_ = f32[8,128,128]{2,1,0:T(8,128)S(1)} custom-call(f32[8,128,128]{2,1,0:T(8,128)S(1)} %shard_map.101.refs_2_.coef_in, f32[4,64,128]{2,1,0:T(8,128)S(1)} %collective-permute-done.6.refs_0_, f32[16,16,128]{2,1,0:T(8,128)S(1)} %get-tuple-element.95.refs_1_.place, ...), custom_call_target="tpu_custom_call", output_to_operand_aliasing={{}: (0, {})} | custom-call | bytes 60000 | tf_op jit(solution)/shard_map/pallas_call | solution.py:36
  20.9 0.9 %shard_map.106 = (f32[3,9,144,128]{3,2,1,0:T(8,128)S(1)}, f32[3,9,144,128]{3,2,1,0:T(8,128)S(1)}) custom-call(f32[3,9,144,128]{3,2,1,0:T(8,128)S(1)} %get-tuple-element.110.refs_0_, f32[3,9,144,128]{3,2,1,0:T(8,128)S(1)} %get-tuple-element.111.refs_1_, ...), custom_call_target="tpu_custom_call", output_to_operand_aliasing={{0}: (0, {}), {1}: (1, {})} | custom-call | bytes 110000 | tf_op jit(solution)/shard_map/pallas_call | solution.py:36
  21.9 1.7 %collective-permute-done.7.refs_5_.refs_6_ = f32[2,128,128]{2,1,0:T(8,128)S(1)} collective-permute-done((f32[2,128,128]{2,1,0:T(8,128)S(1)}, f32[2,128,128]{2,1,0:T(8,128)S(1)}, u32[]{:S(2)}, u32[]{:S(2)}) %collective-permute-start.7) | collective-permute-done | bytes 131104 | tf_op jit(solution)/shard_map/ppermute | solution.py:585
  23.8 1.7 %collective-permute-start.9 = (f32[2,128,128]{2,1,0:T(8,128)S(1)}, f32[2,128,128]{2,1,0:T(8,128)S(1)}, u32[]{:S(2)}, u32[]{:S(2)}) collective-permute-start(f32[2,128,128]{2,1,0:T(8,128)S(1)} %get-tuple-element.128), channel_id=1, source_target_pairs={{0,1},{1,0},{2,3},{3,2},{4,5},{5,4},{6,7},{7,6},{8,9},{9,8},{10,11... | collective-permute-start | bytes 393224 | tf_op jit(solution)/shard_map/ppermute | solution.py:585
  25.6 1.2 %shard_map.108 = (f32[3,9,144,128]{3,2,1,0:T(8,128)S(1)}, f32[3,9,144,128]{3,2,1,0:T(8,128)S(1)}, f32[3,9,144,128]{3,2,1,0:T(8,128)S(1)}, f32[8,144,128]{2,1,0:T(8,128)S(1)}) custom-call(f32[3,9,144,128]{3,2,1,0:T(8,128)S(1)} %get-tuple-element.108.refs_0_, ...), custom_call_target="tpu_custom_call", output_to_operand_aliasing={{0}: (0, {}), {1}: (1, {}), {2}: (2, {}), {3}: (3, {})} | custom-call | bytes 120000 | tf_op jit(solution)/shard_map/pallas_call | solution.py:36
  27.0 1.2 %collective-permute-start.10 = (f32[2,128,128]{2,1,0:T(8,128)S(1)}, f32[2,128,128]{2,1,0:T(8,128)S(1)}, u32[]{:S(2)}, u32[]{:S(2)}) collective-permute-start(f32[2,128,128]{2,1,0:T(8,128)S(1)} %get-tuple-element.135), channel_id=1, source_target_pairs={{0,1},{1,0},{2,3},{3,2},{4,5},{5,4},{6,7},{7,6},{8,9},{9,8},{10,11... | collective-permute-start | bytes 393224 | tf_op jit(solution)/shard_map/ppermute | solution.py:585
  28.2 0.9 %shard_map.110 = (f32[3,9,144,128]{3,2,1,0:T(8,128)S(1)}, f32[3,9,144,128]{3,2,1,0:T(8,128)S(1)}) custom-call(f32[3,9,144,128]{3,2,1,0:T(8,128)S(1)} %get-tuple-element.124.refs_0_, f32[3,9,144,128]{3,2,1,0:T(8,128)S(1)} %get-tuple-element.125.refs_1_, ...), custom_call_target="tpu_custom_call", output_to_operand_aliasing={{0}: (0, {}), {1}: (1, {})} | custom-call | bytes 110000 | tf_op jit(solution)/shard_map/pallas_call | solution.py:36
  29.6 1.7 %collective-permute-start.11 = (f32[2,128,128]{2,1,0:T(8,128)S(1)}, f32[2,128,128]{2,1,0:T(8,128)S(1)}, u32[]{:S(2)}, u32[]{:S(2)}) collective-permute-start(f32[2,128,128]{2,1,0:T(8,128)S(1)} %get-tuple-element.146), channel_id=1, source_target_pairs={{0,1},{1,0},{2,3},{3,2},{4,5},{5,4},{6,7},{7,6},{8,9},{9,8},{10,11... | collective-permute-start | bytes 393224 | tf_op jit(solution)/shard_map/ppermute | solution.py:585
  31.3 1.2 %shard_map.112 = (f32[3,9,144,128]{3,2,1,0:T(8,128)S(1)}, f32[3,9,144,128]{3,2,1,0:T(8,128)S(1)}, f32[3,9,144,128]{3,2,1,0:T(8,128)S(1)}, f32[8,144,128]{2,1,0:T(8,128)S(1)}) custom-call(f32[3,9,144,128]{3,2,1,0:T(8,128)S(1)} %get-tuple-element.122.refs_0_, ...), custom_call_target="tpu_custom_call", output_to_operand_aliasing={{0}: (0, {}), {1}: (1, {}), {2}: (2, {}), {3}: (3, {})} | custom-call | bytes 120000 | tf_op jit(solution)/shard_map/pallas_call | solution.py:36
  32.5 0.6 %collective-permute-done.10.refs_5_.refs_6_ = f32[2,128,128]{2,1,0:T(8,128)S(1)} collective-permute-done((f32[2,128,128]{2,1,0:T(8,128)S(1)}, f32[2,128,128]{2,1,0:T(8,128)S(1)}, u32[]{:S(2)}, u32[]{:S(2)}) %collective-permute-start.10) | collective-permute-done | bytes 131104 | tf_op jit(solution)/shard_map/ppermute | solution.py:585
  33.4 1.5 %collective-permute-start.12 = (f32[2,128,128]{2,1,0:T(8,128)S(1)}, f32[2,128,128]{2,1,0:T(8,128)S(1)}, u32[]{:S(2)}, u32[]{:S(2)}) collective-permute-start(f32[2,128,128]{2,1,0:T(8,128)S(1)} %get-tuple-element.149), channel_id=1, source_target_pairs={{0,1},{1,0},{2,3},{3,2},{4,5},{5,4},{6,7},{7,6},{8,9},{9,8},{10,11... | collective-permute-start | bytes 393224 | tf_op jit(solution)/shard_map/ppermute | solution.py:585
  34.8 0.9 %shard_map.114 = (f32[3,9,144,128]{3,2,1,0:T(8,128)S(1)}, f32[3,9,144,128]{3,2,1,0:T(8,128)S(1)}) custom-call(f32[3,9,144,128]{3,2,1,0:T(8,128)S(1)} %get-tuple-element.138.refs_0_, f32[3,9,144,128]{3,2,1,0:T(8,128)S(1)} %get-tuple-element.139.refs_1_, ...), custom_call_target="tpu_custom_call", output_to_operand_aliasing={{0}: (0, {}), {1}: (1, {})} | custom-call | bytes 110000 | tf_op jit(solution)/shard_map/pallas_call | solution.py:36
  35.8 1.2 %shard_map.115 = (f32[3,9,144,128]{3,2,1,0:T(8,128)S(1)}, f32[3,9,144,128]{3,2,1,0:T(8,128)S(1)}, f32[3,9,144,128]{3,2,1,0:T(8,128)S(1)}, f32[8,144,128]{2,1,0:T(8,128)S(1)}) custom-call(f32[3,9,144,128]{3,2,1,0:T(8,128)S(1)} %get-tuple-element.136.refs_0_, ...), custom_call_target="tpu_custom_call", output_to_operand_aliasing={{0}: (0, {}), {1}: (1, {}), {2}: (2, {}), {3}: (3, {})} | custom-call | bytes 120000 | tf_op jit(solution)/shard_map/pallas_call | solution.py:36
  37.1 0.7 %shard_map.119 = (f32[4,48,128]{2,1,0:T(8,128)S(1)}, f32[4,48,128]{2,1,0:T(8,128)S(1)}, f32[4,48,128]{2,1,0:T(8,128)S(1)}, f32[4,48,128]{2,1,0:T(8,128)S(1)}) custom-call(f32[8,144,128]{2,1,0:T(8,128)S(1)} %get-tuple-element.152.total, f32[3,9,144,128]{3,2,1,0:T(8,128)S(1)} %get-tuple-element.147.refs_2_.after, s32[16]{0:T(128)} %block_ids_far.1), custom_call_target="tpu_custom_call" | custom-call | bytes 80000 | tf_op jit(solution)/shard_map/pallas_call | solution.py:36
  39.4 1.6 %collective-permute-start.15 = (f32[4,48,128]{2,1,0:T(8,128)S(1)}, f32[4,48,128]{2,1,0:T(8,128)S(1)}, u32[]{:S(2)}, u32[]{:S(2)}) collective-permute-start(f32[4,48,128]{2,1,0:T(8,128)S(1)} %get-tuple-element.160), channel_id=1, source_target_pairs={{0,4},{2,6},{4,0},{6,2},{8,12},{10,14},{12,8},{14,10},{16,20},{18,... | collective-permute-start | bytes 294920 | tf_op jit(solution)/shard_map/ppermute | solution.py:585
  41.4 0.7 %collective-permute-done.16.refs_2_ = f32[4,16,128]{2,1,0:T(8,128)S(1)} collective-permute-done((f32[4,16,128]{2,1,0:T(8,128)S(1)}, f32[4,16,128]{2,1,0:T(8,128)S(1)}, u32[]{:S(2)}, u32[]{:S(2)}) %collective-permute-start.16) | collective-permute-done | bytes 32800 | tf_op jit(solution)/shard_map/ppermute | solution.py:585
  42.9 3.4 %collective-permute-done.18.refs_3_ = f32[4,16,128]{2,1,0:T(8,128)S(1)} collective-permute-done((f32[4,16,128]{2,1,0:T(8,128)S(1)}, f32[4,16,128]{2,1,0:T(8,128)S(1)}, u32[]{:S(2)}, u32[]{:S(2)}) %collective-permute-start.18) | collective-permute-done | bytes 32800 | tf_op jit(solution)/shard_map/ppermute | solution.py:585
  46.4 2.5 %collective-permute-start.20 = (f32[64,128]{1,0:T(8,128)S(1)}, f32[64,128]{1,0:T(8,128)S(1)}, u32[]{:S(2)}, u32[]{:S(2)}) collective-permute-start(f32[64,128]{1,0:T(8,128)S(1)} %get-tuple-element.168), channel_id=1, source_target_pairs={{0,16},{2,18},{4,20},{6,22},{8,24},{10,26},{12,28},{14,30},{16,0},... | collective-permute-start | bytes 98312 | tf_op jit(solution)/shard_map/ppermute | solution.py:585
  48.9 1.9 %collective-permute-start.21 = (f32[64,128]{1,0:T(8,128)S(1)}, f32[64,128]{1,0:T(8,128)S(1)}, u32[]{:S(2)}, u32[]{:S(2)}) collective-permute-start(f32[64,128]{1,0:T(8,128)S(1)} %get-tuple-element.169), channel_id=1, source_target_pairs={{0,24},{2,26},{4,28},{6,30},{8,16},{10,18},{12,20},{14,22},{16,8},... | collective-permute-start | bytes 98312 | tf_op jit(solution)/shard_map/ppermute | solution.py:585
  50.8 1.7 %shard_map.118 = f32[1,6,8,128,128]{4,3,2,1,0:T(8,128)} custom-call(f32[3,9,144,128]{3,2,1,0:T(8,128)S(1)} %get-tuple-element.150.e, f32[3,9,144,128]{3,2,1,0:T(8,128)S(1)} %get-tuple-element.151.h), custom_call_target="tpu_custom_call" | custom-call | bytes 170000 | tf_op jit(solution)/shard_map/pallas_call | solution.py:36
  52.5 2.1 %collective-permute-done.21.refs_3_ = f32[64,128]{1,0:T(8,128)S(1)} collective-permute-done((f32[64,128]{1,0:T(8,128)S(1)}, f32[64,128]{1,0:T(8,128)S(1)}, u32[]{:S(2)}, u32[]{:S(2)}) %collective-permute-start.21) | collective-permute-done | bytes 32800 | tf_op jit(solution)/shard_map/ppermute | solution.py:585
  54.6 0.6 %shard_map.124 = f32[64,128]{1,0:T(8,128)} custom-call(f32[64,128]{1,0:T(8,128)S(1)} %get-tuple-element.166.refs_0_, f32[64,128]{1,0:T(8,128)S(1)} %collective-permute-done.19.refs_1_, f32[64,128]{1,0:T(8,128)S(1)} %collective-permute-done.20.refs_2_, f32[64,128]{1,0:T(8,128)S(1)} %collective-permute-done.21.refs_3_), custom_call_target="tpu_custom_call" | custom-call | bytes 30000 | tf_op jit(solution)/shard_map/pallas_call | solution.py:36
  (46 shorter events, 6.6 us)
Async XLA Ops:
  0.6 12.5 %copy-start = (f32[1,6,8,128,128]{4,3,2,1,0:T(8,128)S(1)}, f32[1,6,8,128,128]{4,3,2,1,0:T(8,128)}, u32[]{:S(2)}) copy-start(f32[1,6,8,128,128]{4,3,2,1,0:T(8,128)} %given.3) | copy-start | bytes 9437188
  0.6 8.6 %collective-permute-start.2 = (f32[64,128]{1,0:T(8,128)}, f32[64,128]{1,0:T(8,128)S(1)}, u32[]{:S(2)}, u32[]{:S(2)}) collective-permute-start(f32[64,128]{1,0:T(8,128)} %bitcast.2), channel_id=1, source_target_pairs={{0,24},{2,26},{4,28},{6,30},{8,16},{10,18},{12,20},{14,22},{16,8},... | collective-permute-start | bytes 98312 | tf_op jit(solution)/shard_map/ppermute | solution.py:585
  5.8 5.0 %collective-permute-start.1 = (f32[64,128]{1,0:T(8,128)}, f32[64,128]{1,0:T(8,128)S(1)}, u32[]{:S(2)}, u32[]{:S(2)}) collective-permute-start(f32[64,128]{1,0:T(8,128)} %bitcast.3), channel_id=1, source_target_pairs={{0,16},{2,18},{4,20},{6,22},{8,24},{10,26},{12,28},{14,30},{16,0},... | collective-permute-start | bytes 98312 | tf_op jit(solution)/shard_map/ppermute | solution.py:585
  5.8 5.0 %collective-permute-start = (f32[64,128]{1,0:T(8,128)}, f32[64,128]{1,0:T(8,128)S(1)}, u32[]{:S(2)}, u32[]{:S(2)}) collective-permute-start(f32[64,128]{1,0:T(8,128)} %bitcast.4), channel_id=1, source_target_pairs={{0,8},{2,10},{4,12},{6,14},{8,0},{10,2},{12,4},{14,6},{16,24},{18,... | collective-permute-start | bytes 98312 | tf_op jit(solution)/shard_map/ppermute | solution.py:585
  7.8 6.5 %copy-start.1 = (f32[1,6,8,128,128]{4,3,2,1,0:T(8,128)S(1)}, f32[1,6,8,128,128]{4,3,2,1,0:T(8,128)}, u32[]{:S(2)}) copy-start(f32[1,6,8,128,128]{4,3,2,1,0:T(8,128)} %given.2) | copy-start | bytes 9437188
  7.8 8.4 %collective-permute-start.3 = (f32[2,2,128,128]{3,2,1,0:T(8,128)S(1)}, f32[2,2,128,128]{3,2,1,0:T(8,128)S(1)}, u32[]{:S(2)}, u32[]{:S(2)}) collective-permute-start(f32[2,2,128,128]{3,2,1,0:T(8,128)S(1)} %get-tuple-element.93), channel_id=1, source_target_pairs={{0,1},{1,0},{2,3},{3,2},{4,5},{5,4},{6,7},{7,6},{8,9},{9,8},{10,11... | collective-permute-start | bytes 786440 | tf_op jit(solution)/shard_map/ppermute | solution.py:585
  10.8 5.0 %collective-permute-start.4 = (f32[4,64,128]{2,1,0:T(8,128)S(1)}, f32[4,64,128]{2,1,0:T(8,128)S(1)}, u32[]{:S(2)}, u32[]{:S(2)}) collective-permute-start(f32[4,64,128]{2,1,0:T(8,128)S(1)} %shard_map.96.near.refs_8_), channel_id=1, source_target_pairs={{0,4},{2,6},{4,0},{6,2},{8,12},{10,14},{12,8},{14,10},{16,20},{18,... | collective-permute-start | bytes 393224 | tf_op jit(solution)/shard_map/ppermute | solution.py:585
  13.0 3.2 %collective-permute-start.5 = (f32[4,64,128]{2,1,0:T(8,128)S(1)}, f32[4,64,128]{2,1,0:T(8,128)S(1)}, u32[]{:S(2)}, u32[]{:S(2)}) collective-permute-start(f32[4,64,128]{2,1,0:T(8,128)S(1)} %shard_map.96.near.refs_8_), channel_id=1, source_target_pairs={{0,2},{2,0},{4,6},{6,4},{8,10},{10,8},{12,14},{14,12},{16,18},{18,... | collective-permute-start | bytes 393224 | tf_op jit(solution)/shard_map/ppermute | solution.py:585
  15.8 1.4 %collective-permute-start.6 = (f32[4,64,128]{2,1,0:T(8,128)S(1)}, f32[4,64,128]{2,1,0:T(8,128)S(1)}, u32[]{:S(2)}, u32[]{:S(2)}) collective-permute-start(f32[4,64,128]{2,1,0:T(8,128)S(1)} %shard_map.99.refs_9_), channel_id=1, source_target_pairs={{0,2},{2,0},{4,6},{6,4},{8,10},{10,8},{12,14},{14,12},{16,18},{18,... | collective-permute-start | bytes 393224 | tf_op jit(solution)/shard_map/ppermute | solution.py:585
  17.5 6.1 %collective-permute-start.7 = (f32[2,128,128]{2,1,0:T(8,128)S(1)}, f32[2,128,128]{2,1,0:T(8,128)S(1)}, u32[]{:S(2)}, u32[]{:S(2)}) collective-permute-start(f32[2,128,128]{2,1,0:T(8,128)S(1)} %get-tuple-element.114), channel_id=1, source_target_pairs={{0,1},{1,0},{2,3},{3,2},{4,5},{5,4},{6,7},{7,6},{8,9},{9,8},{10,11... | collective-permute-start | bytes 393224 | tf_op jit(solution)/shard_map/ppermute | solution.py:585
  20.3 6.4 %collective-permute-start.8 = (f32[2,128,128]{2,1,0:T(8,128)S(1)}, f32[2,128,128]{2,1,0:T(8,128)S(1)}, u32[]{:S(2)}, u32[]{:S(2)}) collective-permute-start(f32[2,128,128]{2,1,0:T(8,128)S(1)} %get-tuple-element.121), channel_id=1, source_target_pairs={{0,1},{1,0},{2,3},{3,2},{4,5},{5,4},{6,7},{7,6},{8,9},{9,8},{10,11... | collective-permute-start | bytes 393224 | tf_op jit(solution)/shard_map/ppermute | solution.py:585
  23.8 5.5 %collective-permute-start.9 = (f32[2,128,128]{2,1,0:T(8,128)S(1)}, f32[2,128,128]{2,1,0:T(8,128)S(1)}, u32[]{:S(2)}, u32[]{:S(2)}) collective-permute-start(f32[2,128,128]{2,1,0:T(8,128)S(1)} %get-tuple-element.128), channel_id=1, source_target_pairs={{0,1},{1,0},{2,3},{3,2},{4,5},{5,4},{6,7},{7,6},{8,9},{9,8},{10,11... | collective-permute-start | bytes 393224 | tf_op jit(solution)/shard_map/ppermute | solution.py:585
  27.0 6.1 %collective-permute-start.10 = (f32[2,128,128]{2,1,0:T(8,128)S(1)}, f32[2,128,128]{2,1,0:T(8,128)S(1)}, u32[]{:S(2)}, u32[]{:S(2)}) collective-permute-start(f32[2,128,128]{2,1,0:T(8,128)S(1)} %get-tuple-element.135), channel_id=1, source_target_pairs={{0,1},{1,0},{2,3},{3,2},{4,5},{5,4},{6,7},{7,6},{8,9},{9,8},{10,11... | collective-permute-start | bytes 393224 | tf_op jit(solution)/shard_map/ppermute | solution.py:585
  29.6 7.4 %collective-permute-start.11 = (f32[2,128,128]{2,1,0:T(8,128)S(1)}, f32[2,128,128]{2,1,0:T(8,128)S(1)}, u32[]{:S(2)}, u32[]{:S(2)}) collective-permute-start(f32[2,128,128]{2,1,0:T(8,128)S(1)} %get-tuple-element.146), channel_id=1, source_target_pairs={{0,1},{1,0},{2,3},{3,2},{4,5},{5,4},{6,7},{7,6},{8,9},{9,8},{10,11... | collective-permute-start | bytes 393224 | tf_op jit(solution)/shard_map/ppermute | solution.py:585
  33.4 5.0 %collective-permute-start.12 = (f32[2,128,128]{2,1,0:T(8,128)S(1)}, f32[2,128,128]{2,1,0:T(8,128)S(1)}, u32[]{:S(2)}, u32[]{:S(2)}) collective-permute-start(f32[2,128,128]{2,1,0:T(8,128)S(1)} %get-tuple-element.149), channel_id=1, source_target_pairs={{0,1},{1,0},{2,3},{3,2},{4,5},{5,4},{6,7},{7,6},{8,9},{9,8},{10,11... | collective-permute-start | bytes 393224 | tf_op jit(solution)/shard_map/ppermute | solution.py:585
  37.8 1.4 %collective-permute-start.13 = (f32[4,48,128]{2,1,0:T(8,128)S(1)}, f32[4,48,128]{2,1,0:T(8,128)S(1)}, u32[]{:S(2)}, u32[]{:S(2)}) collective-permute-start(f32[4,48,128]{2,1,0:T(8,128)S(1)} %get-tuple-element.155), channel_id=1, source_target_pairs={{0,2},{2,0},{4,6},{6,4},{8,10},{10,8},{12,14},{14,12},{16,18},{18,... | collective-permute-start | bytes 294920 | tf_op jit(solution)/shard_map/ppermute | solution.py:585
  37.9 1.4 %collective-permute-start.14 = (f32[4,48,128]{2,1,0:T(8,128)S(1)}, f32[4,48,128]{2,1,0:T(8,128)S(1)}, u32[]{:S(2)}, u32[]{:S(2)}) collective-permute-start(f32[4,48,128]{2,1,0:T(8,128)S(1)} %get-tuple-element.156), channel_id=1, source_target_pairs={{0,2},{2,0},{4,6},{6,4},{8,10},{10,8},{12,14},{14,12},{16,18},{18,... | collective-permute-start | bytes 294920 | tf_op jit(solution)/shard_map/ppermute | solution.py:585
  39.4 6.9 %collective-permute-start.15 = (f32[4,48,128]{2,1,0:T(8,128)S(1)}, f32[4,48,128]{2,1,0:T(8,128)S(1)}, u32[]{:S(2)}, u32[]{:S(2)}) collective-permute-start(f32[4,48,128]{2,1,0:T(8,128)S(1)} %get-tuple-element.160), channel_id=1, source_target_pairs={{0,4},{2,6},{4,0},{6,2},{8,12},{10,14},{12,8},{14,10},{16,20},{18,... | collective-permute-start | bytes 294920 | tf_op jit(solution)/shard_map/ppermute | solution.py:585
  40.9 1.2 %collective-permute-start.16 = (f32[4,16,128]{2,1,0:T(8,128)S(1)}, f32[4,16,128]{2,1,0:T(8,128)S(1)}, u32[]{:S(2)}, u32[]{:S(2)}) collective-permute-start(f32[4,16,128]{2,1,0:T(8,128)S(1)} %get-tuple-element.162), channel_id=1, source_target_pairs={{0,2},{2,0},{4,6},{6,4},{8,10},{10,8},{12,14},{14,12},{16,18},{18,... | collective-permute-start | bytes 98312 | tf_op jit(solution)/shard_map/ppermute | solution.py:585
  41.0 1.3 %collective-permute-start.17 = (f32[4,16,128]{2,1,0:T(8,128)S(1)}, f32[4,16,128]{2,1,0:T(8,128)S(1)}, u32[]{:S(2)}, u32[]{:S(2)}) collective-permute-start(f32[4,16,128]{2,1,0:T(8,128)S(1)} %get-tuple-element.163), channel_id=1, source_target_pairs={{0,2},{2,0},{4,6},{6,4},{8,10},{10,8},{12,14},{14,12},{16,18},{18,... | collective-permute-start | bytes 98312 | tf_op jit(solution)/shard_map/ppermute | solution.py:585
  42.3 4.0 %collective-permute-start.18 = (f32[4,16,128]{2,1,0:T(8,128)S(1)}, f32[4,16,128]{2,1,0:T(8,128)S(1)}, u32[]{:S(2)}, u32[]{:S(2)}) collective-permute-start(f32[4,16,128]{2,1,0:T(8,128)S(1)} %get-tuple-element.165), channel_id=1, source_target_pairs={{0,4},{2,6},{4,0},{6,2},{8,12},{10,14},{12,8},{14,10},{16,20},{18,... | collective-permute-start | bytes 98312 | tf_op jit(solution)/shard_map/ppermute | solution.py:585
  46.3 6.2 %collective-permute-start.19 = (f32[64,128]{1,0:T(8,128)S(1)}, f32[64,128]{1,0:T(8,128)S(1)}, u32[]{:S(2)}, u32[]{:S(2)}) collective-permute-start(f32[64,128]{1,0:T(8,128)S(1)} %get-tuple-element.167), channel_id=1, source_target_pairs={{0,8},{2,10},{4,12},{6,14},{8,0},{10,2},{12,4},{14,6},{16,24},{18,... | collective-permute-start | bytes 98312 | tf_op jit(solution)/shard_map/ppermute | solution.py:585
  46.4 6.1 %collective-permute-start.20 = (f32[64,128]{1,0:T(8,128)S(1)}, f32[64,128]{1,0:T(8,128)S(1)}, u32[]{:S(2)}, u32[]{:S(2)}) collective-permute-start(f32[64,128]{1,0:T(8,128)S(1)} %get-tuple-element.168), channel_id=1, source_target_pairs={{0,16},{2,18},{4,20},{6,22},{8,24},{10,26},{12,28},{14,30},{16,0},... | collective-permute-start | bytes 98312 | tf_op jit(solution)/shard_map/ppermute | solution.py:585
  48.9 5.7 %collective-permute-start.21 = (f32[64,128]{1,0:T(8,128)S(1)}, f32[64,128]{1,0:T(8,128)S(1)}, u32[]{:S(2)}, u32[]{:S(2)}) collective-permute-start(f32[64,128]{1,0:T(8,128)S(1)} %get-tuple-element.169), channel_id=1, source_target_pairs={{0,24},{2,26},{4,28},{6,30},{8,16},{10,18},{12,20},{14,22},{16,8},... | collective-permute-start | bytes 98312 | tf_op jit(solution)/shard_map/ppermute | solution.py:585

commit v12 on v11

--- a/solution.py
+++ b/solution.py
@@ -505,9 +505,9 @@
     lax.fori_loop(1, depth - 1, body, 0, unroll=2)
     fetch.wait()
     inner = pl.ds(0, (depth - 2) * block_rows)
-    for part, masks in zip(parts, layout):
-        for slot, mask in enumerate(masks):
-            part[slot] = blocks[block_ids[me ^ mask], inner, :]
+    for slot, mask in enumerate(mask for masks in layout for mask in masks):
+        part = parts[slot // parts[0].shape[0]]
+        part[slot % part.shape[0]] = blocks[block_ids[me ^ mask], inner, :]
 
 
 def filter_edge_kernel(layout, total, edges, place, *rest):
@@ -533,9 +533,14 @@
             parts[slot // parts[0].shape[0]][slot % parts[0].shape[0], target, :] = value
 
 
-def add_kernel(count, *refs):
-    for a, b, out in zip(refs[:count], refs[count : 2 * count], refs[-count:]):
-        out[...] = a[...] + b[...]
+def add_kernel(pairs, count, *refs):
+    outs = refs[-count:]
+    size, per = refs[0].shape[0], outs[0].shape[0]
+    for pair in range(pairs):
+        kept, got = refs[pair], refs[pairs + pair]
+        for first in range(0, size, per):
+            part = pl.ds(first, per)
+            outs[(pair * size + first) // per][...] = kept[part] + got[part]
 
 
 def join_kernel(count, block_rows, *refs):
@@ -624,26 +629,26 @@
     coef_shape = on_chip(depth, width_x, width_y)
     plane = on_chip(width_x, width_y)
 
-    def by_owner(kernel, layers, operands, specs, scratch, micros):
-        shape = on_chip(far, layers * block_rows, width_y)
+    def by_owner(kernel, layers, operands, specs, scratch, micros, messages):
+        slots = middle * far // messages
         parts = call(
             kernel,
-            [shape] * len(layout),
-            [IN_VMEM] * len(layout),
+            [on_chip(slots, layers * block_rows, width_y)] * (2 * messages),
+            [IN_VMEM] * (2 * messages),
             operands,
             specs,
             scratch,
             micros=micros,
         )
-        return list(parts[:middle]), [swap_over(part, "grp", 1) for part in parts[middle:]]
+        return list(parts[:messages]), [swap_over(part, "grp", 1) for part in parts[messages:]]
 
     def add_middle(kept, got, after):
         sums = call(
-            functools.partial(add_kernel, middle),
-            [on_chip(*part.shape) for part in kept],
+            functools.partial(add_kernel, len(kept), middle),
+            [on_chip(far, *kept[0].shape[1:])] * middle,
             [IN_VMEM] * middle,
             kept + got + after,
-            [IN_VMEM] * (2 * middle + len(after)),
+            [IN_VMEM] * (len(kept + got + after)),
         )
         return [sums[0]] + [
             swap_over(part, "grp", mask) for part, mask in zip(sums[1:], middle_masks[1:])
@@ -764,6 +769,7 @@
                     pltpu.SemaphoreType.DMA,
                 ],
                 0.8,
+                middle,
             )
         if step == 0:
             coef = call(
@@ -816,6 +822,7 @@
             pltpu.VMEM((2, width_x, width_y), F32),
         ],
         0.3,
+        1,
     )
     inner = add_middle(*inner, ends[0][:1])
     ends = add_middle(*ends, [])
@@ -826,7 +833,7 @@
         inner + ends,
         [IN_VMEM] * (2 * middle),
     )
-    got = [swap_over(part, "grp", mask) for part, mask in zip(pieces[1:], far_masks[1:])]
+    got = [swap_over(part, "grp", mask) for part, mask in zip(pieces[:0:-1], far_masks[:0:-1])]
     scale = 3.0 / (STEPS * math.sqrt(ngrp))
     grad = call(
         functools.partial(last_kernel, scale),

time: 55.4 us -> 53.4 us (0.964)
  waiting for transfers between devices: 11.4 us -> 9.39 us
    ppermute x22 -> x21, waiting for transfers between devices: 11.4 us -> 9.39 us  [swap_over(): lax.ppermute(array, axis, [(i, i ^ mask) for i in range(lax.axis_size(axi...]
    ppermute x22 -> x21, starting transfers between devices: 25.2 us -> 25.2 us  [swap_over(): lax.ppermute(array, axis, [(i, i ^ mask) for i in range(lax.axis_size(axi...]
  transfers between devices with their start and end apart: 22 -> 21, of which waited for: 12 -> 10; matrix products, arithmetic and copies ran while one was open for 0% -> 0% of each run, Pallas kernels for 29% -> 30%
where the time goes in v12:
time: 53.4 us; the launch traced here: 53.2 us
  starting transfers between devices  25.2 us (47%)
  Pallas kernels  17 us (32%)
  waiting for transfers between devices  9.39 us (18%)
  between operations  1.56 us (3%)
    ppermute x21, starting transfers between devices, swap_over(): lax.ppermute(array, axis, [(i, i ^ mask) for i in range(lax.axis_size(axi...  25.2 us
    pallas_call x30, Pallas kernels, call(): pl.pallas_call(kernel, out_shape=outs, in_specs=specs, out_specs=out_spec...  17 us
    ppermute x21, waiting for transfers between devices, swap_over(): lax.ppermute(array, axis, [(i, i ^ mask) for i in range(lax.axis_size(axi...  9.39 us
  transfers between devices with their start and end apart: 21, of which 10 were waited for; matrix products, arithmetic and copies ran while one was open for 0% of the time, Pallas kernels for 30%

profile of v12, /device:TPU:0, one launch (start us, length us, event | category | flops | bytes accessed | tf_op | source)
XLA Modules:
  0.0 53.2 jit_solution(73961415463163096)
XLA Ops:
  0.6 5.1 %collective-permute-start.2 = (f32[64,128]{1,0:T(8,128)}, f32[64,128]{1,0:T(8,128)S(1)}, u32[]{:S(2)}, u32[]{:S(2)}) collective-permute-start(f32[64,128]{1,0:T(8,128)} %bitcast.2), channel_id=1, source_target_pairs={{0,24},{2,26},{4,28},{6,30},{8,16},{10,18},{12,20},{14,22},{16,8},... | collective-permute-start | bytes 98312 | tf_op jit(solution)/shard_map/ppermute | solution.py:590
  5.8 0.6 %collective-permute-start = (f32[64,128]{1,0:T(8,128)}, f32[64,128]{1,0:T(8,128)S(1)}, u32[]{:S(2)}, u32[]{:S(2)}) collective-permute-start(f32[64,128]{1,0:T(8,128)} %bitcast.4), channel_id=1, source_target_pairs={{0,8},{2,10},{4,12},{6,14},{8,0},{10,2},{12,4},{14,6},{16,24},{18,... | collective-permute-start | bytes 98312 | tf_op jit(solution)/shard_map/ppermute | solution.py:590
  6.4 1.4 %shard_map.95 = (f32[64,128]{1,0:T(8,128)S(1)}, f32[2,2,128,128]{3,2,1,0:T(8,128)S(1)}) custom-call(f32[1,6,8,128,128]{4,3,2,1,0:T(8,128)} %given.2, f32[1,6,8,128,128]{4,3,2,1,0:T(8,128)} %given.3, f32[64,128]{1,0:T(8,128)} %bitcast.5), custom_call_target="tpu_custom_call" | custom-call | bytes 30000 | tf_op jit(solution)/shard_map/pallas_call | solution.py:36
  7.8 1.4 %collective-permute-start.3 = (f32[2,2,128,128]{3,2,1,0:T(8,128)S(1)}, f32[2,2,128,128]{3,2,1,0:T(8,128)S(1)}, u32[]{:S(2)}, u32[]{:S(2)}) collective-permute-start(f32[2,2,128,128]{3,2,1,0:T(8,128)S(1)} %get-tuple-element.91), channel_id=1, source_target_pairs={{0,1},{1,0},{2,3},{3,2},{4,5},{5,4},{6,7},{7,6},{8,9},{9,8},{10,11... | collective-permute-start | bytes 786440 | tf_op jit(solution)/shard_map/ppermute | solution.py:590
  9.2 1.5 %collective-permute-done.1.refs_2_ = f32[64,128]{1,0:T(8,128)S(1)} collective-permute-done((f32[64,128]{1,0:T(8,128)}, f32[64,128]{1,0:T(8,128)S(1)}, u32[]{:S(2)}, u32[]{:S(2)}) %collective-permute-start.1) | collective-permute-done | bytes 32800 | tf_op jit(solution)/shard_map/ppermute | solution.py:590
  10.8 1.6 %collective-permute-start.4 = (f32[4,64,128]{2,1,0:T(8,128)S(1)}, f32[4,64,128]{2,1,0:T(8,128)S(1)}, u32[]{:S(2)}, u32[]{:S(2)}) collective-permute-start(f32[4,64,128]{2,1,0:T(8,128)S(1)} %shard_map.96.near.refs_8_), channel_id=1, source_target_pairs={{0,4},{2,6},{4,0},{6,2},{8,12},{10,14},{12,8},{14,10},{16,20},{18,... | collective-permute-start | bytes 393224 | tf_op jit(solution)/shard_map/ppermute | solution.py:590
  13.1 1.2 %shard_map.98 = (f32[3,9,144,128]{3,2,1,0:T(8,128)S(1)}, f32[3,9,144,128]{3,2,1,0:T(8,128)S(1)}, f32[3,8,128,128]{3,2,1,0:T(8,128)S(1)}) custom-call(f32[1,6,8,128,128]{4,3,2,1,0:T(8,128)S(1)} %copy-done, f32[4,64,128]{2,1,0:T(8,128)S(1)} %shard_map.96.near.refs_8_), custom_call_target="tpu_custom_call" | custom-call | bytes 120000 | tf_op jit(solution)/shard_map/pallas_call | solution.py:36
  14.3 1.4 %shard_map.97 = (f32[3,9,144,128]{3,2,1,0:T(8,128)S(1)}, f32[3,9,144,128]{3,2,1,0:T(8,128)S(1)}, f32[3,8,128,128]{3,2,1,0:T(8,128)S(1)}, f32[8,144,128]{2,1,0:T(...) custom-call(f32[1,6,8,128,128]{4,3,2,1,0:T(8,128)S(1)} %copy-done.1,, ...), custom_call_target="tpu_custom_call" | custom-call | bytes 150000 | tf_op jit(solution)/shard_map/pallas_call | solution.py:36
  16.2 0.7 %shard_map.100 = (f32[3,9,144,128]{3,2,1,0:T(8,128)S(1)}, f32[3,8,128,128]{3,2,1,0:T(8,128)S(1)}, f32[3,9,144,128]{3,2,1,0:T(8,128)S(1)}, f32[3,8,128,128]{3,2,1,0:T(8,128)S(1)}, f32[16,64,128]{2,1,0:T(8,128)S(1)}) custom-call(f32[3,9,144,128]{3,2,1,0:T(8,128)S(1)} %get-tuple-element.86.refs_, ...), custom_call_target="tpu_custom_call", output_to_operand_aliasing={{0}: (0, {}), {1}: (1, {}), {2}: (2, {}), {3}: (3, {})} | custom-call | bytes 60000 | tf_op jit(solution)/shard_map/pallas_call | solution.py:36
  17.5 1.5 %collective-permute-start.7 = (f32[2,128,128]{2,1,0:T(8,128)S(1)}, f32[2,128,128]{2,1,0:T(8,128)S(1)}, u32[]{:S(2)}, u32[]{:S(2)}) collective-permute-start(f32[2,128,128]{2,1,0:T(8,128)S(1)} %get-tuple-element.112), channel_id=1, source_target_pairs={{0,1},{1,0},{2,3},{3,2},{4,5},{5,4},{6,7},{7,6},{8,9},{9,8},{10,11... | collective-permute-start | bytes 393224 | tf_op jit(solution)/shard_map/ppermute | solution.py:590
  19.0 0.6 %shard_map.103.coef.refs_4_.refs_2_ = f32[8,128,128]{2,1,0:T(8,128)S(1)} custom-call(f32[8,128,128]{2,1,0:T(8,128)S(1)} %shard_map.101.refs_2_.coef_in, f32[4,64,128]{2,1,0:T(8,128)S(1)} %collective-permute-done.6.refs_0_, f32[16,16,128]{2,1,0:T(8,128)S(1)} %get-tuple-element.93.refs_1_.place, ...), custom_call_target="tpu_custom_call", output_to_operand_aliasing={{}: (0, {})} | custom-call | bytes 60000 | tf_op jit(solution)/shard_map/pallas_call | solution.py:36
  20.9 0.9 %shard_map.106 = (f32[3,9,144,128]{3,2,1,0:T(8,128)S(1)}, f32[3,9,144,128]{3,2,1,0:T(8,128)S(1)}) custom-call(f32[3,9,144,128]{3,2,1,0:T(8,128)S(1)} %get-tuple-element.108.refs_0_, f32[3,9,144,128]{3,2,1,0:T(8,128)S(1)} %get-tuple-element.109.refs_1_, ...), custom_call_target="tpu_custom_call", output_to_operand_aliasing={{0}: (0, {}), {1}: (1, {})} | custom-call | bytes 110000 | tf_op jit(solution)/shard_map/pallas_call | solution.py:36
  21.9 1.7 %collective-permute-done.7.refs_5_.refs_6_ = f32[2,128,128]{2,1,0:T(8,128)S(1)} collective-permute-done((f32[2,128,128]{2,1,0:T(8,128)S(1)}, f32[2,128,128]{2,1,0:T(8,128)S(1)}, u32[]{:S(2)}, u32[]{:S(2)}) %collective-permute-start.7) | collective-permute-done | bytes 131104 | tf_op jit(solution)/shard_map/ppermute | solution.py:590
  23.8 1.7 %collective-permute-start.9 = (f32[2,128,128]{2,1,0:T(8,128)S(1)}, f32[2,128,128]{2,1,0:T(8,128)S(1)}, u32[]{:S(2)}, u32[]{:S(2)}) collective-permute-start(f32[2,128,128]{2,1,0:T(8,128)S(1)} %get-tuple-element.126), channel_id=1, source_target_pairs={{0,1},{1,0},{2,3},{3,2},{4,5},{5,4},{6,7},{7,6},{8,9},{9,8},{10,11... | collective-permute-start | bytes 393224 | tf_op jit(solution)/shard_map/ppermute | solution.py:590
  25.6 1.2 %shard_map.108 = (f32[3,9,144,128]{3,2,1,0:T(8,128)S(1)}, f32[3,9,144,128]{3,2,1,0:T(8,128)S(1)}, f32[3,9,144,128]{3,2,1,0:T(8,128)S(1)}, f32[8,144,128]{2,1,0:T(8,128)S(1)}) custom-call(f32[3,9,144,128]{3,2,1,0:T(8,128)S(1)} %get-tuple-element.106.refs_0_, ...), custom_call_target="tpu_custom_call", output_to_operand_aliasing={{0}: (0, {}), {1}: (1, {}), {2}: (2, {}), {3}: (3, {})} | custom-call | bytes 120000 | tf_op jit(solution)/shard_map/pallas_call | solution.py:36
  27.0 1.2 %collective-permute-start.10 = (f32[2,128,128]{2,1,0:T(8,128)S(1)}, f32[2,128,128]{2,1,0:T(8,128)S(1)}, u32[]{:S(2)}, u32[]{:S(2)}) collective-permute-start(f32[2,128,128]{2,1,0:T(8,128)S(1)} %get-tuple-element.133), channel_id=1, source_target_pairs={{0,1},{1,0},{2,3},{3,2},{4,5},{5,4},{6,7},{7,6},{8,9},{9,8},{10,11... | collective-permute-start | bytes 393224 | tf_op jit(solution)/shard_map/ppermute | solution.py:590
  28.2 0.9 %shard_map.110 = (f32[3,9,144,128]{3,2,1,0:T(8,128)S(1)}, f32[3,9,144,128]{3,2,1,0:T(8,128)S(1)}) custom-call(f32[3,9,144,128]{3,2,1,0:T(8,128)S(1)} %get-tuple-element.122.refs_0_, f32[3,9,144,128]{3,2,1,0:T(8,128)S(1)} %get-tuple-element.123.refs_1_, ...), custom_call_target="tpu_custom_call", output_to_operand_aliasing={{0}: (0, {}), {1}: (1, {})} | custom-call | bytes 110000 | tf_op jit(solution)/shard_map/pallas_call | solution.py:36
  29.6 1.7 %collective-permute-start.11 = (f32[2,128,128]{2,1,0:T(8,128)S(1)}, f32[2,128,128]{2,1,0:T(8,128)S(1)}, u32[]{:S(2)}, u32[]{:S(2)}) collective-permute-start(f32[2,128,128]{2,1,0:T(8,128)S(1)} %get-tuple-element.144), channel_id=1, source_target_pairs={{0,1},{1,0},{2,3},{3,2},{4,5},{5,4},{6,7},{7,6},{8,9},{9,8},{10,11... | collective-permute-start | bytes 393224 | tf_op jit(solution)/shard_map/ppermute | solution.py:590
  31.3 1.2 %shard_map.112 = (f32[3,9,144,128]{3,2,1,0:T(8,128)S(1)}, f32[3,9,144,128]{3,2,1,0:T(8,128)S(1)}, f32[3,9,144,128]{3,2,1,0:T(8,128)S(1)}, f32[8,144,128]{2,1,0:T(8,128)S(1)}) custom-call(f32[3,9,144,128]{3,2,1,0:T(8,128)S(1)} %get-tuple-element.120.refs_0_, ...), custom_call_target="tpu_custom_call", output_to_operand_aliasing={{0}: (0, {}), {1}: (1, {}), {2}: (2, {}), {3}: (3, {})} | custom-call | bytes 120000 | tf_op jit(solution)/shard_map/pallas_call | solution.py:36
  32.5 0.6 %collective-permute-done.10.refs_5_.refs_6_ = f32[2,128,128]{2,1,0:T(8,128)S(1)} collective-permute-done((f32[2,128,128]{2,1,0:T(8,128)S(1)}, f32[2,128,128]{2,1,0:T(8,128)S(1)}, u32[]{:S(2)}, u32[]{:S(2)}) %collective-permute-start.10) | collective-permute-done | bytes 131104 | tf_op jit(solution)/shard_map/ppermute | solution.py:590
  33.4 1.5 %collective-permute-start.12 = (f32[2,128,128]{2,1,0:T(8,128)S(1)}, f32[2,128,128]{2,1,0:T(8,128)S(1)}, u32[]{:S(2)}, u32[]{:S(2)}) collective-permute-start(f32[2,128,128]{2,1,0:T(8,128)S(1)} %get-tuple-element.147), channel_id=1, source_target_pairs={{0,1},{1,0},{2,3},{3,2},{4,5},{5,4},{6,7},{7,6},{8,9},{9,8},{10,11... | collective-permute-start | bytes 393224 | tf_op jit(solution)/shard_map/ppermute | solution.py:590
  34.8 0.9 %shard_map.114 = (f32[3,9,144,128]{3,2,1,0:T(8,128)S(1)}, f32[3,9,144,128]{3,2,1,0:T(8,128)S(1)}) custom-call(f32[3,9,144,128]{3,2,1,0:T(8,128)S(1)} %get-tuple-element.136.refs_0_, f32[3,9,144,128]{3,2,1,0:T(8,128)S(1)} %get-tuple-element.137.refs_1_, ...), custom_call_target="tpu_custom_call", output_to_operand_aliasing={{0}: (0, {}), {1}: (1, {})} | custom-call | bytes 110000 | tf_op jit(solution)/shard_map/pallas_call | solution.py:36
  35.8 1.2 %shard_map.115 = (f32[3,9,144,128]{3,2,1,0:T(8,128)S(1)}, f32[3,9,144,128]{3,2,1,0:T(8,128)S(1)}, f32[3,9,144,128]{3,2,1,0:T(8,128)S(1)}, f32[8,144,128]{2,1,0:T(8,128)S(1)}) custom-call(f32[3,9,144,128]{3,2,1,0:T(8,128)S(1)} %get-tuple-element.134.refs_0_, ...), custom_call_target="tpu_custom_call", output_to_operand_aliasing={{0}: (0, {}), {1}: (1, {}), {2}: (2, {}), {3}: (3, {})} | custom-call | bytes 120000 | tf_op jit(solution)/shard_map/pallas_call | solution.py:36
  37.1 0.7 %shard_map.119 = (f32[4,48,128]{2,1,0:T(8,128)S(1)}, f32[4,48,128]{2,1,0:T(8,128)S(1)}, f32[4,48,128]{2,1,0:T(8,128)S(1)}, f32[4,48,128]{2,1,0:T(8,128)S(1)}) custom-call(f32[8,144,128]{2,1,0:T(8,128)S(1)} %get-tuple-element.150.total, f32[3,9,144,128]{3,2,1,0:T(8,128)S(1)} %get-tuple-element.145.refs_2_.after, s32[16]{0:T(128)} %block_ids_far.1), custom_call_target="tpu_custom_call" | custom-call | bytes 80000 | tf_op jit(solution)/shard_map/pallas_call | solution.py:36
  39.4 1.6 %collective-permute-start.15 = (f32[4,48,128]{2,1,0:T(8,128)S(1)}, f32[4,48,128]{2,1,0:T(8,128)S(1)}, u32[]{:S(2)}, u32[]{:S(2)}) collective-permute-start(f32[4,48,128]{2,1,0:T(8,128)S(1)} %get-tuple-element.158), channel_id=1, source_target_pairs={{0,4},{2,6},{4,0},{6,2},{8,12},{10,14},{12,8},{14,10},{16,20},{18,... | collective-permute-start | bytes 294920 | tf_op jit(solution)/shard_map/ppermute | solution.py:590
  40.9 0.9 %collective-permute-start.17 = (f32[4,16,128]{2,1,0:T(8,128)S(1)}, f32[4,16,128]{2,1,0:T(8,128)S(1)}, u32[]{:S(2)}, u32[]{:S(2)}) collective-permute-start(f32[4,16,128]{2,1,0:T(8,128)S(1)} %get-tuple-element.161), channel_id=1, source_target_pairs={{0,4},{2,6},{4,0},{6,2},{8,12},{10,14},{12,8},{14,10},{16,20},{18,... | collective-permute-start | bytes 98312 | tf_op jit(solution)/shard_map/ppermute | solution.py:590
  41.9 3.3 %collective-permute-done.17.refs_3_ = f32[4,16,128]{2,1,0:T(8,128)S(1)} collective-permute-done((f32[4,16,128]{2,1,0:T(8,128)S(1)}, f32[4,16,128]{2,1,0:T(8,128)S(1)}, u32[]{:S(2)}, u32[]{:S(2)}) %collective-permute-start.17) | collective-permute-done | bytes 32800 | tf_op jit(solution)/shard_map/ppermute | solution.py:590
  45.2 2.2 %collective-permute-start.18 = (f32[64,128]{1,0:T(8,128)S(1)}, f32[64,128]{1,0:T(8,128)S(1)}, u32[]{:S(2)}, u32[]{:S(2)}) collective-permute-start(f32[64,128]{1,0:T(8,128)S(1)} %get-tuple-element.163), channel_id=1, source_target_pairs={{0,24},{2,26},{4,28},{6,30},{8,16},{10,18},{12,20},{14,22},{16,8},... | collective-permute-start | bytes 98312 | tf_op jit(solution)/shard_map/ppermute | solution.py:590
  47.5 2.2 %collective-permute-start.20 = (f32[64,128]{1,0:T(8,128)S(1)}, f32[64,128]{1,0:T(8,128)S(1)}, u32[]{:S(2)}, u32[]{:S(2)}) collective-permute-start(f32[64,128]{1,0:T(8,128)S(1)} %get-tuple-element.165), channel_id=1, source_target_pairs={{0,8},{2,10},{4,12},{6,14},{8,0},{10,2},{12,4},{14,6},{16,24},{18,... | collective-permute-start | bytes 98312 | tf_op jit(solution)/shard_map/ppermute | solution.py:590
  49.7 1.7 %shard_map.118 = f32[1,6,8,128,128]{4,3,2,1,0:T(8,128)} custom-call(f32[3,9,144,128]{3,2,1,0:T(8,128)S(1)} %get-tuple-element.148.e, f32[3,9,144,128]{3,2,1,0:T(8,128)S(1)} %get-tuple-element.149.h), custom_call_target="tpu_custom_call" | custom-call | bytes 170000 | tf_op jit(solution)/shard_map/pallas_call | solution.py:36
  51.4 1.1 %collective-permute-done.19.refs_2_ = f32[64,128]{1,0:T(8,128)S(1)} collective-permute-done((f32[64,128]{1,0:T(8,128)S(1)}, f32[64,128]{1,0:T(8,128)S(1)}, u32[]{:S(2)}, u32[]{:S(2)}) %collective-permute-start.19) | collective-permute-done | bytes 32800 | tf_op jit(solution)/shard_map/ppermute | solution.py:590
  52.5 0.6 %shard_map.124 = f32[64,128]{1,0:T(8,128)} custom-call(f32[64,128]{1,0:T(8,128)S(1)} %get-tuple-element.162.refs_0_, f32[64,128]{1,0:T(8,128)S(1)} %collective-permute-done.18.refs_1_, f32[64,128]{1,0:T(8,128)S(1)} %collective-permute-done.19.refs_2_, f32[64,128]{1,0:T(8,128)S(1)} %collective-permute-done.20.refs_3_), custom_call_target="tpu_custom_call" | custom-call | bytes 30000 | tf_op jit(solution)/shard_map/pallas_call | solution.py:36
  (44 shorter events, 5.3 us)
Async XLA Ops:
  0.6 12.5 %copy-start = (f32[1,6,8,128,128]{4,3,2,1,0:T(8,128)S(1)}, f32[1,6,8,128,128]{4,3,2,1,0:T(8,128)}, u32[]{:S(2)}) copy-start(f32[1,6,8,128,128]{4,3,2,1,0:T(8,128)} %given.3) | copy-start | bytes 9437188
  0.6 8.6 %collective-permute-start.2 = (f32[64,128]{1,0:T(8,128)}, f32[64,128]{1,0:T(8,128)S(1)}, u32[]{:S(2)}, u32[]{:S(2)}) collective-permute-start(f32[64,128]{1,0:T(8,128)} %bitcast.2), channel_id=1, source_target_pairs={{0,24},{2,26},{4,28},{6,30},{8,16},{10,18},{12,20},{14,22},{16,8},... | collective-permute-start | bytes 98312 | tf_op jit(solution)/shard_map/ppermute | solution.py:590
  5.8 5.0 %collective-permute-start.1 = (f32[64,128]{1,0:T(8,128)}, f32[64,128]{1,0:T(8,128)S(1)}, u32[]{:S(2)}, u32[]{:S(2)}) collective-permute-start(f32[64,128]{1,0:T(8,128)} %bitcast.3), channel_id=1, source_target_pairs={{0,16},{2,18},{4,20},{6,22},{8,24},{10,26},{12,28},{14,30},{16,0},... | collective-permute-start | bytes 98312 | tf_op jit(solution)/shard_map/ppermute | solution.py:590
  5.8 5.0 %collective-permute-start = (f32[64,128]{1,0:T(8,128)}, f32[64,128]{1,0:T(8,128)S(1)}, u32[]{:S(2)}, u32[]{:S(2)}) collective-permute-start(f32[64,128]{1,0:T(8,128)} %bitcast.4), channel_id=1, source_target_pairs={{0,8},{2,10},{4,12},{6,14},{8,0},{10,2},{12,4},{14,6},{16,24},{18,... | collective-permute-start | bytes 98312 | tf_op jit(solution)/shard_map/ppermute | solution.py:590
  7.8 6.5 %copy-start.1 = (f32[1,6,8,128,128]{4,3,2,1,0:T(8,128)S(1)}, f32[1,6,8,128,128]{4,3,2,1,0:T(8,128)}, u32[]{:S(2)}) copy-start(f32[1,6,8,128,128]{4,3,2,1,0:T(8,128)} %given.2) | copy-start | bytes 9437188
  7.8 8.4 %collective-permute-start.3 = (f32[2,2,128,128]{3,2,1,0:T(8,128)S(1)}, f32[2,2,128,128]{3,2,1,0:T(8,128)S(1)}, u32[]{:S(2)}, u32[]{:S(2)}) collective-permute-start(f32[2,2,128,128]{3,2,1,0:T(8,128)S(1)} %get-tuple-element.91), channel_id=1, source_target_pairs={{0,1},{1,0},{2,3},{3,2},{4,5},{5,4},{6,7},{7,6},{8,9},{9,8},{10,11... | collective-permute-start | bytes 786440 | tf_op jit(solution)/shard_map/ppermute | solution.py:590
  10.8 5.0 %collective-permute-start.4 = (f32[4,64,128]{2,1,0:T(8,128)S(1)}, f32[4,64,128]{2,1,0:T(8,128)S(1)}, u32[]{:S(2)}, u32[]{:S(2)}) collective-permute-start(f32[4,64,128]{2,1,0:T(8,128)S(1)} %shard_map.96.near.refs_8_), channel_id=1, source_target_pairs={{0,4},{2,6},{4,0},{6,2},{8,12},{10,14},{12,8},{14,10},{16,20},{18,... | collective-permute-start | bytes 393224 | tf_op jit(solution)/shard_map/ppermute | solution.py:590
  13.0 3.2 %collective-permute-start.5 = (f32[4,64,128]{2,1,0:T(8,128)S(1)}, f32[4,64,128]{2,1,0:T(8,128)S(1)}, u32[]{:S(2)}, u32[]{:S(2)}) collective-permute-start(f32[4,64,128]{2,1,0:T(8,128)S(1)} %shard_map.96.near.refs_8_), channel_id=1, source_target_pairs={{0,2},{2,0},{4,6},{6,4},{8,10},{10,8},{12,14},{14,12},{16,18},{18,... | collective-permute-start | bytes 393224 | tf_op jit(solution)/shard_map/ppermute | solution.py:590
  15.8 1.4 %collective-permute-start.6 = (f32[4,64,128]{2,1,0:T(8,128)S(1)}, f32[4,64,128]{2,1,0:T(8,128)S(1)}, u32[]{:S(2)}, u32[]{:S(2)}) collective-permute-start(f32[4,64,128]{2,1,0:T(8,128)S(1)} %shard_map.99.refs_9_), channel_id=1, source_target_pairs={{0,2},{2,0},{4,6},{6,4},{8,10},{10,8},{12,14},{14,12},{16,18},{18,... | collective-permute-start | bytes 393224 | tf_op jit(solution)/shard_map/ppermute | solution.py:590
  17.5 6.1 %collective-permute-start.7 = (f32[2,128,128]{2,1,0:T(8,128)S(1)}, f32[2,128,128]{2,1,0:T(8,128)S(1)}, u32[]{:S(2)}, u32[]{:S(2)}) collective-permute-start(f32[2,128,128]{2,1,0:T(8,128)S(1)} %get-tuple-element.112), channel_id=1, source_target_pairs={{0,1},{1,0},{2,3},{3,2},{4,5},{5,4},{6,7},{7,6},{8,9},{9,8},{10,11... | collective-permute-start | bytes 393224 | tf_op jit(solution)/shard_map/ppermute | solution.py:590
  20.3 6.4 %collective-permute-start.8 = (f32[2,128,128]{2,1,0:T(8,128)S(1)}, f32[2,128,128]{2,1,0:T(8,128)S(1)}, u32[]{:S(2)}, u32[]{:S(2)}) collective-permute-start(f32[2,128,128]{2,1,0:T(8,128)S(1)} %get-tuple-element.119), channel_id=1, source_target_pairs={{0,1},{1,0},{2,3},{3,2},{4,5},{5,4},{6,7},{7,6},{8,9},{9,8},{10,11... | collective-permute-start | bytes 393224 | tf_op jit(solution)/shard_map/ppermute | solution.py:590
  23.8 5.5 %collective-permute-start.9 = (f32[2,128,128]{2,1,0:T(8,128)S(1)}, f32[2,128,128]{2,1,0:T(8,128)S(1)}, u32[]{:S(2)}, u32[]{:S(2)}) collective-permute-start(f32[2,128,128]{2,1,0:T(8,128)S(1)} %get-tuple-element.126), channel_id=1, source_target_pairs={{0,1},{1,0},{2,3},{3,2},{4,5},{5,4},{6,7},{7,6},{8,9},{9,8},{10,11... | collective-permute-start | bytes 393224 | tf_op jit(solution)/shard_map/ppermute | solution.py:590
  27.0 6.1 %collective-permute-start.10 = (f32[2,128,128]{2,1,0:T(8,128)S(1)}, f32[2,128,128]{2,1,0:T(8,128)S(1)}, u32[]{:S(2)}, u32[]{:S(2)}) collective-permute-start(f32[2,128,128]{2,1,0:T(8,128)S(1)} %get-tuple-element.133), channel_id=1, source_target_pairs={{0,1},{1,0},{2,3},{3,2},{4,5},{5,4},{6,7},{7,6},{8,9},{9,8},{10,11... | collective-permute-start | bytes 393224 | tf_op jit(solution)/shard_map/ppermute | solution.py:590
  29.6 7.4 %collective-permute-start.11 = (f32[2,128,128]{2,1,0:T(8,128)S(1)}, f32[2,128,128]{2,1,0:T(8,128)S(1)}, u32[]{:S(2)}, u32[]{:S(2)}) collective-permute-start(f32[2,128,128]{2,1,0:T(8,128)S(1)} %get-tuple-element.144), channel_id=1, source_target_pairs={{0,1},{1,0},{2,3},{3,2},{4,5},{5,4},{6,7},{7,6},{8,9},{9,8},{10,11... | collective-permute-start | bytes 393224 | tf_op jit(solution)/shard_map/ppermute | solution.py:590
  33.4 5.0 %collective-permute-start.12 = (f32[2,128,128]{2,1,0:T(8,128)S(1)}, f32[2,128,128]{2,1,0:T(8,128)S(1)}, u32[]{:S(2)}, u32[]{:S(2)}) collective-permute-start(f32[2,128,128]{2,1,0:T(8,128)S(1)} %get-tuple-element.147), channel_id=1, source_target_pairs={{0,1},{1,0},{2,3},{3,2},{4,5},{5,4},{6,7},{7,6},{8,9},{9,8},{10,11... | collective-permute-start | bytes 393224 | tf_op jit(solution)/shard_map/ppermute | solution.py:590
  37.8 1.4 %collective-permute-start.13 = (f32[4,48,128]{2,1,0:T(8,128)S(1)}, f32[4,48,128]{2,1,0:T(8,128)S(1)}, u32[]{:S(2)}, u32[]{:S(2)}) collective-permute-start(f32[4,48,128]{2,1,0:T(8,128)S(1)} %get-tuple-element.153), channel_id=1, source_target_pairs={{0,2},{2,0},{4,6},{6,4},{8,10},{10,8},{12,14},{14,12},{16,18},{18,... | collective-permute-start | bytes 294920 | tf_op jit(solution)/shard_map/ppermute | solution.py:590
  37.9 1.4 %collective-permute-start.14 = (f32[4,48,128]{2,1,0:T(8,128)S(1)}, f32[4,48,128]{2,1,0:T(8,128)S(1)}, u32[]{:S(2)}, u32[]{:S(2)}) collective-permute-start(f32[4,48,128]{2,1,0:T(8,128)S(1)} %get-tuple-element.154), channel_id=1, source_target_pairs={{0,2},{2,0},{4,6},{6,4},{8,10},{10,8},{12,14},{14,12},{16,18},{18,... | collective-permute-start | bytes 294920 | tf_op jit(solution)/shard_map/ppermute | solution.py:590
  38.8 2.1 %collective-permute-start.16 = (f32[8,16,128]{2,1,0:T(8,128)S(1)}, f32[8,16,128]{2,1,0:T(8,128)S(1)}, u32[]{:S(2)}, u32[]{:S(2)}) collective-permute-start(f32[8,16,128]{2,1,0:T(8,128)S(1)} %get-tuple-element.159), channel_id=1, source_target_pairs={{0,2},{2,0},{4,6},{6,4},{8,10},{10,8},{12,14},{14,12},{16,18},{18,... | collective-permute-start | bytes 196616 | tf_op jit(solution)/shard_map/ppermute | solution.py:590
  39.4 5.8 %collective-permute-start.15 = (f32[4,48,128]{2,1,0:T(8,128)S(1)}, f32[4,48,128]{2,1,0:T(8,128)S(1)}, u32[]{:S(2)}, u32[]{:S(2)}) collective-permute-start(f32[4,48,128]{2,1,0:T(8,128)S(1)} %get-tuple-element.158), channel_id=1, source_target_pairs={{0,4},{2,6},{4,0},{6,2},{8,12},{10,14},{12,8},{14,10},{16,20},{18,... | collective-permute-start | bytes 294920 | tf_op jit(solution)/shard_map/ppermute | solution.py:590
  40.9 4.2 %collective-permute-start.17 = (f32[4,16,128]{2,1,0:T(8,128)S(1)}, f32[4,16,128]{2,1,0:T(8,128)S(1)}, u32[]{:S(2)}, u32[]{:S(2)}) collective-permute-start(f32[4,16,128]{2,1,0:T(8,128)S(1)} %get-tuple-element.161), channel_id=1, source_target_pairs={{0,4},{2,6},{4,0},{6,2},{8,12},{10,14},{12,8},{14,10},{16,20},{18,... | collective-permute-start | bytes 98312 | tf_op jit(solution)/shard_map/ppermute | solution.py:590
  45.2 6.2 %collective-permute-start.18 = (f32[64,128]{1,0:T(8,128)S(1)}, f32[64,128]{1,0:T(8,128)S(1)}, u32[]{:S(2)}, u32[]{:S(2)}) collective-permute-start(f32[64,128]{1,0:T(8,128)S(1)} %get-tuple-element.163), channel_id=1, source_target_pairs={{0,24},{2,26},{4,28},{6,30},{8,16},{10,18},{12,20},{14,22},{16,8},... | collective-permute-start | bytes 98312 | tf_op jit(solution)/shard_map/ppermute | solution.py:590
  47.4 5.1 %collective-permute-start.19 = (f32[64,128]{1,0:T(8,128)S(1)}, f32[64,128]{1,0:T(8,128)S(1)}, u32[]{:S(2)}, u32[]{:S(2)}) collective-permute-start(f32[64,128]{1,0:T(8,128)S(1)} %get-tuple-element.164), channel_id=1, source_target_pairs={{0,16},{2,18},{4,20},{6,22},{8,24},{10,26},{12,28},{14,30},{16,0},... | collective-permute-start | bytes 98312 | tf_op jit(solution)/shard_map/ppermute | solution.py:590
  47.5 5.1 %collective-permute-start.20 = (f32[64,128]{1,0:T(8,128)S(1)}, f32[64,128]{1,0:T(8,128)S(1)}, u32[]{:S(2)}, u32[]{:S(2)}) collective-permute-start(f32[64,128]{1,0:T(8,128)S(1)} %get-tuple-element.165), channel_id=1, source_target_pairs={{0,8},{2,10},{4,12},{6,14},{8,0},{10,2},{12,4},{14,6},{16,24},{18,... | collective-permute-start | bytes 98312 | tf_op jit(solution)/shard_map/ppermute | solution.py:590

commit v13 on v12

--- a/solution.py
+++ b/solution.py
@@ -544,9 +544,11 @@
 
 
 def join_kernel(count, block_rows, *refs):
-    inner, edge, outs = refs[:count], refs[count : 2 * count], refs[2 * count :]
-    rows = outs[0].shape[0]
-    for slot, out in enumerate(outs):
+    inner, edge, joined = refs[:count], refs[count : 2 * count], refs[2 * count]
+    rows = joined.shape[1]
+    mine = lax.axis_index("grp") // (2 * count)
+    for slot in range(joined.shape[0]):
+        out = joined.at[mine ^ slot]
         middle, ends = inner[0][slot], edge[0][slot]
         for a, b in zip(inner[1:], edge[1:]):
             middle, ends = middle + a[slot], ends + b[slot]
@@ -555,11 +557,11 @@
         out[pl.ds(rows - block_rows, block_rows), :] = ends[block_rows:]
 
 
-def last_kernel(scale, *refs):
-    value = refs[0][...]
-    for ref in refs[1:-1]:
-        value = value + ref[...]
-    refs[-1][...] = value * scale
+def last_kernel(scale, got, out):
+    value = got[0]
+    for slot in range(1, got.shape[0]):
+        value = value + got[slot]
+    out[...] = value * scale
 
 
 def out_kernel(e, h, finals, halves, sems):
@@ -826,21 +828,22 @@
     )
     inner = add_middle(*inner, ends[0][:1])
     ends = add_middle(*ends, [])
-    pieces = call(
+    joined = call(
         functools.partial(join_kernel, middle, block_rows),
-        [on_chip(*piece)] * far,
-        [IN_VMEM] * far,
+        on_chip(*group),
+        IN_VMEM,
         inner + ends,
         [IN_VMEM] * (2 * middle),
     )
-    got = [swap_over(part, "grp", mask) for part, mask in zip(pieces[:0:-1], far_masks[:0:-1])]
+    lines = [[step * 2 * middle + line for step in range(far)] for line in range(2 * middle)]
+    got = lax.all_to_all(joined, "grp", 0, 0, axis_index_groups=lines)
     scale = 3.0 / (STEPS * math.sqrt(ngrp))
     grad = call(
         functools.partial(last_kernel, scale),
         jax.ShapeDtypeStruct(piece, F32),
         IN_VMEM,
-        [pieces[0]] + got,
-        [IN_VMEM] * far,
+        [got],
+        [IN_VMEM],
     )
     finals = call(
         out_kernel,

time: 53.4 us -> 56.3 us (1.054)
  local copies, waits for them, and re-layouts: 0.01 us -> 1.57 us
  waiting for transfers between devices: 9.39 us -> 10.6 us
  Pallas kernels: 17 us -> 17.8 us
  starting transfers between devices: 25.2 us -> 24.5 us
    ppermute x21 -> x18, starting transfers between devices: 25.2 us -> 21.1 us  [swap_over(): lax.ppermute(array, axis, [(i, i ^ mask) for i in range(lax.axis_size(axi...]
    all_to_all x0 -> x1, starting transfers between devices: none -> 3.38 us  [per_device(): got = lax.all_to_all(joined, 'grp', 0, 0, axis_index_groups=lines)]
    all_to_all x0 -> x1, waiting for transfers between devices: none -> 2.81 us  [per_device(): got = lax.all_to_all(joined, 'grp', 0, 0, axis_index_groups=lines)]
    ppermute x21 -> x18, waiting for transfers between devices: 9.39 us -> 7.8 us  [swap_over(): lax.ppermute(array, axis, [(i, i ^ mask) for i in range(lax.axis_size(axi...]
    unnamed x4 -> x8, local copies, waits for them, and re-layouts: 0.01 us -> 1.57 us
    pallas_call x30, Pallas kernels: 17 us -> 17.8 us  [call(): pl.pallas_call(kernel, out_shape=outs, in_specs=specs, out_specs=out_spec...]
  transfers between devices with their start and end apart: 21 -> 19, of which waited for: 10 -> 10; matrix products, arithmetic and copies ran while one was open for 0% -> 0% of each run, Pallas kernels for 30% -> 29%
where the time goes in v13:
time: 56.3 us; the launch traced here: 56 us
  starting transfers between devices  24.5 us (44%)
  Pallas kernels  17.8 us (32%)
  waiting for transfers between devices  10.6 us (19%)
  local copies, waits for them, and re-layouts  1.57 us (3%)
  between operations  1.57 us (3%)
    ppermute x18, starting transfers between devices, swap_over(): lax.ppermute(array, axis, [(i, i ^ mask) for i in range(lax.axis_size(axi...  21.1 us
    pallas_call x30, Pallas kernels, call(): pl.pallas_call(kernel, out_shape=outs, in_specs=specs, out_specs=out_spec...  17.8 us
    ppermute x18, waiting for transfers between devices, swap_over(): lax.ppermute(array, axis, [(i, i ^ mask) for i in range(lax.axis_size(axi...  7.8 us
    all_to_all x1, starting transfers between devices, per_device(): got = lax.all_to_all(joined, 'grp', 0, 0, axis_index_groups=lines)  3.38 us
    all_to_all x1, waiting for transfers between devices, per_device(): got = lax.all_to_all(joined, 'grp', 0, 0, axis_index_groups=lines)  2.81 us
    unnamed x8, local copies, waits for them, and re-layouts  1.57 us
  transfers between devices with their start and end apart: 19, of which 10 were waited for; matrix products, arithmetic and copies ran while one was open for 0% of the time, Pallas kernels for 29%

profile of v13, /device:TPU:0, one launch (start us, length us, event | category | flops | bytes accessed | tf_op | source)
XLA Modules:
  0.0 56.0 jit_solution(9472546424698713583)
XLA Ops:
  0.6 5.1 %collective-permute-start.2 = (f32[64,128]{1,0:T(8,128)}, f32[64,128]{1,0:T(8,128)S(1)}, u32[]{:S(2)}, u32[]{:S(2)}) collective-permute-start(f32[64,128]{1,0:T(8,128)} %bitcast.2), channel_id=1, source_target_pairs={{0,24},{2,26},{4,28},{6,30},{8,16},{10,18},{12,20},{14,22},{16,8},... | collective-permute-start | bytes 98312 | tf_op jit(solution)/shard_map/ppermute | solution.py:592
  5.8 0.6 %collective-permute-start = (f32[64,128]{1,0:T(8,128)}, f32[64,128]{1,0:T(8,128)S(1)}, u32[]{:S(2)}, u32[]{:S(2)}) collective-permute-start(f32[64,128]{1,0:T(8,128)} %bitcast.4), channel_id=1, source_target_pairs={{0,8},{2,10},{4,12},{6,14},{8,0},{10,2},{12,4},{14,6},{16,24},{18,... | collective-permute-start | bytes 98312 | tf_op jit(solution)/shard_map/ppermute | solution.py:592
  6.4 1.4 %shard_map.95 = (f32[64,128]{1,0:T(8,128)S(1)}, f32[2,2,128,128]{3,2,1,0:T(8,128)S(1)}) custom-call(f32[1,6,8,128,128]{4,3,2,1,0:T(8,128)} %given.2, f32[1,6,8,128,128]{4,3,2,1,0:T(8,128)} %given.3, f32[64,128]{1,0:T(8,128)} %bitcast.5), custom_call_target="tpu_custom_call" | custom-call | bytes 30000 | tf_op jit(solution)/shard_map/pallas_call | solution.py:36
  7.8 1.4 %collective-permute-start.3 = (f32[2,2,128,128]{3,2,1,0:T(8,128)S(1)}, f32[2,2,128,128]{3,2,1,0:T(8,128)S(1)}, u32[]{:S(2)}, u32[]{:S(2)}) collective-permute-start(f32[2,2,128,128]{3,2,1,0:T(8,128)S(1)} %get-tuple-element.87), channel_id=1, source_target_pairs={{0,1},{1,0},{2,3},{3,2},{4,5},{5,4},{6,7},{7,6},{8,9},{9,8},{10,11... | collective-permute-start | bytes 786440 | tf_op jit(solution)/shard_map/ppermute | solution.py:592
  9.2 1.5 %collective-permute-done.1.refs_2_ = f32[64,128]{1,0:T(8,128)S(1)} collective-permute-done((f32[64,128]{1,0:T(8,128)}, f32[64,128]{1,0:T(8,128)S(1)}, u32[]{:S(2)}, u32[]{:S(2)}) %collective-permute-start.1) | collective-permute-done | bytes 32800 | tf_op jit(solution)/shard_map/ppermute | solution.py:592
  10.8 1.6 %collective-permute-start.4 = (f32[4,64,128]{2,1,0:T(8,128)S(1)}, f32[4,64,128]{2,1,0:T(8,128)S(1)}, u32[]{:S(2)}, u32[]{:S(2)}) collective-permute-start(f32[4,64,128]{2,1,0:T(8,128)S(1)} %shard_map.96.near.refs_8_), channel_id=1, source_target_pairs={{0,4},{2,6},{4,0},{6,2},{8,12},{10,14},{12,8},{14,10},{16,20},{18,... | collective-permute-start | bytes 393224 | tf_op jit(solution)/shard_map/ppermute | solution.py:592
  13.1 1.2 %shard_map.98 = (f32[3,9,144,128]{3,2,1,0:T(8,128)S(1)}, f32[3,9,144,128]{3,2,1,0:T(8,128)S(1)}, f32[3,8,128,128]{3,2,1,0:T(8,128)S(1)}) custom-call(f32[1,6,8,128,128]{4,3,2,1,0:T(8,128)S(1)} %copy-done.2, f32[4,64,128]{2,1,0:T(8,128)S(1)} %shard_map.96.near.refs_8_), custom_call_target="tpu_custom_call" | custom-call | bytes 120000 | tf_op jit(solution)/shard_map/pallas_call | solution.py:36
  14.3 1.4 %shard_map.97 = (f32[3,9,144,128]{3,2,1,0:T(8,128)S(1)}, f32[3,9,144,128]{3,2,1,0:T(8,128)S(1)}, f32[3,8,128,128]{3,2,1,0:T(8,128)S(1)}, f32[8,144,128]{2,1,0:T(...) custom-call(f32[1,6,8,128,128]{4,3,2,1,0:T(8,128)S(1)} %copy-done.3,, ...), custom_call_target="tpu_custom_call" | custom-call | bytes 150000 | tf_op jit(solution)/shard_map/pallas_call | solution.py:36
  16.2 0.7 %shard_map.100 = (f32[3,9,144,128]{3,2,1,0:T(8,128)S(1)}, f32[3,8,128,128]{3,2,1,0:T(8,128)S(1)}, f32[3,9,144,128]{3,2,1,0:T(8,128)S(1)}, f32[3,8,128,128]{3,2,1,0:T(8,128)S(1)}, f32[16,64,128]{2,1,0:T(8,128)S(1)}) custom-call(f32[3,9,144,128]{3,2,1,0:T(8,128)S(1)} %get-tuple-element.82.refs_, ...), custom_call_target="tpu_custom_call", output_to_operand_aliasing={{0}: (0, {}), {1}: (1, {}), {2}: (2, {}), {3}: (3, {})} | custom-call | bytes 60000 | tf_op jit(solution)/shard_map/pallas_call | solution.py:36
  17.5 1.5 %collective-permute-start.7 = (f32[2,128,128]{2,1,0:T(8,128)S(1)}, f32[2,128,128]{2,1,0:T(8,128)S(1)}, u32[]{:S(2)}, u32[]{:S(2)}) collective-permute-start(f32[2,128,128]{2,1,0:T(8,128)S(1)} %get-tuple-element.108), channel_id=1, source_target_pairs={{0,1},{1,0},{2,3},{3,2},{4,5},{5,4},{6,7},{7,6},{8,9},{9,8},{10,11... | collective-permute-start | bytes 393224 | tf_op jit(solution)/shard_map/ppermute | solution.py:592
  19.1 0.6 %shard_map.103.coef.refs_4_.refs_2_ = f32[8,128,128]{2,1,0:T(8,128)S(1)} custom-call(f32[8,128,128]{2,1,0:T(8,128)S(1)} %shard_map.101.refs_2_.coef_in, f32[4,64,128]{2,1,0:T(8,128)S(1)} %collective-permute-done.6.refs_0_, f32[16,16,128]{2,1,0:T(8,128)S(1)} %get-tuple-element.89.refs_1_.place, ...), custom_call_target="tpu_custom_call", output_to_operand_aliasing={{}: (0, {})} | custom-call | bytes 60000 | tf_op jit(solution)/shard_map/pallas_call | solution.py:36
  21.0 1.1 %shard_map.106 = (f32[3,9,144,128]{3,2,1,0:T(8,128)S(1)}, f32[3,9,144,128]{3,2,1,0:T(8,128)S(1)}) custom-call(f32[3,9,144,128]{3,2,1,0:T(8,128)S(1)} %get-tuple-element.104.refs_0_, f32[3,9,144,128]{3,2,1,0:T(8,128)S(1)} %get-tuple-element.105.refs_1_, ...), custom_call_target="tpu_custom_call", output_to_operand_aliasing={{0}: (0, {}), {1}: (1, {})} | custom-call | bytes 110000 | tf_op jit(solution)/shard_map/pallas_call | solution.py:36
  22.1 1.5 %collective-permute-done.7.refs_5_.refs_6_ = f32[2,128,128]{2,1,0:T(8,128)S(1)} collective-permute-done((f32[2,128,128]{2,1,0:T(8,128)S(1)}, f32[2,128,128]{2,1,0:T(8,128)S(1)}, u32[]{:S(2)}, u32[]{:S(2)}) %collective-permute-start.7) | collective-permute-done | bytes 131104 | tf_op jit(solution)/shard_map/ppermute | solution.py:592
  23.8 1.8 %collective-permute-start.9 = (f32[2,128,128]{2,1,0:T(8,128)S(1)}, f32[2,128,128]{2,1,0:T(8,128)S(1)}, u32[]{:S(2)}, u32[]{:S(2)}) collective-permute-start(f32[2,128,128]{2,1,0:T(8,128)S(1)} %get-tuple-element.122), channel_id=1, source_target_pairs={{0,1},{1,0},{2,3},{3,2},{4,5},{5,4},{6,7},{7,6},{8,9},{9,8},{10,11... | collective-permute-start | bytes 393224 | tf_op jit(solution)/shard_map/ppermute | solution.py:592
  25.6 1.0 %shard_map.108 = (f32[3,9,144,128]{3,2,1,0:T(8,128)S(1)}, f32[3,9,144,128]{3,2,1,0:T(8,128)S(1)}, f32[3,9,144,128]{3,2,1,0:T(8,128)S(1)}, f32[8,144,128]{2,1,0:T(8,128)S(1)}) custom-call(f32[3,9,144,128]{3,2,1,0:T(8,128)S(1)} %get-tuple-element.102.refs_0_, ...), custom_call_target="tpu_custom_call", output_to_operand_aliasing={{0}: (0, {}), {1}: (1, {}), {2}: (2, {}), {3}: (3, {})} | custom-call | bytes 120000 | tf_op jit(solution)/shard_map/pallas_call | solution.py:36
  26.8 1.4 %collective-permute-start.10 = (f32[2,128,128]{2,1,0:T(8,128)S(1)}, f32[2,128,128]{2,1,0:T(8,128)S(1)}, u32[]{:S(2)}, u32[]{:S(2)}) collective-permute-start(f32[2,128,128]{2,1,0:T(8,128)S(1)} %get-tuple-element.129), channel_id=1, source_target_pairs={{0,1},{1,0},{2,3},{3,2},{4,5},{5,4},{6,7},{7,6},{8,9},{9,8},{10,11... | collective-permute-start | bytes 393224 | tf_op jit(solution)/shard_map/ppermute | solution.py:592
  28.2 1.1 %shard_map.110 = (f32[3,9,144,128]{3,2,1,0:T(8,128)S(1)}, f32[3,9,144,128]{3,2,1,0:T(8,128)S(1)}) custom-call(f32[3,9,144,128]{3,2,1,0:T(8,128)S(1)} %get-tuple-element.118.refs_0_, f32[3,9,144,128]{3,2,1,0:T(8,128)S(1)} %get-tuple-element.119.refs_1_, ...), custom_call_target="tpu_custom_call", output_to_operand_aliasing={{0}: (0, {}), {1}: (1, {})} | custom-call | bytes 110000 | tf_op jit(solution)/shard_map/pallas_call | solution.py:36
  29.6 1.7 %collective-permute-start.11 = (f32[2,128,128]{2,1,0:T(8,128)S(1)}, f32[2,128,128]{2,1,0:T(8,128)S(1)}, u32[]{:S(2)}, u32[]{:S(2)}) collective-permute-start(f32[2,128,128]{2,1,0:T(8,128)S(1)} %get-tuple-element.140), channel_id=1, source_target_pairs={{0,1},{1,0},{2,3},{3,2},{4,5},{5,4},{6,7},{7,6},{8,9},{9,8},{10,11... | collective-permute-start | bytes 393224 | tf_op jit(solution)/shard_map/ppermute | solution.py:592
  31.3 1.0 %shard_map.112 = (f32[3,9,144,128]{3,2,1,0:T(8,128)S(1)}, f32[3,9,144,128]{3,2,1,0:T(8,128)S(1)}, f32[3,9,144,128]{3,2,1,0:T(8,128)S(1)}, f32[8,144,128]{2,1,0:T(8,128)S(1)}) custom-call(f32[3,9,144,128]{3,2,1,0:T(8,128)S(1)} %get-tuple-element.116.refs_0_, ...), custom_call_target="tpu_custom_call", output_to_operand_aliasing={{0}: (0, {}), {1}: (1, {}), {2}: (2, {}), {3}: (3, {})} | custom-call | bytes 120000 | tf_op jit(solution)/shard_map/pallas_call | solution.py:36
  33.0 1.9 %collective-permute-start.12 = (f32[2,128,128]{2,1,0:T(8,128)S(1)}, f32[2,128,128]{2,1,0:T(8,128)S(1)}, u32[]{:S(2)}, u32[]{:S(2)}) collective-permute-start(f32[2,128,128]{2,1,0:T(8,128)S(1)} %get-tuple-element.143), channel_id=1, source_target_pairs={{0,1},{1,0},{2,3},{3,2},{4,5},{5,4},{6,7},{7,6},{8,9},{9,8},{10,11... | collective-permute-start | bytes 393224 | tf_op jit(solution)/shard_map/ppermute | solution.py:592
  34.8 1.1 %shard_map.114 = (f32[3,9,144,128]{3,2,1,0:T(8,128)S(1)}, f32[3,9,144,128]{3,2,1,0:T(8,128)S(1)}) custom-call(f32[3,9,144,128]{3,2,1,0:T(8,128)S(1)} %get-tuple-element.132.refs_0_, f32[3,9,144,128]{3,2,1,0:T(8,128)S(1)} %get-tuple-element.133.refs_1_, ...), custom_call_target="tpu_custom_call", output_to_operand_aliasing={{0}: (0, {}), {1}: (1, {})} | custom-call | bytes 110000 | tf_op jit(solution)/shard_map/pallas_call | solution.py:36
  35.9 1.0 %shard_map.115 = (f32[3,9,144,128]{3,2,1,0:T(8,128)S(1)}, f32[3,9,144,128]{3,2,1,0:T(8,128)S(1)}, f32[3,9,144,128]{3,2,1,0:T(8,128)S(1)}, f32[8,144,128]{2,1,0:T(8,128)S(1)}) custom-call(f32[3,9,144,128]{3,2,1,0:T(8,128)S(1)} %get-tuple-element.130.refs_0_, ...), custom_call_target="tpu_custom_call", output_to_operand_aliasing={{0}: (0, {}), {1}: (1, {}), {2}: (2, {}), {3}: (3, {})} | custom-call | bytes 120000 | tf_op jit(solution)/shard_map/pallas_call | solution.py:36
  37.1 0.7 %shard_map.119 = (f32[4,48,128]{2,1,0:T(8,128)S(1)}, f32[4,48,128]{2,1,0:T(8,128)S(1)}, f32[4,48,128]{2,1,0:T(8,128)S(1)}, f32[4,48,128]{2,1,0:T(8,128)S(1)}) custom-call(f32[8,144,128]{2,1,0:T(8,128)S(1)} %get-tuple-element.146.total, f32[3,9,144,128]{3,2,1,0:T(8,128)S(1)} %get-tuple-element.141.refs_2_.after, s32[16]{0:T(128)} %block_ids_far.1), custom_call_target="tpu_custom_call" | custom-call | bytes 80000 | tf_op jit(solution)/shard_map/pallas_call | solution.py:36
  39.4 1.6 %collective-permute-start.15 = (f32[4,48,128]{2,1,0:T(8,128)S(1)}, f32[4,48,128]{2,1,0:T(8,128)S(1)}, u32[]{:S(2)}, u32[]{:S(2)}) collective-permute-start(f32[4,48,128]{2,1,0:T(8,128)S(1)} %get-tuple-element.154), channel_id=1, source_target_pairs={{0,4},{2,6},{4,0},{6,2},{8,12},{10,14},{12,8},{14,10},{16,20},{18,... | collective-permute-start | bytes 294920 | tf_op jit(solution)/shard_map/ppermute | solution.py:592
  41.0 0.8 %collective-permute-start.17 = (f32[4,16,128]{2,1,0:T(8,128)S(1)}, f32[4,16,128]{2,1,0:T(8,128)S(1)}, u32[]{:S(2)}, u32[]{:S(2)}) collective-permute-start(f32[4,16,128]{2,1,0:T(8,128)S(1)} %get-tuple-element.157), channel_id=1, source_target_pairs={{0,4},{2,6},{4,0},{6,2},{8,12},{10,14},{12,8},{14,10},{16,20},{18,... | collective-permute-start | bytes 98312 | tf_op jit(solution)/shard_map/ppermute | solution.py:592
  41.7 3.5 %collective-permute-done.17.refs_3_ = f32[4,16,128]{2,1,0:T(8,128)S(1)} collective-permute-done((f32[4,16,128]{2,1,0:T(8,128)S(1)}, f32[4,16,128]{2,1,0:T(8,128)S(1)}, u32[]{:S(2)}, u32[]{:S(2)}) %collective-permute-start.17) | collective-permute-done | bytes 32800 | tf_op jit(solution)/shard_map/ppermute | solution.py:592
  45.2 0.7 %shard_map.123 = f32[4,64,128]{2,1,0:T(8,128)} custom-call(f32[4,48,128]{2,1,0:T(8,128)S(1)} %get-tuple-element.153.refs_0_, f32[4,48,128]{2,1,0:T(8,128)S(1)} %collective-permute-done.15.refs_1_, f32[4,16,128]{2,1,0:T(8,128)S(1)} %get-tuple-element.156.refs_2_, f32[4,16,128]{2,1,0:T(8,128)S(1)} %collective-permute-done.17.refs_3_), custom_call_target="tpu_custom_call" | custom-call | bytes 30000 | tf_op jit(solution)/shard_map/pallas_call | solution.py:36
  45.9 3.4 %all-to-all-start = ((f32[4,64,128]{2,1,0:T(8,128)}), f32[4,64,128]{2,1,0:T(8,128)S(1)}, u32[]{:S(2)}, u32[]{:S(2)}) async-start(f32[4,64,128]{2,1,0:T(8,128)} %shard_map.123), calls=%async_computation | async-start | bytes 262144 | tf_op jit(solution)/shard_map/all_to_all | solution.py:839
  49.3 1.6 %copy-done.1 = f32[3,9,144,128]{3,2,1,0:T(8,128)S(1)} copy-done((f32[3,9,144,128]{3,2,1,0:T(8,128)S(1)}, f32[3,9,144,128]{3,2,1,0:T(8,128)}, u32[]{:S(2)}) %copy-start.1) | copy-done | bytes 1990680
  50.8 1.7 %shard_map.118 = f32[1,6,8,128,128]{4,3,2,1,0:T(8,128)} custom-call(f32[3,9,144,128]{3,2,1,0:T(8,128)S(1)} %get-tuple-element.144.e, f32[3,9,144,128]{3,2,1,0:T(8,128)S(1)} %copy-done.1), custom_call_target="tpu_custom_call" | custom-call | bytes 170000 | tf_op jit(solution)/shard_map/pallas_call | solution.py:36
  52.5 2.8 %all-to-all-done.got = f32[4,64,128]{2,1,0:T(8,128)S(1)} async-done(((f32[4,64,128]{2,1,0:T(8,128)}), f32[4,64,128]{2,1,0:T(8,128)S(1)}, u32[]{:S(2)}, u32[]{:S(2)}) %all-to-all-start) | async-done | bytes 131104 | tf_op jit(solution)/shard_map/all_to_all | solution.py:839
  55.4 0.6 %shard_map.124 = f32[64,128]{1,0:T(8,128)} custom-call(f32[4,64,128]{2,1,0:T(8,128)S(1)} %all-to-all-done.got), custom_call_target="tpu_custom_call" | custom-call | bytes 30000 | tf_op jit(solution)/shard_map/pallas_call | solution.py:36
  (44 shorter events, 5.5 us)
Async XLA Ops:
  0.6 12.5 %copy-start.2 = (f32[1,6,8,128,128]{4,3,2,1,0:T(8,128)S(1)}, f32[1,6,8,128,128]{4,3,2,1,0:T(8,128)}, u32[]{:S(2)}) copy-start(f32[1,6,8,128,128]{4,3,2,1,0:T(8,128)} %given.3) | copy-start | bytes 9437188
  0.6 8.6 %collective-permute-start.2 = (f32[64,128]{1,0:T(8,128)}, f32[64,128]{1,0:T(8,128)S(1)}, u32[]{:S(2)}, u32[]{:S(2)}) collective-permute-start(f32[64,128]{1,0:T(8,128)} %bitcast.2), channel_id=1, source_target_pairs={{0,24},{2,26},{4,28},{6,30},{8,16},{10,18},{12,20},{14,22},{16,8},... | collective-permute-start | bytes 98312 | tf_op jit(solution)/shard_map/ppermute | solution.py:592
  5.8 5.0 %collective-permute-start.1 = (f32[64,128]{1,0:T(8,128)}, f32[64,128]{1,0:T(8,128)S(1)}, u32[]{:S(2)}, u32[]{:S(2)}) collective-permute-start(f32[64,128]{1,0:T(8,128)} %bitcast.3), channel_id=1, source_target_pairs={{0,16},{2,18},{4,20},{6,22},{8,24},{10,26},{12,28},{14,30},{16,0},... | collective-permute-start | bytes 98312 | tf_op jit(solution)/shard_map/ppermute | solution.py:592
  5.8 5.0 %collective-permute-start = (f32[64,128]{1,0:T(8,128)}, f32[64,128]{1,0:T(8,128)S(1)}, u32[]{:S(2)}, u32[]{:S(2)}) collective-permute-start(f32[64,128]{1,0:T(8,128)} %bitcast.4), channel_id=1, source_target_pairs={{0,8},{2,10},{4,12},{6,14},{8,0},{10,2},{12,4},{14,6},{16,24},{18,... | collective-permute-start | bytes 98312 | tf_op jit(solution)/shard_map/ppermute | solution.py:592
  7.8 6.5 %copy-start.3 = (f32[1,6,8,128,128]{4,3,2,1,0:T(8,128)S(1)}, f32[1,6,8,128,128]{4,3,2,1,0:T(8,128)}, u32[]{:S(2)}) copy-start(f32[1,6,8,128,128]{4,3,2,1,0:T(8,128)} %given.2) | copy-start | bytes 9437188
  7.8 8.4 %collective-permute-start.3 = (f32[2,2,128,128]{3,2,1,0:T(8,128)S(1)}, f32[2,2,128,128]{3,2,1,0:T(8,128)S(1)}, u32[]{:S(2)}, u32[]{:S(2)}) collective-permute-start(f32[2,2,128,128]{3,2,1,0:T(8,128)S(1)} %get-tuple-element.87), channel_id=1, source_target_pairs={{0,1},{1,0},{2,3},{3,2},{4,5},{5,4},{6,7},{7,6},{8,9},{9,8},{10,11... | collective-permute-start | bytes 786440 | tf_op jit(solution)/shard_map/ppermute | solution.py:592
  10.8 5.0 %collective-permute-start.4 = (f32[4,64,128]{2,1,0:T(8,128)S(1)}, f32[4,64,128]{2,1,0:T(8,128)S(1)}, u32[]{:S(2)}, u32[]{:S(2)}) collective-permute-start(f32[4,64,128]{2,1,0:T(8,128)S(1)} %shard_map.96.near.refs_8_), channel_id=1, source_target_pairs={{0,4},{2,6},{4,0},{6,2},{8,12},{10,14},{12,8},{14,10},{16,20},{18,... | collective-permute-start | bytes 393224 | tf_op jit(solution)/shard_map/ppermute | solution.py:592
  13.0 3.2 %collective-permute-start.5 = (f32[4,64,128]{2,1,0:T(8,128)S(1)}, f32[4,64,128]{2,1,0:T(8,128)S(1)}, u32[]{:S(2)}, u32[]{:S(2)}) collective-permute-start(f32[4,64,128]{2,1,0:T(8,128)S(1)} %shard_map.96.near.refs_8_), channel_id=1, source_target_pairs={{0,2},{2,0},{4,6},{6,4},{8,10},{10,8},{12,14},{14,12},{16,18},{18,... | collective-permute-start | bytes 393224 | tf_op jit(solution)/shard_map/ppermute | solution.py:592
  15.8 1.4 %collective-permute-start.6 = (f32[4,64,128]{2,1,0:T(8,128)S(1)}, f32[4,64,128]{2,1,0:T(8,128)S(1)}, u32[]{:S(2)}, u32[]{:S(2)}) collective-permute-start(f32[4,64,128]{2,1,0:T(8,128)S(1)} %shard_map.99.refs_9_), channel_id=1, source_target_pairs={{0,2},{2,0},{4,6},{6,4},{8,10},{10,8},{12,14},{14,12},{16,18},{18,... | collective-permute-start | bytes 393224 | tf_op jit(solution)/shard_map/ppermute | solution.py:592
  17.5 6.0 %collective-permute-start.7 = (f32[2,128,128]{2,1,0:T(8,128)S(1)}, f32[2,128,128]{2,1,0:T(8,128)S(1)}, u32[]{:S(2)}, u32[]{:S(2)}) collective-permute-start(f32[2,128,128]{2,1,0:T(8,128)S(1)} %get-tuple-element.108), channel_id=1, source_target_pairs={{0,1},{1,0},{2,3},{3,2},{4,5},{5,4},{6,7},{7,6},{8,9},{9,8},{10,11... | collective-permute-start | bytes 393224 | tf_op jit(solution)/shard_map/ppermute | solution.py:592
  20.4 6.2 %collective-permute-start.8 = (f32[2,128,128]{2,1,0:T(8,128)S(1)}, f32[2,128,128]{2,1,0:T(8,128)S(1)}, u32[]{:S(2)}, u32[]{:S(2)}) collective-permute-start(f32[2,128,128]{2,1,0:T(8,128)S(1)} %get-tuple-element.115), channel_id=1, source_target_pairs={{0,1},{1,0},{2,3},{3,2},{4,5},{5,4},{6,7},{7,6},{8,9},{9,8},{10,11... | collective-permute-start | bytes 393224 | tf_op jit(solution)/shard_map/ppermute | solution.py:592
  23.8 5.6 %collective-permute-start.9 = (f32[2,128,128]{2,1,0:T(8,128)S(1)}, f32[2,128,128]{2,1,0:T(8,128)S(1)}, u32[]{:S(2)}, u32[]{:S(2)}) collective-permute-start(f32[2,128,128]{2,1,0:T(8,128)S(1)} %get-tuple-element.122), channel_id=1, source_target_pairs={{0,1},{1,0},{2,3},{3,2},{4,5},{5,4},{6,7},{7,6},{8,9},{9,8},{10,11... | collective-permute-start | bytes 393224 | tf_op jit(solution)/shard_map/ppermute | solution.py:592
  26.8 5.9 %collective-permute-start.10 = (f32[2,128,128]{2,1,0:T(8,128)S(1)}, f32[2,128,128]{2,1,0:T(8,128)S(1)}, u32[]{:S(2)}, u32[]{:S(2)}) collective-permute-start(f32[2,128,128]{2,1,0:T(8,128)S(1)} %get-tuple-element.129), channel_id=1, source_target_pairs={{0,1},{1,0},{2,3},{3,2},{4,5},{5,4},{6,7},{7,6},{8,9},{9,8},{10,11... | collective-permute-start | bytes 393224 | tf_op jit(solution)/shard_map/ppermute | solution.py:592
  29.6 7.4 %collective-permute-start.11 = (f32[2,128,128]{2,1,0:T(8,128)S(1)}, f32[2,128,128]{2,1,0:T(8,128)S(1)}, u32[]{:S(2)}, u32[]{:S(2)}) collective-permute-start(f32[2,128,128]{2,1,0:T(8,128)S(1)} %get-tuple-element.140), channel_id=1, source_target_pairs={{0,1},{1,0},{2,3},{3,2},{4,5},{5,4},{6,7},{7,6},{8,9},{9,8},{10,11... | collective-permute-start | bytes 393224 | tf_op jit(solution)/shard_map/ppermute | solution.py:592
  33.0 5.5 %collective-permute-start.12 = (f32[2,128,128]{2,1,0:T(8,128)S(1)}, f32[2,128,128]{2,1,0:T(8,128)S(1)}, u32[]{:S(2)}, u32[]{:S(2)}) collective-permute-start(f32[2,128,128]{2,1,0:T(8,128)S(1)} %get-tuple-element.143), channel_id=1, source_target_pairs={{0,1},{1,0},{2,3},{3,2},{4,5},{5,4},{6,7},{7,6},{8,9},{9,8},{10,11... | collective-permute-start | bytes 393224 | tf_op jit(solution)/shard_map/ppermute | solution.py:592
  37.1 1.4 %copy-start = (f32[3,9,144,128]{3,2,1,0:T(8,128)}, f32[3,9,144,128]{3,2,1,0:T(8,128)S(1)}, u32[]{:S(2)}) copy-start(f32[3,9,144,128]{3,2,1,0:T(8,128)S(1)} %get-tuple-element.145.h) | copy-start | bytes 5971972
  37.9 1.4 %collective-permute-start.13 = (f32[4,48,128]{2,1,0:T(8,128)S(1)}, f32[4,48,128]{2,1,0:T(8,128)S(1)}, u32[]{:S(2)}, u32[]{:S(2)}) collective-permute-start(f32[4,48,128]{2,1,0:T(8,128)S(1)} %get-tuple-element.149), channel_id=1, source_target_pairs={{0,2},{2,0},{4,6},{6,4},{8,10},{10,8},{12,14},{14,12},{16,18},{18,... | collective-permute-start | bytes 294920 | tf_op jit(solution)/shard_map/ppermute | solution.py:592
  37.9 1.4 %collective-permute-start.14 = (f32[4,48,128]{2,1,0:T(8,128)S(1)}, f32[4,48,128]{2,1,0:T(8,128)S(1)}, u32[]{:S(2)}, u32[]{:S(2)}) collective-permute-start(f32[4,48,128]{2,1,0:T(8,128)S(1)} %get-tuple-element.150), channel_id=1, source_target_pairs={{0,2},{2,0},{4,6},{6,4},{8,10},{10,8},{12,14},{14,12},{16,18},{18,... | collective-permute-start | bytes 294920 | tf_op jit(solution)/shard_map/ppermute | solution.py:592
  38.9 2.1 %collective-permute-start.16 = (f32[8,16,128]{2,1,0:T(8,128)S(1)}, f32[8,16,128]{2,1,0:T(8,128)S(1)}, u32[]{:S(2)}, u32[]{:S(2)}) collective-permute-start(f32[8,16,128]{2,1,0:T(8,128)S(1)} %get-tuple-element.155), channel_id=1, source_target_pairs={{0,2},{2,0},{4,6},{6,4},{8,10},{10,8},{12,14},{14,12},{16,18},{18,... | collective-permute-start | bytes 196616 | tf_op jit(solution)/shard_map/ppermute | solution.py:592
  39.4 5.8 %collective-permute-start.15 = (f32[4,48,128]{2,1,0:T(8,128)S(1)}, f32[4,48,128]{2,1,0:T(8,128)S(1)}, u32[]{:S(2)}, u32[]{:S(2)}) collective-permute-start(f32[4,48,128]{2,1,0:T(8,128)S(1)} %get-tuple-element.154), channel_id=1, source_target_pairs={{0,4},{2,6},{4,0},{6,2},{8,12},{10,14},{12,8},{14,10},{16,20},{18,... | collective-permute-start | bytes 294920 | tf_op jit(solution)/shard_map/ppermute | solution.py:592
  41.0 4.2 %collective-permute-start.17 = (f32[4,16,128]{2,1,0:T(8,128)S(1)}, f32[4,16,128]{2,1,0:T(8,128)S(1)}, u32[]{:S(2)}, u32[]{:S(2)}) collective-permute-start(f32[4,16,128]{2,1,0:T(8,128)S(1)} %get-tuple-element.157), channel_id=1, source_target_pairs={{0,4},{2,6},{4,0},{6,2},{8,12},{10,14},{12,8},{14,10},{16,20},{18,... | collective-permute-start | bytes 98312 | tf_op jit(solution)/shard_map/ppermute | solution.py:592
  45.9 9.5 %all-to-all-start = ((f32[4,64,128]{2,1,0:T(8,128)}), f32[4,64,128]{2,1,0:T(8,128)S(1)}, u32[]{:S(2)}, u32[]{:S(2)}) async-start(f32[4,64,128]{2,1,0:T(8,128)} %shard_map.123), calls=%async_computation | async-start | bytes 262144 | tf_op jit(solution)/shard_map/all_to_all | solution.py:839
  49.3 1.6 %copy-start.1 = (f32[3,9,144,128]{3,2,1,0:T(8,128)S(1)}, f32[3,9,144,128]{3,2,1,0:T(8,128)}, u32[]{:S(2)}) copy-start(f32[3,9,144,128]{3,2,1,0:T(8,128)} %copy-done) | copy-start | bytes 5971972

commit v14 on v12

--- a/solution.py
+++ b/solution.py
@@ -193,32 +193,33 @@
                 else:
                     row = lax.broadcasted_iota(jnp.int32, ez.shape, 0)
                     ez_after = jnp.where(row == size - 1, 0.0, pltpu.roll(ez, size - 1, 0))
-                pay[evo, 0, here, :] = (hx + hx) - ((next_col(ez) - ez) + ey)
-                pay[evo, 1, here, :] = (hy + hy) + (ex + (ez_after - ez))
+                pay[evo][0, here, :] = (hx + hx) - ((next_col(ez) - ez) + ey)
+                pay[evo][1, here, :] = (hy + hy) + (ex + (ez_after - ez))
 
     def down(pay):
         copies = []
         for evo, given in enumerate((fwd, adj)):
             for c in range(2):
                 copies.append(
-                    pltpu.make_async_copy(given.at[0, c, 0], pay.at[evo, c], sems.at[evo, c])
+                    pltpu.make_async_copy(given.at[0, c, 0], pay[evo].at[c], sems.at[evo, c])
                 )
         for copy in copies:
             copy.start()
         for copy in copies:
             copy.wait()
 
-    if len(pays) == 2:
-        up(pays[0])
-        down(pays[1])
+    half = len(pays) // 2
+    if half == 2:
+        up(pays[0::2])
+        down(pays[1::2])
     else:
-        pl.when(has_up)(lambda: up(pays[0]))
-        pl.when(has_low)(lambda: down(pays[0]))
+        pl.when(has_up)(lambda: up(pays))
+        pl.when(has_low)(lambda: down(pays))
     held_copy.wait()
 
 
 def first_fwd_kernel(
-    layout, given, near, wave_idx, source_far, ids_far, idx_far, eps_far,
+    layout, given, other, near, wave_idx, source_far, ids_far, idx_far, eps_far,
     e, h, curls, total, edges, forced, drives, base, place,
     source, block_ids, material_idx, material_eps, sems,
 ):
@@ -302,28 +303,29 @@
     lax.fori_loop(1, win.top, body, 0)
 
 
-def settle_kernel(layout, *refs):
-    refs = list(refs)
-    del refs[:4]
-    e_fwd, e_adj, below, above = (refs.pop(0) for _ in range(4))
-    parts = [refs.pop(0) for _ in layout]
-    ids_far, h_fwd, curls_fwd, h_adj, curls_adj, blocks, block_ids, sem = refs
+def settle_kernel(h_in, curls_in, e, below, above, h, curls):
+    win = Window(e, h)
+    has_up, has_low = neighbours()
+    pl.when(has_up)(lambda: win.take_above(above))
+    pl.when(has_low)(lambda: win.take_below(below))
+    win.put_curl(curls, win.top, win.top - 1)
+    win.put_curl(curls, 0, win.under)
+
+
+def settle_adj_kernel(
+    masks, h_in, curls_in, e, below, above, near, near_across, ids_far,
+    h, curls, blocks, block_ids, sem,
+):
     fetch = pltpu.make_async_copy(ids_far, block_ids, sem)
     fetch.start()
     nothing = jnp.zeros(blocks.shape[1:], F32)
     for block in range(blocks.shape[0]):
         blocks[block] = nothing
-    has_up, has_low = neighbours()
-    for evo, (e, h, curls) in enumerate(((e_fwd, h_fwd, curls_fwd), (e_adj, h_adj, curls_adj))):
-        win = Window(e, h)
-        pl.when(has_up)(lambda: win.take_above(above.at[evo]))
-        pl.when(has_low)(lambda: win.take_below(below.at[evo]))
-        win.put_curl(curls, win.top, win.top - 1)
-        win.put_curl(curls, 0, win.under)
+    settle_kernel(h_in, curls_in, e, below, above, h, curls)
     fetch.wait()
     me = lax.axis_index("grp")
-    for part, masks in zip(parts, layout):
-        for slot, mask in enumerate(masks):
+    for part, part_masks in zip((near, near_across), masks):
+        for slot, mask in enumerate(part_masks):
             blocks[block_ids[me ^ mask]] = part[slot]
 
 
@@ -423,35 +425,48 @@
     placed[pl.ds(PAD + rows, PAD), :] = margin
 
 
-def place_layer(layer, first_slot, parts, place, blocks, placed):
-    nblock = blocks.shape[0]
+def place_layer(pieces, place, start, placed):
+    nblock = place.shape[0]
     block_rows = (placed.shape[0] - 2 * PAD) // nblock
     clear_margins(placed)
-    start = layer * block_rows
-    source = pl.ds(start if isinstance(layer, int) else pl.multiple_of(start, block_rows), block_rows)
-    pieces = [part[slot, source, :] for part in parts for slot in range(part.shape[0])]
     for block in range(nblock):
-        value = blocks[block, source, :]
-        for slot, piece in enumerate(pieces):
-            value = value + place[first_slot + slot, pl.ds(block, 1), :] * piece
+        value = start(block)
+        for slot, piece in pieces:
+            term = place[slot, pl.ds(block, 1), :] * piece
+            value = term if value is None else value + term
         placed[pl.ds(PAD + block * block_rows, block_rows), :] = value
 
 
-def coef_edge_kernel(first_slot, count, *refs):
-    parts, (place, base, blocks, coef, placed) = refs[:count], refs[count:]
+def coef_edge_kernel(count, *refs):
+    parts, (place, base, coef, placed) = refs[:count], refs[count:]
+    far = parts[0].shape[0]
+    block_rows = base.shape[0] // place.shape[0]
     edge_layers = (0, coef.shape[0] - 1)
     for which, layer in enumerate(edge_layers):
-        place_layer(layer, first_slot, parts, place, blocks, placed.at[which])
+        pieces = []
+        for number, part in enumerate(parts):
+            first = (layer if number % (count // 2) == 0 else which) * block_rows
+            for slot in range(far):
+                pieces.append((number * far + slot, part[slot, pl.ds(first, block_rows), :]))
+        place_layer(pieces, place, lambda block: None, placed.at[which])
     for which, layer in enumerate(edge_layers):
         coef_layer(layer, coef, placed.at[which], base)
 
 
-def coef_inner_kernel(first_slot, count, coef_in, *refs):
-    parts, (place, base, blocks, coef, placed) = refs[:count], refs[count:]
+def coef_inner_kernel(numbers, coef_in, *refs):
+    parts, (place, base, blocks, coef, placed) = refs[: len(numbers)], refs[len(numbers) :]
+    block_rows = base.shape[0] // place.shape[0]
 
     def body(layer, carry):
         there = placed.at[lax.rem(layer, 2)]
-        place_layer(layer, first_slot, parts, place, blocks, there)
+        late = pl.ds(pl.multiple_of((layer - 1) * block_rows, block_rows), block_rows)
+        source = pl.ds(pl.multiple_of(layer * block_rows, block_rows), block_rows)
+        pieces = []
+        for number, part in zip(numbers, parts):
+            far = part.shape[0]
+            for slot in range(far):
+                pieces.append((number * far + slot, part[slot, late, :]))
+        place_layer(pieces, place, lambda block: blocks[block, source, :], there)
         coef_layer(layer, coef, there, base)
         return carry
 
@@ -477,10 +492,14 @@
     )
 
 
-def pack_kernel(*refs):
-    out = refs[-1]
-    for slot, ref in enumerate(refs[:-1]):
-        out[slot] = ref[...]
+def pack_kernel(block_rows, *refs):
+    pieces, (near, ends, rest) = refs[:-3], refs[-3:]
+    rows = near.shape[1]
+    for slot, piece in enumerate(pieces):
+        near[slot] = piece[...]
+        ends[slot, pl.ds(0, block_rows), :] = piece[pl.ds(0, block_rows), :]
+        ends[slot, pl.ds(block_rows, block_rows), :] = piece[pl.ds(rows - block_rows, block_rows), :]
+        rest[slot] = piece[pl.ds(block_rows, rows - 2 * block_rows), :]
 
 
 def filter_inner_kernel(layout, total, after, block_ids_far, *rest):
@@ -658,16 +677,27 @@
     got = [swap_over(design, "grp", mask) for mask in far_masks[1:]]
     own, *pays = call(
         opening_kernel,
-        [on_chip(*piece)] + [on_chip(2, 2, width_x, width_y)] * npay,
-        [IN_VMEM] * (1 + npay),
+        [on_chip(*piece)] + [halo_shape] * (2 * npay),
+        [IN_VMEM] * (1 + 2 * npay),
         [fwd_fields, adj_fields, design],
         [IN_HBM] * 3,
         [pltpu.VMEM((2, 5, width_x, width_y), F32), pltpu.SemaphoreType.DMA((3, 5))],
     )
-    below, above = trade(pays)
-
-    near = call(pack_kernel, on_chip(*group), IN_VMEM, [own] + got, [IN_VMEM] * far)
-    others = [swap_over(near, "grp", mask) for mask in middle_masks[1:]]
+    first_fwd, first_adj = trade(pays[:npay]), trade(pays[npay:])
+
+    near, near_ends, near_rest = call(
+        functools.partial(pack_kernel, block_rows),
+        [
+            on_chip(*group),
+            on_chip(far, 2 * block_rows, width_y),
+            on_chip(far, (depth - 2) * block_rows, width_y),
+        ],
+        [IN_VMEM] * 3,
+        [own] + got,
+        [IN_VMEM] * far,
+    )
+    ends = [swap_over(near_ends, "grp", mask) for mask in middle_masks[1:]]
+    rest = [swap_over(near_rest, "grp", mask) for mask in middle_masks[1:]]
     near_across = swap_over(near, "grp", 1)
 
     e_fwd, h_fwd, curls_fwd, total, edges, forced, drives, base, place = call(
@@ -684,8 +714,8 @@
             on_chip(nblock, nblock, width_y),
         ],
         [IN_VMEM] * 9,
-        [fwd_fields, near, wave_idx, source_pos, block_ids, material_idx, material_eps],
-        [IN_VMEM] * 2 + [IN_SMEM] + [IN_HBM] * 4,
+        [fwd_fields, adj_fields, near, wave_idx, source_pos, block_ids, material_idx, material_eps],
+        [IN_VMEM] * 3 + [IN_SMEM] + [IN_HBM] * 4,
         [
             pltpu.SMEM(source_pos.shape, jnp.int32),
             pltpu.SMEM(block_ids.shape, jnp.int32),
@@ -695,40 +725,27 @@
         ],
         micros=1.5,
     )
-    e_adj, h_adj, curls_adj = call(
-        first_kernel,
-        [field_shape, field_shape, curls_shape],
-        [IN_VMEM] * 3,
-        [adj_fields, near],
-        [IN_VMEM, IN_VMEM],
-        micros=1.2,
-    )
-    others = [tie(part, [e_fwd, e_adj]) for part in others]
-    early = [near] + others + [near_across]
-    last = [swap_over(part, "grp", 1) for part in others]
-    first_slot = far * len(early)
-
-    h_fwd, curls_fwd, h_adj, curls_adj, blocks = call(
-        functools.partial(settle_kernel, layout[: len(early)]),
-        [field_shape, curls_shape] * 2 + [on_chip(nblock, *piece)],
+    ends = [tie(part, [e_fwd]) for part in ends]
+    ends = [near] + ends + [near_across] + [swap_over(part, "grp", 1) for part in ends]
+    h_fwd, curls_fwd = call(
+        settle_kernel,
+        [field_shape, curls_shape],
+        [IN_VMEM] * 2,
+        [h_fwd, curls_fwd, e_fwd] + first_fwd,
         [IN_VMEM] * 5,
-        [h_fwd, curls_fwd, h_adj, curls_adj, e_fwd, e_adj, below, above] + early + [block_ids],
-        [IN_VMEM] * (8 + len(early)) + [IN_HBM],
-        [pltpu.SMEM(block_ids.shape, jnp.int32), pltpu.SemaphoreType.DMA],
-        aliases={0: 0, 1: 1, 2: 2, 3: 3},
-        micros=0.6,
+        aliases={0: 0, 1: 1},
     )
     placed = pltpu.VMEM((2, width_x + 2 * PAD, width_y), F32)
     coef = call(
-        functools.partial(coef_edge_kernel, first_slot, len(last)),
+        functools.partial(coef_edge_kernel, len(ends)),
         coef_shape,
         IN_VMEM,
-        last + [place, base, blocks],
-        [IN_VMEM] * (len(last) + 3),
+        ends + [place, base],
+        [IN_VMEM] * (len(ends) + 2),
         [placed],
     )
 
-    arrived_fwd, arrived_adj = [curls_fwd], [curls_adj]
+    arrived_fwd, arrived_adj = [curls_fwd], []
     for step in range(STEPS):
         more = npay if step < STEPS - 1 else 0
 
@@ -745,6 +762,29 @@
         if more:
             e_fwd, h_fwd, *pays = edge_fwd(e_fwd, h_fwd)
             arrived_fwd_next = trade(pays)
+        if step == 0:
+            e_adj, h_adj, curls_adj = call(
+                first_kernel,
+                [field_shape, field_shape, curls_shape],
+                [IN_VMEM] * 3,
+                [adj_fields, pays[0]],
+                [IN_VMEM, IN_VMEM],
+                micros=1.2,
+            )
+            rest = [tie(part, [e_adj]) for part in rest]
+            rest = rest + [swap_over(part, "grp", 1) for part in rest]
+            late_numbers = [*range(1, middle), *range(middle + 1, 2 * middle)]
+            h_adj, curls_adj, blocks = call(
+                functools.partial(settle_adj_kernel, [layout[0], layout[middle]]),
+                [field_shape, curls_shape, on_chip(nblock, *piece)],
+                [IN_VMEM] * 3,
+                [h_adj, curls_adj, e_adj] + first_adj + [near, near_across, block_ids],
+                [IN_VMEM] * 7 + [IN_HBM],
+                [pltpu.SMEM(block_ids.shape, jnp.int32), pltpu.SemaphoreType.DMA],
+                aliases={0: 0, 1: 1},
+                micros=0.6,
+            )
+            arrived_adj = [curls_adj]
         if step > 0:
             e_adj, h_adj, e_fwd, total = call(
                 functools.partial(inner_kernel, step, 1),
@@ -771,13 +811,24 @@
                 0.8,
                 middle,
             )
+        e_adj, h_adj, e_fwd, edges, *pays = call(
+            functools.partial(edge_kernel, step, 1),
+            [field_shape] * 3 + [edges_shape] + [halo_shape] * more,
+            [IN_VMEM] * (4 + more),
+            [e_adj, h_adj, e_fwd, edges, coef] + arrived_adj,
+            [IN_VMEM] * (5 + len(arrived_adj)),
+            aliases={0: 0, 1: 1, 2: 2, 3: 3},
+        )
+        if not more:
+            break
+        arrived_fwd, arrived_adj = arrived_fwd_next, trade(pays)
         if step == 0:
             coef = call(
-                functools.partial(coef_inner_kernel, first_slot, len(last)),
+                functools.partial(coef_inner_kernel, late_numbers),
                 coef_shape,
                 IN_VMEM,
-                [coef] + last + [place, base, blocks],
-                [IN_VMEM] * (len(last) + 4),
+                [coef] + rest + [place, base, blocks],
+                [IN_VMEM] * (len(rest) + 4),
                 [placed],
                 aliases={0: 0},
                 micros=0.6,
@@ -791,17 +842,6 @@
                 aliases={0: 0, 1: 1, 2: 2},
                 micros=0.5,
             )
-        e_adj, h_adj, e_fwd, edges, *pays = call(
-            functools.partial(edge_kernel, step, 1),
-            [field_shape] * 3 + [edges_shape] + [halo_shape] * more,
-            [IN_VMEM] * (4 + more),
-            [e_adj, h_adj, e_fwd, edges, coef] + arrived_adj,
-            [IN_VMEM] * (5 + len(arrived_adj)),
-            aliases={0: 0, 1: 1, 2: 2, 3: 3},
-        )
-        if not more:
-            break
-        arrived_fwd, arrived_adj = arrived_fwd_next, trade(pays)
         e_fwd, h_fwd = call(
             functools.partial(inner_kernel, step + 1, 0),
             [field_shape] * 2,

time: 53.4 us -> 54.9 us (1.028)
  Pallas kernels: 17 us -> 18.5 us
  starting transfers between devices: 25.2 us -> 24.1 us
  waiting for transfers between devices: 9.39 us -> 10.4 us
    pallas_call x30 -> x32, Pallas kernels: 17 us -> 18.5 us  [call(): pl.pallas_call(kernel, out_shape=outs, in_specs=specs, out_specs=out_spec...]
    ppermute x21 -> x24, starting transfers between devices: 25.2 us -> 24.1 us  [swap_over(): lax.ppermute(array, axis, [(i, i ^ mask) for i in range(lax.axis_size(axi...]
    ppermute x21 -> x24, waiting for transfers between devices: 9.39 us -> 10.4 us  [swap_over(): lax.ppermute(array, axis, [(i, i ^ mask) for i in range(lax.axis_size(axi...]
  transfers between devices with their start and end apart: 21 -> 24, of which waited for: 10 -> 9; matrix products, arithmetic and copies ran while one was open for 0% -> 0% of each run, Pallas kernels for 30% -> 33%
where the time goes in v14:
time: 54.9 us; the launch traced here: 54.7 us
  starting transfers between devices  24.1 us (44%)
  Pallas kernels  18.5 us (34%)
  waiting for transfers between devices  10.4 us (19%)
  between operations  1.66 us (3%)
    ppermute x24, starting transfers between devices, swap_over(): lax.ppermute(array, axis, [(i, i ^ mask) for i in range(lax.axis_size(axi...  24.1 us
    pallas_call x32, Pallas kernels, call(): pl.pallas_call(kernel, out_shape=outs, in_specs=specs, out_specs=out_spec...  18.5 us
    ppermute x24, waiting for transfers between devices, swap_over(): lax.ppermute(array, axis, [(i, i ^ mask) for i in range(lax.axis_size(axi...  10.4 us
  transfers between devices with their start and end apart: 24, of which 9 were waited for; matrix products, arithmetic and copies ran while one was open for 0% of the time, Pallas kernels for 33%

profile of v14, /device:TPU:0, one launch (start us, length us, event | category | flops | bytes accessed | tf_op | source)
XLA Modules:
  0.0 54.7 jit_solution(16468197871999618921)
XLA Ops:
  0.6 3.1 %collective-permute-start = (f32[64,128]{1,0:T(8,128)}, f32[64,128]{1,0:T(8,128)S(1)}, u32[]{:S(2)}, u32[]{:S(2)}) collective-permute-start(f32[64,128]{1,0:T(8,128)} %bitcast.2), channel_id=1, source_target_pairs={{0,8},{2,10},{4,12},{6,14},{8,0},{10,2},{12,4},{14,6},{16,24},{18,... | collective-permute-start | bytes 98312 | tf_op jit(solution)/shard_map/ppermute | solution.py:609
  3.7 2.6 %collective-permute-start.1 = (f32[64,128]{1,0:T(8,128)}, f32[64,128]{1,0:T(8,128)S(1)}, u32[]{:S(2)}, u32[]{:S(2)}) collective-permute-start(f32[64,128]{1,0:T(8,128)} %bitcast.3), channel_id=1, source_target_pairs={{0,16},{2,18},{4,20},{6,22},{8,24},{10,26},{12,28},{14,30},{16,0},... | collective-permute-start | bytes 98312 | tf_op jit(solution)/shard_map/ppermute | solution.py:609
  6.3 1.4 %shard_map.95 = (f32[64,128]{1,0:T(8,128)S(1)}, f32[2,128,128]{2,1,0:T(8,128)S(1)}, f32[2,128,128]{2,1,0:T(8,128)S(1)}) custom-call(f32[1,6,8,128,128]{4,3,2,1,0:T(8,128)} %given.2, f32[1,6,8,128,128]{4,3,2,1,0:T(8,128)} %given.3, f32[64,128]{1,0:T(8,128)} %bitcast.5), custom_call_target="tpu_custom_call" | custom-call | bytes 30000 | tf_op jit(solution)/shard_map/pallas_call | solution.py:36
  7.7 1.5 %collective-permute-start.3 = (f32[2,128,128]{2,1,0:T(8,128)S(1)}, f32[2,128,128]{2,1,0:T(8,128)S(1)}, u32[]{:S(2)}, u32[]{:S(2)}) collective-permute-start(f32[2,128,128]{2,1,0:T(8,128)S(1)} %get-tuple-element.93), channel_id=1, source_target_pairs={{0,1},{1,0},{2,3},{3,2},{4,5},{5,4},{6,7},{7,6},{8,9},{9,8},{10,11... | collective-permute-start | bytes 393224 | tf_op jit(solution)/shard_map/ppermute | solution.py:609
  9.3 2.9 %collective-permute-done.2.refs_3_ = f32[64,128]{1,0:T(8,128)S(1)} collective-permute-done((f32[64,128]{1,0:T(8,128)}, f32[64,128]{1,0:T(8,128)S(1)}, u32[]{:S(2)}, u32[]{:S(2)}) %collective-permute-start.2) | collective-permute-done | bytes 32800 | tf_op jit(solution)/shard_map/ppermute | solution.py:609
  12.4 1.6 %collective-permute-start.4 = (f32[4,16,128]{2,1,0:T(8,128)S(1)}, f32[4,16,128]{2,1,0:T(8,128)S(1)}, u32[]{:S(2)}, u32[]{:S(2)}) collective-permute-start(f32[4,16,128]{2,1,0:T(8,128)S(1)} %get-tuple-element.95), channel_id=1, source_target_pairs={{0,4},{2,6},{4,0},{6,2},{8,12},{10,14},{12,8},{14,10},{16,20},{18,... | collective-permute-start | bytes 98312 | tf_op jit(solution)/shard_map/ppermute | solution.py:609
  13.9 0.5 collective-permute-start.8
  14.4 1.5 %collective-permute-start.7 = (f32[2,128,128]{2,1,0:T(8,128)S(1)}, f32[2,128,128]{2,1,0:T(8,128)S(1)}, u32[]{:S(2)}, u32[]{:S(2)}) collective-permute-start(f32[2,128,128]{2,1,0:T(8,128)S(1)} %get-tuple-element.105), channel_id=1, source_target_pairs={{0,1},{1,0},{2,3},{3,2},{4,5},{5,4},{6,7},{7,6},{8,9},{9,8},{10,11... | collective-permute-start | bytes 393224 | tf_op jit(solution)/shard_map/ppermute | solution.py:609
  16.6 1.4 %shard_map.97 = (f32[3,9,144,128]{3,2,1,0:T(8,128)S(1)}, f32[3,9,144,128]{3,2,1,0:T(8,128)S(1)}, f32[3,8,128,128]{3,2,1,0:T(8,128)S(1)}, f32[8,144,128]{2,1,0:T(...) custom-call(f32[1,6,8,128,128]{4,3,2,1,0:T(8,128)S(1)} %copy-done.1,, ...), custom_call_target="tpu_custom_call" | custom-call | bytes 150000 | tf_op jit(solution)/shard_map/pallas_call | solution.py:36
  18.3 1.0 %collective-permute-done.6.refs_3_ = f32[4,16,128]{2,1,0:T(8,128)S(1)} collective-permute-done((f32[4,16,128]{2,1,0:T(8,128)S(1)}, f32[4,16,128]{2,1,0:T(8,128)S(1)}, u32[]{:S(2)}, u32[]{:S(2)}) %collective-permute-start.6) | collective-permute-done | bytes 32800 | tf_op jit(solution)/shard_map/ppermute | solution.py:609
  20.3 1.2 %shard_map.102 = (f32[3,9,144,128]{3,2,1,0:T(8,128)S(1)}, f32[3,9,144,128]{3,2,1,0:T(8,128)S(1)}, f32[3,8,128,128]{3,2,1,0:T(8,128)S(1)}) custom-call(f32[1,6,8,128,128]{4,3,2,1,0:T(8,128)S(1)} %copy-done, f32[2,128,128]{2,1,0:T(8,128)S(1)} %get-tuple-element.101.near), custom_call_target="tpu_custom_call" | custom-call | bytes 120000 | tf_op jit(solution)/shard_map/pallas_call | solution.py:36
  21.6 0.7 %shard_map.103 = (f32[3,9,144,128]{3,2,1,0:T(8,128)S(1)}, f32[3,8,128,128]{3,2,1,0:T(8,128)S(1)}, f32[16,64,128]{2,1,0:T(8,128)S(1)}) custom-call(f32[3,9,144,128]{3,2,1,0:T(8,128)S(1)} %get-tuple-element.103.h_in, f32[3,8,128,128]{3,2,1,0:T(8,128)S(1)} %get-tuple-element.104.curls_in, ...), custom_call_target="tpu_custom_call", output_to_operand_aliasing={{0}: (0, {}), {1}: (1, {})} | custom-call | bytes 60000 | tf_op jit(solution)/shard_map/pallas_call | solution.py:36
  22.4 1.6 %collective-permute-start.11 = (f32[2,128,128]{2,1,0:T(8,128)S(1)}, f32[2,128,128]{2,1,0:T(8,128)S(1)}, u32[]{:S(2)}, u32[]{:S(2)}) collective-permute-start(f32[2,128,128]{2,1,0:T(8,128)S(1)} %get-tuple-element.127), channel_id=1, source_target_pairs={{0,1},{1,0},{2,3},{3,2},{4,5},{5,4},{6,7},{7,6},{8,9},{9,8},{10,11... | collective-permute-start | bytes 393224 | tf_op jit(solution)/shard_map/ppermute | solution.py:609
  24.0 0.7 %shard_map.106.coef.refs_2_.refs_4_ = f32[8,128,128]{2,1,0:T(8,128)S(1)} custom-call(f32[8,128,128]{2,1,0:T(8,128)S(1)} %shard_map.100.refs_2_.refs_4_.coef_in, f32[4,48,128]{2,1,0:T(8,128)S(1)} %shard_map.105.refs_0_, f32[4,48,128]{2,1,0:T(8,128)S(1)} %collective-permute-done.9.refs_1_, ...), custom_call_target="tpu_custom_call", output_to_operand_aliasing={{}: (0, {})} | custom-call | bytes 60000 | tf_op jit(solution)/shard_map/pallas_call | solution.py:36
  25.3 1.2 %shard_map.108 = (f32[3,9,144,128]{3,2,1,0:T(8,128)S(1)}, f32[3,9,144,128]{3,2,1,0:T(8,128)S(1)}) custom-call(f32[3,9,144,128]{3,2,1,0:T(8,128)S(1)} %get-tuple-element.117.refs_0_, f32[3,9,144,128]{3,2,1,0:T(8,128)S(1)} %get-tuple-element.118.refs_1_, ...), custom_call_target="tpu_custom_call", output_to_operand_aliasing={{0}: (0, {}), {1}: (1, {})} | custom-call | bytes 110000 | tf_op jit(solution)/shard_map/pallas_call | solution.py:36
  26.7 0.6 %collective-permute-start.12 = (f32[2,128,128]{2,1,0:T(8,128)S(1)}, f32[2,128,128]{2,1,0:T(8,128)S(1)}, u32[]{:S(2)}, u32[]{:S(2)}) collective-permute-start(f32[2,128,128]{2,1,0:T(8,128)S(1)} %get-tuple-element.134), channel_id=1, source_target_pairs={{0,1},{1,0},{2,3},{3,2},{4,5},{5,4},{6,7},{7,6},{8,9},{9,8},{10,11... | collective-permute-start | bytes 393224 | tf_op jit(solution)/shard_map/ppermute | solution.py:609
  27.3 1.3 %shard_map.110 = (f32[3,9,144,128]{3,2,1,0:T(8,128)S(1)}, f32[3,9,144,128]{3,2,1,0:T(8,128)S(1)}, f32[3,9,144,128]{3,2,1,0:T(8,128)S(1)}, f32[8,144,128]{2,1,0:T(8,128)S(1)}) custom-call(f32[3,9,144,128]{3,2,1,0:T(8,128)S(1)} %get-tuple-element.115.refs_0_, ...), custom_call_target="tpu_custom_call", output_to_operand_aliasing={{0}: (0, {}), {1}: (1, {}), {2}: (2, {}), {3}: (3, {})} | custom-call | bytes 120000 | tf_op jit(solution)/shard_map/pallas_call | solution.py:36
  28.8 1.6 %collective-permute-start.13 = (f32[2,128,128]{2,1,0:T(8,128)S(1)}, f32[2,128,128]{2,1,0:T(8,128)S(1)}, u32[]{:S(2)}, u32[]{:S(2)}) collective-permute-start(f32[2,128,128]{2,1,0:T(8,128)S(1)} %get-tuple-element.141), channel_id=1, source_target_pairs={{0,1},{1,0},{2,3},{3,2},{4,5},{5,4},{6,7},{7,6},{8,9},{9,8},{10,11... | collective-permute-start | bytes 393224 | tf_op jit(solution)/shard_map/ppermute | solution.py:609
  30.4 1.2 %shard_map.112 = (f32[3,9,144,128]{3,2,1,0:T(8,128)S(1)}, f32[3,9,144,128]{3,2,1,0:T(8,128)S(1)}) custom-call(f32[3,9,144,128]{3,2,1,0:T(8,128)S(1)} %get-tuple-element.130.refs_0_, f32[3,9,144,128]{3,2,1,0:T(8,128)S(1)} %get-tuple-element.131.refs_1_, ...), custom_call_target="tpu_custom_call", output_to_operand_aliasing={{0}: (0, {}), {1}: (1, {})} | custom-call | bytes 110000 | tf_op jit(solution)/shard_map/pallas_call | solution.py:36
  31.6 1.5 %collective-permute-done.12.refs_5_.refs_6_ = f32[2,128,128]{2,1,0:T(8,128)S(1)} collective-permute-done((f32[2,128,128]{2,1,0:T(8,128)S(1)}, f32[2,128,128]{2,1,0:T(8,128)S(1)}, u32[]{:S(2)}, u32[]{:S(2)}) %collective-permute-start.12) | collective-permute-done | bytes 131104 | tf_op jit(solution)/shard_map/ppermute | solution.py:609
  33.4 1.3 %shard_map.114 = (f32[3,9,144,128]{3,2,1,0:T(8,128)S(1)}, f32[3,9,144,128]{3,2,1,0:T(8,128)S(1)}, f32[3,9,144,128]{3,2,1,0:T(8,128)S(1)}, f32[8,144,128]{2,1,0:T(8,128)S(1)}) custom-call(f32[3,9,144,128]{3,2,1,0:T(8,128)S(1)} %get-tuple-element.128.refs_0_, ...), custom_call_target="tpu_custom_call", output_to_operand_aliasing={{0}: (0, {}), {1}: (1, {}), {2}: (2, {}), {3}: (3, {})} | custom-call | bytes 120000 | tf_op jit(solution)/shard_map/pallas_call | solution.py:36
  34.7 1.0 %collective-permute-done.13.refs_5_.refs_6_ = f32[2,128,128]{2,1,0:T(8,128)S(1)} collective-permute-done((f32[2,128,128]{2,1,0:T(8,128)S(1)}, f32[2,128,128]{2,1,0:T(8,128)S(1)}, u32[]{:S(2)}, u32[]{:S(2)}) %collective-permute-start.13) | collective-permute-done | bytes 131104 | tf_op jit(solution)/shard_map/ppermute | solution.py:609
  35.9 1.1 %collective-permute-start.15 = (f32[2,128,128]{2,1,0:T(8,128)S(1)}, f32[2,128,128]{2,1,0:T(8,128)S(1)}, u32[]{:S(2)}, u32[]{:S(2)}) collective-permute-start(f32[2,128,128]{2,1,0:T(8,128)S(1)} %get-tuple-element.155), channel_id=1, source_target_pairs={{0,1},{1,0},{2,3},{3,2},{4,5},{5,4},{6,7},{7,6},{8,9},{9,8},{10,11... | collective-permute-start | bytes 393224 | tf_op jit(solution)/shard_map/ppermute | solution.py:609
  37.0 1.2 %shard_map.116 = (f32[3,9,144,128]{3,2,1,0:T(8,128)S(1)}, f32[3,9,144,128]{3,2,1,0:T(8,128)S(1)}) custom-call(f32[3,9,144,128]{3,2,1,0:T(8,128)S(1)} %get-tuple-element.144.refs_0_, f32[3,9,144,128]{3,2,1,0:T(8,128)S(1)} %get-tuple-element.145.refs_1_, ...), custom_call_target="tpu_custom_call", output_to_operand_aliasing={{0}: (0, {}), {1}: (1, {})} | custom-call | bytes 110000 | tf_op jit(solution)/shard_map/pallas_call | solution.py:36
  38.2 1.3 %shard_map.117 = (f32[3,9,144,128]{3,2,1,0:T(8,128)S(1)}, f32[3,9,144,128]{3,2,1,0:T(8,128)S(1)}, f32[3,9,144,128]{3,2,1,0:T(8,128)S(1)}, f32[8,144,128]{2,1,0:T(8,128)S(1)}) custom-call(f32[3,9,144,128]{3,2,1,0:T(8,128)S(1)} %get-tuple-element.142.refs_0_, ...), custom_call_target="tpu_custom_call", output_to_operand_aliasing={{0}: (0, {}), {1}: (1, {}), {2}: (2, {}), {3}: (3, {})} | custom-call | bytes 120000 | tf_op jit(solution)/shard_map/pallas_call | solution.py:36
  39.6 0.7 %shard_map.121 = (f32[4,48,128]{2,1,0:T(8,128)S(1)}, f32[4,48,128]{2,1,0:T(8,128)S(1)}, f32[4,48,128]{2,1,0:T(8,128)S(1)}, f32[4,48,128]{2,1,0:T(8,128)S(1)}) custom-call(f32[8,144,128]{2,1,0:T(8,128)S(1)} %get-tuple-element.158.total, f32[3,9,144,128]{3,2,1,0:T(8,128)S(1)} %get-tuple-element.153.refs_2_.after, s32[16]{0:T(128)} %block_ids_far.1), custom_call_target="tpu_custom_call" | custom-call | bytes 80000 | tf_op jit(solution)/shard_map/pallas_call | solution.py:36
  41.9 1.6 %collective-permute-start.18 = (f32[4,48,128]{2,1,0:T(8,128)S(1)}, f32[4,48,128]{2,1,0:T(8,128)S(1)}, u32[]{:S(2)}, u32[]{:S(2)}) collective-permute-start(f32[4,48,128]{2,1,0:T(8,128)S(1)} %get-tuple-element.166), channel_id=1, source_target_pairs={{0,4},{2,6},{4,0},{6,2},{8,12},{10,14},{12,8},{14,10},{16,20},{18,... | collective-permute-start | bytes 294920 | tf_op jit(solution)/shard_map/ppermute | solution.py:609
  43.5 1.0 %collective-permute-start.20 = (f32[4,16,128]{2,1,0:T(8,128)S(1)}, f32[4,16,128]{2,1,0:T(8,128)S(1)}, u32[]{:S(2)}, u32[]{:S(2)}) collective-permute-start(f32[4,16,128]{2,1,0:T(8,128)S(1)} %get-tuple-element.169), channel_id=1, source_target_pairs={{0,4},{2,6},{4,0},{6,2},{8,12},{10,14},{12,8},{14,10},{16,20},{18,... | collective-permute-start | bytes 98312 | tf_op jit(solution)/shard_map/ppermute | solution.py:609
  44.5 3.2 %collective-permute-done.20.refs_3_ = f32[4,16,128]{2,1,0:T(8,128)S(1)} collective-permute-done((f32[4,16,128]{2,1,0:T(8,128)S(1)}, f32[4,16,128]{2,1,0:T(8,128)S(1)}, u32[]{:S(2)}, u32[]{:S(2)}) %collective-permute-start.20) | collective-permute-done | bytes 32800 | tf_op jit(solution)/shard_map/ppermute | solution.py:609
  48.3 3.9 %collective-permute-start.23 = (f32[64,128]{1,0:T(8,128)S(1)}, f32[64,128]{1,0:T(8,128)S(1)}, u32[]{:S(2)}, u32[]{:S(2)}) collective-permute-start(f32[64,128]{1,0:T(8,128)S(1)} %get-tuple-element.173), channel_id=1, source_target_pairs={{0,8},{2,10},{4,12},{6,14},{8,0},{10,2},{12,4},{14,6},{16,24},{18,... | collective-permute-start | bytes 98312 | tf_op jit(solution)/shard_map/ppermute | solution.py:609
  52.2 1.7 %shard_map.120 = f32[1,6,8,128,128]{4,3,2,1,0:T(8,128)} custom-call(f32[3,9,144,128]{3,2,1,0:T(8,128)S(1)} %get-tuple-element.156.e, f32[3,9,144,128]{3,2,1,0:T(8,128)S(1)} %get-tuple-element.157.h), custom_call_target="tpu_custom_call" | custom-call | bytes 170000 | tf_op jit(solution)/shard_map/pallas_call | solution.py:36
  54.1 0.6 %shard_map.126 = f32[64,128]{1,0:T(8,128)} custom-call(f32[64,128]{1,0:T(8,128)S(1)} %get-tuple-element.170.refs_0_, f32[64,128]{1,0:T(8,128)S(1)} %collective-permute-done.21.refs_1_, f32[64,128]{1,0:T(8,128)S(1)} %collective-permute-done.22.refs_2_, f32[64,128]{1,0:T(8,128)S(1)} %collective-permute-done.23.refs_3_), custom_call_target="tpu_custom_call" | custom-call | bytes 30000 | tf_op jit(solution)/shard_map/pallas_call | solution.py:36
  (52 shorter events, 5.5 us)
Async XLA Ops:
  0.6 16.0 %copy-start = (f32[1,6,8,128,128]{4,3,2,1,0:T(8,128)S(1)}, f32[1,6,8,128,128]{4,3,2,1,0:T(8,128)}, u32[]{:S(2)}) copy-start(f32[1,6,8,128,128]{4,3,2,1,0:T(8,128)} %given.3) | copy-start | bytes 9437188
  0.6 16.0 %copy-start.1 = (f32[1,6,8,128,128]{4,3,2,1,0:T(8,128)S(1)}, f32[1,6,8,128,128]{4,3,2,1,0:T(8,128)}, u32[]{:S(2)}) copy-start(f32[1,6,8,128,128]{4,3,2,1,0:T(8,128)} %given.2) | copy-start | bytes 9437188
  0.6 8.6 %collective-permute-start = (f32[64,128]{1,0:T(8,128)}, f32[64,128]{1,0:T(8,128)S(1)}, u32[]{:S(2)}, u32[]{:S(2)}) collective-permute-start(f32[64,128]{1,0:T(8,128)} %bitcast.2), channel_id=1, source_target_pairs={{0,8},{2,10},{4,12},{6,14},{8,0},{10,2},{12,4},{14,6},{16,24},{18,... | collective-permute-start | bytes 98312 | tf_op jit(solution)/shard_map/ppermute | solution.py:609
  3.7 5.6 %collective-permute-start.1 = (f32[64,128]{1,0:T(8,128)}, f32[64,128]{1,0:T(8,128)S(1)}, u32[]{:S(2)}, u32[]{:S(2)}) collective-permute-start(f32[64,128]{1,0:T(8,128)} %bitcast.3), channel_id=1, source_target_pairs={{0,16},{2,18},{4,20},{6,22},{8,24},{10,26},{12,28},{14,30},{16,0},... | collective-permute-start | bytes 98312 | tf_op jit(solution)/shard_map/ppermute | solution.py:609
  6.3 5.9 %collective-permute-start.2 = (f32[64,128]{1,0:T(8,128)}, f32[64,128]{1,0:T(8,128)S(1)}, u32[]{:S(2)}, u32[]{:S(2)}) collective-permute-start(f32[64,128]{1,0:T(8,128)} %bitcast.4), channel_id=1, source_target_pairs={{0,24},{2,26},{4,28},{6,30},{8,16},{10,18},{12,20},{14,22},{16,8},... | collective-permute-start | bytes 98312 | tf_op jit(solution)/shard_map/ppermute | solution.py:609
  7.7 10.4 %collective-permute-start.3 = (f32[2,128,128]{2,1,0:T(8,128)S(1)}, f32[2,128,128]{2,1,0:T(8,128)S(1)}, u32[]{:S(2)}, u32[]{:S(2)}) collective-permute-start(f32[2,128,128]{2,1,0:T(8,128)S(1)} %get-tuple-element.93), channel_id=1, source_target_pairs={{0,1},{1,0},{2,3},{3,2},{4,5},{5,4},{6,7},{7,6},{8,9},{9,8},{10,11... | collective-permute-start | bytes 393224 | tf_op jit(solution)/shard_map/ppermute | solution.py:609
  12.3 7.0 %collective-permute-start.5 = (f32[4,64,128]{2,1,0:T(8,128)S(1)}, f32[4,64,128]{2,1,0:T(8,128)S(1)}, u32[]{:S(2)}, u32[]{:S(2)}) collective-permute-start(f32[4,64,128]{2,1,0:T(8,128)S(1)} %get-tuple-element.89.near.refs_0_), channel_id=1, source_target_pairs={{0,2},{2,0},{4,6},{6,4},{8,10},{10,8},{12,14},{14,12},{16,18},{18,... | collective-permute-start | bytes 393224 | tf_op jit(solution)/shard_map/ppermute | solution.py:609
  12.4 5.7 %collective-permute-start.4 = (f32[4,16,128]{2,1,0:T(8,128)S(1)}, f32[4,16,128]{2,1,0:T(8,128)S(1)}, u32[]{:S(2)}, u32[]{:S(2)}) collective-permute-start(f32[4,16,128]{2,1,0:T(8,128)S(1)} %get-tuple-element.95), channel_id=1, source_target_pairs={{0,4},{2,6},{4,0},{6,2},{8,12},{10,14},{12,8},{14,10},{16,20},{18,... | collective-permute-start | bytes 98312 | tf_op jit(solution)/shard_map/ppermute | solution.py:609
  13.9 7.6 %collective-permute-start.8 = (f32[4,48,128]{2,1,0:T(8,128)S(1)}, f32[4,48,128]{2,1,0:T(8,128)S(1)}, u32[]{:S(2)}, u32[]{:S(2)}) collective-permute-start(f32[4,48,128]{2,1,0:T(8,128)S(1)} %get-tuple-element.113), channel_id=1, source_target_pairs={{0,4},{2,6},{4,0},{6,2},{8,12},{10,14},{12,8},{14,10},{16,20},{18,... | collective-permute-start | bytes 294920 | tf_op jit(solution)/shard_map/ppermute | solution.py:609
  14.4 7.1 %collective-permute-start.7 = (f32[2,128,128]{2,1,0:T(8,128)S(1)}, f32[2,128,128]{2,1,0:T(8,128)S(1)}, u32[]{:S(2)}, u32[]{:S(2)}) collective-permute-start(f32[2,128,128]{2,1,0:T(8,128)S(1)} %get-tuple-element.105), channel_id=1, source_target_pairs={{0,1},{1,0},{2,3},{3,2},{4,5},{5,4},{6,7},{7,6},{8,9},{9,8},{10,11... | collective-permute-start | bytes 393224 | tf_op jit(solution)/shard_map/ppermute | solution.py:609
  18.0 1.3 %collective-permute-start.6 = (f32[4,16,128]{2,1,0:T(8,128)S(1)}, f32[4,16,128]{2,1,0:T(8,128)S(1)}, u32[]{:S(2)}, u32[]{:S(2)}) collective-permute-start(f32[4,16,128]{2,1,0:T(8,128)S(1)} %shard_map.99.refs_1_), channel_id=1, source_target_pairs={{0,2},{2,0},{4,6},{6,4},{8,10},{10,8},{12,14},{14,12},{16,18},{18,... | collective-permute-start | bytes 98312 | tf_op jit(solution)/shard_map/ppermute | solution.py:609
  19.8 6.7 %collective-permute-start.10 = (f32[2,128,128]{2,1,0:T(8,128)S(1)}, f32[2,128,128]{2,1,0:T(8,128)S(1)}, u32[]{:S(2)}, u32[]{:S(2)}) collective-permute-start(f32[2,128,128]{2,1,0:T(8,128)S(1)} %get-tuple-element.101.near), channel_id=1, source_target_pairs={{0,1},{1,0},{2,3},{3,2},{4,5},{5,4},{6,7},{7,6},{8,9},{9,8},{10,11... | collective-permute-start | bytes 393224 | tf_op jit(solution)/shard_map/ppermute | solution.py:609
  21.5 2.5 %collective-permute-start.9 = (f32[4,48,128]{2,1,0:T(8,128)S(1)}, f32[4,48,128]{2,1,0:T(8,128)S(1)}, u32[]{:S(2)}, u32[]{:S(2)}) collective-permute-start(f32[4,48,128]{2,1,0:T(8,128)S(1)} %shard_map.105.refs_0_), channel_id=1, source_target_pairs={{0,2},{2,0},{4,6},{6,4},{8,10},{10,8},{12,14},{14,12},{16,18},{18,... | collective-permute-start | bytes 294920 | tf_op jit(solution)/shard_map/ppermute | solution.py:609
  22.4 6.1 %collective-permute-start.11 = (f32[2,128,128]{2,1,0:T(8,128)S(1)}, f32[2,128,128]{2,1,0:T(8,128)S(1)}, u32[]{:S(2)}, u32[]{:S(2)}) collective-permute-start(f32[2,128,128]{2,1,0:T(8,128)S(1)} %get-tuple-element.127), channel_id=1, source_target_pairs={{0,1},{1,0},{2,3},{3,2},{4,5},{5,4},{6,7},{7,6},{8,9},{9,8},{10,11... | collective-permute-start | bytes 393224 | tf_op jit(solution)/shard_map/ppermute | solution.py:609
  26.7 6.4 %collective-permute-start.12 = (f32[2,128,128]{2,1,0:T(8,128)S(1)}, f32[2,128,128]{2,1,0:T(8,128)S(1)}, u32[]{:S(2)}, u32[]{:S(2)}) collective-permute-start(f32[2,128,128]{2,1,0:T(8,128)S(1)} %get-tuple-element.134), channel_id=1, source_target_pairs={{0,1},{1,0},{2,3},{3,2},{4,5},{5,4},{6,7},{7,6},{8,9},{9,8},{10,11... | collective-permute-start | bytes 393224 | tf_op jit(solution)/shard_map/ppermute | solution.py:609
  28.8 6.8 %collective-permute-start.13 = (f32[2,128,128]{2,1,0:T(8,128)S(1)}, f32[2,128,128]{2,1,0:T(8,128)S(1)}, u32[]{:S(2)}, u32[]{:S(2)}) collective-permute-start(f32[2,128,128]{2,1,0:T(8,128)S(1)} %get-tuple-element.141), channel_id=1, source_target_pairs={{0,1},{1,0},{2,3},{3,2},{4,5},{5,4},{6,7},{7,6},{8,9},{9,8},{10,11... | collective-permute-start | bytes 393224 | tf_op jit(solution)/shard_map/ppermute | solution.py:609
  33.3 6.2 %collective-permute-start.14 = (f32[2,128,128]{2,1,0:T(8,128)S(1)}, f32[2,128,128]{2,1,0:T(8,128)S(1)}, u32[]{:S(2)}, u32[]{:S(2)}) collective-permute-start(f32[2,128,128]{2,1,0:T(8,128)S(1)} %get-tuple-element.152), channel_id=1, source_target_pairs={{0,1},{1,0},{2,3},{3,2},{4,5},{5,4},{6,7},{7,6},{8,9},{9,8},{10,11... | collective-permute-start | bytes 393224 | tf_op jit(solution)/shard_map/ppermute | solution.py:609
  35.9 5.3 %collective-permute-start.15 = (f32[2,128,128]{2,1,0:T(8,128)S(1)}, f32[2,128,128]{2,1,0:T(8,128)S(1)}, u32[]{:S(2)}, u32[]{:S(2)}) collective-permute-start(f32[2,128,128]{2,1,0:T(8,128)S(1)} %get-tuple-element.155), channel_id=1, source_target_pairs={{0,1},{1,0},{2,3},{3,2},{4,5},{5,4},{6,7},{7,6},{8,9},{9,8},{10,11... | collective-permute-start | bytes 393224 | tf_op jit(solution)/shard_map/ppermute | solution.py:609
  40.3 1.4 %collective-permute-start.16 = (f32[4,48,128]{2,1,0:T(8,128)S(1)}, f32[4,48,128]{2,1,0:T(8,128)S(1)}, u32[]{:S(2)}, u32[]{:S(2)}) collective-permute-start(f32[4,48,128]{2,1,0:T(8,128)S(1)} %get-tuple-element.161), channel_id=1, source_target_pairs={{0,2},{2,0},{4,6},{6,4},{8,10},{10,8},{12,14},{14,12},{16,18},{18,... | collective-permute-start | bytes 294920 | tf_op jit(solution)/shard_map/ppermute | solution.py:609
  40.4 1.4 %collective-permute-start.17 = (f32[4,48,128]{2,1,0:T(8,128)S(1)}, f32[4,48,128]{2,1,0:T(8,128)S(1)}, u32[]{:S(2)}, u32[]{:S(2)}) collective-permute-start(f32[4,48,128]{2,1,0:T(8,128)S(1)} %get-tuple-element.162), channel_id=1, source_target_pairs={{0,2},{2,0},{4,6},{6,4},{8,10},{10,8},{12,14},{14,12},{16,18},{18,... | collective-permute-start | bytes 294920 | tf_op jit(solution)/shard_map/ppermute | solution.py:609
  41.6 1.9 %collective-permute-start.19 = (f32[8,16,128]{2,1,0:T(8,128)S(1)}, f32[8,16,128]{2,1,0:T(8,128)S(1)}, u32[]{:S(2)}, u32[]{:S(2)}) collective-permute-start(f32[8,16,128]{2,1,0:T(8,128)S(1)} %get-tuple-element.167), channel_id=1, source_target_pairs={{0,2},{2,0},{4,6},{6,4},{8,10},{10,8},{12,14},{14,12},{16,18},{18,... | collective-permute-start | bytes 196616 | tf_op jit(solution)/shard_map/ppermute | solution.py:609
  41.9 5.8 %collective-permute-start.18 = (f32[4,48,128]{2,1,0:T(8,128)S(1)}, f32[4,48,128]{2,1,0:T(8,128)S(1)}, u32[]{:S(2)}, u32[]{:S(2)}) collective-permute-start(f32[4,48,128]{2,1,0:T(8,128)S(1)} %get-tuple-element.166), channel_id=1, source_target_pairs={{0,4},{2,6},{4,0},{6,2},{8,12},{10,14},{12,8},{14,10},{16,20},{18,... | collective-permute-start | bytes 294920 | tf_op jit(solution)/shard_map/ppermute | solution.py:609
  43.5 4.2 %collective-permute-start.20 = (f32[4,16,128]{2,1,0:T(8,128)S(1)}, f32[4,16,128]{2,1,0:T(8,128)S(1)}, u32[]{:S(2)}, u32[]{:S(2)}) collective-permute-start(f32[4,16,128]{2,1,0:T(8,128)S(1)} %get-tuple-element.169), channel_id=1, source_target_pairs={{0,4},{2,6},{4,0},{6,2},{8,12},{10,14},{12,8},{14,10},{16,20},{18,... | collective-permute-start | bytes 98312 | tf_op jit(solution)/shard_map/ppermute | solution.py:609
  47.7 6.2 %collective-permute-start.21 = (f32[64,128]{1,0:T(8,128)S(1)}, f32[64,128]{1,0:T(8,128)S(1)}, u32[]{:S(2)}, u32[]{:S(2)}) collective-permute-start(f32[64,128]{1,0:T(8,128)S(1)} %get-tuple-element.171), channel_id=1, source_target_pairs={{0,24},{2,26},{4,28},{6,30},{8,16},{10,18},{12,20},{14,22},{16,8},... | collective-permute-start | bytes 98312 | tf_op jit(solution)/shard_map/ppermute | solution.py:609
  48.1 5.8 %collective-permute-start.22 = (f32[64,128]{1,0:T(8,128)S(1)}, f32[64,128]{1,0:T(8,128)S(1)}, u32[]{:S(2)}, u32[]{:S(2)}) collective-permute-start(f32[64,128]{1,0:T(8,128)S(1)} %get-tuple-element.172), channel_id=1, source_target_pairs={{0,16},{2,18},{4,20},{6,22},{8,24},{10,26},{12,28},{14,30},{16,0},... | collective-permute-start | bytes 98312 | tf_op jit(solution)/shard_map/ppermute | solution.py:609
  48.3 5.8 %collective-permute-start.23 = (f32[64,128]{1,0:T(8,128)S(1)}, f32[64,128]{1,0:T(8,128)S(1)}, u32[]{:S(2)}, u32[]{:S(2)}) collective-permute-start(f32[64,128]{1,0:T(8,128)S(1)} %get-tuple-element.173), channel_id=1, source_target_pairs={{0,8},{2,10},{4,12},{6,14},{8,0},{10,2},{12,4},{14,6},{16,24},{18,... | collective-permute-start | bytes 98312 | tf_op jit(solution)/shard_map/ppermute | solution.py:609

commit v15 on v12

--- a/solution.py
+++ b/solution.py
@@ -771,6 +771,17 @@
                 0.8,
                 middle,
             )
+        e_adj, h_adj, e_fwd, edges, *pays = call(
+            functools.partial(edge_kernel, step, 1),
+            [field_shape] * 3 + [edges_shape] + [halo_shape] * more,
+            [IN_VMEM] * (4 + more),
+            [e_adj, h_adj, e_fwd, edges, coef] + arrived_adj,
+            [IN_VMEM] * (5 + len(arrived_adj)),
+            aliases={0: 0, 1: 1, 2: 2, 3: 3},
+        )
+        if not more:
+            break
+        arrived_fwd, arrived_adj = arrived_fwd_next, trade(pays)
         if step == 0:
             coef = call(
                 functools.partial(coef_inner_kernel, first_slot, len(last)),
@@ -791,17 +802,6 @@
                 aliases={0: 0, 1: 1, 2: 2},
                 micros=0.5,
             )
-        e_adj, h_adj, e_fwd, edges, *pays = call(
-            functools.partial(edge_kernel, step, 1),
-            [field_shape] * 3 + [edges_shape] + [halo_shape] * more,
-            [IN_VMEM] * (4 + more),
-            [e_adj, h_adj, e_fwd, edges, coef] + arrived_adj,
-            [IN_VMEM] * (5 + len(arrived_adj)),
-            aliases={0: 0, 1: 1, 2: 2, 3: 3},
-        )
-        if not more:
-            break
-        arrived_fwd, arrived_adj = arrived_fwd_next, trade(pays)
         e_fwd, h_fwd = call(
             functools.partial(inner_kernel, step + 1, 0),
             [field_shape] * 2,

time: 53.4 us -> 53.4 us (level)
  waiting for transfers between devices: 9.39 us -> 9.99 us
  starting transfers between devices: 25.2 us -> 24.6 us
    ppermute x21, waiting for transfers between devices: 9.39 us -> 9.99 us  [swap_over(): lax.ppermute(array, axis, [(i, i ^ mask) for i in range(lax.axis_size(axi...]
    ppermute x21, starting transfers between devices: 25.2 us -> 24.6 us  [swap_over(): lax.ppermute(array, axis, [(i, i ^ mask) for i in range(lax.axis_size(axi...]
where the time goes in v15:
time: 53.4 us; the launch traced here: 53.2 us
  starting transfers between devices  24.6 us (46%)
  Pallas kernels  17 us (32%)
  waiting for transfers between devices  9.99 us (19%)
  between operations  1.56 us (3%)
    ppermute x21, starting transfers between devices, swap_over(): lax.ppermute(array, axis, [(i, i ^ mask) for i in range(lax.axis_size(axi...  24.6 us
    pallas_call x30, Pallas kernels, call(): pl.pallas_call(kernel, out_shape=outs, in_specs=specs, out_specs=out_spec...  17 us
    ppermute x21, waiting for transfers between devices, swap_over(): lax.ppermute(array, axis, [(i, i ^ mask) for i in range(lax.axis_size(axi...  9.99 us
  transfers between devices with their start and end apart: 21, of which 10 were waited for; matrix products, arithmetic and copies ran while one was open for 0% of the time, Pallas kernels for 30%

profile of v15, /device:TPU:0, one launch (start us, length us, event | category | flops | bytes accessed | tf_op | source)
XLA Modules:
  0.0 53.2 jit_solution(13822227820508421124)
XLA Ops:
  0.6 5.1 %collective-permute-start.2 = (f32[64,128]{1,0:T(8,128)}, f32[64,128]{1,0:T(8,128)S(1)}, u32[]{:S(2)}, u32[]{:S(2)}) collective-permute-start(f32[64,128]{1,0:T(8,128)} %bitcast.2), channel_id=1, source_target_pairs={{0,24},{2,26},{4,28},{6,30},{8,16},{10,18},{12,20},{14,22},{16,8},... | collective-permute-start | bytes 98312 | tf_op jit(solution)/shard_map/ppermute | solution.py:590
  5.8 0.6 %collective-permute-start = (f32[64,128]{1,0:T(8,128)}, f32[64,128]{1,0:T(8,128)S(1)}, u32[]{:S(2)}, u32[]{:S(2)}) collective-permute-start(f32[64,128]{1,0:T(8,128)} %bitcast.4), channel_id=1, source_target_pairs={{0,8},{2,10},{4,12},{6,14},{8,0},{10,2},{12,4},{14,6},{16,24},{18,... | collective-permute-start | bytes 98312 | tf_op jit(solution)/shard_map/ppermute | solution.py:590
  6.4 1.4 %shard_map.95 = (f32[64,128]{1,0:T(8,128)S(1)}, f32[2,2,128,128]{3,2,1,0:T(8,128)S(1)}) custom-call(f32[1,6,8,128,128]{4,3,2,1,0:T(8,128)} %given.3, f32[1,6,8,128,128]{4,3,2,1,0:T(8,128)} %given.2, f32[64,128]{1,0:T(8,128)} %bitcast.5), custom_call_target="tpu_custom_call" | custom-call | bytes 30000 | tf_op jit(solution)/shard_map/pallas_call | solution.py:36
  7.8 1.4 %collective-permute-start.3 = (f32[2,2,128,128]{3,2,1,0:T(8,128)S(1)}, f32[2,2,128,128]{3,2,1,0:T(8,128)S(1)}, u32[]{:S(2)}, u32[]{:S(2)}) collective-permute-start(f32[2,2,128,128]{3,2,1,0:T(8,128)S(1)} %get-tuple-element.91), channel_id=1, source_target_pairs={{0,1},{1,0},{2,3},{3,2},{4,5},{5,4},{6,7},{7,6},{8,9},{9,8},{10,11... | collective-permute-start | bytes 786440 | tf_op jit(solution)/shard_map/ppermute | solution.py:590
  9.2 1.5 %collective-permute-done.1.refs_2_ = f32[64,128]{1,0:T(8,128)S(1)} collective-permute-done((f32[64,128]{1,0:T(8,128)}, f32[64,128]{1,0:T(8,128)S(1)}, u32[]{:S(2)}, u32[]{:S(2)}) %collective-permute-start.1) | collective-permute-done | bytes 32800 | tf_op jit(solution)/shard_map/ppermute | solution.py:590
  10.8 1.6 %collective-permute-start.4 = (f32[4,64,128]{2,1,0:T(8,128)S(1)}, f32[4,64,128]{2,1,0:T(8,128)S(1)}, u32[]{:S(2)}, u32[]{:S(2)}) collective-permute-start(f32[4,64,128]{2,1,0:T(8,128)S(1)} %shard_map.96.near.refs_8_), channel_id=1, source_target_pairs={{0,4},{2,6},{4,0},{6,2},{8,12},{10,14},{12,8},{14,10},{16,20},{18,... | collective-permute-start | bytes 393224 | tf_op jit(solution)/shard_map/ppermute | solution.py:590
  13.1 1.2 %shard_map.97 = (f32[3,9,144,128]{3,2,1,0:T(8,128)S(1)}, f32[3,9,144,128]{3,2,1,0:T(8,128)S(1)}, f32[3,8,128,128]{3,2,1,0:T(8,128)S(1)}) custom-call(f32[1,6,8,128,128]{4,3,2,1,0:T(8,128)S(1)} %copy-done, f32[4,64,128]{2,1,0:T(8,128)S(1)} %shard_map.96.near.refs_8_), custom_call_target="tpu_custom_call" | custom-call | bytes 120000 | tf_op jit(solution)/shard_map/pallas_call | solution.py:36
  14.3 1.4 %shard_map.98 = (f32[3,9,144,128]{3,2,1,0:T(8,128)S(1)}, f32[3,9,144,128]{3,2,1,0:T(8,128)S(1)}, f32[3,8,128,128]{3,2,1,0:T(8,128)S(1)}, f32[8,144,128]{2,1,0:T(...) custom-call(f32[1,6,8,128,128]{4,3,2,1,0:T(8,128)S(1)} %copy-done.1,, ...), custom_call_target="tpu_custom_call" | custom-call | bytes 150000 | tf_op jit(solution)/shard_map/pallas_call | solution.py:36
  16.2 0.7 %shard_map.100 = (f32[3,9,144,128]{3,2,1,0:T(8,128)S(1)}, f32[3,8,128,128]{3,2,1,0:T(8,128)S(1)}, f32[3,9,144,128]{3,2,1,0:T(8,128)S(1)}, f32[3,8,128,128]{3,2,1,0:T(8,128)S(1)}, f32[16,64,128]{2,1,0:T(8,128)S(1)}) custom-call(f32[3,9,144,128]{3,2,1,0:T(8,128)S(1)} %get-tuple-element.86.refs_, ...), custom_call_target="tpu_custom_call", output_to_operand_aliasing={{0}: (0, {}), {1}: (1, {}), {2}: (2, {}), {3}: (3, {})} | custom-call | bytes 60000 | tf_op jit(solution)/shard_map/pallas_call | solution.py:36
  17.5 1.5 %collective-permute-start.7 = (f32[2,128,128]{2,1,0:T(8,128)S(1)}, f32[2,128,128]{2,1,0:T(8,128)S(1)}, u32[]{:S(2)}, u32[]{:S(2)}) collective-permute-start(f32[2,128,128]{2,1,0:T(8,128)S(1)} %get-tuple-element.112), channel_id=1, source_target_pairs={{0,1},{1,0},{2,3},{3,2},{4,5},{5,4},{6,7},{7,6},{8,9},{9,8},{10,11... | collective-permute-start | bytes 393224 | tf_op jit(solution)/shard_map/ppermute | solution.py:590
  19.8 0.6 %shard_map.104.coef.refs_2_.refs_4_ = f32[8,128,128]{2,1,0:T(8,128)S(1)} custom-call(f32[8,128,128]{2,1,0:T(8,128)S(1)} %shard_map.101.refs_2_.refs_4_.coef_in, f32[4,64,128]{2,1,0:T(8,128)S(1)} %collective-permute-done.6.refs_0_, f32[16,16,128]{2,1,0:T(8,128)S(1)} %get-tuple-element.94.refs_1_.place, ...), custom_call_target="tpu_custom_call", output_to_operand_aliasing={{}: (0, {})} | custom-call | bytes 60000 | tf_op jit(solution)/shard_map/pallas_call | solution.py:36
  20.9 0.9 %shard_map.106 = (f32[3,9,144,128]{3,2,1,0:T(8,128)S(1)}, f32[3,9,144,128]{3,2,1,0:T(8,128)S(1)}) custom-call(f32[3,9,144,128]{3,2,1,0:T(8,128)S(1)} %get-tuple-element.108.refs_0_, f32[3,9,144,128]{3,2,1,0:T(8,128)S(1)} %get-tuple-element.109.refs_1_, ...), custom_call_target="tpu_custom_call", output_to_operand_aliasing={{0}: (0, {}), {1}: (1, {})} | custom-call | bytes 110000 | tf_op jit(solution)/shard_map/pallas_call | solution.py:36
  21.8 2.1 %collective-permute-done.7.refs_5_.refs_6_ = f32[2,128,128]{2,1,0:T(8,128)S(1)} collective-permute-done((f32[2,128,128]{2,1,0:T(8,128)S(1)}, f32[2,128,128]{2,1,0:T(8,128)S(1)}, u32[]{:S(2)}, u32[]{:S(2)}) %collective-permute-start.7) | collective-permute-done | bytes 131104 | tf_op jit(solution)/shard_map/ppermute | solution.py:590
  24.1 1.4 %collective-permute-start.9 = (f32[2,128,128]{2,1,0:T(8,128)S(1)}, f32[2,128,128]{2,1,0:T(8,128)S(1)}, u32[]{:S(2)}, u32[]{:S(2)}) collective-permute-start(f32[2,128,128]{2,1,0:T(8,128)S(1)} %get-tuple-element.126), channel_id=1, source_target_pairs={{0,1},{1,0},{2,3},{3,2},{4,5},{5,4},{6,7},{7,6},{8,9},{9,8},{10,11... | collective-permute-start | bytes 393224 | tf_op jit(solution)/shard_map/ppermute | solution.py:590
  25.5 1.2 %shard_map.108 = (f32[3,9,144,128]{3,2,1,0:T(8,128)S(1)}, f32[3,9,144,128]{3,2,1,0:T(8,128)S(1)}, f32[3,9,144,128]{3,2,1,0:T(8,128)S(1)}, f32[8,144,128]{2,1,0:T(8,128)S(1)}) custom-call(f32[3,9,144,128]{3,2,1,0:T(8,128)S(1)} %get-tuple-element.106.refs_0_, ...), custom_call_target="tpu_custom_call", output_to_operand_aliasing={{0}: (0, {}), {1}: (1, {}), {2}: (2, {}), {3}: (3, {})} | custom-call | bytes 120000 | tf_op jit(solution)/shard_map/pallas_call | solution.py:36
  27.0 1.3 %collective-permute-start.10 = (f32[2,128,128]{2,1,0:T(8,128)S(1)}, f32[2,128,128]{2,1,0:T(8,128)S(1)}, u32[]{:S(2)}, u32[]{:S(2)}) collective-permute-start(f32[2,128,128]{2,1,0:T(8,128)S(1)} %get-tuple-element.133), channel_id=1, source_target_pairs={{0,1},{1,0},{2,3},{3,2},{4,5},{5,4},{6,7},{7,6},{8,9},{9,8},{10,11... | collective-permute-start | bytes 393224 | tf_op jit(solution)/shard_map/ppermute | solution.py:590
  28.2 0.9 %shard_map.110 = (f32[3,9,144,128]{3,2,1,0:T(8,128)S(1)}, f32[3,9,144,128]{3,2,1,0:T(8,128)S(1)}) custom-call(f32[3,9,144,128]{3,2,1,0:T(8,128)S(1)} %get-tuple-element.122.refs_0_, f32[3,9,144,128]{3,2,1,0:T(8,128)S(1)} %get-tuple-element.123.refs_1_, ...), custom_call_target="tpu_custom_call", output_to_operand_aliasing={{0}: (0, {}), {1}: (1, {})} | custom-call | bytes 110000 | tf_op jit(solution)/shard_map/pallas_call | solution.py:36
  30.0 1.3 %collective-permute-start.11 = (f32[2,128,128]{2,1,0:T(8,128)S(1)}, f32[2,128,128]{2,1,0:T(8,128)S(1)}, u32[]{:S(2)}, u32[]{:S(2)}) collective-permute-start(f32[2,128,128]{2,1,0:T(8,128)S(1)} %get-tuple-element.144), channel_id=1, source_target_pairs={{0,1},{1,0},{2,3},{3,2},{4,5},{5,4},{6,7},{7,6},{8,9},{9,8},{10,11... | collective-permute-start | bytes 393224 | tf_op jit(solution)/shard_map/ppermute | solution.py:590
  31.3 1.2 %shard_map.112 = (f32[3,9,144,128]{3,2,1,0:T(8,128)S(1)}, f32[3,9,144,128]{3,2,1,0:T(8,128)S(1)}, f32[3,9,144,128]{3,2,1,0:T(8,128)S(1)}, f32[8,144,128]{2,1,0:T(8,128)S(1)}) custom-call(f32[3,9,144,128]{3,2,1,0:T(8,128)S(1)} %get-tuple-element.120.refs_0_, ...), custom_call_target="tpu_custom_call", output_to_operand_aliasing={{0}: (0, {}), {1}: (1, {}), {2}: (2, {}), {3}: (3, {})} | custom-call | bytes 120000 | tf_op jit(solution)/shard_map/pallas_call | solution.py:36
  32.4 0.6 %collective-permute-done.10.refs_5_.refs_6_ = f32[2,128,128]{2,1,0:T(8,128)S(1)} collective-permute-done((f32[2,128,128]{2,1,0:T(8,128)S(1)}, f32[2,128,128]{2,1,0:T(8,128)S(1)}, u32[]{:S(2)}, u32[]{:S(2)}) %collective-permute-start.10) | collective-permute-done | bytes 131104 | tf_op jit(solution)/shard_map/ppermute | solution.py:590
  33.3 1.5 %collective-permute-start.12 = (f32[2,128,128]{2,1,0:T(8,128)S(1)}, f32[2,128,128]{2,1,0:T(8,128)S(1)}, u32[]{:S(2)}, u32[]{:S(2)}) collective-permute-start(f32[2,128,128]{2,1,0:T(8,128)S(1)} %get-tuple-element.147), channel_id=1, source_target_pairs={{0,1},{1,0},{2,3},{3,2},{4,5},{5,4},{6,7},{7,6},{8,9},{9,8},{10,11... | collective-permute-start | bytes 393224 | tf_op jit(solution)/shard_map/ppermute | solution.py:590
  34.8 0.9 %shard_map.114 = (f32[3,9,144,128]{3,2,1,0:T(8,128)S(1)}, f32[3,9,144,128]{3,2,1,0:T(8,128)S(1)}) custom-call(f32[3,9,144,128]{3,2,1,0:T(8,128)S(1)} %get-tuple-element.136.refs_0_, f32[3,9,144,128]{3,2,1,0:T(8,128)S(1)} %get-tuple-element.137.refs_1_, ...), custom_call_target="tpu_custom_call", output_to_operand_aliasing={{0}: (0, {}), {1}: (1, {})} | custom-call | bytes 110000 | tf_op jit(solution)/shard_map/pallas_call | solution.py:36
  35.8 1.2 %shard_map.115 = (f32[3,9,144,128]{3,2,1,0:T(8,128)S(1)}, f32[3,9,144,128]{3,2,1,0:T(8,128)S(1)}, f32[3,9,144,128]{3,2,1,0:T(8,128)S(1)}, f32[8,144,128]{2,1,0:T(8,128)S(1)}) custom-call(f32[3,9,144,128]{3,2,1,0:T(8,128)S(1)} %get-tuple-element.134.refs_0_, ...), custom_call_target="tpu_custom_call", output_to_operand_aliasing={{0}: (0, {}), {1}: (1, {}), {2}: (2, {}), {3}: (3, {})} | custom-call | bytes 120000 | tf_op jit(solution)/shard_map/pallas_call | solution.py:36
  37.1 0.7 %shard_map.119 = (f32[4,48,128]{2,1,0:T(8,128)S(1)}, f32[4,48,128]{2,1,0:T(8,128)S(1)}, f32[4,48,128]{2,1,0:T(8,128)S(1)}, f32[4,48,128]{2,1,0:T(8,128)S(1)}) custom-call(f32[8,144,128]{2,1,0:T(8,128)S(1)} %get-tuple-element.150.total, f32[3,9,144,128]{3,2,1,0:T(8,128)S(1)} %get-tuple-element.145.refs_2_.after, s32[16]{0:T(128)} %block_ids_far.1), custom_call_target="tpu_custom_call" | custom-call | bytes 80000 | tf_op jit(solution)/shard_map/pallas_call | solution.py:36
  39.4 1.5 %collective-permute-start.15 = (f32[4,48,128]{2,1,0:T(8,128)S(1)}, f32[4,48,128]{2,1,0:T(8,128)S(1)}, u32[]{:S(2)}, u32[]{:S(2)}) collective-permute-start(f32[4,48,128]{2,1,0:T(8,128)S(1)} %get-tuple-element.158), channel_id=1, source_target_pairs={{0,4},{2,6},{4,0},{6,2},{8,12},{10,14},{12,8},{14,10},{16,20},{18,... | collective-permute-start | bytes 294920 | tf_op jit(solution)/shard_map/ppermute | solution.py:590
  40.9 1.1 %collective-permute-start.17 = (f32[4,16,128]{2,1,0:T(8,128)S(1)}, f32[4,16,128]{2,1,0:T(8,128)S(1)}, u32[]{:S(2)}, u32[]{:S(2)}) collective-permute-start(f32[4,16,128]{2,1,0:T(8,128)S(1)} %get-tuple-element.161), channel_id=1, source_target_pairs={{0,4},{2,6},{4,0},{6,2},{8,12},{10,14},{12,8},{14,10},{16,20},{18,... | collective-permute-start | bytes 98312 | tf_op jit(solution)/shard_map/ppermute | solution.py:590
  42.0 3.2 %collective-permute-done.17.refs_3_ = f32[4,16,128]{2,1,0:T(8,128)S(1)} collective-permute-done((f32[4,16,128]{2,1,0:T(8,128)S(1)}, f32[4,16,128]{2,1,0:T(8,128)S(1)}, u32[]{:S(2)}, u32[]{:S(2)}) %collective-permute-start.17) | collective-permute-done | bytes 32800 | tf_op jit(solution)/shard_map/ppermute | solution.py:590
  45.2 2.2 %collective-permute-start.18 = (f32[64,128]{1,0:T(8,128)S(1)}, f32[64,128]{1,0:T(8,128)S(1)}, u32[]{:S(2)}, u32[]{:S(2)}) collective-permute-start(f32[64,128]{1,0:T(8,128)S(1)} %get-tuple-element.163), channel_id=1, source_target_pairs={{0,24},{2,26},{4,28},{6,30},{8,16},{10,18},{12,20},{14,22},{16,8},... | collective-permute-start | bytes 98312 | tf_op jit(solution)/shard_map/ppermute | solution.py:590
  47.4 2.2 %collective-permute-start.20 = (f32[64,128]{1,0:T(8,128)S(1)}, f32[64,128]{1,0:T(8,128)S(1)}, u32[]{:S(2)}, u32[]{:S(2)}) collective-permute-start(f32[64,128]{1,0:T(8,128)S(1)} %get-tuple-element.165), channel_id=1, source_target_pairs={{0,8},{2,10},{4,12},{6,14},{8,0},{10,2},{12,4},{14,6},{16,24},{18,... | collective-permute-start | bytes 98312 | tf_op jit(solution)/shard_map/ppermute | solution.py:590
  49.7 1.7 %shard_map.118 = f32[1,6,8,128,128]{4,3,2,1,0:T(8,128)} custom-call(f32[3,9,144,128]{3,2,1,0:T(8,128)S(1)} %get-tuple-element.148.e, f32[3,9,144,128]{3,2,1,0:T(8,128)S(1)} %get-tuple-element.149.h), custom_call_target="tpu_custom_call" | custom-call | bytes 170000 | tf_op jit(solution)/shard_map/pallas_call | solution.py:36
  51.4 1.1 %collective-permute-done.19.refs_2_ = f32[64,128]{1,0:T(8,128)S(1)} collective-permute-done((f32[64,128]{1,0:T(8,128)S(1)}, f32[64,128]{1,0:T(8,128)S(1)}, u32[]{:S(2)}, u32[]{:S(2)}) %collective-permute-start.19) | collective-permute-done | bytes 32800 | tf_op jit(solution)/shard_map/ppermute | solution.py:590
  52.5 0.6 %shard_map.124 = f32[64,128]{1,0:T(8,128)} custom-call(f32[64,128]{1,0:T(8,128)S(1)} %get-tuple-element.162.refs_0_, f32[64,128]{1,0:T(8,128)S(1)} %collective-permute-done.18.refs_1_, f32[64,128]{1,0:T(8,128)S(1)} %collective-permute-done.19.refs_2_, f32[64,128]{1,0:T(8,128)S(1)} %collective-permute-done.20.refs_3_), custom_call_target="tpu_custom_call" | custom-call | bytes 30000 | tf_op jit(solution)/shard_map/pallas_call | solution.py:36
  (44 shorter events, 5.6 us)
Async XLA Ops:
  0.6 12.5 %copy-start = (f32[1,6,8,128,128]{4,3,2,1,0:T(8,128)S(1)}, f32[1,6,8,128,128]{4,3,2,1,0:T(8,128)}, u32[]{:S(2)}) copy-start(f32[1,6,8,128,128]{4,3,2,1,0:T(8,128)} %given.2) | copy-start | bytes 9437188
  0.6 8.6 %collective-permute-start.2 = (f32[64,128]{1,0:T(8,128)}, f32[64,128]{1,0:T(8,128)S(1)}, u32[]{:S(2)}, u32[]{:S(2)}) collective-permute-start(f32[64,128]{1,0:T(8,128)} %bitcast.2), channel_id=1, source_target_pairs={{0,24},{2,26},{4,28},{6,30},{8,16},{10,18},{12,20},{14,22},{16,8},... | collective-permute-start | bytes 98312 | tf_op jit(solution)/shard_map/ppermute | solution.py:590
  5.8 5.0 %collective-permute-start.1 = (f32[64,128]{1,0:T(8,128)}, f32[64,128]{1,0:T(8,128)S(1)}, u32[]{:S(2)}, u32[]{:S(2)}) collective-permute-start(f32[64,128]{1,0:T(8,128)} %bitcast.3), channel_id=1, source_target_pairs={{0,16},{2,18},{4,20},{6,22},{8,24},{10,26},{12,28},{14,30},{16,0},... | collective-permute-start | bytes 98312 | tf_op jit(solution)/shard_map/ppermute | solution.py:590
  5.8 5.0 %collective-permute-start = (f32[64,128]{1,0:T(8,128)}, f32[64,128]{1,0:T(8,128)S(1)}, u32[]{:S(2)}, u32[]{:S(2)}) collective-permute-start(f32[64,128]{1,0:T(8,128)} %bitcast.4), channel_id=1, source_target_pairs={{0,8},{2,10},{4,12},{6,14},{8,0},{10,2},{12,4},{14,6},{16,24},{18,... | collective-permute-start | bytes 98312 | tf_op jit(solution)/shard_map/ppermute | solution.py:590
  7.8 6.5 %copy-start.1 = (f32[1,6,8,128,128]{4,3,2,1,0:T(8,128)S(1)}, f32[1,6,8,128,128]{4,3,2,1,0:T(8,128)}, u32[]{:S(2)}) copy-start(f32[1,6,8,128,128]{4,3,2,1,0:T(8,128)} %given.3) | copy-start | bytes 9437188
  7.8 8.4 %collective-permute-start.3 = (f32[2,2,128,128]{3,2,1,0:T(8,128)S(1)}, f32[2,2,128,128]{3,2,1,0:T(8,128)S(1)}, u32[]{:S(2)}, u32[]{:S(2)}) collective-permute-start(f32[2,2,128,128]{3,2,1,0:T(8,128)S(1)} %get-tuple-element.91), channel_id=1, source_target_pairs={{0,1},{1,0},{2,3},{3,2},{4,5},{5,4},{6,7},{7,6},{8,9},{9,8},{10,11... | collective-permute-start | bytes 786440 | tf_op jit(solution)/shard_map/ppermute | solution.py:590
  10.8 5.0 %collective-permute-start.4 = (f32[4,64,128]{2,1,0:T(8,128)S(1)}, f32[4,64,128]{2,1,0:T(8,128)S(1)}, u32[]{:S(2)}, u32[]{:S(2)}) collective-permute-start(f32[4,64,128]{2,1,0:T(8,128)S(1)} %shard_map.96.near.refs_8_), channel_id=1, source_target_pairs={{0,4},{2,6},{4,0},{6,2},{8,12},{10,14},{12,8},{14,10},{16,20},{18,... | collective-permute-start | bytes 393224 | tf_op jit(solution)/shard_map/ppermute | solution.py:590
  13.0 3.2 %collective-permute-start.5 = (f32[4,64,128]{2,1,0:T(8,128)S(1)}, f32[4,64,128]{2,1,0:T(8,128)S(1)}, u32[]{:S(2)}, u32[]{:S(2)}) collective-permute-start(f32[4,64,128]{2,1,0:T(8,128)S(1)} %shard_map.96.near.refs_8_), channel_id=1, source_target_pairs={{0,2},{2,0},{4,6},{6,4},{8,10},{10,8},{12,14},{14,12},{16,18},{18,... | collective-permute-start | bytes 393224 | tf_op jit(solution)/shard_map/ppermute | solution.py:590
  15.8 1.4 %collective-permute-start.6 = (f32[4,64,128]{2,1,0:T(8,128)S(1)}, f32[4,64,128]{2,1,0:T(8,128)S(1)}, u32[]{:S(2)}, u32[]{:S(2)}) collective-permute-start(f32[4,64,128]{2,1,0:T(8,128)S(1)} %shard_map.99.refs_9_), channel_id=1, source_target_pairs={{0,2},{2,0},{4,6},{6,4},{8,10},{10,8},{12,14},{14,12},{16,18},{18,... | collective-permute-start | bytes 393224 | tf_op jit(solution)/shard_map/ppermute | solution.py:590
  17.5 6.4 %collective-permute-start.7 = (f32[2,128,128]{2,1,0:T(8,128)S(1)}, f32[2,128,128]{2,1,0:T(8,128)S(1)}, u32[]{:S(2)}, u32[]{:S(2)}) collective-permute-start(f32[2,128,128]{2,1,0:T(8,128)S(1)} %get-tuple-element.112), channel_id=1, source_target_pairs={{0,1},{1,0},{2,3},{3,2},{4,5},{5,4},{6,7},{7,6},{8,9},{9,8},{10,11... | collective-permute-start | bytes 393224 | tf_op jit(solution)/shard_map/ppermute | solution.py:590
  19.2 7.5 %collective-permute-start.8 = (f32[2,128,128]{2,1,0:T(8,128)S(1)}, f32[2,128,128]{2,1,0:T(8,128)S(1)}, u32[]{:S(2)}, u32[]{:S(2)}) collective-permute-start(f32[2,128,128]{2,1,0:T(8,128)S(1)} %get-tuple-element.119), channel_id=1, source_target_pairs={{0,1},{1,0},{2,3},{3,2},{4,5},{5,4},{6,7},{7,6},{8,9},{9,8},{10,11... | collective-permute-start | bytes 393224 | tf_op jit(solution)/shard_map/ppermute | solution.py:590
  24.1 5.6 %collective-permute-start.9 = (f32[2,128,128]{2,1,0:T(8,128)S(1)}, f32[2,128,128]{2,1,0:T(8,128)S(1)}, u32[]{:S(2)}, u32[]{:S(2)}) collective-permute-start(f32[2,128,128]{2,1,0:T(8,128)S(1)} %get-tuple-element.126), channel_id=1, source_target_pairs={{0,1},{1,0},{2,3},{3,2},{4,5},{5,4},{6,7},{7,6},{8,9},{9,8},{10,11... | collective-permute-start | bytes 393224 | tf_op jit(solution)/shard_map/ppermute | solution.py:590
  27.0 6.1 %collective-permute-start.10 = (f32[2,128,128]{2,1,0:T(8,128)S(1)}, f32[2,128,128]{2,1,0:T(8,128)S(1)}, u32[]{:S(2)}, u32[]{:S(2)}) collective-permute-start(f32[2,128,128]{2,1,0:T(8,128)S(1)} %get-tuple-element.133), channel_id=1, source_target_pairs={{0,1},{1,0},{2,3},{3,2},{4,5},{5,4},{6,7},{7,6},{8,9},{9,8},{10,11... | collective-permute-start | bytes 393224 | tf_op jit(solution)/shard_map/ppermute | solution.py:590
  30.0 7.0 %collective-permute-start.11 = (f32[2,128,128]{2,1,0:T(8,128)S(1)}, f32[2,128,128]{2,1,0:T(8,128)S(1)}, u32[]{:S(2)}, u32[]{:S(2)}) collective-permute-start(f32[2,128,128]{2,1,0:T(8,128)S(1)} %get-tuple-element.144), channel_id=1, source_target_pairs={{0,1},{1,0},{2,3},{3,2},{4,5},{5,4},{6,7},{7,6},{8,9},{9,8},{10,11... | collective-permute-start | bytes 393224 | tf_op jit(solution)/shard_map/ppermute | solution.py:590
  33.3 5.1 %collective-permute-start.12 = (f32[2,128,128]{2,1,0:T(8,128)S(1)}, f32[2,128,128]{2,1,0:T(8,128)S(1)}, u32[]{:S(2)}, u32[]{:S(2)}) collective-permute-start(f32[2,128,128]{2,1,0:T(8,128)S(1)} %get-tuple-element.147), channel_id=1, source_target_pairs={{0,1},{1,0},{2,3},{3,2},{4,5},{5,4},{6,7},{7,6},{8,9},{9,8},{10,11... | collective-permute-start | bytes 393224 | tf_op jit(solution)/shard_map/ppermute | solution.py:590
  37.8 1.4 %collective-permute-start.13 = (f32[4,48,128]{2,1,0:T(8,128)S(1)}, f32[4,48,128]{2,1,0:T(8,128)S(1)}, u32[]{:S(2)}, u32[]{:S(2)}) collective-permute-start(f32[4,48,128]{2,1,0:T(8,128)S(1)} %get-tuple-element.153), channel_id=1, source_target_pairs={{0,2},{2,0},{4,6},{6,4},{8,10},{10,8},{12,14},{14,12},{16,18},{18,... | collective-permute-start | bytes 294920 | tf_op jit(solution)/shard_map/ppermute | solution.py:590
  37.9 1.4 %collective-permute-start.14 = (f32[4,48,128]{2,1,0:T(8,128)S(1)}, f32[4,48,128]{2,1,0:T(8,128)S(1)}, u32[]{:S(2)}, u32[]{:S(2)}) collective-permute-start(f32[4,48,128]{2,1,0:T(8,128)S(1)} %get-tuple-element.154), channel_id=1, source_target_pairs={{0,2},{2,0},{4,6},{6,4},{8,10},{10,8},{12,14},{14,12},{16,18},{18,... | collective-permute-start | bytes 294920 | tf_op jit(solution)/shard_map/ppermute | solution.py:590
  38.8 2.1 %collective-permute-start.16 = (f32[8,16,128]{2,1,0:T(8,128)S(1)}, f32[8,16,128]{2,1,0:T(8,128)S(1)}, u32[]{:S(2)}, u32[]{:S(2)}) collective-permute-start(f32[8,16,128]{2,1,0:T(8,128)S(1)} %get-tuple-element.159), channel_id=1, source_target_pairs={{0,2},{2,0},{4,6},{6,4},{8,10},{10,8},{12,14},{14,12},{16,18},{18,... | collective-permute-start | bytes 196616 | tf_op jit(solution)/shard_map/ppermute | solution.py:590
  39.4 5.8 %collective-permute-start.15 = (f32[4,48,128]{2,1,0:T(8,128)S(1)}, f32[4,48,128]{2,1,0:T(8,128)S(1)}, u32[]{:S(2)}, u32[]{:S(2)}) collective-permute-start(f32[4,48,128]{2,1,0:T(8,128)S(1)} %get-tuple-element.158), channel_id=1, source_target_pairs={{0,4},{2,6},{4,0},{6,2},{8,12},{10,14},{12,8},{14,10},{16,20},{18,... | collective-permute-start | bytes 294920 | tf_op jit(solution)/shard_map/ppermute | solution.py:590
  40.9 4.3 %collective-permute-start.17 = (f32[4,16,128]{2,1,0:T(8,128)S(1)}, f32[4,16,128]{2,1,0:T(8,128)S(1)}, u32[]{:S(2)}, u32[]{:S(2)}) collective-permute-start(f32[4,16,128]{2,1,0:T(8,128)S(1)} %get-tuple-element.161), channel_id=1, source_target_pairs={{0,4},{2,6},{4,0},{6,2},{8,12},{10,14},{12,8},{14,10},{16,20},{18,... | collective-permute-start | bytes 98312 | tf_op jit(solution)/shard_map/ppermute | solution.py:590
  45.2 6.2 %collective-permute-start.18 = (f32[64,128]{1,0:T(8,128)S(1)}, f32[64,128]{1,0:T(8,128)S(1)}, u32[]{:S(2)}, u32[]{:S(2)}) collective-permute-start(f32[64,128]{1,0:T(8,128)S(1)} %get-tuple-element.163), channel_id=1, source_target_pairs={{0,24},{2,26},{4,28},{6,30},{8,16},{10,18},{12,20},{14,22},{16,8},... | collective-permute-start | bytes 98312 | tf_op jit(solution)/shard_map/ppermute | solution.py:590
  47.4 5.1 %collective-permute-start.19 = (f32[64,128]{1,0:T(8,128)S(1)}, f32[64,128]{1,0:T(8,128)S(1)}, u32[]{:S(2)}, u32[]{:S(2)}) collective-permute-start(f32[64,128]{1,0:T(8,128)S(1)} %get-tuple-element.164), channel_id=1, source_target_pairs={{0,16},{2,18},{4,20},{6,22},{8,24},{10,26},{12,28},{14,30},{16,0},... | collective-permute-start | bytes 98312 | tf_op jit(solution)/shard_map/ppermute | solution.py:590
  47.4 5.1 %collective-permute-start.20 = (f32[64,128]{1,0:T(8,128)S(1)}, f32[64,128]{1,0:T(8,128)S(1)}, u32[]{:S(2)}, u32[]{:S(2)}) collective-permute-start(f32[64,128]{1,0:T(8,128)S(1)} %get-tuple-element.165), channel_id=1, source_target_pairs={{0,8},{2,10},{4,12},{6,14},{8,0},{10,2},{12,4},{14,6},{16,24},{18,... | collective-permute-start | bytes 98312 | tf_op jit(solution)/shard_map/ppermute | solution.py:590

commit v16 on v15

--- a/solution.py
+++ b/solution.py
@@ -413,7 +413,8 @@
 def coef_layer(layer, coef, placed, base):
     for first, size in chunks(base.shape[0]):
         here = pl.ds(first, size)
-        coef[layer, here, :] = 0.25 / (base[here, :] + 3.0 * filtered(placed, first, size))
+        smooth = along_columns(along_rows(placed, first, size)) * 0.0625
+        coef[layer, here, :] = 0.25 / (base[here, :] + 3.0 * smooth)
 
 
 def clear_margins(placed):
@@ -458,12 +459,15 @@
     lax.fori_loop(1, coef.shape[0] - 1, body, 0, unroll=2)
 
 
-def filtered(padded, first, size):
+def along_rows(padded, first, size):
     here = padded[pl.ds(PAD + first, size), :]
     before = padded[pl.ds(PAD + first - 1, size), :]
     after = padded[pl.ds(PAD + first + 1, size), :]
-    along = before + 2.0 * here + after
-    return (prev_col(along) + 2.0 * along + next_col(along)) * 0.0625
+    return before + 2.0 * here + after
+
+
+def along_columns(value):
+    return prev_col(value) + 2.0 * value + next_col(value)
 
 
 def tie_kernel(*refs):
@@ -496,7 +500,7 @@
     def body(layer, carry):
         there = wide.at[lax.rem(layer, 2)]
         for first, size in chunks(rows):
-            there[pl.ds(first, size), :] = filtered(total.at[layer], first, size)
+            there[pl.ds(first, size), :] = along_rows(total.at[layer], first, size)
         for block in range(nblock):
             target = pl.ds(pl.multiple_of((layer - 1) * block_rows, block_rows), block_rows)
             blocks[block, target, :] = there[pl.ds(block * block_rows, block_rows), :]
@@ -519,7 +523,7 @@
     for which, layer in enumerate((0, depth - 1)):
         sums[which] = total[layer] + edges[which]
         for first, size in chunks(rows):
-            wide[which, pl.ds(first, size), :] = filtered(sums.at[which], first, size)
+            wide[which, pl.ds(first, size), :] = along_rows(sums.at[which], first, size)
     for which in range(2):
         blocks = [
             wide[which, pl.ds(block * block_rows, block_rows), :] for block in range(nblock)
@@ -559,7 +563,7 @@
     value = refs[0][...]
     for ref in refs[1:-1]:
         value = value + ref[...]
-    refs[-1][...] = value * scale
+    refs[-1][...] = along_columns(value) * (scale * 0.0625)
 
 
 def out_kernel(e, h, finals, halves, sems):

time: 53.4 us -> 53.4 us (level)
  no operation moved by 1% of the time
where the time goes in v16:
time: 53.4 us; the launch traced here: 53.2 us
  starting transfers between devices  24.5 us (46%)
  Pallas kernels  17 us (32%)
  waiting for transfers between devices  10.1 us (19%)
  between operations  1.55 us (3%)
    ppermute x21, starting transfers between devices, swap_over(): lax.ppermute(array, axis, [(i, i ^ mask) for i in range(lax.axis_size(axi...  24.5 us
    pallas_call x30, Pallas kernels, call(): pl.pallas_call(kernel, out_shape=outs, in_specs=specs, out_specs=out_spec...  17 us
    ppermute x21, waiting for transfers between devices, swap_over(): lax.ppermute(array, axis, [(i, i ^ mask) for i in range(lax.axis_size(axi...  10.1 us
  transfers between devices with their start and end apart: 21, of which 10 were waited for; matrix products, arithmetic and copies ran while one was open for 0% of the time, Pallas kernels for 30%

profile of v16, /device:TPU:0, one launch (start us, length us, event | category | flops | bytes accessed | tf_op | source)
XLA Modules:
  0.0 53.2 jit_solution(17122846061728046192)
XLA Ops:
  0.6 5.1 %collective-permute-start.2 = (f32[64,128]{1,0:T(8,128)}, f32[64,128]{1,0:T(8,128)S(1)}, u32[]{:S(2)}, u32[]{:S(2)}) collective-permute-start(f32[64,128]{1,0:T(8,128)} %bitcast.2), channel_id=1, source_target_pairs={{0,24},{2,26},{4,28},{6,30},{8,16},{10,18},{12,20},{14,22},{16,8},... | collective-permute-start | bytes 98312 | tf_op jit(solution)/shard_map/ppermute | solution.py:594
  5.8 0.6 %collective-permute-start = (f32[64,128]{1,0:T(8,128)}, f32[64,128]{1,0:T(8,128)S(1)}, u32[]{:S(2)}, u32[]{:S(2)}) collective-permute-start(f32[64,128]{1,0:T(8,128)} %bitcast.4), channel_id=1, source_target_pairs={{0,8},{2,10},{4,12},{6,14},{8,0},{10,2},{12,4},{14,6},{16,24},{18,... | collective-permute-start | bytes 98312 | tf_op jit(solution)/shard_map/ppermute | solution.py:594
  6.4 1.4 %shard_map.95 = (f32[64,128]{1,0:T(8,128)S(1)}, f32[2,2,128,128]{3,2,1,0:T(8,128)S(1)}) custom-call(f32[1,6,8,128,128]{4,3,2,1,0:T(8,128)} %given.3, f32[1,6,8,128,128]{4,3,2,1,0:T(8,128)} %given.2, f32[64,128]{1,0:T(8,128)} %bitcast.5), custom_call_target="tpu_custom_call" | custom-call | bytes 30000 | tf_op jit(solution)/shard_map/pallas_call | solution.py:36
  7.8 1.4 %collective-permute-start.3 = (f32[2,2,128,128]{3,2,1,0:T(8,128)S(1)}, f32[2,2,128,128]{3,2,1,0:T(8,128)S(1)}, u32[]{:S(2)}, u32[]{:S(2)}) collective-permute-start(f32[2,2,128,128]{3,2,1,0:T(8,128)S(1)} %get-tuple-element.91), channel_id=1, source_target_pairs={{0,1},{1,0},{2,3},{3,2},{4,5},{5,4},{6,7},{7,6},{8,9},{9,8},{10,11... | collective-permute-start | bytes 786440 | tf_op jit(solution)/shard_map/ppermute | solution.py:594
  9.2 1.5 %collective-permute-done.1.refs_2_ = f32[64,128]{1,0:T(8,128)S(1)} collective-permute-done((f32[64,128]{1,0:T(8,128)}, f32[64,128]{1,0:T(8,128)S(1)}, u32[]{:S(2)}, u32[]{:S(2)}) %collective-permute-start.1) | collective-permute-done | bytes 32800 | tf_op jit(solution)/shard_map/ppermute | solution.py:594
  10.8 1.6 %collective-permute-start.4 = (f32[4,64,128]{2,1,0:T(8,128)S(1)}, f32[4,64,128]{2,1,0:T(8,128)S(1)}, u32[]{:S(2)}, u32[]{:S(2)}) collective-permute-start(f32[4,64,128]{2,1,0:T(8,128)S(1)} %shard_map.96.near.refs_8_), channel_id=1, source_target_pairs={{0,4},{2,6},{4,0},{6,2},{8,12},{10,14},{12,8},{14,10},{16,20},{18,... | collective-permute-start | bytes 393224 | tf_op jit(solution)/shard_map/ppermute | solution.py:594
  13.1 1.2 %shard_map.97 = (f32[3,9,144,128]{3,2,1,0:T(8,128)S(1)}, f32[3,9,144,128]{3,2,1,0:T(8,128)S(1)}, f32[3,8,128,128]{3,2,1,0:T(8,128)S(1)}) custom-call(f32[1,6,8,128,128]{4,3,2,1,0:T(8,128)S(1)} %copy-done, f32[4,64,128]{2,1,0:T(8,128)S(1)} %shard_map.96.near.refs_8_), custom_call_target="tpu_custom_call" | custom-call | bytes 120000 | tf_op jit(solution)/shard_map/pallas_call | solution.py:36
  14.3 1.4 %shard_map.98 = (f32[3,9,144,128]{3,2,1,0:T(8,128)S(1)}, f32[3,9,144,128]{3,2,1,0:T(8,128)S(1)}, f32[3,8,128,128]{3,2,1,0:T(8,128)S(1)}, f32[8,144,128]{2,1,0:T(...) custom-call(f32[1,6,8,128,128]{4,3,2,1,0:T(8,128)S(1)} %copy-done.1,, ...), custom_call_target="tpu_custom_call" | custom-call | bytes 150000 | tf_op jit(solution)/shard_map/pallas_call | solution.py:36
  16.2 0.7 %shard_map.100 = (f32[3,9,144,128]{3,2,1,0:T(8,128)S(1)}, f32[3,8,128,128]{3,2,1,0:T(8,128)S(1)}, f32[3,9,144,128]{3,2,1,0:T(8,128)S(1)}, f32[3,8,128,128]{3,2,1,0:T(8,128)S(1)}, f32[16,64,128]{2,1,0:T(8,128)S(1)}) custom-call(f32[3,9,144,128]{3,2,1,0:T(8,128)S(1)} %get-tuple-element.86.refs_, ...), custom_call_target="tpu_custom_call", output_to_operand_aliasing={{0}: (0, {}), {1}: (1, {}), {2}: (2, {}), {3}: (3, {})} | custom-call | bytes 60000 | tf_op jit(solution)/shard_map/pallas_call | solution.py:36
  17.5 1.5 %collective-permute-start.7 = (f32[2,128,128]{2,1,0:T(8,128)S(1)}, f32[2,128,128]{2,1,0:T(8,128)S(1)}, u32[]{:S(2)}, u32[]{:S(2)}) collective-permute-start(f32[2,128,128]{2,1,0:T(8,128)S(1)} %get-tuple-element.112), channel_id=1, source_target_pairs={{0,1},{1,0},{2,3},{3,2},{4,5},{5,4},{6,7},{7,6},{8,9},{9,8},{10,11... | collective-permute-start | bytes 393224 | tf_op jit(solution)/shard_map/ppermute | solution.py:594
  19.8 0.6 %shard_map.104.coef.refs_2_.refs_4_ = f32[8,128,128]{2,1,0:T(8,128)S(1)} custom-call(f32[8,128,128]{2,1,0:T(8,128)S(1)} %shard_map.101.refs_2_.refs_4_.coef_in, f32[4,64,128]{2,1,0:T(8,128)S(1)} %collective-permute-done.6.refs_0_, f32[16,16,128]{2,1,0:T(8,128)S(1)} %get-tuple-element.94.refs_1_.place, ...), custom_call_target="tpu_custom_call", output_to_operand_aliasing={{}: (0, {})} | custom-call | bytes 60000 | tf_op jit(solution)/shard_map/pallas_call | solution.py:36
  20.9 0.9 %shard_map.106 = (f32[3,9,144,128]{3,2,1,0:T(8,128)S(1)}, f32[3,9,144,128]{3,2,1,0:T(8,128)S(1)}) custom-call(f32[3,9,144,128]{3,2,1,0:T(8,128)S(1)} %get-tuple-element.108.refs_0_, f32[3,9,144,128]{3,2,1,0:T(8,128)S(1)} %get-tuple-element.109.refs_1_, ...), custom_call_target="tpu_custom_call", output_to_operand_aliasing={{0}: (0, {}), {1}: (1, {})} | custom-call | bytes 110000 | tf_op jit(solution)/shard_map/pallas_call | solution.py:36
  21.8 2.1 %collective-permute-done.7.refs_5_.refs_6_ = f32[2,128,128]{2,1,0:T(8,128)S(1)} collective-permute-done((f32[2,128,128]{2,1,0:T(8,128)S(1)}, f32[2,128,128]{2,1,0:T(8,128)S(1)}, u32[]{:S(2)}, u32[]{:S(2)}) %collective-permute-start.7) | collective-permute-done | bytes 131104 | tf_op jit(solution)/shard_map/ppermute | solution.py:594
  24.1 1.4 %collective-permute-start.9 = (f32[2,128,128]{2,1,0:T(8,128)S(1)}, f32[2,128,128]{2,1,0:T(8,128)S(1)}, u32[]{:S(2)}, u32[]{:S(2)}) collective-permute-start(f32[2,128,128]{2,1,0:T(8,128)S(1)} %get-tuple-element.126), channel_id=1, source_target_pairs={{0,1},{1,0},{2,3},{3,2},{4,5},{5,4},{6,7},{7,6},{8,9},{9,8},{10,11... | collective-permute-start | bytes 393224 | tf_op jit(solution)/shard_map/ppermute | solution.py:594
  25.5 1.2 %shard_map.108 = (f32[3,9,144,128]{3,2,1,0:T(8,128)S(1)}, f32[3,9,144,128]{3,2,1,0:T(8,128)S(1)}, f32[3,9,144,128]{3,2,1,0:T(8,128)S(1)}, f32[8,144,128]{2,1,0:T(8,128)S(1)}) custom-call(f32[3,9,144,128]{3,2,1,0:T(8,128)S(1)} %get-tuple-element.106.refs_0_, ...), custom_call_target="tpu_custom_call", output_to_operand_aliasing={{0}: (0, {}), {1}: (1, {}), {2}: (2, {}), {3}: (3, {})} | custom-call | bytes 120000 | tf_op jit(solution)/shard_map/pallas_call | solution.py:36
  27.0 1.3 %collective-permute-start.10 = (f32[2,128,128]{2,1,0:T(8,128)S(1)}, f32[2,128,128]{2,1,0:T(8,128)S(1)}, u32[]{:S(2)}, u32[]{:S(2)}) collective-permute-start(f32[2,128,128]{2,1,0:T(8,128)S(1)} %get-tuple-element.133), channel_id=1, source_target_pairs={{0,1},{1,0},{2,3},{3,2},{4,5},{5,4},{6,7},{7,6},{8,9},{9,8},{10,11... | collective-permute-start | bytes 393224 | tf_op jit(solution)/shard_map/ppermute | solution.py:594
  28.2 0.9 %shard_map.110 = (f32[3,9,144,128]{3,2,1,0:T(8,128)S(1)}, f32[3,9,144,128]{3,2,1,0:T(8,128)S(1)}) custom-call(f32[3,9,144,128]{3,2,1,0:T(8,128)S(1)} %get-tuple-element.122.refs_0_, f32[3,9,144,128]{3,2,1,0:T(8,128)S(1)} %get-tuple-element.123.refs_1_, ...), custom_call_target="tpu_custom_call", output_to_operand_aliasing={{0}: (0, {}), {1}: (1, {})} | custom-call | bytes 110000 | tf_op jit(solution)/shard_map/pallas_call | solution.py:36
  30.0 1.3 %collective-permute-start.11 = (f32[2,128,128]{2,1,0:T(8,128)S(1)}, f32[2,128,128]{2,1,0:T(8,128)S(1)}, u32[]{:S(2)}, u32[]{:S(2)}) collective-permute-start(f32[2,128,128]{2,1,0:T(8,128)S(1)} %get-tuple-element.144), channel_id=1, source_target_pairs={{0,1},{1,0},{2,3},{3,2},{4,5},{5,4},{6,7},{7,6},{8,9},{9,8},{10,11... | collective-permute-start | bytes 393224 | tf_op jit(solution)/shard_map/ppermute | solution.py:594
  31.3 1.2 %shard_map.112 = (f32[3,9,144,128]{3,2,1,0:T(8,128)S(1)}, f32[3,9,144,128]{3,2,1,0:T(8,128)S(1)}, f32[3,9,144,128]{3,2,1,0:T(8,128)S(1)}, f32[8,144,128]{2,1,0:T(8,128)S(1)}) custom-call(f32[3,9,144,128]{3,2,1,0:T(8,128)S(1)} %get-tuple-element.120.refs_0_, ...), custom_call_target="tpu_custom_call", output_to_operand_aliasing={{0}: (0, {}), {1}: (1, {}), {2}: (2, {}), {3}: (3, {})} | custom-call | bytes 120000 | tf_op jit(solution)/shard_map/pallas_call | solution.py:36
  32.4 0.6 %collective-permute-done.10.refs_5_.refs_6_ = f32[2,128,128]{2,1,0:T(8,128)S(1)} collective-permute-done((f32[2,128,128]{2,1,0:T(8,128)S(1)}, f32[2,128,128]{2,1,0:T(8,128)S(1)}, u32[]{:S(2)}, u32[]{:S(2)}) %collective-permute-start.10) | collective-permute-done | bytes 131104 | tf_op jit(solution)/shard_map/ppermute | solution.py:594
  33.3 1.5 %collective-permute-start.12 = (f32[2,128,128]{2,1,0:T(8,128)S(1)}, f32[2,128,128]{2,1,0:T(8,128)S(1)}, u32[]{:S(2)}, u32[]{:S(2)}) collective-permute-start(f32[2,128,128]{2,1,0:T(8,128)S(1)} %get-tuple-element.147), channel_id=1, source_target_pairs={{0,1},{1,0},{2,3},{3,2},{4,5},{5,4},{6,7},{7,6},{8,9},{9,8},{10,11... | collective-permute-start | bytes 393224 | tf_op jit(solution)/shard_map/ppermute | solution.py:594
  34.8 0.9 %shard_map.114 = (f32[3,9,144,128]{3,2,1,0:T(8,128)S(1)}, f32[3,9,144,128]{3,2,1,0:T(8,128)S(1)}) custom-call(f32[3,9,144,128]{3,2,1,0:T(8,128)S(1)} %get-tuple-element.136.refs_0_, f32[3,9,144,128]{3,2,1,0:T(8,128)S(1)} %get-tuple-element.137.refs_1_, ...), custom_call_target="tpu_custom_call", output_to_operand_aliasing={{0}: (0, {}), {1}: (1, {})} | custom-call | bytes 110000 | tf_op jit(solution)/shard_map/pallas_call | solution.py:36
  35.8 1.2 %shard_map.115 = (f32[3,9,144,128]{3,2,1,0:T(8,128)S(1)}, f32[3,9,144,128]{3,2,1,0:T(8,128)S(1)}, f32[3,9,144,128]{3,2,1,0:T(8,128)S(1)}, f32[8,144,128]{2,1,0:T(8,128)S(1)}) custom-call(f32[3,9,144,128]{3,2,1,0:T(8,128)S(1)} %get-tuple-element.134.refs_0_, ...), custom_call_target="tpu_custom_call", output_to_operand_aliasing={{0}: (0, {}), {1}: (1, {}), {2}: (2, {}), {3}: (3, {})} | custom-call | bytes 120000 | tf_op jit(solution)/shard_map/pallas_call | solution.py:36
  37.1 0.7 %shard_map.119 = (f32[4,48,128]{2,1,0:T(8,128)S(1)}, f32[4,48,128]{2,1,0:T(8,128)S(1)}, f32[4,48,128]{2,1,0:T(8,128)S(1)}, f32[4,48,128]{2,1,0:T(8,128)S(1)}) custom-call(f32[8,144,128]{2,1,0:T(8,128)S(1)} %get-tuple-element.150.total, f32[3,9,144,128]{3,2,1,0:T(8,128)S(1)} %get-tuple-element.145.refs_2_.after, s32[16]{0:T(128)} %block_ids_far.1), custom_call_target="tpu_custom_call" | custom-call | bytes 80000 | tf_op jit(solution)/shard_map/pallas_call | solution.py:36
  39.4 1.6 %collective-permute-start.15 = (f32[4,48,128]{2,1,0:T(8,128)S(1)}, f32[4,48,128]{2,1,0:T(8,128)S(1)}, u32[]{:S(2)}, u32[]{:S(2)}) collective-permute-start(f32[4,48,128]{2,1,0:T(8,128)S(1)} %get-tuple-element.158), channel_id=1, source_target_pairs={{0,4},{2,6},{4,0},{6,2},{8,12},{10,14},{12,8},{14,10},{16,20},{18,... | collective-permute-start | bytes 294920 | tf_op jit(solution)/shard_map/ppermute | solution.py:594
  40.9 1.0 %collective-permute-start.17 = (f32[4,16,128]{2,1,0:T(8,128)S(1)}, f32[4,16,128]{2,1,0:T(8,128)S(1)}, u32[]{:S(2)}, u32[]{:S(2)}) collective-permute-start(f32[4,16,128]{2,1,0:T(8,128)S(1)} %get-tuple-element.161), channel_id=1, source_target_pairs={{0,4},{2,6},{4,0},{6,2},{8,12},{10,14},{12,8},{14,10},{16,20},{18,... | collective-permute-start | bytes 98312 | tf_op jit(solution)/shard_map/ppermute | solution.py:594
  41.9 3.3 %collective-permute-done.17.refs_3_ = f32[4,16,128]{2,1,0:T(8,128)S(1)} collective-permute-done((f32[4,16,128]{2,1,0:T(8,128)S(1)}, f32[4,16,128]{2,1,0:T(8,128)S(1)}, u32[]{:S(2)}, u32[]{:S(2)}) %collective-permute-start.17) | collective-permute-done | bytes 32800 | tf_op jit(solution)/shard_map/ppermute | solution.py:594
  45.2 2.1 %collective-permute-start.18 = (f32[64,128]{1,0:T(8,128)S(1)}, f32[64,128]{1,0:T(8,128)S(1)}, u32[]{:S(2)}, u32[]{:S(2)}) collective-permute-start(f32[64,128]{1,0:T(8,128)S(1)} %get-tuple-element.163), channel_id=1, source_target_pairs={{0,24},{2,26},{4,28},{6,30},{8,16},{10,18},{12,20},{14,22},{16,8},... | collective-permute-start | bytes 98312 | tf_op jit(solution)/shard_map/ppermute | solution.py:594
  47.4 2.3 %collective-permute-start.20 = (f32[64,128]{1,0:T(8,128)S(1)}, f32[64,128]{1,0:T(8,128)S(1)}, u32[]{:S(2)}, u32[]{:S(2)}) collective-permute-start(f32[64,128]{1,0:T(8,128)S(1)} %get-tuple-element.165), channel_id=1, source_target_pairs={{0,8},{2,10},{4,12},{6,14},{8,0},{10,2},{12,4},{14,6},{16,24},{18,... | collective-permute-start | bytes 98312 | tf_op jit(solution)/shard_map/ppermute | solution.py:594
  49.7 1.7 %shard_map.118 = f32[1,6,8,128,128]{4,3,2,1,0:T(8,128)} custom-call(f32[3,9,144,128]{3,2,1,0:T(8,128)S(1)} %get-tuple-element.148.e, f32[3,9,144,128]{3,2,1,0:T(8,128)S(1)} %get-tuple-element.149.h), custom_call_target="tpu_custom_call" | custom-call | bytes 170000 | tf_op jit(solution)/shard_map/pallas_call | solution.py:36
  51.4 1.1 %collective-permute-done.19.refs_2_ = f32[64,128]{1,0:T(8,128)S(1)} collective-permute-done((f32[64,128]{1,0:T(8,128)S(1)}, f32[64,128]{1,0:T(8,128)S(1)}, u32[]{:S(2)}, u32[]{:S(2)}) %collective-permute-start.19) | collective-permute-done | bytes 32800 | tf_op jit(solution)/shard_map/ppermute | solution.py:594
  52.5 0.7 %shard_map.124 = f32[64,128]{1,0:T(8,128)} custom-call(f32[64,128]{1,0:T(8,128)S(1)} %get-tuple-element.162.refs_0_, f32[64,128]{1,0:T(8,128)S(1)} %collective-permute-done.18.refs_1_, f32[64,128]{1,0:T(8,128)S(1)} %collective-permute-done.19.refs_2_, f32[64,128]{1,0:T(8,128)S(1)} %collective-permute-done.20.refs_3_), custom_call_target="tpu_custom_call" | custom-call | bytes 30000 | tf_op jit(solution)/shard_map/pallas_call | solution.py:36
  (44 shorter events, 5.6 us)
Async XLA Ops:
  0.6 12.5 %copy-start = (f32[1,6,8,128,128]{4,3,2,1,0:T(8,128)S(1)}, f32[1,6,8,128,128]{4,3,2,1,0:T(8,128)}, u32[]{:S(2)}) copy-start(f32[1,6,8,128,128]{4,3,2,1,0:T(8,128)} %given.2) | copy-start | bytes 9437188
  0.6 8.6 %collective-permute-start.2 = (f32[64,128]{1,0:T(8,128)}, f32[64,128]{1,0:T(8,128)S(1)}, u32[]{:S(2)}, u32[]{:S(2)}) collective-permute-start(f32[64,128]{1,0:T(8,128)} %bitcast.2), channel_id=1, source_target_pairs={{0,24},{2,26},{4,28},{6,30},{8,16},{10,18},{12,20},{14,22},{16,8},... | collective-permute-start | bytes 98312 | tf_op jit(solution)/shard_map/ppermute | solution.py:594
  5.8 5.0 %collective-permute-start.1 = (f32[64,128]{1,0:T(8,128)}, f32[64,128]{1,0:T(8,128)S(1)}, u32[]{:S(2)}, u32[]{:S(2)}) collective-permute-start(f32[64,128]{1,0:T(8,128)} %bitcast.3), channel_id=1, source_target_pairs={{0,16},{2,18},{4,20},{6,22},{8,24},{10,26},{12,28},{14,30},{16,0},... | collective-permute-start | bytes 98312 | tf_op jit(solution)/shard_map/ppermute | solution.py:594
  5.8 5.0 %collective-permute-start = (f32[64,128]{1,0:T(8,128)}, f32[64,128]{1,0:T(8,128)S(1)}, u32[]{:S(2)}, u32[]{:S(2)}) collective-permute-start(f32[64,128]{1,0:T(8,128)} %bitcast.4), channel_id=1, source_target_pairs={{0,8},{2,10},{4,12},{6,14},{8,0},{10,2},{12,4},{14,6},{16,24},{18,... | collective-permute-start | bytes 98312 | tf_op jit(solution)/shard_map/ppermute | solution.py:594
  7.8 6.5 %copy-start.1 = (f32[1,6,8,128,128]{4,3,2,1,0:T(8,128)S(1)}, f32[1,6,8,128,128]{4,3,2,1,0:T(8,128)}, u32[]{:S(2)}) copy-start(f32[1,6,8,128,128]{4,3,2,1,0:T(8,128)} %given.3) | copy-start | bytes 9437188
  7.8 8.4 %collective-permute-start.3 = (f32[2,2,128,128]{3,2,1,0:T(8,128)S(1)}, f32[2,2,128,128]{3,2,1,0:T(8,128)S(1)}, u32[]{:S(2)}, u32[]{:S(2)}) collective-permute-start(f32[2,2,128,128]{3,2,1,0:T(8,128)S(1)} %get-tuple-element.91), channel_id=1, source_target_pairs={{0,1},{1,0},{2,3},{3,2},{4,5},{5,4},{6,7},{7,6},{8,9},{9,8},{10,11... | collective-permute-start | bytes 786440 | tf_op jit(solution)/shard_map/ppermute | solution.py:594
  10.8 5.0 %collective-permute-start.4 = (f32[4,64,128]{2,1,0:T(8,128)S(1)}, f32[4,64,128]{2,1,0:T(8,128)S(1)}, u32[]{:S(2)}, u32[]{:S(2)}) collective-permute-start(f32[4,64,128]{2,1,0:T(8,128)S(1)} %shard_map.96.near.refs_8_), channel_id=1, source_target_pairs={{0,4},{2,6},{4,0},{6,2},{8,12},{10,14},{12,8},{14,10},{16,20},{18,... | collective-permute-start | bytes 393224 | tf_op jit(solution)/shard_map/ppermute | solution.py:594
  13.0 3.2 %collective-permute-start.5 = (f32[4,64,128]{2,1,0:T(8,128)S(1)}, f32[4,64,128]{2,1,0:T(8,128)S(1)}, u32[]{:S(2)}, u32[]{:S(2)}) collective-permute-start(f32[4,64,128]{2,1,0:T(8,128)S(1)} %shard_map.96.near.refs_8_), channel_id=1, source_target_pairs={{0,2},{2,0},{4,6},{6,4},{8,10},{10,8},{12,14},{14,12},{16,18},{18,... | collective-permute-start | bytes 393224 | tf_op jit(solution)/shard_map/ppermute | solution.py:594
  15.8 1.4 %collective-permute-start.6 = (f32[4,64,128]{2,1,0:T(8,128)S(1)}, f32[4,64,128]{2,1,0:T(8,128)S(1)}, u32[]{:S(2)}, u32[]{:S(2)}) collective-permute-start(f32[4,64,128]{2,1,0:T(8,128)S(1)} %shard_map.99.refs_9_), channel_id=1, source_target_pairs={{0,2},{2,0},{4,6},{6,4},{8,10},{10,8},{12,14},{14,12},{16,18},{18,... | collective-permute-start | bytes 393224 | tf_op jit(solution)/shard_map/ppermute | solution.py:594
  17.5 6.4 %collective-permute-start.7 = (f32[2,128,128]{2,1,0:T(8,128)S(1)}, f32[2,128,128]{2,1,0:T(8,128)S(1)}, u32[]{:S(2)}, u32[]{:S(2)}) collective-permute-start(f32[2,128,128]{2,1,0:T(8,128)S(1)} %get-tuple-element.112), channel_id=1, source_target_pairs={{0,1},{1,0},{2,3},{3,2},{4,5},{5,4},{6,7},{7,6},{8,9},{9,8},{10,11... | collective-permute-start | bytes 393224 | tf_op jit(solution)/shard_map/ppermute | solution.py:594
  19.2 7.5 %collective-permute-start.8 = (f32[2,128,128]{2,1,0:T(8,128)S(1)}, f32[2,128,128]{2,1,0:T(8,128)S(1)}, u32[]{:S(2)}, u32[]{:S(2)}) collective-permute-start(f32[2,128,128]{2,1,0:T(8,128)S(1)} %get-tuple-element.119), channel_id=1, source_target_pairs={{0,1},{1,0},{2,3},{3,2},{4,5},{5,4},{6,7},{7,6},{8,9},{9,8},{10,11... | collective-permute-start | bytes 393224 | tf_op jit(solution)/shard_map/ppermute | solution.py:594
  24.1 5.6 %collective-permute-start.9 = (f32[2,128,128]{2,1,0:T(8,128)S(1)}, f32[2,128,128]{2,1,0:T(8,128)S(1)}, u32[]{:S(2)}, u32[]{:S(2)}) collective-permute-start(f32[2,128,128]{2,1,0:T(8,128)S(1)} %get-tuple-element.126), channel_id=1, source_target_pairs={{0,1},{1,0},{2,3},{3,2},{4,5},{5,4},{6,7},{7,6},{8,9},{9,8},{10,11... | collective-permute-start | bytes 393224 | tf_op jit(solution)/shard_map/ppermute | solution.py:594
  27.0 6.1 %collective-permute-start.10 = (f32[2,128,128]{2,1,0:T(8,128)S(1)}, f32[2,128,128]{2,1,0:T(8,128)S(1)}, u32[]{:S(2)}, u32[]{:S(2)}) collective-permute-start(f32[2,128,128]{2,1,0:T(8,128)S(1)} %get-tuple-element.133), channel_id=1, source_target_pairs={{0,1},{1,0},{2,3},{3,2},{4,5},{5,4},{6,7},{7,6},{8,9},{9,8},{10,11... | collective-permute-start | bytes 393224 | tf_op jit(solution)/shard_map/ppermute | solution.py:594
  30.0 7.0 %collective-permute-start.11 = (f32[2,128,128]{2,1,0:T(8,128)S(1)}, f32[2,128,128]{2,1,0:T(8,128)S(1)}, u32[]{:S(2)}, u32[]{:S(2)}) collective-permute-start(f32[2,128,128]{2,1,0:T(8,128)S(1)} %get-tuple-element.144), channel_id=1, source_target_pairs={{0,1},{1,0},{2,3},{3,2},{4,5},{5,4},{6,7},{7,6},{8,9},{9,8},{10,11... | collective-permute-start | bytes 393224 | tf_op jit(solution)/shard_map/ppermute | solution.py:594
  33.3 5.1 %collective-permute-start.12 = (f32[2,128,128]{2,1,0:T(8,128)S(1)}, f32[2,128,128]{2,1,0:T(8,128)S(1)}, u32[]{:S(2)}, u32[]{:S(2)}) collective-permute-start(f32[2,128,128]{2,1,0:T(8,128)S(1)} %get-tuple-element.147), channel_id=1, source_target_pairs={{0,1},{1,0},{2,3},{3,2},{4,5},{5,4},{6,7},{7,6},{8,9},{9,8},{10,11... | collective-permute-start | bytes 393224 | tf_op jit(solution)/shard_map/ppermute | solution.py:594
  37.8 1.4 %collective-permute-start.13 = (f32[4,48,128]{2,1,0:T(8,128)S(1)}, f32[4,48,128]{2,1,0:T(8,128)S(1)}, u32[]{:S(2)}, u32[]{:S(2)}) collective-permute-start(f32[4,48,128]{2,1,0:T(8,128)S(1)} %get-tuple-element.153), channel_id=1, source_target_pairs={{0,2},{2,0},{4,6},{6,4},{8,10},{10,8},{12,14},{14,12},{16,18},{18,... | collective-permute-start | bytes 294920 | tf_op jit(solution)/shard_map/ppermute | solution.py:594
  37.9 1.4 %collective-permute-start.14 = (f32[4,48,128]{2,1,0:T(8,128)S(1)}, f32[4,48,128]{2,1,0:T(8,128)S(1)}, u32[]{:S(2)}, u32[]{:S(2)}) collective-permute-start(f32[4,48,128]{2,1,0:T(8,128)S(1)} %get-tuple-element.154), channel_id=1, source_target_pairs={{0,2},{2,0},{4,6},{6,4},{8,10},{10,8},{12,14},{14,12},{16,18},{18,... | collective-permute-start | bytes 294920 | tf_op jit(solution)/shard_map/ppermute | solution.py:594
  38.7 2.2 %collective-permute-start.16 = (f32[8,16,128]{2,1,0:T(8,128)S(1)}, f32[8,16,128]{2,1,0:T(8,128)S(1)}, u32[]{:S(2)}, u32[]{:S(2)}) collective-permute-start(f32[8,16,128]{2,1,0:T(8,128)S(1)} %get-tuple-element.159), channel_id=1, source_target_pairs={{0,2},{2,0},{4,6},{6,4},{8,10},{10,8},{12,14},{14,12},{16,18},{18,... | collective-permute-start | bytes 196616 | tf_op jit(solution)/shard_map/ppermute | solution.py:594
  39.4 5.8 %collective-permute-start.15 = (f32[4,48,128]{2,1,0:T(8,128)S(1)}, f32[4,48,128]{2,1,0:T(8,128)S(1)}, u32[]{:S(2)}, u32[]{:S(2)}) collective-permute-start(f32[4,48,128]{2,1,0:T(8,128)S(1)} %get-tuple-element.158), channel_id=1, source_target_pairs={{0,4},{2,6},{4,0},{6,2},{8,12},{10,14},{12,8},{14,10},{16,20},{18,... | collective-permute-start | bytes 294920 | tf_op jit(solution)/shard_map/ppermute | solution.py:594
  40.9 4.2 %collective-permute-start.17 = (f32[4,16,128]{2,1,0:T(8,128)S(1)}, f32[4,16,128]{2,1,0:T(8,128)S(1)}, u32[]{:S(2)}, u32[]{:S(2)}) collective-permute-start(f32[4,16,128]{2,1,0:T(8,128)S(1)} %get-tuple-element.161), channel_id=1, source_target_pairs={{0,4},{2,6},{4,0},{6,2},{8,12},{10,14},{12,8},{14,10},{16,20},{18,... | collective-permute-start | bytes 98312 | tf_op jit(solution)/shard_map/ppermute | solution.py:594
  45.2 6.2 %collective-permute-start.18 = (f32[64,128]{1,0:T(8,128)S(1)}, f32[64,128]{1,0:T(8,128)S(1)}, u32[]{:S(2)}, u32[]{:S(2)}) collective-permute-start(f32[64,128]{1,0:T(8,128)S(1)} %get-tuple-element.163), channel_id=1, source_target_pairs={{0,24},{2,26},{4,28},{6,30},{8,16},{10,18},{12,20},{14,22},{16,8},... | collective-permute-start | bytes 98312 | tf_op jit(solution)/shard_map/ppermute | solution.py:594
  47.3 5.1 %collective-permute-start.19 = (f32[64,128]{1,0:T(8,128)S(1)}, f32[64,128]{1,0:T(8,128)S(1)}, u32[]{:S(2)}, u32[]{:S(2)}) collective-permute-start(f32[64,128]{1,0:T(8,128)S(1)} %get-tuple-element.164), channel_id=1, source_target_pairs={{0,16},{2,18},{4,20},{6,22},{8,24},{10,26},{12,28},{14,30},{16,0},... | collective-permute-start | bytes 98312 | tf_op jit(solution)/shard_map/ppermute | solution.py:594
  47.4 5.1 %collective-permute-start.20 = (f32[64,128]{1,0:T(8,128)S(1)}, f32[64,128]{1,0:T(8,128)S(1)}, u32[]{:S(2)}, u32[]{:S(2)}) collective-permute-start(f32[64,128]{1,0:T(8,128)S(1)} %get-tuple-element.165), channel_id=1, source_target_pairs={{0,8},{2,10},{4,12},{6,14},{8,0},{10,2},{12,4},{14,6},{16,24},{18,... | collective-permute-start | bytes 98312 | tf_op jit(solution)/shard_map/ppermute | solution.py:594

commit v17 on v16

--- a/solution.py
+++ b/solution.py
@@ -487,31 +487,28 @@
         out[slot] = ref[...]
 
 
-def filter_inner_kernel(layout, total, after, block_ids_far, *rest):
-    parts, (blocks, wide, block_ids, sem) = rest[:-4], rest[-4:]
-    fetch = pltpu.make_async_copy(block_ids_far, block_ids, sem)
-    fetch.start()
-    depth = total.shape[0]
-    nblock = blocks.shape[0]
+def filter_inner_kernel(total, after, place, *rest):
+    parts, wide = rest[:-1], rest[-1]
+    nblock = place.shape[0]
     rows = wide.shape[1]
     block_rows = rows // nblock
-    me = lax.axis_index("grp")
+    per = parts[0].shape[0]
 
     def body(layer, carry):
         there = wide.at[lax.rem(layer, 2)]
         for first, size in chunks(rows):
             there[pl.ds(first, size), :] = along_rows(total.at[layer], first, size)
-        for block in range(nblock):
-            target = pl.ds(pl.multiple_of((layer - 1) * block_rows, block_rows), block_rows)
-            blocks[block, target, :] = there[pl.ds(block * block_rows, block_rows), :]
+        blocks = [there[pl.ds(block * block_rows, block_rows), :] for block in range(nblock)]
+        target = pl.ds(pl.multiple_of((layer - 1) * block_rows, block_rows), block_rows)
+        for slot in range(nblock):
+            value = None
+            for block, piece in enumerate(blocks):
+                term = place[slot, pl.ds(block, 1), :] * piece
+                value = term if value is None else value + term
+            parts[slot // per][slot % per, target, :] = value
         return carry
 
-    lax.fori_loop(1, depth - 1, body, 0, unroll=2)
-    fetch.wait()
-    inner = pl.ds(0, (depth - 2) * block_rows)
-    for slot, mask in enumerate(mask for masks in layout for mask in masks):
-        part = parts[slot // parts[0].shape[0]]
-        part[slot % part.shape[0]] = blocks[block_ids[me ^ mask], inner, :]
+    lax.fori_loop(1, total.shape[0] - 1, body, 0, unroll=2)
 
 
 def filter_edge_kernel(layout, total, edges, place, *rest):
@@ -762,16 +759,11 @@
         if not more:
             e_fwd, h_fwd = edge_fwd(e_fwd, h_fwd)
             inner = by_owner(
-                functools.partial(filter_inner_kernel, layout),
+                filter_inner_kernel,
                 depth - 2,
-                [total, e_fwd, block_ids],
-                [IN_VMEM, IN_VMEM, IN_HBM],
-                [
-                    pltpu.VMEM((nblock,) + piece, F32),
-                    pltpu.VMEM((2, width_x, width_y), F32),
-                    pltpu.SMEM(block_ids.shape, jnp.int32),
-                    pltpu.SemaphoreType.DMA,
-                ],
+                [total, e_fwd, place],
+                [IN_VMEM] * 3,
+                [pltpu.VMEM((2, width_x, width_y), F32)],
                 0.8,
                 middle,
             )

time: 53.4 us -> 53.3 us (level)
  transfers between devices with their start and end apart: 21 -> 21, of which waited for: 10 -> 11; matrix products, arithmetic and copies ran while one was open for 0% -> 0% of each run, Pallas kernels for 30% -> 30%
where the time goes in v17:
time: 53.3 us; the launch traced here: 53.1 us
  starting transfers between devices  24.6 us (46%)
  Pallas kernels  16.8 us (32%)
  waiting for transfers between devices  10.2 us (19%)
  between operations  1.56 us (3%)
    ppermute x21, starting transfers between devices, swap_over(): lax.ppermute(array, axis, [(i, i ^ mask) for i in range(lax.axis_size(axi...  24.6 us
    pallas_call x30, Pallas kernels, call(): pl.pallas_call(kernel, out_shape=outs, in_specs=specs, out_specs=out_spec...  16.8 us
    ppermute x21, waiting for transfers between devices, swap_over(): lax.ppermute(array, axis, [(i, i ^ mask) for i in range(lax.axis_size(axi...  10.2 us
  transfers between devices with their start and end apart: 21, of which 11 were waited for; matrix products, arithmetic and copies ran while one was open for 0% of the time, Pallas kernels for 30%

profile of v17, /device:TPU:0, one launch (start us, length us, event | category | flops | bytes accessed | tf_op | source)
XLA Modules:
  0.0 53.1 jit_solution(6099972995492393924)
XLA Ops:
  0.6 5.1 %collective-permute-start.2 = (f32[64,128]{1,0:T(8,128)}, f32[64,128]{1,0:T(8,128)S(1)}, u32[]{:S(2)}, u32[]{:S(2)}) collective-permute-start(f32[64,128]{1,0:T(8,128)} %bitcast.2), channel_id=1, source_target_pairs={{0,24},{2,26},{4,28},{6,30},{8,16},{10,18},{12,20},{14,22},{16,8},... | collective-permute-start | bytes 98312 | tf_op jit(solution)/shard_map/ppermute | solution.py:591
  5.8 0.6 %collective-permute-start = (f32[64,128]{1,0:T(8,128)}, f32[64,128]{1,0:T(8,128)S(1)}, u32[]{:S(2)}, u32[]{:S(2)}) collective-permute-start(f32[64,128]{1,0:T(8,128)} %bitcast.4), channel_id=1, source_target_pairs={{0,8},{2,10},{4,12},{6,14},{8,0},{10,2},{12,4},{14,6},{16,24},{18,... | collective-permute-start | bytes 98312 | tf_op jit(solution)/shard_map/ppermute | solution.py:591
  6.4 1.4 %shard_map.95 = (f32[64,128]{1,0:T(8,128)S(1)}, f32[2,2,128,128]{3,2,1,0:T(8,128)S(1)}) custom-call(f32[1,6,8,128,128]{4,3,2,1,0:T(8,128)} %given.3, f32[1,6,8,128,128]{4,3,2,1,0:T(8,128)} %given.2, f32[64,128]{1,0:T(8,128)} %bitcast.5), custom_call_target="tpu_custom_call" | custom-call | bytes 30000 | tf_op jit(solution)/shard_map/pallas_call | solution.py:36
  7.8 1.4 %collective-permute-start.3 = (f32[2,2,128,128]{3,2,1,0:T(8,128)S(1)}, f32[2,2,128,128]{3,2,1,0:T(8,128)S(1)}, u32[]{:S(2)}, u32[]{:S(2)}) collective-permute-start(f32[2,2,128,128]{3,2,1,0:T(8,128)S(1)} %get-tuple-element.91), channel_id=1, source_target_pairs={{0,1},{1,0},{2,3},{3,2},{4,5},{5,4},{6,7},{7,6},{8,9},{9,8},{10,11... | collective-permute-start | bytes 786440 | tf_op jit(solution)/shard_map/ppermute | solution.py:591
  9.2 1.5 %collective-permute-done.1.refs_2_ = f32[64,128]{1,0:T(8,128)S(1)} collective-permute-done((f32[64,128]{1,0:T(8,128)}, f32[64,128]{1,0:T(8,128)S(1)}, u32[]{:S(2)}, u32[]{:S(2)}) %collective-permute-start.1) | collective-permute-done | bytes 32800 | tf_op jit(solution)/shard_map/ppermute | solution.py:591
  10.8 1.6 %collective-permute-start.4 = (f32[4,64,128]{2,1,0:T(8,128)S(1)}, f32[4,64,128]{2,1,0:T(8,128)S(1)}, u32[]{:S(2)}, u32[]{:S(2)}) collective-permute-start(f32[4,64,128]{2,1,0:T(8,128)S(1)} %shard_map.96.near.refs_8_), channel_id=1, source_target_pairs={{0,4},{2,6},{4,0},{6,2},{8,12},{10,14},{12,8},{14,10},{16,20},{18,... | collective-permute-start | bytes 393224 | tf_op jit(solution)/shard_map/ppermute | solution.py:591
  13.1 1.2 %shard_map.97 = (f32[3,9,144,128]{3,2,1,0:T(8,128)S(1)}, f32[3,9,144,128]{3,2,1,0:T(8,128)S(1)}, f32[3,8,128,128]{3,2,1,0:T(8,128)S(1)}) custom-call(f32[1,6,8,128,128]{4,3,2,1,0:T(8,128)S(1)} %copy-done, f32[4,64,128]{2,1,0:T(8,128)S(1)} %shard_map.96.near.refs_8_), custom_call_target="tpu_custom_call" | custom-call | bytes 120000 | tf_op jit(solution)/shard_map/pallas_call | solution.py:36
  14.3 1.4 %shard_map.98 = (f32[3,9,144,128]{3,2,1,0:T(8,128)S(1)}, f32[3,9,144,128]{3,2,1,0:T(8,128)S(1)}, f32[3,8,128,128]{3,2,1,0:T(8,128)S(1)}, f32[8,144,128]{2,1,0:T(...) custom-call(f32[1,6,8,128,128]{4,3,2,1,0:T(8,128)S(1)} %copy-done.1,, ...), custom_call_target="tpu_custom_call" | custom-call | bytes 150000 | tf_op jit(solution)/shard_map/pallas_call | solution.py:36
  16.2 0.7 %shard_map.100 = (f32[3,9,144,128]{3,2,1,0:T(8,128)S(1)}, f32[3,8,128,128]{3,2,1,0:T(8,128)S(1)}, f32[3,9,144,128]{3,2,1,0:T(8,128)S(1)}, f32[3,8,128,128]{3,2,1,0:T(8,128)S(1)}, f32[16,64,128]{2,1,0:T(8,128)S(1)}) custom-call(f32[3,9,144,128]{3,2,1,0:T(8,128)S(1)} %get-tuple-element.86.refs_, ...), custom_call_target="tpu_custom_call", output_to_operand_aliasing={{0}: (0, {}), {1}: (1, {}), {2}: (2, {}), {3}: (3, {})} | custom-call | bytes 60000 | tf_op jit(solution)/shard_map/pallas_call | solution.py:36
  17.5 1.5 %collective-permute-start.7 = (f32[2,128,128]{2,1,0:T(8,128)S(1)}, f32[2,128,128]{2,1,0:T(8,128)S(1)}, u32[]{:S(2)}, u32[]{:S(2)}) collective-permute-start(f32[2,128,128]{2,1,0:T(8,128)S(1)} %get-tuple-element.112), channel_id=1, source_target_pairs={{0,1},{1,0},{2,3},{3,2},{4,5},{5,4},{6,7},{7,6},{8,9},{9,8},{10,11... | collective-permute-start | bytes 393224 | tf_op jit(solution)/shard_map/ppermute | solution.py:591
  19.8 0.6 %shard_map.104.coef.refs_2_.refs_4_ = f32[8,128,128]{2,1,0:T(8,128)S(1)} custom-call(f32[8,128,128]{2,1,0:T(8,128)S(1)} %shard_map.101.refs_2_.refs_4_.coef_in, f32[4,64,128]{2,1,0:T(8,128)S(1)} %collective-permute-done.6.refs_0_, f32[16,16,128]{2,1,0:T(8,128)S(1)} %get-tuple-element.94.refs_1_.place, ...), custom_call_target="tpu_custom_call", output_to_operand_aliasing={{}: (0, {})} | custom-call | bytes 60000 | tf_op jit(solution)/shard_map/pallas_call | solution.py:36
  20.9 0.9 %shard_map.106 = (f32[3,9,144,128]{3,2,1,0:T(8,128)S(1)}, f32[3,9,144,128]{3,2,1,0:T(8,128)S(1)}) custom-call(f32[3,9,144,128]{3,2,1,0:T(8,128)S(1)} %get-tuple-element.108.refs_0_, f32[3,9,144,128]{3,2,1,0:T(8,128)S(1)} %get-tuple-element.109.refs_1_, ...), custom_call_target="tpu_custom_call", output_to_operand_aliasing={{0}: (0, {}), {1}: (1, {})} | custom-call | bytes 110000 | tf_op jit(solution)/shard_map/pallas_call | solution.py:36
  21.8 2.1 %collective-permute-done.7.refs_5_.refs_6_ = f32[2,128,128]{2,1,0:T(8,128)S(1)} collective-permute-done((f32[2,128,128]{2,1,0:T(8,128)S(1)}, f32[2,128,128]{2,1,0:T(8,128)S(1)}, u32[]{:S(2)}, u32[]{:S(2)}) %collective-permute-start.7) | collective-permute-done | bytes 131104 | tf_op jit(solution)/shard_map/ppermute | solution.py:591
  24.1 1.4 %collective-permute-start.9 = (f32[2,128,128]{2,1,0:T(8,128)S(1)}, f32[2,128,128]{2,1,0:T(8,128)S(1)}, u32[]{:S(2)}, u32[]{:S(2)}) collective-permute-start(f32[2,128,128]{2,1,0:T(8,128)S(1)} %get-tuple-element.126), channel_id=1, source_target_pairs={{0,1},{1,0},{2,3},{3,2},{4,5},{5,4},{6,7},{7,6},{8,9},{9,8},{10,11... | collective-permute-start | bytes 393224 | tf_op jit(solution)/shard_map/ppermute | solution.py:591
  25.5 1.2 %shard_map.108 = (f32[3,9,144,128]{3,2,1,0:T(8,128)S(1)}, f32[3,9,144,128]{3,2,1,0:T(8,128)S(1)}, f32[3,9,144,128]{3,2,1,0:T(8,128)S(1)}, f32[8,144,128]{2,1,0:T(8,128)S(1)}) custom-call(f32[3,9,144,128]{3,2,1,0:T(8,128)S(1)} %get-tuple-element.106.refs_0_, ...), custom_call_target="tpu_custom_call", output_to_operand_aliasing={{0}: (0, {}), {1}: (1, {}), {2}: (2, {}), {3}: (3, {})} | custom-call | bytes 120000 | tf_op jit(solution)/shard_map/pallas_call | solution.py:36
  27.0 1.3 %collective-permute-start.10 = (f32[2,128,128]{2,1,0:T(8,128)S(1)}, f32[2,128,128]{2,1,0:T(8,128)S(1)}, u32[]{:S(2)}, u32[]{:S(2)}) collective-permute-start(f32[2,128,128]{2,1,0:T(8,128)S(1)} %get-tuple-element.133), channel_id=1, source_target_pairs={{0,1},{1,0},{2,3},{3,2},{4,5},{5,4},{6,7},{7,6},{8,9},{9,8},{10,11... | collective-permute-start | bytes 393224 | tf_op jit(solution)/shard_map/ppermute | solution.py:591
  28.2 0.9 %shard_map.110 = (f32[3,9,144,128]{3,2,1,0:T(8,128)S(1)}, f32[3,9,144,128]{3,2,1,0:T(8,128)S(1)}) custom-call(f32[3,9,144,128]{3,2,1,0:T(8,128)S(1)} %get-tuple-element.122.refs_0_, f32[3,9,144,128]{3,2,1,0:T(8,128)S(1)} %get-tuple-element.123.refs_1_, ...), custom_call_target="tpu_custom_call", output_to_operand_aliasing={{0}: (0, {}), {1}: (1, {})} | custom-call | bytes 110000 | tf_op jit(solution)/shard_map/pallas_call | solution.py:36
  29.2 0.6 %collective-permute-done.9.refs_5_.refs_6_ = f32[2,128,128]{2,1,0:T(8,128)S(1)} collective-permute-done((f32[2,128,128]{2,1,0:T(8,128)S(1)}, f32[2,128,128]{2,1,0:T(8,128)S(1)}, u32[]{:S(2)}, u32[]{:S(2)}) %collective-permute-start.9) | collective-permute-done | bytes 131104 | tf_op jit(solution)/shard_map/ppermute | solution.py:591
  30.0 1.3 %collective-permute-start.11 = (f32[2,128,128]{2,1,0:T(8,128)S(1)}, f32[2,128,128]{2,1,0:T(8,128)S(1)}, u32[]{:S(2)}, u32[]{:S(2)}) collective-permute-start(f32[2,128,128]{2,1,0:T(8,128)S(1)} %get-tuple-element.144), channel_id=1, source_target_pairs={{0,1},{1,0},{2,3},{3,2},{4,5},{5,4},{6,7},{7,6},{8,9},{9,8},{10,11... | collective-permute-start | bytes 393224 | tf_op jit(solution)/shard_map/ppermute | solution.py:591
  31.3 1.2 %shard_map.112 = (f32[3,9,144,128]{3,2,1,0:T(8,128)S(1)}, f32[3,9,144,128]{3,2,1,0:T(8,128)S(1)}, f32[3,9,144,128]{3,2,1,0:T(8,128)S(1)}, f32[8,144,128]{2,1,0:T(8,128)S(1)}) custom-call(f32[3,9,144,128]{3,2,1,0:T(8,128)S(1)} %get-tuple-element.120.refs_0_, ...), custom_call_target="tpu_custom_call", output_to_operand_aliasing={{0}: (0, {}), {1}: (1, {}), {2}: (2, {}), {3}: (3, {})} | custom-call | bytes 120000 | tf_op jit(solution)/shard_map/pallas_call | solution.py:36
  32.5 0.6 %collective-permute-done.10.refs_5_.refs_6_ = f32[2,128,128]{2,1,0:T(8,128)S(1)} collective-permute-done((f32[2,128,128]{2,1,0:T(8,128)S(1)}, f32[2,128,128]{2,1,0:T(8,128)S(1)}, u32[]{:S(2)}, u32[]{:S(2)}) %collective-permute-start.10) | collective-permute-done | bytes 131104 | tf_op jit(solution)/shard_map/ppermute | solution.py:591
  33.3 1.5 %collective-permute-start.12 = (f32[2,128,128]{2,1,0:T(8,128)S(1)}, f32[2,128,128]{2,1,0:T(8,128)S(1)}, u32[]{:S(2)}, u32[]{:S(2)}) collective-permute-start(f32[2,128,128]{2,1,0:T(8,128)S(1)} %get-tuple-element.147), channel_id=1, source_target_pairs={{0,1},{1,0},{2,3},{3,2},{4,5},{5,4},{6,7},{7,6},{8,9},{9,8},{10,11... | collective-permute-start | bytes 393224 | tf_op jit(solution)/shard_map/ppermute | solution.py:591
  34.9 0.9 %shard_map.114 = (f32[3,9,144,128]{3,2,1,0:T(8,128)S(1)}, f32[3,9,144,128]{3,2,1,0:T(8,128)S(1)}) custom-call(f32[3,9,144,128]{3,2,1,0:T(8,128)S(1)} %get-tuple-element.136.refs_0_, f32[3,9,144,128]{3,2,1,0:T(8,128)S(1)} %get-tuple-element.137.refs_1_, ...), custom_call_target="tpu_custom_call", output_to_operand_aliasing={{0}: (0, {}), {1}: (1, {})} | custom-call | bytes 110000 | tf_op jit(solution)/shard_map/pallas_call | solution.py:36
  35.8 1.2 %shard_map.115 = (f32[3,9,144,128]{3,2,1,0:T(8,128)S(1)}, f32[3,9,144,128]{3,2,1,0:T(8,128)S(1)}, f32[3,9,144,128]{3,2,1,0:T(8,128)S(1)}, f32[8,144,128]{2,1,0:T(8,128)S(1)}) custom-call(f32[3,9,144,128]{3,2,1,0:T(8,128)S(1)} %get-tuple-element.134.refs_0_, ...), custom_call_target="tpu_custom_call", output_to_operand_aliasing={{0}: (0, {}), {1}: (1, {}), {2}: (2, {}), {3}: (3, {})} | custom-call | bytes 120000 | tf_op jit(solution)/shard_map/pallas_call | solution.py:36
  39.2 1.5 %collective-permute-start.15 = (f32[4,48,128]{2,1,0:T(8,128)S(1)}, f32[4,48,128]{2,1,0:T(8,128)S(1)}, u32[]{:S(2)}, u32[]{:S(2)}) collective-permute-start(f32[4,48,128]{2,1,0:T(8,128)S(1)} %get-tuple-element.158), channel_id=1, source_target_pairs={{0,4},{2,6},{4,0},{6,2},{8,12},{10,14},{12,8},{14,10},{16,20},{18,... | collective-permute-start | bytes 294920 | tf_op jit(solution)/shard_map/ppermute | solution.py:591
  40.8 1.1 %collective-permute-start.17 = (f32[4,16,128]{2,1,0:T(8,128)S(1)}, f32[4,16,128]{2,1,0:T(8,128)S(1)}, u32[]{:S(2)}, u32[]{:S(2)}) collective-permute-start(f32[4,16,128]{2,1,0:T(8,128)S(1)} %get-tuple-element.161), channel_id=1, source_target_pairs={{0,4},{2,6},{4,0},{6,2},{8,12},{10,14},{12,8},{14,10},{16,20},{18,... | collective-permute-start | bytes 98312 | tf_op jit(solution)/shard_map/ppermute | solution.py:591
  41.9 3.1 %collective-permute-done.17.refs_3_ = f32[4,16,128]{2,1,0:T(8,128)S(1)} collective-permute-done((f32[4,16,128]{2,1,0:T(8,128)S(1)}, f32[4,16,128]{2,1,0:T(8,128)S(1)}, u32[]{:S(2)}, u32[]{:S(2)}) %collective-permute-start.17) | collective-permute-done | bytes 32800 | tf_op jit(solution)/shard_map/ppermute | solution.py:591
  45.0 2.3 %collective-permute-start.18 = (f32[64,128]{1,0:T(8,128)S(1)}, f32[64,128]{1,0:T(8,128)S(1)}, u32[]{:S(2)}, u32[]{:S(2)}) collective-permute-start(f32[64,128]{1,0:T(8,128)S(1)} %get-tuple-element.163), channel_id=1, source_target_pairs={{0,24},{2,26},{4,28},{6,30},{8,16},{10,18},{12,20},{14,22},{16,8},... | collective-permute-start | bytes 98312 | tf_op jit(solution)/shard_map/ppermute | solution.py:591
  47.3 2.2 %collective-permute-start.20 = (f32[64,128]{1,0:T(8,128)S(1)}, f32[64,128]{1,0:T(8,128)S(1)}, u32[]{:S(2)}, u32[]{:S(2)}) collective-permute-start(f32[64,128]{1,0:T(8,128)S(1)} %get-tuple-element.165), channel_id=1, source_target_pairs={{0,8},{2,10},{4,12},{6,14},{8,0},{10,2},{12,4},{14,6},{16,24},{18,... | collective-permute-start | bytes 98312 | tf_op jit(solution)/shard_map/ppermute | solution.py:591
  49.5 1.7 %shard_map.118 = f32[1,6,8,128,128]{4,3,2,1,0:T(8,128)} custom-call(f32[3,9,144,128]{3,2,1,0:T(8,128)S(1)} %get-tuple-element.148.e, f32[3,9,144,128]{3,2,1,0:T(8,128)S(1)} %get-tuple-element.149.h), custom_call_target="tpu_custom_call" | custom-call | bytes 170000 | tf_op jit(solution)/shard_map/pallas_call | solution.py:36
  51.2 1.2 %collective-permute-done.19.refs_2_ = f32[64,128]{1,0:T(8,128)S(1)} collective-permute-done((f32[64,128]{1,0:T(8,128)S(1)}, f32[64,128]{1,0:T(8,128)S(1)}, u32[]{:S(2)}, u32[]{:S(2)}) %collective-permute-start.19) | collective-permute-done | bytes 32800 | tf_op jit(solution)/shard_map/ppermute | solution.py:591
  52.4 0.7 %shard_map.124 = f32[64,128]{1,0:T(8,128)} custom-call(f32[64,128]{1,0:T(8,128)S(1)} %get-tuple-element.162.refs_0_, f32[64,128]{1,0:T(8,128)S(1)} %collective-permute-done.18.refs_1_, f32[64,128]{1,0:T(8,128)S(1)} %collective-permute-done.19.refs_2_, f32[64,128]{1,0:T(8,128)S(1)} %collective-permute-done.20.refs_3_), custom_call_target="tpu_custom_call" | custom-call | bytes 30000 | tf_op jit(solution)/shard_map/pallas_call | solution.py:36
  (44 shorter events, 5.6 us)
Async XLA Ops:
  0.6 12.5 %copy-start = (f32[1,6,8,128,128]{4,3,2,1,0:T(8,128)S(1)}, f32[1,6,8,128,128]{4,3,2,1,0:T(8,128)}, u32[]{:S(2)}) copy-start(f32[1,6,8,128,128]{4,3,2,1,0:T(8,128)} %given.2) | copy-start | bytes 9437188
  0.6 8.6 %collective-permute-start.2 = (f32[64,128]{1,0:T(8,128)}, f32[64,128]{1,0:T(8,128)S(1)}, u32[]{:S(2)}, u32[]{:S(2)}) collective-permute-start(f32[64,128]{1,0:T(8,128)} %bitcast.2), channel_id=1, source_target_pairs={{0,24},{2,26},{4,28},{6,30},{8,16},{10,18},{12,20},{14,22},{16,8},... | collective-permute-start | bytes 98312 | tf_op jit(solution)/shard_map/ppermute | solution.py:591
  5.8 5.0 %collective-permute-start.1 = (f32[64,128]{1,0:T(8,128)}, f32[64,128]{1,0:T(8,128)S(1)}, u32[]{:S(2)}, u32[]{:S(2)}) collective-permute-start(f32[64,128]{1,0:T(8,128)} %bitcast.3), channel_id=1, source_target_pairs={{0,16},{2,18},{4,20},{6,22},{8,24},{10,26},{12,28},{14,30},{16,0},... | collective-permute-start | bytes 98312 | tf_op jit(solution)/shard_map/ppermute | solution.py:591
  5.8 5.0 %collective-permute-start = (f32[64,128]{1,0:T(8,128)}, f32[64,128]{1,0:T(8,128)S(1)}, u32[]{:S(2)}, u32[]{:S(2)}) collective-permute-start(f32[64,128]{1,0:T(8,128)} %bitcast.4), channel_id=1, source_target_pairs={{0,8},{2,10},{4,12},{6,14},{8,0},{10,2},{12,4},{14,6},{16,24},{18,... | collective-permute-start | bytes 98312 | tf_op jit(solution)/shard_map/ppermute | solution.py:591
  7.8 6.5 %copy-start.1 = (f32[1,6,8,128,128]{4,3,2,1,0:T(8,128)S(1)}, f32[1,6,8,128,128]{4,3,2,1,0:T(8,128)}, u32[]{:S(2)}) copy-start(f32[1,6,8,128,128]{4,3,2,1,0:T(8,128)} %given.3) | copy-start | bytes 9437188
  7.8 8.4 %collective-permute-start.3 = (f32[2,2,128,128]{3,2,1,0:T(8,128)S(1)}, f32[2,2,128,128]{3,2,1,0:T(8,128)S(1)}, u32[]{:S(2)}, u32[]{:S(2)}) collective-permute-start(f32[2,2,128,128]{3,2,1,0:T(8,128)S(1)} %get-tuple-element.91), channel_id=1, source_target_pairs={{0,1},{1,0},{2,3},{3,2},{4,5},{5,4},{6,7},{7,6},{8,9},{9,8},{10,11... | collective-permute-start | bytes 786440 | tf_op jit(solution)/shard_map/ppermute | solution.py:591
  10.8 5.0 %collective-permute-start.4 = (f32[4,64,128]{2,1,0:T(8,128)S(1)}, f32[4,64,128]{2,1,0:T(8,128)S(1)}, u32[]{:S(2)}, u32[]{:S(2)}) collective-permute-start(f32[4,64,128]{2,1,0:T(8,128)S(1)} %shard_map.96.near.refs_8_), channel_id=1, source_target_pairs={{0,4},{2,6},{4,0},{6,2},{8,12},{10,14},{12,8},{14,10},{16,20},{18,... | collective-permute-start | bytes 393224 | tf_op jit(solution)/shard_map/ppermute | solution.py:591
  13.0 3.2 %collective-permute-start.5 = (f32[4,64,128]{2,1,0:T(8,128)S(1)}, f32[4,64,128]{2,1,0:T(8,128)S(1)}, u32[]{:S(2)}, u32[]{:S(2)}) collective-permute-start(f32[4,64,128]{2,1,0:T(8,128)S(1)} %shard_map.96.near.refs_8_), channel_id=1, source_target_pairs={{0,2},{2,0},{4,6},{6,4},{8,10},{10,8},{12,14},{14,12},{16,18},{18,... | collective-permute-start | bytes 393224 | tf_op jit(solution)/shard_map/ppermute | solution.py:591
  15.8 1.4 %collective-permute-start.6 = (f32[4,64,128]{2,1,0:T(8,128)S(1)}, f32[4,64,128]{2,1,0:T(8,128)S(1)}, u32[]{:S(2)}, u32[]{:S(2)}) collective-permute-start(f32[4,64,128]{2,1,0:T(8,128)S(1)} %shard_map.99.refs_9_), channel_id=1, source_target_pairs={{0,2},{2,0},{4,6},{6,4},{8,10},{10,8},{12,14},{14,12},{16,18},{18,... | collective-permute-start | bytes 393224 | tf_op jit(solution)/shard_map/ppermute | solution.py:591
  17.5 6.4 %collective-permute-start.7 = (f32[2,128,128]{2,1,0:T(8,128)S(1)}, f32[2,128,128]{2,1,0:T(8,128)S(1)}, u32[]{:S(2)}, u32[]{:S(2)}) collective-permute-start(f32[2,128,128]{2,1,0:T(8,128)S(1)} %get-tuple-element.112), channel_id=1, source_target_pairs={{0,1},{1,0},{2,3},{3,2},{4,5},{5,4},{6,7},{7,6},{8,9},{9,8},{10,11... | collective-permute-start | bytes 393224 | tf_op jit(solution)/shard_map/ppermute | solution.py:591
  19.2 7.5 %collective-permute-start.8 = (f32[2,128,128]{2,1,0:T(8,128)S(1)}, f32[2,128,128]{2,1,0:T(8,128)S(1)}, u32[]{:S(2)}, u32[]{:S(2)}) collective-permute-start(f32[2,128,128]{2,1,0:T(8,128)S(1)} %get-tuple-element.119), channel_id=1, source_target_pairs={{0,1},{1,0},{2,3},{3,2},{4,5},{5,4},{6,7},{7,6},{8,9},{9,8},{10,11... | collective-permute-start | bytes 393224 | tf_op jit(solution)/shard_map/ppermute | solution.py:591
  24.1 5.6 %collective-permute-start.9 = (f32[2,128,128]{2,1,0:T(8,128)S(1)}, f32[2,128,128]{2,1,0:T(8,128)S(1)}, u32[]{:S(2)}, u32[]{:S(2)}) collective-permute-start(f32[2,128,128]{2,1,0:T(8,128)S(1)} %get-tuple-element.126), channel_id=1, source_target_pairs={{0,1},{1,0},{2,3},{3,2},{4,5},{5,4},{6,7},{7,6},{8,9},{9,8},{10,11... | collective-permute-start | bytes 393224 | tf_op jit(solution)/shard_map/ppermute | solution.py:591
  27.0 6.1 %collective-permute-start.10 = (f32[2,128,128]{2,1,0:T(8,128)S(1)}, f32[2,128,128]{2,1,0:T(8,128)S(1)}, u32[]{:S(2)}, u32[]{:S(2)}) collective-permute-start(f32[2,128,128]{2,1,0:T(8,128)S(1)} %get-tuple-element.133), channel_id=1, source_target_pairs={{0,1},{1,0},{2,3},{3,2},{4,5},{5,4},{6,7},{7,6},{8,9},{9,8},{10,11... | collective-permute-start | bytes 393224 | tf_op jit(solution)/shard_map/ppermute | solution.py:591
  30.0 7.0 %collective-permute-start.11 = (f32[2,128,128]{2,1,0:T(8,128)S(1)}, f32[2,128,128]{2,1,0:T(8,128)S(1)}, u32[]{:S(2)}, u32[]{:S(2)}) collective-permute-start(f32[2,128,128]{2,1,0:T(8,128)S(1)} %get-tuple-element.144), channel_id=1, source_target_pairs={{0,1},{1,0},{2,3},{3,2},{4,5},{5,4},{6,7},{7,6},{8,9},{9,8},{10,11... | collective-permute-start | bytes 393224 | tf_op jit(solution)/shard_map/ppermute | solution.py:591
  33.3 5.0 %collective-permute-start.12 = (f32[2,128,128]{2,1,0:T(8,128)S(1)}, f32[2,128,128]{2,1,0:T(8,128)S(1)}, u32[]{:S(2)}, u32[]{:S(2)}) collective-permute-start(f32[2,128,128]{2,1,0:T(8,128)S(1)} %get-tuple-element.147), channel_id=1, source_target_pairs={{0,1},{1,0},{2,3},{3,2},{4,5},{5,4},{6,7},{7,6},{8,9},{9,8},{10,11... | collective-permute-start | bytes 393224 | tf_op jit(solution)/shard_map/ppermute | solution.py:591
  37.7 1.4 %collective-permute-start.13 = (f32[4,48,128]{2,1,0:T(8,128)S(1)}, f32[4,48,128]{2,1,0:T(8,128)S(1)}, u32[]{:S(2)}, u32[]{:S(2)}) collective-permute-start(f32[4,48,128]{2,1,0:T(8,128)S(1)} %get-tuple-element.153), channel_id=1, source_target_pairs={{0,2},{2,0},{4,6},{6,4},{8,10},{10,8},{12,14},{14,12},{16,18},{18,... | collective-permute-start | bytes 294920 | tf_op jit(solution)/shard_map/ppermute | solution.py:591
  37.7 1.4 %collective-permute-start.14 = (f32[4,48,128]{2,1,0:T(8,128)S(1)}, f32[4,48,128]{2,1,0:T(8,128)S(1)}, u32[]{:S(2)}, u32[]{:S(2)}) collective-permute-start(f32[4,48,128]{2,1,0:T(8,128)S(1)} %get-tuple-element.154), channel_id=1, source_target_pairs={{0,2},{2,0},{4,6},{6,4},{8,10},{10,8},{12,14},{14,12},{16,18},{18,... | collective-permute-start | bytes 294920 | tf_op jit(solution)/shard_map/ppermute | solution.py:591
  38.7 2.1 %collective-permute-start.16 = (f32[8,16,128]{2,1,0:T(8,128)S(1)}, f32[8,16,128]{2,1,0:T(8,128)S(1)}, u32[]{:S(2)}, u32[]{:S(2)}) collective-permute-start(f32[8,16,128]{2,1,0:T(8,128)S(1)} %get-tuple-element.159), channel_id=1, source_target_pairs={{0,2},{2,0},{4,6},{6,4},{8,10},{10,8},{12,14},{14,12},{16,18},{18,... | collective-permute-start | bytes 196616 | tf_op jit(solution)/shard_map/ppermute | solution.py:591
  39.2 5.8 %collective-permute-start.15 = (f32[4,48,128]{2,1,0:T(8,128)S(1)}, f32[4,48,128]{2,1,0:T(8,128)S(1)}, u32[]{:S(2)}, u32[]{:S(2)}) collective-permute-start(f32[4,48,128]{2,1,0:T(8,128)S(1)} %get-tuple-element.158), channel_id=1, source_target_pairs={{0,4},{2,6},{4,0},{6,2},{8,12},{10,14},{12,8},{14,10},{16,20},{18,... | collective-permute-start | bytes 294920 | tf_op jit(solution)/shard_map/ppermute | solution.py:591
  40.8 4.3 %collective-permute-start.17 = (f32[4,16,128]{2,1,0:T(8,128)S(1)}, f32[4,16,128]{2,1,0:T(8,128)S(1)}, u32[]{:S(2)}, u32[]{:S(2)}) collective-permute-start(f32[4,16,128]{2,1,0:T(8,128)S(1)} %get-tuple-element.161), channel_id=1, source_target_pairs={{0,4},{2,6},{4,0},{6,2},{8,12},{10,14},{12,8},{14,10},{16,20},{18,... | collective-permute-start | bytes 98312 | tf_op jit(solution)/shard_map/ppermute | solution.py:591
  45.0 6.2 %collective-permute-start.18 = (f32[64,128]{1,0:T(8,128)S(1)}, f32[64,128]{1,0:T(8,128)S(1)}, u32[]{:S(2)}, u32[]{:S(2)}) collective-permute-start(f32[64,128]{1,0:T(8,128)S(1)} %get-tuple-element.163), channel_id=1, source_target_pairs={{0,24},{2,26},{4,28},{6,30},{8,16},{10,18},{12,20},{14,22},{16,8},... | collective-permute-start | bytes 98312 | tf_op jit(solution)/shard_map/ppermute | solution.py:591
  47.3 5.1 %collective-permute-start.19 = (f32[64,128]{1,0:T(8,128)S(1)}, f32[64,128]{1,0:T(8,128)S(1)}, u32[]{:S(2)}, u32[]{:S(2)}) collective-permute-start(f32[64,128]{1,0:T(8,128)S(1)} %get-tuple-element.164), channel_id=1, source_target_pairs={{0,16},{2,18},{4,20},{6,22},{8,24},{10,26},{12,28},{14,30},{16,0},... | collective-permute-start | bytes 98312 | tf_op jit(solution)/shard_map/ppermute | solution.py:591
  47.3 5.1 %collective-permute-start.20 = (f32[64,128]{1,0:T(8,128)S(1)}, f32[64,128]{1,0:T(8,128)S(1)}, u32[]{:S(2)}, u32[]{:S(2)}) collective-permute-start(f32[64,128]{1,0:T(8,128)S(1)} %get-tuple-element.165), channel_id=1, source_target_pairs={{0,8},{2,10},{4,12},{6,14},{8,0},{10,2},{12,4},{14,6},{16,24},{18,... | collective-permute-start | bytes 98312 | tf_op jit(solution)/shard_map/ppermute | solution.py:591

commit v18 on v15

--- a/solution.py
+++ b/solution.py
@@ -655,7 +655,9 @@
         ]
 
     design = density.reshape(piece)
-    got = [swap_over(design, "grp", mask) for mask in far_masks[1:]]
+    order = [2, 3, 1] if far == 4 else list(range(1, far))
+    trips = {slot: swap_over(design, "grp", far_masks[slot]) for slot in reversed(order)}
+    got = [trips[slot] for slot in range(1, far)]
     own, *pays = call(
         opening_kernel,
         [on_chip(*piece)] + [on_chip(2, 2, width_x, width_y)] * npay,
@@ -833,7 +835,7 @@
         inner + ends,
         [IN_VMEM] * (2 * middle),
     )
-    got = [swap_over(part, "grp", mask) for part, mask in zip(pieces[:0:-1], far_masks[:0:-1])]
+    got = [swap_over(pieces[slot], "grp", far_masks[slot]) for slot in order]
     scale = 3.0 / (STEPS * math.sqrt(ngrp))
     grad = call(
         functools.partial(last_kernel, scale),

time: 53.4 us -> 53.8 us (level)
  waiting for transfers between devices: 9.99 us -> 11.4 us
  starting transfers between devices: 24.6 us -> 23.7 us
    ppermute x21, waiting for transfers between devices: 9.99 us -> 11.4 us  [swap_over(): lax.ppermute(array, axis, [(i, i ^ mask) for i in range(lax.axis_size(axi...]
    ppermute x21, starting transfers between devices: 24.6 us -> 23.7 us  [swap_over(): lax.ppermute(array, axis, [(i, i ^ mask) for i in range(lax.axis_size(axi...]
where the time goes in v18:
time: 53.8 us; the launch traced here: 53.6 us
  starting transfers between devices  23.7 us (44%)
  Pallas kernels  17 us (32%)
  waiting for transfers between devices  11.4 us (21%)
  between operations  1.56 us (3%)
    ppermute x21, starting transfers between devices, swap_over(): lax.ppermute(array, axis, [(i, i ^ mask) for i in range(lax.axis_size(axi...  23.7 us
    pallas_call x30, Pallas kernels, call(): pl.pallas_call(kernel, out_shape=outs, in_specs=specs, out_specs=out_spec...  17 us
    ppermute x21, waiting for transfers between devices, swap_over(): lax.ppermute(array, axis, [(i, i ^ mask) for i in range(lax.axis_size(axi...  11.4 us
  transfers between devices with their start and end apart: 21, of which 10 were waited for; matrix products, arithmetic and copies ran while one was open for 0% of the time, Pallas kernels for 30%

profile of v18, /device:TPU:0, one launch (start us, length us, event | category | flops | bytes accessed | tf_op | source)
XLA Modules:
  0.0 53.6 jit_solution(13933345324897252542)
XLA Ops:
  0.6 5.1 %collective-permute-start.2 = (f32[64,128]{1,0:T(8,128)}, f32[64,128]{1,0:T(8,128)S(1)}, u32[]{:S(2)}, u32[]{:S(2)}) collective-permute-start(f32[64,128]{1,0:T(8,128)} %bitcast.2), channel_id=1, source_target_pairs={{0,24},{2,26},{4,28},{6,30},{8,16},{10,18},{12,20},{14,22},{16,8},... | collective-permute-start | bytes 98312 | tf_op jit(solution)/shard_map/ppermute | solution.py:590
  5.8 0.6 %collective-permute-start = (f32[64,128]{1,0:T(8,128)}, f32[64,128]{1,0:T(8,128)S(1)}, u32[]{:S(2)}, u32[]{:S(2)}) collective-permute-start(f32[64,128]{1,0:T(8,128)} %bitcast.4), channel_id=1, source_target_pairs={{0,8},{2,10},{4,12},{6,14},{8,0},{10,2},{12,4},{14,6},{16,24},{18,... | collective-permute-start | bytes 98312 | tf_op jit(solution)/shard_map/ppermute | solution.py:590
  6.4 1.4 %shard_map.95 = (f32[64,128]{1,0:T(8,128)S(1)}, f32[2,2,128,128]{3,2,1,0:T(8,128)S(1)}) custom-call(f32[1,6,8,128,128]{4,3,2,1,0:T(8,128)} %given.3, f32[1,6,8,128,128]{4,3,2,1,0:T(8,128)} %given.2, f32[64,128]{1,0:T(8,128)} %bitcast.5), custom_call_target="tpu_custom_call" | custom-call | bytes 30000 | tf_op jit(solution)/shard_map/pallas_call | solution.py:36
  7.8 1.4 %collective-permute-start.3 = (f32[2,2,128,128]{3,2,1,0:T(8,128)S(1)}, f32[2,2,128,128]{3,2,1,0:T(8,128)S(1)}, u32[]{:S(2)}, u32[]{:S(2)}) collective-permute-start(f32[2,2,128,128]{3,2,1,0:T(8,128)S(1)} %get-tuple-element.91), channel_id=1, source_target_pairs={{0,1},{1,0},{2,3},{3,2},{4,5},{5,4},{6,7},{7,6},{8,9},{9,8},{10,11... | collective-permute-start | bytes 786440 | tf_op jit(solution)/shard_map/ppermute | solution.py:590
  9.2 1.5 %collective-permute-done.1.refs_2_ = f32[64,128]{1,0:T(8,128)S(1)} collective-permute-done((f32[64,128]{1,0:T(8,128)}, f32[64,128]{1,0:T(8,128)S(1)}, u32[]{:S(2)}, u32[]{:S(2)}) %collective-permute-start.1) | collective-permute-done | bytes 32800 | tf_op jit(solution)/shard_map/ppermute | solution.py:590
  10.8 1.6 %collective-permute-start.4 = (f32[4,64,128]{2,1,0:T(8,128)S(1)}, f32[4,64,128]{2,1,0:T(8,128)S(1)}, u32[]{:S(2)}, u32[]{:S(2)}) collective-permute-start(f32[4,64,128]{2,1,0:T(8,128)S(1)} %shard_map.96.near.refs_8_), channel_id=1, source_target_pairs={{0,4},{2,6},{4,0},{6,2},{8,12},{10,14},{12,8},{14,10},{16,20},{18,... | collective-permute-start | bytes 393224 | tf_op jit(solution)/shard_map/ppermute | solution.py:590
  13.1 1.2 %shard_map.97 = (f32[3,9,144,128]{3,2,1,0:T(8,128)S(1)}, f32[3,9,144,128]{3,2,1,0:T(8,128)S(1)}, f32[3,8,128,128]{3,2,1,0:T(8,128)S(1)}) custom-call(f32[1,6,8,128,128]{4,3,2,1,0:T(8,128)S(1)} %copy-done, f32[4,64,128]{2,1,0:T(8,128)S(1)} %shard_map.96.near.refs_8_), custom_call_target="tpu_custom_call" | custom-call | bytes 120000 | tf_op jit(solution)/shard_map/pallas_call | solution.py:36
  14.3 1.4 %shard_map.98 = (f32[3,9,144,128]{3,2,1,0:T(8,128)S(1)}, f32[3,9,144,128]{3,2,1,0:T(8,128)S(1)}, f32[3,8,128,128]{3,2,1,0:T(8,128)S(1)}, f32[8,144,128]{2,1,0:T(...) custom-call(f32[1,6,8,128,128]{4,3,2,1,0:T(8,128)S(1)} %copy-done.1,, ...), custom_call_target="tpu_custom_call" | custom-call | bytes 150000 | tf_op jit(solution)/shard_map/pallas_call | solution.py:36
  16.2 0.7 %shard_map.100 = (f32[3,9,144,128]{3,2,1,0:T(8,128)S(1)}, f32[3,8,128,128]{3,2,1,0:T(8,128)S(1)}, f32[3,9,144,128]{3,2,1,0:T(8,128)S(1)}, f32[3,8,128,128]{3,2,1,0:T(8,128)S(1)}, f32[16,64,128]{2,1,0:T(8,128)S(1)}) custom-call(f32[3,9,144,128]{3,2,1,0:T(8,128)S(1)} %get-tuple-element.86.refs_, ...), custom_call_target="tpu_custom_call", output_to_operand_aliasing={{0}: (0, {}), {1}: (1, {}), {2}: (2, {}), {3}: (3, {})} | custom-call | bytes 60000 | tf_op jit(solution)/shard_map/pallas_call | solution.py:36
  17.5 1.5 %collective-permute-start.7 = (f32[2,128,128]{2,1,0:T(8,128)S(1)}, f32[2,128,128]{2,1,0:T(8,128)S(1)}, u32[]{:S(2)}, u32[]{:S(2)}) collective-permute-start(f32[2,128,128]{2,1,0:T(8,128)S(1)} %get-tuple-element.112), channel_id=1, source_target_pairs={{0,1},{1,0},{2,3},{3,2},{4,5},{5,4},{6,7},{7,6},{8,9},{9,8},{10,11... | collective-permute-start | bytes 393224 | tf_op jit(solution)/shard_map/ppermute | solution.py:590
  19.8 0.6 %shard_map.104.coef.refs_2_.refs_4_ = f32[8,128,128]{2,1,0:T(8,128)S(1)} custom-call(f32[8,128,128]{2,1,0:T(8,128)S(1)} %shard_map.101.refs_2_.refs_4_.coef_in, f32[4,64,128]{2,1,0:T(8,128)S(1)} %collective-permute-done.6.refs_0_, f32[16,16,128]{2,1,0:T(8,128)S(1)} %get-tuple-element.94.refs_1_.place, ...), custom_call_target="tpu_custom_call", output_to_operand_aliasing={{}: (0, {})} | custom-call | bytes 60000 | tf_op jit(solution)/shard_map/pallas_call | solution.py:36
  20.9 0.9 %shard_map.106 = (f32[3,9,144,128]{3,2,1,0:T(8,128)S(1)}, f32[3,9,144,128]{3,2,1,0:T(8,128)S(1)}) custom-call(f32[3,9,144,128]{3,2,1,0:T(8,128)S(1)} %get-tuple-element.108.refs_0_, f32[3,9,144,128]{3,2,1,0:T(8,128)S(1)} %get-tuple-element.109.refs_1_, ...), custom_call_target="tpu_custom_call", output_to_operand_aliasing={{0}: (0, {}), {1}: (1, {})} | custom-call | bytes 110000 | tf_op jit(solution)/shard_map/pallas_call | solution.py:36
  21.8 2.1 %collective-permute-done.7.refs_5_.refs_6_ = f32[2,128,128]{2,1,0:T(8,128)S(1)} collective-permute-done((f32[2,128,128]{2,1,0:T(8,128)S(1)}, f32[2,128,128]{2,1,0:T(8,128)S(1)}, u32[]{:S(2)}, u32[]{:S(2)}) %collective-permute-start.7) | collective-permute-done | bytes 131104 | tf_op jit(solution)/shard_map/ppermute | solution.py:590
  24.1 1.4 %collective-permute-start.9 = (f32[2,128,128]{2,1,0:T(8,128)S(1)}, f32[2,128,128]{2,1,0:T(8,128)S(1)}, u32[]{:S(2)}, u32[]{:S(2)}) collective-permute-start(f32[2,128,128]{2,1,0:T(8,128)S(1)} %get-tuple-element.126), channel_id=1, source_target_pairs={{0,1},{1,0},{2,3},{3,2},{4,5},{5,4},{6,7},{7,6},{8,9},{9,8},{10,11... | collective-permute-start | bytes 393224 | tf_op jit(solution)/shard_map/ppermute | solution.py:590
  25.5 1.2 %shard_map.108 = (f32[3,9,144,128]{3,2,1,0:T(8,128)S(1)}, f32[3,9,144,128]{3,2,1,0:T(8,128)S(1)}, f32[3,9,144,128]{3,2,1,0:T(8,128)S(1)}, f32[8,144,128]{2,1,0:T(8,128)S(1)}) custom-call(f32[3,9,144,128]{3,2,1,0:T(8,128)S(1)} %get-tuple-element.106.refs_0_, ...), custom_call_target="tpu_custom_call", output_to_operand_aliasing={{0}: (0, {}), {1}: (1, {}), {2}: (2, {}), {3}: (3, {})} | custom-call | bytes 120000 | tf_op jit(solution)/shard_map/pallas_call | solution.py:36
  27.0 1.3 %collective-permute-start.10 = (f32[2,128,128]{2,1,0:T(8,128)S(1)}, f32[2,128,128]{2,1,0:T(8,128)S(1)}, u32[]{:S(2)}, u32[]{:S(2)}) collective-permute-start(f32[2,128,128]{2,1,0:T(8,128)S(1)} %get-tuple-element.133), channel_id=1, source_target_pairs={{0,1},{1,0},{2,3},{3,2},{4,5},{5,4},{6,7},{7,6},{8,9},{9,8},{10,11... | collective-permute-start | bytes 393224 | tf_op jit(solution)/shard_map/ppermute | solution.py:590
  28.2 0.9 %shard_map.110 = (f32[3,9,144,128]{3,2,1,0:T(8,128)S(1)}, f32[3,9,144,128]{3,2,1,0:T(8,128)S(1)}) custom-call(f32[3,9,144,128]{3,2,1,0:T(8,128)S(1)} %get-tuple-element.122.refs_0_, f32[3,9,144,128]{3,2,1,0:T(8,128)S(1)} %get-tuple-element.123.refs_1_, ...), custom_call_target="tpu_custom_call", output_to_operand_aliasing={{0}: (0, {}), {1}: (1, {})} | custom-call | bytes 110000 | tf_op jit(solution)/shard_map/pallas_call | solution.py:36
  30.0 1.3 %collective-permute-start.11 = (f32[2,128,128]{2,1,0:T(8,128)S(1)}, f32[2,128,128]{2,1,0:T(8,128)S(1)}, u32[]{:S(2)}, u32[]{:S(2)}) collective-permute-start(f32[2,128,128]{2,1,0:T(8,128)S(1)} %get-tuple-element.144), channel_id=1, source_target_pairs={{0,1},{1,0},{2,3},{3,2},{4,5},{5,4},{6,7},{7,6},{8,9},{9,8},{10,11... | collective-permute-start | bytes 393224 | tf_op jit(solution)/shard_map/ppermute | solution.py:590
  31.3 1.2 %shard_map.112 = (f32[3,9,144,128]{3,2,1,0:T(8,128)S(1)}, f32[3,9,144,128]{3,2,1,0:T(8,128)S(1)}, f32[3,9,144,128]{3,2,1,0:T(8,128)S(1)}, f32[8,144,128]{2,1,0:T(8,128)S(1)}) custom-call(f32[3,9,144,128]{3,2,1,0:T(8,128)S(1)} %get-tuple-element.120.refs_0_, ...), custom_call_target="tpu_custom_call", output_to_operand_aliasing={{0}: (0, {}), {1}: (1, {}), {2}: (2, {}), {3}: (3, {})} | custom-call | bytes 120000 | tf_op jit(solution)/shard_map/pallas_call | solution.py:36
  32.4 0.6 %collective-permute-done.10.refs_5_.refs_6_ = f32[2,128,128]{2,1,0:T(8,128)S(1)} collective-permute-done((f32[2,128,128]{2,1,0:T(8,128)S(1)}, f32[2,128,128]{2,1,0:T(8,128)S(1)}, u32[]{:S(2)}, u32[]{:S(2)}) %collective-permute-start.10) | collective-permute-done | bytes 131104 | tf_op jit(solution)/shard_map/ppermute | solution.py:590
  33.3 1.5 %collective-permute-start.12 = (f32[2,128,128]{2,1,0:T(8,128)S(1)}, f32[2,128,128]{2,1,0:T(8,128)S(1)}, u32[]{:S(2)}, u32[]{:S(2)}) collective-permute-start(f32[2,128,128]{2,1,0:T(8,128)S(1)} %get-tuple-element.147), channel_id=1, source_target_pairs={{0,1},{1,0},{2,3},{3,2},{4,5},{5,4},{6,7},{7,6},{8,9},{9,8},{10,11... | collective-permute-start | bytes 393224 | tf_op jit(solution)/shard_map/ppermute | solution.py:590
  34.8 0.9 %shard_map.114 = (f32[3,9,144,128]{3,2,1,0:T(8,128)S(1)}, f32[3,9,144,128]{3,2,1,0:T(8,128)S(1)}) custom-call(f32[3,9,144,128]{3,2,1,0:T(8,128)S(1)} %get-tuple-element.136.refs_0_, f32[3,9,144,128]{3,2,1,0:T(8,128)S(1)} %get-tuple-element.137.refs_1_, ...), custom_call_target="tpu_custom_call", output_to_operand_aliasing={{0}: (0, {}), {1}: (1, {})} | custom-call | bytes 110000 | tf_op jit(solution)/shard_map/pallas_call | solution.py:36
  35.8 1.2 %shard_map.115 = (f32[3,9,144,128]{3,2,1,0:T(8,128)S(1)}, f32[3,9,144,128]{3,2,1,0:T(8,128)S(1)}, f32[3,9,144,128]{3,2,1,0:T(8,128)S(1)}, f32[8,144,128]{2,1,0:T(8,128)S(1)}) custom-call(f32[3,9,144,128]{3,2,1,0:T(8,128)S(1)} %get-tuple-element.134.refs_0_, ...), custom_call_target="tpu_custom_call", output_to_operand_aliasing={{0}: (0, {}), {1}: (1, {}), {2}: (2, {}), {3}: (3, {})} | custom-call | bytes 120000 | tf_op jit(solution)/shard_map/pallas_call | solution.py:36
  37.1 0.7 %shard_map.119 = (f32[4,48,128]{2,1,0:T(8,128)S(1)}, f32[4,48,128]{2,1,0:T(8,128)S(1)}, f32[4,48,128]{2,1,0:T(8,128)S(1)}, f32[4,48,128]{2,1,0:T(8,128)S(1)}) custom-call(f32[8,144,128]{2,1,0:T(8,128)S(1)} %get-tuple-element.150.total, f32[3,9,144,128]{3,2,1,0:T(8,128)S(1)} %get-tuple-element.145.refs_2_.after, s32[16]{0:T(128)} %block_ids_far.1), custom_call_target="tpu_custom_call" | custom-call | bytes 80000 | tf_op jit(solution)/shard_map/pallas_call | solution.py:36
  39.4 1.5 %collective-permute-start.15 = (f32[4,48,128]{2,1,0:T(8,128)S(1)}, f32[4,48,128]{2,1,0:T(8,128)S(1)}, u32[]{:S(2)}, u32[]{:S(2)}) collective-permute-start(f32[4,48,128]{2,1,0:T(8,128)S(1)} %get-tuple-element.158), channel_id=1, source_target_pairs={{0,4},{2,6},{4,0},{6,2},{8,12},{10,14},{12,8},{14,10},{16,20},{18,... | collective-permute-start | bytes 294920 | tf_op jit(solution)/shard_map/ppermute | solution.py:590
  40.9 1.1 %collective-permute-start.17 = (f32[4,16,128]{2,1,0:T(8,128)S(1)}, f32[4,16,128]{2,1,0:T(8,128)S(1)}, u32[]{:S(2)}, u32[]{:S(2)}) collective-permute-start(f32[4,16,128]{2,1,0:T(8,128)S(1)} %get-tuple-element.161), channel_id=1, source_target_pairs={{0,4},{2,6},{4,0},{6,2},{8,12},{10,14},{12,8},{14,10},{16,20},{18,... | collective-permute-start | bytes 98312 | tf_op jit(solution)/shard_map/ppermute | solution.py:590
  42.0 3.2 %collective-permute-done.17.refs_3_ = f32[4,16,128]{2,1,0:T(8,128)S(1)} collective-permute-done((f32[4,16,128]{2,1,0:T(8,128)S(1)}, f32[4,16,128]{2,1,0:T(8,128)S(1)}, u32[]{:S(2)}, u32[]{:S(2)}) %collective-permute-start.17) | collective-permute-done | bytes 32800 | tf_op jit(solution)/shard_map/ppermute | solution.py:590
  45.2 2.1 %collective-permute-start.18 = (f32[64,128]{1,0:T(8,128)S(1)}, f32[64,128]{1,0:T(8,128)S(1)}, u32[]{:S(2)}, u32[]{:S(2)}) collective-permute-start(f32[64,128]{1,0:T(8,128)S(1)} %get-tuple-element.163), channel_id=1, source_target_pairs={{0,16},{2,18},{4,20},{6,22},{8,24},{10,26},{12,28},{14,30},{16,0},... | collective-permute-start | bytes 98312 | tf_op jit(solution)/shard_map/ppermute | solution.py:590
  47.8 1.0 %collective-permute-start.20 = (f32[64,128]{1,0:T(8,128)S(1)}, f32[64,128]{1,0:T(8,128)S(1)}, u32[]{:S(2)}, u32[]{:S(2)}) collective-permute-start(f32[64,128]{1,0:T(8,128)S(1)} %get-tuple-element.165), channel_id=1, source_target_pairs={{0,8},{2,10},{4,12},{6,14},{8,0},{10,2},{12,4},{14,6},{16,24},{18,... | collective-permute-start | bytes 98312 | tf_op jit(solution)/shard_map/ppermute | solution.py:590
  48.8 1.7 %shard_map.118 = f32[1,6,8,128,128]{4,3,2,1,0:T(8,128)} custom-call(f32[3,9,144,128]{3,2,1,0:T(8,128)S(1)} %get-tuple-element.148.e, f32[3,9,144,128]{3,2,1,0:T(8,128)S(1)} %get-tuple-element.149.h), custom_call_target="tpu_custom_call" | custom-call | bytes 170000 | tf_op jit(solution)/shard_map/pallas_call | solution.py:36
  50.5 2.5 %collective-permute-done.19.refs_2_ = f32[64,128]{1,0:T(8,128)S(1)} collective-permute-done((f32[64,128]{1,0:T(8,128)S(1)}, f32[64,128]{1,0:T(8,128)S(1)}, u32[]{:S(2)}, u32[]{:S(2)}) %collective-permute-start.19) | collective-permute-done | bytes 32800 | tf_op jit(solution)/shard_map/ppermute | solution.py:590
  53.0 0.6 %shard_map.124 = f32[64,128]{1,0:T(8,128)} custom-call(f32[64,128]{1,0:T(8,128)S(1)} %get-tuple-element.162.refs_0_, f32[64,128]{1,0:T(8,128)S(1)} %collective-permute-done.18.refs_1_, f32[64,128]{1,0:T(8,128)S(1)} %collective-permute-done.19.refs_2_, f32[64,128]{1,0:T(8,128)S(1)} %collective-permute-done.20.refs_3_), custom_call_target="tpu_custom_call" | custom-call | bytes 30000 | tf_op jit(solution)/shard_map/pallas_call | solution.py:36
  (44 shorter events, 6.1 us)
Async XLA Ops:
  0.6 12.5 %copy-start = (f32[1,6,8,128,128]{4,3,2,1,0:T(8,128)S(1)}, f32[1,6,8,128,128]{4,3,2,1,0:T(8,128)}, u32[]{:S(2)}) copy-start(f32[1,6,8,128,128]{4,3,2,1,0:T(8,128)} %given.2) | copy-start | bytes 9437188
  0.6 8.6 %collective-permute-start.2 = (f32[64,128]{1,0:T(8,128)}, f32[64,128]{1,0:T(8,128)S(1)}, u32[]{:S(2)}, u32[]{:S(2)}) collective-permute-start(f32[64,128]{1,0:T(8,128)} %bitcast.2), channel_id=1, source_target_pairs={{0,24},{2,26},{4,28},{6,30},{8,16},{10,18},{12,20},{14,22},{16,8},... | collective-permute-start | bytes 98312 | tf_op jit(solution)/shard_map/ppermute | solution.py:590
  5.8 5.0 %collective-permute-start.1 = (f32[64,128]{1,0:T(8,128)}, f32[64,128]{1,0:T(8,128)S(1)}, u32[]{:S(2)}, u32[]{:S(2)}) collective-permute-start(f32[64,128]{1,0:T(8,128)} %bitcast.3), channel_id=1, source_target_pairs={{0,16},{2,18},{4,20},{6,22},{8,24},{10,26},{12,28},{14,30},{16,0},... | collective-permute-start | bytes 98312 | tf_op jit(solution)/shard_map/ppermute | solution.py:590
  5.8 5.0 %collective-permute-start = (f32[64,128]{1,0:T(8,128)}, f32[64,128]{1,0:T(8,128)S(1)}, u32[]{:S(2)}, u32[]{:S(2)}) collective-permute-start(f32[64,128]{1,0:T(8,128)} %bitcast.4), channel_id=1, source_target_pairs={{0,8},{2,10},{4,12},{6,14},{8,0},{10,2},{12,4},{14,6},{16,24},{18,... | collective-permute-start | bytes 98312 | tf_op jit(solution)/shard_map/ppermute | solution.py:590
  7.8 6.5 %copy-start.1 = (f32[1,6,8,128,128]{4,3,2,1,0:T(8,128)S(1)}, f32[1,6,8,128,128]{4,3,2,1,0:T(8,128)}, u32[]{:S(2)}) copy-start(f32[1,6,8,128,128]{4,3,2,1,0:T(8,128)} %given.3) | copy-start | bytes 9437188
  7.8 8.4 %collective-permute-start.3 = (f32[2,2,128,128]{3,2,1,0:T(8,128)S(1)}, f32[2,2,128,128]{3,2,1,0:T(8,128)S(1)}, u32[]{:S(2)}, u32[]{:S(2)}) collective-permute-start(f32[2,2,128,128]{3,2,1,0:T(8,128)S(1)} %get-tuple-element.91), channel_id=1, source_target_pairs={{0,1},{1,0},{2,3},{3,2},{4,5},{5,4},{6,7},{7,6},{8,9},{9,8},{10,11... | collective-permute-start | bytes 786440 | tf_op jit(solution)/shard_map/ppermute | solution.py:590
  10.8 5.0 %collective-permute-start.4 = (f32[4,64,128]{2,1,0:T(8,128)S(1)}, f32[4,64,128]{2,1,0:T(8,128)S(1)}, u32[]{:S(2)}, u32[]{:S(2)}) collective-permute-start(f32[4,64,128]{2,1,0:T(8,128)S(1)} %shard_map.96.near.refs_8_), channel_id=1, source_target_pairs={{0,4},{2,6},{4,0},{6,2},{8,12},{10,14},{12,8},{14,10},{16,20},{18,... | collective-permute-start | bytes 393224 | tf_op jit(solution)/shard_map/ppermute | solution.py:590
  13.0 3.2 %collective-permute-start.5 = (f32[4,64,128]{2,1,0:T(8,128)S(1)}, f32[4,64,128]{2,1,0:T(8,128)S(1)}, u32[]{:S(2)}, u32[]{:S(2)}) collective-permute-start(f32[4,64,128]{2,1,0:T(8,128)S(1)} %shard_map.96.near.refs_8_), channel_id=1, source_target_pairs={{0,2},{2,0},{4,6},{6,4},{8,10},{10,8},{12,14},{14,12},{16,18},{18,... | collective-permute-start | bytes 393224 | tf_op jit(solution)/shard_map/ppermute | solution.py:590
  15.8 1.4 %collective-permute-start.6 = (f32[4,64,128]{2,1,0:T(8,128)S(1)}, f32[4,64,128]{2,1,0:T(8,128)S(1)}, u32[]{:S(2)}, u32[]{:S(2)}) collective-permute-start(f32[4,64,128]{2,1,0:T(8,128)S(1)} %shard_map.99.refs_9_), channel_id=1, source_target_pairs={{0,2},{2,0},{4,6},{6,4},{8,10},{10,8},{12,14},{14,12},{16,18},{18,... | collective-permute-start | bytes 393224 | tf_op jit(solution)/shard_map/ppermute | solution.py:590
  17.5 6.4 %collective-permute-start.7 = (f32[2,128,128]{2,1,0:T(8,128)S(1)}, f32[2,128,128]{2,1,0:T(8,128)S(1)}, u32[]{:S(2)}, u32[]{:S(2)}) collective-permute-start(f32[2,128,128]{2,1,0:T(8,128)S(1)} %get-tuple-element.112), channel_id=1, source_target_pairs={{0,1},{1,0},{2,3},{3,2},{4,5},{5,4},{6,7},{7,6},{8,9},{9,8},{10,11... | collective-permute-start | bytes 393224 | tf_op jit(solution)/shard_map/ppermute | solution.py:590
  19.2 7.5 %collective-permute-start.8 = (f32[2,128,128]{2,1,0:T(8,128)S(1)}, f32[2,128,128]{2,1,0:T(8,128)S(1)}, u32[]{:S(2)}, u32[]{:S(2)}) collective-permute-start(f32[2,128,128]{2,1,0:T(8,128)S(1)} %get-tuple-element.119), channel_id=1, source_target_pairs={{0,1},{1,0},{2,3},{3,2},{4,5},{5,4},{6,7},{7,6},{8,9},{9,8},{10,11... | collective-permute-start | bytes 393224 | tf_op jit(solution)/shard_map/ppermute | solution.py:590
  24.1 5.6 %collective-permute-start.9 = (f32[2,128,128]{2,1,0:T(8,128)S(1)}, f32[2,128,128]{2,1,0:T(8,128)S(1)}, u32[]{:S(2)}, u32[]{:S(2)}) collective-permute-start(f32[2,128,128]{2,1,0:T(8,128)S(1)} %get-tuple-element.126), channel_id=1, source_target_pairs={{0,1},{1,0},{2,3},{3,2},{4,5},{5,4},{6,7},{7,6},{8,9},{9,8},{10,11... | collective-permute-start | bytes 393224 | tf_op jit(solution)/shard_map/ppermute | solution.py:590
  27.0 6.1 %collective-permute-start.10 = (f32[2,128,128]{2,1,0:T(8,128)S(1)}, f32[2,128,128]{2,1,0:T(8,128)S(1)}, u32[]{:S(2)}, u32[]{:S(2)}) collective-permute-start(f32[2,128,128]{2,1,0:T(8,128)S(1)} %get-tuple-element.133), channel_id=1, source_target_pairs={{0,1},{1,0},{2,3},{3,2},{4,5},{5,4},{6,7},{7,6},{8,9},{9,8},{10,11... | collective-permute-start | bytes 393224 | tf_op jit(solution)/shard_map/ppermute | solution.py:590
  30.0 7.0 %collective-permute-start.11 = (f32[2,128,128]{2,1,0:T(8,128)S(1)}, f32[2,128,128]{2,1,0:T(8,128)S(1)}, u32[]{:S(2)}, u32[]{:S(2)}) collective-permute-start(f32[2,128,128]{2,1,0:T(8,128)S(1)} %get-tuple-element.144), channel_id=1, source_target_pairs={{0,1},{1,0},{2,3},{3,2},{4,5},{5,4},{6,7},{7,6},{8,9},{9,8},{10,11... | collective-permute-start | bytes 393224 | tf_op jit(solution)/shard_map/ppermute | solution.py:590
  33.3 5.1 %collective-permute-start.12 = (f32[2,128,128]{2,1,0:T(8,128)S(1)}, f32[2,128,128]{2,1,0:T(8,128)S(1)}, u32[]{:S(2)}, u32[]{:S(2)}) collective-permute-start(f32[2,128,128]{2,1,0:T(8,128)S(1)} %get-tuple-element.147), channel_id=1, source_target_pairs={{0,1},{1,0},{2,3},{3,2},{4,5},{5,4},{6,7},{7,6},{8,9},{9,8},{10,11... | collective-permute-start | bytes 393224 | tf_op jit(solution)/shard_map/ppermute | solution.py:590
  37.8 1.4 %collective-permute-start.13 = (f32[4,48,128]{2,1,0:T(8,128)S(1)}, f32[4,48,128]{2,1,0:T(8,128)S(1)}, u32[]{:S(2)}, u32[]{:S(2)}) collective-permute-start(f32[4,48,128]{2,1,0:T(8,128)S(1)} %get-tuple-element.153), channel_id=1, source_target_pairs={{0,2},{2,0},{4,6},{6,4},{8,10},{10,8},{12,14},{14,12},{16,18},{18,... | collective-permute-start | bytes 294920 | tf_op jit(solution)/shard_map/ppermute | solution.py:590
  37.9 1.4 %collective-permute-start.14 = (f32[4,48,128]{2,1,0:T(8,128)S(1)}, f32[4,48,128]{2,1,0:T(8,128)S(1)}, u32[]{:S(2)}, u32[]{:S(2)}) collective-permute-start(f32[4,48,128]{2,1,0:T(8,128)S(1)} %get-tuple-element.154), channel_id=1, source_target_pairs={{0,2},{2,0},{4,6},{6,4},{8,10},{10,8},{12,14},{14,12},{16,18},{18,... | collective-permute-start | bytes 294920 | tf_op jit(solution)/shard_map/ppermute | solution.py:590
  38.8 2.1 %collective-permute-start.16 = (f32[8,16,128]{2,1,0:T(8,128)S(1)}, f32[8,16,128]{2,1,0:T(8,128)S(1)}, u32[]{:S(2)}, u32[]{:S(2)}) collective-permute-start(f32[8,16,128]{2,1,0:T(8,128)S(1)} %get-tuple-element.159), channel_id=1, source_target_pairs={{0,2},{2,0},{4,6},{6,4},{8,10},{10,8},{12,14},{14,12},{16,18},{18,... | collective-permute-start | bytes 196616 | tf_op jit(solution)/shard_map/ppermute | solution.py:590
  39.4 5.8 %collective-permute-start.15 = (f32[4,48,128]{2,1,0:T(8,128)S(1)}, f32[4,48,128]{2,1,0:T(8,128)S(1)}, u32[]{:S(2)}, u32[]{:S(2)}) collective-permute-start(f32[4,48,128]{2,1,0:T(8,128)S(1)} %get-tuple-element.158), channel_id=1, source_target_pairs={{0,4},{2,6},{4,0},{6,2},{8,12},{10,14},{12,8},{14,10},{16,20},{18,... | collective-permute-start | bytes 294920 | tf_op jit(solution)/shard_map/ppermute | solution.py:590
  40.9 4.3 %collective-permute-start.17 = (f32[4,16,128]{2,1,0:T(8,128)S(1)}, f32[4,16,128]{2,1,0:T(8,128)S(1)}, u32[]{:S(2)}, u32[]{:S(2)}) collective-permute-start(f32[4,16,128]{2,1,0:T(8,128)S(1)} %get-tuple-element.161), channel_id=1, source_target_pairs={{0,4},{2,6},{4,0},{6,2},{8,12},{10,14},{12,8},{14,10},{16,20},{18,... | collective-permute-start | bytes 98312 | tf_op jit(solution)/shard_map/ppermute | solution.py:590
  45.2 5.3 %collective-permute-start.18 = (f32[64,128]{1,0:T(8,128)S(1)}, f32[64,128]{1,0:T(8,128)S(1)}, u32[]{:S(2)}, u32[]{:S(2)}) collective-permute-start(f32[64,128]{1,0:T(8,128)S(1)} %get-tuple-element.163), channel_id=1, source_target_pairs={{0,16},{2,18},{4,20},{6,22},{8,24},{10,26},{12,28},{14,30},{16,0},... | collective-permute-start | bytes 98312 | tf_op jit(solution)/shard_map/ppermute | solution.py:590
  47.3 5.7 %collective-permute-start.19 = (f32[64,128]{1,0:T(8,128)S(1)}, f32[64,128]{1,0:T(8,128)S(1)}, u32[]{:S(2)}, u32[]{:S(2)}) collective-permute-start(f32[64,128]{1,0:T(8,128)S(1)} %get-tuple-element.164), channel_id=1, source_target_pairs={{0,24},{2,26},{4,28},{6,30},{8,16},{10,18},{12,20},{14,22},{16,8},... | collective-permute-start | bytes 98312 | tf_op jit(solution)/shard_map/ppermute | solution.py:590
  47.8 5.2 %collective-permute-start.20 = (f32[64,128]{1,0:T(8,128)S(1)}, f32[64,128]{1,0:T(8,128)S(1)}, u32[]{:S(2)}, u32[]{:S(2)}) collective-permute-start(f32[64,128]{1,0:T(8,128)S(1)} %get-tuple-element.165), channel_id=1, source_target_pairs={{0,8},{2,10},{4,12},{6,14},{8,0},{10,2},{12,4},{14,6},{16,24},{18,... | collective-permute-start | bytes 98312 | tf_op jit(solution)/shard_map/ppermute | solution.py:590

commit v19 on v15

--- a/solution.py
+++ b/solution.py
@@ -85,7 +85,7 @@
         for c, value in enumerate(values):
             ref[c, layer, pl.ds(PAD + first, size), :] = value
 
-    def put_h(self, layer, given=None, alone=False):
+    def put_h(self, layer, given=None, alone=False, pay=None):
         for first, size in chunks(self.rows):
             rows = pl.ds(PAD + first, size)
             after = pl.ds(PAD + first + 1, size)
@@ -105,6 +105,9 @@
             hy = hy - (rise_x - (ez_after - ez))
             hz = hz - ((ey_after - ey) - (next_col(ex) - ex))
             self.write(self.h, layer, first, size, (hx, hy, hz))
+            if pay is not None:
+                pay[0, pl.ds(first, size), :] = hx
+                pay[1, pl.ds(first, size), :] = hy
 
     def curl_h(self, layer, lower, first, size):
         rows = pl.ds(PAD + first, size)
@@ -349,9 +352,7 @@
             win.take_above(above)
         win.put_e(top, top - 1, curls, other, edges, 1)
         if pays:
-            win.put_h(top, alone=True)
-            for c in range(2):
-                pays[0][c] = h[c, top, pl.ds(PAD, win.rows), :]
+            win.put_h(top, alone=True, pay=pays[0])
 
     @pl.when(has_low)
     def _():

time: 53.4 us -> 53.3 us (level)
  no operation moved by 1% of the time
where the time goes in v19:
time: 53.3 us; the launch traced here: 53.1 us
  starting transfers between devices  24.6 us (46%)
  Pallas kernels  16.9 us (32%)
  waiting for transfers between devices  10 us (19%)
  between operations  1.56 us (3%)
    ppermute x21, starting transfers between devices, swap_over(): lax.ppermute(array, axis, [(i, i ^ mask) for i in range(lax.axis_size(axi...  24.6 us
    pallas_call x30, Pallas kernels, call(): pl.pallas_call(kernel, out_shape=outs, in_specs=specs, out_specs=out_spec...  16.9 us
    ppermute x21, waiting for transfers between devices, swap_over(): lax.ppermute(array, axis, [(i, i ^ mask) for i in range(lax.axis_size(axi...  10 us
  transfers between devices with their start and end apart: 21, of which 10 were waited for; matrix products, arithmetic and copies ran while one was open for 0% of the time, Pallas kernels for 30%

profile of v19, /device:TPU:0, one launch (start us, length us, event | category | flops | bytes accessed | tf_op | source)
XLA Modules:
  0.0 53.1 jit_solution(13176906146883757746)
XLA Ops:
  0.6 5.1 %collective-permute-start.2 = (f32[64,128]{1,0:T(8,128)}, f32[64,128]{1,0:T(8,128)S(1)}, u32[]{:S(2)}, u32[]{:S(2)}) collective-permute-start(f32[64,128]{1,0:T(8,128)} %bitcast.2), channel_id=1, source_target_pairs={{0,24},{2,26},{4,28},{6,30},{8,16},{10,18},{12,20},{14,22},{16,8},... | collective-permute-start | bytes 98312 | tf_op jit(solution)/shard_map/ppermute | solution.py:591
  5.8 0.6 %collective-permute-start = (f32[64,128]{1,0:T(8,128)}, f32[64,128]{1,0:T(8,128)S(1)}, u32[]{:S(2)}, u32[]{:S(2)}) collective-permute-start(f32[64,128]{1,0:T(8,128)} %bitcast.4), channel_id=1, source_target_pairs={{0,8},{2,10},{4,12},{6,14},{8,0},{10,2},{12,4},{14,6},{16,24},{18,... | collective-permute-start | bytes 98312 | tf_op jit(solution)/shard_map/ppermute | solution.py:591
  6.4 1.4 %shard_map.95 = (f32[64,128]{1,0:T(8,128)S(1)}, f32[2,2,128,128]{3,2,1,0:T(8,128)S(1)}) custom-call(f32[1,6,8,128,128]{4,3,2,1,0:T(8,128)} %given.3, f32[1,6,8,128,128]{4,3,2,1,0:T(8,128)} %given.2, f32[64,128]{1,0:T(8,128)} %bitcast.5), custom_call_target="tpu_custom_call" | custom-call | bytes 30000 | tf_op jit(solution)/shard_map/pallas_call | solution.py:36
  7.8 1.4 %collective-permute-start.3 = (f32[2,2,128,128]{3,2,1,0:T(8,128)S(1)}, f32[2,2,128,128]{3,2,1,0:T(8,128)S(1)}, u32[]{:S(2)}, u32[]{:S(2)}) collective-permute-start(f32[2,2,128,128]{3,2,1,0:T(8,128)S(1)} %get-tuple-element.91), channel_id=1, source_target_pairs={{0,1},{1,0},{2,3},{3,2},{4,5},{5,4},{6,7},{7,6},{8,9},{9,8},{10,11... | collective-permute-start | bytes 786440 | tf_op jit(solution)/shard_map/ppermute | solution.py:591
  9.2 1.5 %collective-permute-done.1.refs_2_ = f32[64,128]{1,0:T(8,128)S(1)} collective-permute-done((f32[64,128]{1,0:T(8,128)}, f32[64,128]{1,0:T(8,128)S(1)}, u32[]{:S(2)}, u32[]{:S(2)}) %collective-permute-start.1) | collective-permute-done | bytes 32800 | tf_op jit(solution)/shard_map/ppermute | solution.py:591
  10.8 1.6 %collective-permute-start.4 = (f32[4,64,128]{2,1,0:T(8,128)S(1)}, f32[4,64,128]{2,1,0:T(8,128)S(1)}, u32[]{:S(2)}, u32[]{:S(2)}) collective-permute-start(f32[4,64,128]{2,1,0:T(8,128)S(1)} %shard_map.96.near.refs_8_), channel_id=1, source_target_pairs={{0,4},{2,6},{4,0},{6,2},{8,12},{10,14},{12,8},{14,10},{16,20},{18,... | collective-permute-start | bytes 393224 | tf_op jit(solution)/shard_map/ppermute | solution.py:591
  13.1 1.2 %shard_map.97 = (f32[3,9,144,128]{3,2,1,0:T(8,128)S(1)}, f32[3,9,144,128]{3,2,1,0:T(8,128)S(1)}, f32[3,8,128,128]{3,2,1,0:T(8,128)S(1)}) custom-call(f32[1,6,8,128,128]{4,3,2,1,0:T(8,128)S(1)} %copy-done, f32[4,64,128]{2,1,0:T(8,128)S(1)} %shard_map.96.near.refs_8_), custom_call_target="tpu_custom_call" | custom-call | bytes 120000 | tf_op jit(solution)/shard_map/pallas_call | solution.py:36
  14.3 1.4 %shard_map.98 = (f32[3,9,144,128]{3,2,1,0:T(8,128)S(1)}, f32[3,9,144,128]{3,2,1,0:T(8,128)S(1)}, f32[3,8,128,128]{3,2,1,0:T(8,128)S(1)}, f32[8,144,128]{2,1,0:T(...) custom-call(f32[1,6,8,128,128]{4,3,2,1,0:T(8,128)S(1)} %copy-done.1,, ...), custom_call_target="tpu_custom_call" | custom-call | bytes 150000 | tf_op jit(solution)/shard_map/pallas_call | solution.py:36
  16.2 0.7 %shard_map.100 = (f32[3,9,144,128]{3,2,1,0:T(8,128)S(1)}, f32[3,8,128,128]{3,2,1,0:T(8,128)S(1)}, f32[3,9,144,128]{3,2,1,0:T(8,128)S(1)}, f32[3,8,128,128]{3,2,1,0:T(8,128)S(1)}, f32[16,64,128]{2,1,0:T(8,128)S(1)}) custom-call(f32[3,9,144,128]{3,2,1,0:T(8,128)S(1)} %get-tuple-element.86.refs_, ...), custom_call_target="tpu_custom_call", output_to_operand_aliasing={{0}: (0, {}), {1}: (1, {}), {2}: (2, {}), {3}: (3, {})} | custom-call | bytes 60000 | tf_op jit(solution)/shard_map/pallas_call | solution.py:36
  17.5 1.5 %collective-permute-start.7 = (f32[2,128,128]{2,1,0:T(8,128)S(1)}, f32[2,128,128]{2,1,0:T(8,128)S(1)}, u32[]{:S(2)}, u32[]{:S(2)}) collective-permute-start(f32[2,128,128]{2,1,0:T(8,128)S(1)} %get-tuple-element.112), channel_id=1, source_target_pairs={{0,1},{1,0},{2,3},{3,2},{4,5},{5,4},{6,7},{7,6},{8,9},{9,8},{10,11... | collective-permute-start | bytes 393224 | tf_op jit(solution)/shard_map/ppermute | solution.py:591
  19.8 0.6 %shard_map.104.coef.refs_2_.refs_4_ = f32[8,128,128]{2,1,0:T(8,128)S(1)} custom-call(f32[8,128,128]{2,1,0:T(8,128)S(1)} %shard_map.101.refs_2_.refs_4_.coef_in, f32[4,64,128]{2,1,0:T(8,128)S(1)} %collective-permute-done.6.refs_0_, f32[16,16,128]{2,1,0:T(8,128)S(1)} %get-tuple-element.94.refs_1_.place, ...), custom_call_target="tpu_custom_call", output_to_operand_aliasing={{}: (0, {})} | custom-call | bytes 60000 | tf_op jit(solution)/shard_map/pallas_call | solution.py:36
  20.9 0.9 %shard_map.106 = (f32[3,9,144,128]{3,2,1,0:T(8,128)S(1)}, f32[3,9,144,128]{3,2,1,0:T(8,128)S(1)}) custom-call(f32[3,9,144,128]{3,2,1,0:T(8,128)S(1)} %get-tuple-element.108.refs_0_, f32[3,9,144,128]{3,2,1,0:T(8,128)S(1)} %get-tuple-element.109.refs_1_, ...), custom_call_target="tpu_custom_call", output_to_operand_aliasing={{0}: (0, {}), {1}: (1, {})} | custom-call | bytes 110000 | tf_op jit(solution)/shard_map/pallas_call | solution.py:36
  21.8 2.1 %collective-permute-done.7.refs_5_.refs_6_ = f32[2,128,128]{2,1,0:T(8,128)S(1)} collective-permute-done((f32[2,128,128]{2,1,0:T(8,128)S(1)}, f32[2,128,128]{2,1,0:T(8,128)S(1)}, u32[]{:S(2)}, u32[]{:S(2)}) %collective-permute-start.7) | collective-permute-done | bytes 131104 | tf_op jit(solution)/shard_map/ppermute | solution.py:591
  24.1 1.4 %collective-permute-start.9 = (f32[2,128,128]{2,1,0:T(8,128)S(1)}, f32[2,128,128]{2,1,0:T(8,128)S(1)}, u32[]{:S(2)}, u32[]{:S(2)}) collective-permute-start(f32[2,128,128]{2,1,0:T(8,128)S(1)} %get-tuple-element.126), channel_id=1, source_target_pairs={{0,1},{1,0},{2,3},{3,2},{4,5},{5,4},{6,7},{7,6},{8,9},{9,8},{10,11... | collective-permute-start | bytes 393224 | tf_op jit(solution)/shard_map/ppermute | solution.py:591
  25.5 1.2 %shard_map.108 = (f32[3,9,144,128]{3,2,1,0:T(8,128)S(1)}, f32[3,9,144,128]{3,2,1,0:T(8,128)S(1)}, f32[3,9,144,128]{3,2,1,0:T(8,128)S(1)}, f32[8,144,128]{2,1,0:T(8,128)S(1)}) custom-call(f32[3,9,144,128]{3,2,1,0:T(8,128)S(1)} %get-tuple-element.106.refs_0_, ...), custom_call_target="tpu_custom_call", output_to_operand_aliasing={{0}: (0, {}), {1}: (1, {}), {2}: (2, {}), {3}: (3, {})} | custom-call | bytes 120000 | tf_op jit(solution)/shard_map/pallas_call | solution.py:36
  26.9 1.3 %collective-permute-start.10 = (f32[2,128,128]{2,1,0:T(8,128)S(1)}, f32[2,128,128]{2,1,0:T(8,128)S(1)}, u32[]{:S(2)}, u32[]{:S(2)}) collective-permute-start(f32[2,128,128]{2,1,0:T(8,128)S(1)} %get-tuple-element.133), channel_id=1, source_target_pairs={{0,1},{1,0},{2,3},{3,2},{4,5},{5,4},{6,7},{7,6},{8,9},{9,8},{10,11... | collective-permute-start | bytes 393224 | tf_op jit(solution)/shard_map/ppermute | solution.py:591
  28.2 0.9 %shard_map.110 = (f32[3,9,144,128]{3,2,1,0:T(8,128)S(1)}, f32[3,9,144,128]{3,2,1,0:T(8,128)S(1)}) custom-call(f32[3,9,144,128]{3,2,1,0:T(8,128)S(1)} %get-tuple-element.122.refs_0_, f32[3,9,144,128]{3,2,1,0:T(8,128)S(1)} %get-tuple-element.123.refs_1_, ...), custom_call_target="tpu_custom_call", output_to_operand_aliasing={{0}: (0, {}), {1}: (1, {})} | custom-call | bytes 110000 | tf_op jit(solution)/shard_map/pallas_call | solution.py:36
  29.2 0.6 %collective-permute-done.9.refs_5_.refs_6_ = f32[2,128,128]{2,1,0:T(8,128)S(1)} collective-permute-done((f32[2,128,128]{2,1,0:T(8,128)S(1)}, f32[2,128,128]{2,1,0:T(8,128)S(1)}, u32[]{:S(2)}, u32[]{:S(2)}) %collective-permute-start.9) | collective-permute-done | bytes 131104 | tf_op jit(solution)/shard_map/ppermute | solution.py:591
  30.0 1.3 %collective-permute-start.11 = (f32[2,128,128]{2,1,0:T(8,128)S(1)}, f32[2,128,128]{2,1,0:T(8,128)S(1)}, u32[]{:S(2)}, u32[]{:S(2)}) collective-permute-start(f32[2,128,128]{2,1,0:T(8,128)S(1)} %get-tuple-element.144), channel_id=1, source_target_pairs={{0,1},{1,0},{2,3},{3,2},{4,5},{5,4},{6,7},{7,6},{8,9},{9,8},{10,11... | collective-permute-start | bytes 393224 | tf_op jit(solution)/shard_map/ppermute | solution.py:591
  31.3 1.2 %shard_map.112 = (f32[3,9,144,128]{3,2,1,0:T(8,128)S(1)}, f32[3,9,144,128]{3,2,1,0:T(8,128)S(1)}, f32[3,9,144,128]{3,2,1,0:T(8,128)S(1)}, f32[8,144,128]{2,1,0:T(8,128)S(1)}) custom-call(f32[3,9,144,128]{3,2,1,0:T(8,128)S(1)} %get-tuple-element.120.refs_0_, ...), custom_call_target="tpu_custom_call", output_to_operand_aliasing={{0}: (0, {}), {1}: (1, {}), {2}: (2, {}), {3}: (3, {})} | custom-call | bytes 120000 | tf_op jit(solution)/shard_map/pallas_call | solution.py:36
  33.3 1.6 %collective-permute-start.12 = (f32[2,128,128]{2,1,0:T(8,128)S(1)}, f32[2,128,128]{2,1,0:T(8,128)S(1)}, u32[]{:S(2)}, u32[]{:S(2)}) collective-permute-start(f32[2,128,128]{2,1,0:T(8,128)S(1)} %get-tuple-element.147), channel_id=1, source_target_pairs={{0,1},{1,0},{2,3},{3,2},{4,5},{5,4},{6,7},{7,6},{8,9},{9,8},{10,11... | collective-permute-start | bytes 393224 | tf_op jit(solution)/shard_map/ppermute | solution.py:591
  34.8 0.9 %shard_map.114 = (f32[3,9,144,128]{3,2,1,0:T(8,128)S(1)}, f32[3,9,144,128]{3,2,1,0:T(8,128)S(1)}) custom-call(f32[3,9,144,128]{3,2,1,0:T(8,128)S(1)} %get-tuple-element.136.refs_0_, f32[3,9,144,128]{3,2,1,0:T(8,128)S(1)} %get-tuple-element.137.refs_1_, ...), custom_call_target="tpu_custom_call", output_to_operand_aliasing={{0}: (0, {}), {1}: (1, {})} | custom-call | bytes 110000 | tf_op jit(solution)/shard_map/pallas_call | solution.py:36
  35.8 1.2 %shard_map.115 = (f32[3,9,144,128]{3,2,1,0:T(8,128)S(1)}, f32[3,9,144,128]{3,2,1,0:T(8,128)S(1)}, f32[3,9,144,128]{3,2,1,0:T(8,128)S(1)}, f32[8,144,128]{2,1,0:T(8,128)S(1)}) custom-call(f32[3,9,144,128]{3,2,1,0:T(8,128)S(1)} %get-tuple-element.134.refs_0_, ...), custom_call_target="tpu_custom_call", output_to_operand_aliasing={{0}: (0, {}), {1}: (1, {}), {2}: (2, {}), {3}: (3, {})} | custom-call | bytes 120000 | tf_op jit(solution)/shard_map/pallas_call | solution.py:36
  37.1 0.7 %shard_map.119 = (f32[4,48,128]{2,1,0:T(8,128)S(1)}, f32[4,48,128]{2,1,0:T(8,128)S(1)}, f32[4,48,128]{2,1,0:T(8,128)S(1)}, f32[4,48,128]{2,1,0:T(8,128)S(1)}) custom-call(f32[8,144,128]{2,1,0:T(8,128)S(1)} %get-tuple-element.150.total, f32[3,9,144,128]{3,2,1,0:T(8,128)S(1)} %get-tuple-element.145.refs_2_.after, s32[16]{0:T(128)} %block_ids_far.1), custom_call_target="tpu_custom_call" | custom-call | bytes 80000 | tf_op jit(solution)/shard_map/pallas_call | solution.py:36
  39.4 1.6 %collective-permute-start.15 = (f32[4,48,128]{2,1,0:T(8,128)S(1)}, f32[4,48,128]{2,1,0:T(8,128)S(1)}, u32[]{:S(2)}, u32[]{:S(2)}) collective-permute-start(f32[4,48,128]{2,1,0:T(8,128)S(1)} %get-tuple-element.158), channel_id=1, source_target_pairs={{0,4},{2,6},{4,0},{6,2},{8,12},{10,14},{12,8},{14,10},{16,20},{18,... | collective-permute-start | bytes 294920 | tf_op jit(solution)/shard_map/ppermute | solution.py:591
  40.9 1.1 %collective-permute-start.17 = (f32[4,16,128]{2,1,0:T(8,128)S(1)}, f32[4,16,128]{2,1,0:T(8,128)S(1)}, u32[]{:S(2)}, u32[]{:S(2)}) collective-permute-start(f32[4,16,128]{2,1,0:T(8,128)S(1)} %get-tuple-element.161), channel_id=1, source_target_pairs={{0,4},{2,6},{4,0},{6,2},{8,12},{10,14},{12,8},{14,10},{16,20},{18,... | collective-permute-start | bytes 98312 | tf_op jit(solution)/shard_map/ppermute | solution.py:591
  42.0 3.2 %collective-permute-done.17.refs_3_ = f32[4,16,128]{2,1,0:T(8,128)S(1)} collective-permute-done((f32[4,16,128]{2,1,0:T(8,128)S(1)}, f32[4,16,128]{2,1,0:T(8,128)S(1)}, u32[]{:S(2)}, u32[]{:S(2)}) %collective-permute-start.17) | collective-permute-done | bytes 32800 | tf_op jit(solution)/shard_map/ppermute | solution.py:591
  45.2 2.2 %collective-permute-start.18 = (f32[64,128]{1,0:T(8,128)S(1)}, f32[64,128]{1,0:T(8,128)S(1)}, u32[]{:S(2)}, u32[]{:S(2)}) collective-permute-start(f32[64,128]{1,0:T(8,128)S(1)} %get-tuple-element.163), channel_id=1, source_target_pairs={{0,24},{2,26},{4,28},{6,30},{8,16},{10,18},{12,20},{14,22},{16,8},... | collective-permute-start | bytes 98312 | tf_op jit(solution)/shard_map/ppermute | solution.py:591
  47.4 2.3 %collective-permute-start.20 = (f32[64,128]{1,0:T(8,128)S(1)}, f32[64,128]{1,0:T(8,128)S(1)}, u32[]{:S(2)}, u32[]{:S(2)}) collective-permute-start(f32[64,128]{1,0:T(8,128)S(1)} %get-tuple-element.165), channel_id=1, source_target_pairs={{0,8},{2,10},{4,12},{6,14},{8,0},{10,2},{12,4},{14,6},{16,24},{18,... | collective-permute-start | bytes 98312 | tf_op jit(solution)/shard_map/ppermute | solution.py:591
  49.7 1.7 %shard_map.118 = f32[1,6,8,128,128]{4,3,2,1,0:T(8,128)} custom-call(f32[3,9,144,128]{3,2,1,0:T(8,128)S(1)} %get-tuple-element.148.e, f32[3,9,144,128]{3,2,1,0:T(8,128)S(1)} %get-tuple-element.149.h), custom_call_target="tpu_custom_call" | custom-call | bytes 170000 | tf_op jit(solution)/shard_map/pallas_call | solution.py:36
  51.4 1.1 %collective-permute-done.19.refs_2_ = f32[64,128]{1,0:T(8,128)S(1)} collective-permute-done((f32[64,128]{1,0:T(8,128)S(1)}, f32[64,128]{1,0:T(8,128)S(1)}, u32[]{:S(2)}, u32[]{:S(2)}) %collective-permute-start.19) | collective-permute-done | bytes 32800 | tf_op jit(solution)/shard_map/ppermute | solution.py:591
  52.5 0.6 %shard_map.124 = f32[64,128]{1,0:T(8,128)} custom-call(f32[64,128]{1,0:T(8,128)S(1)} %get-tuple-element.162.refs_0_, f32[64,128]{1,0:T(8,128)S(1)} %collective-permute-done.18.refs_1_, f32[64,128]{1,0:T(8,128)S(1)} %collective-permute-done.19.refs_2_, f32[64,128]{1,0:T(8,128)S(1)} %collective-permute-done.20.refs_3_), custom_call_target="tpu_custom_call" | custom-call | bytes 30000 | tf_op jit(solution)/shard_map/pallas_call | solution.py:36
  (44 shorter events, 5.6 us)
Async XLA Ops:
  0.6 12.5 %copy-start = (f32[1,6,8,128,128]{4,3,2,1,0:T(8,128)S(1)}, f32[1,6,8,128,128]{4,3,2,1,0:T(8,128)}, u32[]{:S(2)}) copy-start(f32[1,6,8,128,128]{4,3,2,1,0:T(8,128)} %given.2) | copy-start | bytes 9437188
  0.6 8.6 %collective-permute-start.2 = (f32[64,128]{1,0:T(8,128)}, f32[64,128]{1,0:T(8,128)S(1)}, u32[]{:S(2)}, u32[]{:S(2)}) collective-permute-start(f32[64,128]{1,0:T(8,128)} %bitcast.2), channel_id=1, source_target_pairs={{0,24},{2,26},{4,28},{6,30},{8,16},{10,18},{12,20},{14,22},{16,8},... | collective-permute-start | bytes 98312 | tf_op jit(solution)/shard_map/ppermute | solution.py:591
  5.8 5.0 %collective-permute-start.1 = (f32[64,128]{1,0:T(8,128)}, f32[64,128]{1,0:T(8,128)S(1)}, u32[]{:S(2)}, u32[]{:S(2)}) collective-permute-start(f32[64,128]{1,0:T(8,128)} %bitcast.3), channel_id=1, source_target_pairs={{0,16},{2,18},{4,20},{6,22},{8,24},{10,26},{12,28},{14,30},{16,0},... | collective-permute-start | bytes 98312 | tf_op jit(solution)/shard_map/ppermute | solution.py:591
  5.8 5.0 %collective-permute-start = (f32[64,128]{1,0:T(8,128)}, f32[64,128]{1,0:T(8,128)S(1)}, u32[]{:S(2)}, u32[]{:S(2)}) collective-permute-start(f32[64,128]{1,0:T(8,128)} %bitcast.4), channel_id=1, source_target_pairs={{0,8},{2,10},{4,12},{6,14},{8,0},{10,2},{12,4},{14,6},{16,24},{18,... | collective-permute-start | bytes 98312 | tf_op jit(solution)/shard_map/ppermute | solution.py:591
  7.8 6.5 %copy-start.1 = (f32[1,6,8,128,128]{4,3,2,1,0:T(8,128)S(1)}, f32[1,6,8,128,128]{4,3,2,1,0:T(8,128)}, u32[]{:S(2)}) copy-start(f32[1,6,8,128,128]{4,3,2,1,0:T(8,128)} %given.3) | copy-start | bytes 9437188
  7.8 8.4 %collective-permute-start.3 = (f32[2,2,128,128]{3,2,1,0:T(8,128)S(1)}, f32[2,2,128,128]{3,2,1,0:T(8,128)S(1)}, u32[]{:S(2)}, u32[]{:S(2)}) collective-permute-start(f32[2,2,128,128]{3,2,1,0:T(8,128)S(1)} %get-tuple-element.91), channel_id=1, source_target_pairs={{0,1},{1,0},{2,3},{3,2},{4,5},{5,4},{6,7},{7,6},{8,9},{9,8},{10,11... | collective-permute-start | bytes 786440 | tf_op jit(solution)/shard_map/ppermute | solution.py:591
  10.8 5.0 %collective-permute-start.4 = (f32[4,64,128]{2,1,0:T(8,128)S(1)}, f32[4,64,128]{2,1,0:T(8,128)S(1)}, u32[]{:S(2)}, u32[]{:S(2)}) collective-permute-start(f32[4,64,128]{2,1,0:T(8,128)S(1)} %shard_map.96.near.refs_8_), channel_id=1, source_target_pairs={{0,4},{2,6},{4,0},{6,2},{8,12},{10,14},{12,8},{14,10},{16,20},{18,... | collective-permute-start | bytes 393224 | tf_op jit(solution)/shard_map/ppermute | solution.py:591
  13.0 3.2 %collective-permute-start.5 = (f32[4,64,128]{2,1,0:T(8,128)S(1)}, f32[4,64,128]{2,1,0:T(8,128)S(1)}, u32[]{:S(2)}, u32[]{:S(2)}) collective-permute-start(f32[4,64,128]{2,1,0:T(8,128)S(1)} %shard_map.96.near.refs_8_), channel_id=1, source_target_pairs={{0,2},{2,0},{4,6},{6,4},{8,10},{10,8},{12,14},{14,12},{16,18},{18,... | collective-permute-start | bytes 393224 | tf_op jit(solution)/shard_map/ppermute | solution.py:591
  15.8 1.4 %collective-permute-start.6 = (f32[4,64,128]{2,1,0:T(8,128)S(1)}, f32[4,64,128]{2,1,0:T(8,128)S(1)}, u32[]{:S(2)}, u32[]{:S(2)}) collective-permute-start(f32[4,64,128]{2,1,0:T(8,128)S(1)} %shard_map.99.refs_9_), channel_id=1, source_target_pairs={{0,2},{2,0},{4,6},{6,4},{8,10},{10,8},{12,14},{14,12},{16,18},{18,... | collective-permute-start | bytes 393224 | tf_op jit(solution)/shard_map/ppermute | solution.py:591
  17.5 6.4 %collective-permute-start.7 = (f32[2,128,128]{2,1,0:T(8,128)S(1)}, f32[2,128,128]{2,1,0:T(8,128)S(1)}, u32[]{:S(2)}, u32[]{:S(2)}) collective-permute-start(f32[2,128,128]{2,1,0:T(8,128)S(1)} %get-tuple-element.112), channel_id=1, source_target_pairs={{0,1},{1,0},{2,3},{3,2},{4,5},{5,4},{6,7},{7,6},{8,9},{9,8},{10,11... | collective-permute-start | bytes 393224 | tf_op jit(solution)/shard_map/ppermute | solution.py:591
  19.2 7.5 %collective-permute-start.8 = (f32[2,128,128]{2,1,0:T(8,128)S(1)}, f32[2,128,128]{2,1,0:T(8,128)S(1)}, u32[]{:S(2)}, u32[]{:S(2)}) collective-permute-start(f32[2,128,128]{2,1,0:T(8,128)S(1)} %get-tuple-element.119), channel_id=1, source_target_pairs={{0,1},{1,0},{2,3},{3,2},{4,5},{5,4},{6,7},{7,6},{8,9},{9,8},{10,11... | collective-permute-start | bytes 393224 | tf_op jit(solution)/shard_map/ppermute | solution.py:591
  24.1 5.6 %collective-permute-start.9 = (f32[2,128,128]{2,1,0:T(8,128)S(1)}, f32[2,128,128]{2,1,0:T(8,128)S(1)}, u32[]{:S(2)}, u32[]{:S(2)}) collective-permute-start(f32[2,128,128]{2,1,0:T(8,128)S(1)} %get-tuple-element.126), channel_id=1, source_target_pairs={{0,1},{1,0},{2,3},{3,2},{4,5},{5,4},{6,7},{7,6},{8,9},{9,8},{10,11... | collective-permute-start | bytes 393224 | tf_op jit(solution)/shard_map/ppermute | solution.py:591
  26.9 6.1 %collective-permute-start.10 = (f32[2,128,128]{2,1,0:T(8,128)S(1)}, f32[2,128,128]{2,1,0:T(8,128)S(1)}, u32[]{:S(2)}, u32[]{:S(2)}) collective-permute-start(f32[2,128,128]{2,1,0:T(8,128)S(1)} %get-tuple-element.133), channel_id=1, source_target_pairs={{0,1},{1,0},{2,3},{3,2},{4,5},{5,4},{6,7},{7,6},{8,9},{9,8},{10,11... | collective-permute-start | bytes 393224 | tf_op jit(solution)/shard_map/ppermute | solution.py:591
  30.0 7.0 %collective-permute-start.11 = (f32[2,128,128]{2,1,0:T(8,128)S(1)}, f32[2,128,128]{2,1,0:T(8,128)S(1)}, u32[]{:S(2)}, u32[]{:S(2)}) collective-permute-start(f32[2,128,128]{2,1,0:T(8,128)S(1)} %get-tuple-element.144), channel_id=1, source_target_pairs={{0,1},{1,0},{2,3},{3,2},{4,5},{5,4},{6,7},{7,6},{8,9},{9,8},{10,11... | collective-permute-start | bytes 393224 | tf_op jit(solution)/shard_map/ppermute | solution.py:591
  33.3 5.1 %collective-permute-start.12 = (f32[2,128,128]{2,1,0:T(8,128)S(1)}, f32[2,128,128]{2,1,0:T(8,128)S(1)}, u32[]{:S(2)}, u32[]{:S(2)}) collective-permute-start(f32[2,128,128]{2,1,0:T(8,128)S(1)} %get-tuple-element.147), channel_id=1, source_target_pairs={{0,1},{1,0},{2,3},{3,2},{4,5},{5,4},{6,7},{7,6},{8,9},{9,8},{10,11... | collective-permute-start | bytes 393224 | tf_op jit(solution)/shard_map/ppermute | solution.py:591
  37.8 1.4 %collective-permute-start.13 = (f32[4,48,128]{2,1,0:T(8,128)S(1)}, f32[4,48,128]{2,1,0:T(8,128)S(1)}, u32[]{:S(2)}, u32[]{:S(2)}) collective-permute-start(f32[4,48,128]{2,1,0:T(8,128)S(1)} %get-tuple-element.153), channel_id=1, source_target_pairs={{0,2},{2,0},{4,6},{6,4},{8,10},{10,8},{12,14},{14,12},{16,18},{18,... | collective-permute-start | bytes 294920 | tf_op jit(solution)/shard_map/ppermute | solution.py:591
  37.9 1.4 %collective-permute-start.14 = (f32[4,48,128]{2,1,0:T(8,128)S(1)}, f32[4,48,128]{2,1,0:T(8,128)S(1)}, u32[]{:S(2)}, u32[]{:S(2)}) collective-permute-start(f32[4,48,128]{2,1,0:T(8,128)S(1)} %get-tuple-element.154), channel_id=1, source_target_pairs={{0,2},{2,0},{4,6},{6,4},{8,10},{10,8},{12,14},{14,12},{16,18},{18,... | collective-permute-start | bytes 294920 | tf_op jit(solution)/shard_map/ppermute | solution.py:591
  38.8 2.1 %collective-permute-start.16 = (f32[8,16,128]{2,1,0:T(8,128)S(1)}, f32[8,16,128]{2,1,0:T(8,128)S(1)}, u32[]{:S(2)}, u32[]{:S(2)}) collective-permute-start(f32[8,16,128]{2,1,0:T(8,128)S(1)} %get-tuple-element.159), channel_id=1, source_target_pairs={{0,2},{2,0},{4,6},{6,4},{8,10},{10,8},{12,14},{14,12},{16,18},{18,... | collective-permute-start | bytes 196616 | tf_op jit(solution)/shard_map/ppermute | solution.py:591
  39.4 5.8 %collective-permute-start.15 = (f32[4,48,128]{2,1,0:T(8,128)S(1)}, f32[4,48,128]{2,1,0:T(8,128)S(1)}, u32[]{:S(2)}, u32[]{:S(2)}) collective-permute-start(f32[4,48,128]{2,1,0:T(8,128)S(1)} %get-tuple-element.158), channel_id=1, source_target_pairs={{0,4},{2,6},{4,0},{6,2},{8,12},{10,14},{12,8},{14,10},{16,20},{18,... | collective-permute-start | bytes 294920 | tf_op jit(solution)/shard_map/ppermute | solution.py:591
  40.9 4.2 %collective-permute-start.17 = (f32[4,16,128]{2,1,0:T(8,128)S(1)}, f32[4,16,128]{2,1,0:T(8,128)S(1)}, u32[]{:S(2)}, u32[]{:S(2)}) collective-permute-start(f32[4,16,128]{2,1,0:T(8,128)S(1)} %get-tuple-element.161), channel_id=1, source_target_pairs={{0,4},{2,6},{4,0},{6,2},{8,12},{10,14},{12,8},{14,10},{16,20},{18,... | collective-permute-start | bytes 98312 | tf_op jit(solution)/shard_map/ppermute | solution.py:591
  45.2 6.2 %collective-permute-start.18 = (f32[64,128]{1,0:T(8,128)S(1)}, f32[64,128]{1,0:T(8,128)S(1)}, u32[]{:S(2)}, u32[]{:S(2)}) collective-permute-start(f32[64,128]{1,0:T(8,128)S(1)} %get-tuple-element.163), channel_id=1, source_target_pairs={{0,24},{2,26},{4,28},{6,30},{8,16},{10,18},{12,20},{14,22},{16,8},... | collective-permute-start | bytes 98312 | tf_op jit(solution)/shard_map/ppermute | solution.py:591
  47.4 5.1 %collective-permute-start.19 = (f32[64,128]{1,0:T(8,128)S(1)}, f32[64,128]{1,0:T(8,128)S(1)}, u32[]{:S(2)}, u32[]{:S(2)}) collective-permute-start(f32[64,128]{1,0:T(8,128)S(1)} %get-tuple-element.164), channel_id=1, source_target_pairs={{0,16},{2,18},{4,20},{6,22},{8,24},{10,26},{12,28},{14,30},{16,0},... | collective-permute-start | bytes 98312 | tf_op jit(solution)/shard_map/ppermute | solution.py:591
  47.4 5.1 %collective-permute-start.20 = (f32[64,128]{1,0:T(8,128)S(1)}, f32[64,128]{1,0:T(8,128)S(1)}, u32[]{:S(2)}, u32[]{:S(2)}) collective-permute-start(f32[64,128]{1,0:T(8,128)S(1)} %get-tuple-element.165), channel_id=1, source_target_pairs={{0,8},{2,10},{4,12},{6,14},{8,0},{10,2},{12,4},{14,6},{16,24},{18,... | collective-permute-start | bytes 98312 | tf_op jit(solution)/shard_map/ppermute | solution.py:591
